TPU v7x, 32 devices: a whole 2x2x4 slice. The times are simulated.
32 devices in a mesh: gx: 8 (over z, x), gy: 4 (over y, core).
Axes of the slice: x: 2, y: 2, z: 4, core: 2. Of those that a mesh axis runs over, the one named last changes fastest.
Arguments:
- thermal_state: float32 [4, 512, 2048], P(None, 'gx', 'gy'), may hold values from 0 to 1
- baseline_thermal_coefficient: float32 [4, 512, 2048], P(None, 'gx', 'gy'), may hold values from 0.5 to 2
- stirrer_grid_locations: int32 [64], replicated, may hold values from 0 to 1048575
- stirrer_energy_supply: float32 [64], replicated, may hold values from 13107 to 131072
Outputs:
- new_temperature: float32 [4, 512, 2048], P(None, 'gx', 'gy')
Inputs may be any that keep to these rules, and one draw needn't show every extreme that they name: `stirrer_grid_locations`: each entry is a plate cell x * 2048 + y.
All inputs are finite; a program needn't handle non-finite values.
Results may differ from a plain program's by a relative error of at most 0.0023.
Values sent between devices are 32-bit elements; how exact they have to be, the bound alone decides.
No kernel may reach another device: no remote copies, remote signals or barrier semaphores. Data moves between devices by JAX's collectives and lax.ppermute only.
A program may use at most 64 MiB of HBM per device.

v0:
```python
import jax
import jax.numpy as jnp
from jax import lax
from jax.sharding import PartitionSpec as P

RATE = 2000.0
THERMAL_GROWTH = 0.8


def with_halo(array, sides, width):
    for axis, dim in sides:
        count, length = (lax.axis_size(axis), array.shape[dim])
        up = [(i, (i + 1) % count) for i in range(count - 1)]
        down = [(j, i) for i, j in up]
        last = lax.slice_in_dim(array, length - width, length, axis=dim)
        first = lax.slice_in_dim(array, 0, width, axis=dim)
        before = lax.ppermute(last, axis, up)
        after = lax.ppermute(first, axis, down)
        array = jnp.concatenate([before, array, after], axis=dim)
    return array


def shifted_2(value, axis, steps):
    count = lax.axis_size(axis)
    first, last = (max(0, -steps), min(count, count - steps))
    return lax.ppermute(value, axis, [(source, source + steps) for source in range(first, last)])


def shifted(values, stride, traversal_orientation, from_low):
    length = values.shape[traversal_orientation]
    widths = [(0, 0)] * values.ndim
    if from_low:
        widths[traversal_orientation] = (stride, 0)
        return lax.slice_in_dim(jnp.pad(values, widths), 0, length, axis=traversal_orientation)
    widths[traversal_orientation] = (0, stride)
    return lax.slice_in_dim(
        jnp.pad(values, widths), stride, stride + length, axis=traversal_orientation
    )


def reduce_lines(lower_band, upper_band, targets, traversal_orientation):
    length = lower_band.shape[traversal_orientation]
    stride = 1
    while stride < length:
        lower_prev = shifted(lower_band, stride, traversal_orientation, True)
        upper_prev = shifted(upper_band, stride, traversal_orientation, True)
        lower_next = shifted(lower_band, stride, traversal_orientation, False)
        upper_next = shifted(upper_band, stride, traversal_orientation, False)
        pivot = 1.0 - lower_band * upper_prev - upper_band * lower_next
        targets = tuple(
            (
                (
                    target
                    - lower_band * shifted(target, stride, traversal_orientation, True)
                    - upper_band * shifted(target, stride, traversal_orientation, False)
                )
                / pivot
                for target in targets
            )
        )
        lower_band, upper_band = (
            -lower_band * lower_prev / pivot,
            -upper_band * upper_next / pivot,
        )
        stride = stride * 2
    return targets


def ghost_margin(values, traversal_orientation):
    widths = [(0, 0)] * values.ndim
    widths[traversal_orientation] = (1, 1)
    return jnp.pad(values, widths)


def three_rows(padded, traversal_orientation):
    length = padded.shape[traversal_orientation] - 2
    west_cells = lax.slice_in_dim(padded, 0, length, axis=traversal_orientation)
    centre = lax.slice_in_dim(padded, 1, length + 1, axis=traversal_orientation)
    east_cells = lax.slice_in_dim(padded, 2, length + 2, axis=traversal_orientation)
    return (west_cells, centre, east_cells)


def conductances(padded, traversal_orientation):
    west_cells, centre, east_cells = three_rows(padded, traversal_orientation)
    bottom_interface_transfer = jnp.where(
        jnp.minimum(west_cells, centre) > 0.0, 0.5 * (west_cells + centre), 0.0
    )
    top_interface_transfer = jnp.where(
        jnp.minimum(centre, east_cells) > 0.0, 0.5 * (centre + east_cells), 0.0
    )
    return (bottom_interface_transfer, top_interface_transfer)


def diffusion_stencil(
    padded, bottom_interface_transfer, top_interface_transfer, traversal_orientation
):
    west_cells, centre, east_cells = three_rows(padded, traversal_orientation)
    return top_interface_transfer * (east_cells - centre) - bottom_interface_transfer * (
        centre - west_cells
    )


def take_row(values, where_row, traversal_orientation):
    return lax.slice_in_dim(values, where_row, where_row + 1, axis=traversal_orientation)


def partition_solve(
    lower_band, upper_band, target, traversal_orientation, send_next, solve_interface
):
    length = lower_band.shape[traversal_orientation]
    inner_low = lax.slice_in_dim(lower_band, 0, length - 1, axis=traversal_orientation)
    inner_high = lax.slice_in_dim(upper_band, 0, length - 1, axis=traversal_orientation)
    inner_target = lax.slice_in_dim(target, 0, length - 1, axis=traversal_orientation)
    position = lax.broadcasted_iota(jnp.int32, inner_low.shape, traversal_orientation)
    first_row = position == 0
    last_row = position == length - 2
    interior, left_resp, right_resp = reduce_lines(
        jnp.where(first_row, 0.0, inner_low),
        jnp.where(last_row, 0.0, inner_high),
        (inner_target, jnp.where(first_row, inner_low, 0.0), jnp.where(last_row, inner_high, 0.0)),
        traversal_orientation,
    )
    heads = jnp.stack(
        [
            take_row(interior, 0, traversal_orientation),
            take_row(left_resp, 0, traversal_orientation),
            take_row(right_resp, 0, traversal_orientation),
        ],
        0,
    )
    following = send_next(heads)
    sep_low = take_row(lower_band, length - 1, traversal_orientation)
    sep_high = take_row(upper_band, length - 1, traversal_orientation)
    sep_target = take_row(target, length - 1, traversal_orientation)
    last_value = take_row(interior, length - 2, traversal_orientation)
    last_left = take_row(left_resp, length - 2, traversal_orientation)
    last_right = take_row(right_resp, length - 2, traversal_orientation)
    sep_diag = 1.0 - sep_low * last_right - sep_high * following[1]
    coefs = jnp.stack(
        [
            -sep_low * last_left / sep_diag,
            -sep_high * following[2] / sep_diag,
            (sep_target - sep_low * last_value - sep_high * following[0]) / sep_diag,
        ],
        0,
    )
    before_value, own_value = solve_interface(coefs)
    inner_rows = interior - left_resp * before_value - right_resp * own_value
    return jnp.concatenate([inner_rows, own_value], axis=traversal_orientation)


def per_device(
    thermal_state, baseline_thermal_coefficient, stirrer_grid_locations, stirrer_energy_supply
):
    sheet_number, horizontal_grid_number, vertical_grid_number = thermal_state.shape
    thermal_coefficient_of = baseline_thermal_coefficient * (1.0 + THERMAL_GROWTH * thermal_state)
    extended_field = with_halo(
        jnp.concatenate([thermal_state, thermal_coefficient_of], 0), (("gx", 1), ("gy", 2)), 1
    )
    temp_x = extended_field[:sheet_number, :, 1:-1]
    cond_x = extended_field[sheet_number:, :, 1:-1]
    temp_y = extended_field[:sheet_number, 1:-1, :]
    cond_y = extended_field[sheet_number:, 1:-1, :]
    xlow, xhigh = conductances(cond_x, 1)
    ylow, yhigh = conductances(cond_y, 2)
    bottom_depth_limit, top_depth_limit = conductances(ghost_margin(thermal_coefficient_of, 0), 0)
    forward_euler_advance = (
        diffusion_stencil(temp_x, xlow, xhigh, 1)
        + diffusion_stencil(temp_y, ylow, yhigh, 2)
        + diffusion_stencil(ghost_margin(thermal_state, 0), bottom_depth_limit, top_depth_limit, 0)
    )
    plate_width = vertical_grid_number * lax.axis_size("gy")
    local_x = stirrer_grid_locations // plate_width - lax.axis_index("gx") * horizontal_grid_number
    local_y = stirrer_grid_locations % plate_width - lax.axis_index("gy") * vertical_grid_number
    onehot_x = (
        local_x[:, None] == lax.broadcasted_iota(jnp.int32, (1, horizontal_grid_number), 1)
    ).astype(jnp.float32) * stirrer_energy_supply[:, None]
    onehot_y = (
        local_y[:, None] == lax.broadcasted_iota(jnp.int32, (1, vertical_grid_number), 1)
    ).astype(jnp.float32)
    plane = jnp.dot(
        onehot_x.T, onehot_y, precision=lax.Precision.HIGHEST, preferred_element_type=jnp.float32
    )
    target = RATE * forward_euler_advance
    target = jnp.concatenate([target[:1] + plane[None], target[1:]], 0)

    def x_next(heads):
        return shifted_2(heads, "gx", -1)

    def x_interface(coefs):
        whole = lax.all_gather(coefs, "gx", axis=2, tiled=True)
        solved = reduce_lines(whole[0], whole[1], (whole[2],), 1)[0]
        member_index = lax.axis_index("gx")
        own_value = lax.dynamic_slice_in_dim(solved, member_index, 1, 1)
        before_value = lax.dynamic_slice_in_dim(solved, jnp.maximum(member_index - 1, 0), 1, 1) * (
            member_index > 0
        ).astype(jnp.float32)
        return (before_value, own_value)

    x_pivot = 1.0 + RATE * (xlow + xhigh)
    first_pass = partition_solve(
        -RATE * xlow / x_pivot, -RATE * xhigh / x_pivot, target / x_pivot, 1, x_next, x_interface
    )
    moved, moved_cond = (
        lax.all_to_all(first_pass, "gy", split_axis=1, concat_axis=2, tiled=True),
        lax.all_to_all(thermal_coefficient_of, "gy", split_axis=1, concat_axis=2, tiled=True),
    )
    mlow, mhigh = conductances(ghost_margin(moved_cond, 2), 2)
    m_pivot = 1.0 + RATE * (mlow + mhigh)
    solved_lines = reduce_lines(
        -RATE * mlow / m_pivot, -RATE * mhigh / m_pivot, (moved / m_pivot,), 2
    )[0]
    second_pass = lax.all_to_all(solved_lines, "gy", split_axis=2, concat_axis=1, tiled=True)
    z_pivot = 1.0 + RATE * (bottom_depth_limit + top_depth_limit)
    closing_traversal = reduce_lines(
        -RATE * bottom_depth_limit / z_pivot,
        -RATE * top_depth_limit / z_pivot,
        (second_pass / z_pivot,),
        0,
    )[0]
    return thermal_state + closing_traversal


def solution(mesh):
    in_specs = (P(None, "gx", "gy"), P(None, "gx", "gy"), P(), P())
    out_specs = P(None, "gx", "gy")
    return jax.shard_map(
        per_device, mesh=mesh, in_specs=in_specs, out_specs=out_specs, check_vma=False
    )
```

profile of v0, /device:TPU:0, one launch (start us, length us, event | category | flops | bytes accessed | tf_op | source)
XLA Modules:
  0.0 134.7 jit_solution(185758143050149726)
XLA Ops:
  0.0 1.4 %add_multiply_fusion = f32[4,64,512]{2,1,0:T(8,128)S(1)} fusion(f32[4,64,512]{2,1,0:T(8,128)} %param.5, f32[4,64,512]{2,1,0:T(8,128)} %param.4), kind=kLoop, calls=%fused_computation.481 | loop fusion | flops 393216 | bytes 1572864 | tf_op jit(solution)/shard_map/mul | solution.py:156
  1.4 0.9 pad_maximum_fusion.23
  2.3 1.3 collective-permute-start
  3.6 5.5 %collective-permute-start.1 = (f32[8,1,512]{2,1,0:T(1,128)S(1)}, f32[8,1,512]{2,1,0:T(1,128)S(1)}, u32[]{:S(2)}, u32[]{:S(2)}) collective-permute-start(f32[8,1,512]{2,1,0:T(1,128)S(1)} %get-tuple-element.67), channel_id=1, source_target_pairs={{0,4},{4,8},{8,12},{12,16},{16,20},{20,24},{24,28},{1,5},{5,9},{9,... | collective-permute-start | bytes 49160 | tf_op jit(solution)/shard_map/ppermute | solution.py:17
  9.1 0.7 fusion.360
  9.8 0.7 slice.787
  10.5 1.1 pad_maximum_fusion.20
  11.6 1.3 collective-permute-start.2
  12.9 3.0 %collective-permute-start.3 = (f32[8,66,1]{2,1,0:T(8,128)S(1)}, f32[8,66,1]{2,1,0:T(8,128)S(1)}, u32[]{:S(2)}, u32[]{:S(2)}) collective-permute-start(f32[8,66,1]{2,1,0:T(8,128)S(1)} %get-tuple-element.10), channel_id=1, source_target_pairs={{0,1},{1,2},{2,3},{4,5},{5,6},{6,7},{8,9},{9,10},{10,11},{12,13},{... | collective-permute-start | bytes 6344 | tf_op jit(solution)/shard_map/ppermute | solution.py:17
  16.0 1.6 %multiply_divide_fusion = (f32[4,64,512]{2,1,0:T(8,128)}, f32[4,64,512]{2,1,0:T(8,128)}, f32[4,64,512]{2,1,0:T(8,128)S(1)}) fusion(f32[4,64,512]{2,1,0:T(8,128)S(1)} %add_multiply_fusion, f32[4,64,512]{2,1,0:T(8,128)S(1)} %copy-done, f32[8,1,512]{2,1,0:T(1,128)S(1)} %collective-permute-done.1, f32[8,1,512]{2,1,0:T(1,128)S(1)} %collective-permute-done), kind=kLoop, calls=%fused_computation.456 | loop fusion | flops 6422528 | bytes 2654208 | tf_op jit(solution)/shard_map/div | solution.py:217
  17.6 2.5 %fusion.278 = f32[4,64,512]{2,1,0:T(8,128)S(1)} fusion(f32[4,64,512]{2,1,0:T(8,128)S(1)} %copy-done, f32[8,66,1]{2,1,0:T(8,128)S(1)} %collective-permute-done.3, f32[8,1,512]{2,1,0:T(1,128)S(1)} %collective-permute-done, f32[8,1,512]{2,1,0:T(1,128)S(1)} %collective-permute-done.1, f32[4,64,512]{2,1,0:T(8,128)S(1)} %add_multiply_fusion, ...), kind=kLoop, calls=%fused_computation.407 | loop fusion | flops 9437184 | bytes 1609856 | tf_op jit(solution)/shard_map/mul | solution.py:184
  20.1 0.3 fusion
  20.5 0.4 maximum_divide_fusion
  20.9 0.3 slice_select_fusion.1
  21.1 0.3 subtract_divide_fusion.1
  21.5 0.7 fusion.283
  22.2 0.3 fusion.162
  22.5 0.7 fusion.108
  23.1 0.3 fusion.167
  23.4 0.6 fusion.119
  24.0 0.2 fusion.172
  24.2 0.4 fusion.132
  24.6 0.2 fusion.208
  24.8 0.4 fusion.190
  25.3 0.6 fusion.239
  25.9 0.8 copy-done.1
  26.7 0.2 copy-done.2
  26.9 1.3 collective-permute-start.4
  28.2 1.2 copy.14
  29.3 7.3 %all-to-all-start.1 = ((f32[4,64,512]{2,0,1:T(4,128)}), f32[4,64,512]{2,0,1:T(4,128)}, u32[]{:S(2)}, u32[]{:S(2)}) async-start(f32[4,64,512]{2,0,1:T(4,128)} %copy.14), calls=%async_computation.1 | async-start | bytes 1048576 | tf_op jit(solution)/shard_map/all_to_all | solution.py:206
  36.7 0.9 fusion.356
  37.7 34.1 %all_gather.3 = f32[3,4,8,512]{3,1,0,2:T(4,128)S(1)} all-gather(f32[3,4,1,512]{3,1,0,2:T(4,128)S(1)} %copy.8), channel_id=1, replica_groups=mesh['gx'=8,'gy'=4] {'gx'}, dimensions={2}, use_global_device_ids=true | all-gather | bytes 221184 | tf_op jit(solution)/shard_map/all_gather | solution.py:191
  72.0 0.1 fusion.322
  72.0 0.1 fusion.335
  72.2 1.4 %multiply_subtract_fusion = f32[4,63,512]{2,1,0:T(8,128)S(1)} fusion(f32[4,63,512]{2,1,0:T(8,128)} %copy-done.1, f32[4,63,512]{2,1,0:T(8,128)S(1)} %get-tuple-element.44, f32[4,63,512]{2,1,0:T(8,128)} %copy-done.2, f32[4,512]{1,0:T(4,128)S(1)} %bitcast.86, f32[4,512]{1,0:T(4,128)S(1)} %bitcast.87), kind=kLoop, calls=%fused_computation.466 | loop fusion | flops 516096 | bytes 2080768 | tf_op jit(solution)/shard_map/sub | solution.py:148
  73.7 1.1 copy.12
  74.8 4.2 %all-to-all-start = ((f32[4,64,512]{2,0,1:T(4,128)}), f32[4,64,512]{2,0,1:T(4,128)S(1)}, u32[]{:S(2)}, u32[]{:S(2)}) async-start(f32[4,64,512]{2,0,1:T(4,128)} %copy.12), calls=%async_computation | async-start | bytes 1048576 | tf_op jit(solution)/shard_map/all_to_all | solution.py:205
  79.0 1.4 %copy.37 = f32[4,4,16,512]{3,1,2,0:T(4,128)S(1)} copy(f32[4,4,16,512]{3,0,2,1:T(4,128)} %bitcast.15) | data formatting | bytes 1048576 | tf_op jit(solution)/shard_map/all_to_all | solution.py:206
  80.3 0.4 all_to_all.46
  80.7 7.1 %all-to-all-done = f32[4,64,512]{2,0,1:T(4,128)S(1)} async-done(((f32[4,64,512]{2,0,1:T(4,128)}), f32[4,64,512]{2,0,1:T(4,128)S(1)}, u32[]{:S(2)}, u32[]{:S(2)}) %all-to-all-start) | async-done | bytes 524320 | tf_op jit(solution)/shard_map/all_to_all | solution.py:205
  87.8 0.3 copy.38
  88.1 0.4 all_to_all.42
  88.5 0.9 multiply_divide_fusion.2
  89.4 1.4 %fusion.17 = (f32[4,16,2048]{2,1,0:T(8,128)S(1)}, f32[4,16,2048]{2,1,0:T(8,128)S(1)}, f32[4,16,2048]{2,1,0:T(8,128)S(1)}) fusion(f32[4,16,2048]{2,1,0:T(8,128)S(1)} %get-tuple-element.78, f32[4,16,2048]{2,1,0:T(8,128)S(1)} %get-tuple-element.79, f32[4,16,2048]{2,1,0:T(8,128)S(1)} %get-tuple-element.80), kind=kLoop, calls=%fused_computation.146 | loop fusion | flops 3014656 | bytes 3145728 | tf_op jit(solution)/shard_map/div | solution.py:63
  90.8 1.4 %fusion.30 = (f32[4,16,2048]{2,1,0:T(8,128)S(1)}, f32[4,16,2048]{2,1,0:T(8,128)S(1)}, f32[4,16,2048]{2,1,0:T(8,128)S(1)}) fusion(f32[4,16,2048]{2,1,0:T(8,128)S(1)} %get-tuple-element.41, f32[4,16,2048]{2,1,0:T(8,128)S(1)} %get-tuple-element.42, f32[4,16,2048]{2,1,0:T(8,128)S(1)} %get-tuple-element.43), kind=kLoop, calls=%fused_computation.159 | loop fusion | flops 3014656 | bytes 3145728 | tf_op jit(solution)/shard_map/div | solution.py:63
  92.3 1.4 %fusion.43 = (f32[4,16,2048]{2,1,0:T(8,128)S(1)}, f32[4,16,2048]{2,1,0:T(8,128)S(1)}, f32[4,16,2048]{2,1,0:T(8,128)S(1)}) fusion(f32[4,16,2048]{2,1,0:T(8,128)S(1)} %get-tuple-element.38, f32[4,16,2048]{2,1,0:T(8,128)S(1)} %get-tuple-element.39, f32[4,16,2048]{2,1,0:T(8,128)S(1)} %get-tuple-element.40), kind=kLoop, calls=%fused_computation.172 | loop fusion | flops 3014656 | bytes 3145728 | tf_op jit(solution)/shard_map/div | solution.py:63
  93.7 1.4 %fusion.56 = (f32[4,16,2048]{2,1,0:T(8,128)S(1)}, f32[4,16,2048]{2,1,0:T(8,128)S(1)}, f32[4,16,2048]{2,1,0:T(8,128)S(1)}) fusion(f32[4,16,2048]{2,1,0:T(8,128)S(1)} %get-tuple-element.35, f32[4,16,2048]{2,1,0:T(8,128)S(1)} %get-tuple-element.36, f32[4,16,2048]{2,1,0:T(8,128)S(1)} %get-tuple-element.37), kind=kLoop, calls=%fused_computation.185 | loop fusion | flops 3014656 | bytes 3145728 | tf_op jit(solution)/shard_map/div | solution.py:63
  95.1 1.4 %fusion.69 = (f32[4,16,2048]{2,1,0:T(8,128)S(1)}, f32[4,16,2048]{2,1,0:T(8,128)S(1)}, f32[4,16,2048]{2,1,0:T(8,128)S(1)}) fusion(f32[4,16,2048]{2,1,0:T(8,128)S(1)} %get-tuple-element.32, f32[4,16,2048]{2,1,0:T(8,128)S(1)} %get-tuple-element.33, f32[4,16,2048]{2,1,0:T(8,128)S(1)} %get-tuple-element.34), kind=kLoop, calls=%fused_computation.198 | loop fusion | flops 3014656 | bytes 3145728 | tf_op jit(solution)/shard_map/div | solution.py:63
  96.5 1.4 %fusion.82 = (f32[4,16,2048]{2,1,0:T(8,128)S(1)}, f32[4,16,2048]{2,1,0:T(8,128)S(1)}, f32[4,16,2048]{2,1,0:T(8,128)S(1)}) fusion(f32[4,16,2048]{2,1,0:T(8,128)S(1)} %get-tuple-element.29, f32[4,16,2048]{2,1,0:T(8,128)S(1)} %get-tuple-element.30, f32[4,16,2048]{2,1,0:T(8,128)S(1)} %get-tuple-element.31), kind=kLoop, calls=%fused_computation.211 | loop fusion | flops 3014656 | bytes 3145728 | tf_op jit(solution)/shard_map/div | solution.py:63
  98.0 1.6 %fusion.95 = (f32[4,16,2048]{2,1,0:T(8,128)S(1)}, f32[4,16,2048]{2,1,0:T(8,128)S(1)}, f32[4,16,2048]{2,1,0:T(8,128)S(1)}) fusion(f32[4,16,2048]{2,1,0:T(8,128)S(1)} %get-tuple-element.26, f32[4,16,2048]{2,1,0:T(8,128)S(1)} %get-tuple-element.27, f32[4,16,2048]{2,1,0:T(8,128)S(1)} %get-tuple-element.28), kind=kLoop, calls=%fused_computation.224 | loop fusion | flops 3014656 | bytes 3145728 | tf_op jit(solution)/shard_map/div | solution.py:63
  99.6 0.3 fusion.104
  99.9 0.3 fusion.186
  100.2 0.3 fusion.222
  100.6 0.2 fusion.258
  100.8 3.1 %copy.16 = f32[4,16,2048]{1,0,2:T(4,128)} copy(f32[4,16,2048]{2,1,0:T(8,128)S(1)} %fusion.258) | data formatting | bytes 1048576 | tf_op jit(solution)/shard_map/div | solution.py:52
  103.9 5.0 %reshape.3 = f32[4,1,32768]{2,1,0:T(1,128)S(1)} reshape(f32[2048,4,16]{2,1,0:T(4,128)} %bitcast.77) | data formatting | bytes 1048576
  108.9 11.2 %all_to_all.54 = f32[4,1,32768]{2,1,0:T(1,128)S(1)} all-to-all(f32[4,1,32768]{2,1,0:T(1,128)S(1)} %reshape.3), channel_id=1, replica_groups=mesh['gx'=8,'gy'=4] {'gy'}, dimensions={0} | all-to-all | bytes 1048576 | tf_op jit(solution)/shard_map/all_to_all | solution.py:213
  120.2 0.5 broadcast.676
  120.7 2.1 %reduce = f32[4,32768]{1,0:T(4,128)S(1)} reduce(f32[4,1,32768]{2,1,0:T(1,128)S(1)} %all_to_all.54, f32[]{:T(128)} %broadcast.676), dimensions={1}, to_apply=%all_to_all.47.reduce_sub_computation | reduce | bytes 1048580 | tf_op jit(solution)/shard_map/all_to_all | solution.py:213
  122.8 5.0 %reshape.4 = f32[2048,4,16]{2,1,0:T(4,128)} reshape(f32[4,32768]{1,0:T(4,128)S(1)} %reduce) | data formatting | bytes 1048576
  127.8 3.5 %copy.18 = f32[4,4,16,512]{3,2,1,0:T(8,128)S(1)} copy(f32[4,4,16,512]{2,0,3,1:T(4,128)} %bitcast.78) | data formatting | bytes 1048576 | tf_op jit(solution)/shard_map/all_to_all | solution.py:213
  131.3 0.2 bitcast_divide_fusion
  131.5 2.2 %fusion.235 = (f32[4,64,512]{2,1,0:T(8,128)S(1)}, f32[4,64,512]{2,1,0:T(8,128)S(1)}, f32[4,64,512]{2,1,0:T(8,128)S(1)}) fusion(f32[4,64,512]{2,1,0:T(8,128)S(1)} %copy-done.3, f32[4,64,512]{2,1,0:T(8,128)} %get-tuple-element.76, f32[4,64,512]{2,1,0:T(8,128)S(1)} %bitcast_divide_fusion), kind=kLoop, calls=%fused_computation.364 | loop fusion | flops 3014656 | bytes 3145728 | tf_op jit(solution)/shard_map/div | solution.py:63
  133.7 1.0 fusion.268
  (33 shorter events, 0.4 us)
Async XLA Ops:
  0.0 16.0 %copy-start = (f32[4,64,512]{2,1,0:T(8,128)S(1)}, f32[4,64,512]{2,1,0:T(8,128)}, u32[]{:S(2)}) copy-start(f32[4,64,512]{2,1,0:T(8,128)} %param.4) | copy-start | bytes 1572868
  1.4 18.8 %copy-start.4 = (f32[64]{0:T(128)S(1)}, f32[64]{0:T(128)}, u32[]{:S(2)}) copy-start(f32[64]{0:T(128)} %param.7) | copy-start | bytes 772
  2.3 8.2 %collective-permute-start = (f32[8,1,512]{2,1,0:T(1,128)S(1)}, f32[8,1,512]{2,1,0:T(1,128)S(1)}, u32[]{:S(2)}, u32[]{:S(2)}) collective-permute-start(f32[8,1,512]{2,1,0:T(1,128)S(1)} %get-tuple-element.68), channel_id=1, source_target_pairs={{4,0},{8,4},{12,8},{16,12},{20,16},{24,20},{28,24},{5,1},{9,5},{13... | collective-permute-start | bytes 49160 | tf_op jit(solution)/shard_map/ppermute | solution.py:18
  3.6 6.9 %collective-permute-start.1 = (f32[8,1,512]{2,1,0:T(1,128)S(1)}, f32[8,1,512]{2,1,0:T(1,128)S(1)}, u32[]{:S(2)}, u32[]{:S(2)}) collective-permute-start(f32[8,1,512]{2,1,0:T(1,128)S(1)} %get-tuple-element.67), channel_id=1, source_target_pairs={{0,4},{4,8},{8,12},{12,16},{16,20},{20,24},{24,28},{1,5},{5,9},{9,... | collective-permute-start | bytes 49160 | tf_op jit(solution)/shard_map/ppermute | solution.py:17
  11.6 5.9 %collective-permute-start.2 = (f32[8,66,1]{2,1,0:T(8,128)S(1)}, f32[8,66,1]{2,1,0:T(8,128)S(1)}, u32[]{:S(2)}, u32[]{:S(2)}) collective-permute-start(f32[8,66,1]{2,1,0:T(8,128)S(1)} %get-tuple-element.9), channel_id=1, source_target_pairs={{1,0},{2,1},{3,2},{5,4},{6,5},{7,6},{9,8},{10,9},{11,10},{13,12},{... | collective-permute-start | bytes 6344 | tf_op jit(solution)/shard_map/ppermute | solution.py:18
  12.9 4.6 %collective-permute-start.3 = (f32[8,66,1]{2,1,0:T(8,128)S(1)}, f32[8,66,1]{2,1,0:T(8,128)S(1)}, u32[]{:S(2)}, u32[]{:S(2)}) collective-permute-start(f32[8,66,1]{2,1,0:T(8,128)S(1)} %get-tuple-element.10), channel_id=1, source_target_pairs={{0,1},{1,2},{2,3},{4,5},{5,6},{6,7},{8,9},{9,10},{10,11},{12,13},{... | collective-permute-start | bytes 6344 | tf_op jit(solution)/shard_map/ppermute | solution.py:17
  25.8 0.8 copy-start.1
  25.9 1.0 copy-start.2
  26.9 9.8 %collective-permute-start.4 = (f32[3,4,1,512]{3,2,1,0:T(1,128)S(1)}, f32[3,4,1,512]{3,2,1,0:T(1,128)S(1)}, u32[]{:S(2)}, u32[]{:S(2)}) collective-permute-start(f32[3,4,1,512]{3,2,1,0:T(1,128)S(1)} %pad_maximum_fusion.21), channel_id=1, source_target_pairs={{4,0},{8,4},{12,8},{16,12},{20,16},{24,20},{28,24},{5,1},{9,5},{13... | collective-permute-start | bytes 73736 | tf_op jit(solution)/shard_map/ppermute | solution.py:26
  29.3 45.5 %all-to-all-start.1 = ((f32[4,64,512]{2,0,1:T(4,128)}), f32[4,64,512]{2,0,1:T(4,128)}, u32[]{:S(2)}, u32[]{:S(2)}) async-start(f32[4,64,512]{2,0,1:T(4,128)} %copy.14), calls=%async_computation.1 | async-start | bytes 1048576 | tf_op jit(solution)/shard_map/all_to_all | solution.py:206
  74.8 13.0 %all-to-all-start = ((f32[4,64,512]{2,0,1:T(4,128)}), f32[4,64,512]{2,0,1:T(4,128)S(1)}, u32[]{:S(2)}, u32[]{:S(2)}) async-start(f32[4,64,512]{2,0,1:T(4,128)} %copy.12), calls=%async_computation | async-start | bytes 1048576 | tf_op jit(solution)/shard_map/all_to_all | solution.py:205
  127.8 3.7 %copy-start.3 = (f32[4,64,512]{2,1,0:T(8,128)S(1)}, f32[4,64,512]{2,1,0:T(8,128)}, u32[]{:S(2)}) copy-start(f32[4,64,512]{2,1,0:T(8,128)} %get-tuple-element.75) | copy-start | bytes 1572868
where the time goes:
time: 135 us
  blocking collectives  45.4 us (34%)
  other arithmetic  33.9 us (25%)
  starting transfers between devices  23.9 us (18%)
  local copies, waits for them, and re-layouts  23.7 us (18%)
  waiting for transfers between devices  7.11 us (5%)
    all_gather x1, blocking collectives, x_interface(): whole = lax.all_gather(coefs, 'gx', axis=2, tiled=True)  34.1 us
    div x13, other arithmetic, reduce_lines(): -upper_band * upper_next / pivot  13.4 us
    all_to_all x1, blocking collectives, per_device(): lax.all_to_all(solved_lines, 'gy', split_axis=2, concat_axis=1, tiled=True)  11.2 us
    unnamed x17, local copies, waits for them, and re-layouts  11.1 us
    ppermute x2, starting transfers between devices, with_halo(): before = lax.ppermute(last, axis, up)  8.52 us
    all_to_all x1, starting transfers between devices, per_device(): lax.all_to_all(thermal_coefficient_of, 'gy', split_axis=1, concat_axis=2,...  7.35 us
    all_to_all x1, waiting for transfers between devices, per_device(): lax.all_to_all(first_pass, 'gy', split_axis=1, concat_axis=2, tiled=True)  7.09 us
    div x13, other arithmetic, reduce_lines(): (target - lower_band * shifted(target, stride, traversal_orientation, Tru...  4.92 us
  transfers between devices with their start and end apart: 7, of which 1 were waited for; matrix products, arithmetic and copies ran while one was open for 7% of the time, Pallas kernels for 0%

commit v1 on v0

v1 whole, which is shorter than its diff:
```python
import functools

import jax
import jax.numpy as jnp
from jax import lax
from jax.experimental import pallas as pl
from jax.experimental.pallas import tpu as pltpu
from jax.sharding import PartitionSpec as P

RATE = 2000.0
THERMAL_GROWTH = 0.8
LANES = 128
SUBLANES = 8
F32 = jnp.float32
VMEM_LIMIT = 40 * 1024 * 1024


def half_conduct(base, temperature):
    return base * (0.5 * RATE + (0.5 * RATE * THERMAL_GROWTH) * temperature)


def join(a, b, face):
    a00, a0l, all_, a_first, a_last = a
    b00, b0l, bll, b_first, b_last = b
    inv = 1.0 / (1.0 / face + all_ + b00)
    left = a0l * inv
    right = b0l * inv
    jump = b_first - a_last
    joined = (
        a00 - left * a0l,
        left * b0l,
        bll - right * b0l,
        a_first + left * jump,
        b_last - right * jump,
    )
    return joined, (jump * inv, right, left)


def eliminate(cond, target, steps):
    kept = []
    here = cond(0)
    rhs = target(0)
    one = jnp.ones_like(here)
    ground, path, first, first_first = one, one, None, None
    for k in range(steps - 1):
        following = cond(k + 1)
        face = here + following
        inv = 1.0 / (ground + face)
        w = face * inv
        h = rhs * inv
        p = path * inv
        kept.append((w, h, p))
        first = path * h if first is None else first + path * h
        first_first = path * p if first_first is None else first_first + path * p
        path = path * w
        rhs = target(k + 1) + w * rhs
        ground = 1.0 + w * ground
        here = following
    inv = 1.0 / ground
    last = rhs * inv
    first_last = path * inv
    kept.append((inv, last, first_last))
    block = (
        first_first + path * first_last,
        first_last,
        inv,
        first + path * last,
        last,
    )
    return block, kept


def edges_kernel(tlo, thi, blo, bhi, lo, hi):
    sheets, rows, _ = tlo.shape
    lane = lax.broadcasted_iota(jnp.int32, (rows, LANES), 1)
    for t_ref, b_ref, out, source in ((tlo, blo, lo, 0), (thi, bhi, hi, LANES - 1)):
        packed = jnp.zeros((rows, LANES), F32)
        for z in range(sheets):
            t = t_ref[z]
            c = half_conduct(b_ref[z], t)
            packed = jnp.where(lane == z, t[:, source : source + 1], packed)
            packed = jnp.where(lane == sheets + z, c[:, source : source + 1], packed)
        out[...] = packed


def pack_edges(temperature, base):
    sheets, rows, columns = temperature.shape
    last = columns // LANES - 1
    first_block = pl.BlockSpec((sheets, rows, LANES), lambda i: (0, 0, 0))
    last_block = pl.BlockSpec((sheets, rows, LANES), lambda i: (0, 0, last))
    whole = pl.BlockSpec((rows, LANES), lambda i: (0, 0))
    shape = jax.ShapeDtypeStruct((rows, LANES), F32)
    return pl.pallas_call(
        edges_kernel,
        grid=(1,),
        in_specs=[first_block, last_block, first_block, last_block],
        out_specs=[whole, whole],
        out_shape=[shape, shape],
        compiler_params=pltpu.CompilerParams(vmem_limit_bytes=VMEM_LIMIT),
    )(temperature, temperature, base, base)


def x_forward_kernel(
    chips, per, plate, loc, energy, t_ref, b_ref, before, after, w_ref, h_ref, p_ref, chain, send,
    t_s, c_s, q_s, m_s,
):
    sheets, rows, columns = t_ref.shape
    chunks = columns // LANES
    steps = rows // SUBLANES
    x0 = lax.axis_index("gx") * rows
    y0 = lax.axis_index("gy") * columns

    place = loc[...]
    local_x = place // plate - x0
    local_y = place % plate - y0
    count = place.shape[1]
    by_x = jnp.where(
        lax.broadcasted_iota(jnp.int32, (rows, count), 0) == local_x, energy[...], 0.0
    )
    by_y = jnp.where(
        lax.broadcasted_iota(jnp.int32, (columns, count), 0) == local_y, 1.0, 0.0
    ).astype(F32)
    plane = lax.dot_general(
        by_x,
        by_y,
        (((1,), (1,)), ((), ())),
        precision=lax.Precision.HIGHEST,
        preferred_element_type=F32,
    )

    lane = lax.broadcasted_iota(jnp.int32, (SUBLANES, columns), 1)
    for r in range(steps):
        at = slice(r * SUBLANES, (r + 1) * SUBLANES)
        lo = before[at, :]
        hi = after[at, :]
        ts = [t_ref[z, at, :] for z in range(sheets)]
        cs = [half_conduct(b_ref[z, at, :], ts[z]) for z in range(sheets)]
        flux = [(cs[z] + cs[z + 1]) * (ts[z + 1] - ts[z]) for z in range(sheets - 1)]
        for z in range(sheets):
            t, c = ts[z], cs[z]
            t_lo, t_hi = lo[:, z : z + 1], hi[:, z : z + 1]
            c_lo, c_hi = lo[:, sheets + z : sheets + z + 1], hi[:, sheets + z : sheets + z + 1]
            t_next = jnp.where(lane == columns - 1, t_hi, pltpu.roll(t, columns - 1, 1))
            c_next = jnp.where(lane == columns - 1, c_hi, pltpu.roll(c, columns - 1, 1))
            face = jnp.where(c_next > 0.0, c + c_next, 0.0)
            out_flux = face * (t_next - t)
            face_lo = jnp.where(c_lo > 0.0, c[:, :1] + c_lo, 0.0)
            in_flux = jnp.where(lane == 0, face_lo * (t[:, :1] - t_lo), pltpu.roll(out_flux, 1, 1))
            total = t + (out_flux - in_flux)
            if z < sheets - 1:
                total = total + flux[z]
            if z > 0:
                total = total - flux[z - 1]
            if z == 0:
                total = total + plane[at, :]
            for y in range(chunks):
                part = slice(y * LANES, (y + 1) * LANES)
                t_s[z * chunks + y, at, :] = total[:, part]
                c_s[z * chunks + y, at, :] = c[:, part]

    for y in range(chunks):

        def cells(ref):
            return lambda k: jnp.stack(
                [ref[z * chunks + y, pl.ds(k, SUBLANES, stride=steps), :] for z in range(sheets)], 0
            )

        block, kept = eliminate(cells(c_s), cells(t_s), steps)
        for k, (w, h, p) in enumerate(kept):
            w_ref[y, k] = w
            h_ref[y, k] = h
            p_ref[y, k] = p
        views = block + (cells(c_s)(0), cells(c_s)(steps - 1))
        for q, value in enumerate(views):
            for z in range(sheets):
                first = (z * chunks + y) * SUBLANES
                q_s[q, first : first + SUBLANES, :] = value[z]

    lines = sheets * chunks

    def segment(s):
        return [q_s[q, pl.ds(s, lines, stride=SUBLANES), :] for q in range(7)]

    total = segment(0)
    c_first, c_last = total[5], total[6]
    total = tuple(total[:5])
    for s in range(1, SUBLANES):
        item = segment(s)
        total, links = join(total, tuple(item[:5]), c_last + item[5])
        c_last = item[6]
        for q in range(3):
            chain[q, s - 1] = links[q]
    for q, value in enumerate(total + (c_first, c_last)):
        m_s[q] = value
    send[...] = jnp.zeros_like(send)
    for d in range(min(chips, lines // per)):
        for q in range(7):
            send[d, q * per : (q + 1) * per, :] = m_s[q, d * per : (d + 1) * per, :]


def x_forward(temperature, base, before, after, loc, energy, chips, per, plate):
    sheets, rows, columns = temperature.shape
    chunks = columns // LANES
    lines = sheets * chunks
    steps = rows // SUBLANES
    stored = jax.ShapeDtypeStruct((chunks, steps, sheets, SUBLANES, LANES), F32)
    return pl.pallas_call(
        functools.partial(x_forward_kernel, chips, per, plate),
        out_shape=[
            stored,
            stored,
            stored,
            jax.ShapeDtypeStruct((3, SUBLANES - 1, lines, LANES), F32),
            jax.ShapeDtypeStruct((chips, padded(7 * per), LANES), F32),
        ],
        scratch_shapes=[
            pltpu.VMEM((lines, rows, LANES), F32),
            pltpu.VMEM((lines, rows, LANES), F32),
            pltpu.VMEM((7, lines * SUBLANES, LANES), F32),
            pltpu.VMEM((7, lines, LANES), F32),
        ],
        compiler_params=pltpu.CompilerParams(vmem_limit_bytes=VMEM_LIMIT),
    )(loc, energy, temperature, base, before, after)


def padded(rows):
    return -(-rows // SUBLANES) * SUBLANES


def chain_fluxes(item, count):
    _, _, last_last, _, last, _, c_last = item(0)
    links = []
    for k in range(1, count):
        b00, b0l, bll, b_first, b_last, c_first, c_end = item(k)
        inv = 1.0 / (1.0 / (c_last + c_first) + last_last + b00)
        right = b0l * inv
        jump = b_first - last
        links.append((jump * inv, right))
        last = b_last - right * jump
        last_last = bll - right * b0l
        c_last = c_end
    fluxes = [None] * (count - 1)
    flux = None
    for k in range(count - 2, -1, -1):
        own, right = links[k]
        flux = own if flux is None else own + right * flux
        fluxes[k] = flux
    return fluxes


def x_interface_kernel(per, got, send):
    count = got.shape[0]

    def item(k):
        return [got[k, q * per : (q + 1) * per, :] for q in range(7)]

    fluxes = chain_fluxes(item, count)
    zero = jnp.zeros((per, LANES), F32)
    send[...] = jnp.zeros_like(send)
    for k in range(count):
        send[k, 0:per, :] = -fluxes[k - 1] if k > 0 else zero
        send[k, per : 2 * per, :] = fluxes[k] if k < count - 1 else zero


def x_interface(got, per):
    return pl.pallas_call(
        functools.partial(x_interface_kernel, per),
        out_shape=jax.ShapeDtypeStruct((got.shape[0], padded(2 * per), LANES), F32),
        compiler_params=pltpu.CompilerParams(vmem_limit_bytes=VMEM_LIMIT),
    )(got)


Y_PARTS = 4


def y_forward_kernel(
    per, got, chain, xw, xh, xp, t_ref, b_ref, w_ref, h_ref, p_ref, inner, outer, send,
    e_s, f_s, g_s, c_s, q_s,
):
    sheets, rows, columns = t_ref.shape
    chunks = columns // LANES
    lines = sheets * chunks
    x_steps = rows // SUBLANES

    for d in range(lines // per):
        e_s[0, d * per : (d + 1) * per, :] = got[d, 0:per, :]
        e_s[1, d * per : (d + 1) * per, :] = got[d, per : 2 * per, :]
    low = e_s[0]
    flux = e_s[1]
    for s in range(SUBLANES - 1, -1, -1):
        f_s[1, pl.ds(s, lines, stride=SUBLANES), :] = flux
        if s > 0:
            flux = chain[0, s - 1] + chain[1, s - 1] * flux - chain[2, s - 1] * low
            f_s[0, pl.ds(s, lines, stride=SUBLANES), :] = -flux
        else:
            f_s[0, pl.ds(s, lines, stride=SUBLANES), :] = low
    for y in range(chunks):
        ends = [
            jnp.stack(
                [
                    f_s[i, (z * chunks + y) * SUBLANES : (z * chunks + y + 1) * SUBLANES, :]
                    for z in range(sheets)
                ],
                0,
            )
            for i in range(2)
        ]
        value = ends[1]
        for k in range(x_steps - 1, -1, -1):
            value = xw[y, k] * value + (xh[y, k] + xp[y, k] * ends[0])
            for z in range(sheets):
                g_s[z * chunks + y, pl.ds(k, SUBLANES, stride=x_steps), :] = value[z]

    pairs = sheets * rows // LANES
    each = sheets // pairs
    for m in range(pairs):
        for y in range(chunks):
            part = slice(y * LANES, (y + 1) * LANES)
            field, cond = [], []
            for z in range(m * each, (m + 1) * each):
                t = t_ref[z, :, part]
                field.append(g_s[z * chunks + y] - t)
                cond.append(half_conduct(b_ref[z, :, part], t))
            e_y = jnp.concatenate(field, 0).T
            c_y = jnp.concatenate(cond, 0).T
            q_s[0, m, part, :] = e_y
            c_s[m, part, :] = c_y

    span = columns // SUBLANES
    steps = span // Y_PARTS

    def cells(pick):
        return lambda k: jnp.stack(
            [
                jnp.stack([pick(m)[pl.ds(j * steps + k, SUBLANES, stride=span), :] for j in range(Y_PARTS)], 0)
                for m in range(pairs)
            ],
            0,
        )

    cond_of = cells(lambda m: c_s.at[m])
    block, kept = eliminate(cond_of, cells(lambda m: q_s.at[0, m]), steps)
    for k, (w, h, p) in enumerate(kept):
        w_ref[k] = w
        h_ref[k] = h
        p_ref[k] = p
    firsts, lasts = cond_of(0), cond_of(steps - 1)
    total = tuple(v[:, 0] for v in block)
    for j in range(1, Y_PARTS):
        total, links = join(total, tuple(v[:, j] for v in block), lasts[:, j - 1] + firsts[:, j])
        for q in range(3):
            inner[q, j - 1] = links[q]
    views = total + (firsts[:, 0], lasts[:, Y_PARTS - 1])
    for q, value in enumerate(views):
        for m in range(pairs):
            e_s[q, m * SUBLANES : (m + 1) * SUBLANES, :] = value[m]

    def segment(s):
        return [e_s[q, pl.ds(s, pairs, stride=SUBLANES), :] for q in range(7)]

    total = segment(0)
    c_first, c_last = total[5], total[6]
    total = tuple(total[:5])
    for s in range(1, SUBLANES):
        item = segment(s)
        total, links = join(total, tuple(item[:5]), c_last + item[5])
        c_last = item[6]
        for q in range(3):
            outer[q, s - 1] = links[q]
    send[...] = jnp.zeros_like(send)
    for q, value in enumerate(total + (c_first, c_last)):
        for d in range(send.shape[0]):
            send[d, q * pairs : (q + 1) * pairs, :] = value


def y_forward(got, chain, xw, xh, xp, temperature, base, per, gy):
    sheets, rows, columns = temperature.shape
    chunks = columns // LANES
    lines = sheets * chunks
    pairs = sheets * rows // LANES
    steps = columns // SUBLANES // Y_PARTS
    stored = jax.ShapeDtypeStruct((steps, pairs, Y_PARTS, SUBLANES, LANES), F32)
    return pl.pallas_call(
        functools.partial(y_forward_kernel, per),
        out_shape=[
            stored,
            stored,
            stored,
            jax.ShapeDtypeStruct((3, Y_PARTS - 1, pairs, SUBLANES, LANES), F32),
            jax.ShapeDtypeStruct((3, SUBLANES - 1, pairs, LANES), F32),
            jax.ShapeDtypeStruct((gy, padded(7 * pairs), LANES), F32),
        ],
        scratch_shapes=[
            pltpu.VMEM((7, max(lines, pairs * SUBLANES), LANES), F32),
            pltpu.VMEM((2, lines * SUBLANES, LANES), F32),
            pltpu.VMEM((lines, rows, LANES), F32),
            pltpu.VMEM((pairs, columns, LANES), F32),
            pltpu.VMEM((1, pairs, columns, LANES), F32),
        ],
        compiler_params=pltpu.CompilerParams(vmem_limit_bytes=VMEM_LIMIT),
    )(got, chain, xw, xh, xp, temperature, base)


def finish_kernel(got, inner, outer, yw, yh, yp, t_ref, b_ref, out, e_s, u_s):
    sheets, rows, columns = t_ref.shape
    chunks = columns // LANES
    pairs = sheets * rows // LANES
    each = sheets // pairs
    steps = yw.shape[0]
    span = columns // SUBLANES
    count = got.shape[0]
    me = lax.axis_index("gy")

    def item(k):
        return [got[k, q * pairs : (q + 1) * pairs, :] for q in range(7)]

    fluxes = chain_fluxes(item, count)
    low = jnp.zeros((pairs, LANES), F32)
    flux = low
    for k in range(count - 1):
        low = jnp.where(me == k + 1, -fluxes[k], low)
        flux = jnp.where(me == k, fluxes[k], flux)
    for s in range(SUBLANES - 1, -1, -1):
        e_s[1, pl.ds(s, pairs, stride=SUBLANES), :] = flux
        if s > 0:
            flux = outer[0, s - 1] + outer[1, s - 1] * flux - outer[2, s - 1] * low
            e_s[0, pl.ds(s, pairs, stride=SUBLANES), :] = -flux
        else:
            e_s[0, pl.ds(s, pairs, stride=SUBLANES), :] = low
    ends = [
        jnp.stack([e_s[i, m * SUBLANES : (m + 1) * SUBLANES, :] for m in range(pairs)], 0)
        for i in range(2)
    ]
    lows, highs = [None] * Y_PARTS, [None] * Y_PARTS
    flux = ends[1]
    for j in range(Y_PARTS - 1, -1, -1):
        highs[j] = flux
        if j > 0:
            flux = inner[0, j - 1] + inner[1, j - 1] * flux - inner[2, j - 1] * ends[0]
            lows[j] = -flux
        else:
            lows[j] = ends[0]
    low = jnp.stack(lows, 1)
    value = jnp.stack(highs, 1)
    for k in range(steps - 1, -1, -1):
        value = yw[k] * value + (yh[k] + yp[k] * low)
        for m in range(pairs):
            for j in range(Y_PARTS):
                u_s[m, pl.ds(j * steps + k, SUBLANES, stride=span), :] = value[m, j]

    for y in range(chunks):
        part = slice(y * LANES, (y + 1) * LANES)
        turned = [u_s[m, part, :].T for m in range(pairs)]
        for r in range(rows // SUBLANES):
            at = slice(r * SUBLANES, (r + 1) * SUBLANES)
            ts = [t_ref[z, at, part] for z in range(sheets)]
            cs = [half_conduct(b_ref[z, at, part], ts[z]) for z in range(sheets)]
            ground, rhs, kept = None, None, []
            for z in range(sheets):
                first = (z % each) * rows + r * SUBLANES
                own = turned[z // each][first : first + SUBLANES, :]
                if z == 0:
                    rhs = own
                else:
                    face = cs[z - 1] + cs[z]
                    before = 1.0 if ground is None else ground
                    inv = 1.0 / (before + face)
                    w = face * inv
                    kept.append((w, rhs * inv))
                    rhs = own + w * rhs
                    ground = 1.0 + w * before
            value = rhs / ground
            out[sheets - 1, at, part] = ts[sheets - 1] + value
            for z in range(sheets - 2, -1, -1):
                w, h = kept[z]
                value = w * value + h
                out[z, at, part] = ts[z] + value


def finish(got, inner, outer, yw, yh, yp, temperature, base):
    sheets, rows, columns = temperature.shape
    pairs = sheets * rows // LANES
    return pl.pallas_call(
        finish_kernel,
        out_shape=jax.ShapeDtypeStruct(temperature.shape, F32),
        scratch_shapes=[
            pltpu.VMEM((2, pairs * SUBLANES, LANES), F32),
            pltpu.VMEM((pairs, columns, LANES), F32),
        ],
        compiler_params=pltpu.CompilerParams(vmem_limit_bytes=VMEM_LIMIT),
    )(got, inner, outer, yw, yh, yp, temperature, base)


def per_device(temperature, base, locations, energy):
    sheets, rows, columns = temperature.shape
    gx, gy = lax.axis_size("gx"), lax.axis_size("gy")
    lines = sheets * columns // LANES
    per = max(1, lines // gx)
    low_edge, high_edge = pack_edges(temperature, base)
    before = lax.ppermute(high_edge, "gy", [(i, i + 1) for i in range(gy - 1)])
    after = lax.ppermute(low_edge, "gy", [(i + 1, i) for i in range(gy - 1)])
    xw, xh, xp, chain, send = x_forward(
        temperature, base, before, after, locations[None], energy[None], gx, per, columns * gy
    )
    got = lax.all_to_all(send, "gx", split_axis=0, concat_axis=0, tiled=True)
    fluxes = lax.all_to_all(x_interface(got, per), "gx", split_axis=0, concat_axis=0, tiled=True)
    yw, yh, yp, inner, outer, send = y_forward(
        fluxes, chain, xw, xh, xp, temperature, base, per, gy
    )
    got = lax.all_to_all(send, "gy", split_axis=0, concat_axis=0, tiled=True)
    return finish(got, inner, outer, yw, yh, yp, temperature, base)


def solution(mesh):
    in_specs = (P(None, "gx", "gy"), P(None, "gx", "gy"), P(), P())
    out_specs = P(None, "gx", "gy")
    return jax.shard_map(
        per_device, mesh=mesh, in_specs=in_specs, out_specs=out_specs, check_vma=False
    )
```

time: 135 us -> 46.3 us (0.34)
  other arithmetic: 33.9 us -> 0 us
  local copies, waits for them, and re-layouts: 23.7 us -> 2.76 us
  starting transfers between devices: 23.9 us -> 3.65 us
  blocking collectives: 45.4 us -> 29.1 us
  Pallas kernels: 0 us -> 6.44 us
  waiting for transfers between devices: 7.11 us -> 3.93 us
    all_gather x1 -> x0, blocking collectives: 34.1 us -> none  [x_interface(): whole = lax.all_gather(coefs, 'gx', axis=2, tiled=True)]
    div x30 -> x0, other arithmetic: 21.4 us -> none  [the longest x13 13.4 us: reduce_lines(): -upper_band * upper_next / pivot]
    all_to_all x1 -> x3, blocking collectives: 11.2 us -> 29.1 us  [the longest x1 12.5 us: per_device(): got = lax.all_to_all(send, 'gx', split_axis=0, concat_axis=0, tiled=True)]
    all_to_all x2 -> x0, starting transfers between devices: 11.5 us -> none  [the longest x1 7.35 us: per_device(): lax.all_to_all(thermal_coefficient_of, 'gy', split_axis=1, concat_axis=2,...]
    ppermute x5 -> x2, starting transfers between devices: 12.4 us -> 3.65 us  [the longest x1 2.36 us: per_device(): before = lax.ppermute(high_edge, 'gy', [(i, i + 1) for i in range(gy - 1)])]
    unnamed x17 -> x10, local copies, waits for them, and re-layouts: 11.1 us -> 2.76 us
    all_to_all x2 -> x0, waiting for transfers between devices: 7.1 us -> none  [the longest x1 7.09 us: per_device(): lax.all_to_all(first_pass, 'gy', split_axis=1, concat_axis=2, tiled=True)]
    all_to_all x6 -> x0, local copies, waits for them, and re-layouts: 6.48 us -> none  [the longest x2 4.04 us: per_device(): lax.all_to_all(solved_lines, 'gy', split_axis=2, concat_axis=1, tiled=True)]
  transfers between devices with their start and end apart: 7 -> 2, of which waited for: 1 -> 1; matrix products, arithmetic and copies ran while one was open for 7% -> 0% of each run, Pallas kernels for 0% -> 0%
where the time goes in v1:
time: 46.3 us; the launch traced here: 45.9 us
  blocking collectives  29.1 us (63%)
  Pallas kernels  6.44 us (14%)
  waiting for transfers between devices  3.93 us (8%)
  starting transfers between devices  3.65 us (8%)
  local copies, waits for them, and re-layouts  2.76 us (6%)
    all_to_all x1, blocking collectives, per_device(): got = lax.all_to_all(send, 'gx', split_axis=0, concat_axis=0, tiled=True)  12.5 us
    all_to_all x1, blocking collectives, per_device(): lax.all_to_all(x_interface(got, per), 'gx', split_axis=0, concat_axis=0,...  9.06 us
    all_to_all x1, blocking collectives, per_device(): got = lax.all_to_all(send, 'gy', split_axis=0, concat_axis=0, tiled=True)  7.54 us
    ppermute x1, waiting for transfers between devices, per_device(): after = lax.ppermute(low_edge, 'gy', [(i + 1, i) for i in range(gy - 1)])  3.93 us
    pallas_call x1, Pallas kernels, x_forward(): pl.pallas_call(functools.partial(x_forward_kernel, chips, per, plate), ou...  3.06 us
    unnamed x10, local copies, waits for them, and re-layouts  2.76 us
    ppermute x1, starting transfers between devices, per_device(): before = lax.ppermute(high_edge, 'gy', [(i, i + 1) for i in range(gy - 1)])  2.36 us
    pallas_call x1, Pallas kernels, y_forward(): pl.pallas_call(functools.partial(y_forward_kernel, per), out_shape=[store...  1.58 us
  transfers between devices with their start and end apart: 2, of which 1 were waited for; matrix products, arithmetic and copies ran while one was open for 0% of the time, Pallas kernels for 0%

profile of v1, /device:TPU:0, one launch (start us, length us, event | category | flops | bytes accessed | tf_op | source)
XLA Modules:
  0.0 45.9 jit_solution(10984385716139395100)
XLA Ops:
  0.0 0.0 copy-start
  0.0 1.0 %copy-done = f32[4,64,512]{2,1,0:T(8,128)S(1)} copy-done((f32[4,64,512]{2,1,0:T(8,128)S(1)}, f32[4,64,512]{2,1,0:T(8,128)}, u32[]{:S(2)}) %copy-start) | copy-done | bytes 524312
  1.0 0.0 copy-start.2
  1.0 1.0 %copy-done.2 = f32[4,64,512]{2,1,0:T(8,128)S(1)} copy-done((f32[4,64,512]{2,1,0:T(8,128)S(1)}, f32[4,64,512]{2,1,0:T(8,128)}, u32[]{:S(2)}) %copy-start.2) | copy-done | bytes 524312
  2.1 0.2 shard_map.46
  2.3 2.4 %collective-permute-start = (f32[64,128]{1,0:T(8,128)S(1)}, f32[64,128]{1,0:T(8,128)S(1)}, u32[]{:S(2)}, u32[]{:S(2)}) collective-permute-start(f32[64,128]{1,0:T(8,128)S(1)} %get-tuple-element.18), channel_id=1, source_target_pairs={{0,1},{1,2},{2,3},{4,5},{5,6},{6,7},{8,9},{9,10},{10,11},{12,13},{... | collective-permute-start | bytes 98312 | tf_op jit(solution)/shard_map/ppermute | solution.py:500
  4.7 1.3 %collective-permute-start.1 = (f32[64,128]{1,0:T(8,128)S(1)}, f32[64,128]{1,0:T(8,128)S(1)}, u32[]{:S(2)}, u32[]{:S(2)}) collective-permute-start(f32[64,128]{1,0:T(8,128)S(1)} %get-tuple-element.19), channel_id=1, source_target_pairs={{1,0},{2,1},{3,2},{5,4},{6,5},{7,6},{9,8},{10,9},{11,10},{13,12},{... | collective-permute-start | bytes 98312 | tf_op jit(solution)/shard_map/ppermute | solution.py:501
  6.0 0.0 collective-permute-done.before
  6.0 3.9 %collective-permute-done.1.after = f32[64,128]{1,0:T(8,128)S(1)} collective-permute-done((f32[64,128]{1,0:T(8,128)S(1)}, f32[64,128]{1,0:T(8,128)S(1)}, u32[]{:S(2)}, u32[]{:S(2)}) %collective-permute-start.1) | collective-permute-done | bytes 32800 | tf_op jit(solution)/shard_map/ppermute | solution.py:501
  9.9 0.0 copy-start.3
  9.9 0.0 copy-start.4
  9.9 0.7 %copy-done.3 = s32[64]{0:T(128)S(1)} copy-done((s32[64]{0:T(128)S(1)}, s32[64]{0:T(128)}, u32[]{:S(2)}) %copy-start.3) | copy-done | bytes 280
  10.6 0.0 copy-done.4
  10.6 0.0 copy-start.1
  10.6 3.1 %shard_map.47 = (f32[4,8,4,8,128]{4,3,2,1,0:T(8,128)S(1)}, f32[4,8,4,8,128]{4,3,2,1,0:T(8,128)S(1)}, f32[4,8,4,8,128]{4,3,2,1,0:T(8,128)S(1)}, f32[3,7,16,128]{3,2,1,0:T(8,128)S(1)}, f32[8,16,128]{2,1,0:T(8,128)S(1)}) custom-call(s32[1,64]{1,0:T(1,128)S(1)} %bitcast.2, f32[1,64]{1,0:T(1,128)S(1)} %bitcast.3, f32[4,64,512]{2,1,0:T(8,128)S(1)} %copy-done, ...), custom_call_target="tpu_custom_call" | custom-call | tf_op jit(solution)/shard_map/pallas_call | solution.py:207
  13.6 12.5 %all_to_all.15.got = f32[8,16,128]{2,1,0:T(8,128)S(1)} all-to-all(f32[8,16,128]{2,1,0:T(8,128)S(1)} %get-tuple-element.20), channel_id=1, replica_groups=mesh['gx'=8,'gy'=4] {'gx'}, dimensions={0} | all-to-all | bytes 131072 | tf_op jit(solution)/shard_map/all_to_all | solution.py:505
  26.1 0.1 shard_map.48
  26.2 9.1 %all_to_all.16.got = f32[8,8,128]{2,1,0:T(8,128)S(1)} all-to-all(f32[8,8,128]{2,1,0:T(8,128)S(1)} %shard_map.48), channel_id=1, replica_groups=mesh['gx'=8,'gy'=4] {'gx'}, dimensions={0} | all-to-all | bytes 65536 | tf_op jit(solution)/shard_map/all_to_all | solution.py:506
  35.3 0.0 copy-done.1
  35.3 1.6 %shard_map.49 = (f32[16,2,4,8,128]{4,3,2,1,0:T(8,128)S(1)}, f32[16,2,4,8,128]{4,3,2,1,0:T(8,128)S(1)}, f32[16,2,4,8,128]{4,3,2,1,0:T(8,128)S(1)}, f32[3,3,2,8,12...) custom-call(f32[8,8,128]{2,1,0:T(8,128)S(1)} %all_to_all.16.got, ...), custom_call_target="tpu_custom_call" | custom-call | tf_op jit(solution)/shard_map/pallas_call | solution.py:383
  36.9 7.5 %all_to_all.17.got = f32[4,16,128]{2,1,0:T(8,128)S(1)} all-to-all(f32[4,16,128]{2,1,0:T(8,128)S(1)} %get-tuple-element.25), channel_id=1, replica_groups=mesh['gx'=8,'gy'=4] {'gy'}, dimensions={0} | all-to-all | bytes 65536 | tf_op jit(solution)/shard_map/all_to_all | solution.py:510
  44.4 1.5 %shard_map.50 = f32[4,64,512]{2,1,0:T(8,128)} custom-call(f32[4,16,128]{2,1,0:T(8,128)S(1)} %all_to_all.17.got, f32[3,3,2,8,128]{4,3,2,1,0:T(8,128)S(1)} %get-tuple-element.26.inner, f32[3,7,2,128]{3,2,1,0:T(2,128)S(1)} %get-tuple-element.27.outer, f32[16,2,4,8,128]{4,3,2,1,0:T(8,128)S(1)} %get-tuple-element.28.yw, ...), custom_call_target="tpu_custom_call" | custom-call | tf_op jit(solution)/shard_map/pallas_call | solution.py:483
Async XLA Ops:
  0.0 1.0 %copy-start = (f32[4,64,512]{2,1,0:T(8,128)S(1)}, f32[4,64,512]{2,1,0:T(8,128)}, u32[]{:S(2)}) copy-start(f32[4,64,512]{2,1,0:T(8,128)} %t_ref.5) | copy-start | bytes 1572868
  1.0 1.0 %copy-start.2 = (f32[4,64,512]{2,1,0:T(8,128)S(1)}, f32[4,64,512]{2,1,0:T(8,128)}, u32[]{:S(2)}) copy-start(f32[4,64,512]{2,1,0:T(8,128)} %b_ref.5) | copy-start | bytes 1572868
  2.3 3.7 %collective-permute-start = (f32[64,128]{1,0:T(8,128)S(1)}, f32[64,128]{1,0:T(8,128)S(1)}, u32[]{:S(2)}, u32[]{:S(2)}) collective-permute-start(f32[64,128]{1,0:T(8,128)S(1)} %get-tuple-element.18), channel_id=1, source_target_pairs={{0,1},{1,2},{2,3},{4,5},{5,6},{6,7},{8,9},{9,10},{10,11},{12,13},{... | collective-permute-start | bytes 98312 | tf_op jit(solution)/shard_map/ppermute | solution.py:500
  4.7 5.2 %collective-permute-start.1 = (f32[64,128]{1,0:T(8,128)S(1)}, f32[64,128]{1,0:T(8,128)S(1)}, u32[]{:S(2)}, u32[]{:S(2)}) collective-permute-start(f32[64,128]{1,0:T(8,128)S(1)} %get-tuple-element.19), channel_id=1, source_target_pairs={{1,0},{2,1},{3,2},{5,4},{6,5},{7,6},{9,8},{10,9},{11,10},{13,12},{... | collective-permute-start | bytes 98312 | tf_op jit(solution)/shard_map/ppermute | solution.py:501
  9.9 0.7 %copy-start.3 = (s32[64]{0:T(128)S(1)}, s32[64]{0:T(128)}, u32[]{:S(2)}) copy-start(s32[64]{0:T(128)} %param.6) | copy-start | bytes 772
  9.9 0.7 %copy-start.4 = (f32[64]{0:T(128)S(1)}, f32[64]{0:T(128)}, u32[]{:S(2)}) copy-start(f32[64]{0:T(128)} %param.7) | copy-start | bytes 772
  10.6 24.7 %copy-start.1 = (f32[4,64,512]{2,1,0:T(8,128)S(1)}, f32[4,64,512]{2,1,0:T(8,128)}, u32[]{:S(2)}) copy-start(f32[4,64,512]{2,1,0:T(8,128)} %t_ref.5) | copy-start | bytes 1572868

commit v2 on v0

v2 whole, which is shorter than its diff:
```python
import functools

import jax
import jax.numpy as jnp
from jax import lax
from jax.experimental import pallas as pl
from jax.experimental.pallas import tpu as pltpu
from jax.sharding import PartitionSpec as P

RATE = 2000.0
THERMAL_GROWTH = 0.8
LANES = 128
SUBLANES = 8
Y_PARTS = 4
F32 = jnp.float32
MIB = 1024 * 1024
ANYWHERE = pl.BlockSpec(memory_space=pl.ANY)
IN_HBM = pl.BlockSpec(memory_space=pltpu.HBM)
IN_VMEM = pl.BlockSpec(memory_space=pltpu.VMEM)

R00, R0L, RLL, FIRST, LAST, C0, CL = range(7)
COEFS = (R00, R0L, RLL, C0, CL)


def params(limit=40):
    return pltpu.CompilerParams(vmem_limit_bytes=limit * MIB)


def shape_of(*sizes):
    return jax.ShapeDtypeStruct(sizes, F32)


def half_conduct(base, temperature):
    return base * (0.5 * RATE + (0.5 * RATE * THERMAL_GROWTH) * temperature)


def inverse(x):
    guess = pl.reciprocal(x, approx=True)
    return guess * (2.0 - x * guess)


def join_coefs(a, b):
    face = a[CL] + b[C0]
    inv = face * inverse(1.0 + face * (a[RLL] + b[R00]))
    left = a[R0L] * inv
    right = b[R0L] * inv
    joined = {
        R00: a[R00] - left * a[R0L],
        R0L: left * b[R0L],
        RLL: b[RLL] - right * b[R0L],
        C0: a[C0],
        CL: b[CL],
    }
    return joined, (inv, right, left)


def join_targets(a, b, links):
    inv, right, left = links
    jump = b[0] - a[1]
    return (a[0] + left * jump, b[1] - right * jump), jump * inv


def between(own, right, left, low, high):
    return own + right * high - left * low


def tree(items, join):
    levels = []
    while len(items) > 1:
        pairs = [join(items[i], items[i + 1]) for i in range(0, len(items), 2)]
        items = [p[0] for p in pairs]
        levels.append([p[1] for p in pairs])
    return items[0], levels


def descend(levels, low, high):
    ends = [(low, high)]
    for level in reversed(levels):
        below = []
        for (lo, hi), (own, right, left) in zip(ends, level):
            flux = between(own, right, left, lo, hi)
            below += [(lo, flux), (-flux, hi)]
        ends = below
    return ends


def node_offsets(leaves):
    offsets, at, count = [], 0, leaves // 2
    while count:
        offsets.append((at, count))
        at += count
        count //= 2
    return offsets


def factor(cond, steps, keep):
    here = cond(0)
    c_first = here
    one = jnp.ones_like(here)
    ground, path, first_first = one, one, None
    for k in range(steps - 1):
        following = cond(k + 1)
        face = here + following
        inv = inverse(ground + face)
        w = face * inv
        p = path * inv
        keep(k, w, inv, p)
        step = path * p
        first_first = step if first_first is None else first_first + step
        path = path * w
        ground = 1.0 + w * ground
        here = following
    inv = inverse(ground)
    p = path * inv
    keep(steps - 1, inv, inv, p)
    return {R00: first_first + path * p, R0L: p, RLL: inv, C0: c_first, CL: here}


def eliminate(target, steps, w, inv, p, keep):
    rhs = target(0)
    first = None
    for k in range(steps):
        h = rhs * inv(k)
        keep(k, h)
        step = rhs * p(k)
        first = step if first is None else first + step
        if k < steps - 1:
            rhs = target(k + 1) + w(k) * rhs
    return first, h


def load_kernel(t_hbm, b_hbm, loc_hbm, energy_hbm, t_out, b_out, loc, energy, lo, hi, sems):
    chunks, sheets, rows, _ = t_out.shape
    order = [0, chunks - 1] + list(range(1, chunks - 1))
    copies = {}
    for y in order:
        part = pl.ds(y * LANES, LANES)
        copies[y] = [
            pltpu.make_async_copy(src.at[:, :, part], dst.at[y], sems.at[i, y])
            for i, (src, dst) in enumerate(((t_hbm, t_out), (b_hbm, b_out)))
        ]
        for copy in copies[y]:
            copy.start()
    small = [
        pltpu.make_async_copy(loc_hbm, loc, sems.at[2, 0]),
        pltpu.make_async_copy(energy_hbm, energy, sems.at[2, 1]),
    ]
    for copy in small:
        copy.start()
    lane = lax.broadcasted_iota(jnp.int32, (rows, LANES), 1)
    for y, out, source in ((0, lo, 0), (chunks - 1, hi, LANES - 1)):
        for copy in copies[y]:
            copy.wait()
        packed = jnp.zeros((rows, LANES), F32)
        for z in range(sheets):
            t = t_out[y, z]
            c = half_conduct(b_out[y, z], t)
            packed = jnp.where(lane == z, t[:, source : source + 1], packed)
            packed = jnp.where(lane == sheets + z, c[:, source : source + 1], packed)
        out[...] = packed
    for y in range(1, chunks - 1):
        for copy in copies[y]:
            copy.wait()
    for copy in small:
        copy.wait()


def load(temperature, base, locations, energy):
    sheets, rows, columns = temperature.shape
    chunks = columns // LANES
    field = shape_of(chunks, sheets, rows, LANES)
    return pl.pallas_call(
        load_kernel,
        in_specs=[IN_HBM] * 4,
        out_shape=[
            field,
            field,
            jax.ShapeDtypeStruct(locations.shape, jnp.int32),
            jax.ShapeDtypeStruct(energy.shape, F32),
            shape_of(rows, LANES),
            shape_of(rows, LANES),
        ],
        scratch_shapes=[pltpu.SemaphoreType.DMA((3, max(2, chunks)))],
        compiler_params=params(55),
    )(temperature, base, locations, energy)


def source_plane(loc, energy, rows, columns, plate):
    place = loc[...]
    count = place.shape[1]
    local_x = place // plate - lax.axis_index("gx") * rows
    local_y = place % plate - lax.axis_index("gy") * columns
    in_x = lax.broadcasted_iota(jnp.int32, (rows, count), 0) == local_x
    in_y = lax.broadcasted_iota(jnp.int32, (columns, count), 0) == local_y
    by_y = jnp.where(in_y, 1.0, 0.0).astype(jnp.bfloat16)
    left = energy[...]
    plane = None
    for _ in range(3):
        part = left.astype(jnp.bfloat16).astype(F32)
        left = left - part
        term = lax.dot_general(
            jnp.where(in_x, part, 0.0).astype(jnp.bfloat16),
            by_y,
            (((1,), (1,)), ((), ())),
            preferred_element_type=F32,
        )
        plane = term if plane is None else plane + term
    return plane


def x_factor_kernel(plate, loc, energy, t_ref, b_ref, c_ref, total_ref, w_ref, i_ref, p_ref, links, view, q_s):
    chunks, sheets, rows, _ = t_ref.shape
    lines = chunks * sheets
    steps = rows // SUBLANES
    plane = source_plane(loc, energy, rows, chunks * LANES, plate)

    lane = lax.broadcasted_iota(jnp.int32, (SUBLANES, LANES), 1)
    is_first, is_last = lane == 0, lane == LANES - 1
    for r in range(steps):
        at = slice(r * SUBLANES, (r + 1) * SUBLANES)
        before_t, before_c = None, None
        for z in range(sheets):
            ts = [t_ref[y, z, at, :] for y in range(chunks)]
            cs = [half_conduct(b_ref[y, z, at, :], ts[y]) for y in range(chunks)]
            t_turned = [pltpu.roll(v, LANES - 1, 1) for v in ts]
            c_turned = [pltpu.roll(v, LANES - 1, 1) for v in cs]
            flux = []
            for y in range(chunks):
                if y < chunks - 1:
                    t_next = jnp.where(is_last, t_turned[y + 1], t_turned[y])
                    c_next = jnp.where(is_last, c_turned[y + 1], c_turned[y])
                    flux.append((cs[y] + c_next) * (t_next - ts[y]))
                else:
                    inside = (cs[y] + c_turned[y]) * (t_turned[y] - ts[y])
                    flux.append(jnp.where(is_last, 0.0, inside))
            turned = [pltpu.roll(v, 1, 1) for v in flux]
            for y in range(chunks):
                from_low = jnp.where(is_first, turned[y - 1] if y else 0.0, turned[y])
                total = ts[y] + (flux[y] - from_low)
                if z == 0:
                    total = total + plane[at, y * LANES : (y + 1) * LANES]
                else:
                    across = (before_c[y] + cs[y]) * (ts[y] - before_t[y])
                    total = total - across
                    total_ref[y, z - 1, at, :] += across
                total_ref[y, z, at, :] = total
                c_ref[y, z, at, :] = cs[y]
            before_t, before_c = ts, cs

    group = max(1, 8 // sheets)
    for y in range(0, chunks, group):
        members = [(y + i, z) for i in range(group) for z in range(sheets)]
        at = slice(y * sheets, (y + group) * sheets)

        def cond(k):
            return jnp.stack([c_ref[i, z, pl.ds(k, SUBLANES, stride=steps), :] for i, z in members], 0)

        def keep(k, w, inv, p):
            w_ref[k, at] = w
            i_ref[k, at] = inv
            p_ref[k, at] = p

        block = factor(cond, steps, keep)
        for n, q in enumerate(COEFS):
            for i in range(len(members)):
                first = (y * sheets + i) * SUBLANES
                q_s[n, first : first + SUBLANES, :] = block[q][i]

    segments = [
        {q: q_s[n, pl.ds(s, lines, stride=SUBLANES), :] for n, q in enumerate(COEFS)}
        for s in range(SUBLANES)
    ]
    whole, levels = tree(segments, join_coefs)
    for (offset, _), level in zip(node_offsets(SUBLANES), levels):
        for n, values in enumerate(level):
            for i in range(3):
                links[offset + n, i] = values[i]
    for n, q in enumerate(COEFS):
        view[n] = whole[q]


def x_factor(loc, energy, t, b, plate):
    chunks, sheets, rows, _ = t.shape
    lines = chunks * sheets
    steps = rows // SUBLANES
    field = shape_of(*t.shape)
    stored = shape_of(steps, lines, SUBLANES, LANES)
    return pl.pallas_call(
        functools.partial(x_factor_kernel, plate),
        out_shape=[
            field,
            field,
            stored,
            stored,
            stored,
            shape_of(SUBLANES - 1, 3, lines, LANES),
            shape_of(len(COEFS), lines, LANES),
        ],
        scratch_shapes=[pltpu.VMEM((len(COEFS), lines * SUBLANES, LANES), F32)],
        compiler_params=params(),
        cost_estimate=pl.CostEstimate(flops=40 * t.size, bytes_accessed=28 * t.size, transcendentals=0),
    )(loc, energy, t, b)


def x_target_kernel(t_ref, c_ref, total_ref, before, after, w_ref, i_ref, p_ref, links, view, h_ref, own, send, e_s, q_s):
    chunks, sheets, rows, _ = t_ref.shape
    lines = chunks * sheets
    steps = rows // SUBLANES

    lane = lax.broadcasted_iota(jnp.int32, (rows, LANES), 1)
    for y, halo, edge, place in ((0, before, 0, 0), (chunks - 1, after, LANES - 1, 1)):
        for z in range(sheets):
            c_next = halo[:, sheets + z : sheets + z + 1]
            t_next = halo[:, z : z + 1]
            face = jnp.where(c_next > 0.0, c_ref[y, z] + c_next, 0.0)
            flux = jnp.where(lane == edge, face * (t_next - t_ref[y, z]), 0.0)
            base = total_ref[y, z] if place == 0 or chunks > 1 else e_s[0, z]
            e_s[place, z] = base + flux

    def field(y, z):
        if y == chunks - 1:
            return e_s.at[1, z]
        return e_s.at[0, z] if y == 0 else total_ref.at[y, z]

    group = max(1, 8 // sheets)
    for y in range(0, chunks, group):
        members = [(y + i, z) for i in range(group) for z in range(sheets)]
        at = slice(y * sheets, (y + group) * sheets)

        def target(k):
            return jnp.stack([field(i, z)[pl.ds(k, SUBLANES, stride=steps), :] for i, z in members], 0)

        def keep(k, h):
            h_ref[k, at] = h

        ends = eliminate(
            target, steps, lambda k: w_ref[k, at], lambda k: i_ref[k, at], lambda k: p_ref[k, at], keep
        )
        for q in range(2):
            for i in range(len(members)):
                first = (y * sheets + i) * SUBLANES
                q_s[q, first : first + SUBLANES, :] = ends[q][i]
    items = [
        tuple(q_s[q, pl.ds(s, lines, stride=SUBLANES), :] for q in range(2)) for s in range(SUBLANES)
    ]
    for offset, count in node_offsets(SUBLANES):
        joined = []
        for n in range(count):
            ties = tuple(links[offset + n, i] for i in range(3))
            both, flux = join_targets(items[2 * n], items[2 * n + 1], ties)
            own[offset + n] = flux
            joined.append(both)
        items = joined
    for n, q in enumerate(COEFS):
        send[q] = view[n]
    send[FIRST], send[LAST] = items[0]


def x_target(t, c, total, before, after, w, inv, p, links, view):
    chunks, sheets, rows, _ = t.shape
    lines = chunks * sheets
    steps = rows // SUBLANES
    return pl.pallas_call(
        x_target_kernel,
        out_shape=[
            shape_of(steps, lines, SUBLANES, LANES),
            shape_of(SUBLANES - 1, lines, LANES),
            shape_of(7, lines, LANES),
        ],
        scratch_shapes=[
            pltpu.VMEM((2, sheets, rows, LANES), F32),
            pltpu.VMEM((2, lines * SUBLANES, LANES), F32),
        ],
        compiler_params=params(),
    )(t, c, total, before, after, w, inv, p, links, view)


def stages_of(axis):
    return lax.axis_size(axis).bit_length() - 1


def swap(value, axis, stage):
    count = lax.axis_size(axis)
    return lax.ppermute(value, axis, [(i, i ^ (1 << stage)) for i in range(count)])


def on_right(axis, stage):
    return (lax.axis_index(axis) >> stage) % 2 == 1


def toward(right, block):
    return (
        jnp.where(right, block[R00], block[RLL]),
        jnp.where(right, block[FIRST], block[LAST]),
        jnp.where(right, block[C0], block[CL]),
    )


def join_kernel(axis, stage, last, own, got, *refs):
    send, links = refs[-2:]
    right = on_right(axis, stage)
    a = {q: jnp.where(right, got[q], own[q]) for q in range(7)}
    b = {q: jnp.where(right, own[q], got[q]) for q in range(7)}
    joined, ties = join_coefs(a, b)
    (joined[FIRST], joined[LAST]), flux = join_targets((a[FIRST], a[LAST]), (b[FIRST], b[LAST]), ties)
    links[0], links[1], links[2] = flux, ties[1], ties[2]
    if last:
        for n, value in enumerate(toward(on_right(axis, stage + 1), joined)):
            send[n] = value
    else:
        for q in range(7):
            send[q] = joined[q]


def join_stage(own, got, axis, stage, last, after):
    lines = own.shape[1]
    return pl.pallas_call(
        functools.partial(join_kernel, axis, stage, last),
        in_specs=[IN_VMEM] * 2 + [ANYWHERE] * len(after),
        out_shape=[shape_of(3 if last else 7, lines, LANES), shape_of(3, lines, LANES)],
        compiler_params=params(),
    )(own, got, *after)


def gather_line(view, axis, meanwhile=()):
    stages = stages_of(axis)
    links = []
    for stage in range(stages - 1):
        got = swap(view, axis, stage)
        view, tie = join_stage(view, got, axis, stage, stage == stages - 2, meanwhile[stage : stage + 1])
        links.append(tie)
    return view, swap(view, axis, stages - 1), links


def block_ends(axis, own, got, links):
    top = len(links)
    right = on_right(axis, top)
    face = own[2] + got[2]
    jump = jnp.where(right, own[1] - got[1], got[1] - own[1])
    flux = jump * face * inverse(1.0 + face * (own[0] + got[0]))
    low = jnp.where(right, -flux, 0.0)
    high = jnp.where(right, 0.0, flux)
    for stage in range(top - 1, -1, -1):
        tie = links[stage]
        right = on_right(axis, stage)
        flux = between(tie[0], tie[1], tie[2], low, high)
        low, high = jnp.where(right, -flux, low), jnp.where(right, high, flux)
    return low, high


def y_factor_kernel(c_ref, after, w_ref, i_ref, p_ref, inner, outer, view, c_s, q_s):
    chunks, sheets, rows, _ = c_ref.shape
    each = LANES // rows
    pairs = sheets // each
    span = chunks * LANES // SUBLANES
    steps = span // Y_PARTS
    for m in range(pairs):
        for y in range(chunks):
            block = jnp.concatenate([c_ref[y, m * each + i] for i in range(each)], 0)
            c_s[m, y * LANES : (y + 1) * LANES, :] = block.T

    members = [(j, m) for j in range(Y_PARTS) for m in range(pairs)]

    def cond(k):
        return jnp.stack([c_s[m, pl.ds(j * steps + k, SUBLANES, stride=span), :] for j, m in members], 0)

    def keep(k, w, inv, p):
        w_ref[k] = w
        i_ref[k] = inv
        p_ref[k] = p

    block = factor(cond, steps, keep)
    parts = [{q: block[q][j * pairs : (j + 1) * pairs] for q in COEFS} for j in range(Y_PARTS)]
    whole, levels = tree(parts, join_coefs)
    for (offset, _), level in zip(node_offsets(Y_PARTS), levels):
        for n, values in enumerate(level):
            for i in range(3):
                inner[offset + n, i] = values[i]
    for n, q in enumerate(COEFS):
        for m in range(pairs):
            q_s[n, m * SUBLANES : (m + 1) * SUBLANES, :] = whole[q][m]
    segments = [
        {q: q_s[n, pl.ds(s, pairs, stride=SUBLANES), :] for n, q in enumerate(COEFS)}
        for s in range(SUBLANES)
    ]
    whole, levels = tree(segments, join_coefs)
    for (offset, _), level in zip(node_offsets(SUBLANES), levels):
        for n, values in enumerate(level):
            for i in range(3):
                outer[offset + n, i] = values[i]
    for n, q in enumerate(COEFS):
        view[n] = whole[q]


def y_factor(c, after):
    chunks, sheets, rows, _ = c.shape
    pairs = sheets * rows // LANES
    steps = chunks * LANES // SUBLANES // Y_PARTS
    stored = shape_of(steps, Y_PARTS * pairs, SUBLANES, LANES)
    return pl.pallas_call(
        y_factor_kernel,
        in_specs=[IN_VMEM, ANYWHERE],
        out_shape=[
            stored,
            stored,
            stored,
            shape_of(Y_PARTS - 1, 3, pairs, SUBLANES, LANES),
            shape_of(SUBLANES - 1, 3, pairs, LANES),
            shape_of(len(COEFS), pairs, LANES),
        ],
        scratch_shapes=[
            pltpu.VMEM((pairs, chunks * LANES, LANES), F32),
            pltpu.VMEM((len(COEFS), pairs * SUBLANES, LANES), F32),
        ],
        compiler_params=params(),
        cost_estimate=pl.CostEstimate(flops=20 * c.size, bytes_accessed=16 * c.size, transcendentals=0),
    )(c, after)


def z_factor_kernel(c_ref, after, w_ref, i_ref):
    sheets = c_ref.shape[1]
    ground = 1.0
    for z in range(sheets - 1):
        face = c_ref[:, z] + c_ref[:, z + 1]
        inv = inverse(ground + face)
        w = face * inv
        i_ref[z] = inv
        w_ref[z] = w
        ground = 1.0 + w * ground
    i_ref[sheets - 1] = inverse(ground)


def z_factor(c, after):
    chunks, sheets, rows, _ = c.shape
    return pl.pallas_call(
        z_factor_kernel,
        in_specs=[IN_VMEM, ANYWHERE],
        out_shape=[
            shape_of(sheets - 1, chunks, rows, LANES),
            shape_of(sheets, chunks, rows, LANES),
        ],
        compiler_params=params(),
        cost_estimate=pl.CostEstimate(flops=10 * c.size, bytes_accessed=12 * c.size, transcendentals=0),
    )(c, after)


def y_target_kernel(stages, *refs):
    own, got = refs[:2]
    ties = refs[2 : 1 + stages]
    xw, xh, xp, x_links, x_own, t_ref, yw, yi, yp, inner, outer, view = refs[1 + stages : 13 + stages]
    h_ref, inner_own, outer_own, send = refs[13 + stages : 17 + stages]
    f_s, g_s, y_s, q_s = refs[17 + stages :]
    chunks, sheets, rows, _ = t_ref.shape
    lines = chunks * sheets
    x_steps = rows // SUBLANES

    low, high = block_ends("gx", own, got, ties)
    levels = [
        [(x_own[o + n], x_links[o + n, 1], x_links[o + n, 2]) for n in range(count)]
        for o, count in node_offsets(SUBLANES)
    ]
    for s, ends in enumerate(descend(levels, low, high)):
        for i in range(2):
            f_s[i, pl.ds(s, lines, stride=SUBLANES), :] = ends[i]
    group = max(1, 8 // sheets)
    for y in range(0, chunks, group):
        members = [(y + i, z) for i in range(group) for z in range(sheets)]
        at = slice(y * sheets, (y + group) * sheets)
        low, value = (
            jnp.stack(
                [
                    f_s[i, (y * sheets + n) * SUBLANES : (y * sheets + n + 1) * SUBLANES, :]
                    for n in range(len(members))
                ],
                0,
            )
            for i in range(2)
        )
        for k in range(x_steps - 1, -1, -1):
            value = xw[k, at] * value + (xh[k, at] + xp[k, at] * low)
            for n, (i, z) in enumerate(members):
                g_s[i, z, pl.ds(k, SUBLANES, stride=x_steps), :] = value[n]

    each = LANES // rows
    pairs = sheets // each
    span = chunks * LANES // SUBLANES
    steps = span // Y_PARTS
    for m in range(pairs):
        for y in range(chunks):
            block = jnp.concatenate(
                [g_s[y, m * each + i] - t_ref[y, m * each + i] for i in range(each)], 0
            )
            y_s[m, y * LANES : (y + 1) * LANES, :] = block.T
    members = [(j, m) for j in range(Y_PARTS) for m in range(pairs)]

    def target(k):
        return jnp.stack([y_s[m, pl.ds(j * steps + k, SUBLANES, stride=span), :] for j, m in members], 0)

    def keep(k, h):
        h_ref[k] = h

    ends = eliminate(target, steps, lambda k: yw[k], lambda k: yi[k], lambda k: yp[k], keep)
    items = [tuple(v[j * pairs : (j + 1) * pairs] for v in ends) for j in range(Y_PARTS)]
    for offset, count in node_offsets(Y_PARTS):
        joined = []
        for n in range(count):
            tie = tuple(inner[offset + n, i] for i in range(3))
            both, flux = join_targets(items[2 * n], items[2 * n + 1], tie)
            inner_own[offset + n] = flux
            joined.append(both)
        items = joined
    for q in range(2):
        for m in range(pairs):
            q_s[q, m * SUBLANES : (m + 1) * SUBLANES, :] = items[0][q][m]
    items = [
        tuple(q_s[q, pl.ds(s, pairs, stride=SUBLANES), :] for q in range(2)) for s in range(SUBLANES)
    ]
    for offset, count in node_offsets(SUBLANES):
        joined = []
        for n in range(count):
            tie = tuple(outer[offset + n, i] for i in range(3))
            both, flux = join_targets(items[2 * n], items[2 * n + 1], tie)
            outer_own[offset + n] = flux
            joined.append(both)
        items = joined
    for n, q in enumerate(COEFS):
        send[q] = view[n]
    send[FIRST], send[LAST] = items[0]


def y_target(own, got, ties, xw, xh, xp, x_links, x_own, t, yw, yi, yp, inner, outer, view):
    chunks, sheets, rows, _ = t.shape
    lines = chunks * sheets
    pairs = sheets * rows // LANES
    return pl.pallas_call(
        functools.partial(y_target_kernel, len(ties) + 1),
        out_shape=[
            shape_of(*yw.shape),
            shape_of(Y_PARTS - 1, pairs, SUBLANES, LANES),
            shape_of(SUBLANES - 1, pairs, LANES),
            shape_of(7, pairs, LANES),
        ],
        scratch_shapes=[
            pltpu.VMEM((2, lines * SUBLANES, LANES), F32),
            pltpu.VMEM((chunks, sheets, rows, LANES), F32),
            pltpu.VMEM((pairs, chunks * LANES, LANES), F32),
            pltpu.VMEM((2, pairs * SUBLANES, LANES), F32),
        ],
        compiler_params=params(),
    )(own, got, *ties, xw, xh, xp, x_links, x_own, t, yw, yi, yp, inner, outer, view)


def finish_kernel(stages, *refs):
    own, got = refs[:2]
    ties = refs[2 : 1 + stages]
    yw, yh, yp, inner, inner_own, outer, outer_own, zw, zi, t_ref = refs[1 + stages : 11 + stages]
    out, e_s, u_s, o_s, sems = refs[11 + stages :]
    chunks, sheets, rows, _ = t_ref.shape
    each = LANES // rows
    pairs = sheets // each
    steps = yw.shape[0]
    span = chunks * LANES // SUBLANES

    low, high = block_ends("gy", own, got, ties)
    levels = [
        [(outer_own[o + n], outer[o + n, 1], outer[o + n, 2]) for n in range(count)]
        for o, count in node_offsets(SUBLANES)
    ]
    for s, ends in enumerate(descend(levels, low, high)):
        for i in range(2):
            e_s[i, pl.ds(s, pairs, stride=SUBLANES), :] = ends[i]
    low, high = (
        jnp.stack([e_s[i, m * SUBLANES : (m + 1) * SUBLANES, :] for m in range(pairs)], 0)
        for i in range(2)
    )
    levels = [
        [(inner_own[o + n], inner[o + n, 1], inner[o + n, 2]) for n in range(count)]
        for o, count in node_offsets(Y_PARTS)
    ]
    ends = descend(levels, low, high)
    low = jnp.concatenate([e[0] for e in ends], 0)
    value = jnp.concatenate([e[1] for e in ends], 0)
    members = [(j, m) for j in range(Y_PARTS) for m in range(pairs)]
    for k in range(steps - 1, -1, -1):
        value = yw[k] * value + (yh[k] + yp[k] * low)
        for n, (j, m) in enumerate(members):
            u_s[m, pl.ds(j * steps + k, SUBLANES, stride=span), :] = value[n]

    copies = []
    for y in range(chunks):
        part = slice(y * LANES, (y + 1) * LANES)
        turned = [u_s[m, part, :].T for m in range(pairs)]
        rhs, kept = None, []
        for z in range(sheets):
            first = (z % each) * rows
            own_rhs = turned[z // each][first : first + rows, :]
            rhs = own_rhs if z == 0 else own_rhs + zw[z - 1, y] * rhs
            kept.append(rhs * zi[z, y])
        value = kept[-1]
        o_s[y, sheets - 1] = t_ref[y, sheets - 1] + value
        for z in range(sheets - 2, -1, -1):
            value = zw[z, y] * value + kept[z]
            o_s[y, z] = t_ref[y, z] + value
        copy = pltpu.make_async_copy(o_s.at[y], out.at[:, :, pl.ds(y * LANES, LANES)], sems.at[y])
        copy.start()
        copies.append(copy)
    for copy in copies:
        copy.wait()


def finish(own, got, ties, yw, yh, yp, inner, inner_own, outer, outer_own, zw, zi, t):
    chunks, sheets, rows, _ = t.shape
    pairs = sheets * rows // LANES
    return pl.pallas_call(
        functools.partial(finish_kernel, len(ties) + 1),
        out_shape=shape_of(sheets, rows, chunks * LANES),
        out_specs=ANYWHERE,
        scratch_shapes=[
            pltpu.VMEM((2, pairs * SUBLANES, LANES), F32),
            pltpu.VMEM((pairs, chunks * LANES, LANES), F32),
            pltpu.VMEM(t.shape, F32),
            pltpu.SemaphoreType.DMA((chunks,)),
        ],
        compiler_params=params(),
    )(own, got, *ties, yw, yh, yp, inner, inner_own, outer, outer_own, zw, zi, t)


def per_device(temperature, base, locations, energy):
    columns = temperature.shape[2]
    gy = lax.axis_size("gy")
    t, b, loc, heat, low_edge, high_edge = load(temperature, base, locations[None], energy[None])
    before = lax.ppermute(high_edge, "gy", [(i, i + 1) for i in range(gy - 1)])
    after = lax.ppermute(low_edge, "gy", [(i + 1, i) for i in range(gy - 1)])
    c, total, xw, xi, xp, x_links, x_view = x_factor(loc, heat, t, b, columns * gy)
    xh, x_own, view = x_target(t, c, total, before, after, xw, xi, xp, x_links, x_view)
    yw, yi, yp, inner, outer, y_view = y_factor(c, view)
    zw, zi = z_factor(c, view)
    own, got, ties = gather_line(view, "gx", (y_view, zw))
    yh, inner_own, outer_own, view = y_target(
        own, got, ties, xw, xh, xp, x_links, x_own, t, yw, yi, yp, inner, outer, y_view
    )
    own, got, ties = gather_line(view, "gy")
    return finish(own, got, ties, yw, yh, yp, inner, inner_own, outer, outer_own, zw, zi, t)


def solution(mesh):
    in_specs = (P(None, "gx", "gy"), P(None, "gx", "gy"), P(), P())
    out_specs = P(None, "gx", "gy")
    return jax.shard_map(
        per_device, mesh=mesh, in_specs=in_specs, out_specs=out_specs, check_vma=False
    )
```

time: 135 us -> 34.9 us (0.26)
  blocking collectives: 45.4 us -> 0 us
  other arithmetic: 33.9 us -> 0 us
  local copies, waits for them, and re-layouts: 23.7 us -> 2.75 us
  Pallas kernels: 0 us -> 8.13 us
  starting transfers between devices: 23.9 us -> 15.8 us
    all_gather x1 -> x0, blocking collectives: 34.1 us -> none  [x_interface(): whole = lax.all_gather(coefs, 'gx', axis=2, tiled=True)]
    div x30 -> x0, other arithmetic: 21.4 us -> none  [the longest x13 13.4 us: reduce_lines(): -upper_band * upper_next / pivot]
    all_to_all x2 -> x0, starting transfers between devices: 11.5 us -> none  [the longest x1 7.35 us: per_device(): lax.all_to_all(thermal_coefficient_of, 'gy', split_axis=1, concat_axis=2,...]
    all_to_all x1 -> x0, blocking collectives: 11.2 us -> none  [per_device(): lax.all_to_all(solved_lines, 'gy', split_axis=2, concat_axis=1, tiled=True)]
    unnamed x17 -> x10, local copies, waits for them, and re-layouts: 11.1 us -> 2.75 us
    pallas_call x0 -> x10, Pallas kernels: none -> 8.13 us  [the longest x1 2.38 us: load(): pl.pallas_call(load_kernel, in_specs=[IN_HBM] * 4, out_shape=[field, fiel...]
    ppermute x5 -> x7, waiting for transfers between devices: 0.01 us -> 7.79 us  [the longest x5 7.78 us: swap(): lax.ppermute(value, axis, [(i, i ^ 1 << stage) for i in range(count)])]
    all_to_all x2 -> x0, waiting for transfers between devices: 7.1 us -> none  [the longest x1 7.09 us: per_device(): lax.all_to_all(first_pass, 'gy', split_axis=1, concat_axis=2, tiled=True)]
  transfers between devices with their start and end apart: 7 -> 7, of which waited for: 1 -> 5; matrix products, arithmetic and copies ran while one was open for 7% -> 0% of each run, Pallas kernels for 0% -> 9%
where the time goes in v2:
time: 34.9 us; the launch traced here: 34.6 us
  starting transfers between devices  15.8 us (45%)
  Pallas kernels  8.13 us (23%)
  waiting for transfers between devices  7.79 us (22%)
  local copies, waits for them, and re-layouts  2.75 us (8%)
    ppermute x5, starting transfers between devices, swap(): lax.ppermute(value, axis, [(i, i ^ 1 << stage) for i in range(count)])  12.2 us
    ppermute x5, waiting for transfers between devices, swap(): lax.ppermute(value, axis, [(i, i ^ 1 << stage) for i in range(count)])  7.78 us
    unnamed x10, local copies, waits for them, and re-layouts  2.75 us
    pallas_call x1, Pallas kernels, load(): pl.pallas_call(load_kernel, in_specs=[IN_HBM] * 4, out_shape=[field, fiel...  2.38 us
    ppermute x1, starting transfers between devices, per_device(): before = lax.ppermute(high_edge, 'gy', [(i, i + 1) for i in range(gy - 1)])  2.36 us
    pallas_call x1, Pallas kernels, x_factor(): pl.pallas_call(functools.partial(x_factor_kernel, plate), out_shape=[fiel...  2.04 us
    pallas_call x1, Pallas kernels, finish(): pl.pallas_call(functools.partial(finish_kernel, len(ties) + 1), out_shape...  1.34 us
    ppermute x1, starting transfers between devices, per_device(): after = lax.ppermute(low_edge, 'gy', [(i + 1, i) for i in range(gy - 1)])  1.29 us
  transfers between devices with their start and end apart: 7, of which 5 were waited for; matrix products, arithmetic and copies ran while one was open for 0% of the time, Pallas kernels for 9%

profile of v2, /device:TPU:0, one launch (start us, length us, event | category | flops | bytes accessed | tf_op | source)
XLA Modules:
  0.0 34.6 jit_solution(14282232409604409250)
XLA Ops:
  0.0 2.4 %shard_map.46 = (f32[4,4,64,128]{3,2,1,0:T(8,128)}, f32[4,4,64,128]{3,2,1,0:T(8,128)}, s32[1,64]{1,0:T(1,128)}, f32[1,64]{1,0:T(1,128)}, f32[64,128]{1,0:T(8,128)}, /*index=5*/f32[64,128]{1,0:T(8,128)}) custom-call(f32[4,64,512]{2,1,0:T(8,128)} %t_hbm.1, f32[4,64,512]{2,1,0:T(8,128)} %b_hbm.1, s32[1,64]{1,0:T(1,128)} %bitcast.2, f32[1,64]{1,0:T(1,128)} %bitcast.3), custom_call_target="tpu_custom_call" | custom-call | tf_op jit(solution)/shard_map/pallas_call | solution.py:172
  2.4 2.4 %collective-permute-start = (f32[64,128]{1,0:T(8,128)}, f32[64,128]{1,0:T(8,128)S(1)}, u32[]{:S(2)}, u32[]{:S(2)}) collective-permute-start(f32[64,128]{1,0:T(8,128)} %get-tuple-element.45), channel_id=1, source_target_pairs={{0,1},{1,2},{2,3},{4,5},{5,6},{6,7},{8,9},{9,10},{10,11},{12,13},{... | collective-permute-start | bytes 98312 | tf_op jit(solution)/shard_map/ppermute | solution.py:732
  4.8 1.3 %collective-permute-start.1 = (f32[64,128]{1,0:T(8,128)}, f32[64,128]{1,0:T(8,128)S(1)}, u32[]{:S(2)}, u32[]{:S(2)}) collective-permute-start(f32[64,128]{1,0:T(8,128)} %get-tuple-element.46), channel_id=1, source_target_pairs={{1,0},{2,1},{3,2},{5,4},{6,5},{7,6},{9,8},{10,9},{11,10},{13,12},{... | collective-permute-start | bytes 98312 | tf_op jit(solution)/shard_map/ppermute | solution.py:733
  6.1 0.0 copy-start.3
  6.1 0.0 copy-start.4
  6.1 0.6 %copy-done.3 = s32[1,64]{1,0:T(1,128)S(1)} copy-done((s32[1,64]{1,0:T(1,128)S(1)}, s32[1,64]{1,0:T(1,128)}, u32[]{:S(2)}) %copy-start.3) | copy-done | bytes 280
  6.7 0.0 copy-done.4
  6.7 0.0 copy-start
  6.7 1.0 %copy-done = f32[4,4,64,128]{3,2,1,0:T(8,128)S(1)} copy-done((f32[4,4,64,128]{3,2,1,0:T(8,128)S(1)}, f32[4,4,64,128]{3,2,1,0:T(8,128)}, u32[]{:S(2)}) %copy-start) | copy-done | bytes 524312
  7.8 0.0 copy-start.2
  7.8 1.0 %copy-done.2 = f32[4,4,64,128]{3,2,1,0:T(8,128)S(1)} copy-done((f32[4,4,64,128]{3,2,1,0:T(8,128)S(1)}, f32[4,4,64,128]{3,2,1,0:T(8,128)}, u32[]{:S(2)}) %copy-start.2) | copy-done | bytes 524312
  8.8 2.0 %shard_map.47 = (f32[4,4,64,128]{3,2,1,0:T(8,128)S(1)}, f32[4,4,64,128]{3,2,1,0:T(8,128)S(1)}, f32[8,16,8,128]{3,2,1,0:T(8,128)S(1)}, f32[8,16,8,128]{3,2,1,0:T(...) custom-call(s32[1,64]{1,0:T(1,128)S(1)} %copy-done.3, ...), custom_call_target="tpu_custom_call" | custom-call | flops 5242880 | bytes 3670016 | tf_op jit(solution)/shard_map/pallas_call | solution.py:288
  10.9 0.0 collective-permute-done.before
  10.9 0.0 collective-permute-done.1.after
  10.9 0.4 %shard_map.48 = (f32[8,16,8,128]{3,2,1,0:T(8,128)S(1)}, f32[7,16,128]{2,1,0:T(8,128)S(1)}, f32[7,16,128]{2,1,0:T(8,128)S(1)}) custom-call(f32[4,4,64,128]{3,2,1,0:T(8,128)S(1)} %copy-done, f32[4,4,64,128]{3,2,1,0:T(8,128)S(1)} %get-tuple-element.43.c_ref, f32[4,4,64,128]{3,2,1,0:T(8,128)S(1)} %get-tuple-element.44.total_ref, ...), custom_call_target="tpu_custom_call" | custom-call | tf_op jit(solution)/shard_map/pallas_call | solution.py:363
  11.3 2.4 %collective-permute-start.2 = (f32[7,16,128]{2,1,0:T(8,128)S(1)}, f32[7,16,128]{2,1,0:T(8,128)S(1)}, u32[]{:S(2)}, u32[]{:S(2)}) collective-permute-start(f32[7,16,128]{2,1,0:T(8,128)S(1)} %get-tuple-element.52.after.own), channel_id=1, source_target_pairs={{0,4},{4,0},{8,12},{12,8},{16,20},{20,16},{24,28},{28,24},{1,5},{5... | collective-permute-start | bytes 172040 | tf_op jit(solution)/shard_map/ppermute | solution.py:384
  13.7 0.9 %shard_map.49 = (f32[16,8,8,128]{3,2,1,0:T(8,128)S(1)}, f32[16,8,8,128]{3,2,1,0:T(8,128)S(1)}, f32[16,8,8,128]{3,2,1,0:T(8,128)S(1)}, f32[3,3,2,8,128]{4,3,2,1,0...) custom-call(f32[4,4,64,128]{3,2,1,0:T(8,128)S(1)} %get-tuple-element.43.c_ref, ...), custom_call_target="tpu_custom_call" | custom-call | flops 2621440 | bytes 2097152 | tf_op jit(solution)/shard_map/pallas_call | solution.py:500
  14.6 1.2 %collective-permute-done.2.got = f32[7,16,128]{2,1,0:T(8,128)S(1)} collective-permute-done((f32[7,16,128]{2,1,0:T(8,128)S(1)}, f32[7,16,128]{2,1,0:T(8,128)S(1)}, u32[]{:S(2)}, u32[]{:S(2)}) %collective-permute-start.2) | collective-permute-done | bytes 57376 | tf_op jit(solution)/shard_map/ppermute | solution.py:384
  15.9 0.0 copy-start.1
  15.9 2.2 %collective-permute-start.3 = (f32[7,16,128]{2,1,0:T(8,128)S(1)}, f32[7,16,128]{2,1,0:T(8,128)S(1)}, u32[]{:S(2)}, u32[]{:S(2)}) collective-permute-start(f32[7,16,128]{2,1,0:T(8,128)S(1)} %get-tuple-element.54.own), channel_id=1, source_target_pairs={{0,8},{4,12},{8,0},{12,4},{16,24},{20,28},{24,16},{28,20},{1,9},{5... | collective-permute-start | bytes 172040 | tf_op jit(solution)/shard_map/ppermute | solution.py:384
  18.1 0.2 shard_map.51
  18.2 2.0 %collective-permute-done.3.got = f32[7,16,128]{2,1,0:T(8,128)S(1)} collective-permute-done((f32[7,16,128]{2,1,0:T(8,128)S(1)}, f32[7,16,128]{2,1,0:T(8,128)S(1)}, u32[]{:S(2)}, u32[]{:S(2)}) %collective-permute-start.3) | collective-permute-done | bytes 57376 | tf_op jit(solution)/shard_map/ppermute | solution.py:384
  20.3 3.4 %collective-permute-start.4 = (f32[3,16,128]{2,1,0:T(8,128)S(1)}, f32[3,16,128]{2,1,0:T(8,128)S(1)}, u32[]{:S(2)}, u32[]{:S(2)}) collective-permute-start(f32[3,16,128]{2,1,0:T(8,128)S(1)} %get-tuple-element.56.refs_0_), channel_id=1, source_target_pairs={{0,16},{4,20},{8,24},{12,28},{16,0},{20,4},{24,8},{28,12},{1,17},{... | collective-permute-start | bytes 73736 | tf_op jit(solution)/shard_map/ppermute | solution.py:384
  23.7 1.8 %collective-permute-done.4.refs_1_ = f32[3,16,128]{2,1,0:T(8,128)S(1)} collective-permute-done((f32[3,16,128]{2,1,0:T(8,128)S(1)}, f32[3,16,128]{2,1,0:T(8,128)S(1)}, u32[]{:S(2)}, u32[]{:S(2)}) %collective-permute-start.4) | collective-permute-done | bytes 24608 | tf_op jit(solution)/shard_map/ppermute | solution.py:384
  25.5 0.0 copy-done.1
  25.5 0.8 %shard_map.53 = (f32[16,8,8,128]{3,2,1,0:T(8,128)S(1)}, f32[3,2,8,128]{3,2,1,0:T(8,128)S(1)}, f32[7,2,128]{2,1,0:T(2,128)S(1)}, f32[7,2,128]{2,1,0:T(2,128)S(1)}) custom-call(f32[3,16,128]{2,1,0:T(8,128)S(1)} %get-tuple-element.56.refs_0_, f32[3,16,128]{2,1,0:T(8,128)S(1)} %collective-permute-done.4.refs_1_, f32[3,16,128]{2,1,0:T(8,128)S(1)} %get-tuple-element.57.refs_2_, ...), custom_call_target="tpu_custom_call" | custom-call | tf_op jit(solution)/shard_map/pallas_call | solution.py:635
  26.3 0.1 collective-permute-start.5
  26.4 1.2 %collective-permute-done.5.got = f32[7,2,128]{2,1,0:T(2,128)S(1)} collective-permute-done((f32[7,2,128]{2,1,0:T(2,128)S(1)}, f32[7,2,128]{2,1,0:T(2,128)S(1)}, u32[]{:S(2)}, u32[]{:S(2)}) %collective-permute-start.5) | collective-permute-done | bytes 7200 | tf_op jit(solution)/shard_map/ppermute | solution.py:384
  27.5 4.1 %collective-permute-start.6 = (f32[3,2,128]{2,1,0:T(2,128)S(1)}, f32[3,2,128]{2,1,0:T(2,128)S(1)}, u32[]{:S(2)}, u32[]{:S(2)}) collective-permute-start(f32[3,2,128]{2,1,0:T(2,128)S(1)} %get-tuple-element.67.refs_0_), channel_id=1, source_target_pairs={{0,2},{1,3},{2,0},{3,1},{4,6},{5,7},{6,4},{7,5},{8,10},{9,11},{10,... | collective-permute-start | bytes 9224 | tf_op jit(solution)/shard_map/ppermute | solution.py:384
  31.7 1.6 %collective-permute-done.6.refs_1_ = f32[3,2,128]{2,1,0:T(2,128)S(1)} collective-permute-done((f32[3,2,128]{2,1,0:T(2,128)S(1)}, f32[3,2,128]{2,1,0:T(2,128)S(1)}, u32[]{:S(2)}, u32[]{:S(2)}) %collective-permute-start.6) | collective-permute-done | bytes 3104 | tf_op jit(solution)/shard_map/ppermute | solution.py:384
  33.3 1.3 %shard_map.55 = f32[4,64,512]{2,1,0:T(8,128)} custom-call(f32[3,2,128]{2,1,0:T(2,128)S(1)} %get-tuple-element.67.refs_0_, f32[3,2,128]{2,1,0:T(2,128)S(1)} %collective-permute-done.6.refs_1_, f32[3,2,128]{2,1,0:T(2,128)S(1)} %get-tuple-element.68.refs_2_, f32[16,8,8,128]{3,2,1,0:T(8,128)S(1)} %get-tuple-element.61.refs_10_.refs_3_, ...), custom_call_target="tpu_custom_call" | custom-call | tf_op jit(solution)/shard_map/pallas_call | solution.py:714
  (3 shorter events, 0.1 us)
Async XLA Ops:
  2.4 8.5 %collective-permute-start = (f32[64,128]{1,0:T(8,128)}, f32[64,128]{1,0:T(8,128)S(1)}, u32[]{:S(2)}, u32[]{:S(2)}) collective-permute-start(f32[64,128]{1,0:T(8,128)} %get-tuple-element.45), channel_id=1, source_target_pairs={{0,1},{1,2},{2,3},{4,5},{5,6},{6,7},{8,9},{9,10},{10,11},{12,13},{... | collective-permute-start | bytes 98312 | tf_op jit(solution)/shard_map/ppermute | solution.py:732
  4.8 6.1 %collective-permute-start.1 = (f32[64,128]{1,0:T(8,128)}, f32[64,128]{1,0:T(8,128)S(1)}, u32[]{:S(2)}, u32[]{:S(2)}) collective-permute-start(f32[64,128]{1,0:T(8,128)} %get-tuple-element.46), channel_id=1, source_target_pairs={{1,0},{2,1},{3,2},{5,4},{6,5},{7,6},{9,8},{10,9},{11,10},{13,12},{... | collective-permute-start | bytes 98312 | tf_op jit(solution)/shard_map/ppermute | solution.py:733
  6.1 0.7 %copy-start.3 = (s32[1,64]{1,0:T(1,128)S(1)}, s32[1,64]{1,0:T(1,128)}, u32[]{:S(2)}) copy-start(s32[1,64]{1,0:T(1,128)} %get-tuple-element.40.loc) | copy-start | bytes 772
  6.1 0.7 %copy-start.4 = (f32[1,64]{1,0:T(1,128)S(1)}, f32[1,64]{1,0:T(1,128)}, u32[]{:S(2)}) copy-start(f32[1,64]{1,0:T(1,128)} %get-tuple-element.41.energy) | copy-start | bytes 772
  6.7 1.0 %copy-start = (f32[4,4,64,128]{3,2,1,0:T(8,128)S(1)}, f32[4,4,64,128]{3,2,1,0:T(8,128)}, u32[]{:S(2)}) copy-start(f32[4,4,64,128]{3,2,1,0:T(8,128)} %get-tuple-element.39.t_ref.refs_9_.refs_12_) | copy-start | bytes 1572868
  7.8 1.0 %copy-start.2 = (f32[4,4,64,128]{3,2,1,0:T(8,128)S(1)}, f32[4,4,64,128]{3,2,1,0:T(8,128)}, u32[]{:S(2)}) copy-start(f32[4,4,64,128]{3,2,1,0:T(8,128)} %get-tuple-element.42.b_ref) | copy-start | bytes 1572868
  11.3 4.5 %collective-permute-start.2 = (f32[7,16,128]{2,1,0:T(8,128)S(1)}, f32[7,16,128]{2,1,0:T(8,128)S(1)}, u32[]{:S(2)}, u32[]{:S(2)}) collective-permute-start(f32[7,16,128]{2,1,0:T(8,128)S(1)} %get-tuple-element.52.after.own), channel_id=1, source_target_pairs={{0,4},{4,0},{8,12},{12,8},{16,20},{20,16},{24,28},{28,24},{1,5},{5... | collective-permute-start | bytes 172040 | tf_op jit(solution)/shard_map/ppermute | solution.py:384
  15.9 9.6 %copy-start.1 = (f32[4,4,64,128]{3,2,1,0:T(8,128)S(1)}, f32[4,4,64,128]{3,2,1,0:T(8,128)}, u32[]{:S(2)}) copy-start(f32[4,4,64,128]{3,2,1,0:T(8,128)} %get-tuple-element.39.t_ref.refs_9_.refs_12_) | copy-start | bytes 1572868
  15.9 4.3 %collective-permute-start.3 = (f32[7,16,128]{2,1,0:T(8,128)S(1)}, f32[7,16,128]{2,1,0:T(8,128)S(1)}, u32[]{:S(2)}, u32[]{:S(2)}) collective-permute-start(f32[7,16,128]{2,1,0:T(8,128)S(1)} %get-tuple-element.54.own), channel_id=1, source_target_pairs={{0,8},{4,12},{8,0},{12,4},{16,24},{20,28},{24,16},{28,20},{1,9},{5... | collective-permute-start | bytes 172040 | tf_op jit(solution)/shard_map/ppermute | solution.py:384
  20.3 5.2 %collective-permute-start.4 = (f32[3,16,128]{2,1,0:T(8,128)S(1)}, f32[3,16,128]{2,1,0:T(8,128)S(1)}, u32[]{:S(2)}, u32[]{:S(2)}) collective-permute-start(f32[3,16,128]{2,1,0:T(8,128)S(1)} %get-tuple-element.56.refs_0_), channel_id=1, source_target_pairs={{0,16},{4,20},{8,24},{12,28},{16,0},{20,4},{24,8},{28,12},{1,17},{... | collective-permute-start | bytes 73736 | tf_op jit(solution)/shard_map/ppermute | solution.py:384
  26.3 1.2 %collective-permute-start.5 = (f32[7,2,128]{2,1,0:T(2,128)S(1)}, f32[7,2,128]{2,1,0:T(2,128)S(1)}, u32[]{:S(2)}, u32[]{:S(2)}) collective-permute-start(f32[7,2,128]{2,1,0:T(2,128)S(1)} %get-tuple-element.66.own), channel_id=1, source_target_pairs={{0,1},{1,0},{2,3},{3,2},{4,5},{5,4},{6,7},{7,6},{8,9},{9,8},{10,11... | collective-permute-start | bytes 21512 | tf_op jit(solution)/shard_map/ppermute | solution.py:384
  27.5 5.7 %collective-permute-start.6 = (f32[3,2,128]{2,1,0:T(2,128)S(1)}, f32[3,2,128]{2,1,0:T(2,128)S(1)}, u32[]{:S(2)}, u32[]{:S(2)}) collective-permute-start(f32[3,2,128]{2,1,0:T(2,128)S(1)} %get-tuple-element.67.refs_0_), channel_id=1, source_target_pairs={{0,2},{1,3},{2,0},{3,1},{4,6},{5,7},{6,4},{7,5},{8,10},{9,11},{10,... | collective-permute-start | bytes 9224 | tf_op jit(solution)/shard_map/ppermute | solution.py:384

commit v3 on v2

--- a/solution.py
+++ b/solution.py
@@ -129,7 +129,11 @@
     return first, h
 
 
-def load_kernel(t_hbm, b_hbm, loc_hbm, energy_hbm, t_out, b_out, loc, energy, lo, hi, sems):
+def is_odd(axis):
+    return lax.axis_index(axis) % 2 == 1
+
+
+def load_kernel(t_hbm, b_hbm, loc_hbm, energy_hbm, t_out, b_out, loc, energy, near, far, sems):
     chunks, sheets, rows, _ = t_out.shape
     order = [0, chunks - 1] + list(range(1, chunks - 1))
     copies = {}
@@ -148,8 +152,9 @@
     for copy in small:
         copy.start()
     lane = lax.broadcasted_iota(jnp.int32, (rows, LANES), 1)
-    for y, out, source in ((0, lo, 0), (chunks - 1, hi, LANES - 1)):
-        for copy in copies[y]:
+    edges = []
+    for y, source in ((0, 0), (chunks - 1, LANES - 1)):
+        for copy in copies[y] if y or not edges else ():
             copy.wait()
         packed = jnp.zeros((rows, LANES), F32)
         for z in range(sheets):
@@ -157,7 +162,9 @@
             c = half_conduct(b_out[y, z], t)
             packed = jnp.where(lane == z, t[:, source : source + 1], packed)
             packed = jnp.where(lane == sheets + z, c[:, source : source + 1], packed)
-        out[...] = packed
+        edges.append(packed)
+    near[...] = jnp.where(is_odd("gy"), edges[0], edges[1])
+    far[...] = jnp.where(is_odd("gy"), edges[1], edges[0])
     for y in range(1, chunks - 1):
         for copy in copies[y]:
             copy.wait()
@@ -168,21 +175,21 @@
 def load(temperature, base, locations, energy):
     sheets, rows, columns = temperature.shape
     chunks = columns // LANES
-    field = shape_of(chunks, sheets, rows, LANES)
+    field = pltpu.VMEM((chunks, sheets, rows, LANES), F32)
     return pl.pallas_call(
         load_kernel,
         in_specs=[IN_HBM] * 4,
         out_shape=[
             field,
             field,
-            jax.ShapeDtypeStruct(locations.shape, jnp.int32),
-            jax.ShapeDtypeStruct(energy.shape, F32),
-            shape_of(rows, LANES),
-            shape_of(rows, LANES),
+            pltpu.VMEM(locations.shape, jnp.int32),
+            pltpu.VMEM(energy.shape, F32),
+            pltpu.VMEM((rows, LANES), F32),
+            pltpu.VMEM((rows, LANES), F32),
         ],
         scratch_shapes=[pltpu.SemaphoreType.DMA((3, max(2, chunks)))],
-        compiler_params=params(55),
-    )(temperature, base, locations, energy)
+        compiler_params=params(),
+    )(*[pltpu.with_memory_space_constraint(v, pltpu.HBM) for v in (temperature, base, locations, energy)])
 
 
 def source_plane(loc, energy, rows, columns, plate):
@@ -302,11 +309,13 @@
     )(loc, energy, t, b)
 
 
-def x_target_kernel(t_ref, c_ref, total_ref, before, after, w_ref, i_ref, p_ref, links, view, h_ref, own, send, e_s, q_s):
+def x_target_kernel(t_ref, c_ref, total_ref, near, far, w_ref, i_ref, p_ref, links, view, h_ref, own, send, e_s, q_s):
     chunks, sheets, rows, _ = t_ref.shape
     lines = chunks * sheets
     steps = rows // SUBLANES
 
+    before = jnp.where(is_odd("gy"), near[...], far[...])
+    after = jnp.where(is_odd("gy"), far[...], near[...])
     lane = lax.broadcasted_iota(jnp.int32, (rows, LANES), 1)
     for y, halo, edge, place in ((0, before, 0, 0), (chunks - 1, after, LANES - 1, 1)):
         for z in range(sheets):
@@ -356,7 +365,7 @@
     send[FIRST], send[LAST] = items[0]
 
 
-def x_target(t, c, total, before, after, w, inv, p, links, view):
+def x_target(t, c, total, near, far, w, inv, p, links, view):
     chunks, sheets, rows, _ = t.shape
     lines = chunks * sheets
     steps = rows // SUBLANES
@@ -372,7 +381,7 @@
             pltpu.VMEM((2, lines * SUBLANES, LANES), F32),
         ],
         compiler_params=params(),
-    )(t, c, total, before, after, w, inv, p, links, view)
+    )(t, c, total, near, far, w, inv, p, links, view)
 
 
 def stages_of(axis):
@@ -728,11 +737,11 @@
 def per_device(temperature, base, locations, energy):
     columns = temperature.shape[2]
     gy = lax.axis_size("gy")
-    t, b, loc, heat, low_edge, high_edge = load(temperature, base, locations[None], energy[None])
-    before = lax.ppermute(high_edge, "gy", [(i, i + 1) for i in range(gy - 1)])
-    after = lax.ppermute(low_edge, "gy", [(i + 1, i) for i in range(gy - 1)])
+    t, b, loc, heat, near_edge, far_edge = load(temperature, base, locations[None], energy[None])
+    near = lax.ppermute(near_edge, "gy", [(i, i ^ 1) for i in range(gy)])
+    far = lax.ppermute(far_edge, "gy", [(i, (i + 1 ^ 1) - 1) for i in range(1, gy - 1)])
     c, total, xw, xi, xp, x_links, x_view = x_factor(loc, heat, t, b, columns * gy)
-    xh, x_own, view = x_target(t, c, total, before, after, xw, xi, xp, x_links, x_view)
+    xh, x_own, view = x_target(t, c, total, near, far, xw, xi, xp, x_links, x_view)
     yw, yi, yp, inner, outer, y_view = y_factor(c, view)
     zw, zi = z_factor(c, view)
     own, got, ties = gather_line(view, "gx", (y_view, zw))

time: 34.9 us -> 28.9 us (0.83)
  local copies, waits for them, and re-layouts: 2.75 us -> 0 us
  starting transfers between devices: 15.8 us -> 13.6 us
  Pallas kernels: 8.13 us -> 7.18 us
    unnamed x10 -> x0, local copies, waits for them, and re-layouts: 2.75 us -> none
    ppermute x2, starting transfers between devices: 3.65 us -> 1.17 us  [the longest x1 0.65 us: per_device(): lax.ppermute(far_edge, 'gy', [(i, (i + 1 ^ 1) - 1) for i in range(1, gy -...]
    pallas_call x1, Pallas kernels: 2.38 us -> 1.4 us  [load(): pl.pallas_call(load_kernel, in_specs=[IN_HBM] * 4, out_shape=[field, fiel...]
  transfers between devices with their start and end apart: 7 -> 7, of which waited for: 5 -> 5; matrix products, arithmetic and copies ran while one was open for 0% -> 0% of each run, Pallas kernels for 9% -> 11%
where the time goes in v3:
time: 28.9 us; the launch traced here: 28.8 us
  starting transfers between devices  13.6 us (47%)
  waiting for transfers between devices  7.95 us (28%)
  Pallas kernels  7.18 us (25%)
    ppermute x5, starting transfers between devices, swap(): lax.ppermute(value, axis, [(i, i ^ 1 << stage) for i in range(count)])  12.4 us
    ppermute x5, waiting for transfers between devices, swap(): lax.ppermute(value, axis, [(i, i ^ 1 << stage) for i in range(count)])  7.94 us
    pallas_call x1, Pallas kernels, x_factor(): pl.pallas_call(functools.partial(x_factor_kernel, plate), out_shape=[fiel...  2.04 us
    pallas_call x1, Pallas kernels, load(): pl.pallas_call(load_kernel, in_specs=[IN_HBM] * 4, out_shape=[field, fiel...  1.4 us
    pallas_call x1, Pallas kernels, finish(): pl.pallas_call(functools.partial(finish_kernel, len(ties) + 1), out_shape...  1.34 us
    pallas_call x1, Pallas kernels, y_factor(): pl.pallas_call(y_factor_kernel, in_specs=[IN_VMEM, ANYWHERE], out_shape=[...  0.91 us
    pallas_call x1, Pallas kernels, y_target(): pl.pallas_call(functools.partial(y_target_kernel, len(ties) + 1), out_sha...  0.81 us
    ppermute x1, starting transfers between devices, per_device(): lax.ppermute(far_edge, 'gy', [(i, (i + 1 ^ 1) - 1) for i in range(1, gy -...  0.65 us
  transfers between devices with their start and end apart: 7, of which 5 were waited for; matrix products, arithmetic and copies ran while one was open for 0% of the time, Pallas kernels for 11%

profile of v3, /device:TPU:0, one launch (start us, length us, event | category | flops | bytes accessed | tf_op | source)
XLA Modules:
  0.0 28.8 jit_solution(9215888056096179134)
XLA Ops:
  0.0 1.4 %shard_map.46 = (f32[4,4,64,128]{3,2,1,0:T(8,128)S(1)}, f32[4,4,64,128]{3,2,1,0:T(8,128)S(1)}, s32[1,64]{1,0:T(1,128)S(1)}, f32[1,64]{1,0:T(1,128)S(1)}, f32[64,128]{1,0:T(8,128)S(1)}, /*index=5*/f32[64,128]{1,0:T(8,128)S(1)}) custom-call(f32[4,64,512]{2,1,0:T(8,128)} %t_hbm.1, f32[4,64,512]{2,1,0:T(8,128)} %b_hbm.1, s32[1,64]{1,0:T(1,128)} %bitcast.2, ...), custom_call_target="tpu_custom_call" | custom-call | tf_op jit(solution)/shard_map/pallas_call | solution.py:179
  1.4 0.5 %collective-permute-start = (f32[64,128]{1,0:T(8,128)S(1)}, f32[64,128]{1,0:T(8,128)S(1)}, u32[]{:S(2)}, u32[]{:S(2)}) collective-permute-start(f32[64,128]{1,0:T(8,128)S(1)} %get-tuple-element.45), channel_id=1, source_target_pairs={{0,1},{1,0},{2,3},{3,2},{4,5},{5,4},{6,7},{7,6},{8,9},{9,8},{10,11... | collective-permute-start | bytes 98312 | tf_op jit(solution)/shard_map/ppermute | solution.py:741
  1.9 0.7 %collective-permute-start.1 = (f32[64,128]{1,0:T(8,128)S(1)}, f32[64,128]{1,0:T(8,128)S(1)}, u32[]{:S(2)}, u32[]{:S(2)}) collective-permute-start(f32[64,128]{1,0:T(8,128)S(1)} %get-tuple-element.46), channel_id=1, source_target_pairs={{1,2},{2,1},{5,6},{6,5},{9,10},{10,9},{13,14},{14,13},{17,18},{18,... | collective-permute-start | bytes 98312 | tf_op jit(solution)/shard_map/ppermute | solution.py:742
  2.6 2.0 %shard_map.47 = (f32[4,4,64,128]{3,2,1,0:T(8,128)S(1)}, f32[4,4,64,128]{3,2,1,0:T(8,128)S(1)}, f32[8,16,8,128]{3,2,1,0:T(8,128)S(1)}, f32[8,16,8,128]{3,2,1,0:T(...) custom-call(s32[1,64]{1,0:T(1,128)S(1)} %get-tuple-element.40.loc, ...), custom_call_target="tpu_custom_call" | custom-call | flops 5242880 | bytes 3670016 | tf_op jit(solution)/shard_map/pallas_call | solution.py:295
  4.6 0.0 collective-permute-done.near
  4.6 0.0 collective-permute-done.1.far
  4.7 0.5 %shard_map.48 = (f32[8,16,8,128]{3,2,1,0:T(8,128)S(1)}, f32[7,16,128]{2,1,0:T(8,128)S(1)}, f32[7,16,128]{2,1,0:T(8,128)S(1)}) custom-call(f32[4,4,64,128]{3,2,1,0:T(8,128)S(1)} %get-tuple-element.39.t_ref.refs_9_.refs_12_, f32[4,4,64,128]{3,2,1,0:T(8,128)S(1)} %get-tuple-element.43.c_ref, f32[4,4,64,128]{3,2,1,0:T(8,128)S(1)} %get-tuple-element.44.total_ref, ...), custom_call_target="tpu_custom_call" | custom-call | tf_op jit(solution)/shard_map/pallas_call | solution.py:372
  5.1 2.6 %collective-permute-start.2 = (f32[7,16,128]{2,1,0:T(8,128)S(1)}, f32[7,16,128]{2,1,0:T(8,128)S(1)}, u32[]{:S(2)}, u32[]{:S(2)}) collective-permute-start(f32[7,16,128]{2,1,0:T(8,128)S(1)} %get-tuple-element.52.after.own), channel_id=1, source_target_pairs={{0,4},{4,0},{8,12},{12,8},{16,20},{20,16},{24,28},{28,24},{1,5},{5... | collective-permute-start | bytes 172040 | tf_op jit(solution)/shard_map/ppermute | solution.py:393
  7.7 0.9 %shard_map.49 = (f32[16,8,8,128]{3,2,1,0:T(8,128)S(1)}, f32[16,8,8,128]{3,2,1,0:T(8,128)S(1)}, f32[16,8,8,128]{3,2,1,0:T(8,128)S(1)}, f32[3,3,2,8,128]{4,3,2,1,0...) custom-call(f32[4,4,64,128]{3,2,1,0:T(8,128)S(1)} %get-tuple-element.43.c_ref, ...), custom_call_target="tpu_custom_call" | custom-call | flops 2621440 | bytes 2097152 | tf_op jit(solution)/shard_map/pallas_call | solution.py:509
  8.6 1.2 %collective-permute-done.2.got = f32[7,16,128]{2,1,0:T(8,128)S(1)} collective-permute-done((f32[7,16,128]{2,1,0:T(8,128)S(1)}, f32[7,16,128]{2,1,0:T(8,128)S(1)}, u32[]{:S(2)}, u32[]{:S(2)}) %collective-permute-start.2) | collective-permute-done | bytes 57376 | tf_op jit(solution)/shard_map/ppermute | solution.py:393
  9.9 2.2 %collective-permute-start.3 = (f32[7,16,128]{2,1,0:T(8,128)S(1)}, f32[7,16,128]{2,1,0:T(8,128)S(1)}, u32[]{:S(2)}, u32[]{:S(2)}) collective-permute-start(f32[7,16,128]{2,1,0:T(8,128)S(1)} %get-tuple-element.54.own), channel_id=1, source_target_pairs={{0,8},{4,12},{8,0},{12,4},{16,24},{20,28},{24,16},{28,20},{1,9},{5... | collective-permute-start | bytes 172040 | tf_op jit(solution)/shard_map/ppermute | solution.py:393
  12.1 0.2 shard_map.51
  12.2 2.0 %collective-permute-done.3.got = f32[7,16,128]{2,1,0:T(8,128)S(1)} collective-permute-done((f32[7,16,128]{2,1,0:T(8,128)S(1)}, f32[7,16,128]{2,1,0:T(8,128)S(1)}, u32[]{:S(2)}, u32[]{:S(2)}) %collective-permute-start.3) | collective-permute-done | bytes 57376 | tf_op jit(solution)/shard_map/ppermute | solution.py:393
  14.2 3.1 %collective-permute-start.4 = (f32[3,16,128]{2,1,0:T(8,128)S(1)}, f32[3,16,128]{2,1,0:T(8,128)S(1)}, u32[]{:S(2)}, u32[]{:S(2)}) collective-permute-start(f32[3,16,128]{2,1,0:T(8,128)S(1)} %get-tuple-element.56.refs_0_), channel_id=1, source_target_pairs={{0,16},{4,20},{8,24},{12,28},{16,0},{20,4},{24,8},{28,12},{1,17},{... | collective-permute-start | bytes 73736 | tf_op jit(solution)/shard_map/ppermute | solution.py:393
  17.3 2.1 %collective-permute-done.4.refs_1_ = f32[3,16,128]{2,1,0:T(8,128)S(1)} collective-permute-done((f32[3,16,128]{2,1,0:T(8,128)S(1)}, f32[3,16,128]{2,1,0:T(8,128)S(1)}, u32[]{:S(2)}, u32[]{:S(2)}) %collective-permute-start.4) | collective-permute-done | bytes 24608 | tf_op jit(solution)/shard_map/ppermute | solution.py:393
  19.4 0.8 %shard_map.53 = (f32[16,8,8,128]{3,2,1,0:T(8,128)S(1)}, f32[3,2,8,128]{3,2,1,0:T(8,128)S(1)}, f32[7,2,128]{2,1,0:T(2,128)S(1)}, f32[7,2,128]{2,1,0:T(2,128)S(1)}) custom-call(f32[3,16,128]{2,1,0:T(8,128)S(1)} %get-tuple-element.56.refs_0_, f32[3,16,128]{2,1,0:T(8,128)S(1)} %collective-permute-done.4.refs_1_, f32[3,16,128]{2,1,0:T(8,128)S(1)} %get-tuple-element.57.refs_2_, ...), custom_call_target="tpu_custom_call" | custom-call | tf_op jit(solution)/shard_map/pallas_call | solution.py:644
  20.2 0.2 collective-permute-start.5
  20.4 1.1 %collective-permute-done.5.got = f32[7,2,128]{2,1,0:T(2,128)S(1)} collective-permute-done((f32[7,2,128]{2,1,0:T(2,128)S(1)}, f32[7,2,128]{2,1,0:T(2,128)S(1)}, u32[]{:S(2)}, u32[]{:S(2)}) %collective-permute-start.5) | collective-permute-done | bytes 7200 | tf_op jit(solution)/shard_map/ppermute | solution.py:393
  21.5 4.4 %collective-permute-start.6 = (f32[3,2,128]{2,1,0:T(2,128)S(1)}, f32[3,2,128]{2,1,0:T(2,128)S(1)}, u32[]{:S(2)}, u32[]{:S(2)}) collective-permute-start(f32[3,2,128]{2,1,0:T(2,128)S(1)} %get-tuple-element.67.refs_0_), channel_id=1, source_target_pairs={{0,2},{1,3},{2,0},{3,1},{4,6},{5,7},{6,4},{7,5},{8,10},{9,11},{10,... | collective-permute-start | bytes 9224 | tf_op jit(solution)/shard_map/ppermute | solution.py:393
  25.9 1.6 %collective-permute-done.6.refs_1_ = f32[3,2,128]{2,1,0:T(2,128)S(1)} collective-permute-done((f32[3,2,128]{2,1,0:T(2,128)S(1)}, f32[3,2,128]{2,1,0:T(2,128)S(1)}, u32[]{:S(2)}, u32[]{:S(2)}) %collective-permute-start.6) | collective-permute-done | bytes 3104 | tf_op jit(solution)/shard_map/ppermute | solution.py:393
  27.5 1.3 %shard_map.55 = f32[4,64,512]{2,1,0:T(8,128)} custom-call(f32[3,2,128]{2,1,0:T(2,128)S(1)} %get-tuple-element.67.refs_0_, f32[3,2,128]{2,1,0:T(2,128)S(1)} %collective-permute-done.6.refs_1_, f32[3,2,128]{2,1,0:T(2,128)S(1)} %get-tuple-element.68.refs_2_, f32[16,8,8,128]{3,2,1,0:T(8,128)S(1)} %get-tuple-element.61.refs_10_.refs_3_, ...), custom_call_target="tpu_custom_call" | custom-call | tf_op jit(solution)/shard_map/pallas_call | solution.py:723
  (3 shorter events, 0.1 us)
Async XLA Ops:
  1.4 3.2 %collective-permute-start = (f32[64,128]{1,0:T(8,128)S(1)}, f32[64,128]{1,0:T(8,128)S(1)}, u32[]{:S(2)}, u32[]{:S(2)}) collective-permute-start(f32[64,128]{1,0:T(8,128)S(1)} %get-tuple-element.45), channel_id=1, source_target_pairs={{0,1},{1,0},{2,3},{3,2},{4,5},{5,4},{6,7},{7,6},{8,9},{9,8},{10,11... | collective-permute-start | bytes 98312 | tf_op jit(solution)/shard_map/ppermute | solution.py:741
  1.9 2.7 %collective-permute-start.1 = (f32[64,128]{1,0:T(8,128)S(1)}, f32[64,128]{1,0:T(8,128)S(1)}, u32[]{:S(2)}, u32[]{:S(2)}) collective-permute-start(f32[64,128]{1,0:T(8,128)S(1)} %get-tuple-element.46), channel_id=1, source_target_pairs={{1,2},{2,1},{5,6},{6,5},{9,10},{10,9},{13,14},{14,13},{17,18},{18,... | collective-permute-start | bytes 98312 | tf_op jit(solution)/shard_map/ppermute | solution.py:742
  5.1 4.7 %collective-permute-start.2 = (f32[7,16,128]{2,1,0:T(8,128)S(1)}, f32[7,16,128]{2,1,0:T(8,128)S(1)}, u32[]{:S(2)}, u32[]{:S(2)}) collective-permute-start(f32[7,16,128]{2,1,0:T(8,128)S(1)} %get-tuple-element.52.after.own), channel_id=1, source_target_pairs={{0,4},{4,0},{8,12},{12,8},{16,20},{20,16},{24,28},{28,24},{1,5},{5... | collective-permute-start | bytes 172040 | tf_op jit(solution)/shard_map/ppermute | solution.py:393
  9.9 4.3 %collective-permute-start.3 = (f32[7,16,128]{2,1,0:T(8,128)S(1)}, f32[7,16,128]{2,1,0:T(8,128)S(1)}, u32[]{:S(2)}, u32[]{:S(2)}) collective-permute-start(f32[7,16,128]{2,1,0:T(8,128)S(1)} %get-tuple-element.54.own), channel_id=1, source_target_pairs={{0,8},{4,12},{8,0},{12,4},{16,24},{20,28},{24,16},{28,20},{1,9},{5... | collective-permute-start | bytes 172040 | tf_op jit(solution)/shard_map/ppermute | solution.py:393
  14.2 5.2 %collective-permute-start.4 = (f32[3,16,128]{2,1,0:T(8,128)S(1)}, f32[3,16,128]{2,1,0:T(8,128)S(1)}, u32[]{:S(2)}, u32[]{:S(2)}) collective-permute-start(f32[3,16,128]{2,1,0:T(8,128)S(1)} %get-tuple-element.56.refs_0_), channel_id=1, source_target_pairs={{0,16},{4,20},{8,24},{12,28},{16,0},{20,4},{24,8},{28,12},{1,17},{... | collective-permute-start | bytes 73736 | tf_op jit(solution)/shard_map/ppermute | solution.py:393
  20.2 1.2 %collective-permute-start.5 = (f32[7,2,128]{2,1,0:T(2,128)S(1)}, f32[7,2,128]{2,1,0:T(2,128)S(1)}, u32[]{:S(2)}, u32[]{:S(2)}) collective-permute-start(f32[7,2,128]{2,1,0:T(2,128)S(1)} %get-tuple-element.66.own), channel_id=1, source_target_pairs={{0,1},{1,0},{2,3},{3,2},{4,5},{5,4},{6,7},{7,6},{8,9},{9,8},{10,11... | collective-permute-start | bytes 21512 | tf_op jit(solution)/shard_map/ppermute | solution.py:393
  21.5 6.0 %collective-permute-start.6 = (f32[3,2,128]{2,1,0:T(2,128)S(1)}, f32[3,2,128]{2,1,0:T(2,128)S(1)}, u32[]{:S(2)}, u32[]{:S(2)}) collective-permute-start(f32[3,2,128]{2,1,0:T(2,128)S(1)} %get-tuple-element.67.refs_0_), channel_id=1, source_target_pairs={{0,2},{1,3},{2,0},{3,1},{4,6},{5,7},{6,4},{7,5},{8,10},{9,11},{10,... | collective-permute-start | bytes 9224 | tf_op jit(solution)/shard_map/ppermute | solution.py:393

commit v4 on v3

--- a/solution.py
+++ b/solution.py
@@ -133,63 +133,50 @@
     return lax.axis_index(axis) % 2 == 1
 
 
-def load_kernel(t_hbm, b_hbm, loc_hbm, energy_hbm, t_out, b_out, loc, energy, near, far, sems):
-    chunks, sheets, rows, _ = t_out.shape
-    order = [0, chunks - 1] + list(range(1, chunks - 1))
-    copies = {}
-    for y in order:
-        part = pl.ds(y * LANES, LANES)
-        copies[y] = [
-            pltpu.make_async_copy(src.at[:, :, part], dst.at[y], sems.at[i, y])
-            for i, (src, dst) in enumerate(((t_hbm, t_out), (b_hbm, b_out)))
-        ]
-        for copy in copies[y]:
-            copy.start()
-    small = [
+def edges_kernel(t_hbm, b_hbm, loc_hbm, energy_hbm, loc, energy, packed, t_s, b_s, sems):
+    sheets, rows, columns = t_hbm.shape
+    copies = [
         pltpu.make_async_copy(loc_hbm, loc, sems.at[2, 0]),
         pltpu.make_async_copy(energy_hbm, energy, sems.at[2, 1]),
     ]
-    for copy in small:
+    for side, start in enumerate((0, columns - LANES)):
+        for i, (src, dst) in enumerate(((t_hbm, t_s), (b_hbm, b_s))):
+            part = src.at[:, :, pl.ds(start, LANES)]
+            copies.append(pltpu.make_async_copy(part, dst.at[side], sems.at[i, side]))
+    for copy in copies:
         copy.start()
+    for copy in copies:
+        copy.wait()
     lane = lax.broadcasted_iota(jnp.int32, (rows, LANES), 1)
-    edges = []
-    for y, source in ((0, 0), (chunks - 1, LANES - 1)):
-        for copy in copies[y] if y or not edges else ():
-            copy.wait()
-        packed = jnp.zeros((rows, LANES), F32)
+    total = jnp.zeros((rows, LANES), F32)
+    for side, source in enumerate((0, LANES - 1)):
         for z in range(sheets):
-            t = t_out[y, z]
-            c = half_conduct(b_out[y, z], t)
-            packed = jnp.where(lane == z, t[:, source : source + 1], packed)
-            packed = jnp.where(lane == sheets + z, c[:, source : source + 1], packed)
-        edges.append(packed)
-    near[...] = jnp.where(is_odd("gy"), edges[0], edges[1])
-    far[...] = jnp.where(is_odd("gy"), edges[1], edges[0])
-    for y in range(1, chunks - 1):
-        for copy in copies[y]:
-            copy.wait()
-    for copy in small:
-        copy.wait()
-
-
-def load(temperature, base, locations, energy):
-    sheets, rows, columns = temperature.shape
-    chunks = columns // LANES
-    field = pltpu.VMEM((chunks, sheets, rows, LANES), F32)
+            t = t_s[side, z]
+            c = half_conduct(b_s[side, z], t)
+            place = 2 * sheets * side + z
+            total = jnp.where(lane == place, t[:, source : source + 1], total)
+            total = jnp.where(lane == place + sheets, c[:, source : source + 1], total)
+    packed[...] = total
+
+
+def edges(temperature, base, locations, energy):
+    sheets, rows, _ = temperature.shape
+    operands = (temperature, base, locations, energy)
     return pl.pallas_call(
-        load_kernel,
+        edges_kernel,
         in_specs=[IN_HBM] * 4,
         out_shape=[
-            field,
-            field,
             pltpu.VMEM(locations.shape, jnp.int32),
             pltpu.VMEM(energy.shape, F32),
             pltpu.VMEM((rows, LANES), F32),
-            pltpu.VMEM((rows, LANES), F32),
-        ],
-        scratch_shapes=[pltpu.SemaphoreType.DMA((3, max(2, chunks)))],
+        ],
+        scratch_shapes=[
+            pltpu.VMEM((2, sheets, rows, LANES), F32),
+            pltpu.VMEM((2, sheets, rows, LANES), F32),
+            pltpu.SemaphoreType.DMA((3, 2)),
+        ],
         compiler_params=params(),
-    )(*[pltpu.with_memory_space_constraint(v, pltpu.HBM) for v in (temperature, base, locations, energy)])
+    )(*[pltpu.with_memory_space_constraint(v, pltpu.HBM) for v in operands])
 
 
 def source_plane(loc, energy, rows, columns, plate):
@@ -215,8 +202,13 @@
     return plane
 
 
-def x_factor_kernel(plate, loc, energy, t_ref, b_ref, c_ref, total_ref, w_ref, i_ref, p_ref, links, view, q_s):
-    chunks, sheets, rows, _ = t_ref.shape
+def part_of(y):
+    return slice(y * LANES, (y + 1) * LANES)
+
+
+def x_factor_kernel(plate, loc, energy, t_ref, b_ref, after, *refs):
+    c_ref, total_ref, w_ref, i_ref, p_ref, links, view, q_s = refs
+    chunks, sheets, rows, _ = c_ref.shape
     lines = chunks * sheets
     steps = rows // SUBLANES
     plane = source_plane(loc, energy, rows, chunks * LANES, plate)
@@ -227,8 +219,8 @@
         at = slice(r * SUBLANES, (r + 1) * SUBLANES)
         before_t, before_c = None, None
         for z in range(sheets):
-            ts = [t_ref[y, z, at, :] for y in range(chunks)]
-            cs = [half_conduct(b_ref[y, z, at, :], ts[y]) for y in range(chunks)]
+            ts = [t_ref[z, at, part_of(y)] for y in range(chunks)]
+            cs = [half_conduct(b_ref[z, at, part_of(y)], ts[y]) for y in range(chunks)]
             t_turned = [pltpu.roll(v, LANES - 1, 1) for v in ts]
             c_turned = [pltpu.roll(v, LANES - 1, 1) for v in cs]
             flux = []
@@ -245,7 +237,7 @@
                 from_low = jnp.where(is_first, turned[y - 1] if y else 0.0, turned[y])
                 total = ts[y] + (flux[y] - from_low)
                 if z == 0:
-                    total = total + plane[at, y * LANES : (y + 1) * LANES]
+                    total = total + plane[at, part_of(y)]
                 else:
                     across = (before_c[y] + cs[y]) * (ts[y] - before_t[y])
                     total = total - across
@@ -286,14 +278,16 @@
         view[n] = whole[q]
 
 
-def x_factor(loc, energy, t, b, plate):
-    chunks, sheets, rows, _ = t.shape
+def x_factor(loc, energy, t, b, plate, after):
+    sheets, rows, columns = t.shape
+    chunks = columns // LANES
     lines = chunks * sheets
     steps = rows // SUBLANES
-    field = shape_of(*t.shape)
+    field = shape_of(chunks, sheets, rows, LANES)
     stored = shape_of(steps, lines, SUBLANES, LANES)
     return pl.pallas_call(
         functools.partial(x_factor_kernel, plate),
+        in_specs=[IN_VMEM] * 4 + [ANYWHERE],
         out_shape=[
             field,
             field,
@@ -306,11 +300,11 @@
         scratch_shapes=[pltpu.VMEM((len(COEFS), lines * SUBLANES, LANES), F32)],
         compiler_params=params(),
         cost_estimate=pl.CostEstimate(flops=40 * t.size, bytes_accessed=28 * t.size, transcendentals=0),
-    )(loc, energy, t, b)
+    )(loc, energy, t, b, after)
 
 
 def x_target_kernel(t_ref, c_ref, total_ref, near, far, w_ref, i_ref, p_ref, links, view, h_ref, own, send, e_s, q_s):
-    chunks, sheets, rows, _ = t_ref.shape
+    chunks, sheets, rows, _ = c_ref.shape
     lines = chunks * sheets
     steps = rows // SUBLANES
 
@@ -319,10 +313,11 @@
     lane = lax.broadcasted_iota(jnp.int32, (rows, LANES), 1)
     for y, halo, edge, place in ((0, before, 0, 0), (chunks - 1, after, LANES - 1, 1)):
         for z in range(sheets):
-            c_next = halo[:, sheets + z : sheets + z + 1]
-            t_next = halo[:, z : z + 1]
+            at = z if place else 2 * sheets + z
+            t_next = halo[:, at : at + 1]
+            c_next = halo[:, at + sheets : at + sheets + 1]
             face = jnp.where(c_next > 0.0, c_ref[y, z] + c_next, 0.0)
-            flux = jnp.where(lane == edge, face * (t_next - t_ref[y, z]), 0.0)
+            flux = jnp.where(lane == edge, face * (t_next - t_ref[z, :, part_of(y)]), 0.0)
             base = total_ref[y, z] if place == 0 or chunks > 1 else e_s[0, z]
             e_s[place, z] = base + flux
 
@@ -366,7 +361,7 @@
 
 
 def x_target(t, c, total, near, far, w, inv, p, links, view):
-    chunks, sheets, rows, _ = t.shape
+    chunks, sheets, rows, _ = c.shape
     lines = chunks * sheets
     steps = rows // SUBLANES
     return pl.pallas_call(
@@ -388,9 +383,9 @@
     return lax.axis_size(axis).bit_length() - 1
 
 
-def swap(value, axis, stage):
+def swap(value, axis, flip):
     count = lax.axis_size(axis)
-    return lax.ppermute(value, axis, [(i, i ^ (1 << stage)) for i in range(count)])
+    return lax.ppermute(value, axis, [(i, i ^ flip) for i in range(count)])
 
 
 def on_right(axis, stage):
@@ -405,40 +400,71 @@
     )
 
 
-def join_kernel(axis, stage, last, own, got, *refs):
-    send, links = refs[-2:]
-    right = on_right(axis, stage)
-    a = {q: jnp.where(right, got[q], own[q]) for q in range(7)}
-    b = {q: jnp.where(right, own[q], got[q]) for q in range(7)}
+def join(a, b):
     joined, ties = join_coefs(a, b)
     (joined[FIRST], joined[LAST]), flux = join_targets((a[FIRST], a[LAST]), (b[FIRST], b[LAST]), ties)
-    links[0], links[1], links[2] = flux, ties[1], ties[2]
+    return joined, (flux, ties[1], ties[2])
+
+
+def ordered(right, own, other):
+    first = [jnp.where(right, theirs, mine) for mine, theirs in zip(own, other)]
+    second = [jnp.where(right, mine, theirs) for mine, theirs in zip(own, other)]
+    return first, second
+
+
+def join_kernel(axis, stage, width, last, *refs):
+    blocks = [[refs[i][q] for q in range(7)] for i in range(1 << width)]
+    send = refs[-1 - width]
+    links = refs[-width:]
+    for bit in range(width):
+        right = on_right(axis, stage + bit)
+        for i in range(1 << width):
+            if not i >> bit & 1:
+                j = i | 1 << bit
+                blocks[i], blocks[j] = ordered(right, blocks[i], blocks[j])
+    for bit in range(width):
+        pairs = [join(blocks[i], blocks[i + 1]) for i in range(0, len(blocks), 2)]
+        blocks = [p[0] for p in pairs]
+        ties = [p[1] for p in pairs]
+        for upper in range(bit + 1, width):
+            right = on_right(axis, stage + upper)
+            ties = [
+                tuple(jnp.where(right, v, u) for u, v in zip(ties[i], ties[i + 1]))
+                for i in range(0, len(ties), 2)
+            ]
+        for i in range(3):
+            links[bit][i] = ties[0][i]
+    (whole,) = blocks
     if last:
-        for n, value in enumerate(toward(on_right(axis, stage + 1), joined)):
+        for n, value in enumerate(toward(on_right(axis, stage + width), whole)):
             send[n] = value
     else:
         for q in range(7):
-            send[q] = joined[q]
-
-
-def join_stage(own, got, axis, stage, last, after):
+            send[q] = whole[q]
+
+
+def join_stage(own, got, axis, stage, width, last, after):
     lines = own.shape[1]
     return pl.pallas_call(
-        functools.partial(join_kernel, axis, stage, last),
-        in_specs=[IN_VMEM] * 2 + [ANYWHERE] * len(after),
-        out_shape=[shape_of(3 if last else 7, lines, LANES), shape_of(3, lines, LANES)],
+        functools.partial(join_kernel, axis, stage, width, last),
+        in_specs=[IN_VMEM] * (1 + len(got)) + [ANYWHERE] * len(after),
+        out_shape=[shape_of(3 if last else 7, lines, LANES)] + [shape_of(3, lines, LANES)] * width,
         compiler_params=params(),
-    )(own, got, *after)
-
-
-def gather_line(view, axis, meanwhile=()):
+    )(own, *got, *after)
+
+
+def gather_line(view, axis, widest=1, meanwhile=()):
     stages = stages_of(axis)
-    links = []
-    for stage in range(stages - 1):
-        got = swap(view, axis, stage)
-        view, tie = join_stage(view, got, axis, stage, stage == stages - 2, meanwhile[stage : stage + 1])
-        links.append(tie)
-    return view, swap(view, axis, stages - 1), links
+    links, stage = [], 0
+    while stage < stages - 1:
+        width = min(widest, stages - 1 - stage)
+        got = [swap(view, axis, flip << stage) for flip in range(1, 1 << width)]
+        last = stage + width == stages - 1
+        view, *ties = join_stage(view, got, axis, stage, width, last, meanwhile)
+        links += ties
+        stage += width
+        meanwhile = ()
+    return view, swap(view, axis, 1 << stage), links
 
 
 def block_ends(axis, own, got, links):
@@ -559,7 +585,7 @@
     xw, xh, xp, x_links, x_own, t_ref, yw, yi, yp, inner, outer, view = refs[1 + stages : 13 + stages]
     h_ref, inner_own, outer_own, send = refs[13 + stages : 17 + stages]
     f_s, g_s, y_s, q_s = refs[17 + stages :]
-    chunks, sheets, rows, _ = t_ref.shape
+    chunks, sheets, rows, _ = g_s.shape
     lines = chunks * sheets
     x_steps = rows // SUBLANES
 
@@ -597,7 +623,7 @@
     for m in range(pairs):
         for y in range(chunks):
             block = jnp.concatenate(
-                [g_s[y, m * each + i] - t_ref[y, m * each + i] for i in range(each)], 0
+                [g_s[y, m * each + i] - t_ref[m * each + i, :, part_of(y)] for i in range(each)], 0
             )
             y_s[m, y * LANES : (y + 1) * LANES, :] = block.T
     members = [(j, m) for j in range(Y_PARTS) for m in range(pairs)]
@@ -638,7 +664,8 @@
 
 
 def y_target(own, got, ties, xw, xh, xp, x_links, x_own, t, yw, yi, yp, inner, outer, view):
-    chunks, sheets, rows, _ = t.shape
+    sheets, rows, columns = t.shape
+    chunks = columns // LANES
     lines = chunks * sheets
     pairs = sheets * rows // LANES
     return pl.pallas_call(
@@ -664,7 +691,7 @@
     ties = refs[2 : 1 + stages]
     yw, yh, yp, inner, inner_own, outer, outer_own, zw, zi, t_ref = refs[1 + stages : 11 + stages]
     out, e_s, u_s, o_s, sems = refs[11 + stages :]
-    chunks, sheets, rows, _ = t_ref.shape
+    chunks, sheets, rows, _ = o_s.shape
     each = LANES // rows
     pairs = sheets // each
     steps = yw.shape[0]
@@ -697,7 +724,7 @@
 
     copies = []
     for y in range(chunks):
-        part = slice(y * LANES, (y + 1) * LANES)
+        part = part_of(y)
         turned = [u_s[m, part, :].T for m in range(pairs)]
         rhs, kept = None, []
         for z in range(sheets):
@@ -706,10 +733,10 @@
             rhs = own_rhs if z == 0 else own_rhs + zw[z - 1, y] * rhs
             kept.append(rhs * zi[z, y])
         value = kept[-1]
-        o_s[y, sheets - 1] = t_ref[y, sheets - 1] + value
+        o_s[y, sheets - 1] = t_ref[sheets - 1, :, part] + value
         for z in range(sheets - 2, -1, -1):
             value = zw[z, y] * value + kept[z]
-            o_s[y, z] = t_ref[y, z] + value
+            o_s[y, z] = t_ref[z, :, part] + value
         copy = pltpu.make_async_copy(o_s.at[y], out.at[:, :, pl.ds(y * LANES, LANES)], sems.at[y])
         copy.start()
         copies.append(copy)
@@ -718,7 +745,8 @@
 
 
 def finish(own, got, ties, yw, yh, yp, inner, inner_own, outer, outer_own, zw, zi, t):
-    chunks, sheets, rows, _ = t.shape
+    sheets, rows, columns = t.shape
+    chunks = columns // LANES
     pairs = sheets * rows // LANES
     return pl.pallas_call(
         functools.partial(finish_kernel, len(ties) + 1),
@@ -727,7 +755,7 @@
         scratch_shapes=[
             pltpu.VMEM((2, pairs * SUBLANES, LANES), F32),
             pltpu.VMEM((pairs, chunks * LANES, LANES), F32),
-            pltpu.VMEM(t.shape, F32),
+            pltpu.VMEM((chunks, sheets, rows, LANES), F32),
             pltpu.SemaphoreType.DMA((chunks,)),
         ],
         compiler_params=params(),
@@ -737,14 +765,17 @@
 def per_device(temperature, base, locations, energy):
     columns = temperature.shape[2]
     gy = lax.axis_size("gy")
-    t, b, loc, heat, near_edge, far_edge = load(temperature, base, locations[None], energy[None])
-    near = lax.ppermute(near_edge, "gy", [(i, i ^ 1) for i in range(gy)])
-    far = lax.ppermute(far_edge, "gy", [(i, (i + 1 ^ 1) - 1) for i in range(1, gy - 1)])
-    c, total, xw, xi, xp, x_links, x_view = x_factor(loc, heat, t, b, columns * gy)
+    loc, heat, packed = edges(temperature, base, locations[None], energy[None])
+    near = swap(packed, "gy", 1)
+    far = lax.ppermute(
+        near, "gy", [(i, i + 2) for i in range(0, gy - 2, 2)] + [(i, i - 2) for i in range(3, gy, 2)]
+    )
+    t, b = (pltpu.with_memory_space_constraint(v, pltpu.VMEM) for v in (temperature, base))
+    c, total, xw, xi, xp, x_links, x_view = x_factor(loc, heat, t, b, columns * gy, near)
     xh, x_own, view = x_target(t, c, total, near, far, xw, xi, xp, x_links, x_view)
-    yw, yi, yp, inner, outer, y_view = y_factor(c, view)
+    yw, yi, yp, inner, outer, y_view = y_factor(c, x_view)
     zw, zi = z_factor(c, view)
-    own, got, ties = gather_line(view, "gx", (y_view, zw))
+    own, got, ties = gather_line(view, "gx", 2, (y_view, zw))
     yh, inner_own, outer_own, view = y_target(
         own, got, ties, xw, xh, xp, x_links, x_own, t, yw, yi, yp, inner, outer, y_view
     )

time: 28.9 us -> 30.5 us (1.055)
  waiting for transfers between devices: 7.95 us -> 9.41 us
    ppermute x7 -> x8, waiting for transfers between devices: 7.95 us -> 9.41 us  [the longest x7 9.4 us: swap(): return lax.ppermute(value, axis, [(i, i ^ flip) for i in range(count)])]
    pallas_call x5 -> x4, Pallas kernels: 3.51 us -> 3.59 us  [the longest x1 2.05 us: x_factor(): pl.pallas_call(functools.partial(x_factor_kernel, plate), in_specs=[IN_VM...]
    ppermute x7 -> x8, starting transfers between devices: 13.6 us -> 13.7 us  [the longest x7 8.92 us: swap(): return lax.ppermute(value, axis, [(i, i ^ flip) for i in range(count)])]
  transfers between devices with their start and end apart: 7 -> 8, of which waited for: 5 -> 6; matrix products, arithmetic and copies ran while one was open for 0% -> 0% of each run, Pallas kernels for 11% -> 10%
where the time goes in v4:
time: 30.5 us; the launch traced here: 30.4 us
  starting transfers between devices  13.7 us (45%)
  waiting for transfers between devices  9.41 us (31%)
  Pallas kernels  7.17 us (24%)
    ppermute x7, waiting for transfers between devices, swap(): return lax.ppermute(value, axis, [(i, i ^ flip) for i in range(count)])  9.4 us
    ppermute x7, starting transfers between devices, swap(): return lax.ppermute(value, axis, [(i, i ^ flip) for i in range(count)])  8.92 us
    ppermute x1, starting transfers between devices, per_device(): lax.ppermute(near, 'gy', [(i, i + 2) for i in range(0, gy - 2, 2)] + [(i,...  4.76 us
    pallas_call x1, Pallas kernels, x_factor(): pl.pallas_call(functools.partial(x_factor_kernel, plate), in_specs=[IN_VM...  2.05 us
    pallas_call x1, Pallas kernels, edges(): pl.pallas_call(edges_kernel, in_specs=[IN_HBM] * 4, out_shape=[pltpu.VMEM...  1.47 us
    pallas_call x1, Pallas kernels, finish(): pl.pallas_call(functools.partial(finish_kernel, len(ties) + 1), out_shape...  1.33 us
    pallas_call x1, Pallas kernels, y_factor(): pl.pallas_call(y_factor_kernel, in_specs=[IN_VMEM, ANYWHERE], out_shape=[...  0.91 us
    pallas_call x1, Pallas kernels, y_target(): pl.pallas_call(functools.partial(y_target_kernel, len(ties) + 1), out_sha...  0.78 us
  transfers between devices with their start and end apart: 8, of which 6 were waited for; matrix products, arithmetic and copies ran while one was open for 0% of the time, Pallas kernels for 10%

profile of v4, /device:TPU:0, one launch (start us, length us, event | category | flops | bytes accessed | tf_op | source)
XLA Modules:
  0.0 30.4 jit_solution(15307599566759836388)
XLA Ops:
  0.0 0.0 copy-start
  0.0 0.0 copy-start.1
  0.0 1.5 %shard_map.46 = (s32[1,64]{1,0:T(1,128)S(1)}, f32[1,64]{1,0:T(1,128)S(1)}, f32[64,128]{1,0:T(8,128)S(1)}) custom-call(f32[4,64,512]{2,1,0:T(8,128)} %refs_12_.1, f32[4,64,512]{2,1,0:T(8,128)} %b_ref.1, s32[1,64]{1,0:T(1,128)} %bitcast.2, f32[1,64]{1,0:T(1,128)} %bitcast.3), custom_call_target="tpu_custom_call" | custom-call | tf_op jit(solution)/shard_map/pallas_call | solution.py:165
  1.5 0.5 %collective-permute-start = (f32[64,128]{1,0:T(8,128)S(1)}, f32[64,128]{1,0:T(8,128)S(1)}, u32[]{:S(2)}, u32[]{:S(2)}) collective-permute-start(f32[64,128]{1,0:T(8,128)S(1)} %get-tuple-element.37), channel_id=1, source_target_pairs={{0,1},{1,0},{2,3},{3,2},{4,5},{5,4},{6,7},{7,6},{8,9},{9,8},{10,11... | collective-permute-start | bytes 98312 | tf_op jit(solution)/shard_map/ppermute | solution.py:388
  2.0 0.9 %collective-permute-done.after.near = f32[64,128]{1,0:T(8,128)S(1)} collective-permute-done((f32[64,128]{1,0:T(8,128)S(1)}, f32[64,128]{1,0:T(8,128)S(1)}, u32[]{:S(2)}, u32[]{:S(2)}) %collective-permute-start) | collective-permute-done | bytes 32800 | tf_op jit(solution)/shard_map/ppermute | solution.py:388
  2.9 4.8 %collective-permute-start.1 = (f32[64,128]{1,0:T(8,128)S(1)}, f32[64,128]{1,0:T(8,128)S(1)}, u32[]{:S(2)}, u32[]{:S(2)}) collective-permute-start(f32[64,128]{1,0:T(8,128)S(1)} %collective-permute-done.after.near), channel_id=1, source_target_pairs={{0,2},{3,1},{4,6},{7,5},{8,10},{11,9},{12,14},{15,13},{16,18},{19,... | collective-permute-start | bytes 98312 | tf_op jit(solution)/shard_map/ppermute | solution.py:770
  7.6 0.0 copy-done
  7.6 0.0 copy-done.1
  7.6 2.0 %shard_map.47 = (f32[4,4,64,128]{3,2,1,0:T(8,128)S(1)}, f32[4,4,64,128]{3,2,1,0:T(8,128)S(1)}, f32[8,16,8,128]{3,2,1,0:T(8,128)S(1)}, f32[8,16,8,128]{3,2,1,0:T(...) custom-call(s32[1,64]{1,0:T(1,128)S(1)} %get-tuple-element.35.loc, ...), custom_call_target="tpu_custom_call" | custom-call | flops 5242880 | bytes 3670016 | tf_op jit(solution)/shard_map/pallas_call | solution.py:288
  9.7 0.0 collective-permute-done.1.far
  9.7 0.4 %shard_map.48 = (f32[8,16,8,128]{3,2,1,0:T(8,128)S(1)}, f32[7,16,128]{2,1,0:T(8,128)S(1)}, f32[7,16,128]{2,1,0:T(8,128)S(1)}) custom-call(f32[4,64,512]{2,1,0:T(8,128)S(1)} %copy-done, f32[4,4,64,128]{3,2,1,0:T(8,128)S(1)} %get-tuple-element.38.c_ref, f32[4,4,64,128]{3,2,1,0:T(8,128)S(1)} %get-tuple-element.39.total_ref, ...), custom_call_target="tpu_custom_call" | custom-call | tf_op jit(solution)/shard_map/pallas_call | solution.py:367
  10.1 1.6 %collective-permute-start.2 = (f32[7,16,128]{2,1,0:T(8,128)S(1)}, f32[7,16,128]{2,1,0:T(8,128)S(1)}, u32[]{:S(2)}, u32[]{:S(2)}) collective-permute-start(f32[7,16,128]{2,1,0:T(8,128)S(1)} %get-tuple-element.45.after.refs_0_), channel_id=1, source_target_pairs={{0,4},{4,0},{8,12},{12,8},{16,20},{20,16},{24,28},{28,24},{1,5},{5... | collective-permute-start | bytes 172040 | tf_op jit(solution)/shard_map/ppermute | solution.py:388
  11.7 1.6 %collective-permute-start.3 = (f32[7,16,128]{2,1,0:T(8,128)S(1)}, f32[7,16,128]{2,1,0:T(8,128)S(1)}, u32[]{:S(2)}, u32[]{:S(2)}) collective-permute-start(f32[7,16,128]{2,1,0:T(8,128)S(1)} %get-tuple-element.45.after.refs_0_), channel_id=1, source_target_pairs={{0,8},{4,12},{8,0},{12,4},{16,24},{20,28},{24,16},{28,20},{1,9},{5... | collective-permute-start | bytes 172040 | tf_op jit(solution)/shard_map/ppermute | solution.py:388
  13.2 0.4 %collective-permute-start.4 = (f32[7,16,128]{2,1,0:T(8,128)S(1)}, f32[7,16,128]{2,1,0:T(8,128)S(1)}, u32[]{:S(2)}, u32[]{:S(2)}) collective-permute-start(f32[7,16,128]{2,1,0:T(8,128)S(1)} %get-tuple-element.45.after.refs_0_), channel_id=1, source_target_pairs={{0,12},{4,8},{8,4},{12,0},{16,28},{20,24},{24,20},{28,16},{1,13},{... | collective-permute-start | bytes 172040 | tf_op jit(solution)/shard_map/ppermute | solution.py:388
  13.7 0.9 %shard_map.49 = (f32[16,8,8,128]{3,2,1,0:T(8,128)S(1)}, f32[16,8,8,128]{3,2,1,0:T(8,128)S(1)}, f32[16,8,8,128]{3,2,1,0:T(8,128)S(1)}, f32[3,3,2,8,128]{4,3,2,1,0...) custom-call(f32[4,4,64,128]{3,2,1,0:T(8,128)S(1)} %get-tuple-element.38.c_ref, ...), custom_call_target="tpu_custom_call" | custom-call | flops 2621440 | bytes 2097152 | tf_op jit(solution)/shard_map/pallas_call | solution.py:535
  14.6 0.2 shard_map.50
  14.7 0.0 collective-permute-done.2.refs_1_
  14.8 1.1 %collective-permute-done.3.refs_2_ = f32[7,16,128]{2,1,0:T(8,128)S(1)} collective-permute-done((f32[7,16,128]{2,1,0:T(8,128)S(1)}, f32[7,16,128]{2,1,0:T(8,128)S(1)}, u32[]{:S(2)}, u32[]{:S(2)}) %collective-permute-start.3) | collective-permute-done | bytes 57376 | tf_op jit(solution)/shard_map/ppermute | solution.py:388
  15.9 2.5 %collective-permute-done.4.refs_3_ = f32[7,16,128]{2,1,0:T(8,128)S(1)} collective-permute-done((f32[7,16,128]{2,1,0:T(8,128)S(1)}, f32[7,16,128]{2,1,0:T(8,128)S(1)}, u32[]{:S(2)}, u32[]{:S(2)}) %collective-permute-start.4) | collective-permute-done | bytes 57376 | tf_op jit(solution)/shard_map/ppermute | solution.py:388
  18.3 0.1 shard_map.51
  18.4 2.9 %collective-permute-start.5 = (f32[3,16,128]{2,1,0:T(8,128)S(1)}, f32[3,16,128]{2,1,0:T(8,128)S(1)}, u32[]{:S(2)}, u32[]{:S(2)}) collective-permute-start(f32[3,16,128]{2,1,0:T(8,128)S(1)} %get-tuple-element.48.refs_0_), channel_id=1, source_target_pairs={{0,16},{4,20},{8,24},{12,28},{16,0},{20,4},{24,8},{28,12},{1,17},{... | collective-permute-start | bytes 73736 | tf_op jit(solution)/shard_map/ppermute | solution.py:388
  21.3 2.0 %collective-permute-done.5.refs_1_ = f32[3,16,128]{2,1,0:T(8,128)S(1)} collective-permute-done((f32[3,16,128]{2,1,0:T(8,128)S(1)}, f32[3,16,128]{2,1,0:T(8,128)S(1)}, u32[]{:S(2)}, u32[]{:S(2)}) %collective-permute-start.5) | collective-permute-done | bytes 24608 | tf_op jit(solution)/shard_map/ppermute | solution.py:388
  23.3 0.8 %shard_map.52 = (f32[16,8,8,128]{3,2,1,0:T(8,128)S(1)}, f32[3,2,8,128]{3,2,1,0:T(8,128)S(1)}, f32[7,2,128]{2,1,0:T(2,128)S(1)}, f32[7,2,128]{2,1,0:T(2,128)S(1)}) custom-call(f32[3,16,128]{2,1,0:T(8,128)S(1)} %get-tuple-element.48.refs_0_, f32[3,16,128]{2,1,0:T(8,128)S(1)} %collective-permute-done.5.refs_1_, f32[3,16,128]{2,1,0:T(8,128)S(1)} %get-tuple-element.49.refs_2_, ...), custom_call_target="tpu_custom_call" | custom-call | tf_op jit(solution)/shard_map/pallas_call | solution.py:671
  24.1 0.1 collective-permute-start.6
  24.2 1.2 %collective-permute-done.6.refs_1_ = f32[7,2,128]{2,1,0:T(2,128)S(1)} collective-permute-done((f32[7,2,128]{2,1,0:T(2,128)S(1)}, f32[7,2,128]{2,1,0:T(2,128)S(1)}, u32[]{:S(2)}, u32[]{:S(2)}) %collective-permute-start.6) | collective-permute-done | bytes 7200 | tf_op jit(solution)/shard_map/ppermute | solution.py:388
  25.4 1.9 %collective-permute-start.7 = (f32[3,2,128]{2,1,0:T(2,128)S(1)}, f32[3,2,128]{2,1,0:T(2,128)S(1)}, u32[]{:S(2)}, u32[]{:S(2)}) collective-permute-start(f32[3,2,128]{2,1,0:T(2,128)S(1)} %get-tuple-element.59.refs_0_), channel_id=1, source_target_pairs={{0,2},{1,3},{2,0},{3,1},{4,6},{5,7},{6,4},{7,5},{8,10},{9,11},{10,... | collective-permute-start | bytes 9224 | tf_op jit(solution)/shard_map/ppermute | solution.py:388
  27.2 1.8 %collective-permute-done.7.refs_1_ = f32[3,2,128]{2,1,0:T(2,128)S(1)} collective-permute-done((f32[3,2,128]{2,1,0:T(2,128)S(1)}, f32[3,2,128]{2,1,0:T(2,128)S(1)}, u32[]{:S(2)}, u32[]{:S(2)}) %collective-permute-start.7) | collective-permute-done | bytes 3104 | tf_op jit(solution)/shard_map/ppermute | solution.py:388
  29.0 1.3 %shard_map.54 = f32[4,64,512]{2,1,0:T(8,128)} custom-call(f32[3,2,128]{2,1,0:T(2,128)S(1)} %get-tuple-element.59.refs_0_, f32[3,2,128]{2,1,0:T(2,128)S(1)} %collective-permute-done.7.refs_1_, f32[3,2,128]{2,1,0:T(2,128)S(1)} %get-tuple-element.60.refs_2_, f32[16,8,8,128]{3,2,1,0:T(8,128)S(1)} %get-tuple-element.53.refs_10_.refs_3_, ...), custom_call_target="tpu_custom_call" | custom-call | tf_op jit(solution)/shard_map/pallas_call | solution.py:751
  (1 shorter events, 0.0 us)
Async XLA Ops:
  0.0 7.6 %copy-start = (f32[4,64,512]{2,1,0:T(8,128)S(1)}, f32[4,64,512]{2,1,0:T(8,128)}, u32[]{:S(2)}) copy-start(f32[4,64,512]{2,1,0:T(8,128)} %refs_12_.1) | copy-start | bytes 1572868
  0.0 7.6 %copy-start.1 = (f32[4,64,512]{2,1,0:T(8,128)S(1)}, f32[4,64,512]{2,1,0:T(8,128)}, u32[]{:S(2)}) copy-start(f32[4,64,512]{2,1,0:T(8,128)} %b_ref.1) | copy-start | bytes 1572868
  1.5 1.4 %collective-permute-start = (f32[64,128]{1,0:T(8,128)S(1)}, f32[64,128]{1,0:T(8,128)S(1)}, u32[]{:S(2)}, u32[]{:S(2)}) collective-permute-start(f32[64,128]{1,0:T(8,128)S(1)} %get-tuple-element.37), channel_id=1, source_target_pairs={{0,1},{1,0},{2,3},{3,2},{4,5},{5,4},{6,7},{7,6},{8,9},{9,8},{10,11... | collective-permute-start | bytes 98312 | tf_op jit(solution)/shard_map/ppermute | solution.py:388
  2.9 6.8 %collective-permute-start.1 = (f32[64,128]{1,0:T(8,128)S(1)}, f32[64,128]{1,0:T(8,128)S(1)}, u32[]{:S(2)}, u32[]{:S(2)}) collective-permute-start(f32[64,128]{1,0:T(8,128)S(1)} %collective-permute-done.after.near), channel_id=1, source_target_pairs={{0,2},{3,1},{4,6},{7,5},{8,10},{11,9},{12,14},{15,13},{16,18},{19,... | collective-permute-start | bytes 98312 | tf_op jit(solution)/shard_map/ppermute | solution.py:770
  10.1 4.6 %collective-permute-start.2 = (f32[7,16,128]{2,1,0:T(8,128)S(1)}, f32[7,16,128]{2,1,0:T(8,128)S(1)}, u32[]{:S(2)}, u32[]{:S(2)}) collective-permute-start(f32[7,16,128]{2,1,0:T(8,128)S(1)} %get-tuple-element.45.after.refs_0_), channel_id=1, source_target_pairs={{0,4},{4,0},{8,12},{12,8},{16,20},{20,16},{24,28},{28,24},{1,5},{5... | collective-permute-start | bytes 172040 | tf_op jit(solution)/shard_map/ppermute | solution.py:388
  11.7 4.2 %collective-permute-start.3 = (f32[7,16,128]{2,1,0:T(8,128)S(1)}, f32[7,16,128]{2,1,0:T(8,128)S(1)}, u32[]{:S(2)}, u32[]{:S(2)}) collective-permute-start(f32[7,16,128]{2,1,0:T(8,128)S(1)} %get-tuple-element.45.after.refs_0_), channel_id=1, source_target_pairs={{0,8},{4,12},{8,0},{12,4},{16,24},{20,28},{24,16},{28,20},{1,9},{5... | collective-permute-start | bytes 172040 | tf_op jit(solution)/shard_map/ppermute | solution.py:388
  13.2 5.1 %collective-permute-start.4 = (f32[7,16,128]{2,1,0:T(8,128)S(1)}, f32[7,16,128]{2,1,0:T(8,128)S(1)}, u32[]{:S(2)}, u32[]{:S(2)}) collective-permute-start(f32[7,16,128]{2,1,0:T(8,128)S(1)} %get-tuple-element.45.after.refs_0_), channel_id=1, source_target_pairs={{0,12},{4,8},{8,4},{12,0},{16,28},{20,24},{24,20},{28,16},{1,13},{... | collective-permute-start | bytes 172040 | tf_op jit(solution)/shard_map/ppermute | solution.py:388
  18.4 4.9 %collective-permute-start.5 = (f32[3,16,128]{2,1,0:T(8,128)S(1)}, f32[3,16,128]{2,1,0:T(8,128)S(1)}, u32[]{:S(2)}, u32[]{:S(2)}) collective-permute-start(f32[3,16,128]{2,1,0:T(8,128)S(1)} %get-tuple-element.48.refs_0_), channel_id=1, source_target_pairs={{0,16},{4,20},{8,24},{12,28},{16,0},{20,4},{24,8},{28,12},{1,17},{... | collective-permute-start | bytes 73736 | tf_op jit(solution)/shard_map/ppermute | solution.py:388
  24.1 1.2 %collective-permute-start.6 = (f32[7,2,128]{2,1,0:T(2,128)S(1)}, f32[7,2,128]{2,1,0:T(2,128)S(1)}, u32[]{:S(2)}, u32[]{:S(2)}) collective-permute-start(f32[7,2,128]{2,1,0:T(2,128)S(1)} %get-tuple-element.58.refs_0_), channel_id=1, source_target_pairs={{0,1},{1,0},{2,3},{3,2},{4,5},{5,4},{6,7},{7,6},{8,9},{9,8},{10,11... | collective-permute-start | bytes 21512 | tf_op jit(solution)/shard_map/ppermute | solution.py:388
  25.4 3.7 %collective-permute-start.7 = (f32[3,2,128]{2,1,0:T(2,128)S(1)}, f32[3,2,128]{2,1,0:T(2,128)S(1)}, u32[]{:S(2)}, u32[]{:S(2)}) collective-permute-start(f32[3,2,128]{2,1,0:T(2,128)S(1)} %get-tuple-element.59.refs_0_), channel_id=1, source_target_pairs={{0,2},{1,3},{2,0},{3,1},{4,6},{5,7},{6,4},{7,5},{8,10},{9,11},{10,... | collective-permute-start | bytes 9224 | tf_op jit(solution)/shard_map/ppermute | solution.py:388

commit v5 on v4

--- a/solution.py
+++ b/solution.py
@@ -303,13 +303,24 @@
     )(loc, energy, t, b, after)
 
 
-def x_target_kernel(t_ref, c_ref, total_ref, near, far, w_ref, i_ref, p_ref, links, view, h_ref, own, send, e_s, q_s):
+def far_side(sources):
+    place = lax.axis_index("gy")
+    paired = (place >> 1) % 2 != place % 2
+    nothing = jnp.zeros(sources[0].shape, F32)
+    by_pair = sources[1][...] if len(sources) > 1 else nothing
+    other = sources[2][...] if len(sources) > 2 else nothing
+    return jnp.where(paired, by_pair, other)
+
+
+def x_target_kernel(count, t_ref, c_ref, total_ref, *refs):
+    w_ref, i_ref, p_ref, links, view, h_ref, own, send, e_s, q_s = refs[count:]
     chunks, sheets, rows, _ = c_ref.shape
     lines = chunks * sheets
     steps = rows // SUBLANES
 
-    before = jnp.where(is_odd("gy"), near[...], far[...])
-    after = jnp.where(is_odd("gy"), far[...], near[...])
+    near, far = refs[0][...], far_side(refs[:count])
+    before = jnp.where(is_odd("gy"), near, far)
+    after = jnp.where(is_odd("gy"), far, near)
     lane = lax.broadcasted_iota(jnp.int32, (rows, LANES), 1)
     for y, halo, edge, place in ((0, before, 0, 0), (chunks - 1, after, LANES - 1, 1)):
         for z in range(sheets):
@@ -360,12 +371,12 @@
     send[FIRST], send[LAST] = items[0]
 
 
-def x_target(t, c, total, near, far, w, inv, p, links, view):
+def x_target(t, c, total, edge_cells, w, inv, p, links, view):
     chunks, sheets, rows, _ = c.shape
     lines = chunks * sheets
     steps = rows // SUBLANES
     return pl.pallas_call(
-        x_target_kernel,
+        functools.partial(x_target_kernel, len(edge_cells)),
         out_shape=[
             shape_of(steps, lines, SUBLANES, LANES),
             shape_of(SUBLANES - 1, lines, LANES),
@@ -376,7 +387,7 @@
             pltpu.VMEM((2, lines * SUBLANES, LANES), F32),
         ],
         compiler_params=params(),
-    )(t, c, total, near, far, w, inv, p, links, view)
+    )(t, c, total, *edge_cells, w, inv, p, links, view)
 
 
 def stages_of(axis):
@@ -413,12 +424,13 @@
 
 
 def join_kernel(axis, stage, width, last, *refs):
-    blocks = [[refs[i][q] for q in range(7)] for i in range(1 << width)]
+    count = 1 << width
+    blocks = [[refs[-i % count][q] for q in range(7)] for i in range(count)]
     send = refs[-1 - width]
     links = refs[-width:]
     for bit in range(width):
         right = on_right(axis, stage + bit)
-        for i in range(1 << width):
+        for i in range(count):
             if not i >> bit & 1:
                 j = i | 1 << bit
                 blocks[i], blocks[j] = ordered(right, blocks[i], blocks[j])
@@ -458,7 +470,7 @@
     links, stage = [], 0
     while stage < stages - 1:
         width = min(widest, stages - 1 - stage)
-        got = [swap(view, axis, flip << stage) for flip in range(1, 1 << width)]
+        got = [swap(view, axis, flip << stage) for flip in range((1 << width) - 1, 0, -1)]
         last = stage + width == stages - 1
         view, *ties = join_stage(view, got, axis, stage, width, last, meanwhile)
         links += ties
@@ -767,12 +779,12 @@
     gy = lax.axis_size("gy")
     loc, heat, packed = edges(temperature, base, locations[None], energy[None])
     near = swap(packed, "gy", 1)
-    far = lax.ppermute(
-        near, "gy", [(i, i + 2) for i in range(0, gy - 2, 2)] + [(i, i - 2) for i in range(3, gy, 2)]
-    )
+    far = [swap(near, "gy", 2)] if gy > 2 else []
+    if gy > 4:
+        far.append(lax.ppermute(near, "gy", [(i, (i + 2 ^ 2) - 2) for i in range(2, gy - 2)]))
     t, b = (pltpu.with_memory_space_constraint(v, pltpu.VMEM) for v in (temperature, base))
     c, total, xw, xi, xp, x_links, x_view = x_factor(loc, heat, t, b, columns * gy, near)
-    xh, x_own, view = x_target(t, c, total, near, far, xw, xi, xp, x_links, x_view)
+    xh, x_own, view = x_target(t, c, total, [near] + far, xw, xi, xp, x_links, x_view)
     yw, yi, yp, inner, outer, y_view = y_factor(c, x_view)
     zw, zi = z_factor(c, view)
     own, got, ties = gather_line(view, "gx", 2, (y_view, zw))

time: 30.5 us -> 27.7 us (0.908)
  starting transfers between devices: 13.7 us -> 11.2 us
    ppermute x1 -> x0, starting transfers between devices: 4.76 us -> none  [per_device(): lax.ppermute(near, 'gy', [(i, i + 2) for i in range(0, gy - 2, 2)] + [(i,...]
    ppermute x7 -> x8, starting transfers between devices: 8.92 us -> 11.2 us  [swap(): return lax.ppermute(value, axis, [(i, i ^ flip) for i in range(count)])]
    ppermute x7 -> x8, waiting for transfers between devices: 9.4 us -> 9.11 us  [swap(): return lax.ppermute(value, axis, [(i, i ^ flip) for i in range(count)])]
  transfers between devices with their start and end apart: 8 -> 8, of which waited for: 6 -> 7; matrix products, arithmetic and copies ran while one was open for 0% -> 0% of each run, Pallas kernels for 10% -> 11%
where the time goes in v5:
time: 27.7 us; the launch traced here: 27.6 us
  starting transfers between devices  11.2 us (40%)
  waiting for transfers between devices  9.11 us (33%)
  Pallas kernels  7.17 us (26%)
    ppermute x8, starting transfers between devices, swap(): return lax.ppermute(value, axis, [(i, i ^ flip) for i in range(count)])  11.2 us
    ppermute x8, waiting for transfers between devices, swap(): return lax.ppermute(value, axis, [(i, i ^ flip) for i in range(count)])  9.11 us
    pallas_call x1, Pallas kernels, x_factor(): pl.pallas_call(functools.partial(x_factor_kernel, plate), in_specs=[IN_VM...  2.05 us
    pallas_call x1, Pallas kernels, edges(): pl.pallas_call(edges_kernel, in_specs=[IN_HBM] * 4, out_shape=[pltpu.VMEM...  1.47 us
    pallas_call x1, Pallas kernels, finish(): pl.pallas_call(functools.partial(finish_kernel, len(ties) + 1), out_shape...  1.33 us
    pallas_call x1, Pallas kernels, y_factor(): pl.pallas_call(y_factor_kernel, in_specs=[IN_VMEM, ANYWHERE], out_shape=[...  0.91 us
    pallas_call x1, Pallas kernels, y_target(): pl.pallas_call(functools.partial(y_target_kernel, len(ties) + 1), out_sha...  0.78 us
  transfers between devices with their start and end apart: 8, of which 7 were waited for; matrix products, arithmetic and copies ran while one was open for 0% of the time, Pallas kernels for 11%

profile of v5, /device:TPU:0, one launch (start us, length us, event | category | flops | bytes accessed | tf_op | source)
XLA Modules:
  0.0 27.6 jit_solution(13283105131523249395)
XLA Ops:
  0.0 0.0 copy-start
  0.0 0.0 copy-start.1
  0.0 1.5 %shard_map.46 = (s32[1,64]{1,0:T(1,128)S(1)}, f32[1,64]{1,0:T(1,128)S(1)}, f32[64,128]{1,0:T(8,128)S(1)}) custom-call(f32[4,64,512]{2,1,0:T(8,128)} %refs_12_.1, f32[4,64,512]{2,1,0:T(8,128)} %b_ref.1, s32[1,64]{1,0:T(1,128)} %bitcast.2, f32[1,64]{1,0:T(1,128)} %bitcast.3), custom_call_target="tpu_custom_call" | custom-call | tf_op jit(solution)/shard_map/pallas_call | solution.py:165
  1.5 0.5 %collective-permute-start = (f32[64,128]{1,0:T(8,128)S(1)}, f32[64,128]{1,0:T(8,128)S(1)}, u32[]{:S(2)}, u32[]{:S(2)}) collective-permute-start(f32[64,128]{1,0:T(8,128)S(1)} %get-tuple-element.37), channel_id=1, source_target_pairs={{0,1},{1,0},{2,3},{3,2},{4,5},{5,4},{6,7},{7,6},{8,9},{9,8},{10,11... | collective-permute-start | bytes 98312 | tf_op jit(solution)/shard_map/ppermute | solution.py:399
  2.0 0.9 %collective-permute-done.after.refs_0_ = f32[64,128]{1,0:T(8,128)S(1)} collective-permute-done((f32[64,128]{1,0:T(8,128)S(1)}, f32[64,128]{1,0:T(8,128)S(1)}, u32[]{:S(2)}, u32[]{:S(2)}) %collective-permute-start) | collective-permute-done | bytes 32800 | tf_op jit(solution)/shard_map/ppermute | solution.py:399
  2.9 2.9 %collective-permute-start.1 = (f32[64,128]{1,0:T(8,128)S(1)}, f32[64,128]{1,0:T(8,128)S(1)}, u32[]{:S(2)}, u32[]{:S(2)}) collective-permute-start(f32[64,128]{1,0:T(8,128)S(1)} %collective-permute-done.after.refs_0_), channel_id=1, source_target_pairs={{0,2},{1,3},{2,0},{3,1},{4,6},{5,7},{6,4},{7,5},{8,10},{9,11},{10,... | collective-permute-start | bytes 98312 | tf_op jit(solution)/shard_map/ppermute | solution.py:399
  5.7 0.0 copy-done
  5.7 0.0 copy-done.1
  5.7 2.0 %shard_map.47 = (f32[4,4,64,128]{3,2,1,0:T(8,128)S(1)}, f32[4,4,64,128]{3,2,1,0:T(8,128)S(1)}, f32[8,16,8,128]{3,2,1,0:T(8,128)S(1)}, f32[8,16,8,128]{3,2,1,0:T(...) custom-call(s32[1,64]{1,0:T(1,128)S(1)} %get-tuple-element.35.loc, ...), custom_call_target="tpu_custom_call" | custom-call | flops 5242880 | bytes 3670016 | tf_op jit(solution)/shard_map/pallas_call | solution.py:288
  7.8 0.0 collective-permute-done.1.refs_1_
  7.8 0.4 %shard_map.48 = (f32[8,16,8,128]{3,2,1,0:T(8,128)S(1)}, f32[7,16,128]{2,1,0:T(8,128)S(1)}, f32[7,16,128]{2,1,0:T(8,128)S(1)}) custom-call(f32[4,64,512]{2,1,0:T(8,128)S(1)} %copy-done, f32[4,4,64,128]{3,2,1,0:T(8,128)S(1)} %get-tuple-element.38.c_ref, f32[4,4,64,128]{3,2,1,0:T(8,128)S(1)} %get-tuple-element.39.total_ref, ...), custom_call_target="tpu_custom_call" | custom-call | tf_op jit(solution)/shard_map/pallas_call | solution.py:378
  8.2 2.9 %collective-permute-start.2 = (f32[7,16,128]{2,1,0:T(8,128)S(1)}, f32[7,16,128]{2,1,0:T(8,128)S(1)}, u32[]{:S(2)}, u32[]{:S(2)}) collective-permute-start(f32[7,16,128]{2,1,0:T(8,128)S(1)} %get-tuple-element.45.after.refs_0_), channel_id=1, source_target_pairs={{0,12},{4,8},{8,4},{12,0},{16,28},{20,24},{24,20},{28,16},{1,13},{... | collective-permute-start | bytes 172040 | tf_op jit(solution)/shard_map/ppermute | solution.py:399
  11.1 0.4 %collective-permute-start.3 = (f32[7,16,128]{2,1,0:T(8,128)S(1)}, f32[7,16,128]{2,1,0:T(8,128)S(1)}, u32[]{:S(2)}, u32[]{:S(2)}) collective-permute-start(f32[7,16,128]{2,1,0:T(8,128)S(1)} %get-tuple-element.45.after.refs_0_), channel_id=1, source_target_pairs={{0,8},{4,12},{8,0},{12,4},{16,24},{20,28},{24,16},{28,20},{1,9},{5... | collective-permute-start | bytes 172040 | tf_op jit(solution)/shard_map/ppermute | solution.py:399
  11.5 0.2 collective-permute-start.4
  11.8 0.9 %shard_map.49 = (f32[16,8,8,128]{3,2,1,0:T(8,128)S(1)}, f32[16,8,8,128]{3,2,1,0:T(8,128)S(1)}, f32[16,8,8,128]{3,2,1,0:T(8,128)S(1)}, f32[3,3,2,8,128]{4,3,2,1,0...) custom-call(f32[4,4,64,128]{3,2,1,0:T(8,128)S(1)} %get-tuple-element.38.c_ref, ...), custom_call_target="tpu_custom_call" | custom-call | flops 2621440 | bytes 2097152 | tf_op jit(solution)/shard_map/pallas_call | solution.py:547
  12.7 0.2 shard_map.50
  12.8 0.9 %collective-permute-done.2.refs_1_ = f32[7,16,128]{2,1,0:T(8,128)S(1)} collective-permute-done((f32[7,16,128]{2,1,0:T(8,128)S(1)}, f32[7,16,128]{2,1,0:T(8,128)S(1)}, u32[]{:S(2)}, u32[]{:S(2)}) %collective-permute-start.2) | collective-permute-done | bytes 57376 | tf_op jit(solution)/shard_map/ppermute | solution.py:399
  13.7 1.5 %collective-permute-done.3.refs_2_ = f32[7,16,128]{2,1,0:T(8,128)S(1)} collective-permute-done((f32[7,16,128]{2,1,0:T(8,128)S(1)}, f32[7,16,128]{2,1,0:T(8,128)S(1)}, u32[]{:S(2)}, u32[]{:S(2)}) %collective-permute-start.3) | collective-permute-done | bytes 57376 | tf_op jit(solution)/shard_map/ppermute | solution.py:399
  15.3 0.4 %collective-permute-done.4.refs_3_ = f32[7,16,128]{2,1,0:T(8,128)S(1)} collective-permute-done((f32[7,16,128]{2,1,0:T(8,128)S(1)}, f32[7,16,128]{2,1,0:T(8,128)S(1)}, u32[]{:S(2)}, u32[]{:S(2)}) %collective-permute-start.4) | collective-permute-done | bytes 57376 | tf_op jit(solution)/shard_map/ppermute | solution.py:399
  15.7 0.1 shard_map.51
  15.8 2.7 %collective-permute-start.5 = (f32[3,16,128]{2,1,0:T(8,128)S(1)}, f32[3,16,128]{2,1,0:T(8,128)S(1)}, u32[]{:S(2)}, u32[]{:S(2)}) collective-permute-start(f32[3,16,128]{2,1,0:T(8,128)S(1)} %get-tuple-element.48.refs_0_), channel_id=1, source_target_pairs={{0,16},{4,20},{8,24},{12,28},{16,0},{20,4},{24,8},{28,12},{1,17},{... | collective-permute-start | bytes 73736 | tf_op jit(solution)/shard_map/ppermute | solution.py:399
  18.4 2.1 %collective-permute-done.5.refs_1_ = f32[3,16,128]{2,1,0:T(8,128)S(1)} collective-permute-done((f32[3,16,128]{2,1,0:T(8,128)S(1)}, f32[3,16,128]{2,1,0:T(8,128)S(1)}, u32[]{:S(2)}, u32[]{:S(2)}) %collective-permute-start.5) | collective-permute-done | bytes 24608 | tf_op jit(solution)/shard_map/ppermute | solution.py:399
  20.6 0.8 %shard_map.52 = (f32[16,8,8,128]{3,2,1,0:T(8,128)S(1)}, f32[3,2,8,128]{3,2,1,0:T(8,128)S(1)}, f32[7,2,128]{2,1,0:T(2,128)S(1)}, f32[7,2,128]{2,1,0:T(2,128)S(1)}) custom-call(f32[3,16,128]{2,1,0:T(8,128)S(1)} %get-tuple-element.48.refs_0_, f32[3,16,128]{2,1,0:T(8,128)S(1)} %collective-permute-done.5.refs_1_, f32[3,16,128]{2,1,0:T(8,128)S(1)} %get-tuple-element.49.refs_2_, ...), custom_call_target="tpu_custom_call" | custom-call | tf_op jit(solution)/shard_map/pallas_call | solution.py:683
  21.3 0.1 collective-permute-start.6
  21.4 1.2 %collective-permute-done.6.refs_1_ = f32[7,2,128]{2,1,0:T(2,128)S(1)} collective-permute-done((f32[7,2,128]{2,1,0:T(2,128)S(1)}, f32[7,2,128]{2,1,0:T(2,128)S(1)}, u32[]{:S(2)}, u32[]{:S(2)}) %collective-permute-start.6) | collective-permute-done | bytes 7200 | tf_op jit(solution)/shard_map/ppermute | solution.py:399
  22.6 1.6 %collective-permute-start.7 = (f32[3,2,128]{2,1,0:T(2,128)S(1)}, f32[3,2,128]{2,1,0:T(2,128)S(1)}, u32[]{:S(2)}, u32[]{:S(2)}) collective-permute-start(f32[3,2,128]{2,1,0:T(2,128)S(1)} %get-tuple-element.59.refs_0_), channel_id=1, source_target_pairs={{0,2},{1,3},{2,0},{3,1},{4,6},{5,7},{6,4},{7,5},{8,10},{9,11},{10,... | collective-permute-start | bytes 9224 | tf_op jit(solution)/shard_map/ppermute | solution.py:399
  24.2 2.1 %collective-permute-done.7.refs_1_ = f32[3,2,128]{2,1,0:T(2,128)S(1)} collective-permute-done((f32[3,2,128]{2,1,0:T(2,128)S(1)}, f32[3,2,128]{2,1,0:T(2,128)S(1)}, u32[]{:S(2)}, u32[]{:S(2)}) %collective-permute-start.7) | collective-permute-done | bytes 3104 | tf_op jit(solution)/shard_map/ppermute | solution.py:399
  26.3 1.3 %shard_map.54 = f32[4,64,512]{2,1,0:T(8,128)} custom-call(f32[3,2,128]{2,1,0:T(2,128)S(1)} %get-tuple-element.59.refs_0_, f32[3,2,128]{2,1,0:T(2,128)S(1)} %collective-permute-done.7.refs_1_, f32[3,2,128]{2,1,0:T(2,128)S(1)} %get-tuple-element.60.refs_2_, f32[16,8,8,128]{3,2,1,0:T(8,128)S(1)} %get-tuple-element.53.refs_10_.refs_3_, ...), custom_call_target="tpu_custom_call" | custom-call | tf_op jit(solution)/shard_map/pallas_call | solution.py:763
  (1 shorter events, 0.0 us)
Async XLA Ops:
  0.0 5.7 %copy-start = (f32[4,64,512]{2,1,0:T(8,128)S(1)}, f32[4,64,512]{2,1,0:T(8,128)}, u32[]{:S(2)}) copy-start(f32[4,64,512]{2,1,0:T(8,128)} %refs_12_.1) | copy-start | bytes 1572868
  0.0 5.7 %copy-start.1 = (f32[4,64,512]{2,1,0:T(8,128)S(1)}, f32[4,64,512]{2,1,0:T(8,128)}, u32[]{:S(2)}) copy-start(f32[4,64,512]{2,1,0:T(8,128)} %b_ref.1) | copy-start | bytes 1572868
  1.5 1.4 %collective-permute-start = (f32[64,128]{1,0:T(8,128)S(1)}, f32[64,128]{1,0:T(8,128)S(1)}, u32[]{:S(2)}, u32[]{:S(2)}) collective-permute-start(f32[64,128]{1,0:T(8,128)S(1)} %get-tuple-element.37), channel_id=1, source_target_pairs={{0,1},{1,0},{2,3},{3,2},{4,5},{5,4},{6,7},{7,6},{8,9},{9,8},{10,11... | collective-permute-start | bytes 98312 | tf_op jit(solution)/shard_map/ppermute | solution.py:399
  2.9 4.9 %collective-permute-start.1 = (f32[64,128]{1,0:T(8,128)S(1)}, f32[64,128]{1,0:T(8,128)S(1)}, u32[]{:S(2)}, u32[]{:S(2)}) collective-permute-start(f32[64,128]{1,0:T(8,128)S(1)} %collective-permute-done.after.refs_0_), channel_id=1, source_target_pairs={{0,2},{1,3},{2,0},{3,1},{4,6},{5,7},{6,4},{7,5},{8,10},{9,11},{10,... | collective-permute-start | bytes 98312 | tf_op jit(solution)/shard_map/ppermute | solution.py:399
  8.2 5.5 %collective-permute-start.2 = (f32[7,16,128]{2,1,0:T(8,128)S(1)}, f32[7,16,128]{2,1,0:T(8,128)S(1)}, u32[]{:S(2)}, u32[]{:S(2)}) collective-permute-start(f32[7,16,128]{2,1,0:T(8,128)S(1)} %get-tuple-element.45.after.refs_0_), channel_id=1, source_target_pairs={{0,12},{4,8},{8,4},{12,0},{16,28},{20,24},{24,20},{28,16},{1,13},{... | collective-permute-start | bytes 172040 | tf_op jit(solution)/shard_map/ppermute | solution.py:399
  11.1 4.2 %collective-permute-start.3 = (f32[7,16,128]{2,1,0:T(8,128)S(1)}, f32[7,16,128]{2,1,0:T(8,128)S(1)}, u32[]{:S(2)}, u32[]{:S(2)}) collective-permute-start(f32[7,16,128]{2,1,0:T(8,128)S(1)} %get-tuple-element.45.after.refs_0_), channel_id=1, source_target_pairs={{0,8},{4,12},{8,0},{12,4},{16,24},{20,28},{24,16},{28,20},{1,9},{5... | collective-permute-start | bytes 172040 | tf_op jit(solution)/shard_map/ppermute | solution.py:399
  11.5 4.2 %collective-permute-start.4 = (f32[7,16,128]{2,1,0:T(8,128)S(1)}, f32[7,16,128]{2,1,0:T(8,128)S(1)}, u32[]{:S(2)}, u32[]{:S(2)}) collective-permute-start(f32[7,16,128]{2,1,0:T(8,128)S(1)} %get-tuple-element.45.after.refs_0_), channel_id=1, source_target_pairs={{0,4},{4,0},{8,12},{12,8},{16,20},{20,16},{24,28},{28,24},{1,5},{5... | collective-permute-start | bytes 172040 | tf_op jit(solution)/shard_map/ppermute | solution.py:399
  15.8 4.8 %collective-permute-start.5 = (f32[3,16,128]{2,1,0:T(8,128)S(1)}, f32[3,16,128]{2,1,0:T(8,128)S(1)}, u32[]{:S(2)}, u32[]{:S(2)}) collective-permute-start(f32[3,16,128]{2,1,0:T(8,128)S(1)} %get-tuple-element.48.refs_0_), channel_id=1, source_target_pairs={{0,16},{4,20},{8,24},{12,28},{16,0},{20,4},{24,8},{28,12},{1,17},{... | collective-permute-start | bytes 73736 | tf_op jit(solution)/shard_map/ppermute | solution.py:399
  21.3 1.2 %collective-permute-start.6 = (f32[7,2,128]{2,1,0:T(2,128)S(1)}, f32[7,2,128]{2,1,0:T(2,128)S(1)}, u32[]{:S(2)}, u32[]{:S(2)}) collective-permute-start(f32[7,2,128]{2,1,0:T(2,128)S(1)} %get-tuple-element.58.refs_0_), channel_id=1, source_target_pairs={{0,1},{1,0},{2,3},{3,2},{4,5},{5,4},{6,7},{7,6},{8,9},{9,8},{10,11... | collective-permute-start | bytes 21512 | tf_op jit(solution)/shard_map/ppermute | solution.py:399
  22.6 3.7 %collective-permute-start.7 = (f32[3,2,128]{2,1,0:T(2,128)S(1)}, f32[3,2,128]{2,1,0:T(2,128)S(1)}, u32[]{:S(2)}, u32[]{:S(2)}) collective-permute-start(f32[3,2,128]{2,1,0:T(2,128)S(1)} %get-tuple-element.59.refs_0_), channel_id=1, source_target_pairs={{0,2},{1,3},{2,0},{3,1},{4,6},{5,7},{6,4},{7,5},{8,10},{9,11},{10,... | collective-permute-start | bytes 9224 | tf_op jit(solution)/shard_map/ppermute | solution.py:399

commit v6 on v5

--- a/solution.py
+++ b/solution.py
@@ -141,8 +141,10 @@
     ]
     for side, start in enumerate((0, columns - LANES)):
         for i, (src, dst) in enumerate(((t_hbm, t_s), (b_hbm, b_s))):
-            part = src.at[:, :, pl.ds(start, LANES)]
-            copies.append(pltpu.make_async_copy(part, dst.at[side], sems.at[i, side]))
+            for z in range(sheets):
+                part = src.at[z, :, pl.ds(start, LANES)]
+                place = side * sheets + z
+                copies.append(pltpu.make_async_copy(part, dst.at[side, z], sems.at[i, place]))
     for copy in copies:
         copy.start()
     for copy in copies:
@@ -173,10 +175,34 @@
         scratch_shapes=[
             pltpu.VMEM((2, sheets, rows, LANES), F32),
             pltpu.VMEM((2, sheets, rows, LANES), F32),
-            pltpu.SemaphoreType.DMA((3, 2)),
+            pltpu.SemaphoreType.DMA((3, 2 * sheets)),
         ],
         compiler_params=params(),
     )(*[pltpu.with_memory_space_constraint(v, pltpu.HBM) for v in operands])
+
+
+def load_kernel(t_hbm, b_hbm, after, t_out, b_out, sems):
+    sheets = t_hbm.shape[0]
+    copies = []
+    for i, (src, dst) in enumerate(((t_hbm, t_out), (b_hbm, b_out))):
+        for z in range(sheets):
+            copies.append(pltpu.make_async_copy(src.at[z], dst.at[z], sems.at[i, z]))
+    for copy in copies:
+        copy.start()
+    for copy in copies:
+        copy.wait()
+
+
+def load(temperature, base, after):
+    fields = [pltpu.with_memory_space_constraint(v, pltpu.HBM) for v in (temperature, base)]
+    return pl.pallas_call(
+        load_kernel,
+        in_specs=[IN_HBM] * 2 + [ANYWHERE],
+        out_shape=[pltpu.VMEM(temperature.shape, F32)] * 2,
+        scratch_shapes=[pltpu.SemaphoreType.DMA((2, temperature.shape[0]))],
+        compiler_params=params(),
+        cost_estimate=pl.CostEstimate(flops=0, bytes_accessed=16 * temperature.size, transcendentals=0),
+    )(*fields, after)
 
 
 def source_plane(loc, energy, rows, columns, plate):
@@ -206,8 +232,33 @@
     return slice(y * LANES, (y + 1) * LANES)
 
 
+def line_groups(chunks, sheets):
+    order = [0, chunks - 1] + list(range(1, chunks - 1))
+    return [[(y, z) for y in order[i : i + 2] for z in range(sheets)] for i in range(0, chunks, 2)]
+
+
+def x_eliminate(field, members, first_line, w_ref, i_ref, p_ref, h_ref, h_line, q_s):
+    steps = w_ref.shape[0]
+    at = slice(first_line, first_line + len(members))
+    kept_at = slice(h_line, h_line + len(members))
+
+    def target(k):
+        return jnp.stack([field(y, z)[pl.ds(k, SUBLANES, stride=steps), :] for y, z in members], 0)
+
+    def keep(k, h):
+        h_ref[k, kept_at] = h
+
+    ends = eliminate(
+        target, steps, lambda k: w_ref[k, at], lambda k: i_ref[k, at], lambda k: p_ref[k, at], keep
+    )
+    for q in range(2):
+        for i in range(len(members)):
+            first = (first_line + i) * SUBLANES
+            q_s[q, first : first + SUBLANES, :] = ends[q][i]
+
+
 def x_factor_kernel(plate, loc, energy, t_ref, b_ref, after, *refs):
-    c_ref, total_ref, w_ref, i_ref, p_ref, links, view, q_s = refs
+    c_ref, total_ref, w_ref, i_ref, p_ref, links, view, h_ref, ends_ref, q_s = refs
     chunks, sheets, rows, _ = c_ref.shape
     lines = chunks * sheets
     steps = rows // SUBLANES
@@ -246,24 +297,28 @@
                 c_ref[y, z, at, :] = cs[y]
             before_t, before_c = ts, cs
 
-    group = max(1, 8 // sheets)
-    for y in range(0, chunks, group):
-        members = [(y + i, z) for i in range(group) for z in range(sheets)]
-        at = slice(y * sheets, (y + group) * sheets)
+    at = 0
+    for n, members in enumerate(line_groups(chunks, sheets)):
 
         def cond(k):
-            return jnp.stack([c_ref[i, z, pl.ds(k, SUBLANES, stride=steps), :] for i, z in members], 0)
+            return jnp.stack([c_ref[y, z, pl.ds(k, SUBLANES, stride=steps), :] for y, z in members], 0)
 
         def keep(k, w, inv, p):
-            w_ref[k, at] = w
-            i_ref[k, at] = inv
-            p_ref[k, at] = p
+            w_ref[k, at : at + len(members)] = w
+            i_ref[k, at : at + len(members)] = inv
+            p_ref[k, at : at + len(members)] = p
 
         block = factor(cond, steps, keep)
-        for n, q in enumerate(COEFS):
-            for i in range(len(members)):
-                first = (y * sheets + i) * SUBLANES
-                q_s[n, first : first + SUBLANES, :] = block[q][i]
+        for i, q in enumerate(COEFS):
+            for j in range(len(members)):
+                first = (at + j) * SUBLANES
+                q_s[i, first : first + SUBLANES, :] = block[q][j]
+        if n > 0:
+            x_eliminate(
+                lambda y, z: total_ref.at[y, z], members, at, w_ref, i_ref, p_ref, h_ref,
+                at - 2 * sheets, ends_ref,
+            )
+        at += len(members)
 
     segments = [
         {q: q_s[n, pl.ds(s, lines, stride=SUBLANES), :] for n, q in enumerate(COEFS)}
@@ -296,6 +351,8 @@
             stored,
             shape_of(SUBLANES - 1, 3, lines, LANES),
             shape_of(len(COEFS), lines, LANES),
+            shape_of(steps, max(1, lines - 2 * sheets), SUBLANES, LANES),
+            shape_of(2, lines * SUBLANES, LANES),
         ],
         scratch_shapes=[pltpu.VMEM((len(COEFS), lines * SUBLANES, LANES), F32)],
         compiler_params=params(),
@@ -312,51 +369,42 @@
     return jnp.where(paired, by_pair, other)
 
 
-def x_target_kernel(count, t_ref, c_ref, total_ref, *refs):
-    w_ref, i_ref, p_ref, links, view, h_ref, own, send, e_s, q_s = refs[count:]
-    chunks, sheets, rows, _ = c_ref.shape
+def x_target_kernel(count, own_cells, t_ref, total_ref, *refs):
+    w_ref, i_ref, p_ref, links, view, ends_ref, h_ref, own, send, e_s, q_s = refs[count:]
+    chunks, sheets, rows, _ = total_ref.shape
     lines = chunks * sheets
-    steps = rows // SUBLANES
 
     near, far = refs[0][...], far_side(refs[:count])
     before = jnp.where(is_odd("gy"), near, far)
     after = jnp.where(is_odd("gy"), far, near)
     lane = lax.broadcasted_iota(jnp.int32, (rows, LANES), 1)
-    for y, halo, edge, place in ((0, before, 0, 0), (chunks - 1, after, LANES - 1, 1)):
+    side = 2 * sheets
+    beyond = jnp.where(lane < side, pltpu.roll(before, LANES - side, 1), pltpu.roll(after, side, 1))
+    mine = own_cells[...]
+    face = jnp.where(beyond > 0.0, mine + beyond, 0.0)
+    flux = pltpu.roll(face, LANES - sheets, 1) * (beyond - mine)
+    for n, (y, edge) in enumerate(((0, 0), (chunks - 1, LANES - 1))):
         for z in range(sheets):
-            at = z if place else 2 * sheets + z
-            t_next = halo[:, at : at + 1]
-            c_next = halo[:, at + sheets : at + sheets + 1]
-            face = jnp.where(c_next > 0.0, c_ref[y, z] + c_next, 0.0)
-            flux = jnp.where(lane == edge, face * (t_next - t_ref[z, :, part_of(y)]), 0.0)
-            base = total_ref[y, z] if place == 0 or chunks > 1 else e_s[0, z]
-            e_s[place, z] = base + flux
-
-    def field(y, z):
-        if y == chunks - 1:
-            return e_s.at[1, z]
-        return e_s.at[0, z] if y == 0 else total_ref.at[y, z]
-
-    group = max(1, 8 // sheets)
-    for y in range(0, chunks, group):
-        members = [(y + i, z) for i in range(group) for z in range(sheets)]
-        at = slice(y * sheets, (y + group) * sheets)
-
-        def target(k):
-            return jnp.stack([field(i, z)[pl.ds(k, SUBLANES, stride=steps), :] for i, z in members], 0)
-
-        def keep(k, h):
-            h_ref[k, at] = h
-
-        ends = eliminate(
-            target, steps, lambda k: w_ref[k, at], lambda k: i_ref[k, at], lambda k: p_ref[k, at], keep
+            at = n * side + z
+            e_s[n, z] = total_ref[y, z] + jnp.where(lane == edge, flux[:, at : at + 1], 0.0)
+
+    members = line_groups(chunks, sheets)[0]
+    x_eliminate(
+        lambda y, z: e_s.at[0 if y == 0 else 1, z], members, 0, w_ref, i_ref, p_ref, h_ref, 0, q_s
+    )
+    split = len(members)
+    items = [
+        tuple(
+            jnp.concatenate(
+                [
+                    q_s[q, pl.ds(s, split, stride=SUBLANES), :],
+                    ends_ref[q, pl.ds(split * SUBLANES + s, lines - split, stride=SUBLANES), :],
+                ],
+                0,
+            )
+            for q in range(2)
         )
-        for q in range(2):
-            for i in range(len(members)):
-                first = (y * sheets + i) * SUBLANES
-                q_s[q, first : first + SUBLANES, :] = ends[q][i]
-    items = [
-        tuple(q_s[q, pl.ds(s, lines, stride=SUBLANES), :] for q in range(2)) for s in range(SUBLANES)
+        for s in range(SUBLANES)
     ]
     for offset, count in node_offsets(SUBLANES):
         joined = []
@@ -371,23 +419,23 @@
     send[FIRST], send[LAST] = items[0]
 
 
-def x_target(t, c, total, edge_cells, w, inv, p, links, view):
-    chunks, sheets, rows, _ = c.shape
+def x_target(own_cells, t, total, edge_cells, w, inv, p, links, view, ends):
+    chunks, sheets, rows, _ = total.shape
     lines = chunks * sheets
     steps = rows // SUBLANES
     return pl.pallas_call(
         functools.partial(x_target_kernel, len(edge_cells)),
         out_shape=[
-            shape_of(steps, lines, SUBLANES, LANES),
+            shape_of(steps, 2 * sheets, SUBLANES, LANES),
             shape_of(SUBLANES - 1, lines, LANES),
             shape_of(7, lines, LANES),
         ],
         scratch_shapes=[
             pltpu.VMEM((2, sheets, rows, LANES), F32),
-            pltpu.VMEM((2, lines * SUBLANES, LANES), F32),
+            pltpu.VMEM((2, 2 * sheets * SUBLANES, LANES), F32),
         ],
         compiler_params=params(),
-    )(t, c, total, *edge_cells, w, inv, p, links, view)
+    )(own_cells, t, total, *edge_cells, w, inv, p, links, view, ends)
 
 
 def stages_of(axis):
@@ -594,9 +642,9 @@
 def y_target_kernel(stages, *refs):
     own, got = refs[:2]
     ties = refs[2 : 1 + stages]
-    xw, xh, xp, x_links, x_own, t_ref, yw, yi, yp, inner, outer, view = refs[1 + stages : 13 + stages]
-    h_ref, inner_own, outer_own, send = refs[13 + stages : 17 + stages]
-    f_s, g_s, y_s, q_s = refs[17 + stages :]
+    xw, xh, xm, xp, x_links, x_own, t_ref, yw, yi, yp, inner, outer, view = refs[1 + stages : 14 + stages]
+    h_ref, inner_own, outer_own, send = refs[14 + stages : 18 + stages]
+    f_s, g_s, y_s, q_s = refs[18 + stages :]
     chunks, sheets, rows, _ = g_s.shape
     lines = chunks * sheets
     x_steps = rows // SUBLANES
@@ -609,24 +657,21 @@
     for s, ends in enumerate(descend(levels, low, high)):
         for i in range(2):
             f_s[i, pl.ds(s, lines, stride=SUBLANES), :] = ends[i]
-    group = max(1, 8 // sheets)
-    for y in range(0, chunks, group):
-        members = [(y + i, z) for i in range(group) for z in range(sheets)]
-        at = slice(y * sheets, (y + group) * sheets)
+    first = 0
+    for n, members in enumerate(line_groups(chunks, sheets)):
+        at = slice(first, first + len(members))
+        h_ref_of, h_at = (xh, at) if n == 0 else (xm, slice(first - 2 * sheets, at.stop - 2 * sheets))
         low, value = (
             jnp.stack(
-                [
-                    f_s[i, (y * sheets + n) * SUBLANES : (y * sheets + n + 1) * SUBLANES, :]
-                    for n in range(len(members))
-                ],
-                0,
+                [f_s[i, j * SUBLANES : (j + 1) * SUBLANES, :] for j in range(at.start, at.stop)], 0
             )
             for i in range(2)
         )
         for k in range(x_steps - 1, -1, -1):
-            value = xw[k, at] * value + (xh[k, at] + xp[k, at] * low)
-            for n, (i, z) in enumerate(members):
-                g_s[i, z, pl.ds(k, SUBLANES, stride=x_steps), :] = value[n]
+            value = xw[k, at] * value + (h_ref_of[k, h_at] + xp[k, at] * low)
+            for j, (y, z) in enumerate(members):
+                g_s[y, z, pl.ds(k, SUBLANES, stride=x_steps), :] = value[j]
+        first = at.stop
 
     each = LANES // rows
     pairs = sheets // each
@@ -675,7 +720,7 @@
     send[FIRST], send[LAST] = items[0]
 
 
-def y_target(own, got, ties, xw, xh, xp, x_links, x_own, t, yw, yi, yp, inner, outer, view):
+def y_target(own, got, ties, xw, xh, xm, xp, x_links, x_own, t, yw, yi, yp, inner, outer, view):
     sheets, rows, columns = t.shape
     chunks = columns // LANES
     lines = chunks * sheets
@@ -695,7 +740,7 @@
             pltpu.VMEM((2, pairs * SUBLANES, LANES), F32),
         ],
         compiler_params=params(),
-    )(own, got, *ties, xw, xh, xp, x_links, x_own, t, yw, yi, yp, inner, outer, view)
+    )(own, got, *ties, xw, xh, xm, xp, x_links, x_own, t, yw, yi, yp, inner, outer, view)
 
 
 def finish_kernel(stages, *refs):
@@ -738,20 +783,25 @@
     for y in range(chunks):
         part = part_of(y)
         turned = [u_s[m, part, :].T for m in range(pairs)]
-        rhs, kept = None, []
-        for z in range(sheets):
-            first = (z % each) * rows
-            own_rhs = turned[z // each][first : first + rows, :]
-            rhs = own_rhs if z == 0 else own_rhs + zw[z - 1, y] * rhs
-            kept.append(rhs * zi[z, y])
-        value = kept[-1]
-        o_s[y, sheets - 1] = t_ref[sheets - 1, :, part] + value
-        for z in range(sheets - 2, -1, -1):
-            value = zw[z, y] * value + kept[z]
-            o_s[y, z] = t_ref[z, :, part] + value
-        copy = pltpu.make_async_copy(o_s.at[y], out.at[:, :, pl.ds(y * LANES, LANES)], sems.at[y])
-        copy.start()
-        copies.append(copy)
+        for half in range(2):
+            at = slice(half * rows // 2, (half + 1) * rows // 2)
+            rhs, kept = None, []
+            for z in range(sheets):
+                first = (z % each) * rows + at.start
+                own_rhs = turned[z // each][first : first + rows // 2, :]
+                rhs = own_rhs if z == 0 else own_rhs + zw[z - 1, y, at, :] * rhs
+                kept.append(rhs * zi[z, y, at, :])
+            value = kept[-1]
+            o_s[y, sheets - 1, at, :] = t_ref[sheets - 1, at, part] + value
+            for z in range(sheets - 2, -1, -1):
+                value = zw[z, y, at, :] * value + kept[z]
+                o_s[y, z, at, :] = t_ref[z, at, part] + value
+            strip = pl.ds(at.start, rows // 2)
+            copy = pltpu.make_async_copy(
+                o_s.at[y, :, strip, :], out.at[:, strip, pl.ds(y * LANES, LANES)], sems.at[y, half]
+            )
+            copy.start()
+            copies.append(copy)
     for copy in copies:
         copy.wait()
 
@@ -768,7 +818,7 @@
             pltpu.VMEM((2, pairs * SUBLANES, LANES), F32),
             pltpu.VMEM((pairs, chunks * LANES, LANES), F32),
             pltpu.VMEM((chunks, sheets, rows, LANES), F32),
-            pltpu.SemaphoreType.DMA((chunks,)),
+            pltpu.SemaphoreType.DMA((chunks, 2)),
         ],
         compiler_params=params(),
     )(own, got, *ties, yw, yh, yp, inner, inner_own, outer, outer_own, zw, zi, t)
@@ -779,17 +829,18 @@
     gy = lax.axis_size("gy")
     loc, heat, packed = edges(temperature, base, locations[None], energy[None])
     near = swap(packed, "gy", 1)
+    t, b = load(temperature, base, packed)
+    near, t, b = lax.optimization_barrier((near, t, b))
     far = [swap(near, "gy", 2)] if gy > 2 else []
     if gy > 4:
         far.append(lax.ppermute(near, "gy", [(i, (i + 2 ^ 2) - 2) for i in range(2, gy - 2)]))
-    t, b = (pltpu.with_memory_space_constraint(v, pltpu.VMEM) for v in (temperature, base))
-    c, total, xw, xi, xp, x_links, x_view = x_factor(loc, heat, t, b, columns * gy, near)
-    xh, x_own, view = x_target(t, c, total, [near] + far, xw, xi, xp, x_links, x_view)
+    c, total, xw, xi, xp, x_links, x_view, xm, ends = x_factor(loc, heat, t, b, columns * gy, near)
+    xh, x_own, view = x_target(packed, t, total, [near] + far, xw, xi, xp, x_links, x_view, ends)
     yw, yi, yp, inner, outer, y_view = y_factor(c, x_view)
     zw, zi = z_factor(c, view)
     own, got, ties = gather_line(view, "gx", 2, (y_view, zw))
     yh, inner_own, outer_own, view = y_target(
-        own, got, ties, xw, xh, xp, x_links, x_own, t, yw, yi, yp, inner, outer, y_view
+        own, got, ties, xw, xh, xm, xp, x_links, x_own, t, yw, yi, yp, inner, outer, y_view
     )
     own, got, ties = gather_line(view, "gy")
     return finish(own, got, ties, yw, yh, yp, inner, inner_own, outer, outer_own, zw, zi, t)

time: 27.7 us -> 28.3 us (1.022)
  Pallas kernels: 7.17 us -> 8.76 us
  waiting for transfers between devices: 9.11 us -> 8.23 us
    pallas_call x0 -> x1, Pallas kernels: none -> 1.35 us  [load(): pl.pallas_call(load_kernel, in_specs=[IN_HBM] * 2 + [ANYWHERE], out_shape...]
    ppermute x8, waiting for transfers between devices: 9.11 us -> 8.23 us  [swap(): return lax.ppermute(value, axis, [(i, i ^ flip) for i in range(count)])]
  transfers between devices with their start and end apart: 8 -> 8, of which waited for: 7 -> 6; matrix products, arithmetic and copies ran while one was open for 0% -> 0% of each run, Pallas kernels for 11% -> 16%
where the time goes in v6:
time: 28.3 us; the launch traced here: 28.1 us
  starting transfers between devices  11 us (39%)
  Pallas kernels  8.76 us (31%)
  waiting for transfers between devices  8.23 us (29%)
    ppermute x8, starting transfers between devices, swap(): return lax.ppermute(value, axis, [(i, i ^ flip) for i in range(count)])  11 us
    ppermute x8, waiting for transfers between devices, swap(): return lax.ppermute(value, axis, [(i, i ^ flip) for i in range(count)])  8.23 us
    pallas_call x1, Pallas kernels, x_factor(): pl.pallas_call(functools.partial(x_factor_kernel, plate), in_specs=[IN_VM...  2.07 us
    pallas_call x1, Pallas kernels, finish(): pl.pallas_call(functools.partial(finish_kernel, len(ties) + 1), out_shape...  1.61 us
    pallas_call x1, Pallas kernels, edges(): pl.pallas_call(edges_kernel, in_specs=[IN_HBM] * 4, out_shape=[pltpu.VMEM...  1.44 us
    pallas_call x1, Pallas kernels, load(): pl.pallas_call(load_kernel, in_specs=[IN_HBM] * 2 + [ANYWHERE], out_shape...  1.35 us
    pallas_call x1, Pallas kernels, y_factor(): pl.pallas_call(y_factor_kernel, in_specs=[IN_VMEM, ANYWHERE], out_shape=[...  0.91 us
    pallas_call x1, Pallas kernels, y_target(): pl.pallas_call(functools.partial(y_target_kernel, len(ties) + 1), out_sha...  0.78 us
  transfers between devices with their start and end apart: 8, of which 6 were waited for; matrix products, arithmetic and copies ran while one was open for 0% of the time, Pallas kernels for 16%

profile of v6, /device:TPU:0, one launch (start us, length us, event | category | flops | bytes accessed | tf_op | source)
XLA Modules:
  0.0 28.1 jit_solution(3415283071166952461)
XLA Ops:
  0.0 1.4 %shard_map.46 = (s32[1,64]{1,0:T(1,128)S(1)}, f32[1,64]{1,0:T(1,128)S(1)}, f32[64,128]{1,0:T(8,128)S(1)}) custom-call(f32[4,64,512]{2,1,0:T(8,128)} %t_hbm.3, f32[4,64,512]{2,1,0:T(8,128)} %b_hbm.3, s32[1,64]{1,0:T(1,128)} %bitcast.2, f32[1,64]{1,0:T(1,128)} %bitcast.3), custom_call_target="tpu_custom_call" | custom-call | tf_op jit(solution)/shard_map/pallas_call | solution.py:167
  1.4 0.5 %collective-permute-start = (f32[64,128]{1,0:T(8,128)S(1)}, f32[64,128]{1,0:T(8,128)S(1)}, u32[]{:S(2)}, u32[]{:S(2)}) collective-permute-start(f32[64,128]{1,0:T(8,128)S(1)} %get-tuple-element.42.after.own_cells), channel_id=1, source_target_pairs={{0,1},{1,0},{2,3},{3,2},{4,5},{5,4},{6,7},{7,6},{8,9},{9,8},{10,11... | collective-permute-start | bytes 98312 | tf_op jit(solution)/shard_map/ppermute | solution.py:447
  2.0 1.3 %shard_map.47 = (f32[4,64,512]{2,1,0:T(8,128)S(1)}, f32[4,64,512]{2,1,0:T(8,128)S(1)}) custom-call(f32[4,64,512]{2,1,0:T(8,128)} %t_hbm.3, f32[4,64,512]{2,1,0:T(8,128)} %b_hbm.3, f32[64,128]{1,0:T(8,128)S(1)} %get-tuple-element.42.after.own_cells), custom_call_target="tpu_custom_call" | custom-call | bytes 2097152 | tf_op jit(solution)/shard_map/pallas_call | solution.py:198
  3.3 0.0 collective-permute-done.after.refs_0_
  3.3 2.6 %collective-permute-start.1 = (f32[64,128]{1,0:T(8,128)S(1)}, f32[64,128]{1,0:T(8,128)S(1)}, u32[]{:S(2)}, u32[]{:S(2)}) collective-permute-start(f32[64,128]{1,0:T(8,128)S(1)} %collective-permute-done.after.refs_0_), channel_id=1, source_target_pairs={{0,2},{1,3},{2,0},{3,1},{4,6},{5,7},{6,4},{7,5},{8,10},{9,11},{10,... | collective-permute-start | bytes 98312 | tf_op jit(solution)/shard_map/ppermute | solution.py:447
  5.9 2.1 %shard_map.48 = (f32[4,4,64,128]{3,2,1,0:T(8,128)S(1)}, f32[4,4,64,128]{3,2,1,0:T(8,128)S(1)}, f32[8,16,8,128]{3,2,1,0:T(8,128)S(1)}, f32[8,16,8,128]{3,2,1,0:T(...) custom-call(s32[1,64]{1,0:T(1,128)S(1)} %get-tuple-element.46.loc, ...), custom_call_target="tpu_custom_call" | custom-call | flops 5242880 | bytes 3670016 | tf_op jit(solution)/shard_map/pallas_call | solution.py:343
  8.0 0.0 collective-permute-done.1.refs_1_
  8.0 0.4 %shard_map.49 = (f32[8,8,8,128]{3,2,1,0:T(8,128)S(1)}, f32[7,16,128]{2,1,0:T(8,128)S(1)}, f32[7,16,128]{2,1,0:T(8,128)S(1)}) custom-call(f32[64,128]{1,0:T(8,128)S(1)} %get-tuple-element.42.after.own_cells, f32[4,64,512]{2,1,0:T(8,128)S(1)} %get-tuple-element.45.t_ref.refs_10_.refs_12_, f32[4,4,64,128]{3,2,1,0:T(8,128)S(1)} %get-tuple-element.50.total_ref, ...), custom_call_target="tpu_custom_call" | custom-call | tf_op jit(solution)/shard_map/pallas_call | solution.py:426
  8.4 2.9 %collective-permute-start.2 = (f32[7,16,128]{2,1,0:T(8,128)S(1)}, f32[7,16,128]{2,1,0:T(8,128)S(1)}, u32[]{:S(2)}, u32[]{:S(2)}) collective-permute-start(f32[7,16,128]{2,1,0:T(8,128)S(1)} %get-tuple-element.57.after.refs_0_), channel_id=1, source_target_pairs={{0,12},{4,8},{8,4},{12,0},{16,28},{20,24},{24,20},{28,16},{1,13},{... | collective-permute-start | bytes 172040 | tf_op jit(solution)/shard_map/ppermute | solution.py:447
  11.3 0.4 %collective-permute-start.3 = (f32[7,16,128]{2,1,0:T(8,128)S(1)}, f32[7,16,128]{2,1,0:T(8,128)S(1)}, u32[]{:S(2)}, u32[]{:S(2)}) collective-permute-start(f32[7,16,128]{2,1,0:T(8,128)S(1)} %get-tuple-element.57.after.refs_0_), channel_id=1, source_target_pairs={{0,8},{4,12},{8,0},{12,4},{16,24},{20,28},{24,16},{28,20},{1,9},{5... | collective-permute-start | bytes 172040 | tf_op jit(solution)/shard_map/ppermute | solution.py:447
  11.7 0.2 collective-permute-start.4
  12.0 0.9 %shard_map.50 = (f32[16,8,8,128]{3,2,1,0:T(8,128)S(1)}, f32[16,8,8,128]{3,2,1,0:T(8,128)S(1)}, f32[16,8,8,128]{3,2,1,0:T(8,128)S(1)}, f32[3,3,2,8,128]{4,3,2,1,0...) custom-call(f32[4,4,64,128]{3,2,1,0:T(8,128)S(1)} %get-tuple-element.58.c_ref, ...), custom_call_target="tpu_custom_call" | custom-call | flops 2621440 | bytes 2097152 | tf_op jit(solution)/shard_map/pallas_call | solution.py:595
  12.9 0.2 shard_map.51
  13.1 0.6 %collective-permute-done.2.refs_1_ = f32[7,16,128]{2,1,0:T(8,128)S(1)} collective-permute-done((f32[7,16,128]{2,1,0:T(8,128)S(1)}, f32[7,16,128]{2,1,0:T(8,128)S(1)}, u32[]{:S(2)}, u32[]{:S(2)}) %collective-permute-start.2) | collective-permute-done | bytes 57376 | tf_op jit(solution)/shard_map/ppermute | solution.py:447
  13.7 1.8 %collective-permute-done.3.refs_2_ = f32[7,16,128]{2,1,0:T(8,128)S(1)} collective-permute-done((f32[7,16,128]{2,1,0:T(8,128)S(1)}, f32[7,16,128]{2,1,0:T(8,128)S(1)}, u32[]{:S(2)}, u32[]{:S(2)}) %collective-permute-start.3) | collective-permute-done | bytes 57376 | tf_op jit(solution)/shard_map/ppermute | solution.py:447
  15.5 0.4 %collective-permute-done.4.refs_3_ = f32[7,16,128]{2,1,0:T(8,128)S(1)} collective-permute-done((f32[7,16,128]{2,1,0:T(8,128)S(1)}, f32[7,16,128]{2,1,0:T(8,128)S(1)}, u32[]{:S(2)}, u32[]{:S(2)}) %collective-permute-start.4) | collective-permute-done | bytes 57376 | tf_op jit(solution)/shard_map/ppermute | solution.py:447
  15.9 0.1 shard_map.52
  16.0 2.7 %collective-permute-start.5 = (f32[3,16,128]{2,1,0:T(8,128)S(1)}, f32[3,16,128]{2,1,0:T(8,128)S(1)}, u32[]{:S(2)}, u32[]{:S(2)}) collective-permute-start(f32[3,16,128]{2,1,0:T(8,128)S(1)} %get-tuple-element.61.refs_0_), channel_id=1, source_target_pairs={{0,16},{4,20},{8,24},{12,28},{16,0},{20,4},{24,8},{28,12},{1,17},{... | collective-permute-start | bytes 73736 | tf_op jit(solution)/shard_map/ppermute | solution.py:447
  18.6 2.1 %collective-permute-done.5.refs_1_ = f32[3,16,128]{2,1,0:T(8,128)S(1)} collective-permute-done((f32[3,16,128]{2,1,0:T(8,128)S(1)}, f32[3,16,128]{2,1,0:T(8,128)S(1)}, u32[]{:S(2)}, u32[]{:S(2)}) %collective-permute-start.5) | collective-permute-done | bytes 24608 | tf_op jit(solution)/shard_map/ppermute | solution.py:447
  20.8 0.8 %shard_map.53 = (f32[16,8,8,128]{3,2,1,0:T(8,128)S(1)}, f32[3,2,8,128]{3,2,1,0:T(8,128)S(1)}, f32[7,2,128]{2,1,0:T(2,128)S(1)}, f32[7,2,128]{2,1,0:T(2,128)S(1)}) custom-call(f32[3,16,128]{2,1,0:T(8,128)S(1)} %get-tuple-element.61.refs_0_, f32[3,16,128]{2,1,0:T(8,128)S(1)} %collective-permute-done.5.refs_1_, f32[3,16,128]{2,1,0:T(8,128)S(1)} %get-tuple-element.62.refs_2_, ...), custom_call_target="tpu_custom_call" | custom-call | tf_op jit(solution)/shard_map/pallas_call | solution.py:728
  21.5 0.1 collective-permute-start.6
  21.6 1.2 %collective-permute-done.6.refs_1_ = f32[7,2,128]{2,1,0:T(2,128)S(1)} collective-permute-done((f32[7,2,128]{2,1,0:T(2,128)S(1)}, f32[7,2,128]{2,1,0:T(2,128)S(1)}, u32[]{:S(2)}, u32[]{:S(2)}) %collective-permute-start.6) | collective-permute-done | bytes 7200 | tf_op jit(solution)/shard_map/ppermute | solution.py:447
  22.8 1.6 %collective-permute-start.7 = (f32[3,2,128]{2,1,0:T(2,128)S(1)}, f32[3,2,128]{2,1,0:T(2,128)S(1)}, u32[]{:S(2)}, u32[]{:S(2)}) collective-permute-start(f32[3,2,128]{2,1,0:T(2,128)S(1)} %get-tuple-element.73.refs_0_), channel_id=1, source_target_pairs={{0,2},{1,3},{2,0},{3,1},{4,6},{5,7},{6,4},{7,5},{8,10},{9,11},{10,... | collective-permute-start | bytes 9224 | tf_op jit(solution)/shard_map/ppermute | solution.py:447
  24.4 2.1 %collective-permute-done.7.refs_1_ = f32[3,2,128]{2,1,0:T(2,128)S(1)} collective-permute-done((f32[3,2,128]{2,1,0:T(2,128)S(1)}, f32[3,2,128]{2,1,0:T(2,128)S(1)}, u32[]{:S(2)}, u32[]{:S(2)}) %collective-permute-start.7) | collective-permute-done | bytes 3104 | tf_op jit(solution)/shard_map/ppermute | solution.py:447
  26.5 1.6 %shard_map.55 = f32[4,64,512]{2,1,0:T(8,128)} custom-call(f32[3,2,128]{2,1,0:T(2,128)S(1)} %get-tuple-element.73.refs_0_, f32[3,2,128]{2,1,0:T(2,128)S(1)} %collective-permute-done.7.refs_1_, f32[3,2,128]{2,1,0:T(2,128)S(1)} %get-tuple-element.74.refs_2_, f32[16,8,8,128]{3,2,1,0:T(8,128)S(1)} %get-tuple-element.67.refs_11_.refs_3_, ...), custom_call_target="tpu_custom_call" | custom-call | tf_op jit(solution)/shard_map/pallas_call | solution.py:813
  (1 shorter events, 0.0 us)
Async XLA Ops:
  1.4 1.9 %collective-permute-start = (f32[64,128]{1,0:T(8,128)S(1)}, f32[64,128]{1,0:T(8,128)S(1)}, u32[]{:S(2)}, u32[]{:S(2)}) collective-permute-start(f32[64,128]{1,0:T(8,128)S(1)} %get-tuple-element.42.after.own_cells), channel_id=1, source_target_pairs={{0,1},{1,0},{2,3},{3,2},{4,5},{5,4},{6,7},{7,6},{8,9},{9,8},{10,11... | collective-permute-start | bytes 98312 | tf_op jit(solution)/shard_map/ppermute | solution.py:447
  3.3 4.7 %collective-permute-start.1 = (f32[64,128]{1,0:T(8,128)S(1)}, f32[64,128]{1,0:T(8,128)S(1)}, u32[]{:S(2)}, u32[]{:S(2)}) collective-permute-start(f32[64,128]{1,0:T(8,128)S(1)} %collective-permute-done.after.refs_0_), channel_id=1, source_target_pairs={{0,2},{1,3},{2,0},{3,1},{4,6},{5,7},{6,4},{7,5},{8,10},{9,11},{10,... | collective-permute-start | bytes 98312 | tf_op jit(solution)/shard_map/ppermute | solution.py:447
  8.4 5.3 %collective-permute-start.2 = (f32[7,16,128]{2,1,0:T(8,128)S(1)}, f32[7,16,128]{2,1,0:T(8,128)S(1)}, u32[]{:S(2)}, u32[]{:S(2)}) collective-permute-start(f32[7,16,128]{2,1,0:T(8,128)S(1)} %get-tuple-element.57.after.refs_0_), channel_id=1, source_target_pairs={{0,12},{4,8},{8,4},{12,0},{16,28},{20,24},{24,20},{28,16},{1,13},{... | collective-permute-start | bytes 172040 | tf_op jit(solution)/shard_map/ppermute | solution.py:447
  11.3 4.2 %collective-permute-start.3 = (f32[7,16,128]{2,1,0:T(8,128)S(1)}, f32[7,16,128]{2,1,0:T(8,128)S(1)}, u32[]{:S(2)}, u32[]{:S(2)}) collective-permute-start(f32[7,16,128]{2,1,0:T(8,128)S(1)} %get-tuple-element.57.after.refs_0_), channel_id=1, source_target_pairs={{0,8},{4,12},{8,0},{12,4},{16,24},{20,28},{24,16},{28,20},{1,9},{5... | collective-permute-start | bytes 172040 | tf_op jit(solution)/shard_map/ppermute | solution.py:447
  11.7 4.2 %collective-permute-start.4 = (f32[7,16,128]{2,1,0:T(8,128)S(1)}, f32[7,16,128]{2,1,0:T(8,128)S(1)}, u32[]{:S(2)}, u32[]{:S(2)}) collective-permute-start(f32[7,16,128]{2,1,0:T(8,128)S(1)} %get-tuple-element.57.after.refs_0_), channel_id=1, source_target_pairs={{0,4},{4,0},{8,12},{12,8},{16,20},{20,16},{24,28},{28,24},{1,5},{5... | collective-permute-start | bytes 172040 | tf_op jit(solution)/shard_map/ppermute | solution.py:447
  16.0 4.8 %collective-permute-start.5 = (f32[3,16,128]{2,1,0:T(8,128)S(1)}, f32[3,16,128]{2,1,0:T(8,128)S(1)}, u32[]{:S(2)}, u32[]{:S(2)}) collective-permute-start(f32[3,16,128]{2,1,0:T(8,128)S(1)} %get-tuple-element.61.refs_0_), channel_id=1, source_target_pairs={{0,16},{4,20},{8,24},{12,28},{16,0},{20,4},{24,8},{28,12},{1,17},{... | collective-permute-start | bytes 73736 | tf_op jit(solution)/shard_map/ppermute | solution.py:447
  21.5 1.2 %collective-permute-start.6 = (f32[7,2,128]{2,1,0:T(2,128)S(1)}, f32[7,2,128]{2,1,0:T(2,128)S(1)}, u32[]{:S(2)}, u32[]{:S(2)}) collective-permute-start(f32[7,2,128]{2,1,0:T(2,128)S(1)} %get-tuple-element.72.refs_0_), channel_id=1, source_target_pairs={{0,1},{1,0},{2,3},{3,2},{4,5},{5,4},{6,7},{7,6},{8,9},{9,8},{10,11... | collective-permute-start | bytes 21512 | tf_op jit(solution)/shard_map/ppermute | solution.py:447
  22.8 3.7 %collective-permute-start.7 = (f32[3,2,128]{2,1,0:T(2,128)S(1)}, f32[3,2,128]{2,1,0:T(2,128)S(1)}, u32[]{:S(2)}, u32[]{:S(2)}) collective-permute-start(f32[3,2,128]{2,1,0:T(2,128)S(1)} %get-tuple-element.73.refs_0_), channel_id=1, source_target_pairs={{0,2},{1,3},{2,0},{3,1},{4,6},{5,7},{6,4},{7,5},{8,10},{9,11},{10,... | collective-permute-start | bytes 9224 | tf_op jit(solution)/shard_map/ppermute | solution.py:447

commit v7 on v6

--- a/solution.py
+++ b/solution.py
@@ -12,6 +12,7 @@
 LANES = 128
 SUBLANES = 8
 Y_PARTS = 4
+OUT_COPIES = 4
 F32 = jnp.float32
 MIB = 1024 * 1024
 ANYWHERE = pl.BlockSpec(memory_space=pl.ANY)
@@ -133,25 +134,23 @@
     return lax.axis_index(axis) % 2 == 1
 
 
-def edges_kernel(t_hbm, b_hbm, loc_hbm, energy_hbm, loc, energy, packed, t_s, b_s, sems):
+def edges_kernel(t_hbm, b_hbm, packed, t_s, b_s, sems):
     sheets, rows, columns = t_hbm.shape
-    copies = [
-        pltpu.make_async_copy(loc_hbm, loc, sems.at[2, 0]),
-        pltpu.make_async_copy(energy_hbm, energy, sems.at[2, 1]),
-    ]
+    sides = []
     for side, start in enumerate((0, columns - LANES)):
-        for i, (src, dst) in enumerate(((t_hbm, t_s), (b_hbm, b_s))):
-            for z in range(sheets):
-                part = src.at[z, :, pl.ds(start, LANES)]
-                place = side * sheets + z
-                copies.append(pltpu.make_async_copy(part, dst.at[side, z], sems.at[i, place]))
-    for copy in copies:
-        copy.start()
-    for copy in copies:
-        copy.wait()
+        sides.append(
+            [
+                pltpu.make_async_copy(src.at[:, :, pl.ds(start, LANES)], dst.at[side], sems.at[i, side])
+                for i, (src, dst) in enumerate(((t_hbm, t_s), (b_hbm, b_s)))
+            ]
+        )
+        for copy in sides[-1]:
+            copy.start()
     lane = lax.broadcasted_iota(jnp.int32, (rows, LANES), 1)
     total = jnp.zeros((rows, LANES), F32)
     for side, source in enumerate((0, LANES - 1)):
+        for copy in sides[side]:
+            copy.wait()
         for z in range(sheets):
             t = t_s[side, z]
             c = half_conduct(b_s[side, z], t)
@@ -161,48 +160,44 @@
     packed[...] = total
 
 
-def edges(temperature, base, locations, energy):
+def edges(temperature, base):
     sheets, rows, _ = temperature.shape
-    operands = (temperature, base, locations, energy)
     return pl.pallas_call(
         edges_kernel,
-        in_specs=[IN_HBM] * 4,
-        out_shape=[
-            pltpu.VMEM(locations.shape, jnp.int32),
-            pltpu.VMEM(energy.shape, F32),
-            pltpu.VMEM((rows, LANES), F32),
-        ],
+        in_specs=[IN_HBM] * 2,
+        out_shape=pltpu.VMEM((rows, LANES), F32),
         scratch_shapes=[
             pltpu.VMEM((2, sheets, rows, LANES), F32),
             pltpu.VMEM((2, sheets, rows, LANES), F32),
-            pltpu.SemaphoreType.DMA((3, 2 * sheets)),
+            pltpu.SemaphoreType.DMA((2, 2)),
         ],
         compiler_params=params(),
-    )(*[pltpu.with_memory_space_constraint(v, pltpu.HBM) for v in operands])
-
-
-def load_kernel(t_hbm, b_hbm, after, t_out, b_out, sems):
-    sheets = t_hbm.shape[0]
-    copies = []
-    for i, (src, dst) in enumerate(((t_hbm, t_out), (b_hbm, b_out))):
-        for z in range(sheets):
-            copies.append(pltpu.make_async_copy(src.at[z], dst.at[z], sems.at[i, z]))
+    )(*[pltpu.with_memory_space_constraint(v, pltpu.HBM) for v in (temperature, base)])
+
+
+def load_kernel(*refs):
+    count = len(refs) // 2 - 1
+    sems = refs[-1]
+    copies = [
+        pltpu.make_async_copy(refs[i], refs[count + 1 + i], sems.at[i]) for i in range(count)
+    ]
     for copy in copies:
         copy.start()
     for copy in copies:
         copy.wait()
 
 
-def load(temperature, base, after):
-    fields = [pltpu.with_memory_space_constraint(v, pltpu.HBM) for v in (temperature, base)]
+def load(values, after):
     return pl.pallas_call(
         load_kernel,
-        in_specs=[IN_HBM] * 2 + [ANYWHERE],
-        out_shape=[pltpu.VMEM(temperature.shape, F32)] * 2,
-        scratch_shapes=[pltpu.SemaphoreType.DMA((2, temperature.shape[0]))],
+        in_specs=[IN_HBM] * len(values) + [ANYWHERE],
+        out_shape=[pltpu.VMEM(v.shape, v.dtype) for v in values],
+        scratch_shapes=[pltpu.SemaphoreType.DMA((len(values),))],
         compiler_params=params(),
-        cost_estimate=pl.CostEstimate(flops=0, bytes_accessed=16 * temperature.size, transcendentals=0),
-    )(*fields, after)
+        cost_estimate=pl.CostEstimate(
+            flops=0, bytes_accessed=16 * values[0].size, transcendentals=0
+        ),
+    )(*[pltpu.with_memory_space_constraint(v, pltpu.HBM) for v in values], after)
 
 
 def source_plane(loc, energy, rows, columns, plate):
@@ -747,8 +742,9 @@
     own, got = refs[:2]
     ties = refs[2 : 1 + stages]
     yw, yh, yp, inner, inner_own, outer, outer_own, zw, zi, t_ref = refs[1 + stages : 11 + stages]
-    out, e_s, u_s, o_s, sems = refs[11 + stages :]
-    chunks, sheets, rows, _ = o_s.shape
+    out, e_s, u_s, n_s, o_s, sems = refs[11 + stages :]
+    sheets, rows, columns = o_s.shape
+    chunks = columns // LANES
     each = LANES // rows
     pairs = sheets // each
     steps = yw.shape[0]
@@ -779,29 +775,31 @@
         for n, (j, m) in enumerate(members):
             u_s[m, pl.ds(j * steps + k, SUBLANES, stride=span), :] = value[n]
 
+    for y in range(chunks):
+        for m in range(pairs):
+            turned = u_s[m, part_of(y), :].T
+            for i in range(each):
+                n_s[m * each + i, :, part_of(y)] = turned[i * rows : (i + 1) * rows, :]
     copies = []
-    for y in range(chunks):
-        part = part_of(y)
-        turned = [u_s[m, part, :].T for m in range(pairs)]
-        for half in range(2):
-            at = slice(half * rows // 2, (half + 1) * rows // 2)
+    block = rows // OUT_COPIES
+    for n in range(OUT_COPIES):
+        at = slice(n * block, (n + 1) * block)
+        for y in range(chunks):
+            part = part_of(y)
             rhs, kept = None, []
             for z in range(sheets):
-                first = (z % each) * rows + at.start
-                own_rhs = turned[z // each][first : first + rows // 2, :]
+                own_rhs = n_s[z, at, part]
                 rhs = own_rhs if z == 0 else own_rhs + zw[z - 1, y, at, :] * rhs
                 kept.append(rhs * zi[z, y, at, :])
             value = kept[-1]
-            o_s[y, sheets - 1, at, :] = t_ref[sheets - 1, at, part] + value
+            o_s[sheets - 1, at, part] = t_ref[sheets - 1, at, part] + value
             for z in range(sheets - 2, -1, -1):
                 value = zw[z, y, at, :] * value + kept[z]
-                o_s[y, z, at, :] = t_ref[z, at, part] + value
-            strip = pl.ds(at.start, rows // 2)
-            copy = pltpu.make_async_copy(
-                o_s.at[y, :, strip, :], out.at[:, strip, pl.ds(y * LANES, LANES)], sems.at[y, half]
-            )
-            copy.start()
-            copies.append(copy)
+                o_s[z, at, part] = t_ref[z, at, part] + value
+        strip = pl.ds(at.start, block)
+        copy = pltpu.make_async_copy(o_s.at[:, strip, :], out.at[:, strip, :], sems.at[n])
+        copy.start()
+        copies.append(copy)
     for copy in copies:
         copy.wait()
 
@@ -817,8 +815,9 @@
         scratch_shapes=[
             pltpu.VMEM((2, pairs * SUBLANES, LANES), F32),
             pltpu.VMEM((pairs, chunks * LANES, LANES), F32),
-            pltpu.VMEM((chunks, sheets, rows, LANES), F32),
-            pltpu.SemaphoreType.DMA((chunks, 2)),
+            pltpu.VMEM(t.shape, F32),
+            pltpu.VMEM(t.shape, F32),
+            pltpu.SemaphoreType.DMA((OUT_COPIES,)),
         ],
         compiler_params=params(),
     )(own, got, *ties, yw, yh, yp, inner, inner_own, outer, outer_own, zw, zi, t)
@@ -827,9 +826,9 @@
 def per_device(temperature, base, locations, energy):
     columns = temperature.shape[2]
     gy = lax.axis_size("gy")
-    loc, heat, packed = edges(temperature, base, locations[None], energy[None])
+    packed = edges(temperature, base)
     near = swap(packed, "gy", 1)
-    t, b = load(temperature, base, packed)
+    t, b, loc, heat = load((temperature, base, locations[None], energy[None]), packed)
     near, t, b = lax.optimization_barrier((near, t, b))
     far = [swap(near, "gy", 2)] if gy > 2 else []
     if gy > 4:

time: 28.3 us -> 27.8 us (0.982)
  Pallas kernels: 8.76 us -> 8.31 us
where the time goes in v7:
time: 27.8 us; the launch traced here: 27.6 us
  starting transfers between devices  11 us (40%)
  Pallas kernels  8.31 us (30%)
  waiting for transfers between devices  8.23 us (30%)
    ppermute x8, starting transfers between devices, swap(): return lax.ppermute(value, axis, [(i, i ^ flip) for i in range(count)])  11 us
    ppermute x8, waiting for transfers between devices, swap(): return lax.ppermute(value, axis, [(i, i ^ flip) for i in range(count)])  8.23 us
    pallas_call x1, Pallas kernels, x_factor(): pl.pallas_call(functools.partial(x_factor_kernel, plate), in_specs=[IN_VM...  2.07 us
    pallas_call x1, Pallas kernels, finish(): pl.pallas_call(functools.partial(finish_kernel, len(ties) + 1), out_shape...  1.43 us
    pallas_call x1, Pallas kernels, edges(): pl.pallas_call(edges_kernel, in_specs=[IN_HBM] * 2, out_shape=pltpu.VMEM(...  1.28 us
    pallas_call x1, Pallas kernels, load(): pl.pallas_call(load_kernel, in_specs=[IN_HBM] * len(values) + [ANYWHERE],...  1.24 us
    pallas_call x1, Pallas kernels, y_factor(): pl.pallas_call(y_factor_kernel, in_specs=[IN_VMEM, ANYWHERE], out_shape=[...  0.91 us
    pallas_call x1, Pallas kernels, y_target(): pl.pallas_call(functools.partial(y_target_kernel, len(ties) + 1), out_sha...  0.78 us
  transfers between devices with their start and end apart: 8, of which 6 were waited for; matrix products, arithmetic and copies ran while one was open for 0% of the time, Pallas kernels for 16%

profile of v7, /device:TPU:0, one launch (start us, length us, event | category | flops | bytes accessed | tf_op | source)
XLA Modules:
  0.0 27.6 jit_solution(13018938157588868845)
XLA Ops:
  0.0 1.3 %shard_map.46.refs_4_.own_cells = f32[64,128]{1,0:T(8,128)S(1)} custom-call(f32[4,64,512]{2,1,0:T(8,128)} %refs_0_.1, f32[4,64,512]{2,1,0:T(8,128)} %refs_1_.1), custom_call_target="tpu_custom_call" | custom-call | tf_op jit(solution)/shard_map/pallas_call | solution.py:165
  1.3 0.5 %collective-permute-start = (f32[64,128]{1,0:T(8,128)S(1)}, f32[64,128]{1,0:T(8,128)S(1)}, u32[]{:S(2)}, u32[]{:S(2)}) collective-permute-start(f32[64,128]{1,0:T(8,128)S(1)} %shard_map.46.refs_4_.own_cells), channel_id=1, source_target_pairs={{0,1},{1,0},{2,3},{3,2},{4,5},{5,4},{6,7},{7,6},{8,9},{9,8},{10,11... | collective-permute-start | bytes 98312 | tf_op jit(solution)/shard_map/ppermute | solution.py:442
  1.8 1.2 %shard_map.47 = (f32[4,64,512]{2,1,0:T(8,128)S(1)}, f32[4,64,512]{2,1,0:T(8,128)S(1)}, s32[1,64]{1,0:T(1,128)S(1)}, f32[1,64]{1,0:T(1,128)S(1)}) custom-call(f32[4,64,512]{2,1,0:T(8,128)} %refs_0_.1, f32[4,64,512]{2,1,0:T(8,128)} %refs_1_.1, s32[1,64]{1,0:T(1,128)} %bitcast.2, f32[1,64]{1,0:T(1,128)} %bitcast.3, f32[64,128]{1,0:T(8,128)S(1)} %shard_map.46.refs_4_.own_cells), custom_call_target="tpu_custom_call" | custom-call | bytes 2097152 | tf_op jit(solution)/shard_map/pallas_call | solution.py:191
  3.0 0.0 collective-permute-done.after.refs_0_
  3.1 2.6 %collective-permute-start.1 = (f32[64,128]{1,0:T(8,128)S(1)}, f32[64,128]{1,0:T(8,128)S(1)}, u32[]{:S(2)}, u32[]{:S(2)}) collective-permute-start(f32[64,128]{1,0:T(8,128)S(1)} %collective-permute-done.after.refs_0_), channel_id=1, source_target_pairs={{0,2},{1,3},{2,0},{3,1},{4,6},{5,7},{6,4},{7,5},{8,10},{9,11},{10,... | collective-permute-start | bytes 98312 | tf_op jit(solution)/shard_map/ppermute | solution.py:442
  5.7 2.1 %shard_map.48 = (f32[4,4,64,128]{3,2,1,0:T(8,128)S(1)}, f32[4,4,64,128]{3,2,1,0:T(8,128)S(1)}, f32[8,16,8,128]{3,2,1,0:T(8,128)S(1)}, f32[8,16,8,128]{3,2,1,0:T(...) custom-call(s32[1,64]{1,0:T(1,128)S(1)} %get-tuple-element.44.loc, ...), custom_call_target="tpu_custom_call" | custom-call | flops 5242880 | bytes 3670016 | tf_op jit(solution)/shard_map/pallas_call | solution.py:338
  7.7 0.0 collective-permute-done.1.refs_1_
  7.7 0.4 %shard_map.49 = (f32[8,8,8,128]{3,2,1,0:T(8,128)S(1)}, f32[7,16,128]{2,1,0:T(8,128)S(1)}, f32[7,16,128]{2,1,0:T(8,128)S(1)}) custom-call(f32[64,128]{1,0:T(8,128)S(1)} %shard_map.46.refs_4_.own_cells, f32[4,64,512]{2,1,0:T(8,128)S(1)} %get-tuple-element.43.t_ref.refs_10_.refs_12_, f32[4,4,64,128]{3,2,1,0:T(8,128)S(1)} %get-tuple-element.48.total_ref, ...), custom_call_target="tpu_custom_call" | custom-call | tf_op jit(solution)/shard_map/pallas_call | solution.py:421
  8.1 2.9 %collective-permute-start.2 = (f32[7,16,128]{2,1,0:T(8,128)S(1)}, f32[7,16,128]{2,1,0:T(8,128)S(1)}, u32[]{:S(2)}, u32[]{:S(2)}) collective-permute-start(f32[7,16,128]{2,1,0:T(8,128)S(1)} %get-tuple-element.55.after.refs_0_), channel_id=1, source_target_pairs={{0,12},{4,8},{8,4},{12,0},{16,28},{20,24},{24,20},{28,16},{1,13},{... | collective-permute-start | bytes 172040 | tf_op jit(solution)/shard_map/ppermute | solution.py:442
  11.0 0.4 %collective-permute-start.3 = (f32[7,16,128]{2,1,0:T(8,128)S(1)}, f32[7,16,128]{2,1,0:T(8,128)S(1)}, u32[]{:S(2)}, u32[]{:S(2)}) collective-permute-start(f32[7,16,128]{2,1,0:T(8,128)S(1)} %get-tuple-element.55.after.refs_0_), channel_id=1, source_target_pairs={{0,8},{4,12},{8,0},{12,4},{16,24},{20,28},{24,16},{28,20},{1,9},{5... | collective-permute-start | bytes 172040 | tf_op jit(solution)/shard_map/ppermute | solution.py:442
  11.4 0.2 collective-permute-start.4
  11.7 0.9 %shard_map.50 = (f32[16,8,8,128]{3,2,1,0:T(8,128)S(1)}, f32[16,8,8,128]{3,2,1,0:T(8,128)S(1)}, f32[16,8,8,128]{3,2,1,0:T(8,128)S(1)}, f32[3,3,2,8,128]{4,3,2,1,0...) custom-call(f32[4,4,64,128]{3,2,1,0:T(8,128)S(1)} %get-tuple-element.56.c_ref, ...), custom_call_target="tpu_custom_call" | custom-call | flops 2621440 | bytes 2097152 | tf_op jit(solution)/shard_map/pallas_call | solution.py:590
  12.6 0.2 shard_map.51
  12.8 0.6 %collective-permute-done.2.refs_1_ = f32[7,16,128]{2,1,0:T(8,128)S(1)} collective-permute-done((f32[7,16,128]{2,1,0:T(8,128)S(1)}, f32[7,16,128]{2,1,0:T(8,128)S(1)}, u32[]{:S(2)}, u32[]{:S(2)}) %collective-permute-start.2) | collective-permute-done | bytes 57376 | tf_op jit(solution)/shard_map/ppermute | solution.py:442
  13.4 1.8 %collective-permute-done.3.refs_2_ = f32[7,16,128]{2,1,0:T(8,128)S(1)} collective-permute-done((f32[7,16,128]{2,1,0:T(8,128)S(1)}, f32[7,16,128]{2,1,0:T(8,128)S(1)}, u32[]{:S(2)}, u32[]{:S(2)}) %collective-permute-start.3) | collective-permute-done | bytes 57376 | tf_op jit(solution)/shard_map/ppermute | solution.py:442
  15.2 0.4 %collective-permute-done.4.refs_3_ = f32[7,16,128]{2,1,0:T(8,128)S(1)} collective-permute-done((f32[7,16,128]{2,1,0:T(8,128)S(1)}, f32[7,16,128]{2,1,0:T(8,128)S(1)}, u32[]{:S(2)}, u32[]{:S(2)}) %collective-permute-start.4) | collective-permute-done | bytes 57376 | tf_op jit(solution)/shard_map/ppermute | solution.py:442
  15.6 0.1 shard_map.52
  15.7 2.7 %collective-permute-start.5 = (f32[3,16,128]{2,1,0:T(8,128)S(1)}, f32[3,16,128]{2,1,0:T(8,128)S(1)}, u32[]{:S(2)}, u32[]{:S(2)}) collective-permute-start(f32[3,16,128]{2,1,0:T(8,128)S(1)} %get-tuple-element.59.refs_0_), channel_id=1, source_target_pairs={{0,16},{4,20},{8,24},{12,28},{16,0},{20,4},{24,8},{28,12},{1,17},{... | collective-permute-start | bytes 73736 | tf_op jit(solution)/shard_map/ppermute | solution.py:442
  18.3 2.1 %collective-permute-done.5.refs_1_ = f32[3,16,128]{2,1,0:T(8,128)S(1)} collective-permute-done((f32[3,16,128]{2,1,0:T(8,128)S(1)}, f32[3,16,128]{2,1,0:T(8,128)S(1)}, u32[]{:S(2)}, u32[]{:S(2)}) %collective-permute-start.5) | collective-permute-done | bytes 24608 | tf_op jit(solution)/shard_map/ppermute | solution.py:442
  20.5 0.8 %shard_map.53 = (f32[16,8,8,128]{3,2,1,0:T(8,128)S(1)}, f32[3,2,8,128]{3,2,1,0:T(8,128)S(1)}, f32[7,2,128]{2,1,0:T(2,128)S(1)}, f32[7,2,128]{2,1,0:T(2,128)S(1)}) custom-call(f32[3,16,128]{2,1,0:T(8,128)S(1)} %get-tuple-element.59.refs_0_, f32[3,16,128]{2,1,0:T(8,128)S(1)} %collective-permute-done.5.refs_1_, f32[3,16,128]{2,1,0:T(8,128)S(1)} %get-tuple-element.60.refs_2_, ...), custom_call_target="tpu_custom_call" | custom-call | tf_op jit(solution)/shard_map/pallas_call | solution.py:723
  21.3 0.1 collective-permute-start.6
  21.3 1.2 %collective-permute-done.6.refs_1_ = f32[7,2,128]{2,1,0:T(2,128)S(1)} collective-permute-done((f32[7,2,128]{2,1,0:T(2,128)S(1)}, f32[7,2,128]{2,1,0:T(2,128)S(1)}, u32[]{:S(2)}, u32[]{:S(2)}) %collective-permute-start.6) | collective-permute-done | bytes 7200 | tf_op jit(solution)/shard_map/ppermute | solution.py:442
  22.5 1.6 %collective-permute-start.7 = (f32[3,2,128]{2,1,0:T(2,128)S(1)}, f32[3,2,128]{2,1,0:T(2,128)S(1)}, u32[]{:S(2)}, u32[]{:S(2)}) collective-permute-start(f32[3,2,128]{2,1,0:T(2,128)S(1)} %get-tuple-element.71.refs_0_), channel_id=1, source_target_pairs={{0,2},{1,3},{2,0},{3,1},{4,6},{5,7},{6,4},{7,5},{8,10},{9,11},{10,... | collective-permute-start | bytes 9224 | tf_op jit(solution)/shard_map/ppermute | solution.py:442
  24.1 2.1 %collective-permute-done.7.refs_1_ = f32[3,2,128]{2,1,0:T(2,128)S(1)} collective-permute-done((f32[3,2,128]{2,1,0:T(2,128)S(1)}, f32[3,2,128]{2,1,0:T(2,128)S(1)}, u32[]{:S(2)}, u32[]{:S(2)}) %collective-permute-start.7) | collective-permute-done | bytes 3104 | tf_op jit(solution)/shard_map/ppermute | solution.py:442
  26.2 1.4 %shard_map.55 = f32[4,64,512]{2,1,0:T(8,128)} custom-call(f32[3,2,128]{2,1,0:T(2,128)S(1)} %get-tuple-element.71.refs_0_, f32[3,2,128]{2,1,0:T(2,128)S(1)} %collective-permute-done.7.refs_1_, f32[3,2,128]{2,1,0:T(2,128)S(1)} %get-tuple-element.72.refs_2_, f32[16,8,8,128]{3,2,1,0:T(8,128)S(1)} %get-tuple-element.65.refs_11_.refs_3_, ...), custom_call_target="tpu_custom_call" | custom-call | tf_op jit(solution)/shard_map/pallas_call | solution.py:811
  (1 shorter events, 0.0 us)
Async XLA Ops:
  1.3 1.8 %collective-permute-start = (f32[64,128]{1,0:T(8,128)S(1)}, f32[64,128]{1,0:T(8,128)S(1)}, u32[]{:S(2)}, u32[]{:S(2)}) collective-permute-start(f32[64,128]{1,0:T(8,128)S(1)} %shard_map.46.refs_4_.own_cells), channel_id=1, source_target_pairs={{0,1},{1,0},{2,3},{3,2},{4,5},{5,4},{6,7},{7,6},{8,9},{9,8},{10,11... | collective-permute-start | bytes 98312 | tf_op jit(solution)/shard_map/ppermute | solution.py:442
  3.1 4.7 %collective-permute-start.1 = (f32[64,128]{1,0:T(8,128)S(1)}, f32[64,128]{1,0:T(8,128)S(1)}, u32[]{:S(2)}, u32[]{:S(2)}) collective-permute-start(f32[64,128]{1,0:T(8,128)S(1)} %collective-permute-done.after.refs_0_), channel_id=1, source_target_pairs={{0,2},{1,3},{2,0},{3,1},{4,6},{5,7},{6,4},{7,5},{8,10},{9,11},{10,... | collective-permute-start | bytes 98312 | tf_op jit(solution)/shard_map/ppermute | solution.py:442
  8.1 5.3 %collective-permute-start.2 = (f32[7,16,128]{2,1,0:T(8,128)S(1)}, f32[7,16,128]{2,1,0:T(8,128)S(1)}, u32[]{:S(2)}, u32[]{:S(2)}) collective-permute-start(f32[7,16,128]{2,1,0:T(8,128)S(1)} %get-tuple-element.55.after.refs_0_), channel_id=1, source_target_pairs={{0,12},{4,8},{8,4},{12,0},{16,28},{20,24},{24,20},{28,16},{1,13},{... | collective-permute-start | bytes 172040 | tf_op jit(solution)/shard_map/ppermute | solution.py:442
  11.0 4.2 %collective-permute-start.3 = (f32[7,16,128]{2,1,0:T(8,128)S(1)}, f32[7,16,128]{2,1,0:T(8,128)S(1)}, u32[]{:S(2)}, u32[]{:S(2)}) collective-permute-start(f32[7,16,128]{2,1,0:T(8,128)S(1)} %get-tuple-element.55.after.refs_0_), channel_id=1, source_target_pairs={{0,8},{4,12},{8,0},{12,4},{16,24},{20,28},{24,16},{28,20},{1,9},{5... | collective-permute-start | bytes 172040 | tf_op jit(solution)/shard_map/ppermute | solution.py:442
  11.4 4.2 %collective-permute-start.4 = (f32[7,16,128]{2,1,0:T(8,128)S(1)}, f32[7,16,128]{2,1,0:T(8,128)S(1)}, u32[]{:S(2)}, u32[]{:S(2)}) collective-permute-start(f32[7,16,128]{2,1,0:T(8,128)S(1)} %get-tuple-element.55.after.refs_0_), channel_id=1, source_target_pairs={{0,4},{4,0},{8,12},{12,8},{16,20},{20,16},{24,28},{28,24},{1,5},{5... | collective-permute-start | bytes 172040 | tf_op jit(solution)/shard_map/ppermute | solution.py:442
  15.7 4.8 %collective-permute-start.5 = (f32[3,16,128]{2,1,0:T(8,128)S(1)}, f32[3,16,128]{2,1,0:T(8,128)S(1)}, u32[]{:S(2)}, u32[]{:S(2)}) collective-permute-start(f32[3,16,128]{2,1,0:T(8,128)S(1)} %get-tuple-element.59.refs_0_), channel_id=1, source_target_pairs={{0,16},{4,20},{8,24},{12,28},{16,0},{20,4},{24,8},{28,12},{1,17},{... | collective-permute-start | bytes 73736 | tf_op jit(solution)/shard_map/ppermute | solution.py:442
  21.3 1.2 %collective-permute-start.6 = (f32[7,2,128]{2,1,0:T(2,128)S(1)}, f32[7,2,128]{2,1,0:T(2,128)S(1)}, u32[]{:S(2)}, u32[]{:S(2)}) collective-permute-start(f32[7,2,128]{2,1,0:T(2,128)S(1)} %get-tuple-element.70.refs_0_), channel_id=1, source_target_pairs={{0,1},{1,0},{2,3},{3,2},{4,5},{5,4},{6,7},{7,6},{8,9},{9,8},{10,11... | collective-permute-start | bytes 21512 | tf_op jit(solution)/shard_map/ppermute | solution.py:442
  22.5 3.7 %collective-permute-start.7 = (f32[3,2,128]{2,1,0:T(2,128)S(1)}, f32[3,2,128]{2,1,0:T(2,128)S(1)}, u32[]{:S(2)}, u32[]{:S(2)}) collective-permute-start(f32[3,2,128]{2,1,0:T(2,128)S(1)} %get-tuple-element.71.refs_0_), channel_id=1, source_target_pairs={{0,2},{1,3},{2,0},{3,1},{4,6},{5,7},{6,4},{7,5},{8,10},{9,11},{10,... | collective-permute-start | bytes 9224 | tf_op jit(solution)/shard_map/ppermute | solution.py:442

commit v8 on v7

--- a/solution.py
+++ b/solution.py
@@ -11,8 +11,6 @@
 THERMAL_GROWTH = 0.8
 LANES = 128
 SUBLANES = 8
-Y_PARTS = 4
-OUT_COPIES = 4
 F32 = jnp.float32
 MIB = 1024 * 1024
 ANYWHERE = pl.BlockSpec(memory_space=pl.ANY)
@@ -253,7 +251,7 @@
 
 
 def x_factor_kernel(plate, loc, energy, t_ref, b_ref, after, *refs):
-    c_ref, total_ref, w_ref, i_ref, p_ref, links, view, h_ref, ends_ref, q_s = refs
+    c_ref, total_ref, w_ref, i_ref, p_ref, links, view, h_ref, ends_ref, t_out, q_s, t_s = refs
     chunks, sheets, rows, _ = c_ref.shape
     lines = chunks * sheets
     steps = rows // SUBLANES
@@ -290,6 +288,7 @@
                     total_ref[y, z - 1, at, :] += across
                 total_ref[y, z, at, :] = total
                 c_ref[y, z, at, :] = cs[y]
+                t_s[y, z, at, :] = ts[y]
             before_t, before_c = ts, cs
 
     at = 0
@@ -313,6 +312,9 @@
                 lambda y, z: total_ref.at[y, z], members, at, w_ref, i_ref, p_ref, h_ref,
                 at - 2 * sheets, ends_ref,
             )
+        for k in range(steps):
+            for i, (y, z) in enumerate(members):
+                t_out[k, at + i] = t_s[y, z, pl.ds(k, SUBLANES, stride=steps), :]
         at += len(members)
 
     segments = [
@@ -348,8 +350,12 @@
             shape_of(len(COEFS), lines, LANES),
             shape_of(steps, max(1, lines - 2 * sheets), SUBLANES, LANES),
             shape_of(2, lines * SUBLANES, LANES),
-        ],
-        scratch_shapes=[pltpu.VMEM((len(COEFS), lines * SUBLANES, LANES), F32)],
+            stored,
+        ],
+        scratch_shapes=[
+            pltpu.VMEM((len(COEFS), lines * SUBLANES, LANES), F32),
+            pltpu.VMEM((chunks, sheets, rows, LANES), F32),
+        ],
         compiler_params=params(),
         cost_estimate=pl.CostEstimate(flops=40 * t.size, bytes_accessed=28 * t.size, transcendentals=0),
     )(loc, energy, t, b, after)
@@ -538,21 +544,53 @@
     return low, high
 
 
-def y_factor_kernel(c_ref, after, w_ref, i_ref, p_ref, inner, outer, view, c_s, q_s):
+def natural(index, parts):
+    span = SUBLANES * parts
+    local = index % span
+    return index - local + local % SUBLANES * parts + local // SUBLANES
+
+
+def turn_matrix(shape, from_natural, parts):
+    row = lax.broadcasted_iota(jnp.int32, shape, 0)
+    column = lax.broadcasted_iota(jnp.int32, shape, 1) % LANES
+    hit = natural(row, parts) == column if from_natural else row == natural(column, parts)
+    return jnp.where(hit, 1.0, 0.0).astype(jnp.bfloat16)
+
+
+def turned(matrix, field):
+    high = field.astype(jnp.bfloat16)
+    low = (field - high.astype(F32)).astype(jnp.bfloat16)
+    both = jnp.concatenate([high, low], 1)
+    return lax.dot_general(
+        matrix, both, (((1,), (1,)), ((), ())), preferred_element_type=F32
+    )
+
+
+def y_factor_kernel(c_ref, after, w_ref, i_ref, p_ref, inner, outer, view, to_y, to_x, c_s, q_s, r_s):
     chunks, sheets, rows, _ = c_ref.shape
     each = LANES // rows
     pairs = sheets // each
-    span = chunks * LANES // SUBLANES
-    steps = span // Y_PARTS
+    x_steps = rows // SUBLANES
+    steps = LANES // SUBLANES
+    to_y[...] = turn_matrix(to_y.shape, True, steps)
+    to_x[...] = turn_matrix(to_x.shape, False, x_steps)
     for m in range(pairs):
         for y in range(chunks):
-            block = jnp.concatenate([c_ref[y, m * each + i] for i in range(each)], 0)
-            c_s[m, y * LANES : (y + 1) * LANES, :] = block.T
-
-    members = [(j, m) for j in range(Y_PARTS) for m in range(pairs)]
+            block = jnp.concatenate(
+                [
+                    c_ref[y, m * each + i, pl.ds(k, SUBLANES, stride=x_steps), :]
+                    for i in range(each)
+                    for k in range(x_steps)
+                ],
+                0,
+            )
+            c_s[m, part_of(y), :] = block.T
+
+    members = [(y, m) for y in range(chunks) for m in range(pairs)]
+    lines = len(members)
 
     def cond(k):
-        return jnp.stack([c_s[m, pl.ds(j * steps + k, SUBLANES, stride=span), :] for j, m in members], 0)
+        return jnp.stack([c_s[m, pl.ds(y * LANES + k, SUBLANES, stride=steps), :] for y, m in members], 0)
 
     def keep(k, w, inv, p):
         w_ref[k] = w
@@ -560,23 +598,27 @@
         p_ref[k] = p
 
     block = factor(cond, steps, keep)
-    parts = [{q: block[q][j * pairs : (j + 1) * pairs] for q in COEFS} for j in range(Y_PARTS)]
-    whole, levels = tree(parts, join_coefs)
-    for (offset, _), level in zip(node_offsets(Y_PARTS), levels):
-        for n, values in enumerate(level):
-            for i in range(3):
-                inner[offset + n, i] = values[i]
     for n, q in enumerate(COEFS):
-        for m in range(pairs):
-            q_s[n, m * SUBLANES : (m + 1) * SUBLANES, :] = whole[q][m]
+        for i in range(lines):
+            q_s[n, i * SUBLANES : (i + 1) * SUBLANES, :] = block[q][i]
     segments = [
-        {q: q_s[n, pl.ds(s, pairs, stride=SUBLANES), :] for n, q in enumerate(COEFS)}
+        {q: q_s[n, pl.ds(s, lines, stride=SUBLANES), :] for n, q in enumerate(COEFS)}
         for s in range(SUBLANES)
     ]
     whole, levels = tree(segments, join_coefs)
     for (offset, _), level in zip(node_offsets(SUBLANES), levels):
         for n, values in enumerate(level):
             for i in range(3):
+                inner[offset + n, i] = values[i]
+    for n, q in enumerate(COEFS):
+        r_s[n] = whole[q]
+    parts = [
+        {q: r_s[n, y * pairs : (y + 1) * pairs, :] for n, q in enumerate(COEFS)} for y in range(chunks)
+    ]
+    whole, levels = tree(parts, join_coefs)
+    for (offset, _), level in zip(node_offsets(chunks), levels):
+        for n, values in enumerate(level):
+            for i in range(3):
                 outer[offset + n, i] = values[i]
     for n, q in enumerate(COEFS):
         view[n] = whole[q]
@@ -585,8 +627,9 @@
 def y_factor(c, after):
     chunks, sheets, rows, _ = c.shape
     pairs = sheets * rows // LANES
-    steps = chunks * LANES // SUBLANES // Y_PARTS
-    stored = shape_of(steps, Y_PARTS * pairs, SUBLANES, LANES)
+    lines = chunks * pairs
+    stored = shape_of(LANES // SUBLANES, lines, SUBLANES, LANES)
+    matrix = jax.ShapeDtypeStruct((LANES, 2 * LANES), jnp.bfloat16)
     return pl.pallas_call(
         y_factor_kernel,
         in_specs=[IN_VMEM, ANYWHERE],
@@ -594,13 +637,16 @@
             stored,
             stored,
             stored,
-            shape_of(Y_PARTS - 1, 3, pairs, SUBLANES, LANES),
-            shape_of(SUBLANES - 1, 3, pairs, LANES),
+            shape_of(SUBLANES - 1, 3, lines, LANES),
+            shape_of(chunks - 1, 3, pairs, LANES),
             shape_of(len(COEFS), pairs, LANES),
+            matrix,
+            matrix,
         ],
         scratch_shapes=[
             pltpu.VMEM((pairs, chunks * LANES, LANES), F32),
-            pltpu.VMEM((len(COEFS), pairs * SUBLANES, LANES), F32),
+            pltpu.VMEM((len(COEFS), lines * SUBLANES, LANES), F32),
+            pltpu.VMEM((len(COEFS), lines, LANES), F32),
         ],
         compiler_params=params(),
         cost_estimate=pl.CostEstimate(flops=20 * c.size, bytes_accessed=16 * c.size, transcendentals=0),
@@ -634,22 +680,41 @@
     )(c, after)
 
 
+def join_tree(items, links, own):
+    for offset, count in node_offsets(len(items)):
+        joined = []
+        for n in range(count):
+            tie = tuple(links[offset + n, i] for i in range(3))
+            both, flux = join_targets(items[2 * n], items[2 * n + 1], tie)
+            own[offset + n] = flux
+            joined.append(both)
+        items = joined
+    return items[0]
+
+
+def tree_ends(leaves, links, own, low, high):
+    levels = [
+        [(own[offset + n], links[offset + n, 1], links[offset + n, 2]) for n in range(count)]
+        for offset, count in node_offsets(leaves)
+    ]
+    return descend(levels, low, high)
+
+
 def y_target_kernel(stages, *refs):
     own, got = refs[:2]
     ties = refs[2 : 1 + stages]
-    xw, xh, xm, xp, x_links, x_own, t_ref, yw, yi, yp, inner, outer, view = refs[1 + stages : 14 + stages]
-    h_ref, inner_own, outer_own, send = refs[14 + stages : 18 + stages]
-    f_s, g_s, y_s, q_s = refs[18 + stages :]
-    chunks, sheets, rows, _ = g_s.shape
-    lines = chunks * sheets
-    x_steps = rows // SUBLANES
+    xw, xh, xm, xp, x_links, x_own, t_ref, yw, yi, yp, inner, outer, view, to_y = refs[1 + stages : 15 + stages]
+    h_ref, inner_own, outer_own, send = refs[15 + stages : 19 + stages]
+    f_s, g_s, q_s, r_s = refs[19 + stages :]
+    x_steps, lines = xw.shape[:2]
+    chunks = g_s.shape[0]
+    sheets = lines // chunks
+    rows = x_steps * SUBLANES
+    pairs = sheets * rows // LANES
+    steps = yw.shape[0]
 
     low, high = block_ends("gx", own, got, ties)
-    levels = [
-        [(x_own[o + n], x_links[o + n, 1], x_links[o + n, 2]) for n in range(count)]
-        for o, count in node_offsets(SUBLANES)
-    ]
-    for s, ends in enumerate(descend(levels, low, high)):
+    for s, ends in enumerate(tree_ends(SUBLANES, x_links, x_own, low, high)):
         for i in range(2):
             f_s[i, pl.ds(s, lines, stride=SUBLANES), :] = ends[i]
     first = 0
@@ -664,163 +729,131 @@
         )
         for k in range(x_steps - 1, -1, -1):
             value = xw[k, at] * value + (h_ref_of[k, h_at] + xp[k, at] * low)
+            field = value - t_ref[k, at]
             for j, (y, z) in enumerate(members):
-                g_s[y, z, pl.ds(k, SUBLANES, stride=x_steps), :] = value[j]
+                place = z * rows + k * SUBLANES
+                g_s[y, place : place + SUBLANES, :] = field[j]
         first = at.stop
 
-    each = LANES // rows
-    pairs = sheets // each
-    span = chunks * LANES // SUBLANES
-    steps = span // Y_PARTS
-    for m in range(pairs):
-        for y in range(chunks):
-            block = jnp.concatenate(
-                [g_s[y, m * each + i] - t_ref[m * each + i, :, part_of(y)] for i in range(each)], 0
-            )
-            y_s[m, y * LANES : (y + 1) * LANES, :] = block.T
-    members = [(j, m) for j in range(Y_PARTS) for m in range(pairs)]
+    fields = [turned(to_y[...], g_s[y]) for y in range(chunks)]
 
     def target(k):
-        return jnp.stack([y_s[m, pl.ds(j * steps + k, SUBLANES, stride=span), :] for j, m in members], 0)
+        at = slice(k * SUBLANES, (k + 1) * SUBLANES)
+        return jnp.stack(
+            [fields[y][at, m * LANES : (m + 1) * LANES] for y in range(chunks) for m in range(pairs)], 0
+        )
 
     def keep(k, h):
         h_ref[k] = h
 
     ends = eliminate(target, steps, lambda k: yw[k], lambda k: yi[k], lambda k: yp[k], keep)
-    items = [tuple(v[j * pairs : (j + 1) * pairs] for v in ends) for j in range(Y_PARTS)]
-    for offset, count in node_offsets(Y_PARTS):
-        joined = []
-        for n in range(count):
-            tie = tuple(inner[offset + n, i] for i in range(3))
-            both, flux = join_targets(items[2 * n], items[2 * n + 1], tie)
-            inner_own[offset + n] = flux
-            joined.append(both)
-        items = joined
     for q in range(2):
-        for m in range(pairs):
-            q_s[q, m * SUBLANES : (m + 1) * SUBLANES, :] = items[0][q][m]
+        for i in range(chunks * pairs):
+            q_s[q, i * SUBLANES : (i + 1) * SUBLANES, :] = ends[q][i]
     items = [
-        tuple(q_s[q, pl.ds(s, pairs, stride=SUBLANES), :] for q in range(2)) for s in range(SUBLANES)
+        tuple(q_s[q, pl.ds(s, chunks * pairs, stride=SUBLANES), :] for q in range(2))
+        for s in range(SUBLANES)
     ]
-    for offset, count in node_offsets(SUBLANES):
-        joined = []
-        for n in range(count):
-            tie = tuple(outer[offset + n, i] for i in range(3))
-            both, flux = join_targets(items[2 * n], items[2 * n + 1], tie)
-            outer_own[offset + n] = flux
-            joined.append(both)
-        items = joined
+    r_s[0], r_s[1] = join_tree(items, inner, inner_own)
+    items = [tuple(r_s[q, y * pairs : (y + 1) * pairs, :] for q in range(2)) for y in range(chunks)]
     for n, q in enumerate(COEFS):
         send[q] = view[n]
-    send[FIRST], send[LAST] = items[0]
-
-
-def y_target(own, got, ties, xw, xh, xm, xp, x_links, x_own, t, yw, yi, yp, inner, outer, view):
-    sheets, rows, columns = t.shape
-    chunks = columns // LANES
-    lines = chunks * sheets
-    pairs = sheets * rows // LANES
+    send[FIRST], send[LAST] = join_tree(items, outer, outer_own)
+
+
+def y_target(own, got, ties, xw, xh, xm, xp, x_links, x_own, t, yw, yi, yp, inner, outer, view, to_y):
+    x_steps, lines = xw.shape[:2]
+    y_lines = yw.shape[1]
+    pairs = view.shape[1]
+    chunks = y_lines // pairs
     return pl.pallas_call(
         functools.partial(y_target_kernel, len(ties) + 1),
         out_shape=[
             shape_of(*yw.shape),
-            shape_of(Y_PARTS - 1, pairs, SUBLANES, LANES),
-            shape_of(SUBLANES - 1, pairs, LANES),
+            shape_of(SUBLANES - 1, y_lines, LANES),
+            shape_of(chunks - 1, pairs, LANES),
             shape_of(7, pairs, LANES),
         ],
         scratch_shapes=[
             pltpu.VMEM((2, lines * SUBLANES, LANES), F32),
-            pltpu.VMEM((chunks, sheets, rows, LANES), F32),
-            pltpu.VMEM((pairs, chunks * LANES, LANES), F32),
-            pltpu.VMEM((2, pairs * SUBLANES, LANES), F32),
+            pltpu.VMEM((chunks, pairs * LANES, LANES), F32),
+            pltpu.VMEM((2, y_lines * SUBLANES, LANES), F32),
+            pltpu.VMEM((2, y_lines, LANES), F32),
         ],
         compiler_params=params(),
-    )(own, got, *ties, xw, xh, xm, xp, x_links, x_own, t, yw, yi, yp, inner, outer, view)
+    )(own, got, *ties, xw, xh, xm, xp, x_links, x_own, t, yw, yi, yp, inner, outer, view, to_y)
 
 
 def finish_kernel(stages, *refs):
     own, got = refs[:2]
     ties = refs[2 : 1 + stages]
-    yw, yh, yp, inner, inner_own, outer, outer_own, zw, zi, t_ref = refs[1 + stages : 11 + stages]
-    out, e_s, u_s, n_s, o_s, sems = refs[11 + stages :]
-    sheets, rows, columns = o_s.shape
-    chunks = columns // LANES
+    yw, yh, yp, inner, inner_own, outer, outer_own, zw, zi, t_ref, to_x = refs[1 + stages : 12 + stages]
+    out, r_s, e_s, u_s, o_s, sems = refs[12 + stages :]
+    chunks, sheets, rows, _ = o_s.shape
     each = LANES // rows
     pairs = sheets // each
     steps = yw.shape[0]
-    span = chunks * LANES // SUBLANES
+    lines = chunks * pairs
 
     low, high = block_ends("gy", own, got, ties)
-    levels = [
-        [(outer_own[o + n], outer[o + n, 1], outer[o + n, 2]) for n in range(count)]
-        for o, count in node_offsets(SUBLANES)
-    ]
-    for s, ends in enumerate(descend(levels, low, high)):
+    for y, ends in enumerate(tree_ends(chunks, outer, outer_own, low, high)):
         for i in range(2):
-            e_s[i, pl.ds(s, pairs, stride=SUBLANES), :] = ends[i]
-    low, high = (
-        jnp.stack([e_s[i, m * SUBLANES : (m + 1) * SUBLANES, :] for m in range(pairs)], 0)
+            r_s[i, y * pairs : (y + 1) * pairs, :] = ends[i]
+    for s, ends in enumerate(tree_ends(SUBLANES, inner, inner_own, r_s[0], r_s[1])):
+        for i in range(2):
+            e_s[i, pl.ds(s, lines, stride=SUBLANES), :] = ends[i]
+    low, value = (
+        jnp.stack([e_s[i, n * SUBLANES : (n + 1) * SUBLANES, :] for n in range(lines)], 0)
         for i in range(2)
     )
-    levels = [
-        [(inner_own[o + n], inner[o + n, 1], inner[o + n, 2]) for n in range(count)]
-        for o, count in node_offsets(Y_PARTS)
-    ]
-    ends = descend(levels, low, high)
-    low = jnp.concatenate([e[0] for e in ends], 0)
-    value = jnp.concatenate([e[1] for e in ends], 0)
-    members = [(j, m) for j in range(Y_PARTS) for m in range(pairs)]
     for k in range(steps - 1, -1, -1):
         value = yw[k] * value + (yh[k] + yp[k] * low)
-        for n, (j, m) in enumerate(members):
-            u_s[m, pl.ds(j * steps + k, SUBLANES, stride=span), :] = value[n]
-
-    for y in range(chunks):
-        for m in range(pairs):
-            turned = u_s[m, part_of(y), :].T
-            for i in range(each):
-                n_s[m * each + i, :, part_of(y)] = turned[i * rows : (i + 1) * rows, :]
+        for y in range(chunks):
+            for m in range(pairs):
+                u_s[m, pl.ds(y * LANES + k, SUBLANES, stride=steps), :] = value[y * pairs + m]
+
     copies = []
-    block = rows // OUT_COPIES
-    for n in range(OUT_COPIES):
-        at = slice(n * block, (n + 1) * block)
-        for y in range(chunks):
+    for first in range(0, chunks, 2):
+        both = slice(first * LANES, (first + 2) * LANES)
+        fields = [turned(to_x[...], u_s[m, both, :]) for m in range(pairs)]
+        for y in range(first, first + 2):
             part = part_of(y)
             rhs, kept = None, []
             for z in range(sheets):
-                own_rhs = n_s[z, at, part]
-                rhs = own_rhs if z == 0 else own_rhs + zw[z - 1, y, at, :] * rhs
-                kept.append(rhs * zi[z, y, at, :])
+                at = z % each * rows
+                own_rhs = fields[z // each][at : at + rows, part_of(y - first)]
+                rhs = own_rhs if z == 0 else own_rhs + zw[z - 1, y] * rhs
+                kept.append(rhs * zi[z, y])
             value = kept[-1]
-            o_s[sheets - 1, at, part] = t_ref[sheets - 1, at, part] + value
+            o_s[y, sheets - 1] = t_ref[sheets - 1, :, part] + value
             for z in range(sheets - 2, -1, -1):
-                value = zw[z, y, at, :] * value + kept[z]
-                o_s[z, at, part] = t_ref[z, at, part] + value
-        strip = pl.ds(at.start, block)
-        copy = pltpu.make_async_copy(o_s.at[:, strip, :], out.at[:, strip, :], sems.at[n])
-        copy.start()
-        copies.append(copy)
+                value = zw[z, y] * value + kept[z]
+                o_s[y, z] = t_ref[z, :, part] + value
+            copy = pltpu.make_async_copy(o_s.at[y], out.at[:, :, pl.ds(y * LANES, LANES)], sems.at[y])
+            copy.start()
+            copies.append(copy)
     for copy in copies:
         copy.wait()
 
 
-def finish(own, got, ties, yw, yh, yp, inner, inner_own, outer, outer_own, zw, zi, t):
+def finish(own, got, ties, yw, yh, yp, inner, inner_own, outer, outer_own, zw, zi, t, to_x):
     sheets, rows, columns = t.shape
     chunks = columns // LANES
     pairs = sheets * rows // LANES
+    lines = chunks * pairs
     return pl.pallas_call(
         functools.partial(finish_kernel, len(ties) + 1),
-        out_shape=shape_of(sheets, rows, chunks * LANES),
+        out_shape=shape_of(sheets, rows, columns),
         out_specs=ANYWHERE,
         scratch_shapes=[
-            pltpu.VMEM((2, pairs * SUBLANES, LANES), F32),
-            pltpu.VMEM((pairs, chunks * LANES, LANES), F32),
-            pltpu.VMEM(t.shape, F32),
-            pltpu.VMEM(t.shape, F32),
-            pltpu.SemaphoreType.DMA((OUT_COPIES,)),
+            pltpu.VMEM((2, lines, LANES), F32),
+            pltpu.VMEM((2, lines * SUBLANES, LANES), F32),
+            pltpu.VMEM((pairs, columns, LANES), F32),
+            pltpu.VMEM((chunks, sheets, rows, LANES), F32),
+            pltpu.SemaphoreType.DMA((chunks,)),
         ],
         compiler_params=params(),
-    )(own, got, *ties, yw, yh, yp, inner, inner_own, outer, outer_own, zw, zi, t)
+    )(own, got, *ties, yw, yh, yp, inner, inner_own, outer, outer_own, zw, zi, t, to_x)
 
 
 def per_device(temperature, base, locations, energy):
@@ -833,16 +866,16 @@
     far = [swap(near, "gy", 2)] if gy > 2 else []
     if gy > 4:
         far.append(lax.ppermute(near, "gy", [(i, (i + 2 ^ 2) - 2) for i in range(2, gy - 2)]))
-    c, total, xw, xi, xp, x_links, x_view, xm, ends = x_factor(loc, heat, t, b, columns * gy, near)
+    c, total, xw, xi, xp, x_links, x_view, xm, ends, t_steps = x_factor(loc, heat, t, b, columns * gy, near)
     xh, x_own, view = x_target(packed, t, total, [near] + far, xw, xi, xp, x_links, x_view, ends)
-    yw, yi, yp, inner, outer, y_view = y_factor(c, x_view)
+    yw, yi, yp, inner, outer, y_view, to_y, to_x = y_factor(c, x_view)
     zw, zi = z_factor(c, view)
     own, got, ties = gather_line(view, "gx", 2, (y_view, zw))
     yh, inner_own, outer_own, view = y_target(
-        own, got, ties, xw, xh, xm, xp, x_links, x_own, t, yw, yi, yp, inner, outer, y_view
+        own, got, ties, xw, xh, xm, xp, x_links, x_own, t_steps, yw, yi, yp, inner, outer, y_view, to_y
     )
     own, got, ties = gather_line(view, "gy")
-    return finish(own, got, ties, yw, yh, yp, inner, inner_own, outer, outer_own, zw, zi, t)
+    return finish(own, got, ties, yw, yh, yp, inner, inner_own, outer, outer_own, zw, zi, t, to_x)
 
 
 def solution(mesh):

time: 27.8 us -> 27.3 us (0.982)
  Pallas kernels: 8.31 us -> 7.67 us
    pallas_call x1, Pallas kernels: 0.78 us -> 0.49 us  [y_target(): pl.pallas_call(functools.partial(y_target_kernel, len(ties) + 1), out_sha...]
    pallas_call x1, Pallas kernels: 0.91 us -> 0.63 us  [y_factor(): pl.pallas_call(y_factor_kernel, in_specs=[IN_VMEM, ANYWHERE], out_shape=[...]
  transfers between devices with their start and end apart: 8 -> 8, of which waited for: 6 -> 6; matrix products, arithmetic and copies ran while one was open for 0% -> 0% of each run, Pallas kernels for 16% -> 15%
where the time goes in v8:
time: 27.3 us; the launch traced here: 27.2 us
  starting transfers between devices  11 us (40%)
  waiting for transfers between devices  8.45 us (31%)
  Pallas kernels  7.67 us (28%)
    ppermute x8, starting transfers between devices, swap(): return lax.ppermute(value, axis, [(i, i ^ flip) for i in range(count)])  11 us
    ppermute x8, waiting for transfers between devices, swap(): return lax.ppermute(value, axis, [(i, i ^ flip) for i in range(count)])  8.45 us
    pallas_call x1, Pallas kernels, x_factor(): pl.pallas_call(functools.partial(x_factor_kernel, plate), in_specs=[IN_VM...  2.14 us
    pallas_call x1, Pallas kernels, edges(): pl.pallas_call(edges_kernel, in_specs=[IN_HBM] * 2, out_shape=pltpu.VMEM(...  1.28 us
    pallas_call x1, Pallas kernels, finish(): pl.pallas_call(functools.partial(finish_kernel, len(ties) + 1), out_shape...  1.28 us
    pallas_call x1, Pallas kernels, load(): pl.pallas_call(load_kernel, in_specs=[IN_HBM] * len(values) + [ANYWHERE],...  1.24 us
    pallas_call x1, Pallas kernels, y_factor(): pl.pallas_call(y_factor_kernel, in_specs=[IN_VMEM, ANYWHERE], out_shape=[...  0.63 us
  transfers between devices with their start and end apart: 8, of which 6 were waited for; matrix products, arithmetic and copies ran while one was open for 0% of the time, Pallas kernels for 15%

profile of v8, /device:TPU:0, one launch (start us, length us, event | category | flops | bytes accessed | tf_op | source)
XLA Modules:
  0.0 27.2 jit_solution(5156676377350110915)
XLA Ops:
  0.0 1.3 %shard_map.46.refs_4_.own_cells = f32[64,128]{1,0:T(8,128)S(1)} custom-call(f32[4,64,512]{2,1,0:T(8,128)} %refs_0_.1, f32[4,64,512]{2,1,0:T(8,128)} %refs_1_.1), custom_call_target="tpu_custom_call" | custom-call | tf_op jit(solution)/shard_map/pallas_call | solution.py:163
  1.3 0.5 %collective-permute-start = (f32[64,128]{1,0:T(8,128)S(1)}, f32[64,128]{1,0:T(8,128)S(1)}, u32[]{:S(2)}, u32[]{:S(2)}) collective-permute-start(f32[64,128]{1,0:T(8,128)S(1)} %shard_map.46.refs_4_.own_cells), channel_id=1, source_target_pairs={{0,1},{1,0},{2,3},{3,2},{4,5},{5,4},{6,7},{7,6},{8,9},{9,8},{10,11... | collective-permute-start | bytes 98312 | tf_op jit(solution)/shard_map/ppermute | solution.py:448
  1.8 1.2 %shard_map.47 = (f32[4,64,512]{2,1,0:T(8,128)S(1)}, f32[4,64,512]{2,1,0:T(8,128)S(1)}, s32[1,64]{1,0:T(1,128)S(1)}, f32[1,64]{1,0:T(1,128)S(1)}) custom-call(f32[4,64,512]{2,1,0:T(8,128)} %refs_0_.1, f32[4,64,512]{2,1,0:T(8,128)} %refs_1_.1, s32[1,64]{1,0:T(1,128)} %bitcast.2, f32[1,64]{1,0:T(1,128)} %bitcast.3, f32[64,128]{1,0:T(8,128)S(1)} %shard_map.46.refs_4_.own_cells), custom_call_target="tpu_custom_call" | custom-call | bytes 2097152 | tf_op jit(solution)/shard_map/pallas_call | solution.py:189
  3.0 0.0 collective-permute-done.after.refs_0_
  3.1 2.6 %collective-permute-start.1 = (f32[64,128]{1,0:T(8,128)S(1)}, f32[64,128]{1,0:T(8,128)S(1)}, u32[]{:S(2)}, u32[]{:S(2)}) collective-permute-start(f32[64,128]{1,0:T(8,128)S(1)} %collective-permute-done.after.refs_0_), channel_id=1, source_target_pairs={{0,2},{1,3},{2,0},{3,1},{4,6},{5,7},{6,4},{7,5},{8,10},{9,11},{10,... | collective-permute-start | bytes 98312 | tf_op jit(solution)/shard_map/ppermute | solution.py:448
  5.7 2.1 %shard_map.48 = (f32[4,4,64,128]{3,2,1,0:T(8,128)S(1)}, f32[4,4,64,128]{3,2,1,0:T(8,128)S(1)}, f32[8,16,8,128]{3,2,1,0:T(8,128)S(1)}, f32[8,16,8,128]{3,2,1,0:T(...) custom-call(s32[1,64]{1,0:T(1,128)S(1)} %get-tuple-element.47.loc, ...), custom_call_target="tpu_custom_call" | custom-call | flops 5242880 | bytes 3670016 | tf_op jit(solution)/shard_map/pallas_call | solution.py:340
  7.8 0.0 collective-permute-done.1.refs_1_
  7.8 0.4 %shard_map.49 = (f32[8,8,8,128]{3,2,1,0:T(8,128)S(1)}, f32[7,16,128]{2,1,0:T(8,128)S(1)}, f32[7,16,128]{2,1,0:T(8,128)S(1)}) custom-call(f32[64,128]{1,0:T(8,128)S(1)} %shard_map.46.refs_4_.own_cells, f32[4,64,512]{2,1,0:T(8,128)S(1)} %get-tuple-element.46.t_ref.refs_12_, f32[4,4,64,128]{3,2,1,0:T(8,128)S(1)} %get-tuple-element.51.total_ref, ...), custom_call_target="tpu_custom_call" | custom-call | tf_op jit(solution)/shard_map/pallas_call | solution.py:427
  8.2 2.8 %collective-permute-start.2 = (f32[7,16,128]{2,1,0:T(8,128)S(1)}, f32[7,16,128]{2,1,0:T(8,128)S(1)}, u32[]{:S(2)}, u32[]{:S(2)}) collective-permute-start(f32[7,16,128]{2,1,0:T(8,128)S(1)} %get-tuple-element.58.after.refs_0_), channel_id=1, source_target_pairs={{0,12},{4,8},{8,4},{12,0},{16,28},{20,24},{24,20},{28,16},{1,13},{... | collective-permute-start | bytes 172040 | tf_op jit(solution)/shard_map/ppermute | solution.py:448
  11.0 0.4 %collective-permute-start.3 = (f32[7,16,128]{2,1,0:T(8,128)S(1)}, f32[7,16,128]{2,1,0:T(8,128)S(1)}, u32[]{:S(2)}, u32[]{:S(2)}) collective-permute-start(f32[7,16,128]{2,1,0:T(8,128)S(1)} %get-tuple-element.58.after.refs_0_), channel_id=1, source_target_pairs={{0,8},{4,12},{8,0},{12,4},{16,24},{20,28},{24,16},{28,20},{1,9},{5... | collective-permute-start | bytes 172040 | tf_op jit(solution)/shard_map/ppermute | solution.py:448
  11.5 0.3 %collective-permute-start.4 = (f32[7,16,128]{2,1,0:T(8,128)S(1)}, f32[7,16,128]{2,1,0:T(8,128)S(1)}, u32[]{:S(2)}, u32[]{:S(2)}) collective-permute-start(f32[7,16,128]{2,1,0:T(8,128)S(1)} %get-tuple-element.58.after.refs_0_), channel_id=1, source_target_pairs={{0,4},{4,0},{8,12},{12,8},{16,20},{20,16},{24,28},{28,24},{1,5},{5... | collective-permute-start | bytes 172040 | tf_op jit(solution)/shard_map/ppermute | solution.py:448
  11.8 0.6 %shard_map.50 = (f32[16,8,8,128]{3,2,1,0:T(8,128)S(1)}, f32[16,8,8,128]{3,2,1,0:T(8,128)S(1)}, f32[16,8,8,128]{3,2,1,0:T(8,128)S(1)}, f32[7,3,8,128]{3,2,1,0:T(8...) custom-call(f32[4,4,64,128]{3,2,1,0:T(8,128)S(1)} %get-tuple-element, ...), custom_call_target="tpu_custom_call" | custom-call | flops 2621440 | bytes 2097152 | tf_op jit(solution)/shard_map/pallas_call | solution.py:633
  12.4 0.2 shard_map.51
  12.6 0.9 %collective-permute-done.2.refs_1_ = f32[7,16,128]{2,1,0:T(8,128)S(1)} collective-permute-done((f32[7,16,128]{2,1,0:T(8,128)S(1)}, f32[7,16,128]{2,1,0:T(8,128)S(1)}, u32[]{:S(2)}, u32[]{:S(2)}) %collective-permute-start.2) | collective-permute-done | bytes 57376 | tf_op jit(solution)/shard_map/ppermute | solution.py:448
  13.5 1.7 %collective-permute-done.3.refs_2_ = f32[7,16,128]{2,1,0:T(8,128)S(1)} collective-permute-done((f32[7,16,128]{2,1,0:T(8,128)S(1)}, f32[7,16,128]{2,1,0:T(8,128)S(1)}, u32[]{:S(2)}, u32[]{:S(2)}) %collective-permute-start.3) | collective-permute-done | bytes 57376 | tf_op jit(solution)/shard_map/ppermute | solution.py:448
  15.2 0.4 %collective-permute-done.4.refs_3_ = f32[7,16,128]{2,1,0:T(8,128)S(1)} collective-permute-done((f32[7,16,128]{2,1,0:T(8,128)S(1)}, f32[7,16,128]{2,1,0:T(8,128)S(1)}, u32[]{:S(2)}, u32[]{:S(2)}) %collective-permute-start.4) | collective-permute-done | bytes 57376 | tf_op jit(solution)/shard_map/ppermute | solution.py:448
  15.6 0.1 shard_map.52
  15.7 2.7 %collective-permute-start.5 = (f32[3,16,128]{2,1,0:T(8,128)S(1)}, f32[3,16,128]{2,1,0:T(8,128)S(1)}, u32[]{:S(2)}, u32[]{:S(2)}) collective-permute-start(f32[3,16,128]{2,1,0:T(8,128)S(1)} %get-tuple-element.62.refs_0_), channel_id=1, source_target_pairs={{0,16},{4,20},{8,24},{12,28},{16,0},{20,4},{24,8},{28,12},{1,17},{... | collective-permute-start | bytes 73736 | tf_op jit(solution)/shard_map/ppermute | solution.py:448
  18.3 2.1 %collective-permute-done.5.refs_1_ = f32[3,16,128]{2,1,0:T(8,128)S(1)} collective-permute-done((f32[3,16,128]{2,1,0:T(8,128)S(1)}, f32[3,16,128]{2,1,0:T(8,128)S(1)}, u32[]{:S(2)}, u32[]{:S(2)}) %collective-permute-start.5) | collective-permute-done | bytes 24608 | tf_op jit(solution)/shard_map/ppermute | solution.py:448
  20.5 0.5 %shard_map.53 = (f32[16,8,8,128]{3,2,1,0:T(8,128)S(1)}, f32[7,8,128]{2,1,0:T(8,128)S(1)}, f32[3,2,128]{2,1,0:T(2,128)S(1)}, f32[7,2,128]{2,1,0:T(2,128)S(1)}) custom-call(f32[3,16,128]{2,1,0:T(8,128)S(1)} %get-tuple-element.62.refs_0_, f32[3,16,128]{2,1,0:T(8,128)S(1)} %collective-permute-done.5.refs_1_, f32[3,16,128]{2,1,0:T(8,128)S(1)} %get-tuple-element.63.refs_2_, ...), custom_call_target="tpu_custom_call" | custom-call | tf_op jit(solution)/shard_map/pallas_call | solution.py:769
  21.0 0.1 collective-permute-start.6
  21.1 1.2 %collective-permute-done.6.refs_1_ = f32[7,2,128]{2,1,0:T(2,128)S(1)} collective-permute-done((f32[7,2,128]{2,1,0:T(2,128)S(1)}, f32[7,2,128]{2,1,0:T(2,128)S(1)}, u32[]{:S(2)}, u32[]{:S(2)}) %collective-permute-start.6) | collective-permute-done | bytes 7200 | tf_op jit(solution)/shard_map/ppermute | solution.py:448
  22.2 1.6 %collective-permute-start.7 = (f32[3,2,128]{2,1,0:T(2,128)S(1)}, f32[3,2,128]{2,1,0:T(2,128)S(1)}, u32[]{:S(2)}, u32[]{:S(2)}) collective-permute-start(f32[3,2,128]{2,1,0:T(2,128)S(1)} %get-tuple-element.76.refs_0_), channel_id=1, source_target_pairs={{0,2},{1,3},{2,0},{3,1},{4,6},{5,7},{6,4},{7,5},{8,10},{9,11},{10,... | collective-permute-start | bytes 9224 | tf_op jit(solution)/shard_map/ppermute | solution.py:448
  23.8 2.1 %collective-permute-done.7.refs_1_ = f32[3,2,128]{2,1,0:T(2,128)S(1)} collective-permute-done((f32[3,2,128]{2,1,0:T(2,128)S(1)}, f32[3,2,128]{2,1,0:T(2,128)S(1)}, u32[]{:S(2)}, u32[]{:S(2)}) %collective-permute-start.7) | collective-permute-done | bytes 3104 | tf_op jit(solution)/shard_map/ppermute | solution.py:448
  25.9 1.3 %shard_map.55 = f32[4,64,512]{2,1,0:T(8,128)} custom-call(f32[3,2,128]{2,1,0:T(2,128)S(1)} %get-tuple-element.76.refs_0_, f32[3,2,128]{2,1,0:T(2,128)S(1)} %collective-permute-done.7.refs_1_, f32[3,2,128]{2,1,0:T(2,128)S(1)} %get-tuple-element.77.refs_2_, f32[16,8,8,128]{3,2,1,0:T(8,128)S(1)} %get-tuple-element.69.refs_11_.refs_3_, ...), custom_call_target="tpu_custom_call" | custom-call | tf_op jit(solution)/shard_map/pallas_call | solution.py:844
  (1 shorter events, 0.0 us)
Async XLA Ops:
  1.3 1.8 %collective-permute-start = (f32[64,128]{1,0:T(8,128)S(1)}, f32[64,128]{1,0:T(8,128)S(1)}, u32[]{:S(2)}, u32[]{:S(2)}) collective-permute-start(f32[64,128]{1,0:T(8,128)S(1)} %shard_map.46.refs_4_.own_cells), channel_id=1, source_target_pairs={{0,1},{1,0},{2,3},{3,2},{4,5},{5,4},{6,7},{7,6},{8,9},{9,8},{10,11... | collective-permute-start | bytes 98312 | tf_op jit(solution)/shard_map/ppermute | solution.py:448
  3.1 4.7 %collective-permute-start.1 = (f32[64,128]{1,0:T(8,128)S(1)}, f32[64,128]{1,0:T(8,128)S(1)}, u32[]{:S(2)}, u32[]{:S(2)}) collective-permute-start(f32[64,128]{1,0:T(8,128)S(1)} %collective-permute-done.after.refs_0_), channel_id=1, source_target_pairs={{0,2},{1,3},{2,0},{3,1},{4,6},{5,7},{6,4},{7,5},{8,10},{9,11},{10,... | collective-permute-start | bytes 98312 | tf_op jit(solution)/shard_map/ppermute | solution.py:448
  8.2 5.3 %collective-permute-start.2 = (f32[7,16,128]{2,1,0:T(8,128)S(1)}, f32[7,16,128]{2,1,0:T(8,128)S(1)}, u32[]{:S(2)}, u32[]{:S(2)}) collective-permute-start(f32[7,16,128]{2,1,0:T(8,128)S(1)} %get-tuple-element.58.after.refs_0_), channel_id=1, source_target_pairs={{0,12},{4,8},{8,4},{12,0},{16,28},{20,24},{24,20},{28,16},{1,13},{... | collective-permute-start | bytes 172040 | tf_op jit(solution)/shard_map/ppermute | solution.py:448
  11.0 4.2 %collective-permute-start.3 = (f32[7,16,128]{2,1,0:T(8,128)S(1)}, f32[7,16,128]{2,1,0:T(8,128)S(1)}, u32[]{:S(2)}, u32[]{:S(2)}) collective-permute-start(f32[7,16,128]{2,1,0:T(8,128)S(1)} %get-tuple-element.58.after.refs_0_), channel_id=1, source_target_pairs={{0,8},{4,12},{8,0},{12,4},{16,24},{20,28},{24,16},{28,20},{1,9},{5... | collective-permute-start | bytes 172040 | tf_op jit(solution)/shard_map/ppermute | solution.py:448
  11.5 4.2 %collective-permute-start.4 = (f32[7,16,128]{2,1,0:T(8,128)S(1)}, f32[7,16,128]{2,1,0:T(8,128)S(1)}, u32[]{:S(2)}, u32[]{:S(2)}) collective-permute-start(f32[7,16,128]{2,1,0:T(8,128)S(1)} %get-tuple-element.58.after.refs_0_), channel_id=1, source_target_pairs={{0,4},{4,0},{8,12},{12,8},{16,20},{20,16},{24,28},{28,24},{1,5},{5... | collective-permute-start | bytes 172040 | tf_op jit(solution)/shard_map/ppermute | solution.py:448
  15.7 4.8 %collective-permute-start.5 = (f32[3,16,128]{2,1,0:T(8,128)S(1)}, f32[3,16,128]{2,1,0:T(8,128)S(1)}, u32[]{:S(2)}, u32[]{:S(2)}) collective-permute-start(f32[3,16,128]{2,1,0:T(8,128)S(1)} %get-tuple-element.62.refs_0_), channel_id=1, source_target_pairs={{0,16},{4,20},{8,24},{12,28},{16,0},{20,4},{24,8},{28,12},{1,17},{... | collective-permute-start | bytes 73736 | tf_op jit(solution)/shard_map/ppermute | solution.py:448
  21.0 1.2 %collective-permute-start.6 = (f32[7,2,128]{2,1,0:T(2,128)S(1)}, f32[7,2,128]{2,1,0:T(2,128)S(1)}, u32[]{:S(2)}, u32[]{:S(2)}) collective-permute-start(f32[7,2,128]{2,1,0:T(2,128)S(1)} %get-tuple-element.75.refs_0_), channel_id=1, source_target_pairs={{0,1},{1,0},{2,3},{3,2},{4,5},{5,4},{6,7},{7,6},{8,9},{9,8},{10,11... | collective-permute-start | bytes 21512 | tf_op jit(solution)/shard_map/ppermute | solution.py:448
  22.2 3.7 %collective-permute-start.7 = (f32[3,2,128]{2,1,0:T(2,128)S(1)}, f32[3,2,128]{2,1,0:T(2,128)S(1)}, u32[]{:S(2)}, u32[]{:S(2)}) collective-permute-start(f32[3,2,128]{2,1,0:T(2,128)S(1)} %get-tuple-element.76.refs_0_), channel_id=1, source_target_pairs={{0,2},{1,3},{2,0},{3,1},{4,6},{5,7},{6,4},{7,5},{8,10},{9,11},{10,... | collective-permute-start | bytes 9224 | tf_op jit(solution)/shard_map/ppermute | solution.py:448

commit v9 on v8

--- a/solution.py
+++ b/solution.py
@@ -528,20 +528,28 @@
     return view, swap(view, axis, 1 << stage), links
 
 
-def block_ends(axis, own, got, links):
-    top = len(links)
-    right = on_right(axis, top)
+def top_flux(axis, stages, own, got):
+    right = on_right(axis, stages - 1)
     face = own[2] + got[2]
     jump = jnp.where(right, own[1] - got[1], got[1] - own[1])
-    flux = jump * face * inverse(1.0 + face * (own[0] + got[0]))
-    low = jnp.where(right, -flux, 0.0)
-    high = jnp.where(right, 0.0, flux)
-    for stage in range(top - 1, -1, -1):
+    return jump * face * inverse(1.0 + face * (own[0] + got[0]))
+
+
+def block_ends(axis, stages, links):
+    shape = links[0].shape[1:] if links else None
+    right = on_right(axis, stages - 1)
+    zero = jnp.zeros(shape, F32)
+    low, high = zero, zero
+    unit_low = zero + jnp.where(right, -1.0, 0.0)
+    unit_high = zero + jnp.where(right, 0.0, 1.0)
+    for stage in range(stages - 2, -1, -1):
         tie = links[stage]
         right = on_right(axis, stage)
         flux = between(tie[0], tie[1], tie[2], low, high)
+        unit = between(0.0, tie[1], tie[2], unit_low, unit_high)
         low, high = jnp.where(right, -flux, low), jnp.where(right, high, flux)
-    return low, high
+        unit_low, unit_high = jnp.where(right, -unit, unit_low), jnp.where(right, unit_high, unit)
+    return (low, high), (unit_low, unit_high)
 
 
 def natural(index, parts):
@@ -694,48 +702,95 @@
 
 def tree_ends(leaves, links, own, low, high):
     levels = [
-        [(own[offset + n], links[offset + n, 1], links[offset + n, 2]) for n in range(count)]
+        [(own(offset + n), links[offset + n, 1], links[offset + n, 2]) for n in range(count)]
         for offset, count in node_offsets(leaves)
     ]
     return descend(levels, low, high)
 
 
-def y_target_kernel(stages, *refs):
-    own, got = refs[:2]
-    ties = refs[2 : 1 + stages]
-    xw, xh, xm, xp, x_links, x_own, t_ref, yw, yi, yp, inner, outer, view, to_y = refs[1 + stages : 15 + stages]
-    h_ref, inner_own, outer_own, send = refs[15 + stages : 19 + stages]
-    f_s, g_s, q_s, r_s = refs[19 + stages :]
+def nothing(node):
+    return 0.0
+
+
+def y_prepare_kernel(stages, *refs):
+    ties = refs[: stages - 1]
+    xw, xh, xm, xp, x_links, x_own, t_ref, to_y = refs[stages - 1 : stages + 7]
+    base, response, f_s, g_s = refs[stages + 7 :]
     x_steps, lines = xw.shape[:2]
-    chunks = g_s.shape[0]
+    chunks = base.shape[0]
     sheets = lines // chunks
     rows = x_steps * SUBLANES
-    pairs = sheets * rows // LANES
-    steps = yw.shape[0]
-
-    low, high = block_ends("gx", own, got, ties)
-    for s, ends in enumerate(tree_ends(SUBLANES, x_links, x_own, low, high)):
-        for i in range(2):
-            f_s[i, pl.ds(s, lines, stride=SUBLANES), :] = ends[i]
+
+    ends, units = block_ends("gx", stages, ties)
+    for n, (own, (low, high)) in enumerate(((lambda i: x_own[i], ends), (nothing, units))):
+        for s, pair in enumerate(tree_ends(SUBLANES, x_links, own, low, high)):
+            for i in range(2):
+                f_s[n, i, pl.ds(s, lines, stride=SUBLANES), :] = pair[i]
     first = 0
     for n, members in enumerate(line_groups(chunks, sheets)):
         at = slice(first, first + len(members))
         h_ref_of, h_at = (xh, at) if n == 0 else (xm, slice(first - 2 * sheets, at.stop - 2 * sheets))
-        low, value = (
-            jnp.stack(
-                [f_s[i, j * SUBLANES : (j + 1) * SUBLANES, :] for j in range(at.start, at.stop)], 0
-            )
-            for i in range(2)
+        (low, value), (unit_low, unit) = (
+            [
+                jnp.stack(
+                    [f_s[q, i, j * SUBLANES : (j + 1) * SUBLANES, :] for j in range(at.start, at.stop)], 0
+                )
+                for i in range(2)
+            ]
+            for q in range(2)
         )
         for k in range(x_steps - 1, -1, -1):
-            value = xw[k, at] * value + (h_ref_of[k, h_at] + xp[k, at] * low)
+            w, p = xw[k, at], xp[k, at]
+            value = w * value + (h_ref_of[k, h_at] + p * low)
+            unit = w * unit + p * unit_low
             field = value - t_ref[k, at]
             for j, (y, z) in enumerate(members):
                 place = z * rows + k * SUBLANES
-                g_s[y, place : place + SUBLANES, :] = field[j]
+                g_s[0, y, place : place + SUBLANES, :] = field[j]
+                g_s[1, y, place : place + SUBLANES, :] = unit[j]
         first = at.stop
 
-    fields = [turned(to_y[...], g_s[y]) for y in range(chunks)]
+    for y in range(chunks):
+        base[y] = turned(to_y[...], g_s[0, y])
+        response[y] = turned(to_y[...], g_s[1, y])
+
+
+def y_prepare(ties, xw, xh, xm, xp, x_links, x_own, t, to_y, chunks):
+    x_steps, lines = xw.shape[:2]
+    width = lines // chunks * x_steps * SUBLANES
+    field = shape_of(chunks, LANES, width)
+    return pl.pallas_call(
+        functools.partial(y_prepare_kernel, len(ties) + 1),
+        out_shape=[field, field],
+        scratch_shapes=[
+            pltpu.VMEM((2, 2, lines * SUBLANES, LANES), F32),
+            pltpu.VMEM((2, chunks, width, LANES), F32),
+        ],
+        compiler_params=params(),
+        cost_estimate=pl.CostEstimate(flops=8 * t.size, bytes_accessed=16 * t.size, transcendentals=0),
+    )(*ties, xw, xh, xm, xp, x_links, x_own, t, to_y)
+
+
+def y_target_kernel(stages, own, got, base, response, yw, yi, yp, inner, outer, view, to_y, *refs):
+    h_ref, inner_own, outer_own, send, q_s, r_s = refs
+    chunks, _, width = base.shape
+    pairs = width // LANES
+    sheets = own.shape[1] // chunks
+    rows = width // sheets
+    steps = yw.shape[0]
+
+    flux = top_flux("gx", stages, own, got)
+    line_of = {member: n for n, member in enumerate(sum(line_groups(chunks, sheets), []))}
+    fields = []
+    for y in range(chunks):
+        spread = jnp.concatenate(
+            [
+                jnp.broadcast_to(flux[line_of[y, z] : line_of[y, z] + 1, :], (rows, LANES))
+                for z in range(sheets)
+            ],
+            0,
+        )
+        fields.append(base[y] + response[y] * turned(to_y[...], spread))
 
     def target(k):
         at = slice(k * SUBLANES, (k + 1) * SUBLANES)
@@ -761,13 +816,12 @@
     send[FIRST], send[LAST] = join_tree(items, outer, outer_own)
 
 
-def y_target(own, got, ties, xw, xh, xm, xp, x_links, x_own, t, yw, yi, yp, inner, outer, view, to_y):
-    x_steps, lines = xw.shape[:2]
+def y_target(own, got, base, response, yw, yi, yp, inner, outer, view, to_y):
     y_lines = yw.shape[1]
     pairs = view.shape[1]
     chunks = y_lines // pairs
     return pl.pallas_call(
-        functools.partial(y_target_kernel, len(ties) + 1),
+        functools.partial(y_target_kernel, stages_of("gx")),
         out_shape=[
             shape_of(*yw.shape),
             shape_of(SUBLANES - 1, y_lines, LANES),
@@ -775,85 +829,145 @@
             shape_of(7, pairs, LANES),
         ],
         scratch_shapes=[
-            pltpu.VMEM((2, lines * SUBLANES, LANES), F32),
-            pltpu.VMEM((chunks, pairs * LANES, LANES), F32),
             pltpu.VMEM((2, y_lines * SUBLANES, LANES), F32),
             pltpu.VMEM((2, y_lines, LANES), F32),
         ],
         compiler_params=params(),
-    )(own, got, *ties, xw, xh, xm, xp, x_links, x_own, t, yw, yi, yp, inner, outer, view, to_y)
-
-
-def finish_kernel(stages, *refs):
-    own, got = refs[:2]
-    ties = refs[2 : 1 + stages]
-    yw, yh, yp, inner, inner_own, outer, outer_own, zw, zi, t_ref, to_x = refs[1 + stages : 12 + stages]
-    out, r_s, e_s, u_s, o_s, sems = refs[12 + stages :]
-    chunks, sheets, rows, _ = o_s.shape
+    )(own, got, base, response, yw, yi, yp, inner, outer, view, to_y)
+
+
+def z_solve(zw, zi, field, at, keep):
+    sheets = zi.shape[0]
+    rhs, kept = None, []
+    for z in range(sheets):
+        rhs = field(z) if z == 0 else field(z) + zw[z - 1, at] * rhs
+        kept.append(rhs * zi[z, at])
+    value = kept[-1]
+    keep(sheets - 1, value)
+    for z in range(sheets - 2, -1, -1):
+        value = zw[z, at] * value + kept[z]
+        keep(z, value)
+
+
+def finish_prepare_kernel(stages, *refs):
+    ties = refs[: stages - 1]
+    yw, yh, yp, inner, inner_own, outer, outer_own, zw, zi, t_ref, to_x = refs[stages - 1 : stages + 10]
+    base, response, r_s, e_s, u_s = refs[stages + 10 :]
+    chunks, sheets, rows, _ = base.shape
     each = LANES // rows
     pairs = sheets // each
     steps = yw.shape[0]
     lines = chunks * pairs
 
-    low, high = block_ends("gy", own, got, ties)
-    for y, ends in enumerate(tree_ends(chunks, outer, outer_own, low, high)):
-        for i in range(2):
-            r_s[i, y * pairs : (y + 1) * pairs, :] = ends[i]
-    for s, ends in enumerate(tree_ends(SUBLANES, inner, inner_own, r_s[0], r_s[1])):
-        for i in range(2):
-            e_s[i, pl.ds(s, lines, stride=SUBLANES), :] = ends[i]
-    low, value = (
-        jnp.stack([e_s[i, n * SUBLANES : (n + 1) * SUBLANES, :] for n in range(lines)], 0)
-        for i in range(2)
+    ends, units = block_ends("gy", stages, ties)
+    both = (
+        (lambda i: outer_own[i], lambda i: inner_own[i], ends),
+        (nothing, nothing, units),
+    )
+    for n, (upper, lower, (low, high)) in enumerate(both):
+        for y, pair in enumerate(tree_ends(chunks, outer, upper, low, high)):
+            for i in range(2):
+                r_s[n, i, y * pairs : (y + 1) * pairs, :] = pair[i]
+        for s, pair in enumerate(tree_ends(SUBLANES, inner, lower, r_s[n, 0], r_s[n, 1])):
+            for i in range(2):
+                e_s[n, i, pl.ds(s, lines, stride=SUBLANES), :] = pair[i]
+    (low, value), (unit_low, unit) = (
+        [
+            jnp.stack([e_s[q, i, n * SUBLANES : (n + 1) * SUBLANES, :] for n in range(lines)], 0)
+            for i in range(2)
+        ]
+        for q in range(2)
     )
     for k in range(steps - 1, -1, -1):
-        value = yw[k] * value + (yh[k] + yp[k] * low)
+        w, p = yw[k], yp[k]
+        value = w * value + (yh[k] + p * low)
+        unit = w * unit + p * unit_low
         for y in range(chunks):
             for m in range(pairs):
-                u_s[m, pl.ds(y * LANES + k, SUBLANES, stride=steps), :] = value[y * pairs + m]
-
-    copies = []
-    for first in range(0, chunks, 2):
-        both = slice(first * LANES, (first + 2) * LANES)
-        fields = [turned(to_x[...], u_s[m, both, :]) for m in range(pairs)]
-        for y in range(first, first + 2):
-            part = part_of(y)
-            rhs, kept = None, []
-            for z in range(sheets):
-                at = z % each * rows
-                own_rhs = fields[z // each][at : at + rows, part_of(y - first)]
-                rhs = own_rhs if z == 0 else own_rhs + zw[z - 1, y] * rhs
-                kept.append(rhs * zi[z, y])
-            value = kept[-1]
-            o_s[y, sheets - 1] = t_ref[sheets - 1, :, part] + value
-            for z in range(sheets - 2, -1, -1):
-                value = zw[z, y] * value + kept[z]
-                o_s[y, z] = t_ref[z, :, part] + value
-            copy = pltpu.make_async_copy(o_s.at[y], out.at[:, :, pl.ds(y * LANES, LANES)], sems.at[y])
-            copy.start()
-            copies.append(copy)
-    for copy in copies:
-        copy.wait()
-
-
-def finish(own, got, ties, yw, yh, yp, inner, inner_own, outer, outer_own, zw, zi, t, to_x):
+                place = pl.ds(y * LANES + k, SUBLANES, stride=steps)
+                u_s[0, m, place, :] = value[y * pairs + m]
+                u_s[1, m, place, :] = unit[y * pairs + m]
+
+    for y in range(chunks):
+        part = part_of(y)
+        fields = [turned(to_x[...], u_s[0, m, part, :]) for m in range(pairs)]
+
+        def field(z):
+            at = z % each * rows
+            return fields[z // each][at : at + rows, :]
+
+        def keep(z, value):
+            base[y, z] = t_ref[z, :, part] + value
+
+        z_solve(zw, zi, field, y, keep)
+        for m in range(pairs):
+            units = turned(to_x[...], u_s[1, m, part, :])
+            for i in range(each):
+                response[y, m * each + i] = units[i * rows : (i + 1) * rows, :]
+
+
+def finish_prepare(ties, yw, yh, yp, inner, inner_own, outer, outer_own, zw, zi, t, to_x):
     sheets, rows, columns = t.shape
     chunks = columns // LANES
     pairs = sheets * rows // LANES
     lines = chunks * pairs
+    field = shape_of(chunks, sheets, rows, LANES)
     return pl.pallas_call(
-        functools.partial(finish_kernel, len(ties) + 1),
-        out_shape=shape_of(sheets, rows, columns),
+        functools.partial(finish_prepare_kernel, len(ties) + 1),
+        out_shape=[field, field],
+        scratch_shapes=[
+            pltpu.VMEM((2, 2, lines, LANES), F32),
+            pltpu.VMEM((2, 2, lines * SUBLANES, LANES), F32),
+            pltpu.VMEM((2, pairs, columns, LANES), F32),
+        ],
+        compiler_params=params(),
+        cost_estimate=pl.CostEstimate(flops=12 * t.size, bytes_accessed=20 * t.size, transcendentals=0),
+    )(*ties, yw, yh, yp, inner, inner_own, outer, outer_own, zw, zi, t, to_x)
+
+
+def finish_kernel(stages, own, got, base, response, zw, zi, to_x, out, o_s, sems):
+    chunks, sheets, rows, _ = base.shape
+    each = LANES // rows
+    pairs = sheets // each
+    copies, _, _, wide = o_s.shape
+
+    flux = top_flux("gy", stages, own, got)
+    spread = [
+        turned(to_x[...], jnp.broadcast_to(flux[m : m + 1, :], (LANES, LANES))) for m in range(pairs)
+    ]
+    started = []
+    for n in range(copies):
+        for y in range(n * chunks // copies, (n + 1) * chunks // copies):
+            part = part_of(y - n * chunks // copies)
+
+            def field(z):
+                at = z % each * rows
+                return response[y, z] * spread[z // each][at : at + rows, :]
+
+            def keep(z, value):
+                o_s[n, z, :, part] = base[y, z] + value
+
+            z_solve(zw, zi, field, y, keep)
+        copy = pltpu.make_async_copy(o_s.at[n], out.at[:, :, pl.ds(n * wide, wide)], sems.at[n])
+        copy.start()
+        started.append(copy)
+    for copy in started:
+        copy.wait()
+
+
+def finish(own, got, base, response, zw, zi, to_x):
+    chunks, sheets, rows, _ = base.shape
+    copies = 2
+    return pl.pallas_call(
+        functools.partial(finish_kernel, stages_of("gy")),
+        out_shape=shape_of(sheets, rows, chunks * LANES),
         out_specs=ANYWHERE,
         scratch_shapes=[
-            pltpu.VMEM((2, lines, LANES), F32),
-            pltpu.VMEM((2, lines * SUBLANES, LANES), F32),
-            pltpu.VMEM((pairs, columns, LANES), F32),
-            pltpu.VMEM((chunks, sheets, rows, LANES), F32),
-            pltpu.SemaphoreType.DMA((chunks,)),
+            pltpu.VMEM((copies, sheets, rows, chunks * LANES // copies), F32),
+            pltpu.SemaphoreType.DMA((copies,)),
         ],
         compiler_params=params(),
-    )(own, got, *ties, yw, yh, yp, inner, inner_own, outer, outer_own, zw, zi, t, to_x)
+    )(own, got, base, response, zw, zi, to_x)
 
 
 def per_device(temperature, base, locations, energy):
@@ -871,11 +985,17 @@
     yw, yi, yp, inner, outer, y_view, to_y, to_x = y_factor(c, x_view)
     zw, zi = z_factor(c, view)
     own, got, ties = gather_line(view, "gx", 2, (y_view, zw))
+    base, response = y_prepare(
+        ties, xw, xh, xm, xp, x_links, x_own, t_steps, to_y, columns // LANES
+    )
     yh, inner_own, outer_own, view = y_target(
-        own, got, ties, xw, xh, xm, xp, x_links, x_own, t_steps, yw, yi, yp, inner, outer, y_view, to_y
+        own, got, base, response, yw, yi, yp, inner, outer, y_view, to_y
     )
     own, got, ties = gather_line(view, "gy")
-    return finish(own, got, ties, yw, yh, yp, inner, inner_own, outer, outer_own, zw, zi, t, to_x)
+    base, response = finish_prepare(
+        ties, yw, yh, yp, inner, inner_own, outer, outer_own, zw, zi, t, to_x
+    )
+    return finish(own, got, base, response, zw, zi, to_x)
 
 
 def solution(mesh):

time: 27.3 us -> 28.3 us (1.037)
  Pallas kernels: 7.67 us -> 8.8 us
    pallas_call x2 -> x4, Pallas kernels: 1.77 us -> 2.91 us  [the longest x1 1.15 us: finish(): pl.pallas_call(functools.partial(finish_kernel, stages_of('gy')), out_sha...]
  transfers between devices with their start and end apart: 8 -> 8, of which waited for: 6 -> 5; matrix products, arithmetic and copies ran while one was open for 0% -> 0% of each run, Pallas kernels for 15% -> 20%
where the time goes in v9:
time: 28.3 us; the launch traced here: 28.1 us
  starting transfers between devices  11 us (39%)
  Pallas kernels  8.8 us (31%)
  waiting for transfers between devices  8.23 us (29%)
    ppermute x8, starting transfers between devices, swap(): return lax.ppermute(value, axis, [(i, i ^ flip) for i in range(count)])  11 us
    ppermute x8, waiting for transfers between devices, swap(): return lax.ppermute(value, axis, [(i, i ^ flip) for i in range(count)])  8.23 us
    pallas_call x1, Pallas kernels, x_factor(): pl.pallas_call(functools.partial(x_factor_kernel, plate), in_specs=[IN_VM...  2.13 us
    pallas_call x1, Pallas kernels, edges(): pl.pallas_call(edges_kernel, in_specs=[IN_HBM] * 2, out_shape=pltpu.VMEM(...  1.28 us
    pallas_call x1, Pallas kernels, load(): pl.pallas_call(load_kernel, in_specs=[IN_HBM] * len(values) + [ANYWHERE],...  1.24 us
    pallas_call x1, Pallas kernels, finish(): pl.pallas_call(functools.partial(finish_kernel, stages_of('gy')), out_sha...  1.15 us
    pallas_call x1, Pallas kernels, finish_prepare(): pl.pallas_call(functools.partial(finish_prepare_kernel, len(ties) + 1), o...  0.79 us
    pallas_call x1, Pallas kernels, y_factor(): pl.pallas_call(y_factor_kernel, in_specs=[IN_VMEM, ANYWHERE], out_shape=[...  0.63 us
  transfers between devices with their start and end apart: 8, of which 5 were waited for; matrix products, arithmetic and copies ran while one was open for 0% of the time, Pallas kernels for 20%

profile of v9, /device:TPU:0, one launch (start us, length us, event | category | flops | bytes accessed | tf_op | source)
XLA Modules:
  0.0 28.1 jit_solution(14422929986284099515)
XLA Ops:
  0.0 1.3 %shard_map.46.refs_4_.own_cells = f32[64,128]{1,0:T(8,128)S(1)} custom-call(f32[4,64,512]{2,1,0:T(8,128)} %refs_0_.1, f32[4,64,512]{2,1,0:T(8,128)} %refs_1_.1), custom_call_target="tpu_custom_call" | custom-call | tf_op jit(solution)/shard_map/pallas_call | solution.py:163
  1.3 0.5 %collective-permute-start = (f32[64,128]{1,0:T(8,128)S(1)}, f32[64,128]{1,0:T(8,128)S(1)}, u32[]{:S(2)}, u32[]{:S(2)}) collective-permute-start(f32[64,128]{1,0:T(8,128)S(1)} %shard_map.46.refs_4_.own_cells), channel_id=1, source_target_pairs={{0,1},{1,0},{2,3},{3,2},{4,5},{5,4},{6,7},{7,6},{8,9},{9,8},{10,11... | collective-permute-start | bytes 98312 | tf_op jit(solution)/shard_map/ppermute | solution.py:448
  1.8 1.2 %shard_map.47 = (f32[4,64,512]{2,1,0:T(8,128)S(1)}, f32[4,64,512]{2,1,0:T(8,128)S(1)}, s32[1,64]{1,0:T(1,128)S(1)}, f32[1,64]{1,0:T(1,128)S(1)}) custom-call(f32[4,64,512]{2,1,0:T(8,128)} %refs_0_.1, f32[4,64,512]{2,1,0:T(8,128)} %refs_1_.1, s32[1,64]{1,0:T(1,128)} %bitcast.2, f32[1,64]{1,0:T(1,128)} %bitcast.3, f32[64,128]{1,0:T(8,128)S(1)} %shard_map.46.refs_4_.own_cells), custom_call_target="tpu_custom_call" | custom-call | bytes 2097152 | tf_op jit(solution)/shard_map/pallas_call | solution.py:189
  3.0 0.0 collective-permute-done.after.refs_0_
  3.1 2.6 %collective-permute-start.1 = (f32[64,128]{1,0:T(8,128)S(1)}, f32[64,128]{1,0:T(8,128)S(1)}, u32[]{:S(2)}, u32[]{:S(2)}) collective-permute-start(f32[64,128]{1,0:T(8,128)S(1)} %collective-permute-done.after.refs_0_), channel_id=1, source_target_pairs={{0,2},{1,3},{2,0},{3,1},{4,6},{5,7},{6,4},{7,5},{8,10},{9,11},{10,... | collective-permute-start | bytes 98312 | tf_op jit(solution)/shard_map/ppermute | solution.py:448
  5.7 2.1 %shard_map.48 = (f32[4,4,64,128]{3,2,1,0:T(8,128)S(1)}, f32[4,4,64,128]{3,2,1,0:T(8,128)S(1)}, f32[8,16,8,128]{3,2,1,0:T(8,128)S(1)}, f32[8,16,8,128]{3,2,1,0:T(...) custom-call(s32[1,64]{1,0:T(1,128)S(1)} %get-tuple-element.51.loc, ...), custom_call_target="tpu_custom_call" | custom-call | flops 5242880 | bytes 3670016 | tf_op jit(solution)/shard_map/pallas_call | solution.py:340
  7.8 0.0 collective-permute-done.1.refs_1_
  7.8 0.4 %shard_map.49 = (f32[8,8,8,128]{3,2,1,0:T(8,128)S(1)}, f32[7,16,128]{2,1,0:T(8,128)S(1)}, f32[7,16,128]{2,1,0:T(8,128)S(1)}) custom-call(f32[64,128]{1,0:T(8,128)S(1)} %shard_map.46.refs_4_.own_cells, f32[4,64,512]{2,1,0:T(8,128)S(1)} %get-tuple-element.50.t_ref.refs_10_, f32[4,4,64,128]{3,2,1,0:T(8,128)S(1)} %get-tuple-element.55.total_ref, ...), custom_call_target="tpu_custom_call" | custom-call | tf_op jit(solution)/shard_map/pallas_call | solution.py:427
  8.2 1.8 %collective-permute-start.4 = (f32[7,16,128]{2,1,0:T(8,128)S(1)}, f32[7,16,128]{2,1,0:T(8,128)S(1)}, u32[]{:S(2)}, u32[]{:S(2)}) collective-permute-start(f32[7,16,128]{2,1,0:T(8,128)S(1)} %get-tuple-element.62.after.refs_0_), channel_id=1, source_target_pairs={{0,4},{4,0},{8,12},{12,8},{16,20},{20,16},{24,28},{28,24},{1,5},{5... | collective-permute-start | bytes 172040 | tf_op jit(solution)/shard_map/ppermute | solution.py:448
  10.0 1.6 %collective-permute-start.3 = (f32[7,16,128]{2,1,0:T(8,128)S(1)}, f32[7,16,128]{2,1,0:T(8,128)S(1)}, u32[]{:S(2)}, u32[]{:S(2)}) collective-permute-start(f32[7,16,128]{2,1,0:T(8,128)S(1)} %get-tuple-element.62.after.refs_0_), channel_id=1, source_target_pairs={{0,8},{4,12},{8,0},{12,4},{16,24},{20,28},{24,16},{28,20},{1,9},{5... | collective-permute-start | bytes 172040 | tf_op jit(solution)/shard_map/ppermute | solution.py:448
  11.6 0.2 collective-permute-start.2
  11.8 0.6 %shard_map.50 = (f32[16,8,8,128]{3,2,1,0:T(8,128)S(1)}, f32[16,8,8,128]{3,2,1,0:T(8,128)S(1)}, f32[16,8,8,128]{3,2,1,0:T(8,128)S(1)}, f32[7,3,8,128]{3,2,1,0:T(8...) custom-call(f32[4,4,64,128]{3,2,1,0:T(8,128)S(1)} %get-tuple-element, ...), custom_call_target="tpu_custom_call" | custom-call | flops 2621440 | bytes 2097152 | tf_op jit(solution)/shard_map/pallas_call | solution.py:641
  12.4 0.2 shard_map.51
  12.6 0.0 collective-permute-done.4.refs_3_
  12.6 2.2 %collective-permute-done.3.refs_2_ = f32[7,16,128]{2,1,0:T(8,128)S(1)} collective-permute-done((f32[7,16,128]{2,1,0:T(8,128)S(1)}, f32[7,16,128]{2,1,0:T(8,128)S(1)}, u32[]{:S(2)}, u32[]{:S(2)}) %collective-permute-start.3) | collective-permute-done | bytes 57376 | tf_op jit(solution)/shard_map/ppermute | solution.py:448
  14.8 1.9 %collective-permute-done.2.refs_1_ = f32[7,16,128]{2,1,0:T(8,128)S(1)} collective-permute-done((f32[7,16,128]{2,1,0:T(8,128)S(1)}, f32[7,16,128]{2,1,0:T(8,128)S(1)}, u32[]{:S(2)}, u32[]{:S(2)}) %collective-permute-start.2) | collective-permute-done | bytes 57376 | tf_op jit(solution)/shard_map/ppermute | solution.py:448
  16.6 0.1 shard_map.52
  16.7 2.7 %collective-permute-start.5 = (f32[3,16,128]{2,1,0:T(8,128)S(1)}, f32[3,16,128]{2,1,0:T(8,128)S(1)}, u32[]{:S(2)}, u32[]{:S(2)}) collective-permute-start(f32[3,16,128]{2,1,0:T(8,128)S(1)} %get-tuple-element.66.own), channel_id=1, source_target_pairs={{0,16},{4,20},{8,24},{12,28},{16,0},{20,4},{24,8},{28,12},{1,17},{... | collective-permute-start | bytes 73736 | tf_op jit(solution)/shard_map/ppermute | solution.py:448
  19.4 0.6 %shard_map.53 = (f32[4,128,256]{2,1,0:T(8,128)S(1)}, f32[4,128,256]{2,1,0:T(8,128)S(1)}) custom-call(f32[3,16,128]{2,1,0:T(8,128)S(1)} %get-tuple-element.67.refs_0_, f32[3,16,128]{2,1,0:T(8,128)S(1)} %get-tuple-element.68.refs_1_, f32[8,16,8,128]{3,2,1,0:T(8,128)S(1)} %get-tuple-element.56.refs_2_, f32[8,8,8,128]{3,2,1,0:T(8,128)S(1)} %get-tuple-element.69.refs_3_, ...), custom_call_target="tpu_custom_call" | custom-call | flops 1048576 | bytes 2097152 | tf_op jit(solution)/shard_map/pallas_call | solution.py:762
  19.9 1.7 %collective-permute-done.5.got = f32[3,16,128]{2,1,0:T(8,128)S(1)} collective-permute-done((f32[3,16,128]{2,1,0:T(8,128)S(1)}, f32[3,16,128]{2,1,0:T(8,128)S(1)}, u32[]{:S(2)}, u32[]{:S(2)}) %collective-permute-start.5) | collective-permute-done | bytes 24608 | tf_op jit(solution)/shard_map/ppermute | solution.py:448
  21.6 0.4 %shard_map.54 = (f32[16,8,8,128]{3,2,1,0:T(8,128)S(1)}, f32[7,8,128]{2,1,0:T(8,128)S(1)}, f32[3,2,128]{2,1,0:T(2,128)S(1)}, f32[7,2,128]{2,1,0:T(2,128)S(1)}) custom-call(f32[3,16,128]{2,1,0:T(8,128)S(1)} %get-tuple-element.66.own, f32[3,16,128]{2,1,0:T(8,128)S(1)} %collective-permute-done.5.got, f32[4,128,256]{2,1,0:T(8,128)S(1)} %get-tuple-element.74.base, ...), custom_call_target="tpu_custom_call" | custom-call | tf_op jit(solution)/shard_map/pallas_call | solution.py:823
  22.0 0.1 collective-permute-start.6
  22.1 1.2 %collective-permute-done.6.refs_1_ = f32[7,2,128]{2,1,0:T(2,128)S(1)} collective-permute-done((f32[7,2,128]{2,1,0:T(2,128)S(1)}, f32[7,2,128]{2,1,0:T(2,128)S(1)}, u32[]{:S(2)}, u32[]{:S(2)}) %collective-permute-start.6) | collective-permute-done | bytes 7200 | tf_op jit(solution)/shard_map/ppermute | solution.py:448
  23.3 1.6 %collective-permute-start.7 = (f32[3,2,128]{2,1,0:T(2,128)S(1)}, f32[3,2,128]{2,1,0:T(2,128)S(1)}, u32[]{:S(2)}, u32[]{:S(2)}) collective-permute-start(f32[3,2,128]{2,1,0:T(2,128)S(1)} %get-tuple-element.82.own), channel_id=1, source_target_pairs={{0,2},{1,3},{2,0},{3,1},{4,6},{5,7},{6,4},{7,5},{8,10},{9,11},{10,... | collective-permute-start | bytes 9224 | tf_op jit(solution)/shard_map/ppermute | solution.py:448
  24.9 0.8 %shard_map.56 = (f32[4,4,64,128]{3,2,1,0:T(8,128)S(1)}, f32[4,4,64,128]{3,2,1,0:T(8,128)S(1)}) custom-call(f32[3,2,128]{2,1,0:T(2,128)S(1)} %get-tuple-element.83.refs_0_, f32[16,8,8,128]{3,2,1,0:T(8,128)S(1)} %get-tuple-element.76.yw.refs_1_, f32[16,8,8,128]{3,2,1,0:T(8,128)S(1)} %get-tuple-element.84.refs_2_, ...), custom_call_target="tpu_custom_call" | custom-call | flops 1572864 | bytes 2621440 | tf_op jit(solution)/shard_map/pallas_call | solution.py:915
  25.7 1.3 %collective-permute-done.7.got = f32[3,2,128]{2,1,0:T(2,128)S(1)} collective-permute-done((f32[3,2,128]{2,1,0:T(2,128)S(1)}, f32[3,2,128]{2,1,0:T(2,128)S(1)}, u32[]{:S(2)}, u32[]{:S(2)}) %collective-permute-start.7) | collective-permute-done | bytes 3104 | tf_op jit(solution)/shard_map/ppermute | solution.py:448
  27.0 1.2 %shard_map.57 = f32[4,64,512]{2,1,0:T(8,128)} custom-call(f32[3,2,128]{2,1,0:T(2,128)S(1)} %get-tuple-element.82.own, f32[3,2,128]{2,1,0:T(2,128)S(1)} %collective-permute-done.7.got, f32[4,4,64,128]{3,2,1,0:T(8,128)S(1)} %get-tuple-element.89.base, f32[4,4,64,128]{3,2,1,0:T(8,128)S(1)} %get-tuple-element.90.response, ...), custom_call_target="tpu_custom_call" | custom-call | tf_op jit(solution)/shard_map/pallas_call | solution.py:961
  (1 shorter events, 0.0 us)
Async XLA Ops:
  1.3 1.8 %collective-permute-start = (f32[64,128]{1,0:T(8,128)S(1)}, f32[64,128]{1,0:T(8,128)S(1)}, u32[]{:S(2)}, u32[]{:S(2)}) collective-permute-start(f32[64,128]{1,0:T(8,128)S(1)} %shard_map.46.refs_4_.own_cells), channel_id=1, source_target_pairs={{0,1},{1,0},{2,3},{3,2},{4,5},{5,4},{6,7},{7,6},{8,9},{9,8},{10,11... | collective-permute-start | bytes 98312 | tf_op jit(solution)/shard_map/ppermute | solution.py:448
  3.1 4.7 %collective-permute-start.1 = (f32[64,128]{1,0:T(8,128)S(1)}, f32[64,128]{1,0:T(8,128)S(1)}, u32[]{:S(2)}, u32[]{:S(2)}) collective-permute-start(f32[64,128]{1,0:T(8,128)S(1)} %collective-permute-done.after.refs_0_), channel_id=1, source_target_pairs={{0,2},{1,3},{2,0},{3,1},{4,6},{5,7},{6,4},{7,5},{8,10},{9,11},{10,... | collective-permute-start | bytes 98312 | tf_op jit(solution)/shard_map/ppermute | solution.py:448
  8.2 4.4 %collective-permute-start.4 = (f32[7,16,128]{2,1,0:T(8,128)S(1)}, f32[7,16,128]{2,1,0:T(8,128)S(1)}, u32[]{:S(2)}, u32[]{:S(2)}) collective-permute-start(f32[7,16,128]{2,1,0:T(8,128)S(1)} %get-tuple-element.62.after.refs_0_), channel_id=1, source_target_pairs={{0,4},{4,0},{8,12},{12,8},{16,20},{20,16},{24,28},{28,24},{1,5},{5... | collective-permute-start | bytes 172040 | tf_op jit(solution)/shard_map/ppermute | solution.py:448
  10.0 4.8 %collective-permute-start.3 = (f32[7,16,128]{2,1,0:T(8,128)S(1)}, f32[7,16,128]{2,1,0:T(8,128)S(1)}, u32[]{:S(2)}, u32[]{:S(2)}) collective-permute-start(f32[7,16,128]{2,1,0:T(8,128)S(1)} %get-tuple-element.62.after.refs_0_), channel_id=1, source_target_pairs={{0,8},{4,12},{8,0},{12,4},{16,24},{20,28},{24,16},{28,20},{1,9},{5... | collective-permute-start | bytes 172040 | tf_op jit(solution)/shard_map/ppermute | solution.py:448
  11.6 5.1 %collective-permute-start.2 = (f32[7,16,128]{2,1,0:T(8,128)S(1)}, f32[7,16,128]{2,1,0:T(8,128)S(1)}, u32[]{:S(2)}, u32[]{:S(2)}) collective-permute-start(f32[7,16,128]{2,1,0:T(8,128)S(1)} %get-tuple-element.62.after.refs_0_), channel_id=1, source_target_pairs={{0,12},{4,8},{8,4},{12,0},{16,28},{20,24},{24,20},{28,16},{1,13},{... | collective-permute-start | bytes 172040 | tf_op jit(solution)/shard_map/ppermute | solution.py:448
  16.7 4.9 %collective-permute-start.5 = (f32[3,16,128]{2,1,0:T(8,128)S(1)}, f32[3,16,128]{2,1,0:T(8,128)S(1)}, u32[]{:S(2)}, u32[]{:S(2)}) collective-permute-start(f32[3,16,128]{2,1,0:T(8,128)S(1)} %get-tuple-element.66.own), channel_id=1, source_target_pairs={{0,16},{4,20},{8,24},{12,28},{16,0},{20,4},{24,8},{28,12},{1,17},{... | collective-permute-start | bytes 73736 | tf_op jit(solution)/shard_map/ppermute | solution.py:448
  22.0 1.2 %collective-permute-start.6 = (f32[7,2,128]{2,1,0:T(2,128)S(1)}, f32[7,2,128]{2,1,0:T(2,128)S(1)}, u32[]{:S(2)}, u32[]{:S(2)}) collective-permute-start(f32[7,2,128]{2,1,0:T(2,128)S(1)} %get-tuple-element.81.refs_0_), channel_id=1, source_target_pairs={{0,1},{1,0},{2,3},{3,2},{4,5},{5,4},{6,7},{7,6},{8,9},{9,8},{10,11... | collective-permute-start | bytes 21512 | tf_op jit(solution)/shard_map/ppermute | solution.py:448
  23.3 3.7 %collective-permute-start.7 = (f32[3,2,128]{2,1,0:T(2,128)S(1)}, f32[3,2,128]{2,1,0:T(2,128)S(1)}, u32[]{:S(2)}, u32[]{:S(2)}) collective-permute-start(f32[3,2,128]{2,1,0:T(2,128)S(1)} %get-tuple-element.82.own), channel_id=1, source_target_pairs={{0,2},{1,3},{2,0},{3,1},{4,6},{5,7},{6,4},{7,5},{8,10},{9,11},{10,... | collective-permute-start | bytes 9224 | tf_op jit(solution)/shard_map/ppermute | solution.py:448

commit v10 on v9

--- a/solution.py
+++ b/solution.py
@@ -130,6 +130,22 @@
 
 def is_odd(axis):
     return lax.axis_index(axis) % 2 == 1
+
+
+def fold(cells, used):
+    total = cells[:SUBLANES]
+    lane = lax.broadcasted_iota(jnp.int32, total.shape, 1)
+    for n in range(1, cells.shape[0] // SUBLANES):
+        part = pltpu.roll(cells[n * SUBLANES : (n + 1) * SUBLANES], n * used, 1)
+        total = jnp.where(lane // used == n, part, total)
+    return total
+
+
+def unfold(cells, used, rows):
+    parts = [cells] + [
+        pltpu.roll(cells, LANES - n * used, 1) for n in range(1, rows // SUBLANES)
+    ]
+    return jnp.concatenate(parts, 0)
 
 
 def edges_kernel(t_hbm, b_hbm, packed, t_s, b_s, sems):
@@ -155,15 +171,16 @@
             place = 2 * sheets * side + z
             total = jnp.where(lane == place, t[:, source : source + 1], total)
             total = jnp.where(lane == place + sheets, c[:, source : source + 1], total)
-    packed[...] = total
+    packed[...] = fold(total, 4 * sheets)
 
 
 def edges(temperature, base):
     sheets, rows, _ = temperature.shape
+    assert rows // SUBLANES * 4 * sheets <= LANES
     return pl.pallas_call(
         edges_kernel,
         in_specs=[IN_HBM] * 2,
-        out_shape=pltpu.VMEM((rows, LANES), F32),
+        out_shape=pltpu.VMEM((SUBLANES, LANES), F32),
         scratch_shapes=[
             pltpu.VMEM((2, sheets, rows, LANES), F32),
             pltpu.VMEM((2, sheets, rows, LANES), F32),
@@ -375,13 +392,13 @@
     chunks, sheets, rows, _ = total_ref.shape
     lines = chunks * sheets
 
-    near, far = refs[0][...], far_side(refs[:count])
+    lane = lax.broadcasted_iota(jnp.int32, (rows, LANES), 1)
+    side = 2 * sheets
+    near, far = (unfold(v, 2 * side, rows) for v in (refs[0][...], far_side(refs[:count])))
     before = jnp.where(is_odd("gy"), near, far)
     after = jnp.where(is_odd("gy"), far, near)
-    lane = lax.broadcasted_iota(jnp.int32, (rows, LANES), 1)
-    side = 2 * sheets
     beyond = jnp.where(lane < side, pltpu.roll(before, LANES - side, 1), pltpu.roll(after, side, 1))
-    mine = own_cells[...]
+    mine = unfold(own_cells[...], 2 * side, rows)
     face = jnp.where(beyond > 0.0, mine + beyond, 0.0)
     flux = pltpu.roll(face, LANES - sheets, 1) * (beyond - mine)
     for n, (y, edge) in enumerate(((0, 0), (chunks - 1, LANES - 1))):
@@ -474,7 +491,7 @@
 
 def join_kernel(axis, stage, width, last, *refs):
     count = 1 << width
-    blocks = [[refs[-i % count][q] for q in range(7)] for i in range(count)]
+    blocks = [[refs[i][q] for q in range(7)] for i in range(count)]
     send = refs[-1 - width]
     links = refs[-width:]
     for bit in range(width):
@@ -519,7 +536,7 @@
     links, stage = [], 0
     while stage < stages - 1:
         width = min(widest, stages - 1 - stage)
-        got = [swap(view, axis, flip << stage) for flip in range((1 << width) - 1, 0, -1)]
+        got = [swap(view, axis, flip << stage) for flip in range(1, 1 << width)]
         last = stage + width == stages - 1
         view, *ties = join_stage(view, got, axis, stage, width, last, meanwhile)
         links += ties
@@ -957,7 +974,7 @@
 
 def finish(own, got, base, response, zw, zi, to_x):
     chunks, sheets, rows, _ = base.shape
-    copies = 2
+    copies = chunks
     return pl.pallas_call(
         functools.partial(finish_kernel, stages_of("gy")),
         out_shape=shape_of(sheets, rows, chunks * LANES),

time: 28.3 us -> 27 us (0.954)
  waiting for transfers between devices: 8.23 us -> 6.9 us
    ppermute x8, waiting for transfers between devices: 8.23 us -> 6.9 us  [swap(): return lax.ppermute(value, axis, [(i, i ^ flip) for i in range(count)])]
  transfers between devices with their start and end apart: 8 -> 8, of which waited for: 5 -> 6; matrix products, arithmetic and copies ran while one was open for 0% -> 0% of each run, Pallas kernels for 20% -> 21%
where the time goes in v10:
time: 27 us; the launch traced here: 26.9 us
  starting transfers between devices  10.9 us (40%)
  Pallas kernels  9 us (33%)
  waiting for transfers between devices  6.9 us (26%)
    ppermute x8, starting transfers between devices, swap(): return lax.ppermute(value, axis, [(i, i ^ flip) for i in range(count)])  10.9 us
    ppermute x8, waiting for transfers between devices, swap(): return lax.ppermute(value, axis, [(i, i ^ flip) for i in range(count)])  6.9 us
    pallas_call x1, Pallas kernels, x_factor(): pl.pallas_call(functools.partial(x_factor_kernel, plate), in_specs=[IN_VM...  2.14 us
    pallas_call x1, Pallas kernels, edges(): pl.pallas_call(edges_kernel, in_specs=[IN_HBM] * 2, out_shape=pltpu.VMEM(...  1.34 us
    pallas_call x1, Pallas kernels, load(): pl.pallas_call(load_kernel, in_specs=[IN_HBM] * len(values) + [ANYWHERE],...  1.24 us
    pallas_call x1, Pallas kernels, finish(): pl.pallas_call(functools.partial(finish_kernel, stages_of('gy')), out_sha...  1.16 us
    pallas_call x1, Pallas kernels, finish_prepare(): pl.pallas_call(functools.partial(finish_prepare_kernel, len(ties) + 1), o...  0.82 us
    pallas_call x1, Pallas kernels, y_factor(): pl.pallas_call(y_factor_kernel, in_specs=[IN_VMEM, ANYWHERE], out_shape=[...  0.63 us
  transfers between devices with their start and end apart: 8, of which 6 were waited for; matrix products, arithmetic and copies ran while one was open for 0% of the time, Pallas kernels for 21%

profile of v10, /device:TPU:0, one launch (start us, length us, event | category | flops | bytes accessed | tf_op | source)
XLA Modules:
  0.0 26.9 jit_solution(13780421594493807385)
XLA Ops:
  0.0 1.3 %shard_map.46.refs_4_.own_cells = f32[8,128]{1,0:T(8,128)S(1)} custom-call(f32[4,64,512]{2,1,0:T(8,128)} %refs_0_.1, f32[4,64,512]{2,1,0:T(8,128)} %refs_1_.1), custom_call_target="tpu_custom_call" | custom-call | tf_op jit(solution)/shard_map/pallas_call | solution.py:180
  1.4 0.5 %collective-permute-start = (f32[8,128]{1,0:T(8,128)S(1)}, f32[8,128]{1,0:T(8,128)S(1)}, u32[]{:S(2)}, u32[]{:S(2)}) collective-permute-start(f32[8,128]{1,0:T(8,128)S(1)} %shard_map.46.refs_4_.own_cells), channel_id=1, source_target_pairs={{0,1},{1,0},{2,3},{3,2},{4,5},{5,4},{6,7},{7,6},{8,9},{9,8},{10,11... | collective-permute-start | bytes 12296 | tf_op jit(solution)/shard_map/ppermute | solution.py:465
  1.9 1.2 %shard_map.47 = (f32[4,64,512]{2,1,0:T(8,128)S(1)}, f32[4,64,512]{2,1,0:T(8,128)S(1)}, s32[1,64]{1,0:T(1,128)S(1)}, f32[1,64]{1,0:T(1,128)S(1)}) custom-call(f32[4,64,512]{2,1,0:T(8,128)} %refs_0_.1, f32[4,64,512]{2,1,0:T(8,128)} %refs_1_.1, s32[1,64]{1,0:T(1,128)} %bitcast.2, f32[1,64]{1,0:T(1,128)} %bitcast.3, f32[8,128]{1,0:T(8,128)S(1)} %shard_map.46.refs_4_.own_cells), custom_call_target="tpu_custom_call" | custom-call | bytes 2097152 | tf_op jit(solution)/shard_map/pallas_call | solution.py:206
  3.1 0.0 collective-permute-done.after.refs_0_
  3.1 2.6 %collective-permute-start.1 = (f32[8,128]{1,0:T(8,128)S(1)}, f32[8,128]{1,0:T(8,128)S(1)}, u32[]{:S(2)}, u32[]{:S(2)}) collective-permute-start(f32[8,128]{1,0:T(8,128)S(1)} %collective-permute-done.after.refs_0_), channel_id=1, source_target_pairs={{0,2},{1,3},{2,0},{3,1},{4,6},{5,7},{6,4},{7,5},{8,10},{9,11},{10,... | collective-permute-start | bytes 12296 | tf_op jit(solution)/shard_map/ppermute | solution.py:465
  5.7 2.1 %shard_map.48 = (f32[4,4,64,128]{3,2,1,0:T(8,128)S(1)}, f32[4,4,64,128]{3,2,1,0:T(8,128)S(1)}, f32[8,16,8,128]{3,2,1,0:T(8,128)S(1)}, f32[8,16,8,128]{3,2,1,0:T(...) custom-call(s32[1,64]{1,0:T(1,128)S(1)} %get-tuple-element.51.loc, ...), custom_call_target="tpu_custom_call" | custom-call | flops 5242880 | bytes 3670016 | tf_op jit(solution)/shard_map/pallas_call | solution.py:357
  7.9 0.0 collective-permute-done.1.refs_1_
  7.9 0.5 %shard_map.49 = (f32[8,8,8,128]{3,2,1,0:T(8,128)S(1)}, f32[7,16,128]{2,1,0:T(8,128)S(1)}, f32[7,16,128]{2,1,0:T(8,128)S(1)}) custom-call(f32[8,128]{1,0:T(8,128)S(1)} %shard_map.46.refs_4_.own_cells, f32[4,64,512]{2,1,0:T(8,128)S(1)} %get-tuple-element.50.t_ref.refs_10_, f32[4,4,64,128]{3,2,1,0:T(8,128)S(1)} %get-tuple-element.55.total_ref, ...), custom_call_target="tpu_custom_call" | custom-call | tf_op jit(solution)/shard_map/pallas_call | solution.py:444
  8.3 2.6 %collective-permute-start.4 = (f32[7,16,128]{2,1,0:T(8,128)S(1)}, f32[7,16,128]{2,1,0:T(8,128)S(1)}, u32[]{:S(2)}, u32[]{:S(2)}) collective-permute-start(f32[7,16,128]{2,1,0:T(8,128)S(1)} %get-tuple-element.62.after.refs_0_), channel_id=1, source_target_pairs={{0,12},{4,8},{8,4},{12,0},{16,28},{20,24},{24,20},{28,16},{1,13},{... | collective-permute-start | bytes 172040 | tf_op jit(solution)/shard_map/ppermute | solution.py:465
  10.9 0.4 %collective-permute-start.3 = (f32[7,16,128]{2,1,0:T(8,128)S(1)}, f32[7,16,128]{2,1,0:T(8,128)S(1)}, u32[]{:S(2)}, u32[]{:S(2)}) collective-permute-start(f32[7,16,128]{2,1,0:T(8,128)S(1)} %get-tuple-element.62.after.refs_0_), channel_id=1, source_target_pairs={{0,8},{4,12},{8,0},{12,4},{16,24},{20,28},{24,16},{28,20},{1,9},{5... | collective-permute-start | bytes 172040 | tf_op jit(solution)/shard_map/ppermute | solution.py:465
  11.4 0.5 %collective-permute-start.2 = (f32[7,16,128]{2,1,0:T(8,128)S(1)}, f32[7,16,128]{2,1,0:T(8,128)S(1)}, u32[]{:S(2)}, u32[]{:S(2)}) collective-permute-start(f32[7,16,128]{2,1,0:T(8,128)S(1)} %get-tuple-element.62.after.refs_0_), channel_id=1, source_target_pairs={{0,4},{4,0},{8,12},{12,8},{16,20},{20,16},{24,28},{28,24},{1,5},{5... | collective-permute-start | bytes 172040 | tf_op jit(solution)/shard_map/ppermute | solution.py:465
  11.9 0.6 %shard_map.50 = (f32[16,8,8,128]{3,2,1,0:T(8,128)S(1)}, f32[16,8,8,128]{3,2,1,0:T(8,128)S(1)}, f32[16,8,8,128]{3,2,1,0:T(8,128)S(1)}, f32[7,3,8,128]{3,2,1,0:T(8...) custom-call(f32[4,4,64,128]{3,2,1,0:T(8,128)S(1)} %get-tuple-element, ...), custom_call_target="tpu_custom_call" | custom-call | flops 2621440 | bytes 2097152 | tf_op jit(solution)/shard_map/pallas_call | solution.py:658
  12.5 0.2 shard_map.51
  12.7 0.9 %collective-permute-done.4.refs_3_ = f32[7,16,128]{2,1,0:T(8,128)S(1)} collective-permute-done((f32[7,16,128]{2,1,0:T(8,128)S(1)}, f32[7,16,128]{2,1,0:T(8,128)S(1)}, u32[]{:S(2)}, u32[]{:S(2)}) %collective-permute-start.4) | collective-permute-done | bytes 57376 | tf_op jit(solution)/shard_map/ppermute | solution.py:465
  13.6 1.5 %collective-permute-done.3.refs_2_ = f32[7,16,128]{2,1,0:T(8,128)S(1)} collective-permute-done((f32[7,16,128]{2,1,0:T(8,128)S(1)}, f32[7,16,128]{2,1,0:T(8,128)S(1)}, u32[]{:S(2)}, u32[]{:S(2)}) %collective-permute-start.3) | collective-permute-done | bytes 57376 | tf_op jit(solution)/shard_map/ppermute | solution.py:465
  15.1 0.4 %collective-permute-done.2.refs_1_ = f32[7,16,128]{2,1,0:T(8,128)S(1)} collective-permute-done((f32[7,16,128]{2,1,0:T(8,128)S(1)}, f32[7,16,128]{2,1,0:T(8,128)S(1)}, u32[]{:S(2)}, u32[]{:S(2)}) %collective-permute-start.2) | collective-permute-done | bytes 57376 | tf_op jit(solution)/shard_map/ppermute | solution.py:465
  15.5 0.1 shard_map.52
  15.6 2.7 %collective-permute-start.5 = (f32[3,16,128]{2,1,0:T(8,128)S(1)}, f32[3,16,128]{2,1,0:T(8,128)S(1)}, u32[]{:S(2)}, u32[]{:S(2)}) collective-permute-start(f32[3,16,128]{2,1,0:T(8,128)S(1)} %get-tuple-element.66.own), channel_id=1, source_target_pairs={{0,16},{4,20},{8,24},{12,28},{16,0},{20,4},{24,8},{28,12},{1,17},{... | collective-permute-start | bytes 73736 | tf_op jit(solution)/shard_map/ppermute | solution.py:465
  18.3 0.6 %shard_map.53 = (f32[4,128,256]{2,1,0:T(8,128)S(1)}, f32[4,128,256]{2,1,0:T(8,128)S(1)}) custom-call(f32[3,16,128]{2,1,0:T(8,128)S(1)} %get-tuple-element.67.refs_0_, f32[3,16,128]{2,1,0:T(8,128)S(1)} %get-tuple-element.68.refs_1_, f32[8,16,8,128]{3,2,1,0:T(8,128)S(1)} %get-tuple-element.56.refs_2_, f32[8,8,8,128]{3,2,1,0:T(8,128)S(1)} %get-tuple-element.69.refs_3_, ...), custom_call_target="tpu_custom_call" | custom-call | flops 1048576 | bytes 2097152 | tf_op jit(solution)/shard_map/pallas_call | solution.py:779
  18.8 1.6 %collective-permute-done.5.got = f32[3,16,128]{2,1,0:T(8,128)S(1)} collective-permute-done((f32[3,16,128]{2,1,0:T(8,128)S(1)}, f32[3,16,128]{2,1,0:T(8,128)S(1)}, u32[]{:S(2)}, u32[]{:S(2)}) %collective-permute-start.5) | collective-permute-done | bytes 24608 | tf_op jit(solution)/shard_map/ppermute | solution.py:465
  20.4 0.4 %shard_map.54 = (f32[16,8,8,128]{3,2,1,0:T(8,128)S(1)}, f32[7,8,128]{2,1,0:T(8,128)S(1)}, f32[3,2,128]{2,1,0:T(2,128)S(1)}, f32[7,2,128]{2,1,0:T(2,128)S(1)}) custom-call(f32[3,16,128]{2,1,0:T(8,128)S(1)} %get-tuple-element.66.own, f32[3,16,128]{2,1,0:T(8,128)S(1)} %collective-permute-done.5.got, f32[4,128,256]{2,1,0:T(8,128)S(1)} %get-tuple-element.74.base, ...), custom_call_target="tpu_custom_call" | custom-call | tf_op jit(solution)/shard_map/pallas_call | solution.py:840
  20.8 0.1 collective-permute-start.6
  20.9 1.2 %collective-permute-done.6.refs_1_ = f32[7,2,128]{2,1,0:T(2,128)S(1)} collective-permute-done((f32[7,2,128]{2,1,0:T(2,128)S(1)}, f32[7,2,128]{2,1,0:T(2,128)S(1)}, u32[]{:S(2)}, u32[]{:S(2)}) %collective-permute-start.6) | collective-permute-done | bytes 7200 | tf_op jit(solution)/shard_map/ppermute | solution.py:465
  22.1 1.5 %collective-permute-start.7 = (f32[3,2,128]{2,1,0:T(2,128)S(1)}, f32[3,2,128]{2,1,0:T(2,128)S(1)}, u32[]{:S(2)}, u32[]{:S(2)}) collective-permute-start(f32[3,2,128]{2,1,0:T(2,128)S(1)} %get-tuple-element.82.own), channel_id=1, source_target_pairs={{0,2},{1,3},{2,0},{3,1},{4,6},{5,7},{6,4},{7,5},{8,10},{9,11},{10,... | collective-permute-start | bytes 9224 | tf_op jit(solution)/shard_map/ppermute | solution.py:465
  23.6 0.8 %shard_map.56 = (f32[4,4,64,128]{3,2,1,0:T(8,128)S(1)}, f32[4,4,64,128]{3,2,1,0:T(8,128)S(1)}) custom-call(f32[3,2,128]{2,1,0:T(2,128)S(1)} %get-tuple-element.83.refs_0_, f32[16,8,8,128]{3,2,1,0:T(8,128)S(1)} %get-tuple-element.76.yw.refs_1_, f32[16,8,8,128]{3,2,1,0:T(8,128)S(1)} %get-tuple-element.84.refs_2_, ...), custom_call_target="tpu_custom_call" | custom-call | flops 1572864 | bytes 2621440 | tf_op jit(solution)/shard_map/pallas_call | solution.py:932
  24.4 1.3 %collective-permute-done.7.got = f32[3,2,128]{2,1,0:T(2,128)S(1)} collective-permute-done((f32[3,2,128]{2,1,0:T(2,128)S(1)}, f32[3,2,128]{2,1,0:T(2,128)S(1)}, u32[]{:S(2)}, u32[]{:S(2)}) %collective-permute-start.7) | collective-permute-done | bytes 3104 | tf_op jit(solution)/shard_map/ppermute | solution.py:465
  25.7 1.2 %shard_map.57 = f32[4,64,512]{2,1,0:T(8,128)} custom-call(f32[3,2,128]{2,1,0:T(2,128)S(1)} %get-tuple-element.82.own, f32[3,2,128]{2,1,0:T(2,128)S(1)} %collective-permute-done.7.got, f32[4,4,64,128]{3,2,1,0:T(8,128)S(1)} %get-tuple-element.89.base, f32[4,4,64,128]{3,2,1,0:T(8,128)S(1)} %get-tuple-element.90.response, ...), custom_call_target="tpu_custom_call" | custom-call | tf_op jit(solution)/shard_map/pallas_call | solution.py:978
  (1 shorter events, 0.0 us)
Async XLA Ops:
  1.4 1.8 %collective-permute-start = (f32[8,128]{1,0:T(8,128)S(1)}, f32[8,128]{1,0:T(8,128)S(1)}, u32[]{:S(2)}, u32[]{:S(2)}) collective-permute-start(f32[8,128]{1,0:T(8,128)S(1)} %shard_map.46.refs_4_.own_cells), channel_id=1, source_target_pairs={{0,1},{1,0},{2,3},{3,2},{4,5},{5,4},{6,7},{7,6},{8,9},{9,8},{10,11... | collective-permute-start | bytes 12296 | tf_op jit(solution)/shard_map/ppermute | solution.py:465
  3.1 4.7 %collective-permute-start.1 = (f32[8,128]{1,0:T(8,128)S(1)}, f32[8,128]{1,0:T(8,128)S(1)}, u32[]{:S(2)}, u32[]{:S(2)}) collective-permute-start(f32[8,128]{1,0:T(8,128)S(1)} %collective-permute-done.after.refs_0_), channel_id=1, source_target_pairs={{0,2},{1,3},{2,0},{3,1},{4,6},{5,7},{6,4},{7,5},{8,10},{9,11},{10,... | collective-permute-start | bytes 12296 | tf_op jit(solution)/shard_map/ppermute | solution.py:465
  8.3 5.3 %collective-permute-start.4 = (f32[7,16,128]{2,1,0:T(8,128)S(1)}, f32[7,16,128]{2,1,0:T(8,128)S(1)}, u32[]{:S(2)}, u32[]{:S(2)}) collective-permute-start(f32[7,16,128]{2,1,0:T(8,128)S(1)} %get-tuple-element.62.after.refs_0_), channel_id=1, source_target_pairs={{0,12},{4,8},{8,4},{12,0},{16,28},{20,24},{24,20},{28,16},{1,13},{... | collective-permute-start | bytes 172040 | tf_op jit(solution)/shard_map/ppermute | solution.py:465
  10.9 4.2 %collective-permute-start.3 = (f32[7,16,128]{2,1,0:T(8,128)S(1)}, f32[7,16,128]{2,1,0:T(8,128)S(1)}, u32[]{:S(2)}, u32[]{:S(2)}) collective-permute-start(f32[7,16,128]{2,1,0:T(8,128)S(1)} %get-tuple-element.62.after.refs_0_), channel_id=1, source_target_pairs={{0,8},{4,12},{8,0},{12,4},{16,24},{20,28},{24,16},{28,20},{1,9},{5... | collective-permute-start | bytes 172040 | tf_op jit(solution)/shard_map/ppermute | solution.py:465
  11.4 4.2 %collective-permute-start.2 = (f32[7,16,128]{2,1,0:T(8,128)S(1)}, f32[7,16,128]{2,1,0:T(8,128)S(1)}, u32[]{:S(2)}, u32[]{:S(2)}) collective-permute-start(f32[7,16,128]{2,1,0:T(8,128)S(1)} %get-tuple-element.62.after.refs_0_), channel_id=1, source_target_pairs={{0,4},{4,0},{8,12},{12,8},{16,20},{20,16},{24,28},{28,24},{1,5},{5... | collective-permute-start | bytes 172040 | tf_op jit(solution)/shard_map/ppermute | solution.py:465
  15.6 4.8 %collective-permute-start.5 = (f32[3,16,128]{2,1,0:T(8,128)S(1)}, f32[3,16,128]{2,1,0:T(8,128)S(1)}, u32[]{:S(2)}, u32[]{:S(2)}) collective-permute-start(f32[3,16,128]{2,1,0:T(8,128)S(1)} %get-tuple-element.66.own), channel_id=1, source_target_pairs={{0,16},{4,20},{8,24},{12,28},{16,0},{20,4},{24,8},{28,12},{1,17},{... | collective-permute-start | bytes 73736 | tf_op jit(solution)/shard_map/ppermute | solution.py:465
  20.8 1.2 %collective-permute-start.6 = (f32[7,2,128]{2,1,0:T(2,128)S(1)}, f32[7,2,128]{2,1,0:T(2,128)S(1)}, u32[]{:S(2)}, u32[]{:S(2)}) collective-permute-start(f32[7,2,128]{2,1,0:T(2,128)S(1)} %get-tuple-element.81.refs_0_), channel_id=1, source_target_pairs={{0,1},{1,0},{2,3},{3,2},{4,5},{5,4},{6,7},{7,6},{8,9},{9,8},{10,11... | collective-permute-start | bytes 21512 | tf_op jit(solution)/shard_map/ppermute | solution.py:465
  22.1 3.7 %collective-permute-start.7 = (f32[3,2,128]{2,1,0:T(2,128)S(1)}, f32[3,2,128]{2,1,0:T(2,128)S(1)}, u32[]{:S(2)}, u32[]{:S(2)}) collective-permute-start(f32[3,2,128]{2,1,0:T(2,128)S(1)} %get-tuple-element.82.own), channel_id=1, source_target_pairs={{0,2},{1,3},{2,0},{3,1},{4,6},{5,7},{6,4},{7,5},{8,10},{9,11},{10,... | collective-permute-start | bytes 9224 | tf_op jit(solution)/shard_map/ppermute | solution.py:465

commit v11 on v10

--- a/solution.py
+++ b/solution.py
@@ -432,9 +432,10 @@
             own[offset + n] = flux
             joined.append(both)
         items = joined
-    for n, q in enumerate(COEFS):
-        send[q] = view[n]
-    send[FIRST], send[LAST] = items[0]
+    for d in range(send.shape[0]):
+        for n, q in enumerate(COEFS):
+            send[d, q] = view[n]
+        send[d, FIRST], send[d, LAST] = items[0]
 
 
 def x_target(own_cells, t, total, edge_cells, w, inv, p, links, view, ends):
@@ -446,7 +447,7 @@
         out_shape=[
             shape_of(steps, 2 * sheets, SUBLANES, LANES),
             shape_of(SUBLANES - 1, lines, LANES),
-            shape_of(7, lines, LANES),
+            shape_of(4, 7, lines, LANES),
         ],
         scratch_shapes=[
             pltpu.VMEM((2, sheets, rows, LANES), F32),
@@ -491,15 +492,12 @@
 
 def join_kernel(axis, stage, width, last, *refs):
     count = 1 << width
-    blocks = [[refs[i][q] for q in range(7)] for i in range(count)]
     send = refs[-1 - width]
     links = refs[-width:]
-    for bit in range(width):
-        right = on_right(axis, stage + bit)
-        for i in range(count):
-            if not i >> bit & 1:
-                j = i | 1 << bit
-                blocks[i], blocks[j] = ordered(right, blocks[i], blocks[j])
+    if width > 1:
+        blocks = [[refs[0][i, q] for q in range(7)] for i in range(count)]
+    else:
+        blocks = list(ordered(on_right(axis, stage), *([ref[q] for q in range(7)] for ref in refs[:2])))
     for bit in range(width):
         pairs = [join(blocks[i], blocks[i + 1]) for i in range(0, len(blocks), 2)]
         blocks = [p[0] for p in pairs]
@@ -521,27 +519,30 @@
             send[q] = whole[q]
 
 
-def join_stage(own, got, axis, stage, width, last, after):
-    lines = own.shape[1]
+def join_stage(got, axis, stage, width, last):
+    lines = got[0].shape[-2]
     return pl.pallas_call(
         functools.partial(join_kernel, axis, stage, width, last),
-        in_specs=[IN_VMEM] * (1 + len(got)) + [ANYWHERE] * len(after),
         out_shape=[shape_of(3 if last else 7, lines, LANES)] + [shape_of(3, lines, LANES)] * width,
         compiler_params=params(),
-    )(own, *got, *after)
-
-
-def gather_line(view, axis, widest=1, meanwhile=()):
+    )(*got)
+
+
+def gather_line(view, axis, first_width=1):
     stages = stages_of(axis)
     links, stage = [], 0
     while stage < stages - 1:
-        width = min(widest, stages - 1 - stage)
-        got = [swap(view, axis, flip << stage) for flip in range(1, 1 << width)]
+        width = 1 if stage else first_width
         last = stage + width == stages - 1
-        view, *ties = join_stage(view, got, axis, stage, width, last, meanwhile)
+        if width > 1:
+            size = 1 << width
+            groups = [list(range(i, i + size)) for i in range(0, 1 << stages, size)]
+            got = [lax.all_to_all(view, axis, 0, 0, axis_index_groups=groups, tiled=True)]
+        else:
+            got = [view, swap(view, axis, 1 << stage)]
+        view, *ties = join_stage(got, axis, stage, width, last)
         links += ties
         stage += width
-        meanwhile = ()
     return view, swap(view, axis, 1 << stage), links
 
 
@@ -1001,7 +1002,7 @@
     xh, x_own, view = x_target(packed, t, total, [near] + far, xw, xi, xp, x_links, x_view, ends)
     yw, yi, yp, inner, outer, y_view, to_y, to_x = y_factor(c, x_view)
     zw, zi = z_factor(c, view)
-    own, got, ties = gather_line(view, "gx", 2, (y_view, zw))
+    own, got, ties = gather_line(view, "gx", 2)
     base, response = y_prepare(
         ties, xw, xh, xm, xp, x_links, x_own, t_steps, to_y, columns // LANES
     )

time: 27 us -> 29.3 us (1.085)
  blocking collectives: 0 us -> 9.4 us
  starting transfers between devices: 10.9 us -> 7.17 us
  waiting for transfers between devices: 6.9 us -> 3.41 us
    all_to_all x0 -> x1, blocking collectives: none -> 9.4 us  [gather_line(): lax.all_to_all(view, axis, 0, 0, axis_index_groups=groups, tiled=True)]
    ppermute x8 -> x5, starting transfers between devices: 10.9 us -> 7.17 us  [swap(): return lax.ppermute(value, axis, [(i, i ^ flip) for i in range(count)])]
    ppermute x8 -> x5, waiting for transfers between devices: 6.9 us -> 3.41 us  [swap(): return lax.ppermute(value, axis, [(i, i ^ flip) for i in range(count)])]
  transfers between devices with their start and end apart: 8 -> 5, of which waited for: 6 -> 3; matrix products, arithmetic and copies ran while one was open for 0% -> 0% of each run, Pallas kernels for 21% -> 19%
where the time goes in v11:
time: 29.3 us; the launch traced here: 29.1 us
  blocking collectives  9.4 us (32%)
  Pallas kernels  9 us (31%)
  starting transfers between devices  7.17 us (24%)
  waiting for transfers between devices  3.41 us (12%)
    all_to_all x1, blocking collectives, gather_line(): lax.all_to_all(view, axis, 0, 0, axis_index_groups=groups, tiled=True)  9.4 us
    ppermute x5, starting transfers between devices, swap(): return lax.ppermute(value, axis, [(i, i ^ flip) for i in range(count)])  7.17 us
    ppermute x5, waiting for transfers between devices, swap(): return lax.ppermute(value, axis, [(i, i ^ flip) for i in range(count)])  3.41 us
    pallas_call x1, Pallas kernels, x_factor(): pl.pallas_call(functools.partial(x_factor_kernel, plate), in_specs=[IN_VM...  2.14 us
    pallas_call x1, Pallas kernels, edges(): pl.pallas_call(edges_kernel, in_specs=[IN_HBM] * 2, out_shape=pltpu.VMEM(...  1.34 us
    pallas_call x1, Pallas kernels, load(): pl.pallas_call(load_kernel, in_specs=[IN_HBM] * len(values) + [ANYWHERE],...  1.24 us
    pallas_call x1, Pallas kernels, finish(): pl.pallas_call(functools.partial(finish_kernel, stages_of('gy')), out_sha...  1.14 us
    pallas_call x1, Pallas kernels, finish_prepare(): pl.pallas_call(functools.partial(finish_prepare_kernel, len(ties) + 1), o...  0.84 us
  transfers between devices with their start and end apart: 5, of which 3 were waited for; matrix products, arithmetic and copies ran while one was open for 0% of the time, Pallas kernels for 19%

profile of v11, /device:TPU:0, one launch (start us, length us, event | category | flops | bytes accessed | tf_op | source)
XLA Modules:
  0.0 29.1 jit_solution(15995051390193139348)
XLA Ops:
  0.0 1.3 %shard_map.46.refs_4_.own_cells = f32[8,128]{1,0:T(8,128)S(1)} custom-call(f32[4,64,512]{2,1,0:T(8,128)} %refs_0_.1, f32[4,64,512]{2,1,0:T(8,128)} %refs_1_.1), custom_call_target="tpu_custom_call" | custom-call | tf_op jit(solution)/shard_map/pallas_call | solution.py:180
  1.4 0.5 %collective-permute-start = (f32[8,128]{1,0:T(8,128)S(1)}, f32[8,128]{1,0:T(8,128)S(1)}, u32[]{:S(2)}, u32[]{:S(2)}) collective-permute-start(f32[8,128]{1,0:T(8,128)S(1)} %shard_map.46.refs_4_.own_cells), channel_id=1, source_target_pairs={{0,1},{1,0},{2,3},{3,2},{4,5},{5,4},{6,7},{7,6},{8,9},{9,8},{10,11... | collective-permute-start | bytes 12296 | tf_op jit(solution)/shard_map/ppermute | solution.py:466
  1.9 1.2 %shard_map.47 = (f32[4,64,512]{2,1,0:T(8,128)S(1)}, f32[4,64,512]{2,1,0:T(8,128)S(1)}, s32[1,64]{1,0:T(1,128)S(1)}, f32[1,64]{1,0:T(1,128)S(1)}) custom-call(f32[4,64,512]{2,1,0:T(8,128)} %refs_0_.1, f32[4,64,512]{2,1,0:T(8,128)} %refs_1_.1, s32[1,64]{1,0:T(1,128)} %bitcast.2, f32[1,64]{1,0:T(1,128)} %bitcast.3, f32[8,128]{1,0:T(8,128)S(1)} %shard_map.46.refs_4_.own_cells), custom_call_target="tpu_custom_call" | custom-call | bytes 2097152 | tf_op jit(solution)/shard_map/pallas_call | solution.py:206
  3.1 0.0 collective-permute-done.after.refs_0_
  3.1 2.6 %collective-permute-start.1 = (f32[8,128]{1,0:T(8,128)S(1)}, f32[8,128]{1,0:T(8,128)S(1)}, u32[]{:S(2)}, u32[]{:S(2)}) collective-permute-start(f32[8,128]{1,0:T(8,128)S(1)} %collective-permute-done.after.refs_0_), channel_id=1, source_target_pairs={{0,2},{1,3},{2,0},{3,1},{4,6},{5,7},{6,4},{7,5},{8,10},{9,11},{10,... | collective-permute-start | bytes 12296 | tf_op jit(solution)/shard_map/ppermute | solution.py:466
  5.7 2.1 %shard_map.48 = (f32[4,4,64,128]{3,2,1,0:T(8,128)S(1)}, f32[4,4,64,128]{3,2,1,0:T(8,128)S(1)}, f32[8,16,8,128]{3,2,1,0:T(8,128)S(1)}, f32[8,16,8,128]{3,2,1,0:T(...) custom-call(s32[1,64]{1,0:T(1,128)S(1)} %get-tuple-element.51.loc, ...), custom_call_target="tpu_custom_call" | custom-call | flops 5242880 | bytes 3670016 | tf_op jit(solution)/shard_map/pallas_call | solution.py:357
  7.9 0.0 collective-permute-done.1.refs_1_
  7.9 0.5 %shard_map.49 = (f32[8,8,8,128]{3,2,1,0:T(8,128)S(1)}, f32[7,16,128]{2,1,0:T(8,128)S(1)}, f32[4,7,16,128]{3,2,1,0:T(8,128)S(1)}) custom-call(f32[8,128]{1,0:T(8,128)S(1)} %shard_map.46.refs_4_.own_cells, f32[4,64,512]{2,1,0:T(8,128)S(1)} %get-tuple-element.50.t_ref.refs_10_, f32[4,4,64,128]{3,2,1,0:T(8,128)S(1)} %get-tuple-element.55.total_ref, ...), custom_call_target="tpu_custom_call" | custom-call | tf_op jit(solution)/shard_map/pallas_call | solution.py:445
  8.3 9.4 %all_to_all.5.refs_0_ = f32[4,7,16,128]{3,2,1,0:T(8,128)S(1)} all-to-all(f32[4,7,16,128]{3,2,1,0:T(8,128)S(1)} %get-tuple-element.62.after), channel_id=1, replica_groups={{0,4,8,12},{16,20,24,28},{1,5,9,13},{17,21,25,29},{2,6,10,14},{18,22,26..., dimensions={0} | all-to-all | bytes 458752 | tf_op jit(solution)/shard_map/all_to_all | solution.py:540
  17.8 2.7 %collective-permute-start.2 = (f32[3,16,128]{2,1,0:T(8,128)S(1)}, f32[3,16,128]{2,1,0:T(8,128)S(1)}, u32[]{:S(2)}, u32[]{:S(2)}) collective-permute-start(f32[3,16,128]{2,1,0:T(8,128)S(1)} %get-tuple-element.63.own), channel_id=1, source_target_pairs={{0,16},{4,20},{8,24},{12,28},{16,0},{20,4},{24,8},{28,12},{1,17},{... | collective-permute-start | bytes 73736 | tf_op jit(solution)/shard_map/ppermute | solution.py:466
  20.4 0.6 %shard_map.51 = (f32[16,8,8,128]{3,2,1,0:T(8,128)S(1)}, f32[16,8,8,128]{3,2,1,0:T(8,128)S(1)}, f32[16,8,8,128]{3,2,1,0:T(8,128)S(1)}, f32[7,3,8,128]{3,2,1,0:T(8...) custom-call(f32[4,4,64,128]{3,2,1,0:T(8,128)S(1)} %get-tuple-element, ...), custom_call_target="tpu_custom_call" | custom-call | flops 2621440 | bytes 2097152 | tf_op jit(solution)/shard_map/pallas_call | solution.py:659
  21.1 0.6 %shard_map.52 = (f32[4,128,256]{2,1,0:T(8,128)S(1)}, f32[4,128,256]{2,1,0:T(8,128)S(1)}) custom-call(f32[3,16,128]{2,1,0:T(8,128)S(1)} %get-tuple-element.64.refs_0_, f32[3,16,128]{2,1,0:T(8,128)S(1)} %get-tuple-element.65.refs_1_, f32[8,16,8,128]{3,2,1,0:T(8,128)S(1)} %get-tuple-element.56.refs_2_, f32[8,8,8,128]{3,2,1,0:T(8,128)S(1)} %get-tuple-element.66.refs_3_, ...), custom_call_target="tpu_custom_call" | custom-call | flops 1048576 | bytes 2097152 | tf_op jit(solution)/shard_map/pallas_call | solution.py:780
  21.7 0.9 %collective-permute-done.2.got = f32[3,16,128]{2,1,0:T(8,128)S(1)} collective-permute-done((f32[3,16,128]{2,1,0:T(8,128)S(1)}, f32[3,16,128]{2,1,0:T(8,128)S(1)}, u32[]{:S(2)}, u32[]{:S(2)}) %collective-permute-start.2) | collective-permute-done | bytes 24608 | tf_op jit(solution)/shard_map/ppermute | solution.py:466
  22.6 0.4 %shard_map.53 = (f32[16,8,8,128]{3,2,1,0:T(8,128)S(1)}, f32[7,8,128]{2,1,0:T(8,128)S(1)}, f32[3,2,128]{2,1,0:T(2,128)S(1)}, f32[7,2,128]{2,1,0:T(2,128)S(1)}) custom-call(f32[3,16,128]{2,1,0:T(8,128)S(1)} %get-tuple-element.63.own, f32[3,16,128]{2,1,0:T(8,128)S(1)} %collective-permute-done.2.got, f32[4,128,256]{2,1,0:T(8,128)S(1)} %get-tuple-element.72.base, ...), custom_call_target="tpu_custom_call" | custom-call | tf_op jit(solution)/shard_map/pallas_call | solution.py:841
  23.0 0.1 collective-permute-start.3
  23.1 1.2 %collective-permute-done.3.refs_1_ = f32[7,2,128]{2,1,0:T(2,128)S(1)} collective-permute-done((f32[7,2,128]{2,1,0:T(2,128)S(1)}, f32[7,2,128]{2,1,0:T(2,128)S(1)}, u32[]{:S(2)}, u32[]{:S(2)}) %collective-permute-start.3) | collective-permute-done | bytes 7200 | tf_op jit(solution)/shard_map/ppermute | solution.py:466
  24.3 1.3 %collective-permute-start.4 = (f32[3,2,128]{2,1,0:T(2,128)S(1)}, f32[3,2,128]{2,1,0:T(2,128)S(1)}, u32[]{:S(2)}, u32[]{:S(2)}) collective-permute-start(f32[3,2,128]{2,1,0:T(2,128)S(1)} %get-tuple-element.81.own), channel_id=1, source_target_pairs={{0,2},{1,3},{2,0},{3,1},{4,6},{5,7},{6,4},{7,5},{8,10},{9,11},{10,... | collective-permute-start | bytes 9224 | tf_op jit(solution)/shard_map/ppermute | solution.py:466
  25.6 0.2 shard_map.55
  25.7 0.8 %shard_map.56 = (f32[4,4,64,128]{3,2,1,0:T(8,128)S(1)}, f32[4,4,64,128]{3,2,1,0:T(8,128)S(1)}) custom-call(f32[3,2,128]{2,1,0:T(2,128)S(1)} %get-tuple-element.82.refs_0_, f32[16,8,8,128]{3,2,1,0:T(8,128)S(1)} %get-tuple-element.74.yw.refs_1_, f32[16,8,8,128]{3,2,1,0:T(8,128)S(1)} %get-tuple-element.83.refs_2_, ...), custom_call_target="tpu_custom_call" | custom-call | flops 1572864 | bytes 2621440 | tf_op jit(solution)/shard_map/pallas_call | solution.py:933
  26.6 1.3 %collective-permute-done.4.got = f32[3,2,128]{2,1,0:T(2,128)S(1)} collective-permute-done((f32[3,2,128]{2,1,0:T(2,128)S(1)}, f32[3,2,128]{2,1,0:T(2,128)S(1)}, u32[]{:S(2)}, u32[]{:S(2)}) %collective-permute-start.4) | collective-permute-done | bytes 3104 | tf_op jit(solution)/shard_map/ppermute | solution.py:466
  27.9 1.1 %shard_map.57 = f32[4,64,512]{2,1,0:T(8,128)} custom-call(f32[3,2,128]{2,1,0:T(2,128)S(1)} %get-tuple-element.81.own, f32[3,2,128]{2,1,0:T(2,128)S(1)} %collective-permute-done.4.got, f32[4,4,64,128]{3,2,1,0:T(8,128)S(1)} %get-tuple-element.89.base, f32[4,4,64,128]{3,2,1,0:T(8,128)S(1)} %get-tuple-element.90.response, ...), custom_call_target="tpu_custom_call" | custom-call | tf_op jit(solution)/shard_map/pallas_call | solution.py:979
  (2 shorter events, 0.1 us)
Async XLA Ops:
  1.4 1.8 %collective-permute-start = (f32[8,128]{1,0:T(8,128)S(1)}, f32[8,128]{1,0:T(8,128)S(1)}, u32[]{:S(2)}, u32[]{:S(2)}) collective-permute-start(f32[8,128]{1,0:T(8,128)S(1)} %shard_map.46.refs_4_.own_cells), channel_id=1, source_target_pairs={{0,1},{1,0},{2,3},{3,2},{4,5},{5,4},{6,7},{7,6},{8,9},{9,8},{10,11... | collective-permute-start | bytes 12296 | tf_op jit(solution)/shard_map/ppermute | solution.py:466
  3.1 4.7 %collective-permute-start.1 = (f32[8,128]{1,0:T(8,128)S(1)}, f32[8,128]{1,0:T(8,128)S(1)}, u32[]{:S(2)}, u32[]{:S(2)}) collective-permute-start(f32[8,128]{1,0:T(8,128)S(1)} %collective-permute-done.after.refs_0_), channel_id=1, source_target_pairs={{0,2},{1,3},{2,0},{3,1},{4,6},{5,7},{6,4},{7,5},{8,10},{9,11},{10,... | collective-permute-start | bytes 12296 | tf_op jit(solution)/shard_map/ppermute | solution.py:466
  17.8 4.8 %collective-permute-start.2 = (f32[3,16,128]{2,1,0:T(8,128)S(1)}, f32[3,16,128]{2,1,0:T(8,128)S(1)}, u32[]{:S(2)}, u32[]{:S(2)}) collective-permute-start(f32[3,16,128]{2,1,0:T(8,128)S(1)} %get-tuple-element.63.own), channel_id=1, source_target_pairs={{0,16},{4,20},{8,24},{12,28},{16,0},{20,4},{24,8},{28,12},{1,17},{... | collective-permute-start | bytes 73736 | tf_op jit(solution)/shard_map/ppermute | solution.py:466
  23.0 1.2 %collective-permute-start.3 = (f32[7,2,128]{2,1,0:T(2,128)S(1)}, f32[7,2,128]{2,1,0:T(2,128)S(1)}, u32[]{:S(2)}, u32[]{:S(2)}) collective-permute-start(f32[7,2,128]{2,1,0:T(2,128)S(1)} %get-tuple-element.80.refs_0_), channel_id=1, source_target_pairs={{0,1},{1,0},{2,3},{3,2},{4,5},{5,4},{6,7},{7,6},{8,9},{9,8},{10,11... | collective-permute-start | bytes 21512 | tf_op jit(solution)/shard_map/ppermute | solution.py:466
  24.3 3.7 %collective-permute-start.4 = (f32[3,2,128]{2,1,0:T(2,128)S(1)}, f32[3,2,128]{2,1,0:T(2,128)S(1)}, u32[]{:S(2)}, u32[]{:S(2)}) collective-permute-start(f32[3,2,128]{2,1,0:T(2,128)S(1)} %get-tuple-element.81.own), channel_id=1, source_target_pairs={{0,2},{1,3},{2,0},{3,1},{4,6},{5,7},{6,4},{7,5},{8,10},{9,11},{10,... | collective-permute-start | bytes 9224 | tf_op jit(solution)/shard_map/ppermute | solution.py:466

commit v12 on v10

--- a/solution.py
+++ b/solution.py
@@ -148,13 +148,14 @@
     return jnp.concatenate(parts, 0)
 
 
-def edges_kernel(t_hbm, b_hbm, packed, t_s, b_s, sems):
-    sheets, rows, columns = t_hbm.shape
+def edges_kernel(sheets, t_hbm, b_hbm, packed, t_s, b_s, sems):
+    columns = t_hbm.shape[1]
+    rows = t_hbm.shape[0] // sheets
     sides = []
     for side, start in enumerate((0, columns - LANES)):
         sides.append(
             [
-                pltpu.make_async_copy(src.at[:, :, pl.ds(start, LANES)], dst.at[side], sems.at[i, side])
+                pltpu.make_async_copy(src.at[:, pl.ds(start, LANES)], dst.at[side], sems.at[i, side])
                 for i, (src, dst) in enumerate(((t_hbm, t_s), (b_hbm, b_s)))
             ]
         )
@@ -166,8 +167,8 @@
         for copy in sides[side]:
             copy.wait()
         for z in range(sheets):
-            t = t_s[side, z]
-            c = half_conduct(b_s[side, z], t)
+            t = t_s[side, z * rows : (z + 1) * rows, :]
+            c = half_conduct(b_s[side, z * rows : (z + 1) * rows, :], t)
             place = 2 * sheets * side + z
             total = jnp.where(lane == place, t[:, source : source + 1], total)
             total = jnp.where(lane == place + sheets, c[:, source : source + 1], total)
@@ -177,17 +178,22 @@
 def edges(temperature, base):
     sheets, rows, _ = temperature.shape
     assert rows // SUBLANES * 4 * sheets <= LANES
+    columns = temperature.shape[2]
+    fields = [
+        pltpu.with_memory_space_constraint(v.reshape(sheets * rows, columns), pltpu.HBM)
+        for v in (temperature, base)
+    ]
     return pl.pallas_call(
-        edges_kernel,
+        functools.partial(edges_kernel, sheets),
         in_specs=[IN_HBM] * 2,
         out_shape=pltpu.VMEM((SUBLANES, LANES), F32),
         scratch_shapes=[
-            pltpu.VMEM((2, sheets, rows, LANES), F32),
-            pltpu.VMEM((2, sheets, rows, LANES), F32),
+            pltpu.VMEM((2, sheets * rows, LANES), F32),
+            pltpu.VMEM((2, sheets * rows, LANES), F32),
             pltpu.SemaphoreType.DMA((2, 2)),
         ],
         compiler_params=params(),
-    )(*[pltpu.with_memory_space_constraint(v, pltpu.HBM) for v in (temperature, base)])
+    )(*fields)
 
 
 def load_kernel(*refs):
@@ -946,7 +952,7 @@
     chunks, sheets, rows, _ = base.shape
     each = LANES // rows
     pairs = sheets // each
-    copies, _, _, wide = o_s.shape
+    copies, _, wide = o_s.shape
 
     flux = top_flux("gy", stages, own, got)
     spread = [
@@ -962,10 +968,10 @@
                 return response[y, z] * spread[z // each][at : at + rows, :]
 
             def keep(z, value):
-                o_s[n, z, :, part] = base[y, z] + value
+                o_s[n, z * rows : (z + 1) * rows, part] = base[y, z] + value
 
             z_solve(zw, zi, field, y, keep)
-        copy = pltpu.make_async_copy(o_s.at[n], out.at[:, :, pl.ds(n * wide, wide)], sems.at[n])
+        copy = pltpu.make_async_copy(o_s.at[n], out.at[:, pl.ds(n * wide, wide)], sems.at[n])
         copy.start()
         started.append(copy)
     for copy in started:
@@ -977,14 +983,14 @@
     copies = chunks
     return pl.pallas_call(
         functools.partial(finish_kernel, stages_of("gy")),
-        out_shape=shape_of(sheets, rows, chunks * LANES),
+        out_shape=shape_of(sheets * rows, chunks * LANES),
         out_specs=ANYWHERE,
         scratch_shapes=[
-            pltpu.VMEM((copies, sheets, rows, chunks * LANES // copies), F32),
+            pltpu.VMEM((copies, sheets * rows, chunks * LANES // copies), F32),
             pltpu.SemaphoreType.DMA((copies,)),
         ],
         compiler_params=params(),
-    )(own, got, base, response, zw, zi, to_x)
+    )(own, got, base, response, zw, zi, to_x).reshape(sheets, rows, chunks * LANES)
 
 
 def per_device(temperature, base, locations, energy):

time: 27 us -> 27 us (level)
  no operation moved by 1% of the time
where the time goes in v12:
time: 27 us; the launch traced here: 26.9 us
  starting transfers between devices  10.9 us (40%)
  Pallas kernels  9 us (33%)
  waiting for transfers between devices  6.9 us (26%)
    ppermute x8, starting transfers between devices, swap(): return lax.ppermute(value, axis, [(i, i ^ flip) for i in range(count)])  10.9 us
    ppermute x8, waiting for transfers between devices, swap(): return lax.ppermute(value, axis, [(i, i ^ flip) for i in range(count)])  6.9 us
    pallas_call x1, Pallas kernels, x_factor(): pl.pallas_call(functools.partial(x_factor_kernel, plate), in_specs=[IN_VM...  2.14 us
    pallas_call x1, Pallas kernels, edges(): pl.pallas_call(functools.partial(edges_kernel, sheets), in_specs=[IN_HBM]...  1.34 us
    pallas_call x1, Pallas kernels, load(): pl.pallas_call(load_kernel, in_specs=[IN_HBM] * len(values) + [ANYWHERE],...  1.24 us
    pallas_call x1, Pallas kernels, finish(): pl.pallas_call(functools.partial(finish_kernel, stages_of('gy')), out_sha...  1.16 us
    pallas_call x1, Pallas kernels, finish_prepare(): pl.pallas_call(functools.partial(finish_prepare_kernel, len(ties) + 1), o...  0.82 us
    pallas_call x1, Pallas kernels, y_factor(): pl.pallas_call(y_factor_kernel, in_specs=[IN_VMEM, ANYWHERE], out_shape=[...  0.63 us
  transfers between devices with their start and end apart: 8, of which 6 were waited for; matrix products, arithmetic and copies ran while one was open for 0% of the time, Pallas kernels for 21%

profile of v12, /device:TPU:0, one launch (start us, length us, event | category | flops | bytes accessed | tf_op | source)
XLA Modules:
  0.0 26.9 jit_solution(13780421594493807385)
XLA Ops:
  0.0 1.3 %shard_map.46.refs_4_.own_cells = f32[8,128]{1,0:T(8,128)S(1)} custom-call(f32[256,512]{1,0:T(8,128)} %bitcast.5, f32[256,512]{1,0:T(8,128)} %bitcast.6), custom_call_target="tpu_custom_call" | custom-call | tf_op jit(solution)/shard_map/pallas_call | solution.py:186
  1.4 0.5 %collective-permute-start = (f32[8,128]{1,0:T(8,128)S(1)}, f32[8,128]{1,0:T(8,128)S(1)}, u32[]{:S(2)}, u32[]{:S(2)}) collective-permute-start(f32[8,128]{1,0:T(8,128)S(1)} %shard_map.46.refs_4_.own_cells), channel_id=1, source_target_pairs={{0,1},{1,0},{2,3},{3,2},{4,5},{5,4},{6,7},{7,6},{8,9},{9,8},{10,11... | collective-permute-start | bytes 12296 | tf_op jit(solution)/shard_map/ppermute | solution.py:471
  1.9 1.2 %shard_map.47 = (f32[4,64,512]{2,1,0:T(8,128)S(1)}, f32[4,64,512]{2,1,0:T(8,128)S(1)}, s32[1,64]{1,0:T(1,128)S(1)}, f32[1,64]{1,0:T(1,128)S(1)}) custom-call(f32[4,64,512]{2,1,0:T(8,128)} %refs_0_.1, f32[4,64,512]{2,1,0:T(8,128)} %refs_1_.1, s32[1,64]{1,0:T(1,128)} %bitcast.7, f32[1,64]{1,0:T(1,128)} %bitcast.8, f32[8,128]{1,0:T(8,128)S(1)} %shard_map.46.refs_4_.own_cells), custom_call_target="tpu_custom_call" | custom-call | bytes 2097152 | tf_op jit(solution)/shard_map/pallas_call | solution.py:212
  3.1 0.0 collective-permute-done.after.refs_0_
  3.1 2.6 %collective-permute-start.1 = (f32[8,128]{1,0:T(8,128)S(1)}, f32[8,128]{1,0:T(8,128)S(1)}, u32[]{:S(2)}, u32[]{:S(2)}) collective-permute-start(f32[8,128]{1,0:T(8,128)S(1)} %collective-permute-done.after.refs_0_), channel_id=1, source_target_pairs={{0,2},{1,3},{2,0},{3,1},{4,6},{5,7},{6,4},{7,5},{8,10},{9,11},{10,... | collective-permute-start | bytes 12296 | tf_op jit(solution)/shard_map/ppermute | solution.py:471
  5.7 2.1 %shard_map.48 = (f32[4,4,64,128]{3,2,1,0:T(8,128)S(1)}, f32[4,4,64,128]{3,2,1,0:T(8,128)S(1)}, f32[8,16,8,128]{3,2,1,0:T(8,128)S(1)}, f32[8,16,8,128]{3,2,1,0:T(...) custom-call(s32[1,64]{1,0:T(1,128)S(1)} %get-tuple-element.51.loc, ...), custom_call_target="tpu_custom_call" | custom-call | flops 5242880 | bytes 3670016 | tf_op jit(solution)/shard_map/pallas_call | solution.py:363
  7.9 0.0 collective-permute-done.1.refs_1_
  7.9 0.5 %shard_map.49 = (f32[8,8,8,128]{3,2,1,0:T(8,128)S(1)}, f32[7,16,128]{2,1,0:T(8,128)S(1)}, f32[7,16,128]{2,1,0:T(8,128)S(1)}) custom-call(f32[8,128]{1,0:T(8,128)S(1)} %shard_map.46.refs_4_.own_cells, f32[4,64,512]{2,1,0:T(8,128)S(1)} %get-tuple-element.50.t_ref.refs_10_, f32[4,4,64,128]{3,2,1,0:T(8,128)S(1)} %get-tuple-element.55.total_ref, ...), custom_call_target="tpu_custom_call" | custom-call | tf_op jit(solution)/shard_map/pallas_call | solution.py:450
  8.3 2.6 %collective-permute-start.4 = (f32[7,16,128]{2,1,0:T(8,128)S(1)}, f32[7,16,128]{2,1,0:T(8,128)S(1)}, u32[]{:S(2)}, u32[]{:S(2)}) collective-permute-start(f32[7,16,128]{2,1,0:T(8,128)S(1)} %get-tuple-element.62.after.refs_0_), channel_id=1, source_target_pairs={{0,12},{4,8},{8,4},{12,0},{16,28},{20,24},{24,20},{28,16},{1,13},{... | collective-permute-start | bytes 172040 | tf_op jit(solution)/shard_map/ppermute | solution.py:471
  10.9 0.4 %collective-permute-start.3 = (f32[7,16,128]{2,1,0:T(8,128)S(1)}, f32[7,16,128]{2,1,0:T(8,128)S(1)}, u32[]{:S(2)}, u32[]{:S(2)}) collective-permute-start(f32[7,16,128]{2,1,0:T(8,128)S(1)} %get-tuple-element.62.after.refs_0_), channel_id=1, source_target_pairs={{0,8},{4,12},{8,0},{12,4},{16,24},{20,28},{24,16},{28,20},{1,9},{5... | collective-permute-start | bytes 172040 | tf_op jit(solution)/shard_map/ppermute | solution.py:471
  11.4 0.5 %collective-permute-start.2 = (f32[7,16,128]{2,1,0:T(8,128)S(1)}, f32[7,16,128]{2,1,0:T(8,128)S(1)}, u32[]{:S(2)}, u32[]{:S(2)}) collective-permute-start(f32[7,16,128]{2,1,0:T(8,128)S(1)} %get-tuple-element.62.after.refs_0_), channel_id=1, source_target_pairs={{0,4},{4,0},{8,12},{12,8},{16,20},{20,16},{24,28},{28,24},{1,5},{5... | collective-permute-start | bytes 172040 | tf_op jit(solution)/shard_map/ppermute | solution.py:471
  11.9 0.6 %shard_map.50 = (f32[16,8,8,128]{3,2,1,0:T(8,128)S(1)}, f32[16,8,8,128]{3,2,1,0:T(8,128)S(1)}, f32[16,8,8,128]{3,2,1,0:T(8,128)S(1)}, f32[7,3,8,128]{3,2,1,0:T(8...) custom-call(f32[4,4,64,128]{3,2,1,0:T(8,128)S(1)} %get-tuple-element, ...), custom_call_target="tpu_custom_call" | custom-call | flops 2621440 | bytes 2097152 | tf_op jit(solution)/shard_map/pallas_call | solution.py:664
  12.5 0.2 shard_map.51
  12.7 0.9 %collective-permute-done.4.refs_3_ = f32[7,16,128]{2,1,0:T(8,128)S(1)} collective-permute-done((f32[7,16,128]{2,1,0:T(8,128)S(1)}, f32[7,16,128]{2,1,0:T(8,128)S(1)}, u32[]{:S(2)}, u32[]{:S(2)}) %collective-permute-start.4) | collective-permute-done | bytes 57376 | tf_op jit(solution)/shard_map/ppermute | solution.py:471
  13.6 1.5 %collective-permute-done.3.refs_2_ = f32[7,16,128]{2,1,0:T(8,128)S(1)} collective-permute-done((f32[7,16,128]{2,1,0:T(8,128)S(1)}, f32[7,16,128]{2,1,0:T(8,128)S(1)}, u32[]{:S(2)}, u32[]{:S(2)}) %collective-permute-start.3) | collective-permute-done | bytes 57376 | tf_op jit(solution)/shard_map/ppermute | solution.py:471
  15.1 0.4 %collective-permute-done.2.refs_1_ = f32[7,16,128]{2,1,0:T(8,128)S(1)} collective-permute-done((f32[7,16,128]{2,1,0:T(8,128)S(1)}, f32[7,16,128]{2,1,0:T(8,128)S(1)}, u32[]{:S(2)}, u32[]{:S(2)}) %collective-permute-start.2) | collective-permute-done | bytes 57376 | tf_op jit(solution)/shard_map/ppermute | solution.py:471
  15.5 0.1 shard_map.52
  15.6 2.7 %collective-permute-start.5 = (f32[3,16,128]{2,1,0:T(8,128)S(1)}, f32[3,16,128]{2,1,0:T(8,128)S(1)}, u32[]{:S(2)}, u32[]{:S(2)}) collective-permute-start(f32[3,16,128]{2,1,0:T(8,128)S(1)} %get-tuple-element.66.own), channel_id=1, source_target_pairs={{0,16},{4,20},{8,24},{12,28},{16,0},{20,4},{24,8},{28,12},{1,17},{... | collective-permute-start | bytes 73736 | tf_op jit(solution)/shard_map/ppermute | solution.py:471
  18.3 0.6 %shard_map.53 = (f32[4,128,256]{2,1,0:T(8,128)S(1)}, f32[4,128,256]{2,1,0:T(8,128)S(1)}) custom-call(f32[3,16,128]{2,1,0:T(8,128)S(1)} %get-tuple-element.67.refs_0_, f32[3,16,128]{2,1,0:T(8,128)S(1)} %get-tuple-element.68.refs_1_, f32[8,16,8,128]{3,2,1,0:T(8,128)S(1)} %get-tuple-element.56.refs_2_, f32[8,8,8,128]{3,2,1,0:T(8,128)S(1)} %get-tuple-element.69.refs_3_, ...), custom_call_target="tpu_custom_call" | custom-call | flops 1048576 | bytes 2097152 | tf_op jit(solution)/shard_map/pallas_call | solution.py:785
  18.8 1.6 %collective-permute-done.5.got = f32[3,16,128]{2,1,0:T(8,128)S(1)} collective-permute-done((f32[3,16,128]{2,1,0:T(8,128)S(1)}, f32[3,16,128]{2,1,0:T(8,128)S(1)}, u32[]{:S(2)}, u32[]{:S(2)}) %collective-permute-start.5) | collective-permute-done | bytes 24608 | tf_op jit(solution)/shard_map/ppermute | solution.py:471
  20.4 0.4 %shard_map.54 = (f32[16,8,8,128]{3,2,1,0:T(8,128)S(1)}, f32[7,8,128]{2,1,0:T(8,128)S(1)}, f32[3,2,128]{2,1,0:T(2,128)S(1)}, f32[7,2,128]{2,1,0:T(2,128)S(1)}) custom-call(f32[3,16,128]{2,1,0:T(8,128)S(1)} %get-tuple-element.66.own, f32[3,16,128]{2,1,0:T(8,128)S(1)} %collective-permute-done.5.got, f32[4,128,256]{2,1,0:T(8,128)S(1)} %get-tuple-element.74.base, ...), custom_call_target="tpu_custom_call" | custom-call | tf_op jit(solution)/shard_map/pallas_call | solution.py:846
  20.8 0.1 collective-permute-start.6
  20.9 1.2 %collective-permute-done.6.refs_1_ = f32[7,2,128]{2,1,0:T(2,128)S(1)} collective-permute-done((f32[7,2,128]{2,1,0:T(2,128)S(1)}, f32[7,2,128]{2,1,0:T(2,128)S(1)}, u32[]{:S(2)}, u32[]{:S(2)}) %collective-permute-start.6) | collective-permute-done | bytes 7200 | tf_op jit(solution)/shard_map/ppermute | solution.py:471
  22.1 1.5 %collective-permute-start.7 = (f32[3,2,128]{2,1,0:T(2,128)S(1)}, f32[3,2,128]{2,1,0:T(2,128)S(1)}, u32[]{:S(2)}, u32[]{:S(2)}) collective-permute-start(f32[3,2,128]{2,1,0:T(2,128)S(1)} %get-tuple-element.82.own), channel_id=1, source_target_pairs={{0,2},{1,3},{2,0},{3,1},{4,6},{5,7},{6,4},{7,5},{8,10},{9,11},{10,... | collective-permute-start | bytes 9224 | tf_op jit(solution)/shard_map/ppermute | solution.py:471
  23.6 0.8 %shard_map.56 = (f32[4,4,64,128]{3,2,1,0:T(8,128)S(1)}, f32[4,4,64,128]{3,2,1,0:T(8,128)S(1)}) custom-call(f32[3,2,128]{2,1,0:T(2,128)S(1)} %get-tuple-element.83.refs_0_, f32[16,8,8,128]{3,2,1,0:T(8,128)S(1)} %get-tuple-element.76.yw.refs_1_, f32[16,8,8,128]{3,2,1,0:T(8,128)S(1)} %get-tuple-element.84.refs_2_, ...), custom_call_target="tpu_custom_call" | custom-call | flops 1572864 | bytes 2621440 | tf_op jit(solution)/shard_map/pallas_call | solution.py:938
  24.4 1.3 %collective-permute-done.7.got = f32[3,2,128]{2,1,0:T(2,128)S(1)} collective-permute-done((f32[3,2,128]{2,1,0:T(2,128)S(1)}, f32[3,2,128]{2,1,0:T(2,128)S(1)}, u32[]{:S(2)}, u32[]{:S(2)}) %collective-permute-start.7) | collective-permute-done | bytes 3104 | tf_op jit(solution)/shard_map/ppermute | solution.py:471
  25.7 1.2 %shard_map.57 = f32[256,512]{1,0:T(8,128)} custom-call(f32[3,2,128]{2,1,0:T(2,128)S(1)} %get-tuple-element.82.own, f32[3,2,128]{2,1,0:T(2,128)S(1)} %collective-permute-done.7.got, f32[4,4,64,128]{3,2,1,0:T(8,128)S(1)} %get-tuple-element.89.base, f32[4,4,64,128]{3,2,1,0:T(8,128)S(1)} %get-tuple-element.90.response, ...), custom_call_target="tpu_custom_call" | custom-call | tf_op jit(solution)/shard_map/pallas_call | solution.py:984
  (1 shorter events, 0.0 us)
Async XLA Ops:
  1.4 1.8 %collective-permute-start = (f32[8,128]{1,0:T(8,128)S(1)}, f32[8,128]{1,0:T(8,128)S(1)}, u32[]{:S(2)}, u32[]{:S(2)}) collective-permute-start(f32[8,128]{1,0:T(8,128)S(1)} %shard_map.46.refs_4_.own_cells), channel_id=1, source_target_pairs={{0,1},{1,0},{2,3},{3,2},{4,5},{5,4},{6,7},{7,6},{8,9},{9,8},{10,11... | collective-permute-start | bytes 12296 | tf_op jit(solution)/shard_map/ppermute | solution.py:471
  3.1 4.7 %collective-permute-start.1 = (f32[8,128]{1,0:T(8,128)S(1)}, f32[8,128]{1,0:T(8,128)S(1)}, u32[]{:S(2)}, u32[]{:S(2)}) collective-permute-start(f32[8,128]{1,0:T(8,128)S(1)} %collective-permute-done.after.refs_0_), channel_id=1, source_target_pairs={{0,2},{1,3},{2,0},{3,1},{4,6},{5,7},{6,4},{7,5},{8,10},{9,11},{10,... | collective-permute-start | bytes 12296 | tf_op jit(solution)/shard_map/ppermute | solution.py:471
  8.3 5.3 %collective-permute-start.4 = (f32[7,16,128]{2,1,0:T(8,128)S(1)}, f32[7,16,128]{2,1,0:T(8,128)S(1)}, u32[]{:S(2)}, u32[]{:S(2)}) collective-permute-start(f32[7,16,128]{2,1,0:T(8,128)S(1)} %get-tuple-element.62.after.refs_0_), channel_id=1, source_target_pairs={{0,12},{4,8},{8,4},{12,0},{16,28},{20,24},{24,20},{28,16},{1,13},{... | collective-permute-start | bytes 172040 | tf_op jit(solution)/shard_map/ppermute | solution.py:471
  10.9 4.2 %collective-permute-start.3 = (f32[7,16,128]{2,1,0:T(8,128)S(1)}, f32[7,16,128]{2,1,0:T(8,128)S(1)}, u32[]{:S(2)}, u32[]{:S(2)}) collective-permute-start(f32[7,16,128]{2,1,0:T(8,128)S(1)} %get-tuple-element.62.after.refs_0_), channel_id=1, source_target_pairs={{0,8},{4,12},{8,0},{12,4},{16,24},{20,28},{24,16},{28,20},{1,9},{5... | collective-permute-start | bytes 172040 | tf_op jit(solution)/shard_map/ppermute | solution.py:471
  11.4 4.2 %collective-permute-start.2 = (f32[7,16,128]{2,1,0:T(8,128)S(1)}, f32[7,16,128]{2,1,0:T(8,128)S(1)}, u32[]{:S(2)}, u32[]{:S(2)}) collective-permute-start(f32[7,16,128]{2,1,0:T(8,128)S(1)} %get-tuple-element.62.after.refs_0_), channel_id=1, source_target_pairs={{0,4},{4,0},{8,12},{12,8},{16,20},{20,16},{24,28},{28,24},{1,5},{5... | collective-permute-start | bytes 172040 | tf_op jit(solution)/shard_map/ppermute | solution.py:471
  15.6 4.8 %collective-permute-start.5 = (f32[3,16,128]{2,1,0:T(8,128)S(1)}, f32[3,16,128]{2,1,0:T(8,128)S(1)}, u32[]{:S(2)}, u32[]{:S(2)}) collective-permute-start(f32[3,16,128]{2,1,0:T(8,128)S(1)} %get-tuple-element.66.own), channel_id=1, source_target_pairs={{0,16},{4,20},{8,24},{12,28},{16,0},{20,4},{24,8},{28,12},{1,17},{... | collective-permute-start | bytes 73736 | tf_op jit(solution)/shard_map/ppermute | solution.py:471
  20.8 1.2 %collective-permute-start.6 = (f32[7,2,128]{2,1,0:T(2,128)S(1)}, f32[7,2,128]{2,1,0:T(2,128)S(1)}, u32[]{:S(2)}, u32[]{:S(2)}) collective-permute-start(f32[7,2,128]{2,1,0:T(2,128)S(1)} %get-tuple-element.81.refs_0_), channel_id=1, source_target_pairs={{0,1},{1,0},{2,3},{3,2},{4,5},{5,4},{6,7},{7,6},{8,9},{9,8},{10,11... | collective-permute-start | bytes 21512 | tf_op jit(solution)/shard_map/ppermute | solution.py:471
  22.1 3.7 %collective-permute-start.7 = (f32[3,2,128]{2,1,0:T(2,128)S(1)}, f32[3,2,128]{2,1,0:T(2,128)S(1)}, u32[]{:S(2)}, u32[]{:S(2)}) collective-permute-start(f32[3,2,128]{2,1,0:T(2,128)S(1)} %get-tuple-element.82.own), channel_id=1, source_target_pairs={{0,2},{1,3},{2,0},{3,1},{4,6},{5,7},{6,4},{7,5},{8,10},{9,11},{10,... | collective-permute-start | bytes 9224 | tf_op jit(solution)/shard_map/ppermute | solution.py:471

commit v13 on v12

--- a/solution.py
+++ b/solution.py
@@ -537,7 +537,7 @@
     )(own, *got, *after)
 
 
-def gather_line(view, axis, widest=1, meanwhile=()):
+def gather_line(view, axis, widest=1, meanwhile=(), one_core=False):
     stages = stages_of(axis)
     links, stage = [], 0
     while stage < stages - 1:
@@ -548,6 +548,10 @@
         links += ties
         stage += width
         meanwhile = ()
+    if one_core and stage:
+        pairs = [(i, i ^ 1 << stage) for i in range(1, 1 << stages, 2)]
+        got = lax.ppermute(view, axis, pairs)
+        return view, (got, swap(got, axis, 1)), links
     return view, swap(view, axis, 1 << stage), links
 
 
@@ -948,12 +952,14 @@
     )(*ties, yw, yh, yp, inner, inner_own, outer, outer_own, zw, zi, t, to_x)
 
 
-def finish_kernel(stages, own, got, base, response, zw, zi, to_x, out, o_s, sems):
+def finish_kernel(stages, own, *refs):
+    *parts, base, response, zw, zi, to_x, out, o_s, sems = refs
     chunks, sheets, rows, _ = base.shape
     each = LANES // rows
     pairs = sheets // each
     copies, _, wide = o_s.shape
 
+    got = [jnp.where(is_odd("gy"), parts[0][q], parts[-1][q]) for q in range(3)]
     flux = top_flux("gy", stages, own, got)
     spread = [
         turned(to_x[...], jnp.broadcast_to(flux[m : m + 1, :], (LANES, LANES))) for m in range(pairs)
@@ -990,7 +996,7 @@
             pltpu.SemaphoreType.DMA((copies,)),
         ],
         compiler_params=params(),
-    )(own, got, base, response, zw, zi, to_x).reshape(sheets, rows, chunks * LANES)
+    )(own, *got, base, response, zw, zi, to_x).reshape(sheets, rows, chunks * LANES)
 
 
 def per_device(temperature, base, locations, energy):
@@ -1014,7 +1020,7 @@
     yh, inner_own, outer_own, view = y_target(
         own, got, base, response, yw, yi, yp, inner, outer, y_view, to_y
     )
-    own, got, ties = gather_line(view, "gy")
+    own, got, ties = gather_line(view, "gy", one_core=True)
     base, response = finish_prepare(
         ties, yw, yh, yp, inner, inner_own, outer, outer_own, zw, zi, t, to_x
     )

time: 27 us -> 28.8 us (1.067)
  starting transfers between devices: 10.9 us -> 13.9 us
  waiting for transfers between devices: 6.9 us -> 5.58 us
    ppermute x8, starting transfers between devices: 10.9 us -> 13.2 us  [swap(): return lax.ppermute(value, axis, [(i, i ^ flip) for i in range(count)])]
    ppermute x8, waiting for transfers between devices: 6.9 us -> 5.58 us  [swap(): return lax.ppermute(value, axis, [(i, i ^ flip) for i in range(count)])]
    ppermute x0 -> x1, starting transfers between devices: none -> 0.66 us  [gather_line(): got = lax.ppermute(view, axis, pairs)]
  transfers between devices with their start and end apart: 8 -> 9, of which waited for: 6 -> 5; matrix products, arithmetic and copies ran while one was open for 0% -> 0% of each run, Pallas kernels for 21% -> 19%
where the time goes in v13:
time: 28.8 us; the launch traced here: 28.6 us
  starting transfers between devices  13.9 us (48%)
  Pallas kernels  9.01 us (31%)
  waiting for transfers between devices  5.58 us (19%)
    ppermute x8, starting transfers between devices, swap(): return lax.ppermute(value, axis, [(i, i ^ flip) for i in range(count)])  13.2 us
    ppermute x8, waiting for transfers between devices, swap(): return lax.ppermute(value, axis, [(i, i ^ flip) for i in range(count)])  5.58 us
    pallas_call x1, Pallas kernels, x_factor(): pl.pallas_call(functools.partial(x_factor_kernel, plate), in_specs=[IN_VM...  2.14 us
    pallas_call x1, Pallas kernels, edges(): pl.pallas_call(functools.partial(edges_kernel, sheets), in_specs=[IN_HBM]...  1.34 us
    pallas_call x1, Pallas kernels, load(): pl.pallas_call(load_kernel, in_specs=[IN_HBM] * len(values) + [ANYWHERE],...  1.24 us
    pallas_call x1, Pallas kernels, finish(): pl.pallas_call(functools.partial(finish_kernel, stages_of('gy')), out_sha...  1.18 us
    pallas_call x1, Pallas kernels, finish_prepare(): pl.pallas_call(functools.partial(finish_prepare_kernel, len(ties) + 1), o...  0.82 us
    ppermute x1, starting transfers between devices, gather_line(): got = lax.ppermute(view, axis, pairs)  0.66 us
  transfers between devices with their start and end apart: 9, of which 5 were waited for; matrix products, arithmetic and copies ran while one was open for 0% of the time, Pallas kernels for 19%

profile of v13, /device:TPU:0, one launch (start us, length us, event | category | flops | bytes accessed | tf_op | source)
XLA Modules:
  0.0 28.6 jit_solution(12238748438525690045)
XLA Ops:
  0.0 1.3 %shard_map.46.refs_4_.own_cells = f32[8,128]{1,0:T(8,128)S(1)} custom-call(f32[256,512]{1,0:T(8,128)} %bitcast.5, f32[256,512]{1,0:T(8,128)} %bitcast.6), custom_call_target="tpu_custom_call" | custom-call | tf_op jit(solution)/shard_map/pallas_call | solution.py:186
  1.4 0.5 %collective-permute-start = (f32[8,128]{1,0:T(8,128)S(1)}, f32[8,128]{1,0:T(8,128)S(1)}, u32[]{:S(2)}, u32[]{:S(2)}) collective-permute-start(f32[8,128]{1,0:T(8,128)S(1)} %shard_map.46.refs_4_.own_cells), channel_id=1, source_target_pairs={{0,1},{1,0},{2,3},{3,2},{4,5},{5,4},{6,7},{7,6},{8,9},{9,8},{10,11... | collective-permute-start | bytes 12296 | tf_op jit(solution)/shard_map/ppermute | solution.py:471
  1.9 1.2 %shard_map.47 = (f32[4,64,512]{2,1,0:T(8,128)S(1)}, f32[4,64,512]{2,1,0:T(8,128)S(1)}, s32[1,64]{1,0:T(1,128)S(1)}, f32[1,64]{1,0:T(1,128)S(1)}) custom-call(f32[4,64,512]{2,1,0:T(8,128)} %refs_0_.1, f32[4,64,512]{2,1,0:T(8,128)} %refs_1_.1, s32[1,64]{1,0:T(1,128)} %bitcast.7, f32[1,64]{1,0:T(1,128)} %bitcast.8, f32[8,128]{1,0:T(8,128)S(1)} %shard_map.46.refs_4_.own_cells), custom_call_target="tpu_custom_call" | custom-call | bytes 2097152 | tf_op jit(solution)/shard_map/pallas_call | solution.py:212
  3.1 0.0 collective-permute-done.after.refs_0_
  3.1 2.6 %collective-permute-start.1 = (f32[8,128]{1,0:T(8,128)S(1)}, f32[8,128]{1,0:T(8,128)S(1)}, u32[]{:S(2)}, u32[]{:S(2)}) collective-permute-start(f32[8,128]{1,0:T(8,128)S(1)} %collective-permute-done.after.refs_0_), channel_id=1, source_target_pairs={{0,2},{1,3},{2,0},{3,1},{4,6},{5,7},{6,4},{7,5},{8,10},{9,11},{10,... | collective-permute-start | bytes 12296 | tf_op jit(solution)/shard_map/ppermute | solution.py:471
  5.7 2.1 %shard_map.48 = (f32[4,4,64,128]{3,2,1,0:T(8,128)S(1)}, f32[4,4,64,128]{3,2,1,0:T(8,128)S(1)}, f32[8,16,8,128]{3,2,1,0:T(8,128)S(1)}, f32[8,16,8,128]{3,2,1,0:T(...) custom-call(s32[1,64]{1,0:T(1,128)S(1)} %get-tuple-element.51.loc, ...), custom_call_target="tpu_custom_call" | custom-call | flops 5242880 | bytes 3670016 | tf_op jit(solution)/shard_map/pallas_call | solution.py:363
  7.9 0.0 collective-permute-done.1.refs_1_
  7.9 0.5 %shard_map.49 = (f32[8,8,8,128]{3,2,1,0:T(8,128)S(1)}, f32[7,16,128]{2,1,0:T(8,128)S(1)}, f32[7,16,128]{2,1,0:T(8,128)S(1)}) custom-call(f32[8,128]{1,0:T(8,128)S(1)} %shard_map.46.refs_4_.own_cells, f32[4,64,512]{2,1,0:T(8,128)S(1)} %get-tuple-element.50.t_ref.refs_10_, f32[4,4,64,128]{3,2,1,0:T(8,128)S(1)} %get-tuple-element.55.total_ref, ...), custom_call_target="tpu_custom_call" | custom-call | tf_op jit(solution)/shard_map/pallas_call | solution.py:450
  8.3 2.6 %collective-permute-start.4 = (f32[7,16,128]{2,1,0:T(8,128)S(1)}, f32[7,16,128]{2,1,0:T(8,128)S(1)}, u32[]{:S(2)}, u32[]{:S(2)}) collective-permute-start(f32[7,16,128]{2,1,0:T(8,128)S(1)} %get-tuple-element.62.after.refs_0_), channel_id=1, source_target_pairs={{0,12},{4,8},{8,4},{12,0},{16,28},{20,24},{24,20},{28,16},{1,13},{... | collective-permute-start | bytes 172040 | tf_op jit(solution)/shard_map/ppermute | solution.py:471
  10.9 0.4 %collective-permute-start.3 = (f32[7,16,128]{2,1,0:T(8,128)S(1)}, f32[7,16,128]{2,1,0:T(8,128)S(1)}, u32[]{:S(2)}, u32[]{:S(2)}) collective-permute-start(f32[7,16,128]{2,1,0:T(8,128)S(1)} %get-tuple-element.62.after.refs_0_), channel_id=1, source_target_pairs={{0,8},{4,12},{8,0},{12,4},{16,24},{20,28},{24,16},{28,20},{1,9},{5... | collective-permute-start | bytes 172040 | tf_op jit(solution)/shard_map/ppermute | solution.py:471
  11.4 0.5 %collective-permute-start.2 = (f32[7,16,128]{2,1,0:T(8,128)S(1)}, f32[7,16,128]{2,1,0:T(8,128)S(1)}, u32[]{:S(2)}, u32[]{:S(2)}) collective-permute-start(f32[7,16,128]{2,1,0:T(8,128)S(1)} %get-tuple-element.62.after.refs_0_), channel_id=1, source_target_pairs={{0,4},{4,0},{8,12},{12,8},{16,20},{20,16},{24,28},{28,24},{1,5},{5... | collective-permute-start | bytes 172040 | tf_op jit(solution)/shard_map/ppermute | solution.py:471
  11.9 0.6 %shard_map.50 = (f32[16,8,8,128]{3,2,1,0:T(8,128)S(1)}, f32[16,8,8,128]{3,2,1,0:T(8,128)S(1)}, f32[16,8,8,128]{3,2,1,0:T(8,128)S(1)}, f32[7,3,8,128]{3,2,1,0:T(8...) custom-call(f32[4,4,64,128]{3,2,1,0:T(8,128)S(1)} %get-tuple-element, ...), custom_call_target="tpu_custom_call" | custom-call | flops 2621440 | bytes 2097152 | tf_op jit(solution)/shard_map/pallas_call | solution.py:668
  12.5 0.2 shard_map.51
  12.7 0.9 %collective-permute-done.4.refs_3_ = f32[7,16,128]{2,1,0:T(8,128)S(1)} collective-permute-done((f32[7,16,128]{2,1,0:T(8,128)S(1)}, f32[7,16,128]{2,1,0:T(8,128)S(1)}, u32[]{:S(2)}, u32[]{:S(2)}) %collective-permute-start.4) | collective-permute-done | bytes 57376 | tf_op jit(solution)/shard_map/ppermute | solution.py:471
  13.6 1.5 %collective-permute-done.3.refs_2_ = f32[7,16,128]{2,1,0:T(8,128)S(1)} collective-permute-done((f32[7,16,128]{2,1,0:T(8,128)S(1)}, f32[7,16,128]{2,1,0:T(8,128)S(1)}, u32[]{:S(2)}, u32[]{:S(2)}) %collective-permute-start.3) | collective-permute-done | bytes 57376 | tf_op jit(solution)/shard_map/ppermute | solution.py:471
  15.1 0.4 %collective-permute-done.2.refs_1_ = f32[7,16,128]{2,1,0:T(8,128)S(1)} collective-permute-done((f32[7,16,128]{2,1,0:T(8,128)S(1)}, f32[7,16,128]{2,1,0:T(8,128)S(1)}, u32[]{:S(2)}, u32[]{:S(2)}) %collective-permute-start.2) | collective-permute-done | bytes 57376 | tf_op jit(solution)/shard_map/ppermute | solution.py:471
  15.5 0.1 shard_map.52
  15.6 2.7 %collective-permute-start.5 = (f32[3,16,128]{2,1,0:T(8,128)S(1)}, f32[3,16,128]{2,1,0:T(8,128)S(1)}, u32[]{:S(2)}, u32[]{:S(2)}) collective-permute-start(f32[3,16,128]{2,1,0:T(8,128)S(1)} %get-tuple-element.66.own), channel_id=1, source_target_pairs={{0,16},{4,20},{8,24},{12,28},{16,0},{20,4},{24,8},{28,12},{1,17},{... | collective-permute-start | bytes 73736 | tf_op jit(solution)/shard_map/ppermute | solution.py:471
  18.3 0.6 %shard_map.53 = (f32[4,128,256]{2,1,0:T(8,128)S(1)}, f32[4,128,256]{2,1,0:T(8,128)S(1)}) custom-call(f32[3,16,128]{2,1,0:T(8,128)S(1)} %get-tuple-element.67.refs_0_, f32[3,16,128]{2,1,0:T(8,128)S(1)} %get-tuple-element.68.refs_1_, f32[8,16,8,128]{3,2,1,0:T(8,128)S(1)} %get-tuple-element.56.refs_2_, f32[8,8,8,128]{3,2,1,0:T(8,128)S(1)} %get-tuple-element.69.refs_3_, ...), custom_call_target="tpu_custom_call" | custom-call | flops 1048576 | bytes 2097152 | tf_op jit(solution)/shard_map/pallas_call | solution.py:789
  18.8 1.6 %collective-permute-done.5.got = f32[3,16,128]{2,1,0:T(8,128)S(1)} collective-permute-done((f32[3,16,128]{2,1,0:T(8,128)S(1)}, f32[3,16,128]{2,1,0:T(8,128)S(1)}, u32[]{:S(2)}, u32[]{:S(2)}) %collective-permute-start.5) | collective-permute-done | bytes 24608 | tf_op jit(solution)/shard_map/ppermute | solution.py:471
  20.4 0.4 %shard_map.54 = (f32[16,8,8,128]{3,2,1,0:T(8,128)S(1)}, f32[7,8,128]{2,1,0:T(8,128)S(1)}, f32[3,2,128]{2,1,0:T(2,128)S(1)}, f32[7,2,128]{2,1,0:T(2,128)S(1)}) custom-call(f32[3,16,128]{2,1,0:T(8,128)S(1)} %get-tuple-element.66.own, f32[3,16,128]{2,1,0:T(8,128)S(1)} %collective-permute-done.5.got, f32[4,128,256]{2,1,0:T(8,128)S(1)} %get-tuple-element.74.base, ...), custom_call_target="tpu_custom_call" | custom-call | tf_op jit(solution)/shard_map/pallas_call | solution.py:850
  20.8 0.1 collective-permute-start.6
  20.9 1.2 %collective-permute-done.6.refs_1_ = f32[7,2,128]{2,1,0:T(2,128)S(1)} collective-permute-done((f32[7,2,128]{2,1,0:T(2,128)S(1)}, f32[7,2,128]{2,1,0:T(2,128)S(1)}, u32[]{:S(2)}, u32[]{:S(2)}) %collective-permute-start.6) | collective-permute-done | bytes 7200 | tf_op jit(solution)/shard_map/ppermute | solution.py:471
  22.1 0.7 %collective-permute-start.7 = (f32[3,2,128]{2,1,0:T(2,128)S(1)}, f32[3,2,128]{2,1,0:T(2,128)S(1)}, u32[]{:S(2)}, u32[]{:S(2)}) collective-permute-start(f32[3,2,128]{2,1,0:T(2,128)S(1)} %get-tuple-element.82.own), channel_id=1, source_target_pairs={{1,3},{3,1},{5,7},{7,5},{9,11},{11,9},{13,15},{15,13},{17,19},{19,... | collective-permute-start | bytes 9224 | tf_op jit(solution)/shard_map/ppermute | solution.py:553
  22.7 0.0 collective-permute-done.7.refs_0_
  22.8 3.8 %collective-permute-start.8 = (f32[3,2,128]{2,1,0:T(2,128)S(1)}, f32[3,2,128]{2,1,0:T(2,128)S(1)}, u32[]{:S(2)}, u32[]{:S(2)}) collective-permute-start(f32[3,2,128]{2,1,0:T(2,128)S(1)} %collective-permute-done.7.refs_0_), channel_id=1, source_target_pairs={{0,1},{1,0},{2,3},{3,2},{4,5},{5,4},{6,7},{7,6},{8,9},{9,8},{10,11... | collective-permute-start | bytes 9224 | tf_op jit(solution)/shard_map/ppermute | solution.py:471
  26.6 0.8 %shard_map.56 = (f32[4,4,64,128]{3,2,1,0:T(8,128)S(1)}, f32[4,4,64,128]{3,2,1,0:T(8,128)S(1)}) custom-call(f32[3,2,128]{2,1,0:T(2,128)S(1)} %get-tuple-element.83.refs_0_, f32[16,8,8,128]{3,2,1,0:T(8,128)S(1)} %get-tuple-element.76.yw.refs_1_, f32[16,8,8,128]{3,2,1,0:T(8,128)S(1)} %get-tuple-element.84.refs_2_, ...), custom_call_target="tpu_custom_call" | custom-call | flops 1572864 | bytes 2621440 | tf_op jit(solution)/shard_map/pallas_call | solution.py:942
  27.4 0.0 collective-permute-done.8.refs_1_
  27.4 1.2 %shard_map.57 = f32[256,512]{1,0:T(8,128)} custom-call(f32[3,2,128]{2,1,0:T(2,128)S(1)} %get-tuple-element.82.own, f32[3,2,128]{2,1,0:T(2,128)S(1)} %collective-permute-done.7.refs_0_, f32[3,2,128]{2,1,0:T(2,128)S(1)} %collective-permute-done.8.refs_1_, f32[4,4,64,128]{3,2,1,0:T(8,128)S(1)} %get-tuple-element.89.refs_2_, ...), custom_call_target="tpu_custom_call" | custom-call | tf_op jit(solution)/shard_map/pallas_call | solution.py:990
  (1 shorter events, 0.0 us)
Async XLA Ops:
  1.4 1.8 %collective-permute-start = (f32[8,128]{1,0:T(8,128)S(1)}, f32[8,128]{1,0:T(8,128)S(1)}, u32[]{:S(2)}, u32[]{:S(2)}) collective-permute-start(f32[8,128]{1,0:T(8,128)S(1)} %shard_map.46.refs_4_.own_cells), channel_id=1, source_target_pairs={{0,1},{1,0},{2,3},{3,2},{4,5},{5,4},{6,7},{7,6},{8,9},{9,8},{10,11... | collective-permute-start | bytes 12296 | tf_op jit(solution)/shard_map/ppermute | solution.py:471
  3.1 4.7 %collective-permute-start.1 = (f32[8,128]{1,0:T(8,128)S(1)}, f32[8,128]{1,0:T(8,128)S(1)}, u32[]{:S(2)}, u32[]{:S(2)}) collective-permute-start(f32[8,128]{1,0:T(8,128)S(1)} %collective-permute-done.after.refs_0_), channel_id=1, source_target_pairs={{0,2},{1,3},{2,0},{3,1},{4,6},{5,7},{6,4},{7,5},{8,10},{9,11},{10,... | collective-permute-start | bytes 12296 | tf_op jit(solution)/shard_map/ppermute | solution.py:471
  8.3 5.3 %collective-permute-start.4 = (f32[7,16,128]{2,1,0:T(8,128)S(1)}, f32[7,16,128]{2,1,0:T(8,128)S(1)}, u32[]{:S(2)}, u32[]{:S(2)}) collective-permute-start(f32[7,16,128]{2,1,0:T(8,128)S(1)} %get-tuple-element.62.after.refs_0_), channel_id=1, source_target_pairs={{0,12},{4,8},{8,4},{12,0},{16,28},{20,24},{24,20},{28,16},{1,13},{... | collective-permute-start | bytes 172040 | tf_op jit(solution)/shard_map/ppermute | solution.py:471
  10.9 4.2 %collective-permute-start.3 = (f32[7,16,128]{2,1,0:T(8,128)S(1)}, f32[7,16,128]{2,1,0:T(8,128)S(1)}, u32[]{:S(2)}, u32[]{:S(2)}) collective-permute-start(f32[7,16,128]{2,1,0:T(8,128)S(1)} %get-tuple-element.62.after.refs_0_), channel_id=1, source_target_pairs={{0,8},{4,12},{8,0},{12,4},{16,24},{20,28},{24,16},{28,20},{1,9},{5... | collective-permute-start | bytes 172040 | tf_op jit(solution)/shard_map/ppermute | solution.py:471
  11.4 4.2 %collective-permute-start.2 = (f32[7,16,128]{2,1,0:T(8,128)S(1)}, f32[7,16,128]{2,1,0:T(8,128)S(1)}, u32[]{:S(2)}, u32[]{:S(2)}) collective-permute-start(f32[7,16,128]{2,1,0:T(8,128)S(1)} %get-tuple-element.62.after.refs_0_), channel_id=1, source_target_pairs={{0,4},{4,0},{8,12},{12,8},{16,20},{20,16},{24,28},{28,24},{1,5},{5... | collective-permute-start | bytes 172040 | tf_op jit(solution)/shard_map/ppermute | solution.py:471
  15.6 4.8 %collective-permute-start.5 = (f32[3,16,128]{2,1,0:T(8,128)S(1)}, f32[3,16,128]{2,1,0:T(8,128)S(1)}, u32[]{:S(2)}, u32[]{:S(2)}) collective-permute-start(f32[3,16,128]{2,1,0:T(8,128)S(1)} %get-tuple-element.66.own), channel_id=1, source_target_pairs={{0,16},{4,20},{8,24},{12,28},{16,0},{20,4},{24,8},{28,12},{1,17},{... | collective-permute-start | bytes 73736 | tf_op jit(solution)/shard_map/ppermute | solution.py:471
  20.8 1.2 %collective-permute-start.6 = (f32[7,2,128]{2,1,0:T(2,128)S(1)}, f32[7,2,128]{2,1,0:T(2,128)S(1)}, u32[]{:S(2)}, u32[]{:S(2)}) collective-permute-start(f32[7,2,128]{2,1,0:T(2,128)S(1)} %get-tuple-element.81.refs_0_), channel_id=1, source_target_pairs={{0,1},{1,0},{2,3},{3,2},{4,5},{5,4},{6,7},{7,6},{8,9},{9,8},{10,11... | collective-permute-start | bytes 21512 | tf_op jit(solution)/shard_map/ppermute | solution.py:471
  22.1 0.7 %collective-permute-start.7 = (f32[3,2,128]{2,1,0:T(2,128)S(1)}, f32[3,2,128]{2,1,0:T(2,128)S(1)}, u32[]{:S(2)}, u32[]{:S(2)}) collective-permute-start(f32[3,2,128]{2,1,0:T(2,128)S(1)} %get-tuple-element.82.own), channel_id=1, source_target_pairs={{1,3},{3,1},{5,7},{7,5},{9,11},{11,9},{13,15},{15,13},{17,19},{19,... | collective-permute-start | bytes 9224 | tf_op jit(solution)/shard_map/ppermute | solution.py:553
  22.8 4.7 %collective-permute-start.8 = (f32[3,2,128]{2,1,0:T(2,128)S(1)}, f32[3,2,128]{2,1,0:T(2,128)S(1)}, u32[]{:S(2)}, u32[]{:S(2)}) collective-permute-start(f32[3,2,128]{2,1,0:T(2,128)S(1)} %collective-permute-done.7.refs_0_), channel_id=1, source_target_pairs={{0,1},{1,0},{2,3},{3,2},{4,5},{5,4},{6,7},{7,6},{8,9},{9,8},{10,11... | collective-permute-start | bytes 9224 | tf_op jit(solution)/shard_map/ppermute | solution.py:471

commit v14 on v13

--- a/solution.py
+++ b/solution.py
@@ -384,25 +384,18 @@
     )(loc, energy, t, b, after)
 
 
-def far_side(sources):
-    place = lax.axis_index("gy")
-    paired = (place >> 1) % 2 != place % 2
-    nothing = jnp.zeros(sources[0].shape, F32)
-    by_pair = sources[1][...] if len(sources) > 1 else nothing
-    other = sources[2][...] if len(sources) > 2 else nothing
-    return jnp.where(paired, by_pair, other)
-
-
-def x_target_kernel(count, own_cells, t_ref, total_ref, *refs):
-    w_ref, i_ref, p_ref, links, view, ends_ref, h_ref, own, send, e_s, q_s = refs[count:]
+def x_target_kernel(own_cells, t_ref, total_ref, near_ref, far_ref, *refs):
+    w_ref, i_ref, p_ref, links, view, ends_ref, h_ref, own, send, e_s, q_s = refs
     chunks, sheets, rows, _ = total_ref.shape
     lines = chunks * sheets
 
     lane = lax.broadcasted_iota(jnp.int32, (rows, LANES), 1)
     side = 2 * sheets
-    near, far = (unfold(v, 2 * side, rows) for v in (refs[0][...], far_side(refs[:count])))
-    before = jnp.where(is_odd("gy"), near, far)
-    after = jnp.where(is_odd("gy"), far, near)
+    place = lax.axis_index("gy")
+    inner = (place > 0) & (place < lax.axis_size("gy") - 1)
+    near, far = near_ref[...], jnp.where(inner, far_ref[...], 0.0)
+    before = unfold(jnp.where(is_odd("gy"), near, far), 2 * side, rows)
+    after = unfold(jnp.where(is_odd("gy"), far, near), 2 * side, rows)
     beyond = jnp.where(lane < side, pltpu.roll(before, LANES - side, 1), pltpu.roll(after, side, 1))
     mine = unfold(own_cells[...], 2 * side, rows)
     face = jnp.where(beyond > 0.0, mine + beyond, 0.0)
@@ -443,12 +436,12 @@
     send[FIRST], send[LAST] = items[0]
 
 
-def x_target(own_cells, t, total, edge_cells, w, inv, p, links, view, ends):
+def x_target(own_cells, t, total, near, far, w, inv, p, links, view, ends):
     chunks, sheets, rows, _ = total.shape
     lines = chunks * sheets
     steps = rows // SUBLANES
     return pl.pallas_call(
-        functools.partial(x_target_kernel, len(edge_cells)),
+        x_target_kernel,
         out_shape=[
             shape_of(steps, 2 * sheets, SUBLANES, LANES),
             shape_of(SUBLANES - 1, lines, LANES),
@@ -459,7 +452,7 @@
             pltpu.VMEM((2, 2 * sheets * SUBLANES, LANES), F32),
         ],
         compiler_params=params(),
-    )(own_cells, t, total, *edge_cells, w, inv, p, links, view, ends)
+    )(own_cells, t, total, near, far, w, inv, p, links, view, ends)
 
 
 def stages_of(axis):
@@ -549,7 +542,7 @@
         stage += width
         meanwhile = ()
     if one_core and stage:
-        pairs = [(i, i ^ 1 << stage) for i in range(1, 1 << stages, 2)]
+        pairs = [(i, i ^ 1 << stage if i % 2 else i) for i in range(1 << stages)]
         got = lax.ppermute(view, axis, pairs)
         return view, (got, swap(got, axis, 1)), links
     return view, swap(view, axis, 1 << stage), links
@@ -1004,13 +997,10 @@
     gy = lax.axis_size("gy")
     packed = edges(temperature, base)
     near = swap(packed, "gy", 1)
+    far = lax.ppermute(packed, "gy", [(i, ((i + 1) % gy ^ 1) - 1 if i else gy - 1) for i in range(gy)])
     t, b, loc, heat = load((temperature, base, locations[None], energy[None]), packed)
-    near, t, b = lax.optimization_barrier((near, t, b))
-    far = [swap(near, "gy", 2)] if gy > 2 else []
-    if gy > 4:
-        far.append(lax.ppermute(near, "gy", [(i, (i + 2 ^ 2) - 2) for i in range(2, gy - 2)]))
-    c, total, xw, xi, xp, x_links, x_view, xm, ends, t_steps = x_factor(loc, heat, t, b, columns * gy, near)
-    xh, x_own, view = x_target(packed, t, total, [near] + far, xw, xi, xp, x_links, x_view, ends)
+    c, total, xw, xi, xp, x_links, x_view, xm, ends, t_steps = x_factor(loc, heat, t, b, columns * gy, packed)
+    xh, x_own, view = x_target(packed, t, total, near, far, xw, xi, xp, x_links, x_view, ends)
     yw, yi, yp, inner, outer, y_view, to_y, to_x = y_factor(c, x_view)
     zw, zi = z_factor(c, view)
     own, got, ties = gather_line(view, "gx", 2, (y_view, zw))

time: 28.8 us -> 28.8 us (level)
    ppermute x0 -> x1, starting transfers between devices: none -> 2.47 us  [per_device(): lax.ppermute(packed, 'gy', [(i, ((i + 1) % gy ^ 1) - 1 if i else gy - 1)...]
    ppermute x8 -> x7, starting transfers between devices: 13.2 us -> 10.8 us  [swap(): return lax.ppermute(value, axis, [(i, i ^ flip) for i in range(count)])]
    ppermute x8 -> x7, waiting for transfers between devices: 5.58 us -> 5.57 us  [swap(): return lax.ppermute(value, axis, [(i, i ^ flip) for i in range(count)])]
where the time goes in v14:
time: 28.8 us; the launch traced here: 28.6 us
  starting transfers between devices  13.9 us (48%)
  Pallas kernels  9.01 us (31%)
  waiting for transfers between devices  5.58 us (19%)
    ppermute x7, starting transfers between devices, swap(): return lax.ppermute(value, axis, [(i, i ^ flip) for i in range(count)])  10.8 us
    ppermute x7, waiting for transfers between devices, swap(): return lax.ppermute(value, axis, [(i, i ^ flip) for i in range(count)])  5.57 us
    ppermute x1, starting transfers between devices, per_device(): lax.ppermute(packed, 'gy', [(i, ((i + 1) % gy ^ 1) - 1 if i else gy - 1)...  2.47 us
    pallas_call x1, Pallas kernels, x_factor(): pl.pallas_call(functools.partial(x_factor_kernel, plate), in_specs=[IN_VM...  2.13 us
    pallas_call x1, Pallas kernels, edges(): pl.pallas_call(functools.partial(edges_kernel, sheets), in_specs=[IN_HBM]...  1.34 us
    pallas_call x1, Pallas kernels, load(): pl.pallas_call(load_kernel, in_specs=[IN_HBM] * len(values) + [ANYWHERE],...  1.24 us
    pallas_call x1, Pallas kernels, finish(): pl.pallas_call(functools.partial(finish_kernel, stages_of('gy')), out_sha...  1.18 us
    pallas_call x1, Pallas kernels, finish_prepare(): pl.pallas_call(functools.partial(finish_prepare_kernel, len(ties) + 1), o...  0.82 us
  transfers between devices with their start and end apart: 9, of which 5 were waited for; matrix products, arithmetic and copies ran while one was open for 0% of the time, Pallas kernels for 19%

profile of v14, /device:TPU:0, one launch (start us, length us, event | category | flops | bytes accessed | tf_op | source)
XLA Modules:
  0.0 28.6 jit_solution(719392292282272211)
XLA Ops:
  0.0 1.3 %shard_map.46.refs_4_.after.own_cells = f32[8,128]{1,0:T(8,128)S(1)} custom-call(f32[256,512]{1,0:T(8,128)} %bitcast.5, f32[256,512]{1,0:T(8,128)} %bitcast.6), custom_call_target="tpu_custom_call" | custom-call | tf_op jit(solution)/shard_map/pallas_call | solution.py:186
  1.4 2.5 %collective-permute-start.1 = (f32[8,128]{1,0:T(8,128)S(1)}, f32[8,128]{1,0:T(8,128)S(1)}, u32[]{:S(2)}, u32[]{:S(2)}) collective-permute-start(f32[8,128]{1,0:T(8,128)S(1)} %shard_map.46.refs_4_.after.own_cells), channel_id=1, source_target_pairs={{0,3},{1,2},{2,1},{3,0},{4,7},{5,6},{6,5},{7,4},{8,11},{9,10},{10,... | collective-permute-start | bytes 12296 | tf_op jit(solution)/shard_map/ppermute | solution.py:1000
  3.8 0.7 %collective-permute-start = (f32[8,128]{1,0:T(8,128)S(1)}, f32[8,128]{1,0:T(8,128)S(1)}, u32[]{:S(2)}, u32[]{:S(2)}) collective-permute-start(f32[8,128]{1,0:T(8,128)S(1)} %shard_map.46.refs_4_.after.own_cells), channel_id=1, source_target_pairs={{0,1},{1,0},{2,3},{3,2},{4,5},{5,4},{6,7},{7,6},{8,9},{9,8},{10,11... | collective-permute-start | bytes 12296 | tf_op jit(solution)/shard_map/ppermute | solution.py:464
  4.5 1.2 %shard_map.47 = (f32[4,64,512]{2,1,0:T(8,128)S(1)}, f32[4,64,512]{2,1,0:T(8,128)S(1)}, s32[1,64]{1,0:T(1,128)S(1)}, f32[1,64]{1,0:T(1,128)S(1)}) custom-call(f32[4,64,512]{2,1,0:T(8,128)} %refs_0_.1, f32[4,64,512]{2,1,0:T(8,128)} %refs_1_.1, s32[1,64]{1,0:T(1,128)} %bitcast.7, f32[1,64]{1,0:T(1,128)} %bitcast.8, f32[8,128]{1,0:T(8,128)S(1)} %shard_map.46.refs_4_.after.own_cells), custom_call_target="tpu_custom_call" | custom-call | bytes 2097152 | tf_op jit(solution)/shard_map/pallas_call | solution.py:212
  5.7 2.1 %shard_map.48 = (f32[4,4,64,128]{3,2,1,0:T(8,128)S(1)}, f32[4,4,64,128]{3,2,1,0:T(8,128)S(1)}, f32[8,16,8,128]{3,2,1,0:T(8,128)S(1)}, f32[8,16,8,128]{3,2,1,0:T(...) custom-call(s32[1,64]{1,0:T(1,128)S(1)} %get-tuple-element.46.loc, ...), custom_call_target="tpu_custom_call" | custom-call | flops 5242880 | bytes 3670016 | tf_op jit(solution)/shard_map/pallas_call | solution.py:363
  7.9 0.0 collective-permute-done.1.far_ref
  7.9 0.0 collective-permute-done.near_ref
  7.9 0.5 %shard_map.49 = (f32[8,8,8,128]{3,2,1,0:T(8,128)S(1)}, f32[7,16,128]{2,1,0:T(8,128)S(1)}, f32[7,16,128]{2,1,0:T(8,128)S(1)}) custom-call(f32[8,128]{1,0:T(8,128)S(1)} %shard_map.46.refs_4_.after.own_cells, f32[4,64,512]{2,1,0:T(8,128)S(1)} %get-tuple-element.45.t_ref.refs_10_, f32[4,4,64,128]{3,2,1,0:T(8,128)S(1)} %get-tuple-element.49.total_ref, ...), custom_call_target="tpu_custom_call" | custom-call | tf_op jit(solution)/shard_map/pallas_call | solution.py:443
  8.4 2.6 %collective-permute-start.4 = (f32[7,16,128]{2,1,0:T(8,128)S(1)}, f32[7,16,128]{2,1,0:T(8,128)S(1)}, u32[]{:S(2)}, u32[]{:S(2)}) collective-permute-start(f32[7,16,128]{2,1,0:T(8,128)S(1)} %get-tuple-element.56.after.refs_0_), channel_id=1, source_target_pairs={{0,12},{4,8},{8,4},{12,0},{16,28},{20,24},{24,20},{28,16},{1,13},{... | collective-permute-start | bytes 172040 | tf_op jit(solution)/shard_map/ppermute | solution.py:464
  10.9 0.4 %collective-permute-start.3 = (f32[7,16,128]{2,1,0:T(8,128)S(1)}, f32[7,16,128]{2,1,0:T(8,128)S(1)}, u32[]{:S(2)}, u32[]{:S(2)}) collective-permute-start(f32[7,16,128]{2,1,0:T(8,128)S(1)} %get-tuple-element.56.after.refs_0_), channel_id=1, source_target_pairs={{0,8},{4,12},{8,0},{12,4},{16,24},{20,28},{24,16},{28,20},{1,9},{5... | collective-permute-start | bytes 172040 | tf_op jit(solution)/shard_map/ppermute | solution.py:464
  11.4 0.5 %collective-permute-start.2 = (f32[7,16,128]{2,1,0:T(8,128)S(1)}, f32[7,16,128]{2,1,0:T(8,128)S(1)}, u32[]{:S(2)}, u32[]{:S(2)}) collective-permute-start(f32[7,16,128]{2,1,0:T(8,128)S(1)} %get-tuple-element.56.after.refs_0_), channel_id=1, source_target_pairs={{0,4},{4,0},{8,12},{12,8},{16,20},{20,16},{24,28},{28,24},{1,5},{5... | collective-permute-start | bytes 172040 | tf_op jit(solution)/shard_map/ppermute | solution.py:464
  11.9 0.6 %shard_map.50 = (f32[16,8,8,128]{3,2,1,0:T(8,128)S(1)}, f32[16,8,8,128]{3,2,1,0:T(8,128)S(1)}, f32[16,8,8,128]{3,2,1,0:T(8,128)S(1)}, f32[7,3,8,128]{3,2,1,0:T(8...) custom-call(f32[4,4,64,128]{3,2,1,0:T(8,128)S(1)} %get-tuple-element, ...), custom_call_target="tpu_custom_call" | custom-call | flops 2621440 | bytes 2097152 | tf_op jit(solution)/shard_map/pallas_call | solution.py:661
  12.6 0.2 shard_map.51
  12.7 1.1 %collective-permute-done.4.refs_3_ = f32[7,16,128]{2,1,0:T(8,128)S(1)} collective-permute-done((f32[7,16,128]{2,1,0:T(8,128)S(1)}, f32[7,16,128]{2,1,0:T(8,128)S(1)}, u32[]{:S(2)}, u32[]{:S(2)}) %collective-permute-start.4) | collective-permute-done | bytes 57376 | tf_op jit(solution)/shard_map/ppermute | solution.py:464
  13.8 1.3 %collective-permute-done.3.refs_2_ = f32[7,16,128]{2,1,0:T(8,128)S(1)} collective-permute-done((f32[7,16,128]{2,1,0:T(8,128)S(1)}, f32[7,16,128]{2,1,0:T(8,128)S(1)}, u32[]{:S(2)}, u32[]{:S(2)}) %collective-permute-start.3) | collective-permute-done | bytes 57376 | tf_op jit(solution)/shard_map/ppermute | solution.py:464
  15.1 0.4 %collective-permute-done.2.refs_1_ = f32[7,16,128]{2,1,0:T(8,128)S(1)} collective-permute-done((f32[7,16,128]{2,1,0:T(8,128)S(1)}, f32[7,16,128]{2,1,0:T(8,128)S(1)}, u32[]{:S(2)}, u32[]{:S(2)}) %collective-permute-start.2) | collective-permute-done | bytes 57376 | tf_op jit(solution)/shard_map/ppermute | solution.py:464
  15.6 0.1 shard_map.52
  15.6 2.7 %collective-permute-start.5 = (f32[3,16,128]{2,1,0:T(8,128)S(1)}, f32[3,16,128]{2,1,0:T(8,128)S(1)}, u32[]{:S(2)}, u32[]{:S(2)}) collective-permute-start(f32[3,16,128]{2,1,0:T(8,128)S(1)} %get-tuple-element.60.own), channel_id=1, source_target_pairs={{0,16},{4,20},{8,24},{12,28},{16,0},{20,4},{24,8},{28,12},{1,17},{... | collective-permute-start | bytes 73736 | tf_op jit(solution)/shard_map/ppermute | solution.py:464
  18.3 0.6 %shard_map.53 = (f32[4,128,256]{2,1,0:T(8,128)S(1)}, f32[4,128,256]{2,1,0:T(8,128)S(1)}) custom-call(f32[3,16,128]{2,1,0:T(8,128)S(1)} %get-tuple-element.61.refs_0_, f32[3,16,128]{2,1,0:T(8,128)S(1)} %get-tuple-element.62.refs_1_, f32[8,16,8,128]{3,2,1,0:T(8,128)S(1)} %get-tuple-element.50.refs_0_.refs_2_, f32[8,8,8,128]{3,2,1,0:T(8,128)S(1)} %get-tuple-element.63.refs_3_, ...), custom_call_target="tpu_custom_call" | custom-call | flops 1048576 | bytes 2097152 | tf_op jit(solution)/shard_map/pallas_call | solution.py:782
  18.8 1.6 %collective-permute-done.5.got = f32[3,16,128]{2,1,0:T(8,128)S(1)} collective-permute-done((f32[3,16,128]{2,1,0:T(8,128)S(1)}, f32[3,16,128]{2,1,0:T(8,128)S(1)}, u32[]{:S(2)}, u32[]{:S(2)}) %collective-permute-start.5) | collective-permute-done | bytes 24608 | tf_op jit(solution)/shard_map/ppermute | solution.py:464
  20.4 0.4 %shard_map.54 = (f32[16,8,8,128]{3,2,1,0:T(8,128)S(1)}, f32[7,8,128]{2,1,0:T(8,128)S(1)}, f32[3,2,128]{2,1,0:T(2,128)S(1)}, f32[7,2,128]{2,1,0:T(2,128)S(1)}) custom-call(f32[3,16,128]{2,1,0:T(8,128)S(1)} %get-tuple-element.60.own, f32[3,16,128]{2,1,0:T(8,128)S(1)} %collective-permute-done.5.got, f32[4,128,256]{2,1,0:T(8,128)S(1)} %get-tuple-element.68.base, ...), custom_call_target="tpu_custom_call" | custom-call | tf_op jit(solution)/shard_map/pallas_call | solution.py:843
  20.8 0.1 collective-permute-start.6
  20.9 1.2 %collective-permute-done.6.refs_1_ = f32[7,2,128]{2,1,0:T(2,128)S(1)} collective-permute-done((f32[7,2,128]{2,1,0:T(2,128)S(1)}, f32[7,2,128]{2,1,0:T(2,128)S(1)}, u32[]{:S(2)}, u32[]{:S(2)}) %collective-permute-start.6) | collective-permute-done | bytes 7200 | tf_op jit(solution)/shard_map/ppermute | solution.py:464
  22.1 0.7 %collective-permute-start.7 = (f32[3,2,128]{2,1,0:T(2,128)S(1)}, f32[3,2,128]{2,1,0:T(2,128)S(1)}, u32[]{:S(2)}, u32[]{:S(2)}) collective-permute-start(f32[3,2,128]{2,1,0:T(2,128)S(1)} %get-tuple-element.76.own), channel_id=1, source_target_pairs={{0,0},{1,3},{2,2},{3,1},{4,4},{5,7},{6,6},{7,5},{8,8},{9,11},{10,1... | collective-permute-start | bytes 9224 | tf_op jit(solution)/shard_map/ppermute | solution.py:546
  22.8 0.0 collective-permute-done.7.refs_0_
  22.8 3.8 %collective-permute-start.8 = (f32[3,2,128]{2,1,0:T(2,128)S(1)}, f32[3,2,128]{2,1,0:T(2,128)S(1)}, u32[]{:S(2)}, u32[]{:S(2)}) collective-permute-start(f32[3,2,128]{2,1,0:T(2,128)S(1)} %collective-permute-done.7.refs_0_), channel_id=1, source_target_pairs={{0,1},{1,0},{2,3},{3,2},{4,5},{5,4},{6,7},{7,6},{8,9},{9,8},{10,11... | collective-permute-start | bytes 9224 | tf_op jit(solution)/shard_map/ppermute | solution.py:464
  26.6 0.8 %shard_map.56 = (f32[4,4,64,128]{3,2,1,0:T(8,128)S(1)}, f32[4,4,64,128]{3,2,1,0:T(8,128)S(1)}) custom-call(f32[3,2,128]{2,1,0:T(2,128)S(1)} %get-tuple-element.77.refs_0_, f32[16,8,8,128]{3,2,1,0:T(8,128)S(1)} %get-tuple-element.70.yw.refs_1_, f32[16,8,8,128]{3,2,1,0:T(8,128)S(1)} %get-tuple-element.78.refs_2_, ...), custom_call_target="tpu_custom_call" | custom-call | flops 1572864 | bytes 2621440 | tf_op jit(solution)/shard_map/pallas_call | solution.py:935
  27.4 0.0 collective-permute-done.8.refs_1_
  27.4 1.2 %shard_map.57 = f32[256,512]{1,0:T(8,128)} custom-call(f32[3,2,128]{2,1,0:T(2,128)S(1)} %get-tuple-element.76.own, f32[3,2,128]{2,1,0:T(2,128)S(1)} %collective-permute-done.7.refs_0_, f32[3,2,128]{2,1,0:T(2,128)S(1)} %collective-permute-done.8.refs_1_, f32[4,4,64,128]{3,2,1,0:T(8,128)S(1)} %get-tuple-element.83.refs_2_, ...), custom_call_target="tpu_custom_call" | custom-call | tf_op jit(solution)/shard_map/pallas_call | solution.py:983
  (1 shorter events, 0.0 us)
Async XLA Ops:
  1.4 6.5 %collective-permute-start.1 = (f32[8,128]{1,0:T(8,128)S(1)}, f32[8,128]{1,0:T(8,128)S(1)}, u32[]{:S(2)}, u32[]{:S(2)}) collective-permute-start(f32[8,128]{1,0:T(8,128)S(1)} %shard_map.46.refs_4_.after.own_cells), channel_id=1, source_target_pairs={{0,3},{1,2},{2,1},{3,0},{4,7},{5,6},{6,5},{7,4},{8,11},{9,10},{10,... | collective-permute-start | bytes 12296 | tf_op jit(solution)/shard_map/ppermute | solution.py:1000
  3.8 4.1 %collective-permute-start = (f32[8,128]{1,0:T(8,128)S(1)}, f32[8,128]{1,0:T(8,128)S(1)}, u32[]{:S(2)}, u32[]{:S(2)}) collective-permute-start(f32[8,128]{1,0:T(8,128)S(1)} %shard_map.46.refs_4_.after.own_cells), channel_id=1, source_target_pairs={{0,1},{1,0},{2,3},{3,2},{4,5},{5,4},{6,7},{7,6},{8,9},{9,8},{10,11... | collective-permute-start | bytes 12296 | tf_op jit(solution)/shard_map/ppermute | solution.py:464
  8.4 5.4 %collective-permute-start.4 = (f32[7,16,128]{2,1,0:T(8,128)S(1)}, f32[7,16,128]{2,1,0:T(8,128)S(1)}, u32[]{:S(2)}, u32[]{:S(2)}) collective-permute-start(f32[7,16,128]{2,1,0:T(8,128)S(1)} %get-tuple-element.56.after.refs_0_), channel_id=1, source_target_pairs={{0,12},{4,8},{8,4},{12,0},{16,28},{20,24},{24,20},{28,16},{1,13},{... | collective-permute-start | bytes 172040 | tf_op jit(solution)/shard_map/ppermute | solution.py:464
  10.9 4.2 %collective-permute-start.3 = (f32[7,16,128]{2,1,0:T(8,128)S(1)}, f32[7,16,128]{2,1,0:T(8,128)S(1)}, u32[]{:S(2)}, u32[]{:S(2)}) collective-permute-start(f32[7,16,128]{2,1,0:T(8,128)S(1)} %get-tuple-element.56.after.refs_0_), channel_id=1, source_target_pairs={{0,8},{4,12},{8,0},{12,4},{16,24},{20,28},{24,16},{28,20},{1,9},{5... | collective-permute-start | bytes 172040 | tf_op jit(solution)/shard_map/ppermute | solution.py:464
  11.4 4.2 %collective-permute-start.2 = (f32[7,16,128]{2,1,0:T(8,128)S(1)}, f32[7,16,128]{2,1,0:T(8,128)S(1)}, u32[]{:S(2)}, u32[]{:S(2)}) collective-permute-start(f32[7,16,128]{2,1,0:T(8,128)S(1)} %get-tuple-element.56.after.refs_0_), channel_id=1, source_target_pairs={{0,4},{4,0},{8,12},{12,8},{16,20},{20,16},{24,28},{28,24},{1,5},{5... | collective-permute-start | bytes 172040 | tf_op jit(solution)/shard_map/ppermute | solution.py:464
  15.6 4.8 %collective-permute-start.5 = (f32[3,16,128]{2,1,0:T(8,128)S(1)}, f32[3,16,128]{2,1,0:T(8,128)S(1)}, u32[]{:S(2)}, u32[]{:S(2)}) collective-permute-start(f32[3,16,128]{2,1,0:T(8,128)S(1)} %get-tuple-element.60.own), channel_id=1, source_target_pairs={{0,16},{4,20},{8,24},{12,28},{16,0},{20,4},{24,8},{28,12},{1,17},{... | collective-permute-start | bytes 73736 | tf_op jit(solution)/shard_map/ppermute | solution.py:464
  20.8 1.2 %collective-permute-start.6 = (f32[7,2,128]{2,1,0:T(2,128)S(1)}, f32[7,2,128]{2,1,0:T(2,128)S(1)}, u32[]{:S(2)}, u32[]{:S(2)}) collective-permute-start(f32[7,2,128]{2,1,0:T(2,128)S(1)} %get-tuple-element.75.refs_0_), channel_id=1, source_target_pairs={{0,1},{1,0},{2,3},{3,2},{4,5},{5,4},{6,7},{7,6},{8,9},{9,8},{10,11... | collective-permute-start | bytes 21512 | tf_op jit(solution)/shard_map/ppermute | solution.py:464
  22.1 0.7 %collective-permute-start.7 = (f32[3,2,128]{2,1,0:T(2,128)S(1)}, f32[3,2,128]{2,1,0:T(2,128)S(1)}, u32[]{:S(2)}, u32[]{:S(2)}) collective-permute-start(f32[3,2,128]{2,1,0:T(2,128)S(1)} %get-tuple-element.76.own), channel_id=1, source_target_pairs={{0,0},{1,3},{2,2},{3,1},{4,4},{5,7},{6,6},{7,5},{8,8},{9,11},{10,1... | collective-permute-start | bytes 9224 | tf_op jit(solution)/shard_map/ppermute | solution.py:546
  22.8 4.7 %collective-permute-start.8 = (f32[3,2,128]{2,1,0:T(2,128)S(1)}, f32[3,2,128]{2,1,0:T(2,128)S(1)}, u32[]{:S(2)}, u32[]{:S(2)}) collective-permute-start(f32[3,2,128]{2,1,0:T(2,128)S(1)} %collective-permute-done.7.refs_0_), channel_id=1, source_target_pairs={{0,1},{1,0},{2,3},{3,2},{4,5},{5,4},{6,7},{7,6},{8,9},{9,8},{10,11... | collective-permute-start | bytes 9224 | tf_op jit(solution)/shard_map/ppermute | solution.py:464

commit v15 on v14

--- a/solution.py
+++ b/solution.py
@@ -148,77 +148,49 @@
     return jnp.concatenate(parts, 0)
 
 
-def edges_kernel(sheets, t_hbm, b_hbm, packed, t_s, b_s, sems):
-    columns = t_hbm.shape[1]
-    rows = t_hbm.shape[0] // sheets
-    sides = []
-    for side, start in enumerate((0, columns - LANES)):
-        sides.append(
-            [
-                pltpu.make_async_copy(src.at[:, pl.ds(start, LANES)], dst.at[side], sems.at[i, side])
-                for i, (src, dst) in enumerate(((t_hbm, t_s), (b_hbm, b_s)))
-            ]
-        )
-        for copy in sides[-1]:
-            copy.start()
+def load_kernel(t_hbm, b_hbm, loc_hbm, energy_hbm, t_out, b_out, loc, energy, packed, sems):
+    sheets, rows, columns = t_hbm.shape
+    parts = [(0, LANES), (columns - LANES, LANES), (LANES, columns - 2 * LANES)]
+    copies = []
+    for n, (start, size) in enumerate(parts):
+        part = pl.ds(start, size)
+        for i, (src, dst) in enumerate(((t_hbm, t_out), (b_hbm, b_out))):
+            copies.append(
+                pltpu.make_async_copy(src.at[:, :, part], dst.at[:, :, part], sems.at[i, n])
+            )
+    copies.append(pltpu.make_async_copy(loc_hbm, loc, sems.at[2, 0]))
+    copies.append(pltpu.make_async_copy(energy_hbm, energy, sems.at[2, 1]))
+    for copy in copies:
+        copy.start()
     lane = lax.broadcasted_iota(jnp.int32, (rows, LANES), 1)
     total = jnp.zeros((rows, LANES), F32)
     for side, source in enumerate((0, LANES - 1)):
-        for copy in sides[side]:
+        for copy in copies[2 * side : 2 * side + 2]:
             copy.wait()
+        part = slice(parts[side][0], parts[side][0] + LANES)
         for z in range(sheets):
-            t = t_s[side, z * rows : (z + 1) * rows, :]
-            c = half_conduct(b_s[side, z * rows : (z + 1) * rows, :], t)
+            t = t_out[z, :, part]
+            c = half_conduct(b_out[z, :, part], t)
             place = 2 * sheets * side + z
             total = jnp.where(lane == place, t[:, source : source + 1], total)
             total = jnp.where(lane == place + sheets, c[:, source : source + 1], total)
     packed[...] = fold(total, 4 * sheets)
-
-
-def edges(temperature, base):
-    sheets, rows, _ = temperature.shape
-    assert rows // SUBLANES * 4 * sheets <= LANES
-    columns = temperature.shape[2]
-    fields = [
-        pltpu.with_memory_space_constraint(v.reshape(sheets * rows, columns), pltpu.HBM)
-        for v in (temperature, base)
-    ]
-    return pl.pallas_call(
-        functools.partial(edges_kernel, sheets),
-        in_specs=[IN_HBM] * 2,
-        out_shape=pltpu.VMEM((SUBLANES, LANES), F32),
-        scratch_shapes=[
-            pltpu.VMEM((2, sheets * rows, LANES), F32),
-            pltpu.VMEM((2, sheets * rows, LANES), F32),
-            pltpu.SemaphoreType.DMA((2, 2)),
-        ],
-        compiler_params=params(),
-    )(*fields)
-
-
-def load_kernel(*refs):
-    count = len(refs) // 2 - 1
-    sems = refs[-1]
-    copies = [
-        pltpu.make_async_copy(refs[i], refs[count + 1 + i], sems.at[i]) for i in range(count)
-    ]
-    for copy in copies:
-        copy.start()
-    for copy in copies:
+    for copy in copies[4:]:
         copy.wait()
 
 
-def load(values, after):
+def load(temperature, base, locations, energy):
+    sheets, rows, columns = temperature.shape
+    assert rows // SUBLANES * 4 * sheets <= LANES and columns > 2 * LANES
+    operands = (temperature, base, locations, energy)
     return pl.pallas_call(
         load_kernel,
-        in_specs=[IN_HBM] * len(values) + [ANYWHERE],
-        out_shape=[pltpu.VMEM(v.shape, v.dtype) for v in values],
-        scratch_shapes=[pltpu.SemaphoreType.DMA((len(values),))],
+        in_specs=[IN_HBM] * 4,
+        out_shape=[pltpu.VMEM(v.shape, v.dtype) for v in operands]
+        + [pltpu.VMEM((SUBLANES, LANES), F32)],
+        scratch_shapes=[pltpu.SemaphoreType.DMA((3, 3))],
         compiler_params=params(),
-        cost_estimate=pl.CostEstimate(
-            flops=0, bytes_accessed=16 * values[0].size, transcendentals=0
-        ),
-    )(*[pltpu.with_memory_space_constraint(v, pltpu.HBM) for v in values], after)
+    )(*[pltpu.with_memory_space_constraint(v, pltpu.HBM) for v in operands])
 
 
 def source_plane(loc, energy, rows, columns, plate):
@@ -530,7 +502,7 @@
     )(own, *got, *after)
 
 
-def gather_line(view, axis, widest=1, meanwhile=(), one_core=False):
+def gather_line(view, axis, widest=1, meanwhile=()):
     stages = stages_of(axis)
     links, stage = [], 0
     while stage < stages - 1:
@@ -541,10 +513,6 @@
         links += ties
         stage += width
         meanwhile = ()
-    if one_core and stage:
-        pairs = [(i, i ^ 1 << stage if i % 2 else i) for i in range(1 << stages)]
-        got = lax.ppermute(view, axis, pairs)
-        return view, (got, swap(got, axis, 1)), links
     return view, swap(view, axis, 1 << stage), links
 
 
@@ -945,14 +913,12 @@
     )(*ties, yw, yh, yp, inner, inner_own, outer, outer_own, zw, zi, t, to_x)
 
 
-def finish_kernel(stages, own, *refs):
-    *parts, base, response, zw, zi, to_x, out, o_s, sems = refs
+def finish_kernel(stages, own, got, base, response, zw, zi, to_x, out, o_s, sems):
     chunks, sheets, rows, _ = base.shape
     each = LANES // rows
     pairs = sheets // each
     copies, _, wide = o_s.shape
 
-    got = [jnp.where(is_odd("gy"), parts[0][q], parts[-1][q]) for q in range(3)]
     flux = top_flux("gy", stages, own, got)
     spread = [
         turned(to_x[...], jnp.broadcast_to(flux[m : m + 1, :], (LANES, LANES))) for m in range(pairs)
@@ -989,16 +955,15 @@
             pltpu.SemaphoreType.DMA((copies,)),
         ],
         compiler_params=params(),
-    )(own, *got, base, response, zw, zi, to_x).reshape(sheets, rows, chunks * LANES)
+    )(own, got, base, response, zw, zi, to_x).reshape(sheets, rows, chunks * LANES)
 
 
 def per_device(temperature, base, locations, energy):
     columns = temperature.shape[2]
     gy = lax.axis_size("gy")
-    packed = edges(temperature, base)
+    t, b, loc, heat, packed = load(temperature, base, locations[None], energy[None])
     near = swap(packed, "gy", 1)
     far = lax.ppermute(packed, "gy", [(i, ((i + 1) % gy ^ 1) - 1 if i else gy - 1) for i in range(gy)])
-    t, b, loc, heat = load((temperature, base, locations[None], energy[None]), packed)
     c, total, xw, xi, xp, x_links, x_view, xm, ends, t_steps = x_factor(loc, heat, t, b, columns * gy, packed)
     xh, x_own, view = x_target(packed, t, total, near, far, xw, xi, xp, x_links, x_view, ends)
     yw, yi, yp, inner, outer, y_view, to_y, to_x = y_factor(c, x_view)
@@ -1010,7 +975,7 @@
     yh, inner_own, outer_own, view = y_target(
         own, got, base, response, yw, yi, yp, inner, outer, y_view, to_y
     )
-    own, got, ties = gather_line(view, "gy", one_core=True)
+    own, got, ties = gather_line(view, "gy")
     base, response = finish_prepare(
         ties, yw, yh, yp, inner, inner_own, outer, outer_own, zw, zi, t, to_x
     )

time: 28.8 us -> 25.9 us (0.90)
  starting transfers between devices: 13.9 us -> 10.3 us
  waiting for transfers between devices: 5.58 us -> 7.58 us
  Pallas kernels: 9.01 us -> 7.82 us
    ppermute x7, starting transfers between devices: 10.8 us -> 7.79 us  [swap(): return lax.ppermute(value, axis, [(i, i ^ flip) for i in range(count)])]
    ppermute x7, waiting for transfers between devices: 5.57 us -> 7.57 us  [swap(): return lax.ppermute(value, axis, [(i, i ^ flip) for i in range(count)])]
    pallas_call x2 -> x1, Pallas kernels: 2.58 us -> 1.39 us  [load(): pl.pallas_call(load_kernel, in_specs=[IN_HBM] * 4, out_shape=[pltpu.VMEM(...]
    ppermute x1 -> x0, starting transfers between devices: 0.66 us -> none  [gather_line(): got = lax.ppermute(view, axis, pairs)]
  transfers between devices with their start and end apart: 9 -> 8, of which waited for: 5 -> 6; matrix products, arithmetic and copies ran while one was open for 0% -> 0% of each run, Pallas kernels for 19% -> 17%
where the time goes in v15:
time: 25.9 us; the launch traced here: 25.7 us
  starting transfers between devices  10.3 us (40%)
  Pallas kernels  7.82 us (30%)
  waiting for transfers between devices  7.58 us (29%)
    ppermute x7, starting transfers between devices, swap(): return lax.ppermute(value, axis, [(i, i ^ flip) for i in range(count)])  7.79 us
    ppermute x7, waiting for transfers between devices, swap(): return lax.ppermute(value, axis, [(i, i ^ flip) for i in range(count)])  7.57 us
    ppermute x1, starting transfers between devices, per_device(): lax.ppermute(packed, 'gy', [(i, ((i + 1) % gy ^ 1) - 1 if i else gy - 1)...  2.47 us
    pallas_call x1, Pallas kernels, x_factor(): pl.pallas_call(functools.partial(x_factor_kernel, plate), in_specs=[IN_VM...  2.14 us
    pallas_call x1, Pallas kernels, load(): pl.pallas_call(load_kernel, in_specs=[IN_HBM] * 4, out_shape=[pltpu.VMEM(...  1.39 us
    pallas_call x1, Pallas kernels, finish(): pl.pallas_call(functools.partial(finish_kernel, stages_of('gy')), out_sha...  1.16 us
    pallas_call x1, Pallas kernels, finish_prepare(): pl.pallas_call(functools.partial(finish_prepare_kernel, len(ties) + 1), o...  0.82 us
    pallas_call x1, Pallas kernels, y_factor(): pl.pallas_call(y_factor_kernel, in_specs=[IN_VMEM, ANYWHERE], out_shape=[...  0.63 us
  transfers between devices with their start and end apart: 8, of which 6 were waited for; matrix products, arithmetic and copies ran while one was open for 0% of the time, Pallas kernels for 17%

profile of v15, /device:TPU:0, one launch (start us, length us, event | category | flops | bytes accessed | tf_op | source)
XLA Modules:
  0.0 25.7 jit_solution(15722809846910315861)
XLA Ops:
  0.0 1.4 %shard_map.46 = (f32[4,64,512]{2,1,0:T(8,128)S(1)}, f32[4,64,512]{2,1,0:T(8,128)S(1)}, s32[1,64]{1,0:T(1,128)S(1)}, f32[1,64]{1,0:T(1,128)S(1)}, f32[8,128]{1,0:T(8,128)S(1)}) custom-call(f32[4,64,512]{2,1,0:T(8,128)} %t_hbm.1, f32[4,64,512]{2,1,0:T(8,128)} %b_hbm.1, s32[1,64]{1,0:T(1,128)} %bitcast.3, f32[1,64]{1,0:T(1,128)} %bitcast.4), custom_call_target="tpu_custom_call" | custom-call | tf_op jit(solution)/shard_map/pallas_call | solution.py:186
  1.4 2.5 %collective-permute-start.1 = (f32[8,128]{1,0:T(8,128)S(1)}, f32[8,128]{1,0:T(8,128)S(1)}, u32[]{:S(2)}, u32[]{:S(2)}) collective-permute-start(f32[8,128]{1,0:T(8,128)S(1)} %get-tuple-element.46.after.own_cells), channel_id=1, source_target_pairs={{0,3},{1,2},{2,1},{3,0},{4,7},{5,6},{6,5},{7,4},{8,11},{9,10},{10,... | collective-permute-start | bytes 12296 | tf_op jit(solution)/shard_map/ppermute | solution.py:966
  3.9 0.7 %collective-permute-start = (f32[8,128]{1,0:T(8,128)S(1)}, f32[8,128]{1,0:T(8,128)S(1)}, u32[]{:S(2)}, u32[]{:S(2)}) collective-permute-start(f32[8,128]{1,0:T(8,128)S(1)} %get-tuple-element.46.after.own_cells), channel_id=1, source_target_pairs={{0,1},{1,0},{2,3},{3,2},{4,5},{5,4},{6,7},{7,6},{8,9},{9,8},{10,11... | collective-permute-start | bytes 12296 | tf_op jit(solution)/shard_map/ppermute | solution.py:436
  4.5 2.1 %shard_map.47 = (f32[4,4,64,128]{3,2,1,0:T(8,128)S(1)}, f32[4,4,64,128]{3,2,1,0:T(8,128)S(1)}, f32[8,16,8,128]{3,2,1,0:T(8,128)S(1)}, f32[8,16,8,128]{3,2,1,0:T(...) custom-call(s32[1,64]{1,0:T(1,128)S(1)} %get-tuple-element.48.loc, ...), custom_call_target="tpu_custom_call" | custom-call | flops 5242880 | bytes 3670016 | tf_op jit(solution)/shard_map/pallas_call | solution.py:335
  6.7 0.0 collective-permute-done.1.far_ref
  6.7 0.0 collective-permute-done.near_ref
  6.7 0.5 %shard_map.48 = (f32[8,8,8,128]{3,2,1,0:T(8,128)S(1)}, f32[7,16,128]{2,1,0:T(8,128)S(1)}, f32[7,16,128]{2,1,0:T(8,128)S(1)}) custom-call(f32[8,128]{1,0:T(8,128)S(1)} %get-tuple-element.46.after.own_cells, f32[4,64,512]{2,1,0:T(8,128)S(1)} %get-tuple-element.47.t_ref.refs_10_, f32[4,4,64,128]{3,2,1,0:T(8,128)S(1)} %get-tuple-element.51.total_ref, ...), custom_call_target="tpu_custom_call" | custom-call | tf_op jit(solution)/shard_map/pallas_call | solution.py:415
  7.2 2.6 %collective-permute-start.4 = (f32[7,16,128]{2,1,0:T(8,128)S(1)}, f32[7,16,128]{2,1,0:T(8,128)S(1)}, u32[]{:S(2)}, u32[]{:S(2)}) collective-permute-start(f32[7,16,128]{2,1,0:T(8,128)S(1)} %get-tuple-element.58.after.refs_0_), channel_id=1, source_target_pairs={{0,12},{4,8},{8,4},{12,0},{16,28},{20,24},{24,20},{28,16},{1,13},{... | collective-permute-start | bytes 172040 | tf_op jit(solution)/shard_map/ppermute | solution.py:436
  9.8 0.4 %collective-permute-start.3 = (f32[7,16,128]{2,1,0:T(8,128)S(1)}, f32[7,16,128]{2,1,0:T(8,128)S(1)}, u32[]{:S(2)}, u32[]{:S(2)}) collective-permute-start(f32[7,16,128]{2,1,0:T(8,128)S(1)} %get-tuple-element.58.after.refs_0_), channel_id=1, source_target_pairs={{0,8},{4,12},{8,0},{12,4},{16,24},{20,28},{24,16},{28,20},{1,9},{5... | collective-permute-start | bytes 172040 | tf_op jit(solution)/shard_map/ppermute | solution.py:436
  10.2 0.5 %collective-permute-start.2 = (f32[7,16,128]{2,1,0:T(8,128)S(1)}, f32[7,16,128]{2,1,0:T(8,128)S(1)}, u32[]{:S(2)}, u32[]{:S(2)}) collective-permute-start(f32[7,16,128]{2,1,0:T(8,128)S(1)} %get-tuple-element.58.after.refs_0_), channel_id=1, source_target_pairs={{0,4},{4,0},{8,12},{12,8},{16,20},{20,16},{24,28},{28,24},{1,5},{5... | collective-permute-start | bytes 172040 | tf_op jit(solution)/shard_map/ppermute | solution.py:436
  10.7 0.6 %shard_map.49 = (f32[16,8,8,128]{3,2,1,0:T(8,128)S(1)}, f32[16,8,8,128]{3,2,1,0:T(8,128)S(1)}, f32[16,8,8,128]{3,2,1,0:T(8,128)S(1)}, f32[7,3,8,128]{3,2,1,0:T(8...) custom-call(f32[4,4,64,128]{3,2,1,0:T(8,128)S(1)} %get-tuple-element, ...), custom_call_target="tpu_custom_call" | custom-call | flops 2621440 | bytes 2097152 | tf_op jit(solution)/shard_map/pallas_call | solution.py:629
  11.4 0.2 shard_map.50
  11.5 1.1 %collective-permute-done.4.refs_3_ = f32[7,16,128]{2,1,0:T(8,128)S(1)} collective-permute-done((f32[7,16,128]{2,1,0:T(8,128)S(1)}, f32[7,16,128]{2,1,0:T(8,128)S(1)}, u32[]{:S(2)}, u32[]{:S(2)}) %collective-permute-start.4) | collective-permute-done | bytes 57376 | tf_op jit(solution)/shard_map/ppermute | solution.py:436
  12.6 1.3 %collective-permute-done.3.refs_2_ = f32[7,16,128]{2,1,0:T(8,128)S(1)} collective-permute-done((f32[7,16,128]{2,1,0:T(8,128)S(1)}, f32[7,16,128]{2,1,0:T(8,128)S(1)}, u32[]{:S(2)}, u32[]{:S(2)}) %collective-permute-start.3) | collective-permute-done | bytes 57376 | tf_op jit(solution)/shard_map/ppermute | solution.py:436
  13.9 0.4 %collective-permute-done.2.refs_1_ = f32[7,16,128]{2,1,0:T(8,128)S(1)} collective-permute-done((f32[7,16,128]{2,1,0:T(8,128)S(1)}, f32[7,16,128]{2,1,0:T(8,128)S(1)}, u32[]{:S(2)}, u32[]{:S(2)}) %collective-permute-start.2) | collective-permute-done | bytes 57376 | tf_op jit(solution)/shard_map/ppermute | solution.py:436
  14.4 0.1 shard_map.51
  14.4 2.7 %collective-permute-start.5 = (f32[3,16,128]{2,1,0:T(8,128)S(1)}, f32[3,16,128]{2,1,0:T(8,128)S(1)}, u32[]{:S(2)}, u32[]{:S(2)}) collective-permute-start(f32[3,16,128]{2,1,0:T(8,128)S(1)} %get-tuple-element.62.own), channel_id=1, source_target_pairs={{0,16},{4,20},{8,24},{12,28},{16,0},{20,4},{24,8},{28,12},{1,17},{... | collective-permute-start | bytes 73736 | tf_op jit(solution)/shard_map/ppermute | solution.py:436
  17.1 0.6 %shard_map.52 = (f32[4,128,256]{2,1,0:T(8,128)S(1)}, f32[4,128,256]{2,1,0:T(8,128)S(1)}) custom-call(f32[3,16,128]{2,1,0:T(8,128)S(1)} %get-tuple-element.63.refs_0_, f32[3,16,128]{2,1,0:T(8,128)S(1)} %get-tuple-element.64.refs_1_, f32[8,16,8,128]{3,2,1,0:T(8,128)S(1)} %get-tuple-element.52.refs_0_.refs_2_, f32[8,8,8,128]{3,2,1,0:T(8,128)S(1)} %get-tuple-element.65.refs_3_, ...), custom_call_target="tpu_custom_call" | custom-call | flops 1048576 | bytes 2097152 | tf_op jit(solution)/shard_map/pallas_call | solution.py:750
  17.7 1.6 %collective-permute-done.5.got = f32[3,16,128]{2,1,0:T(8,128)S(1)} collective-permute-done((f32[3,16,128]{2,1,0:T(8,128)S(1)}, f32[3,16,128]{2,1,0:T(8,128)S(1)}, u32[]{:S(2)}, u32[]{:S(2)}) %collective-permute-start.5) | collective-permute-done | bytes 24608 | tf_op jit(solution)/shard_map/ppermute | solution.py:436
  19.2 0.4 %shard_map.53 = (f32[16,8,8,128]{3,2,1,0:T(8,128)S(1)}, f32[7,8,128]{2,1,0:T(8,128)S(1)}, f32[3,2,128]{2,1,0:T(2,128)S(1)}, f32[7,2,128]{2,1,0:T(2,128)S(1)}) custom-call(f32[3,16,128]{2,1,0:T(8,128)S(1)} %get-tuple-element.62.own, f32[3,16,128]{2,1,0:T(8,128)S(1)} %collective-permute-done.5.got, f32[4,128,256]{2,1,0:T(8,128)S(1)} %get-tuple-element.70.base, ...), custom_call_target="tpu_custom_call" | custom-call | tf_op jit(solution)/shard_map/pallas_call | solution.py:811
  19.7 0.1 collective-permute-start.6
  19.7 1.2 %collective-permute-done.6.refs_1_ = f32[7,2,128]{2,1,0:T(2,128)S(1)} collective-permute-done((f32[7,2,128]{2,1,0:T(2,128)S(1)}, f32[7,2,128]{2,1,0:T(2,128)S(1)}, u32[]{:S(2)}, u32[]{:S(2)}) %collective-permute-start.6) | collective-permute-done | bytes 7200 | tf_op jit(solution)/shard_map/ppermute | solution.py:436
  20.9 0.8 %collective-permute-start.7 = (f32[3,2,128]{2,1,0:T(2,128)S(1)}, f32[3,2,128]{2,1,0:T(2,128)S(1)}, u32[]{:S(2)}, u32[]{:S(2)}) collective-permute-start(f32[3,2,128]{2,1,0:T(2,128)S(1)} %get-tuple-element.78.own), channel_id=1, source_target_pairs={{0,2},{1,3},{2,0},{3,1},{4,6},{5,7},{6,4},{7,5},{8,10},{9,11},{10,... | collective-permute-start | bytes 9224 | tf_op jit(solution)/shard_map/ppermute | solution.py:436
  21.7 0.8 %shard_map.55 = (f32[4,4,64,128]{3,2,1,0:T(8,128)S(1)}, f32[4,4,64,128]{3,2,1,0:T(8,128)S(1)}) custom-call(f32[3,2,128]{2,1,0:T(2,128)S(1)} %get-tuple-element.79.refs_0_, f32[16,8,8,128]{3,2,1,0:T(8,128)S(1)} %get-tuple-element.72.yw.refs_1_, f32[16,8,8,128]{3,2,1,0:T(8,128)S(1)} %get-tuple-element.80.refs_2_, ...), custom_call_target="tpu_custom_call" | custom-call | flops 1572864 | bytes 2621440 | tf_op jit(solution)/shard_map/pallas_call | solution.py:903
  22.6 2.0 %collective-permute-done.7.got = f32[3,2,128]{2,1,0:T(2,128)S(1)} collective-permute-done((f32[3,2,128]{2,1,0:T(2,128)S(1)}, f32[3,2,128]{2,1,0:T(2,128)S(1)}, u32[]{:S(2)}, u32[]{:S(2)}) %collective-permute-start.7) | collective-permute-done | bytes 3104 | tf_op jit(solution)/shard_map/ppermute | solution.py:436
  24.6 1.2 %shard_map.56 = f32[256,512]{1,0:T(8,128)} custom-call(f32[3,2,128]{2,1,0:T(2,128)S(1)} %get-tuple-element.78.own, f32[3,2,128]{2,1,0:T(2,128)S(1)} %collective-permute-done.7.got, f32[4,4,64,128]{3,2,1,0:T(8,128)S(1)} %get-tuple-element.85.base, f32[4,4,64,128]{3,2,1,0:T(8,128)S(1)} %get-tuple-element.86.response, ...), custom_call_target="tpu_custom_call" | custom-call | tf_op jit(solution)/shard_map/pallas_call | solution.py:949
  (1 shorter events, 0.0 us)
Async XLA Ops:
  1.4 5.3 %collective-permute-start.1 = (f32[8,128]{1,0:T(8,128)S(1)}, f32[8,128]{1,0:T(8,128)S(1)}, u32[]{:S(2)}, u32[]{:S(2)}) collective-permute-start(f32[8,128]{1,0:T(8,128)S(1)} %get-tuple-element.46.after.own_cells), channel_id=1, source_target_pairs={{0,3},{1,2},{2,1},{3,0},{4,7},{5,6},{6,5},{7,4},{8,11},{9,10},{10,... | collective-permute-start | bytes 12296 | tf_op jit(solution)/shard_map/ppermute | solution.py:966
  3.9 2.8 %collective-permute-start = (f32[8,128]{1,0:T(8,128)S(1)}, f32[8,128]{1,0:T(8,128)S(1)}, u32[]{:S(2)}, u32[]{:S(2)}) collective-permute-start(f32[8,128]{1,0:T(8,128)S(1)} %get-tuple-element.46.after.own_cells), channel_id=1, source_target_pairs={{0,1},{1,0},{2,3},{3,2},{4,5},{5,4},{6,7},{7,6},{8,9},{9,8},{10,11... | collective-permute-start | bytes 12296 | tf_op jit(solution)/shard_map/ppermute | solution.py:436
  7.2 5.4 %collective-permute-start.4 = (f32[7,16,128]{2,1,0:T(8,128)S(1)}, f32[7,16,128]{2,1,0:T(8,128)S(1)}, u32[]{:S(2)}, u32[]{:S(2)}) collective-permute-start(f32[7,16,128]{2,1,0:T(8,128)S(1)} %get-tuple-element.58.after.refs_0_), channel_id=1, source_target_pairs={{0,12},{4,8},{8,4},{12,0},{16,28},{20,24},{24,20},{28,16},{1,13},{... | collective-permute-start | bytes 172040 | tf_op jit(solution)/shard_map/ppermute | solution.py:436
  9.8 4.2 %collective-permute-start.3 = (f32[7,16,128]{2,1,0:T(8,128)S(1)}, f32[7,16,128]{2,1,0:T(8,128)S(1)}, u32[]{:S(2)}, u32[]{:S(2)}) collective-permute-start(f32[7,16,128]{2,1,0:T(8,128)S(1)} %get-tuple-element.58.after.refs_0_), channel_id=1, source_target_pairs={{0,8},{4,12},{8,0},{12,4},{16,24},{20,28},{24,16},{28,20},{1,9},{5... | collective-permute-start | bytes 172040 | tf_op jit(solution)/shard_map/ppermute | solution.py:436
  10.2 4.2 %collective-permute-start.2 = (f32[7,16,128]{2,1,0:T(8,128)S(1)}, f32[7,16,128]{2,1,0:T(8,128)S(1)}, u32[]{:S(2)}, u32[]{:S(2)}) collective-permute-start(f32[7,16,128]{2,1,0:T(8,128)S(1)} %get-tuple-element.58.after.refs_0_), channel_id=1, source_target_pairs={{0,4},{4,0},{8,12},{12,8},{16,20},{20,16},{24,28},{28,24},{1,5},{5... | collective-permute-start | bytes 172040 | tf_op jit(solution)/shard_map/ppermute | solution.py:436
  14.4 4.8 %collective-permute-start.5 = (f32[3,16,128]{2,1,0:T(8,128)S(1)}, f32[3,16,128]{2,1,0:T(8,128)S(1)}, u32[]{:S(2)}, u32[]{:S(2)}) collective-permute-start(f32[3,16,128]{2,1,0:T(8,128)S(1)} %get-tuple-element.62.own), channel_id=1, source_target_pairs={{0,16},{4,20},{8,24},{12,28},{16,0},{20,4},{24,8},{28,12},{1,17},{... | collective-permute-start | bytes 73736 | tf_op jit(solution)/shard_map/ppermute | solution.py:436
  19.7 1.2 %collective-permute-start.6 = (f32[7,2,128]{2,1,0:T(2,128)S(1)}, f32[7,2,128]{2,1,0:T(2,128)S(1)}, u32[]{:S(2)}, u32[]{:S(2)}) collective-permute-start(f32[7,2,128]{2,1,0:T(2,128)S(1)} %get-tuple-element.77.refs_0_), channel_id=1, source_target_pairs={{0,1},{1,0},{2,3},{3,2},{4,5},{5,4},{6,7},{7,6},{8,9},{9,8},{10,11... | collective-permute-start | bytes 21512 | tf_op jit(solution)/shard_map/ppermute | solution.py:436
  20.9 3.7 %collective-permute-start.7 = (f32[3,2,128]{2,1,0:T(2,128)S(1)}, f32[3,2,128]{2,1,0:T(2,128)S(1)}, u32[]{:S(2)}, u32[]{:S(2)}) collective-permute-start(f32[3,2,128]{2,1,0:T(2,128)S(1)} %get-tuple-element.78.own), channel_id=1, source_target_pairs={{0,2},{1,3},{2,0},{3,1},{4,6},{5,7},{6,4},{7,5},{8,10},{9,11},{10,... | collective-permute-start | bytes 9224 | tf_op jit(solution)/shard_map/ppermute | solution.py:436

commit v16 on v15

--- a/solution.py
+++ b/solution.py
@@ -502,7 +502,7 @@
     )(own, *got, *after)
 
 
-def gather_line(view, axis, widest=1, meanwhile=()):
+def gather_line(view, axis, widest=1, meanwhile=(), cross=False):
     stages = stages_of(axis)
     links, stage = [], 0
     while stage < stages - 1:
@@ -513,7 +513,7 @@
         links += ties
         stage += width
         meanwhile = ()
-    return view, swap(view, axis, 1 << stage), links
+    return view, swap(view, axis, 1 << stage | (cross and stage > 0)), links
 
 
 def top_flux(axis, stages, own, got):
@@ -975,7 +975,7 @@
     yh, inner_own, outer_own, view = y_target(
         own, got, base, response, yw, yi, yp, inner, outer, y_view, to_y
     )
-    own, got, ties = gather_line(view, "gy")
+    own, got, ties = gather_line(view, "gy", cross=True)
     base, response = finish_prepare(
         ties, yw, yh, yp, inner, inner_own, outer, outer_own, zw, zi, t, to_x
     )

time: 25.9 us -> 25.3 us (0.977)
  waiting for transfers between devices: 7.58 us -> 7.23 us
  starting transfers between devices: 10.3 us -> 10 us
    ppermute x7, waiting for transfers between devices: 7.57 us -> 7.23 us  [swap(): return lax.ppermute(value, axis, [(i, i ^ flip) for i in range(count)])]
where the time goes in v16:
time: 25.3 us; the launch traced here: 25.2 us
  starting transfers between devices  10 us (40%)
  Pallas kernels  7.82 us (31%)
  waiting for transfers between devices  7.23 us (29%)
    ppermute x7, starting transfers between devices, swap(): return lax.ppermute(value, axis, [(i, i ^ flip) for i in range(count)])  7.56 us
    ppermute x7, waiting for transfers between devices, swap(): return lax.ppermute(value, axis, [(i, i ^ flip) for i in range(count)])  7.23 us
    ppermute x1, starting transfers between devices, per_device(): lax.ppermute(packed, 'gy', [(i, ((i + 1) % gy ^ 1) - 1 if i else gy - 1)...  2.47 us
    pallas_call x1, Pallas kernels, x_factor(): pl.pallas_call(functools.partial(x_factor_kernel, plate), in_specs=[IN_VM...  2.14 us
    pallas_call x1, Pallas kernels, load(): pl.pallas_call(load_kernel, in_specs=[IN_HBM] * 4, out_shape=[pltpu.VMEM(...  1.39 us
    pallas_call x1, Pallas kernels, finish(): pl.pallas_call(functools.partial(finish_kernel, stages_of('gy')), out_sha...  1.16 us
    pallas_call x1, Pallas kernels, finish_prepare(): pl.pallas_call(functools.partial(finish_prepare_kernel, len(ties) + 1), o...  0.82 us
    pallas_call x1, Pallas kernels, y_factor(): pl.pallas_call(y_factor_kernel, in_specs=[IN_VMEM, ANYWHERE], out_shape=[...  0.63 us
  transfers between devices with their start and end apart: 8, of which 6 were waited for; matrix products, arithmetic and copies ran while one was open for 0% of the time, Pallas kernels for 17%

profile of v16, /device:TPU:0, one launch (start us, length us, event | category | flops | bytes accessed | tf_op | source)
XLA Modules:
  0.0 25.2 jit_solution(13026011036189045702)
XLA Ops:
  0.0 1.4 %shard_map.46 = (f32[4,64,512]{2,1,0:T(8,128)S(1)}, f32[4,64,512]{2,1,0:T(8,128)S(1)}, s32[1,64]{1,0:T(1,128)S(1)}, f32[1,64]{1,0:T(1,128)S(1)}, f32[8,128]{1,0:T(8,128)S(1)}) custom-call(f32[4,64,512]{2,1,0:T(8,128)} %t_hbm.1, f32[4,64,512]{2,1,0:T(8,128)} %b_hbm.1, s32[1,64]{1,0:T(1,128)} %bitcast.3, f32[1,64]{1,0:T(1,128)} %bitcast.4), custom_call_target="tpu_custom_call" | custom-call | tf_op jit(solution)/shard_map/pallas_call | solution.py:186
  1.4 2.5 %collective-permute-start.1 = (f32[8,128]{1,0:T(8,128)S(1)}, f32[8,128]{1,0:T(8,128)S(1)}, u32[]{:S(2)}, u32[]{:S(2)}) collective-permute-start(f32[8,128]{1,0:T(8,128)S(1)} %get-tuple-element.46.after.own_cells), channel_id=1, source_target_pairs={{0,3},{1,2},{2,1},{3,0},{4,7},{5,6},{6,5},{7,4},{8,11},{9,10},{10,... | collective-permute-start | bytes 12296 | tf_op jit(solution)/shard_map/ppermute | solution.py:966
  3.9 0.7 %collective-permute-start = (f32[8,128]{1,0:T(8,128)S(1)}, f32[8,128]{1,0:T(8,128)S(1)}, u32[]{:S(2)}, u32[]{:S(2)}) collective-permute-start(f32[8,128]{1,0:T(8,128)S(1)} %get-tuple-element.46.after.own_cells), channel_id=1, source_target_pairs={{0,1},{1,0},{2,3},{3,2},{4,5},{5,4},{6,7},{7,6},{8,9},{9,8},{10,11... | collective-permute-start | bytes 12296 | tf_op jit(solution)/shard_map/ppermute | solution.py:436
  4.5 2.1 %shard_map.47 = (f32[4,4,64,128]{3,2,1,0:T(8,128)S(1)}, f32[4,4,64,128]{3,2,1,0:T(8,128)S(1)}, f32[8,16,8,128]{3,2,1,0:T(8,128)S(1)}, f32[8,16,8,128]{3,2,1,0:T(...) custom-call(s32[1,64]{1,0:T(1,128)S(1)} %get-tuple-element.48.loc, ...), custom_call_target="tpu_custom_call" | custom-call | flops 5242880 | bytes 3670016 | tf_op jit(solution)/shard_map/pallas_call | solution.py:335
  6.7 0.0 collective-permute-done.1.far_ref
  6.7 0.0 collective-permute-done.near_ref
  6.7 0.5 %shard_map.48 = (f32[8,8,8,128]{3,2,1,0:T(8,128)S(1)}, f32[7,16,128]{2,1,0:T(8,128)S(1)}, f32[7,16,128]{2,1,0:T(8,128)S(1)}) custom-call(f32[8,128]{1,0:T(8,128)S(1)} %get-tuple-element.46.after.own_cells, f32[4,64,512]{2,1,0:T(8,128)S(1)} %get-tuple-element.47.t_ref.refs_10_, f32[4,4,64,128]{3,2,1,0:T(8,128)S(1)} %get-tuple-element.51.total_ref, ...), custom_call_target="tpu_custom_call" | custom-call | tf_op jit(solution)/shard_map/pallas_call | solution.py:415
  7.2 2.6 %collective-permute-start.4 = (f32[7,16,128]{2,1,0:T(8,128)S(1)}, f32[7,16,128]{2,1,0:T(8,128)S(1)}, u32[]{:S(2)}, u32[]{:S(2)}) collective-permute-start(f32[7,16,128]{2,1,0:T(8,128)S(1)} %get-tuple-element.58.after.refs_0_), channel_id=1, source_target_pairs={{0,12},{4,8},{8,4},{12,0},{16,28},{20,24},{24,20},{28,16},{1,13},{... | collective-permute-start | bytes 172040 | tf_op jit(solution)/shard_map/ppermute | solution.py:436
  9.8 0.4 %collective-permute-start.3 = (f32[7,16,128]{2,1,0:T(8,128)S(1)}, f32[7,16,128]{2,1,0:T(8,128)S(1)}, u32[]{:S(2)}, u32[]{:S(2)}) collective-permute-start(f32[7,16,128]{2,1,0:T(8,128)S(1)} %get-tuple-element.58.after.refs_0_), channel_id=1, source_target_pairs={{0,8},{4,12},{8,0},{12,4},{16,24},{20,28},{24,16},{28,20},{1,9},{5... | collective-permute-start | bytes 172040 | tf_op jit(solution)/shard_map/ppermute | solution.py:436
  10.2 0.5 %collective-permute-start.2 = (f32[7,16,128]{2,1,0:T(8,128)S(1)}, f32[7,16,128]{2,1,0:T(8,128)S(1)}, u32[]{:S(2)}, u32[]{:S(2)}) collective-permute-start(f32[7,16,128]{2,1,0:T(8,128)S(1)} %get-tuple-element.58.after.refs_0_), channel_id=1, source_target_pairs={{0,4},{4,0},{8,12},{12,8},{16,20},{20,16},{24,28},{28,24},{1,5},{5... | collective-permute-start | bytes 172040 | tf_op jit(solution)/shard_map/ppermute | solution.py:436
  10.7 0.6 %shard_map.49 = (f32[16,8,8,128]{3,2,1,0:T(8,128)S(1)}, f32[16,8,8,128]{3,2,1,0:T(8,128)S(1)}, f32[16,8,8,128]{3,2,1,0:T(8,128)S(1)}, f32[7,3,8,128]{3,2,1,0:T(8...) custom-call(f32[4,4,64,128]{3,2,1,0:T(8,128)S(1)} %get-tuple-element, ...), custom_call_target="tpu_custom_call" | custom-call | flops 2621440 | bytes 2097152 | tf_op jit(solution)/shard_map/pallas_call | solution.py:629
  11.4 0.2 shard_map.50
  11.5 1.1 %collective-permute-done.4.refs_3_ = f32[7,16,128]{2,1,0:T(8,128)S(1)} collective-permute-done((f32[7,16,128]{2,1,0:T(8,128)S(1)}, f32[7,16,128]{2,1,0:T(8,128)S(1)}, u32[]{:S(2)}, u32[]{:S(2)}) %collective-permute-start.4) | collective-permute-done | bytes 57376 | tf_op jit(solution)/shard_map/ppermute | solution.py:436
  12.6 1.3 %collective-permute-done.3.refs_2_ = f32[7,16,128]{2,1,0:T(8,128)S(1)} collective-permute-done((f32[7,16,128]{2,1,0:T(8,128)S(1)}, f32[7,16,128]{2,1,0:T(8,128)S(1)}, u32[]{:S(2)}, u32[]{:S(2)}) %collective-permute-start.3) | collective-permute-done | bytes 57376 | tf_op jit(solution)/shard_map/ppermute | solution.py:436
  13.9 0.4 %collective-permute-done.2.refs_1_ = f32[7,16,128]{2,1,0:T(8,128)S(1)} collective-permute-done((f32[7,16,128]{2,1,0:T(8,128)S(1)}, f32[7,16,128]{2,1,0:T(8,128)S(1)}, u32[]{:S(2)}, u32[]{:S(2)}) %collective-permute-start.2) | collective-permute-done | bytes 57376 | tf_op jit(solution)/shard_map/ppermute | solution.py:436
  14.4 0.1 shard_map.51
  14.4 2.7 %collective-permute-start.5 = (f32[3,16,128]{2,1,0:T(8,128)S(1)}, f32[3,16,128]{2,1,0:T(8,128)S(1)}, u32[]{:S(2)}, u32[]{:S(2)}) collective-permute-start(f32[3,16,128]{2,1,0:T(8,128)S(1)} %get-tuple-element.62.own), channel_id=1, source_target_pairs={{0,16},{4,20},{8,24},{12,28},{16,0},{20,4},{24,8},{28,12},{1,17},{... | collective-permute-start | bytes 73736 | tf_op jit(solution)/shard_map/ppermute | solution.py:436
  17.1 0.6 %shard_map.52 = (f32[4,128,256]{2,1,0:T(8,128)S(1)}, f32[4,128,256]{2,1,0:T(8,128)S(1)}) custom-call(f32[3,16,128]{2,1,0:T(8,128)S(1)} %get-tuple-element.63.refs_0_, f32[3,16,128]{2,1,0:T(8,128)S(1)} %get-tuple-element.64.refs_1_, f32[8,16,8,128]{3,2,1,0:T(8,128)S(1)} %get-tuple-element.52.refs_0_.refs_2_, f32[8,8,8,128]{3,2,1,0:T(8,128)S(1)} %get-tuple-element.65.refs_3_, ...), custom_call_target="tpu_custom_call" | custom-call | flops 1048576 | bytes 2097152 | tf_op jit(solution)/shard_map/pallas_call | solution.py:750
  17.7 1.6 %collective-permute-done.5.got = f32[3,16,128]{2,1,0:T(8,128)S(1)} collective-permute-done((f32[3,16,128]{2,1,0:T(8,128)S(1)}, f32[3,16,128]{2,1,0:T(8,128)S(1)}, u32[]{:S(2)}, u32[]{:S(2)}) %collective-permute-start.5) | collective-permute-done | bytes 24608 | tf_op jit(solution)/shard_map/ppermute | solution.py:436
  19.2 0.4 %shard_map.53 = (f32[16,8,8,128]{3,2,1,0:T(8,128)S(1)}, f32[7,8,128]{2,1,0:T(8,128)S(1)}, f32[3,2,128]{2,1,0:T(2,128)S(1)}, f32[7,2,128]{2,1,0:T(2,128)S(1)}) custom-call(f32[3,16,128]{2,1,0:T(8,128)S(1)} %get-tuple-element.62.own, f32[3,16,128]{2,1,0:T(8,128)S(1)} %collective-permute-done.5.got, f32[4,128,256]{2,1,0:T(8,128)S(1)} %get-tuple-element.70.base, ...), custom_call_target="tpu_custom_call" | custom-call | tf_op jit(solution)/shard_map/pallas_call | solution.py:811
  19.7 0.1 collective-permute-start.6
  19.7 1.2 %collective-permute-done.6.refs_1_ = f32[7,2,128]{2,1,0:T(2,128)S(1)} collective-permute-done((f32[7,2,128]{2,1,0:T(2,128)S(1)}, f32[7,2,128]{2,1,0:T(2,128)S(1)}, u32[]{:S(2)}, u32[]{:S(2)}) %collective-permute-start.6) | collective-permute-done | bytes 7200 | tf_op jit(solution)/shard_map/ppermute | solution.py:436
  20.9 0.6 %collective-permute-start.7 = (f32[3,2,128]{2,1,0:T(2,128)S(1)}, f32[3,2,128]{2,1,0:T(2,128)S(1)}, u32[]{:S(2)}, u32[]{:S(2)}) collective-permute-start(f32[3,2,128]{2,1,0:T(2,128)S(1)} %get-tuple-element.78.own), channel_id=1, source_target_pairs={{0,3},{1,2},{2,1},{3,0},{4,7},{5,6},{6,5},{7,4},{8,11},{9,10},{10,... | collective-permute-start | bytes 9224 | tf_op jit(solution)/shard_map/ppermute | solution.py:436
  21.5 0.8 %shard_map.55 = (f32[4,4,64,128]{3,2,1,0:T(8,128)S(1)}, f32[4,4,64,128]{3,2,1,0:T(8,128)S(1)}) custom-call(f32[3,2,128]{2,1,0:T(2,128)S(1)} %get-tuple-element.79.refs_0_, f32[16,8,8,128]{3,2,1,0:T(8,128)S(1)} %get-tuple-element.72.yw.refs_1_, f32[16,8,8,128]{3,2,1,0:T(8,128)S(1)} %get-tuple-element.80.refs_2_, ...), custom_call_target="tpu_custom_call" | custom-call | flops 1572864 | bytes 2621440 | tf_op jit(solution)/shard_map/pallas_call | solution.py:903
  22.3 1.7 %collective-permute-done.7.got = f32[3,2,128]{2,1,0:T(2,128)S(1)} collective-permute-done((f32[3,2,128]{2,1,0:T(2,128)S(1)}, f32[3,2,128]{2,1,0:T(2,128)S(1)}, u32[]{:S(2)}, u32[]{:S(2)}) %collective-permute-start.7) | collective-permute-done | bytes 3104 | tf_op jit(solution)/shard_map/ppermute | solution.py:436
  24.0 1.2 %shard_map.56 = f32[256,512]{1,0:T(8,128)} custom-call(f32[3,2,128]{2,1,0:T(2,128)S(1)} %get-tuple-element.78.own, f32[3,2,128]{2,1,0:T(2,128)S(1)} %collective-permute-done.7.got, f32[4,4,64,128]{3,2,1,0:T(8,128)S(1)} %get-tuple-element.85.base, f32[4,4,64,128]{3,2,1,0:T(8,128)S(1)} %get-tuple-element.86.response, ...), custom_call_target="tpu_custom_call" | custom-call | tf_op jit(solution)/shard_map/pallas_call | solution.py:949
  (1 shorter events, 0.0 us)
Async XLA Ops:
  1.4 5.3 %collective-permute-start.1 = (f32[8,128]{1,0:T(8,128)S(1)}, f32[8,128]{1,0:T(8,128)S(1)}, u32[]{:S(2)}, u32[]{:S(2)}) collective-permute-start(f32[8,128]{1,0:T(8,128)S(1)} %get-tuple-element.46.after.own_cells), channel_id=1, source_target_pairs={{0,3},{1,2},{2,1},{3,0},{4,7},{5,6},{6,5},{7,4},{8,11},{9,10},{10,... | collective-permute-start | bytes 12296 | tf_op jit(solution)/shard_map/ppermute | solution.py:966
  3.9 2.8 %collective-permute-start = (f32[8,128]{1,0:T(8,128)S(1)}, f32[8,128]{1,0:T(8,128)S(1)}, u32[]{:S(2)}, u32[]{:S(2)}) collective-permute-start(f32[8,128]{1,0:T(8,128)S(1)} %get-tuple-element.46.after.own_cells), channel_id=1, source_target_pairs={{0,1},{1,0},{2,3},{3,2},{4,5},{5,4},{6,7},{7,6},{8,9},{9,8},{10,11... | collective-permute-start | bytes 12296 | tf_op jit(solution)/shard_map/ppermute | solution.py:436
  7.2 5.4 %collective-permute-start.4 = (f32[7,16,128]{2,1,0:T(8,128)S(1)}, f32[7,16,128]{2,1,0:T(8,128)S(1)}, u32[]{:S(2)}, u32[]{:S(2)}) collective-permute-start(f32[7,16,128]{2,1,0:T(8,128)S(1)} %get-tuple-element.58.after.refs_0_), channel_id=1, source_target_pairs={{0,12},{4,8},{8,4},{12,0},{16,28},{20,24},{24,20},{28,16},{1,13},{... | collective-permute-start | bytes 172040 | tf_op jit(solution)/shard_map/ppermute | solution.py:436
  9.8 4.2 %collective-permute-start.3 = (f32[7,16,128]{2,1,0:T(8,128)S(1)}, f32[7,16,128]{2,1,0:T(8,128)S(1)}, u32[]{:S(2)}, u32[]{:S(2)}) collective-permute-start(f32[7,16,128]{2,1,0:T(8,128)S(1)} %get-tuple-element.58.after.refs_0_), channel_id=1, source_target_pairs={{0,8},{4,12},{8,0},{12,4},{16,24},{20,28},{24,16},{28,20},{1,9},{5... | collective-permute-start | bytes 172040 | tf_op jit(solution)/shard_map/ppermute | solution.py:436
  10.2 4.2 %collective-permute-start.2 = (f32[7,16,128]{2,1,0:T(8,128)S(1)}, f32[7,16,128]{2,1,0:T(8,128)S(1)}, u32[]{:S(2)}, u32[]{:S(2)}) collective-permute-start(f32[7,16,128]{2,1,0:T(8,128)S(1)} %get-tuple-element.58.after.refs_0_), channel_id=1, source_target_pairs={{0,4},{4,0},{8,12},{12,8},{16,20},{20,16},{24,28},{28,24},{1,5},{5... | collective-permute-start | bytes 172040 | tf_op jit(solution)/shard_map/ppermute | solution.py:436
  14.4 4.8 %collective-permute-start.5 = (f32[3,16,128]{2,1,0:T(8,128)S(1)}, f32[3,16,128]{2,1,0:T(8,128)S(1)}, u32[]{:S(2)}, u32[]{:S(2)}) collective-permute-start(f32[3,16,128]{2,1,0:T(8,128)S(1)} %get-tuple-element.62.own), channel_id=1, source_target_pairs={{0,16},{4,20},{8,24},{12,28},{16,0},{20,4},{24,8},{28,12},{1,17},{... | collective-permute-start | bytes 73736 | tf_op jit(solution)/shard_map/ppermute | solution.py:436
  19.7 1.2 %collective-permute-start.6 = (f32[7,2,128]{2,1,0:T(2,128)S(1)}, f32[7,2,128]{2,1,0:T(2,128)S(1)}, u32[]{:S(2)}, u32[]{:S(2)}) collective-permute-start(f32[7,2,128]{2,1,0:T(2,128)S(1)} %get-tuple-element.77.refs_0_), channel_id=1, source_target_pairs={{0,1},{1,0},{2,3},{3,2},{4,5},{5,4},{6,7},{7,6},{8,9},{9,8},{10,11... | collective-permute-start | bytes 21512 | tf_op jit(solution)/shard_map/ppermute | solution.py:436
  20.9 3.1 %collective-permute-start.7 = (f32[3,2,128]{2,1,0:T(2,128)S(1)}, f32[3,2,128]{2,1,0:T(2,128)S(1)}, u32[]{:S(2)}, u32[]{:S(2)}) collective-permute-start(f32[3,2,128]{2,1,0:T(2,128)S(1)} %get-tuple-element.78.own), channel_id=1, source_target_pairs={{0,3},{1,2},{2,1},{3,0},{4,7},{5,6},{6,5},{7,4},{8,11},{9,10},{10,... | collective-permute-start | bytes 9224 | tf_op jit(solution)/shard_map/ppermute | solution.py:436

commit v17 on v16

--- a/solution.py
+++ b/solution.py
@@ -133,22 +133,16 @@
 
 
 def fold(cells, used):
-    total = cells[:SUBLANES]
+    steps = cells.shape[0] // SUBLANES
+    total = cells[pl.ds(0, SUBLANES, stride=steps), :]
     lane = lax.broadcasted_iota(jnp.int32, total.shape, 1)
-    for n in range(1, cells.shape[0] // SUBLANES):
-        part = pltpu.roll(cells[n * SUBLANES : (n + 1) * SUBLANES], n * used, 1)
-        total = jnp.where(lane // used == n, part, total)
+    for k in range(1, steps):
+        part = pltpu.roll(cells[pl.ds(k, SUBLANES, stride=steps), :], k * used, 1)
+        total = jnp.where(lane // used == k, part, total)
     return total
 
 
-def unfold(cells, used, rows):
-    parts = [cells] + [
-        pltpu.roll(cells, LANES - n * used, 1) for n in range(1, rows // SUBLANES)
-    ]
-    return jnp.concatenate(parts, 0)
-
-
-def load_kernel(t_hbm, b_hbm, loc_hbm, energy_hbm, t_out, b_out, loc, energy, packed, sems):
+def load_kernel(t_hbm, b_hbm, loc_hbm, energy_hbm, t_out, b_out, loc, energy, packed, swapped, cells, sems):
     sheets, rows, columns = t_hbm.shape
     parts = [(0, LANES), (columns - LANES, LANES), (LANES, columns - 2 * LANES)]
     copies = []
@@ -163,7 +157,8 @@
     for copy in copies:
         copy.start()
     lane = lax.broadcasted_iota(jnp.int32, (rows, LANES), 1)
-    total = jnp.zeros((rows, LANES), F32)
+    edge_t = jnp.zeros((rows, LANES), F32)
+    edge_c = edge_t
     for side, source in enumerate((0, LANES - 1)):
         for copy in copies[2 * side : 2 * side + 2]:
             copy.wait()
@@ -171,24 +166,32 @@
         for z in range(sheets):
             t = t_out[z, :, part]
             c = half_conduct(b_out[z, :, part], t)
-            place = 2 * sheets * side + z
-            total = jnp.where(lane == place, t[:, source : source + 1], total)
-            total = jnp.where(lane == place + sheets, c[:, source : source + 1], total)
-    packed[...] = fold(total, 4 * sheets)
+            place = lane == sheets * side + z
+            edge_t = jnp.where(place, t[:, source : source + 1], edge_t)
+            edge_c = jnp.where(place, c[:, source : source + 1], edge_c)
+    cells[0], cells[1] = edge_t, edge_c
+    in_low = lax.broadcasted_iota(jnp.int32, (SUBLANES, LANES), 1) % (2 * sheets) < sheets
+    for i in range(2):
+        at = slice(i * SUBLANES, (i + 1) * SUBLANES)
+        folded = fold(cells.at[i], 2 * sheets)
+        packed[at, :] = folded
+        swapped[at, :] = jnp.where(
+            in_low, pltpu.roll(folded, LANES - sheets, 1), pltpu.roll(folded, sheets, 1)
+        )
     for copy in copies[4:]:
         copy.wait()
 
 
 def load(temperature, base, locations, energy):
     sheets, rows, columns = temperature.shape
-    assert rows // SUBLANES * 4 * sheets <= LANES and columns > 2 * LANES
+    assert rows // SUBLANES * 2 * sheets <= LANES and columns > 2 * LANES
     operands = (temperature, base, locations, energy)
     return pl.pallas_call(
         load_kernel,
         in_specs=[IN_HBM] * 4,
         out_shape=[pltpu.VMEM(v.shape, v.dtype) for v in operands]
-        + [pltpu.VMEM((SUBLANES, LANES), F32)],
-        scratch_shapes=[pltpu.SemaphoreType.DMA((3, 3))],
+        + [pltpu.VMEM((2 * SUBLANES, LANES), F32)] * 2,
+        scratch_shapes=[pltpu.VMEM((2, rows, LANES), F32), pltpu.SemaphoreType.DMA((3, 3))],
         compiler_params=params(),
     )(*[pltpu.with_memory_space_constraint(v, pltpu.HBM) for v in operands])
 
@@ -225,13 +228,13 @@
     return [[(y, z) for y in order[i : i + 2] for z in range(sheets)] for i in range(0, chunks, 2)]
 
 
-def x_eliminate(field, members, first_line, w_ref, i_ref, p_ref, h_ref, h_line, q_s):
+def x_eliminate(cells, members, first_line, w_ref, i_ref, p_ref, h_ref, h_line, q_s):
     steps = w_ref.shape[0]
     at = slice(first_line, first_line + len(members))
     kept_at = slice(h_line, h_line + len(members))
 
     def target(k):
-        return jnp.stack([field(y, z)[pl.ds(k, SUBLANES, stride=steps), :] for y, z in members], 0)
+        return jnp.stack([cells(y, z, k) for y, z in members], 0)
 
     def keep(k, h):
         h_ref[k, kept_at] = h
@@ -304,8 +307,8 @@
                 q_s[i, first : first + SUBLANES, :] = block[q][j]
         if n > 0:
             x_eliminate(
-                lambda y, z: total_ref.at[y, z], members, at, w_ref, i_ref, p_ref, h_ref,
-                at - 2 * sheets, ends_ref,
+                lambda y, z, k: total_ref[y, z, pl.ds(k, SUBLANES, stride=steps), :],
+                members, at, w_ref, i_ref, p_ref, h_ref, at - 2 * sheets, ends_ref,
             )
         for k in range(steps):
             for i, (y, z) in enumerate(members):
@@ -356,31 +359,32 @@
     )(loc, energy, t, b, after)
 
 
-def x_target_kernel(own_cells, t_ref, total_ref, near_ref, far_ref, *refs):
-    w_ref, i_ref, p_ref, links, view, ends_ref, h_ref, own, send, e_s, q_s = refs
+def x_target_kernel(own_cells, total_ref, near, far, *refs):
+    w_ref, i_ref, p_ref, links, view, ends_ref, h_ref, own, send, q_s = refs
     chunks, sheets, rows, _ = total_ref.shape
     lines = chunks * sheets
-
-    lane = lax.broadcasted_iota(jnp.int32, (rows, LANES), 1)
-    side = 2 * sheets
+    steps = rows // SUBLANES
+
     place = lax.axis_index("gy")
     inner = (place > 0) & (place < lax.axis_size("gy") - 1)
-    near, far = near_ref[...], jnp.where(inner, far_ref[...], 0.0)
-    before = unfold(jnp.where(is_odd("gy"), near, far), 2 * side, rows)
-    after = unfold(jnp.where(is_odd("gy"), far, near), 2 * side, rows)
-    beyond = jnp.where(lane < side, pltpu.roll(before, LANES - side, 1), pltpu.roll(after, side, 1))
-    mine = unfold(own_cells[...], 2 * side, rows)
-    face = jnp.where(beyond > 0.0, mine + beyond, 0.0)
-    flux = pltpu.roll(face, LANES - sheets, 1) * (beyond - mine)
-    for n, (y, edge) in enumerate(((0, 0), (chunks - 1, LANES - 1))):
-        for z in range(sheets):
-            at = n * side + z
-            e_s[n, z] = total_ref[y, z] + jnp.where(lane == edge, flux[:, at : at + 1], 0.0)
+    lane = lax.broadcasted_iota(jnp.int32, (SUBLANES, LANES), 1)
+    side = 2 * sheets
+    is_near = (lane % side >= sheets).astype(jnp.int32) == place % 2
+    t, c = (
+        jnp.where(is_near, near[at, :], jnp.where(inner, far[at, :], 0.0))
+        for at in (slice(0, SUBLANES), slice(SUBLANES, 2 * SUBLANES))
+    )
+    face = jnp.where(c > 0.0, own_cells[SUBLANES:, :] + c, 0.0)
+    flux = face * (t - own_cells[:SUBLANES, :])
+
+    def cells(y, z, k):
+        at = k * side + (sheets + z if y == 0 else z)
+        edge = 0 if y == 0 else LANES - 1
+        inflow = jnp.where(lane == edge, flux[:, at : at + 1], 0.0)
+        return total_ref[y, z, pl.ds(k, SUBLANES, stride=steps), :] + inflow
 
     members = line_groups(chunks, sheets)[0]
-    x_eliminate(
-        lambda y, z: e_s.at[0 if y == 0 else 1, z], members, 0, w_ref, i_ref, p_ref, h_ref, 0, q_s
-    )
+    x_eliminate(cells, members, 0, w_ref, i_ref, p_ref, h_ref, 0, q_s)
     split = len(members)
     items = [
         tuple(
@@ -408,7 +412,7 @@
     send[FIRST], send[LAST] = items[0]
 
 
-def x_target(own_cells, t, total, near, far, w, inv, p, links, view, ends):
+def x_target(own_cells, total, near, far, w, inv, p, links, view, ends):
     chunks, sheets, rows, _ = total.shape
     lines = chunks * sheets
     steps = rows // SUBLANES
@@ -420,11 +424,10 @@
             shape_of(7, lines, LANES),
         ],
         scratch_shapes=[
-            pltpu.VMEM((2, sheets, rows, LANES), F32),
             pltpu.VMEM((2, 2 * sheets * SUBLANES, LANES), F32),
         ],
         compiler_params=params(),
-    )(own_cells, t, total, near, far, w, inv, p, links, view, ends)
+    )(own_cells, total, near, far, w, inv, p, links, view, ends)
 
 
 def stages_of(axis):
@@ -961,11 +964,11 @@
 def per_device(temperature, base, locations, energy):
     columns = temperature.shape[2]
     gy = lax.axis_size("gy")
-    t, b, loc, heat, packed = load(temperature, base, locations[None], energy[None])
+    t, b, loc, heat, packed, swapped = load(temperature, base, locations[None], energy[None])
     near = swap(packed, "gy", 1)
     far = lax.ppermute(packed, "gy", [(i, ((i + 1) % gy ^ 1) - 1 if i else gy - 1) for i in range(gy)])
     c, total, xw, xi, xp, x_links, x_view, xm, ends, t_steps = x_factor(loc, heat, t, b, columns * gy, packed)
-    xh, x_own, view = x_target(packed, t, total, near, far, xw, xi, xp, x_links, x_view, ends)
+    xh, x_own, view = x_target(swapped, total, near, far, xw, xi, xp, x_links, x_view, ends)
     yw, yi, yp, inner, outer, y_view, to_y, to_x = y_factor(c, x_view)
     zw, zi = z_factor(c, view)
     own, got, ties = gather_line(view, "gx", 2, (y_view, zw))

time: 25.3 us -> 25.1 us (level)
  no operation moved by 1% of the time
where the time goes in v17:
time: 25.1 us; the launch traced here: 25 us
  starting transfers between devices  10.1 us (40%)
  Pallas kernels  7.57 us (30%)
  waiting for transfers between devices  7.17 us (29%)
    ppermute x7, starting transfers between devices, swap(): return lax.ppermute(value, axis, [(i, i ^ flip) for i in range(count)])  7.67 us
    ppermute x7, waiting for transfers between devices, swap(): return lax.ppermute(value, axis, [(i, i ^ flip) for i in range(count)])  7.17 us
    ppermute x1, starting transfers between devices, per_device(): lax.ppermute(packed, 'gy', [(i, ((i + 1) % gy ^ 1) - 1 if i else gy - 1)...  2.47 us
    pallas_call x1, Pallas kernels, x_factor(): pl.pallas_call(functools.partial(x_factor_kernel, plate), in_specs=[IN_VM...  2.12 us
    pallas_call x1, Pallas kernels, load(): pl.pallas_call(load_kernel, in_specs=[IN_HBM] * 4, out_shape=[pltpu.VMEM(...  1.49 us
    pallas_call x1, Pallas kernels, finish(): pl.pallas_call(functools.partial(finish_kernel, stages_of('gy')), out_sha...  1.16 us
    pallas_call x1, Pallas kernels, finish_prepare(): pl.pallas_call(functools.partial(finish_prepare_kernel, len(ties) + 1), o...  0.77 us
    pallas_call x1, Pallas kernels, y_factor(): pl.pallas_call(y_factor_kernel, in_specs=[IN_VMEM, ANYWHERE], out_shape=[...  0.63 us
  transfers between devices with their start and end apart: 8, of which 6 were waited for; matrix products, arithmetic and copies ran while one was open for 0% of the time, Pallas kernels for 17%

profile of v17, /device:TPU:0, one launch (start us, length us, event | category | flops | bytes accessed | tf_op | source)
XLA Modules:
  0.0 25.0 jit_solution(5206823670169975726)
XLA Ops:
  0.0 1.5 %shard_map.46 = (f32[4,64,512]{2,1,0:T(8,128)S(1)}, f32[4,64,512]{2,1,0:T(8,128)S(1)}, s32[1,64]{1,0:T(1,128)S(1)}, f32[1,64]{1,0:T(1,128)S(1)}, f32[16,128]{1,0:T(8,128)S(1)}, /*index=5*/f32[16,128]{1,0:T(8,128)S(1)}) custom-call(f32[4,64,512]{2,1,0:T(8,128)} %t_hbm.1, f32[4,64,512]{2,1,0:T(8,128)} %b_hbm.1, s32[1,64]{1,0:T(1,128)} %bitcast.3, f32[1,64]{1,0:T(1,128)} %bitcast.4), custom_call_target="tpu_custom_call" | custom-call | tf_op jit(solution)/shard_map/pallas_call | solution.py:189
  1.5 2.5 %collective-permute-start.1 = (f32[16,128]{1,0:T(8,128)S(1)}, f32[16,128]{1,0:T(8,128)S(1)}, u32[]{:S(2)}, u32[]{:S(2)}) collective-permute-start(f32[16,128]{1,0:T(8,128)S(1)} %get-tuple-element.52.after), channel_id=1, source_target_pairs={{0,3},{1,2},{2,1},{3,0},{4,7},{5,6},{6,5},{7,4},{8,11},{9,10},{10,... | collective-permute-start | bytes 24584 | tf_op jit(solution)/shard_map/ppermute | solution.py:969
  4.0 0.7 %collective-permute-start = (f32[16,128]{1,0:T(8,128)S(1)}, f32[16,128]{1,0:T(8,128)S(1)}, u32[]{:S(2)}, u32[]{:S(2)}) collective-permute-start(f32[16,128]{1,0:T(8,128)S(1)} %get-tuple-element.52.after), channel_id=1, source_target_pairs={{0,1},{1,0},{2,3},{3,2},{4,5},{5,4},{6,7},{7,6},{8,9},{9,8},{10,11... | collective-permute-start | bytes 24584 | tf_op jit(solution)/shard_map/ppermute | solution.py:439
  4.6 2.1 %shard_map.47 = (f32[4,4,64,128]{3,2,1,0:T(8,128)S(1)}, f32[4,4,64,128]{3,2,1,0:T(8,128)S(1)}, f32[8,16,8,128]{3,2,1,0:T(8,128)S(1)}, f32[8,16,8,128]{3,2,1,0:T(...) custom-call(s32[1,64]{1,0:T(1,128)S(1)} %get-tuple-element.48.loc, ...), custom_call_target="tpu_custom_call" | custom-call | flops 5242880 | bytes 3670016 | tf_op jit(solution)/shard_map/pallas_call | solution.py:338
  6.8 0.0 collective-permute-done.1.far
  6.8 0.0 collective-permute-done.near
  6.8 0.2 shard_map.48
  7.0 2.6 %collective-permute-start.4 = (f32[7,16,128]{2,1,0:T(8,128)S(1)}, f32[7,16,128]{2,1,0:T(8,128)S(1)}, u32[]{:S(2)}, u32[]{:S(2)}) collective-permute-start(f32[7,16,128]{2,1,0:T(8,128)S(1)} %get-tuple-element.60.after.refs_0_), channel_id=1, source_target_pairs={{0,12},{4,8},{8,4},{12,0},{16,28},{20,24},{24,20},{28,16},{1,13},{... | collective-permute-start | bytes 172040 | tf_op jit(solution)/shard_map/ppermute | solution.py:439
  9.6 0.4 %collective-permute-start.3 = (f32[7,16,128]{2,1,0:T(8,128)S(1)}, f32[7,16,128]{2,1,0:T(8,128)S(1)}, u32[]{:S(2)}, u32[]{:S(2)}) collective-permute-start(f32[7,16,128]{2,1,0:T(8,128)S(1)} %get-tuple-element.60.after.refs_0_), channel_id=1, source_target_pairs={{0,8},{4,12},{8,0},{12,4},{16,24},{20,28},{24,16},{28,20},{1,9},{5... | collective-permute-start | bytes 172040 | tf_op jit(solution)/shard_map/ppermute | solution.py:439
  10.0 0.5 %collective-permute-start.2 = (f32[7,16,128]{2,1,0:T(8,128)S(1)}, f32[7,16,128]{2,1,0:T(8,128)S(1)}, u32[]{:S(2)}, u32[]{:S(2)}) collective-permute-start(f32[7,16,128]{2,1,0:T(8,128)S(1)} %get-tuple-element.60.after.refs_0_), channel_id=1, source_target_pairs={{0,4},{4,0},{8,12},{12,8},{16,20},{20,16},{24,28},{28,24},{1,5},{5... | collective-permute-start | bytes 172040 | tf_op jit(solution)/shard_map/ppermute | solution.py:439
  10.6 0.6 %shard_map.49 = (f32[16,8,8,128]{3,2,1,0:T(8,128)S(1)}, f32[16,8,8,128]{3,2,1,0:T(8,128)S(1)}, f32[16,8,8,128]{3,2,1,0:T(8,128)S(1)}, f32[7,3,8,128]{3,2,1,0:T(8...) custom-call(f32[4,4,64,128]{3,2,1,0:T(8,128)S(1)} %get-tuple-element, ...), custom_call_target="tpu_custom_call" | custom-call | flops 2621440 | bytes 2097152 | tf_op jit(solution)/shard_map/pallas_call | solution.py:632
  11.2 0.2 shard_map.50
  11.4 1.1 %collective-permute-done.4.refs_3_ = f32[7,16,128]{2,1,0:T(8,128)S(1)} collective-permute-done((f32[7,16,128]{2,1,0:T(8,128)S(1)}, f32[7,16,128]{2,1,0:T(8,128)S(1)}, u32[]{:S(2)}, u32[]{:S(2)}) %collective-permute-start.4) | collective-permute-done | bytes 57376 | tf_op jit(solution)/shard_map/ppermute | solution.py:439
  12.4 1.3 %collective-permute-done.3.refs_2_ = f32[7,16,128]{2,1,0:T(8,128)S(1)} collective-permute-done((f32[7,16,128]{2,1,0:T(8,128)S(1)}, f32[7,16,128]{2,1,0:T(8,128)S(1)}, u32[]{:S(2)}, u32[]{:S(2)}) %collective-permute-start.3) | collective-permute-done | bytes 57376 | tf_op jit(solution)/shard_map/ppermute | solution.py:439
  13.8 0.4 %collective-permute-done.2.refs_1_ = f32[7,16,128]{2,1,0:T(8,128)S(1)} collective-permute-done((f32[7,16,128]{2,1,0:T(8,128)S(1)}, f32[7,16,128]{2,1,0:T(8,128)S(1)}, u32[]{:S(2)}, u32[]{:S(2)}) %collective-permute-start.2) | collective-permute-done | bytes 57376 | tf_op jit(solution)/shard_map/ppermute | solution.py:439
  14.2 0.1 shard_map.51
  14.3 2.7 %collective-permute-start.5 = (f32[3,16,128]{2,1,0:T(8,128)S(1)}, f32[3,16,128]{2,1,0:T(8,128)S(1)}, u32[]{:S(2)}, u32[]{:S(2)}) collective-permute-start(f32[3,16,128]{2,1,0:T(8,128)S(1)} %get-tuple-element.64.own), channel_id=1, source_target_pairs={{0,16},{4,20},{8,24},{12,28},{16,0},{20,4},{24,8},{28,12},{1,17},{... | collective-permute-start | bytes 73736 | tf_op jit(solution)/shard_map/ppermute | solution.py:439
  16.9 0.6 %shard_map.52 = (f32[4,128,256]{2,1,0:T(8,128)S(1)}, f32[4,128,256]{2,1,0:T(8,128)S(1)}) custom-call(f32[3,16,128]{2,1,0:T(8,128)S(1)} %get-tuple-element.65.refs_0_, f32[3,16,128]{2,1,0:T(8,128)S(1)} %get-tuple-element.66.refs_1_, f32[8,16,8,128]{3,2,1,0:T(8,128)S(1)} %get-tuple-element.54.refs_0_.refs_2_, f32[8,8,8,128]{3,2,1,0:T(8,128)S(1)} %get-tuple-element.67.refs_3_, ...), custom_call_target="tpu_custom_call" | custom-call | flops 1048576 | bytes 2097152 | tf_op jit(solution)/shard_map/pallas_call | solution.py:753
  17.5 1.6 %collective-permute-done.5.got = f32[3,16,128]{2,1,0:T(8,128)S(1)} collective-permute-done((f32[3,16,128]{2,1,0:T(8,128)S(1)}, f32[3,16,128]{2,1,0:T(8,128)S(1)}, u32[]{:S(2)}, u32[]{:S(2)}) %collective-permute-start.5) | collective-permute-done | bytes 24608 | tf_op jit(solution)/shard_map/ppermute | solution.py:439
  19.1 0.4 %shard_map.53 = (f32[16,8,8,128]{3,2,1,0:T(8,128)S(1)}, f32[7,8,128]{2,1,0:T(8,128)S(1)}, f32[3,2,128]{2,1,0:T(2,128)S(1)}, f32[7,2,128]{2,1,0:T(2,128)S(1)}) custom-call(f32[3,16,128]{2,1,0:T(8,128)S(1)} %get-tuple-element.64.own, f32[3,16,128]{2,1,0:T(8,128)S(1)} %collective-permute-done.5.got, f32[4,128,256]{2,1,0:T(8,128)S(1)} %get-tuple-element.72.base, ...), custom_call_target="tpu_custom_call" | custom-call | tf_op jit(solution)/shard_map/pallas_call | solution.py:814
  19.5 0.1 collective-permute-start.6
  19.5 1.2 %collective-permute-done.6.refs_1_ = f32[7,2,128]{2,1,0:T(2,128)S(1)} collective-permute-done((f32[7,2,128]{2,1,0:T(2,128)S(1)}, f32[7,2,128]{2,1,0:T(2,128)S(1)}, u32[]{:S(2)}, u32[]{:S(2)}) %collective-permute-start.6) | collective-permute-done | bytes 7200 | tf_op jit(solution)/shard_map/ppermute | solution.py:439
  20.7 0.7 %collective-permute-start.7 = (f32[3,2,128]{2,1,0:T(2,128)S(1)}, f32[3,2,128]{2,1,0:T(2,128)S(1)}, u32[]{:S(2)}, u32[]{:S(2)}) collective-permute-start(f32[3,2,128]{2,1,0:T(2,128)S(1)} %get-tuple-element.80.own), channel_id=1, source_target_pairs={{0,3},{1,2},{2,1},{3,0},{4,7},{5,6},{6,5},{7,4},{8,11},{9,10},{10,... | collective-permute-start | bytes 9224 | tf_op jit(solution)/shard_map/ppermute | solution.py:439
  21.4 0.8 %shard_map.55 = (f32[4,4,64,128]{3,2,1,0:T(8,128)S(1)}, f32[4,4,64,128]{3,2,1,0:T(8,128)S(1)}) custom-call(f32[3,2,128]{2,1,0:T(2,128)S(1)} %get-tuple-element.81.refs_0_, f32[16,8,8,128]{3,2,1,0:T(8,128)S(1)} %get-tuple-element.74.yw.refs_1_, f32[16,8,8,128]{3,2,1,0:T(8,128)S(1)} %get-tuple-element.82.refs_2_, ...), custom_call_target="tpu_custom_call" | custom-call | flops 1572864 | bytes 2621440 | tf_op jit(solution)/shard_map/pallas_call | solution.py:906
  22.2 1.6 %collective-permute-done.7.got = f32[3,2,128]{2,1,0:T(2,128)S(1)} collective-permute-done((f32[3,2,128]{2,1,0:T(2,128)S(1)}, f32[3,2,128]{2,1,0:T(2,128)S(1)}, u32[]{:S(2)}, u32[]{:S(2)}) %collective-permute-start.7) | collective-permute-done | bytes 3104 | tf_op jit(solution)/shard_map/ppermute | solution.py:439
  23.8 1.2 %shard_map.56 = f32[256,512]{1,0:T(8,128)} custom-call(f32[3,2,128]{2,1,0:T(2,128)S(1)} %get-tuple-element.80.own, f32[3,2,128]{2,1,0:T(2,128)S(1)} %collective-permute-done.7.got, f32[4,4,64,128]{3,2,1,0:T(8,128)S(1)} %get-tuple-element.87.base, f32[4,4,64,128]{3,2,1,0:T(8,128)S(1)} %get-tuple-element.88.response, ...), custom_call_target="tpu_custom_call" | custom-call | tf_op jit(solution)/shard_map/pallas_call | solution.py:952
  (1 shorter events, 0.0 us)
Async XLA Ops:
  1.5 5.3 %collective-permute-start.1 = (f32[16,128]{1,0:T(8,128)S(1)}, f32[16,128]{1,0:T(8,128)S(1)}, u32[]{:S(2)}, u32[]{:S(2)}) collective-permute-start(f32[16,128]{1,0:T(8,128)S(1)} %get-tuple-element.52.after), channel_id=1, source_target_pairs={{0,3},{1,2},{2,1},{3,0},{4,7},{5,6},{6,5},{7,4},{8,11},{9,10},{10,... | collective-permute-start | bytes 24584 | tf_op jit(solution)/shard_map/ppermute | solution.py:969
  4.0 2.8 %collective-permute-start = (f32[16,128]{1,0:T(8,128)S(1)}, f32[16,128]{1,0:T(8,128)S(1)}, u32[]{:S(2)}, u32[]{:S(2)}) collective-permute-start(f32[16,128]{1,0:T(8,128)S(1)} %get-tuple-element.52.after), channel_id=1, source_target_pairs={{0,1},{1,0},{2,3},{3,2},{4,5},{5,4},{6,7},{7,6},{8,9},{9,8},{10,11... | collective-permute-start | bytes 24584 | tf_op jit(solution)/shard_map/ppermute | solution.py:439
  7.0 5.4 %collective-permute-start.4 = (f32[7,16,128]{2,1,0:T(8,128)S(1)}, f32[7,16,128]{2,1,0:T(8,128)S(1)}, u32[]{:S(2)}, u32[]{:S(2)}) collective-permute-start(f32[7,16,128]{2,1,0:T(8,128)S(1)} %get-tuple-element.60.after.refs_0_), channel_id=1, source_target_pairs={{0,12},{4,8},{8,4},{12,0},{16,28},{20,24},{24,20},{28,16},{1,13},{... | collective-permute-start | bytes 172040 | tf_op jit(solution)/shard_map/ppermute | solution.py:439
  9.6 4.2 %collective-permute-start.3 = (f32[7,16,128]{2,1,0:T(8,128)S(1)}, f32[7,16,128]{2,1,0:T(8,128)S(1)}, u32[]{:S(2)}, u32[]{:S(2)}) collective-permute-start(f32[7,16,128]{2,1,0:T(8,128)S(1)} %get-tuple-element.60.after.refs_0_), channel_id=1, source_target_pairs={{0,8},{4,12},{8,0},{12,4},{16,24},{20,28},{24,16},{28,20},{1,9},{5... | collective-permute-start | bytes 172040 | tf_op jit(solution)/shard_map/ppermute | solution.py:439
  10.0 4.2 %collective-permute-start.2 = (f32[7,16,128]{2,1,0:T(8,128)S(1)}, f32[7,16,128]{2,1,0:T(8,128)S(1)}, u32[]{:S(2)}, u32[]{:S(2)}) collective-permute-start(f32[7,16,128]{2,1,0:T(8,128)S(1)} %get-tuple-element.60.after.refs_0_), channel_id=1, source_target_pairs={{0,4},{4,0},{8,12},{12,8},{16,20},{20,16},{24,28},{28,24},{1,5},{5... | collective-permute-start | bytes 172040 | tf_op jit(solution)/shard_map/ppermute | solution.py:439
  14.3 4.8 %collective-permute-start.5 = (f32[3,16,128]{2,1,0:T(8,128)S(1)}, f32[3,16,128]{2,1,0:T(8,128)S(1)}, u32[]{:S(2)}, u32[]{:S(2)}) collective-permute-start(f32[3,16,128]{2,1,0:T(8,128)S(1)} %get-tuple-element.64.own), channel_id=1, source_target_pairs={{0,16},{4,20},{8,24},{12,28},{16,0},{20,4},{24,8},{28,12},{1,17},{... | collective-permute-start | bytes 73736 | tf_op jit(solution)/shard_map/ppermute | solution.py:439
  19.5 1.2 %collective-permute-start.6 = (f32[7,2,128]{2,1,0:T(2,128)S(1)}, f32[7,2,128]{2,1,0:T(2,128)S(1)}, u32[]{:S(2)}, u32[]{:S(2)}) collective-permute-start(f32[7,2,128]{2,1,0:T(2,128)S(1)} %get-tuple-element.79.refs_0_), channel_id=1, source_target_pairs={{0,1},{1,0},{2,3},{3,2},{4,5},{5,4},{6,7},{7,6},{8,9},{9,8},{10,11... | collective-permute-start | bytes 21512 | tf_op jit(solution)/shard_map/ppermute | solution.py:439
  20.7 3.1 %collective-permute-start.7 = (f32[3,2,128]{2,1,0:T(2,128)S(1)}, f32[3,2,128]{2,1,0:T(2,128)S(1)}, u32[]{:S(2)}, u32[]{:S(2)}) collective-permute-start(f32[3,2,128]{2,1,0:T(2,128)S(1)} %get-tuple-element.80.own), channel_id=1, source_target_pairs={{0,3},{1,2},{2,1},{3,0},{4,7},{5,6},{6,5},{7,4},{8,11},{9,10},{10,... | collective-permute-start | bytes 9224 | tf_op jit(solution)/shard_map/ppermute | solution.py:439

commit v18 on v17

--- a/solution.py
+++ b/solution.py
@@ -142,7 +142,7 @@
     return total
 
 
-def load_kernel(t_hbm, b_hbm, loc_hbm, energy_hbm, t_out, b_out, loc, energy, packed, swapped, cells, sems):
+def load_kernel(t_hbm, b_hbm, loc_hbm, energy_hbm, t_out, b_out, loc, energy, packed, cells, sems):
     sheets, rows, columns = t_hbm.shape
     parts = [(0, LANES), (columns - LANES, LANES), (LANES, columns - 2 * LANES)]
     copies = []
@@ -170,14 +170,8 @@
             edge_t = jnp.where(place, t[:, source : source + 1], edge_t)
             edge_c = jnp.where(place, c[:, source : source + 1], edge_c)
     cells[0], cells[1] = edge_t, edge_c
-    in_low = lax.broadcasted_iota(jnp.int32, (SUBLANES, LANES), 1) % (2 * sheets) < sheets
     for i in range(2):
-        at = slice(i * SUBLANES, (i + 1) * SUBLANES)
-        folded = fold(cells.at[i], 2 * sheets)
-        packed[at, :] = folded
-        swapped[at, :] = jnp.where(
-            in_low, pltpu.roll(folded, LANES - sheets, 1), pltpu.roll(folded, sheets, 1)
-        )
+        packed[i * SUBLANES : (i + 1) * SUBLANES, :] = fold(cells.at[i], 2 * sheets)
     for copy in copies[4:]:
         copy.wait()
 
@@ -190,7 +184,7 @@
         load_kernel,
         in_specs=[IN_HBM] * 4,
         out_shape=[pltpu.VMEM(v.shape, v.dtype) for v in operands]
-        + [pltpu.VMEM((2 * SUBLANES, LANES), F32)] * 2,
+        + [pltpu.VMEM((2 * SUBLANES, LANES), F32)],
         scratch_shapes=[pltpu.VMEM((2, rows, LANES), F32), pltpu.SemaphoreType.DMA((3, 3))],
         compiler_params=params(),
     )(*[pltpu.with_memory_space_constraint(v, pltpu.HBM) for v in operands])
@@ -248,12 +242,17 @@
             q_s[q, first : first + SUBLANES, :] = ends[q][i]
 
 
-def x_factor_kernel(plate, loc, energy, t_ref, b_ref, after, *refs):
-    c_ref, total_ref, w_ref, i_ref, p_ref, links, view, h_ref, ends_ref, t_out, q_s, t_s = refs
+def x_factor_kernel(plate, loc, energy, t_ref, b_ref, own_cells, *refs):
+    c_ref, total_ref, w_ref, i_ref, p_ref, links, view, h_ref, ends_ref, t_out, swapped, q_s, t_s = refs
     chunks, sheets, rows, _ = c_ref.shape
     lines = chunks * sheets
     steps = rows // SUBLANES
     plane = source_plane(loc, energy, rows, chunks * LANES, plate)
+    mine = own_cells[...]
+    in_low = lax.broadcasted_iota(jnp.int32, mine.shape, 1) % (2 * sheets) < sheets
+    swapped[...] = jnp.where(
+        in_low, pltpu.roll(mine, LANES - sheets, 1), pltpu.roll(mine, sheets, 1)
+    )
 
     lane = lax.broadcasted_iota(jnp.int32, (SUBLANES, LANES), 1)
     is_first, is_last = lane == 0, lane == LANES - 1
@@ -328,7 +327,7 @@
         view[n] = whole[q]
 
 
-def x_factor(loc, energy, t, b, plate, after):
+def x_factor(loc, energy, t, b, plate, own_cells):
     sheets, rows, columns = t.shape
     chunks = columns // LANES
     lines = chunks * sheets
@@ -337,7 +336,7 @@
     stored = shape_of(steps, lines, SUBLANES, LANES)
     return pl.pallas_call(
         functools.partial(x_factor_kernel, plate),
-        in_specs=[IN_VMEM] * 4 + [ANYWHERE],
+        in_specs=[IN_VMEM] * 5,
         out_shape=[
             field,
             field,
@@ -349,6 +348,7 @@
             shape_of(steps, max(1, lines - 2 * sheets), SUBLANES, LANES),
             shape_of(2, lines * SUBLANES, LANES),
             stored,
+            shape_of(*own_cells.shape),
         ],
         scratch_shapes=[
             pltpu.VMEM((len(COEFS), lines * SUBLANES, LANES), F32),
@@ -356,7 +356,7 @@
         ],
         compiler_params=params(),
         cost_estimate=pl.CostEstimate(flops=40 * t.size, bytes_accessed=28 * t.size, transcendentals=0),
-    )(loc, energy, t, b, after)
+    )(loc, energy, t, b, own_cells)
 
 
 def x_target_kernel(own_cells, total_ref, near, far, *refs):
@@ -556,16 +556,20 @@
     return jnp.where(hit, 1.0, 0.0).astype(jnp.bfloat16)
 
 
-def turned(matrix, field):
-    high = field.astype(jnp.bfloat16)
-    low = (field - high.astype(F32)).astype(jnp.bfloat16)
-    both = jnp.concatenate([high, low], 1)
+def turned(matrix, field, rows=None):
+    high = field.astype(jnp.bfloat16).astype(F32)
+    both = jnp.concatenate([high, field - high], 1)
+    if rows:
+        both = jnp.concatenate(
+            [jnp.broadcast_to(both[n : n + 1, :], (rows, 2 * LANES)) for n in range(field.shape[0])], 0
+        )
+    both = both.astype(jnp.bfloat16)
     return lax.dot_general(
         matrix, both, (((1,), (1,)), ((), ())), preferred_element_type=F32
     )
 
 
-def y_factor_kernel(c_ref, after, w_ref, i_ref, p_ref, inner, outer, view, to_y, to_x, c_s, q_s, r_s):
+def y_factor_kernel(c_ref, after, w_ref, i_ref, p_ref, inner, outer, view, to_y, to_x, unit_low, unit_high, c_s, q_s, r_s):
     chunks, sheets, rows, _ = c_ref.shape
     each = LANES // rows
     pairs = sheets // each
@@ -622,6 +626,25 @@
     for n, q in enumerate(COEFS):
         view[n] = whole[q]
 
+    one = jnp.ones((pairs, LANES), F32)
+    for n, (low, high, field) in enumerate(((one, 0.0 * one, unit_low), (0.0 * one, one, unit_high))):
+        for y, pair in enumerate(tree_ends(chunks, outer, nothing, low, high)):
+            for i in range(2):
+                r_s[2 * n + i, y * pairs : (y + 1) * pairs, :] = pair[i]
+        for s, pair in enumerate(tree_ends(SUBLANES, inner, nothing, r_s[2 * n], r_s[2 * n + 1])):
+            for i in range(2):
+                q_s[2 * n + i, pl.ds(s, lines, stride=SUBLANES), :] = pair[i]
+        low, value = (
+            jnp.stack(
+                [q_s[2 * n + i, j * SUBLANES : (j + 1) * SUBLANES, :] for j in range(lines)], 0
+            )
+            for i in range(2)
+        )
+        for k in range(steps - 1, -1, -1):
+            value = w_ref[k] * value + p_ref[k] * low
+            for j, (y, m) in enumerate(members):
+                field[y, k * SUBLANES : (k + 1) * SUBLANES, part_of(m)] = value[j]
+
 
 def y_factor(c, after):
     chunks, sheets, rows, _ = c.shape
@@ -641,6 +664,8 @@
             shape_of(len(COEFS), pairs, LANES),
             matrix,
             matrix,
+            shape_of(chunks, LANES, pairs * LANES),
+            shape_of(chunks, LANES, pairs * LANES),
         ],
         scratch_shapes=[
             pltpu.VMEM((pairs, chunks * LANES, LANES), F32),
@@ -705,8 +730,8 @@
 
 def y_prepare_kernel(stages, *refs):
     ties = refs[: stages - 1]
-    xw, xh, xm, xp, x_links, x_own, t_ref, to_y = refs[stages - 1 : stages + 7]
-    base, response, f_s, g_s = refs[stages + 7 :]
+    xw, xh, xm, xp, x_links, x_own, t_ref, to_y, y_low, y_high = refs[stages - 1 : stages + 9]
+    base, response, to_first, to_last, fixed, f_s, g_s = refs[stages + 9 :]
     x_steps, lines = xw.shape[:2]
     chunks = base.shape[0]
     sheets = lines // chunks
@@ -741,90 +766,127 @@
                 g_s[1, y, place : place + SUBLANES, :] = unit[j]
         first = at.stop
 
+    totals = [None, None]
     for y in range(chunks):
-        base[y] = turned(to_y[...], g_s[0, y])
-        response[y] = turned(to_y[...], g_s[1, y])
-
-
-def y_prepare(ties, xw, xh, xm, xp, x_links, x_own, t, to_y, chunks):
+        field = turned(to_y[...], g_s[0, y])
+        answer = turned(to_y[...], g_s[1, y])
+        base[y] = field
+        response[y] = answer
+        for i, (unit, weight) in enumerate(((y_low, to_first), (y_high, to_last))):
+            weight[y] = unit[y] * answer
+            part = unit[y] * field
+            totals[i] = part if y == 0 else totals[i] + part
+    for i in range(2):
+        put_sums(fixed.at[i], totals[i])
+
+
+def put_sums(out, field):
+    total = jnp.sum(field, 0, keepdims=True)
+    for m in range(out.shape[0]):
+        out[m : m + 1, :] = total[:, part_of(m)]
+
+
+def y_prepare(ties, xw, xh, xm, xp, x_links, x_own, t, to_y, unit_low, unit_high):
+    chunks = unit_low.shape[0]
     x_steps, lines = xw.shape[:2]
     width = lines // chunks * x_steps * SUBLANES
     field = shape_of(chunks, LANES, width)
     return pl.pallas_call(
         functools.partial(y_prepare_kernel, len(ties) + 1),
-        out_shape=[field, field],
+        out_shape=[field] * 4 + [shape_of(2, width // LANES, LANES)],
         scratch_shapes=[
             pltpu.VMEM((2, 2, lines * SUBLANES, LANES), F32),
             pltpu.VMEM((2, chunks, width, LANES), F32),
         ],
         compiler_params=params(),
         cost_estimate=pl.CostEstimate(flops=8 * t.size, bytes_accessed=16 * t.size, transcendentals=0),
-    )(*ties, xw, xh, xm, xp, x_links, x_own, t, to_y)
-
-
-def y_target_kernel(stages, own, got, base, response, yw, yi, yp, inner, outer, view, to_y, *refs):
-    h_ref, inner_own, outer_own, send, q_s, r_s = refs
+    )(*ties, xw, xh, xm, xp, x_links, x_own, t, to_y, unit_low, unit_high)
+
+
+def y_target_kernel(stages, own, got, to_first, to_last, fixed, view, to_y, spread, send, r_s):
+    chunks, _, width = to_first.shape
+    sheets = own.shape[1] // chunks
+    rows = width // sheets
+
+    flux = top_flux("gx", stages, own, got)
+    line_of = {member: n for n, member in enumerate(sum(line_groups(chunks, sheets), []))}
+    totals = [None, None]
+    for y in range(chunks):
+        own_flux = jnp.concatenate([flux[line_of[y, z] : line_of[y, z] + 1, :] for z in range(sheets)], 0)
+        wide = turned(to_y[...], own_flux, rows)
+        spread[y] = wide
+        for i, weight in enumerate((to_first, to_last)):
+            part = weight[y] * wide
+            totals[i] = part if y == 0 else totals[i] + part
+    for n, q in enumerate(COEFS):
+        send[q] = view[n]
+    for i, q in enumerate((FIRST, LAST)):
+        put_sums(r_s.at[i], totals[i])
+        send[q] = fixed[i] + r_s[i]
+
+
+def y_target(own, got, to_first, to_last, fixed, view, to_y):
+    pairs = view.shape[1]
+    return pl.pallas_call(
+        functools.partial(y_target_kernel, stages_of("gx")),
+        out_shape=[shape_of(*to_first.shape), shape_of(7, pairs, LANES)],
+        scratch_shapes=[pltpu.VMEM((2, pairs, LANES), F32)],
+        compiler_params=params(),
+    )(own, got, to_first, to_last, fixed, view, to_y)
+
+
+def y_eliminate_kernel(base, response, spread, yw, yi, yp, inner, outer, after, *refs):
+    h_ref, inner_own, outer_own, q_s, r_s = refs
     chunks, _, width = base.shape
     pairs = width // LANES
-    sheets = own.shape[1] // chunks
-    rows = width // sheets
     steps = yw.shape[0]
-
-    flux = top_flux("gx", stages, own, got)
-    line_of = {member: n for n, member in enumerate(sum(line_groups(chunks, sheets), []))}
-    fields = []
-    for y in range(chunks):
-        spread = jnp.concatenate(
+    members = [(y, m) for y in range(chunks) for m in range(pairs)]
+
+    def target(k):
+        at = slice(k * SUBLANES, (k + 1) * SUBLANES)
+        return jnp.stack(
             [
-                jnp.broadcast_to(flux[line_of[y, z] : line_of[y, z] + 1, :], (rows, LANES))
-                for z in range(sheets)
+                base[y, at, part_of(m)] + response[y, at, part_of(m)] * spread[y, at, part_of(m)]
+                for y, m in members
             ],
             0,
         )
-        fields.append(base[y] + response[y] * turned(to_y[...], spread))
-
-    def target(k):
-        at = slice(k * SUBLANES, (k + 1) * SUBLANES)
-        return jnp.stack(
-            [fields[y][at, m * LANES : (m + 1) * LANES] for y in range(chunks) for m in range(pairs)], 0
-        )
 
     def keep(k, h):
         h_ref[k] = h
 
     ends = eliminate(target, steps, lambda k: yw[k], lambda k: yi[k], lambda k: yp[k], keep)
     for q in range(2):
-        for i in range(chunks * pairs):
+        for i in range(len(members)):
             q_s[q, i * SUBLANES : (i + 1) * SUBLANES, :] = ends[q][i]
     items = [
-        tuple(q_s[q, pl.ds(s, chunks * pairs, stride=SUBLANES), :] for q in range(2))
+        tuple(q_s[q, pl.ds(s, len(members), stride=SUBLANES), :] for q in range(2))
         for s in range(SUBLANES)
     ]
     r_s[0], r_s[1] = join_tree(items, inner, inner_own)
     items = [tuple(r_s[q, y * pairs : (y + 1) * pairs, :] for q in range(2)) for y in range(chunks)]
-    for n, q in enumerate(COEFS):
-        send[q] = view[n]
-    send[FIRST], send[LAST] = join_tree(items, outer, outer_own)
-
-
-def y_target(own, got, base, response, yw, yi, yp, inner, outer, view, to_y):
+    join_tree(items, outer, outer_own)
+
+
+def y_eliminate(base, response, spread, yw, yi, yp, inner, outer, after):
     y_lines = yw.shape[1]
-    pairs = view.shape[1]
+    pairs = outer.shape[2]
     chunks = y_lines // pairs
     return pl.pallas_call(
-        functools.partial(y_target_kernel, stages_of("gx")),
+        y_eliminate_kernel,
+        in_specs=[IN_VMEM] * 8 + [ANYWHERE],
         out_shape=[
             shape_of(*yw.shape),
             shape_of(SUBLANES - 1, y_lines, LANES),
             shape_of(chunks - 1, pairs, LANES),
-            shape_of(7, pairs, LANES),
         ],
         scratch_shapes=[
             pltpu.VMEM((2, y_lines * SUBLANES, LANES), F32),
             pltpu.VMEM((2, y_lines, LANES), F32),
         ],
         compiler_params=params(),
-    )(own, got, base, response, yw, yi, yp, inner, outer, view, to_y)
+        cost_estimate=pl.CostEstimate(flops=8 * base.size, bytes_accessed=16 * base.size, transcendentals=0),
+    )(base, response, spread, yw, yi, yp, inner, outer, after)
 
 
 def z_solve(zw, zi, field, at, keep):
@@ -924,7 +986,7 @@
 
     flux = top_flux("gy", stages, own, got)
     spread = [
-        turned(to_x[...], jnp.broadcast_to(flux[m : m + 1, :], (LANES, LANES))) for m in range(pairs)
+        turned(to_x[...], flux[m : m + 1, :], LANES) for m in range(pairs)
     ]
     started = []
     for n in range(copies):
@@ -964,21 +1026,20 @@
 def per_device(temperature, base, locations, energy):
     columns = temperature.shape[2]
     gy = lax.axis_size("gy")
-    t, b, loc, heat, packed, swapped = load(temperature, base, locations[None], energy[None])
+    t, b, loc, heat, packed = load(temperature, base, locations[None], energy[None])
     near = swap(packed, "gy", 1)
     far = lax.ppermute(packed, "gy", [(i, ((i + 1) % gy ^ 1) - 1 if i else gy - 1) for i in range(gy)])
-    c, total, xw, xi, xp, x_links, x_view, xm, ends, t_steps = x_factor(loc, heat, t, b, columns * gy, packed)
+    c, total, xw, xi, xp, x_links, x_view, xm, ends, t_steps, swapped = x_factor(loc, heat, t, b, columns * gy, packed)
     xh, x_own, view = x_target(swapped, total, near, far, xw, xi, xp, x_links, x_view, ends)
-    yw, yi, yp, inner, outer, y_view, to_y, to_x = y_factor(c, x_view)
+    yw, yi, yp, inner, outer, y_view, to_y, to_x, unit_low, unit_high = y_factor(c, x_view)
     zw, zi = z_factor(c, view)
     own, got, ties = gather_line(view, "gx", 2, (y_view, zw))
-    base, response = y_prepare(
-        ties, xw, xh, xm, xp, x_links, x_own, t_steps, to_y, columns // LANES
+    base, response, to_first, to_last, fixed = y_prepare(
+        ties, xw, xh, xm, xp, x_links, x_own, t_steps, to_y, unit_low, unit_high
     )
-    yh, inner_own, outer_own, view = y_target(
-        own, got, base, response, yw, yi, yp, inner, outer, y_view, to_y
-    )
-    own, got, ties = gather_line(view, "gy", cross=True)
+    spread, view = y_target(own, got, to_first, to_last, fixed, y_view, to_y)
+    yh, inner_own, outer_own = y_eliminate(base, response, spread, yw, yi, yp, inner, outer, view)
+    own, got, ties = gather_line(view, "gy", meanwhile=(yh,), cross=True)
     base, response = finish_prepare(
         ties, yw, yh, yp, inner, inner_own, outer, outer_own, zw, zi, t, to_x
     )

time: 25.1 us -> 25 us (level)
  waiting for transfers between devices: 7.17 us -> 6.56 us
  Pallas kernels: 7.57 us -> 8.09 us
    ppermute x7, waiting for transfers between devices: 7.17 us -> 6.56 us  [swap(): return lax.ppermute(value, axis, [(i, i ^ flip) for i in range(count)])]
    pallas_call x0 -> x1, Pallas kernels: none -> 0.26 us  [y_eliminate(): pl.pallas_call(y_eliminate_kernel, in_specs=[IN_VMEM] * 8 + [ANYWHERE], o...]
  transfers between devices with their start and end apart: 8 -> 8, of which waited for: 6 -> 6; matrix products, arithmetic and copies ran while one was open for 0% -> 0% of each run, Pallas kernels for 17% -> 20%
where the time goes in v18:
time: 25 us; the launch traced here: 24.9 us
  starting transfers between devices  10.1 us (40%)
  Pallas kernels  8.09 us (32%)
  waiting for transfers between devices  6.56 us (26%)
    ppermute x7, starting transfers between devices, swap(): return lax.ppermute(value, axis, [(i, i ^ flip) for i in range(count)])  7.66 us
    ppermute x7, waiting for transfers between devices, swap(): return lax.ppermute(value, axis, [(i, i ^ flip) for i in range(count)])  6.56 us
    ppermute x1, starting transfers between devices, per_device(): lax.ppermute(packed, 'gy', [(i, ((i + 1) % gy ^ 1) - 1 if i else gy - 1)...  2.47 us
    pallas_call x1, Pallas kernels, x_factor(): pl.pallas_call(functools.partial(x_factor_kernel, plate), in_specs=[IN_VM...  2.13 us
    pallas_call x1, Pallas kernels, load(): pl.pallas_call(load_kernel, in_specs=[IN_HBM] * 4, out_shape=[pltpu.VMEM(...  1.42 us
    pallas_call x1, Pallas kernels, finish(): pl.pallas_call(functools.partial(finish_kernel, stages_of('gy')), out_sha...  1.15 us
    pallas_call x1, Pallas kernels, y_factor(): pl.pallas_call(y_factor_kernel, in_specs=[IN_VMEM, ANYWHERE], out_shape=[...  0.84 us
    pallas_call x1, Pallas kernels, finish_prepare(): pl.pallas_call(functools.partial(finish_prepare_kernel, len(ties) + 1), o...  0.82 us
  transfers between devices with their start and end apart: 8, of which 6 were waited for; matrix products, arithmetic and copies ran while one was open for 0% of the time, Pallas kernels for 20%

profile of v18, /device:TPU:0, one launch (start us, length us, event | category | flops | bytes accessed | tf_op | source)
XLA Modules:
  0.0 24.9 jit_solution(14725564016195494468)
XLA Ops:
  0.0 1.4 %shard_map.46 = (f32[4,64,512]{2,1,0:T(8,128)S(1)}, f32[4,64,512]{2,1,0:T(8,128)S(1)}, s32[1,64]{1,0:T(1,128)S(1)}, f32[1,64]{1,0:T(1,128)S(1)}, f32[16,128]{1,0:T(8,128)S(1)}) custom-call(f32[4,64,512]{2,1,0:T(8,128)} %t_hbm.1, f32[4,64,512]{2,1,0:T(8,128)} %b_hbm.1, s32[1,64]{1,0:T(1,128)} %bitcast.3, f32[1,64]{1,0:T(1,128)} %bitcast.4), custom_call_target="tpu_custom_call" | custom-call | tf_op jit(solution)/shard_map/pallas_call | solution.py:183
  1.4 2.5 %collective-permute-start.1 = (f32[16,128]{1,0:T(8,128)S(1)}, f32[16,128]{1,0:T(8,128)S(1)}, u32[]{:S(2)}, u32[]{:S(2)}) collective-permute-start(f32[16,128]{1,0:T(8,128)S(1)} %get-tuple-element.57.own_cells), channel_id=1, source_target_pairs={{0,3},{1,2},{2,1},{3,0},{4,7},{5,6},{6,5},{7,4},{8,11},{9,10},{10,... | collective-permute-start | bytes 24584 | tf_op jit(solution)/shard_map/ppermute | solution.py:1031
  3.9 0.7 %collective-permute-start = (f32[16,128]{1,0:T(8,128)S(1)}, f32[16,128]{1,0:T(8,128)S(1)}, u32[]{:S(2)}, u32[]{:S(2)}) collective-permute-start(f32[16,128]{1,0:T(8,128)S(1)} %get-tuple-element.57.own_cells), channel_id=1, source_target_pairs={{0,1},{1,0},{2,3},{3,2},{4,5},{5,4},{6,7},{7,6},{8,9},{9,8},{10,11... | collective-permute-start | bytes 24584 | tf_op jit(solution)/shard_map/ppermute | solution.py:439
  4.6 2.1 %shard_map.47 = (f32[4,4,64,128]{3,2,1,0:T(8,128)S(1)}, f32[4,4,64,128]{3,2,1,0:T(8,128)S(1)}, f32[8,16,8,128]{3,2,1,0:T(8,128)S(1)}, f32[8,16,8,128]{3,2,1,0:T(...) custom-call(s32[1,64]{1,0:T(1,128)S(1)} %get-tuple-element.53.loc, ...), custom_call_target="tpu_custom_call" | custom-call | flops 5242880 | bytes 3670016 | tf_op jit(solution)/shard_map/pallas_call | solution.py:337
  6.7 0.0 collective-permute-done.1.far
  6.7 0.0 collective-permute-done.near
  6.7 0.2 shard_map.48
  7.0 2.6 %collective-permute-start.4 = (f32[7,16,128]{2,1,0:T(8,128)S(1)}, f32[7,16,128]{2,1,0:T(8,128)S(1)}, u32[]{:S(2)}, u32[]{:S(2)}) collective-permute-start(f32[7,16,128]{2,1,0:T(8,128)S(1)} %get-tuple-element.66.after.refs_0_), channel_id=1, source_target_pairs={{0,12},{4,8},{8,4},{12,0},{16,28},{20,24},{24,20},{28,16},{1,13},{... | collective-permute-start | bytes 172040 | tf_op jit(solution)/shard_map/ppermute | solution.py:439
  9.5 0.4 %collective-permute-start.3 = (f32[7,16,128]{2,1,0:T(8,128)S(1)}, f32[7,16,128]{2,1,0:T(8,128)S(1)}, u32[]{:S(2)}, u32[]{:S(2)}) collective-permute-start(f32[7,16,128]{2,1,0:T(8,128)S(1)} %get-tuple-element.66.after.refs_0_), channel_id=1, source_target_pairs={{0,8},{4,12},{8,0},{12,4},{16,24},{20,28},{24,16},{28,20},{1,9},{5... | collective-permute-start | bytes 172040 | tf_op jit(solution)/shard_map/ppermute | solution.py:439
  10.0 0.5 %collective-permute-start.2 = (f32[7,16,128]{2,1,0:T(8,128)S(1)}, f32[7,16,128]{2,1,0:T(8,128)S(1)}, u32[]{:S(2)}, u32[]{:S(2)}) collective-permute-start(f32[7,16,128]{2,1,0:T(8,128)S(1)} %get-tuple-element.66.after.refs_0_), channel_id=1, source_target_pairs={{0,4},{4,0},{8,12},{12,8},{16,20},{20,16},{24,28},{28,24},{1,5},{5... | collective-permute-start | bytes 172040 | tf_op jit(solution)/shard_map/ppermute | solution.py:439
  10.5 0.8 %shard_map.49 = (f32[16,8,8,128]{3,2,1,0:T(8,128)S(1)}, f32[16,8,8,128]{3,2,1,0:T(8,128)S(1)}, f32[16,8,8,128]{3,2,1,0:T(8,128)S(1)}, f32[7,3,8,128]{3,2,1,0:T(8...) custom-call(f32[4,4,64,128]{3,2,1,0:T(8,128)S(1)} %get-tuple-element, ...), custom_call_target="tpu_custom_call" | custom-call | flops 2621440 | bytes 2097152 | tf_op jit(solution)/shard_map/pallas_call | solution.py:655
  11.4 0.2 shard_map.50
  11.5 0.9 %collective-permute-done.4.refs_3_ = f32[7,16,128]{2,1,0:T(8,128)S(1)} collective-permute-done((f32[7,16,128]{2,1,0:T(8,128)S(1)}, f32[7,16,128]{2,1,0:T(8,128)S(1)}, u32[]{:S(2)}, u32[]{:S(2)}) %collective-permute-start.4) | collective-permute-done | bytes 57376 | tf_op jit(solution)/shard_map/ppermute | solution.py:439
  12.4 1.3 %collective-permute-done.3.refs_2_ = f32[7,16,128]{2,1,0:T(8,128)S(1)} collective-permute-done((f32[7,16,128]{2,1,0:T(8,128)S(1)}, f32[7,16,128]{2,1,0:T(8,128)S(1)}, u32[]{:S(2)}, u32[]{:S(2)}) %collective-permute-start.3) | collective-permute-done | bytes 57376 | tf_op jit(solution)/shard_map/ppermute | solution.py:439
  13.7 0.4 %collective-permute-done.2.refs_1_ = f32[7,16,128]{2,1,0:T(8,128)S(1)} collective-permute-done((f32[7,16,128]{2,1,0:T(8,128)S(1)}, f32[7,16,128]{2,1,0:T(8,128)S(1)}, u32[]{:S(2)}, u32[]{:S(2)}) %collective-permute-start.2) | collective-permute-done | bytes 57376 | tf_op jit(solution)/shard_map/ppermute | solution.py:439
  14.2 0.1 shard_map.51
  14.2 2.7 %collective-permute-start.5 = (f32[3,16,128]{2,1,0:T(8,128)S(1)}, f32[3,16,128]{2,1,0:T(8,128)S(1)}, u32[]{:S(2)}, u32[]{:S(2)}) collective-permute-start(f32[3,16,128]{2,1,0:T(8,128)S(1)} %get-tuple-element.70.own), channel_id=1, source_target_pairs={{0,16},{4,20},{8,24},{12,28},{16,0},{20,4},{24,8},{28,12},{1,17},{... | collective-permute-start | bytes 73736 | tf_op jit(solution)/shard_map/ppermute | solution.py:439
  16.9 0.7 %shard_map.52 = (f32[4,128,256]{2,1,0:T(8,128)S(1)}, f32[4,128,256]{2,1,0:T(8,128)S(1)}, f32[4,128,256]{2,1,0:T(8,128)S(1)}, f32[4,128,256]{2,1,0:T(8,128)S(1)}, f32[2,2,128]{2,1,0:T(2,128)S(1)}) custom-call(f32[3,16,128]{2,1,0:T(8,128)S(1)} %get-tuple-element.71.refs_0_, f32[3,16,128]{2,1,0:T(8,128)S(1)} %get-tuple-element.72.refs_1_, ...), custom_call_target="tpu_custom_call" | custom-call | flops 1048576 | bytes 2097152 | tf_op jit(solution)/shard_map/pallas_call | solution.py:794
  17.5 1.5 %collective-permute-done.5.got = f32[3,16,128]{2,1,0:T(8,128)S(1)} collective-permute-done((f32[3,16,128]{2,1,0:T(8,128)S(1)}, f32[3,16,128]{2,1,0:T(8,128)S(1)}, u32[]{:S(2)}, u32[]{:S(2)}) %collective-permute-start.5) | collective-permute-done | bytes 24608 | tf_op jit(solution)/shard_map/ppermute | solution.py:439
  19.0 0.3 %shard_map.53 = (f32[4,128,256]{2,1,0:T(8,128)S(1)}, f32[7,2,128]{2,1,0:T(2,128)S(1)}) custom-call(f32[3,16,128]{2,1,0:T(8,128)S(1)} %get-tuple-element.70.own, f32[3,16,128]{2,1,0:T(8,128)S(1)} %collective-permute-done.5.got, f32[4,128,256]{2,1,0:T(8,128)S(1)} %get-tuple-element.80.to_first, f32[4,128,256]{2,1,0:T(8,128)S(1)} %get-tuple-element.81.to_last, ...), custom_call_target="tpu_custom_call" | custom-call | tf_op jit(solution)/shard_map/pallas_call | solution.py:830
  19.4 0.1 collective-permute-start.6
  19.5 0.3 %shard_map.54 = (f32[16,8,8,128]{3,2,1,0:T(8,128)S(1)}, f32[7,8,128]{2,1,0:T(8,128)S(1)}, f32[3,2,128]{2,1,0:T(2,128)S(1)}) custom-call(f32[4,128,256]{2,1,0:T(8,128)S(1)} %get-tuple-element.84.base, f32[4,128,256]{2,1,0:T(8,128)S(1)} %get-tuple-element.85.response, f32[4,128,256]{2,1,0:T(8,128)S(1)} %get-tuple-element.86.spread, ...), custom_call_target="tpu_custom_call" | custom-call | flops 1048576 | bytes 2097152 | tf_op jit(solution)/shard_map/pallas_call | solution.py:875
  19.7 0.9 %collective-permute-done.6.refs_1_ = f32[7,2,128]{2,1,0:T(2,128)S(1)} collective-permute-done((f32[7,2,128]{2,1,0:T(2,128)S(1)}, f32[7,2,128]{2,1,0:T(2,128)S(1)}, u32[]{:S(2)}, u32[]{:S(2)}) %collective-permute-start.6) | collective-permute-done | bytes 7200 | tf_op jit(solution)/shard_map/ppermute | solution.py:439
  20.6 0.7 %collective-permute-start.7 = (f32[3,2,128]{2,1,0:T(2,128)S(1)}, f32[3,2,128]{2,1,0:T(2,128)S(1)}, u32[]{:S(2)}, u32[]{:S(2)}) collective-permute-start(f32[3,2,128]{2,1,0:T(2,128)S(1)} %get-tuple-element.93.own), channel_id=1, source_target_pairs={{0,3},{1,2},{2,1},{3,0},{4,7},{5,6},{6,5},{7,4},{8,11},{9,10},{10,... | collective-permute-start | bytes 9224 | tf_op jit(solution)/shard_map/ppermute | solution.py:439
  21.3 0.8 %shard_map.56 = (f32[4,4,64,128]{3,2,1,0:T(8,128)S(1)}, f32[4,4,64,128]{3,2,1,0:T(8,128)S(1)}) custom-call(f32[3,2,128]{2,1,0:T(2,128)S(1)} %get-tuple-element.94.refs_0_, f32[16,8,8,128]{3,2,1,0:T(8,128)S(1)} %get-tuple-element.87.yw.refs_1_, f32[16,8,8,128]{3,2,1,0:T(8,128)S(1)} %get-tuple-element.92.refs_2_, ...), custom_call_target="tpu_custom_call" | custom-call | flops 1572864 | bytes 2621440 | tf_op jit(solution)/shard_map/pallas_call | solution.py:968
  22.2 1.6 %collective-permute-done.7.got = f32[3,2,128]{2,1,0:T(2,128)S(1)} collective-permute-done((f32[3,2,128]{2,1,0:T(2,128)S(1)}, f32[3,2,128]{2,1,0:T(2,128)S(1)}, u32[]{:S(2)}, u32[]{:S(2)}) %collective-permute-start.7) | collective-permute-done | bytes 3104 | tf_op jit(solution)/shard_map/ppermute | solution.py:439
  23.7 1.2 %shard_map.57 = f32[256,512]{1,0:T(8,128)} custom-call(f32[3,2,128]{2,1,0:T(2,128)S(1)} %get-tuple-element.93.own, f32[3,2,128]{2,1,0:T(2,128)S(1)} %collective-permute-done.7.got, f32[4,4,64,128]{3,2,1,0:T(8,128)S(1)} %get-tuple-element.99.base, f32[4,4,64,128]{3,2,1,0:T(8,128)S(1)} %get-tuple-element.100.response, ...), custom_call_target="tpu_custom_call" | custom-call | tf_op jit(solution)/shard_map/pallas_call | solution.py:1014
  (1 shorter events, 0.0 us)
Async XLA Ops:
  1.4 5.3 %collective-permute-start.1 = (f32[16,128]{1,0:T(8,128)S(1)}, f32[16,128]{1,0:T(8,128)S(1)}, u32[]{:S(2)}, u32[]{:S(2)}) collective-permute-start(f32[16,128]{1,0:T(8,128)S(1)} %get-tuple-element.57.own_cells), channel_id=1, source_target_pairs={{0,3},{1,2},{2,1},{3,0},{4,7},{5,6},{6,5},{7,4},{8,11},{9,10},{10,... | collective-permute-start | bytes 24584 | tf_op jit(solution)/shard_map/ppermute | solution.py:1031
  3.9 2.8 %collective-permute-start = (f32[16,128]{1,0:T(8,128)S(1)}, f32[16,128]{1,0:T(8,128)S(1)}, u32[]{:S(2)}, u32[]{:S(2)}) collective-permute-start(f32[16,128]{1,0:T(8,128)S(1)} %get-tuple-element.57.own_cells), channel_id=1, source_target_pairs={{0,1},{1,0},{2,3},{3,2},{4,5},{5,4},{6,7},{7,6},{8,9},{9,8},{10,11... | collective-permute-start | bytes 24584 | tf_op jit(solution)/shard_map/ppermute | solution.py:439
  7.0 5.4 %collective-permute-start.4 = (f32[7,16,128]{2,1,0:T(8,128)S(1)}, f32[7,16,128]{2,1,0:T(8,128)S(1)}, u32[]{:S(2)}, u32[]{:S(2)}) collective-permute-start(f32[7,16,128]{2,1,0:T(8,128)S(1)} %get-tuple-element.66.after.refs_0_), channel_id=1, source_target_pairs={{0,12},{4,8},{8,4},{12,0},{16,28},{20,24},{24,20},{28,16},{1,13},{... | collective-permute-start | bytes 172040 | tf_op jit(solution)/shard_map/ppermute | solution.py:439
  9.5 4.2 %collective-permute-start.3 = (f32[7,16,128]{2,1,0:T(8,128)S(1)}, f32[7,16,128]{2,1,0:T(8,128)S(1)}, u32[]{:S(2)}, u32[]{:S(2)}) collective-permute-start(f32[7,16,128]{2,1,0:T(8,128)S(1)} %get-tuple-element.66.after.refs_0_), channel_id=1, source_target_pairs={{0,8},{4,12},{8,0},{12,4},{16,24},{20,28},{24,16},{28,20},{1,9},{5... | collective-permute-start | bytes 172040 | tf_op jit(solution)/shard_map/ppermute | solution.py:439
  10.0 4.2 %collective-permute-start.2 = (f32[7,16,128]{2,1,0:T(8,128)S(1)}, f32[7,16,128]{2,1,0:T(8,128)S(1)}, u32[]{:S(2)}, u32[]{:S(2)}) collective-permute-start(f32[7,16,128]{2,1,0:T(8,128)S(1)} %get-tuple-element.66.after.refs_0_), channel_id=1, source_target_pairs={{0,4},{4,0},{8,12},{12,8},{16,20},{20,16},{24,28},{28,24},{1,5},{5... | collective-permute-start | bytes 172040 | tf_op jit(solution)/shard_map/ppermute | solution.py:439
  14.2 4.8 %collective-permute-start.5 = (f32[3,16,128]{2,1,0:T(8,128)S(1)}, f32[3,16,128]{2,1,0:T(8,128)S(1)}, u32[]{:S(2)}, u32[]{:S(2)}) collective-permute-start(f32[3,16,128]{2,1,0:T(8,128)S(1)} %get-tuple-element.70.own), channel_id=1, source_target_pairs={{0,16},{4,20},{8,24},{12,28},{16,0},{20,4},{24,8},{28,12},{1,17},{... | collective-permute-start | bytes 73736 | tf_op jit(solution)/shard_map/ppermute | solution.py:439
  19.4 1.2 %collective-permute-start.6 = (f32[7,2,128]{2,1,0:T(2,128)S(1)}, f32[7,2,128]{2,1,0:T(2,128)S(1)}, u32[]{:S(2)}, u32[]{:S(2)}) collective-permute-start(f32[7,2,128]{2,1,0:T(2,128)S(1)} %get-tuple-element.83.after.refs_0_), channel_id=1, source_target_pairs={{0,1},{1,0},{2,3},{3,2},{4,5},{5,4},{6,7},{7,6},{8,9},{9,8},{10,11... | collective-permute-start | bytes 21512 | tf_op jit(solution)/shard_map/ppermute | solution.py:439
  20.6 3.1 %collective-permute-start.7 = (f32[3,2,128]{2,1,0:T(2,128)S(1)}, f32[3,2,128]{2,1,0:T(2,128)S(1)}, u32[]{:S(2)}, u32[]{:S(2)}) collective-permute-start(f32[3,2,128]{2,1,0:T(2,128)S(1)} %get-tuple-element.93.own), channel_id=1, source_target_pairs={{0,3},{1,2},{2,1},{3,0},{4,7},{5,6},{6,5},{7,4},{8,11},{9,10},{10,... | collective-permute-start | bytes 9224 | tf_op jit(solution)/shard_map/ppermute | solution.py:439

commit v19 on v18

--- a/solution.py
+++ b/solution.py
@@ -13,6 +13,7 @@
 SUBLANES = 8
 F32 = jnp.float32
 MIB = 1024 * 1024
+ORDER = (2, 1, 3)
 ANYWHERE = pl.BlockSpec(memory_space=pl.ANY)
 IN_HBM = pl.BlockSpec(memory_space=pltpu.HBM)
 IN_VMEM = pl.BlockSpec(memory_space=pltpu.VMEM)
@@ -463,9 +464,14 @@
     return first, second
 
 
+def flips_of(width):
+    return ORDER if width == 2 else range(1, 1 << width)
+
+
 def join_kernel(axis, stage, width, last, *refs):
     count = 1 << width
-    blocks = [[refs[i][q] for q in range(7)] for i in range(count)]
+    at = {flip: 1 + n for n, flip in enumerate(flips_of(width))}
+    blocks = [[refs[at.get(i, 0)][q] for q in range(7)] for i in range(count)]
     send = refs[-1 - width]
     links = refs[-width:]
     for bit in range(width):
@@ -510,7 +516,7 @@
     links, stage = [], 0
     while stage < stages - 1:
         width = min(widest, stages - 1 - stage)
-        got = [swap(view, axis, flip << stage) for flip in range(1, 1 << width)]
+        got = [swap(view, axis, flip << stage) for flip in flips_of(width)]
         last = stage + width == stages - 1
         view, *ties = join_stage(view, got, axis, stage, width, last, meanwhile)
         links += ties

time: 25 us -> 25.2 us (level)
  transfers between devices with their start and end apart: 8 -> 8, of which waited for: 6 -> 6; matrix products, arithmetic and copies ran while one was open for 0% -> 0% of each run, Pallas kernels for 20% -> 19%
where the time goes in v19:
time: 25.2 us; the launch traced here: 25.1 us
  starting transfers between devices  10.1 us (40%)
  Pallas kernels  8.09 us (32%)
  waiting for transfers between devices  6.8 us (27%)
    ppermute x7, starting transfers between devices, swap(): return lax.ppermute(value, axis, [(i, i ^ flip) for i in range(count)])  7.66 us
    ppermute x7, waiting for transfers between devices, swap(): return lax.ppermute(value, axis, [(i, i ^ flip) for i in range(count)])  6.79 us
    ppermute x1, starting transfers between devices, per_device(): lax.ppermute(packed, 'gy', [(i, ((i + 1) % gy ^ 1) - 1 if i else gy - 1)...  2.47 us
    pallas_call x1, Pallas kernels, x_factor(): pl.pallas_call(functools.partial(x_factor_kernel, plate), in_specs=[IN_VM...  2.13 us
    pallas_call x1, Pallas kernels, load(): pl.pallas_call(load_kernel, in_specs=[IN_HBM] * 4, out_shape=[pltpu.VMEM(...  1.42 us
    pallas_call x1, Pallas kernels, finish(): pl.pallas_call(functools.partial(finish_kernel, stages_of('gy')), out_sha...  1.15 us
    pallas_call x1, Pallas kernels, y_factor(): pl.pallas_call(y_factor_kernel, in_specs=[IN_VMEM, ANYWHERE], out_shape=[...  0.84 us
    pallas_call x1, Pallas kernels, finish_prepare(): pl.pallas_call(functools.partial(finish_prepare_kernel, len(ties) + 1), o...  0.82 us
  transfers between devices with their start and end apart: 8, of which 6 were waited for; matrix products, arithmetic and copies ran while one was open for 0% of the time, Pallas kernels for 19%

profile of v19, /device:TPU:0, one launch (start us, length us, event | category | flops | bytes accessed | tf_op | source)
XLA Modules:
  0.0 25.1 jit_solution(13908339715478553337)
XLA Ops:
  0.0 1.4 %shard_map.46 = (f32[4,64,512]{2,1,0:T(8,128)S(1)}, f32[4,64,512]{2,1,0:T(8,128)S(1)}, s32[1,64]{1,0:T(1,128)S(1)}, f32[1,64]{1,0:T(1,128)S(1)}, f32[16,128]{1,0:T(8,128)S(1)}) custom-call(f32[4,64,512]{2,1,0:T(8,128)} %t_hbm.1, f32[4,64,512]{2,1,0:T(8,128)} %b_hbm.1, s32[1,64]{1,0:T(1,128)} %bitcast.3, f32[1,64]{1,0:T(1,128)} %bitcast.4), custom_call_target="tpu_custom_call" | custom-call | tf_op jit(solution)/shard_map/pallas_call | solution.py:184
  1.4 2.5 %collective-permute-start.1 = (f32[16,128]{1,0:T(8,128)S(1)}, f32[16,128]{1,0:T(8,128)S(1)}, u32[]{:S(2)}, u32[]{:S(2)}) collective-permute-start(f32[16,128]{1,0:T(8,128)S(1)} %get-tuple-element.57.own_cells), channel_id=1, source_target_pairs={{0,3},{1,2},{2,1},{3,0},{4,7},{5,6},{6,5},{7,4},{8,11},{9,10},{10,... | collective-permute-start | bytes 24584 | tf_op jit(solution)/shard_map/ppermute | solution.py:1037
  3.9 0.7 %collective-permute-start = (f32[16,128]{1,0:T(8,128)S(1)}, f32[16,128]{1,0:T(8,128)S(1)}, u32[]{:S(2)}, u32[]{:S(2)}) collective-permute-start(f32[16,128]{1,0:T(8,128)S(1)} %get-tuple-element.57.own_cells), channel_id=1, source_target_pairs={{0,1},{1,0},{2,3},{3,2},{4,5},{5,4},{6,7},{7,6},{8,9},{9,8},{10,11... | collective-permute-start | bytes 24584 | tf_op jit(solution)/shard_map/ppermute | solution.py:440
  4.6 2.1 %shard_map.47 = (f32[4,4,64,128]{3,2,1,0:T(8,128)S(1)}, f32[4,4,64,128]{3,2,1,0:T(8,128)S(1)}, f32[8,16,8,128]{3,2,1,0:T(8,128)S(1)}, f32[8,16,8,128]{3,2,1,0:T(...) custom-call(s32[1,64]{1,0:T(1,128)S(1)} %get-tuple-element.53.loc, ...), custom_call_target="tpu_custom_call" | custom-call | flops 5242880 | bytes 3670016 | tf_op jit(solution)/shard_map/pallas_call | solution.py:338
  6.7 0.0 collective-permute-done.1.far
  6.7 0.0 collective-permute-done.near
  6.7 0.2 shard_map.48
  7.0 2.6 %collective-permute-start.4 = (f32[7,16,128]{2,1,0:T(8,128)S(1)}, f32[7,16,128]{2,1,0:T(8,128)S(1)}, u32[]{:S(2)}, u32[]{:S(2)}) collective-permute-start(f32[7,16,128]{2,1,0:T(8,128)S(1)} %get-tuple-element.66.after.refs_0_), channel_id=1, source_target_pairs={{0,12},{4,8},{8,4},{12,0},{16,28},{20,24},{24,20},{28,16},{1,13},{... | collective-permute-start | bytes 172040 | tf_op jit(solution)/shard_map/ppermute | solution.py:440
  9.5 0.5 %collective-permute-start.3 = (f32[7,16,128]{2,1,0:T(8,128)S(1)}, f32[7,16,128]{2,1,0:T(8,128)S(1)}, u32[]{:S(2)}, u32[]{:S(2)}) collective-permute-start(f32[7,16,128]{2,1,0:T(8,128)S(1)} %get-tuple-element.66.after.refs_0_), channel_id=1, source_target_pairs={{0,4},{4,0},{8,12},{12,8},{16,20},{20,16},{24,28},{28,24},{1,5},{5... | collective-permute-start | bytes 172040 | tf_op jit(solution)/shard_map/ppermute | solution.py:440
  10.1 0.5 %collective-permute-start.2 = (f32[7,16,128]{2,1,0:T(8,128)S(1)}, f32[7,16,128]{2,1,0:T(8,128)S(1)}, u32[]{:S(2)}, u32[]{:S(2)}) collective-permute-start(f32[7,16,128]{2,1,0:T(8,128)S(1)} %get-tuple-element.66.after.refs_0_), channel_id=1, source_target_pairs={{0,8},{4,12},{8,0},{12,4},{16,24},{20,28},{24,16},{28,20},{1,9},{5... | collective-permute-start | bytes 172040 | tf_op jit(solution)/shard_map/ppermute | solution.py:440
  10.5 0.8 %shard_map.49 = (f32[16,8,8,128]{3,2,1,0:T(8,128)S(1)}, f32[16,8,8,128]{3,2,1,0:T(8,128)S(1)}, f32[16,8,8,128]{3,2,1,0:T(8,128)S(1)}, f32[7,3,8,128]{3,2,1,0:T(8...) custom-call(f32[4,4,64,128]{3,2,1,0:T(8,128)S(1)} %get-tuple-element, ...), custom_call_target="tpu_custom_call" | custom-call | flops 2621440 | bytes 2097152 | tf_op jit(solution)/shard_map/pallas_call | solution.py:661
  11.4 0.2 shard_map.50
  11.5 0.6 %collective-permute-done.4.refs_3_ = f32[7,16,128]{2,1,0:T(8,128)S(1)} collective-permute-done((f32[7,16,128]{2,1,0:T(8,128)S(1)}, f32[7,16,128]{2,1,0:T(8,128)S(1)}, u32[]{:S(2)}, u32[]{:S(2)}) %collective-permute-start.4) | collective-permute-done | bytes 57376 | tf_op jit(solution)/shard_map/ppermute | solution.py:440
  12.1 1.6 %collective-permute-done.3.refs_2_ = f32[7,16,128]{2,1,0:T(8,128)S(1)} collective-permute-done((f32[7,16,128]{2,1,0:T(8,128)S(1)}, f32[7,16,128]{2,1,0:T(8,128)S(1)}, u32[]{:S(2)}, u32[]{:S(2)}) %collective-permute-start.3) | collective-permute-done | bytes 57376 | tf_op jit(solution)/shard_map/ppermute | solution.py:440
  13.7 0.5 %collective-permute-done.2.refs_1_ = f32[7,16,128]{2,1,0:T(8,128)S(1)} collective-permute-done((f32[7,16,128]{2,1,0:T(8,128)S(1)}, f32[7,16,128]{2,1,0:T(8,128)S(1)}, u32[]{:S(2)}, u32[]{:S(2)}) %collective-permute-start.2) | collective-permute-done | bytes 57376 | tf_op jit(solution)/shard_map/ppermute | solution.py:440
  14.3 0.1 shard_map.51
  14.3 2.7 %collective-permute-start.5 = (f32[3,16,128]{2,1,0:T(8,128)S(1)}, f32[3,16,128]{2,1,0:T(8,128)S(1)}, u32[]{:S(2)}, u32[]{:S(2)}) collective-permute-start(f32[3,16,128]{2,1,0:T(8,128)S(1)} %get-tuple-element.70.own), channel_id=1, source_target_pairs={{0,16},{4,20},{8,24},{12,28},{16,0},{20,4},{24,8},{28,12},{1,17},{... | collective-permute-start | bytes 73736 | tf_op jit(solution)/shard_map/ppermute | solution.py:440
  17.0 0.7 %shard_map.52 = (f32[4,128,256]{2,1,0:T(8,128)S(1)}, f32[4,128,256]{2,1,0:T(8,128)S(1)}, f32[4,128,256]{2,1,0:T(8,128)S(1)}, f32[4,128,256]{2,1,0:T(8,128)S(1)}, f32[2,2,128]{2,1,0:T(2,128)S(1)}) custom-call(f32[3,16,128]{2,1,0:T(8,128)S(1)} %get-tuple-element.71.refs_0_, f32[3,16,128]{2,1,0:T(8,128)S(1)} %get-tuple-element.72.refs_1_, ...), custom_call_target="tpu_custom_call" | custom-call | flops 1048576 | bytes 2097152 | tf_op jit(solution)/shard_map/pallas_call | solution.py:800
  17.6 1.6 %collective-permute-done.5.got = f32[3,16,128]{2,1,0:T(8,128)S(1)} collective-permute-done((f32[3,16,128]{2,1,0:T(8,128)S(1)}, f32[3,16,128]{2,1,0:T(8,128)S(1)}, u32[]{:S(2)}, u32[]{:S(2)}) %collective-permute-start.5) | collective-permute-done | bytes 24608 | tf_op jit(solution)/shard_map/ppermute | solution.py:440
  19.3 0.4 %shard_map.53 = (f32[4,128,256]{2,1,0:T(8,128)S(1)}, f32[7,2,128]{2,1,0:T(2,128)S(1)}) custom-call(f32[3,16,128]{2,1,0:T(8,128)S(1)} %get-tuple-element.70.own, f32[3,16,128]{2,1,0:T(8,128)S(1)} %collective-permute-done.5.got, f32[4,128,256]{2,1,0:T(8,128)S(1)} %get-tuple-element.80.to_first, f32[4,128,256]{2,1,0:T(8,128)S(1)} %get-tuple-element.81.to_last, ...), custom_call_target="tpu_custom_call" | custom-call | tf_op jit(solution)/shard_map/pallas_call | solution.py:836
  19.6 0.1 collective-permute-start.6
  19.7 0.3 %shard_map.54 = (f32[16,8,8,128]{3,2,1,0:T(8,128)S(1)}, f32[7,8,128]{2,1,0:T(8,128)S(1)}, f32[3,2,128]{2,1,0:T(2,128)S(1)}) custom-call(f32[4,128,256]{2,1,0:T(8,128)S(1)} %get-tuple-element.84.base, f32[4,128,256]{2,1,0:T(8,128)S(1)} %get-tuple-element.85.response, f32[4,128,256]{2,1,0:T(8,128)S(1)} %get-tuple-element.86.spread, ...), custom_call_target="tpu_custom_call" | custom-call | flops 1048576 | bytes 2097152 | tf_op jit(solution)/shard_map/pallas_call | solution.py:881
  19.9 0.9 %collective-permute-done.6.refs_1_ = f32[7,2,128]{2,1,0:T(2,128)S(1)} collective-permute-done((f32[7,2,128]{2,1,0:T(2,128)S(1)}, f32[7,2,128]{2,1,0:T(2,128)S(1)}, u32[]{:S(2)}, u32[]{:S(2)}) %collective-permute-start.6) | collective-permute-done | bytes 7200 | tf_op jit(solution)/shard_map/ppermute | solution.py:440
  20.9 0.7 %collective-permute-start.7 = (f32[3,2,128]{2,1,0:T(2,128)S(1)}, f32[3,2,128]{2,1,0:T(2,128)S(1)}, u32[]{:S(2)}, u32[]{:S(2)}) collective-permute-start(f32[3,2,128]{2,1,0:T(2,128)S(1)} %get-tuple-element.93.own), channel_id=1, source_target_pairs={{0,3},{1,2},{2,1},{3,0},{4,7},{5,6},{6,5},{7,4},{8,11},{9,10},{10,... | collective-permute-start | bytes 9224 | tf_op jit(solution)/shard_map/ppermute | solution.py:440
  21.6 0.8 %shard_map.56 = (f32[4,4,64,128]{3,2,1,0:T(8,128)S(1)}, f32[4,4,64,128]{3,2,1,0:T(8,128)S(1)}) custom-call(f32[3,2,128]{2,1,0:T(2,128)S(1)} %get-tuple-element.94.refs_0_, f32[16,8,8,128]{3,2,1,0:T(8,128)S(1)} %get-tuple-element.87.yw.refs_1_, f32[16,8,8,128]{3,2,1,0:T(8,128)S(1)} %get-tuple-element.92.refs_2_, ...), custom_call_target="tpu_custom_call" | custom-call | flops 1572864 | bytes 2621440 | tf_op jit(solution)/shard_map/pallas_call | solution.py:974
  22.4 1.6 %collective-permute-done.7.got = f32[3,2,128]{2,1,0:T(2,128)S(1)} collective-permute-done((f32[3,2,128]{2,1,0:T(2,128)S(1)}, f32[3,2,128]{2,1,0:T(2,128)S(1)}, u32[]{:S(2)}, u32[]{:S(2)}) %collective-permute-start.7) | collective-permute-done | bytes 3104 | tf_op jit(solution)/shard_map/ppermute | solution.py:440
  24.0 1.2 %shard_map.57 = f32[256,512]{1,0:T(8,128)} custom-call(f32[3,2,128]{2,1,0:T(2,128)S(1)} %get-tuple-element.93.own, f32[3,2,128]{2,1,0:T(2,128)S(1)} %collective-permute-done.7.got, f32[4,4,64,128]{3,2,1,0:T(8,128)S(1)} %get-tuple-element.99.base, f32[4,4,64,128]{3,2,1,0:T(8,128)S(1)} %get-tuple-element.100.response, ...), custom_call_target="tpu_custom_call" | custom-call | tf_op jit(solution)/shard_map/pallas_call | solution.py:1020
  (1 shorter events, 0.0 us)
Async XLA Ops:
  1.4 5.3 %collective-permute-start.1 = (f32[16,128]{1,0:T(8,128)S(1)}, f32[16,128]{1,0:T(8,128)S(1)}, u32[]{:S(2)}, u32[]{:S(2)}) collective-permute-start(f32[16,128]{1,0:T(8,128)S(1)} %get-tuple-element.57.own_cells), channel_id=1, source_target_pairs={{0,3},{1,2},{2,1},{3,0},{4,7},{5,6},{6,5},{7,4},{8,11},{9,10},{10,... | collective-permute-start | bytes 24584 | tf_op jit(solution)/shard_map/ppermute | solution.py:1037
  3.9 2.8 %collective-permute-start = (f32[16,128]{1,0:T(8,128)S(1)}, f32[16,128]{1,0:T(8,128)S(1)}, u32[]{:S(2)}, u32[]{:S(2)}) collective-permute-start(f32[16,128]{1,0:T(8,128)S(1)} %get-tuple-element.57.own_cells), channel_id=1, source_target_pairs={{0,1},{1,0},{2,3},{3,2},{4,5},{5,4},{6,7},{7,6},{8,9},{9,8},{10,11... | collective-permute-start | bytes 24584 | tf_op jit(solution)/shard_map/ppermute | solution.py:440
  7.0 5.2 %collective-permute-start.4 = (f32[7,16,128]{2,1,0:T(8,128)S(1)}, f32[7,16,128]{2,1,0:T(8,128)S(1)}, u32[]{:S(2)}, u32[]{:S(2)}) collective-permute-start(f32[7,16,128]{2,1,0:T(8,128)S(1)} %get-tuple-element.66.after.refs_0_), channel_id=1, source_target_pairs={{0,12},{4,8},{8,4},{12,0},{16,28},{20,24},{24,20},{28,16},{1,13},{... | collective-permute-start | bytes 172040 | tf_op jit(solution)/shard_map/ppermute | solution.py:440
  9.5 4.2 %collective-permute-start.3 = (f32[7,16,128]{2,1,0:T(8,128)S(1)}, f32[7,16,128]{2,1,0:T(8,128)S(1)}, u32[]{:S(2)}, u32[]{:S(2)}) collective-permute-start(f32[7,16,128]{2,1,0:T(8,128)S(1)} %get-tuple-element.66.after.refs_0_), channel_id=1, source_target_pairs={{0,4},{4,0},{8,12},{12,8},{16,20},{20,16},{24,28},{28,24},{1,5},{5... | collective-permute-start | bytes 172040 | tf_op jit(solution)/shard_map/ppermute | solution.py:440
  10.1 4.2 %collective-permute-start.2 = (f32[7,16,128]{2,1,0:T(8,128)S(1)}, f32[7,16,128]{2,1,0:T(8,128)S(1)}, u32[]{:S(2)}, u32[]{:S(2)}) collective-permute-start(f32[7,16,128]{2,1,0:T(8,128)S(1)} %get-tuple-element.66.after.refs_0_), channel_id=1, source_target_pairs={{0,8},{4,12},{8,0},{12,4},{16,24},{20,28},{24,16},{28,20},{1,9},{5... | collective-permute-start | bytes 172040 | tf_op jit(solution)/shard_map/ppermute | solution.py:440
  14.3 4.9 %collective-permute-start.5 = (f32[3,16,128]{2,1,0:T(8,128)S(1)}, f32[3,16,128]{2,1,0:T(8,128)S(1)}, u32[]{:S(2)}, u32[]{:S(2)}) collective-permute-start(f32[3,16,128]{2,1,0:T(8,128)S(1)} %get-tuple-element.70.own), channel_id=1, source_target_pairs={{0,16},{4,20},{8,24},{12,28},{16,0},{20,4},{24,8},{28,12},{1,17},{... | collective-permute-start | bytes 73736 | tf_op jit(solution)/shard_map/ppermute | solution.py:440
  19.6 1.2 %collective-permute-start.6 = (f32[7,2,128]{2,1,0:T(2,128)S(1)}, f32[7,2,128]{2,1,0:T(2,128)S(1)}, u32[]{:S(2)}, u32[]{:S(2)}) collective-permute-start(f32[7,2,128]{2,1,0:T(2,128)S(1)} %get-tuple-element.83.after.refs_0_), channel_id=1, source_target_pairs={{0,1},{1,0},{2,3},{3,2},{4,5},{5,4},{6,7},{7,6},{8,9},{9,8},{10,11... | collective-permute-start | bytes 21512 | tf_op jit(solution)/shard_map/ppermute | solution.py:440
  20.9 3.1 %collective-permute-start.7 = (f32[3,2,128]{2,1,0:T(2,128)S(1)}, f32[3,2,128]{2,1,0:T(2,128)S(1)}, u32[]{:S(2)}, u32[]{:S(2)}) collective-permute-start(f32[3,2,128]{2,1,0:T(2,128)S(1)} %get-tuple-element.93.own), channel_id=1, source_target_pairs={{0,3},{1,2},{2,1},{3,0},{4,7},{5,6},{6,5},{7,4},{8,11},{9,10},{10,... | collective-permute-start | bytes 9224 | tf_op jit(solution)/shard_map/ppermute | solution.py:440

commit v20 on v18

--- a/solution.py
+++ b/solution.py
@@ -13,6 +13,7 @@
 SUBLANES = 8
 F32 = jnp.float32
 MIB = 1024 * 1024
+OUT_COPIES = 4
 ANYWHERE = pl.BlockSpec(memory_space=pl.ANY)
 IN_HBM = pl.BlockSpec(memory_space=pltpu.HBM)
 IN_VMEM = pl.BlockSpec(memory_space=pltpu.VMEM)
@@ -144,14 +145,12 @@
 
 def load_kernel(t_hbm, b_hbm, loc_hbm, energy_hbm, t_out, b_out, loc, energy, packed, cells, sems):
     sheets, rows, columns = t_hbm.shape
-    parts = [(0, LANES), (columns - LANES, LANES), (LANES, columns - 2 * LANES)]
+    halves = 2
     copies = []
-    for n, (start, size) in enumerate(parts):
-        part = pl.ds(start, size)
+    for n in range(halves):
+        part = pl.ds(n * sheets // halves, sheets // halves)
         for i, (src, dst) in enumerate(((t_hbm, t_out), (b_hbm, b_out))):
-            copies.append(
-                pltpu.make_async_copy(src.at[:, :, part], dst.at[:, :, part], sems.at[i, n])
-            )
+            copies.append(pltpu.make_async_copy(src.at[part], dst.at[part], sems.at[i, n]))
     copies.append(pltpu.make_async_copy(loc_hbm, loc, sems.at[2, 0]))
     copies.append(pltpu.make_async_copy(energy_hbm, energy, sems.at[2, 1]))
     for copy in copies:
@@ -159,20 +158,21 @@
     lane = lax.broadcasted_iota(jnp.int32, (rows, LANES), 1)
     edge_t = jnp.zeros((rows, LANES), F32)
     edge_c = edge_t
-    for side, source in enumerate((0, LANES - 1)):
-        for copy in copies[2 * side : 2 * side + 2]:
+    for n in range(halves):
+        for copy in copies[2 * n : 2 * n + 2]:
             copy.wait()
-        part = slice(parts[side][0], parts[side][0] + LANES)
-        for z in range(sheets):
-            t = t_out[z, :, part]
-            c = half_conduct(b_out[z, :, part], t)
-            place = lane == sheets * side + z
-            edge_t = jnp.where(place, t[:, source : source + 1], edge_t)
-            edge_c = jnp.where(place, c[:, source : source + 1], edge_c)
+        for z in range(n * sheets // halves, (n + 1) * sheets // halves):
+            for side, part in enumerate((slice(0, LANES), slice(columns - LANES, columns))):
+                source = 0 if side == 0 else LANES - 1
+                t = t_out[z, :, part]
+                c = half_conduct(b_out[z, :, part], t)
+                place = lane == sheets * side + z
+                edge_t = jnp.where(place, t[:, source : source + 1], edge_t)
+                edge_c = jnp.where(place, c[:, source : source + 1], edge_c)
     cells[0], cells[1] = edge_t, edge_c
     for i in range(2):
         packed[i * SUBLANES : (i + 1) * SUBLANES, :] = fold(cells.at[i], 2 * sheets)
-    for copy in copies[4:]:
+    for copy in copies[2 * halves :]:
         copy.wait()
 
 
@@ -893,12 +893,12 @@
     sheets = zi.shape[0]
     rhs, kept = None, []
     for z in range(sheets):
-        rhs = field(z) if z == 0 else field(z) + zw[z - 1, at] * rhs
-        kept.append(rhs * zi[z, at])
+        rhs = field(z) if z == 0 else field(z) + zw[(z - 1, *at)] * rhs
+        kept.append(rhs * zi[(z, *at)])
     value = kept[-1]
     keep(sheets - 1, value)
     for z in range(sheets - 2, -1, -1):
-        value = zw[z, at] * value + kept[z]
+        value = zw[(z, *at)] * value + kept[z]
         keep(z, value)
 
 
@@ -952,7 +952,7 @@
         def keep(z, value):
             base[y, z] = t_ref[z, :, part] + value
 
-        z_solve(zw, zi, field, y, keep)
+        z_solve(zw, zi, field, (y,), keep)
         for m in range(pairs):
             units = turned(to_x[...], u_s[1, m, part, :])
             for i in range(each):
@@ -982,26 +982,26 @@
     chunks, sheets, rows, _ = base.shape
     each = LANES // rows
     pairs = sheets // each
-    copies, _, wide = o_s.shape
-
     flux = top_flux("gy", stages, own, got)
     spread = [
         turned(to_x[...], flux[m : m + 1, :], LANES) for m in range(pairs)
     ]
     started = []
-    for n in range(copies):
-        for y in range(n * chunks // copies, (n + 1) * chunks // copies):
-            part = part_of(y - n * chunks // copies)
+    block = rows // OUT_COPIES
+    for n in range(OUT_COPIES):
+        strip = slice(n * block, (n + 1) * block)
+        for y in range(chunks):
 
             def field(z):
-                at = z % each * rows
-                return response[y, z] * spread[z // each][at : at + rows, :]
+                at = z % each * rows + strip.start
+                return response[y, z, strip, :] * spread[z // each][at : at + block, :]
 
             def keep(z, value):
-                o_s[n, z * rows : (z + 1) * rows, part] = base[y, z] + value
-
-            z_solve(zw, zi, field, y, keep)
-        copy = pltpu.make_async_copy(o_s.at[n], out.at[:, pl.ds(n * wide, wide)], sems.at[n])
+                o_s[z, strip, part_of(y)] = base[y, z, strip, :] + value
+
+            z_solve(zw, zi, field, (y, strip), keep)
+        at = pl.ds(strip.start, block)
+        copy = pltpu.make_async_copy(o_s.at[:, at, :], out.at[:, at, :], sems.at[n])
         copy.start()
         started.append(copy)
     for copy in started:
@@ -1010,17 +1010,14 @@
 
 def finish(own, got, base, response, zw, zi, to_x):
     chunks, sheets, rows, _ = base.shape
-    copies = chunks
+    shape = (sheets, rows, chunks * LANES)
     return pl.pallas_call(
         functools.partial(finish_kernel, stages_of("gy")),
-        out_shape=shape_of(sheets * rows, chunks * LANES),
+        out_shape=shape_of(*shape),
         out_specs=ANYWHERE,
-        scratch_shapes=[
-            pltpu.VMEM((copies, sheets * rows, chunks * LANES // copies), F32),
-            pltpu.SemaphoreType.DMA((copies,)),
-        ],
+        scratch_shapes=[pltpu.VMEM(shape, F32), pltpu.SemaphoreType.DMA((OUT_COPIES,))],
         compiler_params=params(),
-    )(own, got, base, response, zw, zi, to_x).reshape(sheets, rows, chunks * LANES)
+    )(own, got, base, response, zw, zi, to_x)
 
 
 def per_device(temperature, base, locations, energy):

time: 25 us -> 25 us (level)
  no operation moved by 1% of the time
where the time goes in v20:
time: 25 us; the launch traced here: 24.9 us
  starting transfers between devices  10.1 us (40%)
  Pallas kernels  8.09 us (32%)
  waiting for transfers between devices  6.57 us (26%)
    ppermute x7, starting transfers between devices, swap(): return lax.ppermute(value, axis, [(i, i ^ flip) for i in range(count)])  7.66 us
    ppermute x7, waiting for transfers between devices, swap(): return lax.ppermute(value, axis, [(i, i ^ flip) for i in range(count)])  6.56 us
    ppermute x1, starting transfers between devices, per_device(): lax.ppermute(packed, 'gy', [(i, ((i + 1) % gy ^ 1) - 1 if i else gy - 1)...  2.47 us
    pallas_call x1, Pallas kernels, x_factor(): pl.pallas_call(functools.partial(x_factor_kernel, plate), in_specs=[IN_VM...  2.13 us
    pallas_call x1, Pallas kernels, load(): pl.pallas_call(load_kernel, in_specs=[IN_HBM] * 4, out_shape=[pltpu.VMEM(...  1.5 us
    pallas_call x1, Pallas kernels, finish(): pl.pallas_call(functools.partial(finish_kernel, stages_of('gy')), out_sha...  1.07 us
    pallas_call x1, Pallas kernels, y_factor(): pl.pallas_call(y_factor_kernel, in_specs=[IN_VMEM, ANYWHERE], out_shape=[...  0.84 us
    pallas_call x1, Pallas kernels, finish_prepare(): pl.pallas_call(functools.partial(finish_prepare_kernel, len(ties) + 1), o...  0.82 us
  transfers between devices with their start and end apart: 8, of which 6 were waited for; matrix products, arithmetic and copies ran while one was open for 0% of the time, Pallas kernels for 20%

profile of v20, /device:TPU:0, one launch (start us, length us, event | category | flops | bytes accessed | tf_op | source)
XLA Modules:
  0.0 24.9 jit_solution(11335209760183486589)
XLA Ops:
  0.0 1.5 %shard_map.46 = (f32[4,64,512]{2,1,0:T(8,128)S(1)}, f32[4,64,512]{2,1,0:T(8,128)S(1)}, s32[1,64]{1,0:T(1,128)S(1)}, f32[1,64]{1,0:T(1,128)S(1)}, f32[16,128]{1,0:T(8,128)S(1)}) custom-call(f32[4,64,512]{2,1,0:T(8,128)} %t_hbm.1, f32[4,64,512]{2,1,0:T(8,128)} %b_hbm.1, s32[1,64]{1,0:T(1,128)} %bitcast.2, f32[1,64]{1,0:T(1,128)} %bitcast.3), custom_call_target="tpu_custom_call" | custom-call | tf_op jit(solution)/shard_map/pallas_call | solution.py:183
  1.5 2.5 %collective-permute-start.1 = (f32[16,128]{1,0:T(8,128)S(1)}, f32[16,128]{1,0:T(8,128)S(1)}, u32[]{:S(2)}, u32[]{:S(2)}) collective-permute-start(f32[16,128]{1,0:T(8,128)S(1)} %get-tuple-element.57.own_cells), channel_id=1, source_target_pairs={{0,3},{1,2},{2,1},{3,0},{4,7},{5,6},{6,5},{7,4},{8,11},{9,10},{10,... | collective-permute-start | bytes 24584 | tf_op jit(solution)/shard_map/ppermute | solution.py:1028
  4.0 0.7 %collective-permute-start = (f32[16,128]{1,0:T(8,128)S(1)}, f32[16,128]{1,0:T(8,128)S(1)}, u32[]{:S(2)}, u32[]{:S(2)}) collective-permute-start(f32[16,128]{1,0:T(8,128)S(1)} %get-tuple-element.57.own_cells), channel_id=1, source_target_pairs={{0,1},{1,0},{2,3},{3,2},{4,5},{5,4},{6,7},{7,6},{8,9},{9,8},{10,11... | collective-permute-start | bytes 24584 | tf_op jit(solution)/shard_map/ppermute | solution.py:439
  4.7 2.1 %shard_map.47 = (f32[4,4,64,128]{3,2,1,0:T(8,128)S(1)}, f32[4,4,64,128]{3,2,1,0:T(8,128)S(1)}, f32[8,16,8,128]{3,2,1,0:T(8,128)S(1)}, f32[8,16,8,128]{3,2,1,0:T(...) custom-call(s32[1,64]{1,0:T(1,128)S(1)} %get-tuple-element.53.loc, ...), custom_call_target="tpu_custom_call" | custom-call | flops 5242880 | bytes 3670016 | tf_op jit(solution)/shard_map/pallas_call | solution.py:337
  6.8 0.0 collective-permute-done.1.far
  6.8 0.0 collective-permute-done.near
  6.8 0.2 shard_map.48
  7.1 2.6 %collective-permute-start.4 = (f32[7,16,128]{2,1,0:T(8,128)S(1)}, f32[7,16,128]{2,1,0:T(8,128)S(1)}, u32[]{:S(2)}, u32[]{:S(2)}) collective-permute-start(f32[7,16,128]{2,1,0:T(8,128)S(1)} %get-tuple-element.66.after.refs_0_), channel_id=1, source_target_pairs={{0,12},{4,8},{8,4},{12,0},{16,28},{20,24},{24,20},{28,16},{1,13},{... | collective-permute-start | bytes 172040 | tf_op jit(solution)/shard_map/ppermute | solution.py:439
  9.6 0.5 %collective-permute-start.3 = (f32[7,16,128]{2,1,0:T(8,128)S(1)}, f32[7,16,128]{2,1,0:T(8,128)S(1)}, u32[]{:S(2)}, u32[]{:S(2)}) collective-permute-start(f32[7,16,128]{2,1,0:T(8,128)S(1)} %get-tuple-element.66.after.refs_0_), channel_id=1, source_target_pairs={{0,8},{4,12},{8,0},{12,4},{16,24},{20,28},{24,16},{28,20},{1,9},{5... | collective-permute-start | bytes 172040 | tf_op jit(solution)/shard_map/ppermute | solution.py:439
  10.1 0.5 %collective-permute-start.2 = (f32[7,16,128]{2,1,0:T(8,128)S(1)}, f32[7,16,128]{2,1,0:T(8,128)S(1)}, u32[]{:S(2)}, u32[]{:S(2)}) collective-permute-start(f32[7,16,128]{2,1,0:T(8,128)S(1)} %get-tuple-element.66.after.refs_0_), channel_id=1, source_target_pairs={{0,4},{4,0},{8,12},{12,8},{16,20},{20,16},{24,28},{28,24},{1,5},{5... | collective-permute-start | bytes 172040 | tf_op jit(solution)/shard_map/ppermute | solution.py:439
  10.6 0.8 %shard_map.49 = (f32[16,8,8,128]{3,2,1,0:T(8,128)S(1)}, f32[16,8,8,128]{3,2,1,0:T(8,128)S(1)}, f32[16,8,8,128]{3,2,1,0:T(8,128)S(1)}, f32[7,3,8,128]{3,2,1,0:T(8...) custom-call(f32[4,4,64,128]{3,2,1,0:T(8,128)S(1)} %get-tuple-element, ...), custom_call_target="tpu_custom_call" | custom-call | flops 2621440 | bytes 2097152 | tf_op jit(solution)/shard_map/pallas_call | solution.py:655
  11.5 0.2 shard_map.50
  11.6 0.9 %collective-permute-done.4.refs_3_ = f32[7,16,128]{2,1,0:T(8,128)S(1)} collective-permute-done((f32[7,16,128]{2,1,0:T(8,128)S(1)}, f32[7,16,128]{2,1,0:T(8,128)S(1)}, u32[]{:S(2)}, u32[]{:S(2)}) %collective-permute-start.4) | collective-permute-done | bytes 57376 | tf_op jit(solution)/shard_map/ppermute | solution.py:439
  12.5 1.3 %collective-permute-done.3.refs_2_ = f32[7,16,128]{2,1,0:T(8,128)S(1)} collective-permute-done((f32[7,16,128]{2,1,0:T(8,128)S(1)}, f32[7,16,128]{2,1,0:T(8,128)S(1)}, u32[]{:S(2)}, u32[]{:S(2)}) %collective-permute-start.3) | collective-permute-done | bytes 57376 | tf_op jit(solution)/shard_map/ppermute | solution.py:439
  13.8 0.5 %collective-permute-done.2.refs_1_ = f32[7,16,128]{2,1,0:T(8,128)S(1)} collective-permute-done((f32[7,16,128]{2,1,0:T(8,128)S(1)}, f32[7,16,128]{2,1,0:T(8,128)S(1)}, u32[]{:S(2)}, u32[]{:S(2)}) %collective-permute-start.2) | collective-permute-done | bytes 57376 | tf_op jit(solution)/shard_map/ppermute | solution.py:439
  14.3 0.1 shard_map.51
  14.3 2.7 %collective-permute-start.5 = (f32[3,16,128]{2,1,0:T(8,128)S(1)}, f32[3,16,128]{2,1,0:T(8,128)S(1)}, u32[]{:S(2)}, u32[]{:S(2)}) collective-permute-start(f32[3,16,128]{2,1,0:T(8,128)S(1)} %get-tuple-element.70.own), channel_id=1, source_target_pairs={{0,16},{4,20},{8,24},{12,28},{16,0},{20,4},{24,8},{28,12},{1,17},{... | collective-permute-start | bytes 73736 | tf_op jit(solution)/shard_map/ppermute | solution.py:439
  17.0 0.7 %shard_map.52 = (f32[4,128,256]{2,1,0:T(8,128)S(1)}, f32[4,128,256]{2,1,0:T(8,128)S(1)}, f32[4,128,256]{2,1,0:T(8,128)S(1)}, f32[4,128,256]{2,1,0:T(8,128)S(1)}, f32[2,2,128]{2,1,0:T(2,128)S(1)}) custom-call(f32[3,16,128]{2,1,0:T(8,128)S(1)} %get-tuple-element.71.refs_0_, f32[3,16,128]{2,1,0:T(8,128)S(1)} %get-tuple-element.72.refs_1_, ...), custom_call_target="tpu_custom_call" | custom-call | flops 1048576 | bytes 2097152 | tf_op jit(solution)/shard_map/pallas_call | solution.py:794
  17.6 1.5 %collective-permute-done.5.got = f32[3,16,128]{2,1,0:T(8,128)S(1)} collective-permute-done((f32[3,16,128]{2,1,0:T(8,128)S(1)}, f32[3,16,128]{2,1,0:T(8,128)S(1)}, u32[]{:S(2)}, u32[]{:S(2)}) %collective-permute-start.5) | collective-permute-done | bytes 24608 | tf_op jit(solution)/shard_map/ppermute | solution.py:439
  19.1 0.4 %shard_map.53 = (f32[4,128,256]{2,1,0:T(8,128)S(1)}, f32[7,2,128]{2,1,0:T(2,128)S(1)}) custom-call(f32[3,16,128]{2,1,0:T(8,128)S(1)} %get-tuple-element.70.own, f32[3,16,128]{2,1,0:T(8,128)S(1)} %collective-permute-done.5.got, f32[4,128,256]{2,1,0:T(8,128)S(1)} %get-tuple-element.80.to_first, f32[4,128,256]{2,1,0:T(8,128)S(1)} %get-tuple-element.81.to_last, ...), custom_call_target="tpu_custom_call" | custom-call | tf_op jit(solution)/shard_map/pallas_call | solution.py:830
  19.5 0.1 collective-permute-start.6
  19.5 0.3 %shard_map.54 = (f32[16,8,8,128]{3,2,1,0:T(8,128)S(1)}, f32[7,8,128]{2,1,0:T(8,128)S(1)}, f32[3,2,128]{2,1,0:T(2,128)S(1)}) custom-call(f32[4,128,256]{2,1,0:T(8,128)S(1)} %get-tuple-element.84.base, f32[4,128,256]{2,1,0:T(8,128)S(1)} %get-tuple-element.85.response, f32[4,128,256]{2,1,0:T(8,128)S(1)} %get-tuple-element.86.spread, ...), custom_call_target="tpu_custom_call" | custom-call | flops 1048576 | bytes 2097152 | tf_op jit(solution)/shard_map/pallas_call | solution.py:875
  19.8 0.9 %collective-permute-done.6.refs_1_ = f32[7,2,128]{2,1,0:T(2,128)S(1)} collective-permute-done((f32[7,2,128]{2,1,0:T(2,128)S(1)}, f32[7,2,128]{2,1,0:T(2,128)S(1)}, u32[]{:S(2)}, u32[]{:S(2)}) %collective-permute-start.6) | collective-permute-done | bytes 7200 | tf_op jit(solution)/shard_map/ppermute | solution.py:439
  20.7 0.7 %collective-permute-start.7 = (f32[3,2,128]{2,1,0:T(2,128)S(1)}, f32[3,2,128]{2,1,0:T(2,128)S(1)}, u32[]{:S(2)}, u32[]{:S(2)}) collective-permute-start(f32[3,2,128]{2,1,0:T(2,128)S(1)} %get-tuple-element.93.own), channel_id=1, source_target_pairs={{0,3},{1,2},{2,1},{3,0},{4,7},{5,6},{6,5},{7,4},{8,11},{9,10},{10,... | collective-permute-start | bytes 9224 | tf_op jit(solution)/shard_map/ppermute | solution.py:439
  21.4 0.8 %shard_map.56 = (f32[4,4,64,128]{3,2,1,0:T(8,128)S(1)}, f32[4,4,64,128]{3,2,1,0:T(8,128)S(1)}) custom-call(f32[3,2,128]{2,1,0:T(2,128)S(1)} %get-tuple-element.94.refs_0_, f32[16,8,8,128]{3,2,1,0:T(8,128)S(1)} %get-tuple-element.87.yw.refs_1_, f32[16,8,8,128]{3,2,1,0:T(8,128)S(1)} %get-tuple-element.92.refs_2_, ...), custom_call_target="tpu_custom_call" | custom-call | flops 1572864 | bytes 2621440 | tf_op jit(solution)/shard_map/pallas_call | solution.py:968
  22.2 1.6 %collective-permute-done.7.got = f32[3,2,128]{2,1,0:T(2,128)S(1)} collective-permute-done((f32[3,2,128]{2,1,0:T(2,128)S(1)}, f32[3,2,128]{2,1,0:T(2,128)S(1)}, u32[]{:S(2)}, u32[]{:S(2)}) %collective-permute-start.7) | collective-permute-done | bytes 3104 | tf_op jit(solution)/shard_map/ppermute | solution.py:439
  23.8 1.1 %shard_map.57 = f32[4,64,512]{2,1,0:T(8,128)} custom-call(f32[3,2,128]{2,1,0:T(2,128)S(1)} %get-tuple-element.93.own, f32[3,2,128]{2,1,0:T(2,128)S(1)} %collective-permute-done.7.got, f32[4,4,64,128]{3,2,1,0:T(8,128)S(1)} %get-tuple-element.99.base, f32[4,4,64,128]{3,2,1,0:T(8,128)S(1)} %get-tuple-element.100.response, ...), custom_call_target="tpu_custom_call" | custom-call | tf_op jit(solution)/shard_map/pallas_call | solution.py:1014
  (1 shorter events, 0.0 us)
Async XLA Ops:
  1.5 5.3 %collective-permute-start.1 = (f32[16,128]{1,0:T(8,128)S(1)}, f32[16,128]{1,0:T(8,128)S(1)}, u32[]{:S(2)}, u32[]{:S(2)}) collective-permute-start(f32[16,128]{1,0:T(8,128)S(1)} %get-tuple-element.57.own_cells), channel_id=1, source_target_pairs={{0,3},{1,2},{2,1},{3,0},{4,7},{5,6},{6,5},{7,4},{8,11},{9,10},{10,... | collective-permute-start | bytes 24584 | tf_op jit(solution)/shard_map/ppermute | solution.py:1028
  4.0 2.8 %collective-permute-start = (f32[16,128]{1,0:T(8,128)S(1)}, f32[16,128]{1,0:T(8,128)S(1)}, u32[]{:S(2)}, u32[]{:S(2)}) collective-permute-start(f32[16,128]{1,0:T(8,128)S(1)} %get-tuple-element.57.own_cells), channel_id=1, source_target_pairs={{0,1},{1,0},{2,3},{3,2},{4,5},{5,4},{6,7},{7,6},{8,9},{9,8},{10,11... | collective-permute-start | bytes 24584 | tf_op jit(solution)/shard_map/ppermute | solution.py:439
  7.1 5.4 %collective-permute-start.4 = (f32[7,16,128]{2,1,0:T(8,128)S(1)}, f32[7,16,128]{2,1,0:T(8,128)S(1)}, u32[]{:S(2)}, u32[]{:S(2)}) collective-permute-start(f32[7,16,128]{2,1,0:T(8,128)S(1)} %get-tuple-element.66.after.refs_0_), channel_id=1, source_target_pairs={{0,12},{4,8},{8,4},{12,0},{16,28},{20,24},{24,20},{28,16},{1,13},{... | collective-permute-start | bytes 172040 | tf_op jit(solution)/shard_map/ppermute | solution.py:439
  9.6 4.2 %collective-permute-start.3 = (f32[7,16,128]{2,1,0:T(8,128)S(1)}, f32[7,16,128]{2,1,0:T(8,128)S(1)}, u32[]{:S(2)}, u32[]{:S(2)}) collective-permute-start(f32[7,16,128]{2,1,0:T(8,128)S(1)} %get-tuple-element.66.after.refs_0_), channel_id=1, source_target_pairs={{0,8},{4,12},{8,0},{12,4},{16,24},{20,28},{24,16},{28,20},{1,9},{5... | collective-permute-start | bytes 172040 | tf_op jit(solution)/shard_map/ppermute | solution.py:439
  10.1 4.2 %collective-permute-start.2 = (f32[7,16,128]{2,1,0:T(8,128)S(1)}, f32[7,16,128]{2,1,0:T(8,128)S(1)}, u32[]{:S(2)}, u32[]{:S(2)}) collective-permute-start(f32[7,16,128]{2,1,0:T(8,128)S(1)} %get-tuple-element.66.after.refs_0_), channel_id=1, source_target_pairs={{0,4},{4,0},{8,12},{12,8},{16,20},{20,16},{24,28},{28,24},{1,5},{5... | collective-permute-start | bytes 172040 | tf_op jit(solution)/shard_map/ppermute | solution.py:439
  14.3 4.8 %collective-permute-start.5 = (f32[3,16,128]{2,1,0:T(8,128)S(1)}, f32[3,16,128]{2,1,0:T(8,128)S(1)}, u32[]{:S(2)}, u32[]{:S(2)}) collective-permute-start(f32[3,16,128]{2,1,0:T(8,128)S(1)} %get-tuple-element.70.own), channel_id=1, source_target_pairs={{0,16},{4,20},{8,24},{12,28},{16,0},{20,4},{24,8},{28,12},{1,17},{... | collective-permute-start | bytes 73736 | tf_op jit(solution)/shard_map/ppermute | solution.py:439
  19.5 1.2 %collective-permute-start.6 = (f32[7,2,128]{2,1,0:T(2,128)S(1)}, f32[7,2,128]{2,1,0:T(2,128)S(1)}, u32[]{:S(2)}, u32[]{:S(2)}) collective-permute-start(f32[7,2,128]{2,1,0:T(2,128)S(1)} %get-tuple-element.83.after.refs_0_), channel_id=1, source_target_pairs={{0,1},{1,0},{2,3},{3,2},{4,5},{5,4},{6,7},{7,6},{8,9},{9,8},{10,11... | collective-permute-start | bytes 21512 | tf_op jit(solution)/shard_map/ppermute | solution.py:439
  20.7 3.1 %collective-permute-start.7 = (f32[3,2,128]{2,1,0:T(2,128)S(1)}, f32[3,2,128]{2,1,0:T(2,128)S(1)}, u32[]{:S(2)}, u32[]{:S(2)}) collective-permute-start(f32[3,2,128]{2,1,0:T(2,128)S(1)} %get-tuple-element.93.own), channel_id=1, source_target_pairs={{0,3},{1,2},{2,1},{3,0},{4,7},{5,6},{6,5},{7,4},{8,11},{9,10},{10,... | collective-permute-start | bytes 9224 | tf_op jit(solution)/shard_map/ppermute | solution.py:439

commit v21 on v20

--- a/solution.py
+++ b/solution.py
@@ -145,12 +145,11 @@
 
 def load_kernel(t_hbm, b_hbm, loc_hbm, energy_hbm, t_out, b_out, loc, energy, packed, cells, sems):
     sheets, rows, columns = t_hbm.shape
-    halves = 2
     copies = []
-    for n in range(halves):
-        part = pl.ds(n * sheets // halves, sheets // halves)
+    for n, start in enumerate((0, columns - LANES)):
+        part = pl.ds(start, LANES)
         for i, (src, dst) in enumerate(((t_hbm, t_out), (b_hbm, b_out))):
-            copies.append(pltpu.make_async_copy(src.at[part], dst.at[part], sems.at[i, n]))
+            copies.append(pltpu.make_async_copy(src.at[:, :, part], dst.at[n], sems.at[i, n]))
     copies.append(pltpu.make_async_copy(loc_hbm, loc, sems.at[2, 0]))
     copies.append(pltpu.make_async_copy(energy_hbm, energy, sems.at[2, 1]))
     for copy in copies:
@@ -158,21 +157,19 @@
     lane = lax.broadcasted_iota(jnp.int32, (rows, LANES), 1)
     edge_t = jnp.zeros((rows, LANES), F32)
     edge_c = edge_t
-    for n in range(halves):
-        for copy in copies[2 * n : 2 * n + 2]:
+    for side, source in enumerate((0, LANES - 1)):
+        for copy in copies[2 * side : 2 * side + 2]:
             copy.wait()
-        for z in range(n * sheets // halves, (n + 1) * sheets // halves):
-            for side, part in enumerate((slice(0, LANES), slice(columns - LANES, columns))):
-                source = 0 if side == 0 else LANES - 1
-                t = t_out[z, :, part]
-                c = half_conduct(b_out[z, :, part], t)
-                place = lane == sheets * side + z
-                edge_t = jnp.where(place, t[:, source : source + 1], edge_t)
-                edge_c = jnp.where(place, c[:, source : source + 1], edge_c)
+        for z in range(sheets):
+            t = t_out[side, z]
+            c = half_conduct(b_out[side, z], t)
+            place = lane == sheets * side + z
+            edge_t = jnp.where(place, t[:, source : source + 1], edge_t)
+            edge_c = jnp.where(place, c[:, source : source + 1], edge_c)
     cells[0], cells[1] = edge_t, edge_c
     for i in range(2):
         packed[i * SUBLANES : (i + 1) * SUBLANES, :] = fold(cells.at[i], 2 * sheets)
-    for copy in copies[2 * halves :]:
+    for copy in copies[4:]:
         copy.wait()
 
 
@@ -183,9 +180,10 @@
     return pl.pallas_call(
         load_kernel,
         in_specs=[IN_HBM] * 4,
-        out_shape=[pltpu.VMEM(v.shape, v.dtype) for v in operands]
+        out_shape=[pltpu.VMEM((2, sheets, rows, LANES), F32)] * 2
+        + [pltpu.VMEM(v.shape, v.dtype) for v in operands[2:]]
         + [pltpu.VMEM((2 * SUBLANES, LANES), F32)],
-        scratch_shapes=[pltpu.VMEM((2, rows, LANES), F32), pltpu.SemaphoreType.DMA((3, 3))],
+        scratch_shapes=[pltpu.VMEM((2, rows, LANES), F32), pltpu.SemaphoreType.DMA((3, 2))],
         compiler_params=params(),
     )(*[pltpu.with_memory_space_constraint(v, pltpu.HBM) for v in operands])
 
@@ -242,17 +240,48 @@
             q_s[q, first : first + SUBLANES, :] = ends[q][i]
 
 
-def x_factor_kernel(plate, loc, energy, t_ref, b_ref, own_cells, *refs):
-    c_ref, total_ref, w_ref, i_ref, p_ref, links, view, h_ref, ends_ref, t_out, swapped, q_s, t_s = refs
+def x_factor_kernel(plate, loc, energy, t_edge, b_edge, own_cells, t_hbm, b_hbm, *refs):
+    c_ref, total_ref, w_ref, i_ref, p_ref, links, view, h_ref, ends_ref, t_out, swapped, t_s, q_s, t_m, b_m, sems = refs
     chunks, sheets, rows, _ = c_ref.shape
     lines = chunks * sheets
     steps = rows // SUBLANES
+    middle = pl.ds(LANES, (chunks - 2) * LANES)
+    copies = [
+        pltpu.make_async_copy(src.at[:, :, middle], dst, sems.at[i])
+        for i, (src, dst) in enumerate(((t_hbm, t_m), (b_hbm, b_m)))
+    ]
+    for copy in copies:
+        copy.start()
     plane = source_plane(loc, energy, rows, chunks * LANES, plate)
     mine = own_cells[...]
     in_low = lax.broadcasted_iota(jnp.int32, mine.shape, 1) % (2 * sheets) < sheets
     swapped[...] = jnp.where(
         in_low, pltpu.roll(mine, LANES - sheets, 1), pltpu.roll(mine, sheets, 1)
     )
+
+    def factor_group(members, at):
+        def cond(k):
+            return jnp.stack([c_ref[y, z, pl.ds(k, SUBLANES, stride=steps), :] for y, z in members], 0)
+
+        def keep(k, w, inv, p):
+            w_ref[k, at : at + len(members)] = w
+            i_ref[k, at : at + len(members)] = inv
+            p_ref[k, at : at + len(members)] = p
+
+        block = factor(cond, steps, keep)
+        for i, q in enumerate(COEFS):
+            for j in range(len(members)):
+                first = (at + j) * SUBLANES
+                q_s[i, first : first + SUBLANES, :] = block[q][j]
+
+    groups = line_groups(chunks, sheets)
+    for y, side in ((0, 0), (chunks - 1, 1)):
+        for z in range(sheets):
+            t_s[y, z] = t_edge[side, z]
+            c_ref[y, z] = half_conduct(b_edge[side, z], t_edge[side, z])
+    factor_group(groups[0], 0)
+    for copy in copies:
+        copy.wait()
 
     lane = lax.broadcasted_iota(jnp.int32, (SUBLANES, LANES), 1)
     is_first, is_last = lane == 0, lane == LANES - 1
@@ -260,8 +289,16 @@
         at = slice(r * SUBLANES, (r + 1) * SUBLANES)
         before_t, before_c = None, None
         for z in range(sheets):
-            ts = [t_ref[z, at, part_of(y)] for y in range(chunks)]
-            cs = [half_conduct(b_ref[z, at, part_of(y)], ts[y]) for y in range(chunks)]
+            ts, cs = [], []
+            for y in range(chunks):
+                if y in (0, chunks - 1):
+                    ts.append(t_s[y, z, at, :])
+                    cs.append(c_ref[y, z, at, :])
+                else:
+                    ts.append(t_m[z, at, part_of(y - 1)])
+                    cs.append(half_conduct(b_m[z, at, part_of(y - 1)], ts[y]))
+                    t_s[y, z, at, :] = ts[y]
+                    c_ref[y, z, at, :] = cs[y]
             t_turned = [pltpu.roll(v, LANES - 1, 1) for v in ts]
             c_turned = [pltpu.roll(v, LANES - 1, 1) for v in cs]
             flux = []
@@ -284,27 +321,12 @@
                     total = total - across
                     total_ref[y, z - 1, at, :] += across
                 total_ref[y, z, at, :] = total
-                c_ref[y, z, at, :] = cs[y]
-                t_s[y, z, at, :] = ts[y]
             before_t, before_c = ts, cs
 
     at = 0
-    for n, members in enumerate(line_groups(chunks, sheets)):
-
-        def cond(k):
-            return jnp.stack([c_ref[y, z, pl.ds(k, SUBLANES, stride=steps), :] for y, z in members], 0)
-
-        def keep(k, w, inv, p):
-            w_ref[k, at : at + len(members)] = w
-            i_ref[k, at : at + len(members)] = inv
-            p_ref[k, at : at + len(members)] = p
-
-        block = factor(cond, steps, keep)
-        for i, q in enumerate(COEFS):
-            for j in range(len(members)):
-                first = (at + j) * SUBLANES
-                q_s[i, first : first + SUBLANES, :] = block[q][j]
+    for n, members in enumerate(groups):
         if n > 0:
+            factor_group(members, at)
             x_eliminate(
                 lambda y, z, k: total_ref[y, z, pl.ds(k, SUBLANES, stride=steps), :],
                 members, at, w_ref, i_ref, p_ref, h_ref, at - 2 * sheets, ends_ref,
@@ -327,8 +349,8 @@
         view[n] = whole[q]
 
 
-def x_factor(loc, energy, t, b, plate, own_cells):
-    sheets, rows, columns = t.shape
+def x_factor(loc, energy, t_edge, b_edge, temperature, base, plate, own_cells):
+    sheets, rows, columns = temperature.shape
     chunks = columns // LANES
     lines = chunks * sheets
     steps = rows // SUBLANES
@@ -336,7 +358,7 @@
     stored = shape_of(steps, lines, SUBLANES, LANES)
     return pl.pallas_call(
         functools.partial(x_factor_kernel, plate),
-        in_specs=[IN_VMEM] * 5,
+        in_specs=[IN_VMEM] * 5 + [IN_HBM] * 2,
         out_shape=[
             field,
             field,
@@ -349,14 +371,22 @@
             shape_of(2, lines * SUBLANES, LANES),
             stored,
             shape_of(*own_cells.shape),
+            field,
         ],
         scratch_shapes=[
             pltpu.VMEM((len(COEFS), lines * SUBLANES, LANES), F32),
-            pltpu.VMEM((chunks, sheets, rows, LANES), F32),
+            pltpu.VMEM((sheets, rows, columns - 2 * LANES), F32),
+            pltpu.VMEM((sheets, rows, columns - 2 * LANES), F32),
+            pltpu.SemaphoreType.DMA((2,)),
         ],
         compiler_params=params(),
-        cost_estimate=pl.CostEstimate(flops=40 * t.size, bytes_accessed=28 * t.size, transcendentals=0),
-    )(loc, energy, t, b, own_cells)
+        cost_estimate=pl.CostEstimate(
+            flops=40 * temperature.size, bytes_accessed=28 * temperature.size, transcendentals=0
+        ),
+    )(
+        loc, energy, t_edge, b_edge, own_cells,
+        *[pltpu.with_memory_space_constraint(v, pltpu.HBM) for v in (temperature, base)],
+    )
 
 
 def x_target_kernel(own_cells, total_ref, near, far, *refs):
@@ -950,7 +980,7 @@
             return fields[z // each][at : at + rows, :]
 
         def keep(z, value):
-            base[y, z] = t_ref[z, :, part] + value
+            base[y, z] = t_ref[y, z] + value
 
         z_solve(zw, zi, field, (y,), keep)
         for m in range(pairs):
@@ -960,8 +990,7 @@
 
 
 def finish_prepare(ties, yw, yh, yp, inner, inner_own, outer, outer_own, zw, zi, t, to_x):
-    sheets, rows, columns = t.shape
-    chunks = columns // LANES
+    chunks, sheets, rows, _ = t.shape
     pairs = sheets * rows // LANES
     lines = chunks * pairs
     field = shape_of(chunks, sheets, rows, LANES)
@@ -971,7 +1000,7 @@
         scratch_shapes=[
             pltpu.VMEM((2, 2, lines, LANES), F32),
             pltpu.VMEM((2, 2, lines * SUBLANES, LANES), F32),
-            pltpu.VMEM((2, pairs, columns, LANES), F32),
+            pltpu.VMEM((2, pairs, chunks * LANES, LANES), F32),
         ],
         compiler_params=params(),
         cost_estimate=pl.CostEstimate(flops=12 * t.size, bytes_accessed=20 * t.size, transcendentals=0),
@@ -1023,10 +1052,12 @@
 def per_device(temperature, base, locations, energy):
     columns = temperature.shape[2]
     gy = lax.axis_size("gy")
-    t, b, loc, heat, packed = load(temperature, base, locations[None], energy[None])
+    t_edge, b_edge, loc, heat, packed = load(temperature, base, locations[None], energy[None])
     near = swap(packed, "gy", 1)
     far = lax.ppermute(packed, "gy", [(i, ((i + 1) % gy ^ 1) - 1 if i else gy - 1) for i in range(gy)])
-    c, total, xw, xi, xp, x_links, x_view, xm, ends, t_steps, swapped = x_factor(loc, heat, t, b, columns * gy, packed)
+    c, total, xw, xi, xp, x_links, x_view, xm, ends, t_steps, swapped, t = x_factor(
+        loc, heat, t_edge, b_edge, temperature, base, columns * gy, packed
+    )
     xh, x_own, view = x_target(swapped, total, near, far, xw, xi, xp, x_links, x_view, ends)
     yw, yi, yp, inner, outer, y_view, to_y, to_x, unit_low, unit_high = y_factor(c, x_view)
     zw, zi = z_factor(c, view)

time: 25 us -> 26 us (1.040)
  Pallas kernels: 8.09 us -> 9.03 us
  waiting for transfers between devices: 6.57 us -> 6.96 us
  starting transfers between devices: 10.1 us -> 9.76 us
    pallas_call x1, Pallas kernels: 2.13 us -> 3.21 us  [x_factor(): pl.pallas_call(functools.partial(x_factor_kernel, plate), in_specs=[IN_VM...]
    ppermute x7, waiting for transfers between devices: 6.56 us -> 6.96 us  [swap(): return lax.ppermute(value, axis, [(i, i ^ flip) for i in range(count)])]
    ppermute x7, starting transfers between devices: 7.66 us -> 7.29 us  [swap(): return lax.ppermute(value, axis, [(i, i ^ flip) for i in range(count)])]
  transfers between devices with their start and end apart: 8 -> 8, of which waited for: 6 -> 6; matrix products, arithmetic and copies ran while one was open for 0% -> 0% of each run, Pallas kernels for 20% -> 23%
where the time goes in v21:
time: 26 us; the launch traced here: 25.8 us
  starting transfers between devices  9.76 us (38%)
  Pallas kernels  9.03 us (35%)
  waiting for transfers between devices  6.96 us (27%)
    ppermute x7, starting transfers between devices, swap(): return lax.ppermute(value, axis, [(i, i ^ flip) for i in range(count)])  7.29 us
    ppermute x7, waiting for transfers between devices, swap(): return lax.ppermute(value, axis, [(i, i ^ flip) for i in range(count)])  6.96 us
    pallas_call x1, Pallas kernels, x_factor(): pl.pallas_call(functools.partial(x_factor_kernel, plate), in_specs=[IN_VM...  3.21 us
    ppermute x1, starting transfers between devices, per_device(): lax.ppermute(packed, 'gy', [(i, ((i + 1) % gy ^ 1) - 1 if i else gy - 1)...  2.47 us
    pallas_call x1, Pallas kernels, load(): pl.pallas_call(load_kernel, in_specs=[IN_HBM] * 4, out_shape=[pltpu.VMEM(...  1.39 us
    pallas_call x1, Pallas kernels, finish(): pl.pallas_call(functools.partial(finish_kernel, stages_of('gy')), out_sha...  1.07 us
    pallas_call x1, Pallas kernels, y_factor(): pl.pallas_call(y_factor_kernel, in_specs=[IN_VMEM, ANYWHERE], out_shape=[...  0.84 us
    pallas_call x1, Pallas kernels, finish_prepare(): pl.pallas_call(functools.partial(finish_prepare_kernel, len(ties) + 1), o...  0.81 us
  transfers between devices with their start and end apart: 8, of which 6 were waited for; matrix products, arithmetic and copies ran while one was open for 0% of the time, Pallas kernels for 23%

profile of v21, /device:TPU:0, one launch (start us, length us, event | category | flops | bytes accessed | tf_op | source)
XLA Modules:
  0.0 25.8 jit_solution(15802300138129979151)
XLA Ops:
  0.0 1.4 %shard_map.46 = (f32[2,4,64,128]{3,2,1,0:T(8,128)S(1)}, f32[2,4,64,128]{3,2,1,0:T(8,128)S(1)}, s32[1,64]{1,0:T(1,128)S(1)}, f32[1,64]{1,0:T(1,128)S(1)}, f32[16,128]{1,0:T(8,128)S(1)}) custom-call(f32[4,64,512]{2,1,0:T(8,128)} %t_hbm.3, f32[4,64,512]{2,1,0:T(8,128)} %b_hbm.3, s32[1,64]{1,0:T(1,128)} %bitcast.2, f32[1,64]{1,0:T(1,128)} %bitcast.3), custom_call_target="tpu_custom_call" | custom-call | tf_op jit(solution)/shard_map/pallas_call | solution.py:180
  1.4 2.5 %collective-permute-start.1 = (f32[16,128]{1,0:T(8,128)S(1)}, f32[16,128]{1,0:T(8,128)S(1)}, u32[]{:S(2)}, u32[]{:S(2)}) collective-permute-start(f32[16,128]{1,0:T(8,128)S(1)} %get-tuple-element.58.own_cells), channel_id=1, source_target_pairs={{0,3},{1,2},{2,1},{3,0},{4,7},{5,6},{6,5},{7,4},{8,11},{9,10},{10,... | collective-permute-start | bytes 24584 | tf_op jit(solution)/shard_map/ppermute | solution.py:1057
  3.9 0.7 %collective-permute-start = (f32[16,128]{1,0:T(8,128)S(1)}, f32[16,128]{1,0:T(8,128)S(1)}, u32[]{:S(2)}, u32[]{:S(2)}) collective-permute-start(f32[16,128]{1,0:T(8,128)S(1)} %get-tuple-element.58.own_cells), channel_id=1, source_target_pairs={{0,1},{1,0},{2,3},{3,2},{4,5},{5,4},{6,7},{7,6},{8,9},{9,8},{10,11... | collective-permute-start | bytes 24584 | tf_op jit(solution)/shard_map/ppermute | solution.py:469
  4.5 3.2 %shard_map.47 = (f32[4,4,64,128]{3,2,1,0:T(8,128)S(1)}, f32[4,4,64,128]{3,2,1,0:T(8,128)S(1)}, f32[8,16,8,128]{3,2,1,0:T(8,128)S(1)}, f32[8,16,8,128]{3,2,1,0:T(...) custom-call(s32[1,64]{1,0:T(1,128)S(1)} %get-tuple-element.54.loc, ...), custom_call_target="tpu_custom_call" | custom-call | flops 5242880 | bytes 3670016 | tf_op jit(solution)/shard_map/pallas_call | solution.py:359
  7.8 0.0 collective-permute-done.1.far
  7.8 0.0 collective-permute-done.near
  7.8 0.2 shard_map.48
  8.0 2.6 %collective-permute-start.4 = (f32[7,16,128]{2,1,0:T(8,128)S(1)}, f32[7,16,128]{2,1,0:T(8,128)S(1)}, u32[]{:S(2)}, u32[]{:S(2)}) collective-permute-start(f32[7,16,128]{2,1,0:T(8,128)S(1)} %get-tuple-element.67.after.refs_0_), channel_id=1, source_target_pairs={{0,12},{4,8},{8,4},{12,0},{16,28},{20,24},{24,20},{28,16},{1,13},{... | collective-permute-start | bytes 172040 | tf_op jit(solution)/shard_map/ppermute | solution.py:469
  10.6 0.4 %collective-permute-start.3 = (f32[7,16,128]{2,1,0:T(8,128)S(1)}, f32[7,16,128]{2,1,0:T(8,128)S(1)}, u32[]{:S(2)}, u32[]{:S(2)}) collective-permute-start(f32[7,16,128]{2,1,0:T(8,128)S(1)} %get-tuple-element.67.after.refs_0_), channel_id=1, source_target_pairs={{0,8},{4,12},{8,0},{12,4},{16,24},{20,28},{24,16},{28,20},{1,9},{5... | collective-permute-start | bytes 172040 | tf_op jit(solution)/shard_map/ppermute | solution.py:469
  11.0 0.5 %collective-permute-start.2 = (f32[7,16,128]{2,1,0:T(8,128)S(1)}, f32[7,16,128]{2,1,0:T(8,128)S(1)}, u32[]{:S(2)}, u32[]{:S(2)}) collective-permute-start(f32[7,16,128]{2,1,0:T(8,128)S(1)} %get-tuple-element.67.after.refs_0_), channel_id=1, source_target_pairs={{0,4},{4,0},{8,12},{12,8},{16,20},{20,16},{24,28},{28,24},{1,5},{5... | collective-permute-start | bytes 172040 | tf_op jit(solution)/shard_map/ppermute | solution.py:469
  11.6 0.8 %shard_map.49 = (f32[16,8,8,128]{3,2,1,0:T(8,128)S(1)}, f32[16,8,8,128]{3,2,1,0:T(8,128)S(1)}, f32[16,8,8,128]{3,2,1,0:T(8,128)S(1)}, f32[7,3,8,128]{3,2,1,0:T(8...) custom-call(f32[4,4,64,128]{3,2,1,0:T(8,128)S(1)} %get-tuple-element, ...), custom_call_target="tpu_custom_call" | custom-call | flops 2621440 | bytes 2097152 | tf_op jit(solution)/shard_map/pallas_call | solution.py:685
  12.4 0.2 shard_map.50
  12.6 0.9 %collective-permute-done.4.refs_3_ = f32[7,16,128]{2,1,0:T(8,128)S(1)} collective-permute-done((f32[7,16,128]{2,1,0:T(8,128)S(1)}, f32[7,16,128]{2,1,0:T(8,128)S(1)}, u32[]{:S(2)}, u32[]{:S(2)}) %collective-permute-start.4) | collective-permute-done | bytes 57376 | tf_op jit(solution)/shard_map/ppermute | solution.py:469
  13.4 1.3 %collective-permute-done.3.refs_2_ = f32[7,16,128]{2,1,0:T(8,128)S(1)} collective-permute-done((f32[7,16,128]{2,1,0:T(8,128)S(1)}, f32[7,16,128]{2,1,0:T(8,128)S(1)}, u32[]{:S(2)}, u32[]{:S(2)}) %collective-permute-start.3) | collective-permute-done | bytes 57376 | tf_op jit(solution)/shard_map/ppermute | solution.py:469
  14.8 0.4 %collective-permute-done.2.refs_1_ = f32[7,16,128]{2,1,0:T(8,128)S(1)} collective-permute-done((f32[7,16,128]{2,1,0:T(8,128)S(1)}, f32[7,16,128]{2,1,0:T(8,128)S(1)}, u32[]{:S(2)}, u32[]{:S(2)}) %collective-permute-start.2) | collective-permute-done | bytes 57376 | tf_op jit(solution)/shard_map/ppermute | solution.py:469
  15.2 0.1 shard_map.51
  15.3 2.7 %collective-permute-start.5 = (f32[3,16,128]{2,1,0:T(8,128)S(1)}, f32[3,16,128]{2,1,0:T(8,128)S(1)}, u32[]{:S(2)}, u32[]{:S(2)}) collective-permute-start(f32[3,16,128]{2,1,0:T(8,128)S(1)} %get-tuple-element.71.own), channel_id=1, source_target_pairs={{0,16},{4,20},{8,24},{12,28},{16,0},{20,4},{24,8},{28,12},{1,17},{... | collective-permute-start | bytes 73736 | tf_op jit(solution)/shard_map/ppermute | solution.py:469
  17.9 0.7 %shard_map.52 = (f32[4,128,256]{2,1,0:T(8,128)S(1)}, f32[4,128,256]{2,1,0:T(8,128)S(1)}, f32[4,128,256]{2,1,0:T(8,128)S(1)}, f32[4,128,256]{2,1,0:T(8,128)S(1)}, f32[2,2,128]{2,1,0:T(2,128)S(1)}) custom-call(f32[3,16,128]{2,1,0:T(8,128)S(1)} %get-tuple-element.72.refs_0_, f32[3,16,128]{2,1,0:T(8,128)S(1)} %get-tuple-element.73.refs_1_, ...), custom_call_target="tpu_custom_call" | custom-call | flops 1048576 | bytes 2097152 | tf_op jit(solution)/shard_map/pallas_call | solution.py:824
  18.6 1.5 %collective-permute-done.5.got = f32[3,16,128]{2,1,0:T(8,128)S(1)} collective-permute-done((f32[3,16,128]{2,1,0:T(8,128)S(1)}, f32[3,16,128]{2,1,0:T(8,128)S(1)}, u32[]{:S(2)}, u32[]{:S(2)}) %collective-permute-start.5) | collective-permute-done | bytes 24608 | tf_op jit(solution)/shard_map/ppermute | solution.py:469
  20.1 0.4 %shard_map.53 = (f32[4,128,256]{2,1,0:T(8,128)S(1)}, f32[7,2,128]{2,1,0:T(2,128)S(1)}) custom-call(f32[3,16,128]{2,1,0:T(8,128)S(1)} %get-tuple-element.71.own, f32[3,16,128]{2,1,0:T(8,128)S(1)} %collective-permute-done.5.got, f32[4,128,256]{2,1,0:T(8,128)S(1)} %get-tuple-element.81.to_first, f32[4,128,256]{2,1,0:T(8,128)S(1)} %get-tuple-element.82.to_last, ...), custom_call_target="tpu_custom_call" | custom-call | tf_op jit(solution)/shard_map/pallas_call | solution.py:860
  20.4 0.1 collective-permute-start.6
  20.5 0.2 shard_map.54
  20.7 0.9 %collective-permute-done.6.refs_1_ = f32[7,2,128]{2,1,0:T(2,128)S(1)} collective-permute-done((f32[7,2,128]{2,1,0:T(2,128)S(1)}, f32[7,2,128]{2,1,0:T(2,128)S(1)}, u32[]{:S(2)}, u32[]{:S(2)}) %collective-permute-start.6) | collective-permute-done | bytes 7200 | tf_op jit(solution)/shard_map/ppermute | solution.py:469
  21.7 0.3 %collective-permute-start.7 = (f32[3,2,128]{2,1,0:T(2,128)S(1)}, f32[3,2,128]{2,1,0:T(2,128)S(1)}, u32[]{:S(2)}, u32[]{:S(2)}) collective-permute-start(f32[3,2,128]{2,1,0:T(2,128)S(1)} %get-tuple-element.94.own), channel_id=1, source_target_pairs={{0,3},{1,2},{2,1},{3,0},{4,7},{5,6},{6,5},{7,4},{8,11},{9,10},{10,... | collective-permute-start | bytes 9224 | tf_op jit(solution)/shard_map/ppermute | solution.py:469
  22.0 0.8 %shard_map.56 = (f32[4,4,64,128]{3,2,1,0:T(8,128)S(1)}, f32[4,4,64,128]{3,2,1,0:T(8,128)S(1)}) custom-call(f32[3,2,128]{2,1,0:T(2,128)S(1)} %get-tuple-element.95.refs_0_, f32[16,8,8,128]{3,2,1,0:T(8,128)S(1)} %get-tuple-element.88.yw.refs_1_, f32[16,8,8,128]{3,2,1,0:T(8,128)S(1)} %get-tuple-element.93.refs_2_, ...), custom_call_target="tpu_custom_call" | custom-call | flops 1572864 | bytes 2621440 | tf_op jit(solution)/shard_map/pallas_call | solution.py:997
  22.8 1.9 %collective-permute-done.7.got = f32[3,2,128]{2,1,0:T(2,128)S(1)} collective-permute-done((f32[3,2,128]{2,1,0:T(2,128)S(1)}, f32[3,2,128]{2,1,0:T(2,128)S(1)}, u32[]{:S(2)}, u32[]{:S(2)}) %collective-permute-start.7) | collective-permute-done | bytes 3104 | tf_op jit(solution)/shard_map/ppermute | solution.py:469
  24.8 1.1 %shard_map.57 = f32[4,64,512]{2,1,0:T(8,128)} custom-call(f32[3,2,128]{2,1,0:T(2,128)S(1)} %get-tuple-element.94.own, f32[3,2,128]{2,1,0:T(2,128)S(1)} %collective-permute-done.7.got, f32[4,4,64,128]{3,2,1,0:T(8,128)S(1)} %get-tuple-element.101.base, f32[4,4,64,128]{3,2,1,0:T(8,128)S(1)} %get-tuple-element.102.response, ...), custom_call_target="tpu_custom_call" | custom-call | tf_op jit(solution)/shard_map/pallas_call | solution.py:1043
  (1 shorter events, 0.0 us)
Async XLA Ops:
  1.4 6.4 %collective-permute-start.1 = (f32[16,128]{1,0:T(8,128)S(1)}, f32[16,128]{1,0:T(8,128)S(1)}, u32[]{:S(2)}, u32[]{:S(2)}) collective-permute-start(f32[16,128]{1,0:T(8,128)S(1)} %get-tuple-element.58.own_cells), channel_id=1, source_target_pairs={{0,3},{1,2},{2,1},{3,0},{4,7},{5,6},{6,5},{7,4},{8,11},{9,10},{10,... | collective-permute-start | bytes 24584 | tf_op jit(solution)/shard_map/ppermute | solution.py:1057
  3.9 3.9 %collective-permute-start = (f32[16,128]{1,0:T(8,128)S(1)}, f32[16,128]{1,0:T(8,128)S(1)}, u32[]{:S(2)}, u32[]{:S(2)}) collective-permute-start(f32[16,128]{1,0:T(8,128)S(1)} %get-tuple-element.58.own_cells), channel_id=1, source_target_pairs={{0,1},{1,0},{2,3},{3,2},{4,5},{5,4},{6,7},{7,6},{8,9},{9,8},{10,11... | collective-permute-start | bytes 24584 | tf_op jit(solution)/shard_map/ppermute | solution.py:469
  8.0 5.4 %collective-permute-start.4 = (f32[7,16,128]{2,1,0:T(8,128)S(1)}, f32[7,16,128]{2,1,0:T(8,128)S(1)}, u32[]{:S(2)}, u32[]{:S(2)}) collective-permute-start(f32[7,16,128]{2,1,0:T(8,128)S(1)} %get-tuple-element.67.after.refs_0_), channel_id=1, source_target_pairs={{0,12},{4,8},{8,4},{12,0},{16,28},{20,24},{24,20},{28,16},{1,13},{... | collective-permute-start | bytes 172040 | tf_op jit(solution)/shard_map/ppermute | solution.py:469
  10.6 4.2 %collective-permute-start.3 = (f32[7,16,128]{2,1,0:T(8,128)S(1)}, f32[7,16,128]{2,1,0:T(8,128)S(1)}, u32[]{:S(2)}, u32[]{:S(2)}) collective-permute-start(f32[7,16,128]{2,1,0:T(8,128)S(1)} %get-tuple-element.67.after.refs_0_), channel_id=1, source_target_pairs={{0,8},{4,12},{8,0},{12,4},{16,24},{20,28},{24,16},{28,20},{1,9},{5... | collective-permute-start | bytes 172040 | tf_op jit(solution)/shard_map/ppermute | solution.py:469
  11.0 4.2 %collective-permute-start.2 = (f32[7,16,128]{2,1,0:T(8,128)S(1)}, f32[7,16,128]{2,1,0:T(8,128)S(1)}, u32[]{:S(2)}, u32[]{:S(2)}) collective-permute-start(f32[7,16,128]{2,1,0:T(8,128)S(1)} %get-tuple-element.67.after.refs_0_), channel_id=1, source_target_pairs={{0,4},{4,0},{8,12},{12,8},{16,20},{20,16},{24,28},{28,24},{1,5},{5... | collective-permute-start | bytes 172040 | tf_op jit(solution)/shard_map/ppermute | solution.py:469
  15.3 4.8 %collective-permute-start.5 = (f32[3,16,128]{2,1,0:T(8,128)S(1)}, f32[3,16,128]{2,1,0:T(8,128)S(1)}, u32[]{:S(2)}, u32[]{:S(2)}) collective-permute-start(f32[3,16,128]{2,1,0:T(8,128)S(1)} %get-tuple-element.71.own), channel_id=1, source_target_pairs={{0,16},{4,20},{8,24},{12,28},{16,0},{20,4},{24,8},{28,12},{1,17},{... | collective-permute-start | bytes 73736 | tf_op jit(solution)/shard_map/ppermute | solution.py:469
  20.4 1.2 %collective-permute-start.6 = (f32[7,2,128]{2,1,0:T(2,128)S(1)}, f32[7,2,128]{2,1,0:T(2,128)S(1)}, u32[]{:S(2)}, u32[]{:S(2)}) collective-permute-start(f32[7,2,128]{2,1,0:T(2,128)S(1)} %get-tuple-element.84.after.refs_0_), channel_id=1, source_target_pairs={{0,1},{1,0},{2,3},{3,2},{4,5},{5,4},{6,7},{7,6},{8,9},{9,8},{10,11... | collective-permute-start | bytes 21512 | tf_op jit(solution)/shard_map/ppermute | solution.py:469
  21.7 3.1 %collective-permute-start.7 = (f32[3,2,128]{2,1,0:T(2,128)S(1)}, f32[3,2,128]{2,1,0:T(2,128)S(1)}, u32[]{:S(2)}, u32[]{:S(2)}) collective-permute-start(f32[3,2,128]{2,1,0:T(2,128)S(1)} %get-tuple-element.94.own), channel_id=1, source_target_pairs={{0,3},{1,2},{2,1},{3,0},{4,7},{5,6},{6,5},{7,4},{8,11},{9,10},{10,... | collective-permute-start | bytes 9224 | tf_op jit(solution)/shard_map/ppermute | solution.py:469

commit v22 on v20

--- a/solution.py
+++ b/solution.py
@@ -143,49 +143,48 @@
     return total
 
 
-def load_kernel(t_hbm, b_hbm, loc_hbm, energy_hbm, t_out, b_out, loc, energy, packed, cells, sems):
+def load_kernel(t_hbm, b_hbm, t_out, b_out, packed, cells, sems):
     sheets, rows, columns = t_hbm.shape
-    halves = 2
+    parts = [(0, LANES), (columns - LANES, LANES), (LANES, columns - 2 * LANES)]
     copies = []
-    for n in range(halves):
-        part = pl.ds(n * sheets // halves, sheets // halves)
+    for n, (start, size) in enumerate(parts):
+        part = pl.ds(start, size)
         for i, (src, dst) in enumerate(((t_hbm, t_out), (b_hbm, b_out))):
-            copies.append(pltpu.make_async_copy(src.at[part], dst.at[part], sems.at[i, n]))
-    copies.append(pltpu.make_async_copy(loc_hbm, loc, sems.at[2, 0]))
-    copies.append(pltpu.make_async_copy(energy_hbm, energy, sems.at[2, 1]))
+            copies.append(
+                pltpu.make_async_copy(src.at[:, :, part], dst.at[:, :, part], sems.at[i, n])
+            )
     for copy in copies:
         copy.start()
     lane = lax.broadcasted_iota(jnp.int32, (rows, LANES), 1)
     edge_t = jnp.zeros((rows, LANES), F32)
     edge_c = edge_t
-    for n in range(halves):
-        for copy in copies[2 * n : 2 * n + 2]:
+    for side, source in enumerate((0, LANES - 1)):
+        for copy in copies[2 * side : 2 * side + 2]:
             copy.wait()
-        for z in range(n * sheets // halves, (n + 1) * sheets // halves):
-            for side, part in enumerate((slice(0, LANES), slice(columns - LANES, columns))):
-                source = 0 if side == 0 else LANES - 1
-                t = t_out[z, :, part]
-                c = half_conduct(b_out[z, :, part], t)
-                place = lane == sheets * side + z
-                edge_t = jnp.where(place, t[:, source : source + 1], edge_t)
-                edge_c = jnp.where(place, c[:, source : source + 1], edge_c)
+        part = slice(parts[side][0], parts[side][0] + LANES)
+        for z in range(sheets):
+            t = t_out[z, :, part]
+            c = half_conduct(b_out[z, :, part], t)
+            place = lane == sheets * side + z
+            edge_t = jnp.where(place, t[:, source : source + 1], edge_t)
+            edge_c = jnp.where(place, c[:, source : source + 1], edge_c)
     cells[0], cells[1] = edge_t, edge_c
     for i in range(2):
         packed[i * SUBLANES : (i + 1) * SUBLANES, :] = fold(cells.at[i], 2 * sheets)
-    for copy in copies[2 * halves :]:
+    for copy in copies[4:]:
         copy.wait()
 
 
-def load(temperature, base, locations, energy):
+def load(temperature, base):
     sheets, rows, columns = temperature.shape
     assert rows // SUBLANES * 2 * sheets <= LANES and columns > 2 * LANES
-    operands = (temperature, base, locations, energy)
+    operands = (temperature, base)
     return pl.pallas_call(
         load_kernel,
-        in_specs=[IN_HBM] * 4,
+        in_specs=[IN_HBM] * 2,
         out_shape=[pltpu.VMEM(v.shape, v.dtype) for v in operands]
         + [pltpu.VMEM((2 * SUBLANES, LANES), F32)],
-        scratch_shapes=[pltpu.VMEM((2, rows, LANES), F32), pltpu.SemaphoreType.DMA((3, 3))],
+        scratch_shapes=[pltpu.VMEM((2, rows, LANES), F32), pltpu.SemaphoreType.DMA((2, 3))],
         compiler_params=params(),
     )(*[pltpu.with_memory_space_constraint(v, pltpu.HBM) for v in operands])
 
@@ -242,12 +241,17 @@
             q_s[q, first : first + SUBLANES, :] = ends[q][i]
 
 
-def x_factor_kernel(plate, loc, energy, t_ref, b_ref, own_cells, *refs):
-    c_ref, total_ref, w_ref, i_ref, p_ref, links, view, h_ref, ends_ref, t_out, swapped, q_s, t_s = refs
+def x_factor_kernel(plate, loc_hbm, energy_hbm, t_ref, b_ref, own_cells, *refs):
+    c_ref, total_ref, w_ref, i_ref, p_ref, links, view, h_ref, ends_ref, t_out, swapped, q_s, t_s, loc, energy, sems = refs
     chunks, sheets, rows, _ = c_ref.shape
     lines = chunks * sheets
     steps = rows // SUBLANES
-    plane = source_plane(loc, energy, rows, chunks * LANES, plate)
+    copies = [
+        pltpu.make_async_copy(src, dst, sems.at[i])
+        for i, (src, dst) in enumerate(((loc_hbm, loc), (energy_hbm, energy)))
+    ]
+    for copy in copies:
+        copy.start()
     mine = own_cells[...]
     in_low = lax.broadcasted_iota(jnp.int32, mine.shape, 1) % (2 * sheets) < sheets
     swapped[...] = jnp.where(
@@ -277,9 +281,7 @@
             for y in range(chunks):
                 from_low = jnp.where(is_first, turned[y - 1] if y else 0.0, turned[y])
                 total = ts[y] + (flux[y] - from_low)
-                if z == 0:
-                    total = total + plane[at, part_of(y)]
-                else:
+                if z > 0:
                     across = (before_c[y] + cs[y]) * (ts[y] - before_t[y])
                     total = total - across
                     total_ref[y, z - 1, at, :] += across
@@ -287,6 +289,12 @@
                 c_ref[y, z, at, :] = cs[y]
                 t_s[y, z, at, :] = ts[y]
             before_t, before_c = ts, cs
+
+    for copy in copies:
+        copy.wait()
+    plane = source_plane(loc, energy, rows, chunks * LANES, plate)
+    for y in range(chunks):
+        total_ref[y, 0] += plane[:, part_of(y)]
 
     at = 0
     for n, members in enumerate(line_groups(chunks, sheets)):
@@ -336,7 +344,7 @@
     stored = shape_of(steps, lines, SUBLANES, LANES)
     return pl.pallas_call(
         functools.partial(x_factor_kernel, plate),
-        in_specs=[IN_VMEM] * 5,
+        in_specs=[IN_HBM] * 2 + [IN_VMEM] * 3,
         out_shape=[
             field,
             field,
@@ -353,10 +361,13 @@
         scratch_shapes=[
             pltpu.VMEM((len(COEFS), lines * SUBLANES, LANES), F32),
             pltpu.VMEM((chunks, sheets, rows, LANES), F32),
+            pltpu.VMEM(loc.shape, loc.dtype),
+            pltpu.VMEM(energy.shape, energy.dtype),
+            pltpu.SemaphoreType.DMA((2,)),
         ],
         compiler_params=params(),
         cost_estimate=pl.CostEstimate(flops=40 * t.size, bytes_accessed=28 * t.size, transcendentals=0),
-    )(loc, energy, t, b, own_cells)
+    )(*[pltpu.with_memory_space_constraint(v, pltpu.HBM) for v in (loc, energy)], t, b, own_cells)
 
 
 def x_target_kernel(own_cells, total_ref, near, far, *refs):
@@ -1023,10 +1034,12 @@
 def per_device(temperature, base, locations, energy):
     columns = temperature.shape[2]
     gy = lax.axis_size("gy")
-    t, b, loc, heat, packed = load(temperature, base, locations[None], energy[None])
+    t, b, packed = load(temperature, base)
     near = swap(packed, "gy", 1)
     far = lax.ppermute(packed, "gy", [(i, ((i + 1) % gy ^ 1) - 1 if i else gy - 1) for i in range(gy)])
-    c, total, xw, xi, xp, x_links, x_view, xm, ends, t_steps, swapped = x_factor(loc, heat, t, b, columns * gy, packed)
+    c, total, xw, xi, xp, x_links, x_view, xm, ends, t_steps, swapped = x_factor(
+        locations[None], energy[None], t, b, columns * gy, packed
+    )
     xh, x_own, view = x_target(swapped, total, near, far, xw, xi, xp, x_links, x_view, ends)
     yw, yi, yp, inner, outer, y_view, to_y, to_x, unit_low, unit_high = y_factor(c, x_view)
     zw, zi = z_factor(c, view)

time: 25 us -> 25.2 us (level)
  waiting for transfers between devices: 6.57 us -> 6.93 us
  starting transfers between devices: 10.1 us -> 9.78 us
    ppermute x7, waiting for transfers between devices: 6.56 us -> 6.93 us  [swap(): return lax.ppermute(value, axis, [(i, i ^ flip) for i in range(count)])]
    ppermute x7, starting transfers between devices: 7.66 us -> 7.31 us  [swap(): return lax.ppermute(value, axis, [(i, i ^ flip) for i in range(count)])]
  transfers between devices with their start and end apart: 8 -> 8, of which waited for: 6 -> 6; matrix products, arithmetic and copies ran while one was open for 0% -> 0% of each run, Pallas kernels for 20% -> 21%
where the time goes in v22:
time: 25.2 us; the launch traced here: 25.1 us
  starting transfers between devices  9.78 us (39%)
  Pallas kernels  8.3 us (33%)
  waiting for transfers between devices  6.93 us (28%)
    ppermute x7, starting transfers between devices, swap(): return lax.ppermute(value, axis, [(i, i ^ flip) for i in range(count)])  7.31 us
    ppermute x7, waiting for transfers between devices, swap(): return lax.ppermute(value, axis, [(i, i ^ flip) for i in range(count)])  6.93 us
    pallas_call x1, Pallas kernels, x_factor(): pl.pallas_call(functools.partial(x_factor_kernel, plate), in_specs=[IN_HB...  2.48 us
    ppermute x1, starting transfers between devices, per_device(): lax.ppermute(packed, 'gy', [(i, ((i + 1) % gy ^ 1) - 1 if i else gy - 1)...  2.47 us
    pallas_call x1, Pallas kernels, load(): pl.pallas_call(load_kernel, in_specs=[IN_HBM] * 2, out_shape=[pltpu.VMEM(...  1.39 us
    pallas_call x1, Pallas kernels, finish(): pl.pallas_call(functools.partial(finish_kernel, stages_of('gy')), out_sha...  1.07 us
    pallas_call x1, Pallas kernels, y_factor(): pl.pallas_call(y_factor_kernel, in_specs=[IN_VMEM, ANYWHERE], out_shape=[...  0.84 us
    pallas_call x1, Pallas kernels, finish_prepare(): pl.pallas_call(functools.partial(finish_prepare_kernel, len(ties) + 1), o...  0.8 us
  transfers between devices with their start and end apart: 8, of which 6 were waited for; matrix products, arithmetic and copies ran while one was open for 0% of the time, Pallas kernels for 21%

profile of v22, /device:TPU:0, one launch (start us, length us, event | category | flops | bytes accessed | tf_op | source)
XLA Modules:
  0.0 25.1 jit_solution(18075782526158709619)
XLA Ops:
  0.0 1.4 %shard_map.46 = (f32[4,64,512]{2,1,0:T(8,128)S(1)}, f32[4,64,512]{2,1,0:T(8,128)S(1)}, f32[16,128]{1,0:T(8,128)S(1)}) custom-call(f32[4,64,512]{2,1,0:T(8,128)} %t_hbm.1, f32[4,64,512]{2,1,0:T(8,128)} %b_hbm.1), custom_call_target="tpu_custom_call" | custom-call | tf_op jit(solution)/shard_map/pallas_call | solution.py:182
  1.4 2.5 %collective-permute-start.1 = (f32[16,128]{1,0:T(8,128)S(1)}, f32[16,128]{1,0:T(8,128)S(1)}, u32[]{:S(2)}, u32[]{:S(2)}) collective-permute-start(f32[16,128]{1,0:T(8,128)S(1)} %get-tuple-element.53.own_cells), channel_id=1, source_target_pairs={{0,3},{1,2},{2,1},{3,0},{4,7},{5,6},{6,5},{7,4},{8,11},{9,10},{10,... | collective-permute-start | bytes 24584 | tf_op jit(solution)/shard_map/ppermute | solution.py:1039
  3.9 0.7 %collective-permute-start = (f32[16,128]{1,0:T(8,128)S(1)}, f32[16,128]{1,0:T(8,128)S(1)}, u32[]{:S(2)}, u32[]{:S(2)}) collective-permute-start(f32[16,128]{1,0:T(8,128)S(1)} %get-tuple-element.53.own_cells), channel_id=1, source_target_pairs={{0,1},{1,0},{2,3},{3,2},{4,5},{5,4},{6,7},{7,6},{8,9},{9,8},{10,11... | collective-permute-start | bytes 24584 | tf_op jit(solution)/shard_map/ppermute | solution.py:450
  4.5 2.5 %shard_map.47 = (f32[4,4,64,128]{3,2,1,0:T(8,128)S(1)}, f32[4,4,64,128]{3,2,1,0:T(8,128)S(1)}, f32[8,16,8,128]{3,2,1,0:T(8,128)S(1)}, f32[8,16,8,128]{3,2,1,0:T(...) custom-call(s32[1,64]{1,0:T(1,128)} %bitcast.2, ...), custom_call_target="tpu_custom_call" | custom-call | flops 5242880 | bytes 3670016 | tf_op jit(solution)/shard_map/pallas_call | solution.py:345
  7.0 0.0 collective-permute-done.1.far
  7.0 0.0 collective-permute-done.near
  7.1 0.2 shard_map.48
  7.3 2.6 %collective-permute-start.4 = (f32[7,16,128]{2,1,0:T(8,128)S(1)}, f32[7,16,128]{2,1,0:T(8,128)S(1)}, u32[]{:S(2)}, u32[]{:S(2)}) collective-permute-start(f32[7,16,128]{2,1,0:T(8,128)S(1)} %get-tuple-element.62.after.refs_0_), channel_id=1, source_target_pairs={{0,12},{4,8},{8,4},{12,0},{16,28},{20,24},{24,20},{28,16},{1,13},{... | collective-permute-start | bytes 172040 | tf_op jit(solution)/shard_map/ppermute | solution.py:450
  9.9 0.4 %collective-permute-start.3 = (f32[7,16,128]{2,1,0:T(8,128)S(1)}, f32[7,16,128]{2,1,0:T(8,128)S(1)}, u32[]{:S(2)}, u32[]{:S(2)}) collective-permute-start(f32[7,16,128]{2,1,0:T(8,128)S(1)} %get-tuple-element.62.after.refs_0_), channel_id=1, source_target_pairs={{0,8},{4,12},{8,0},{12,4},{16,24},{20,28},{24,16},{28,20},{1,9},{5... | collective-permute-start | bytes 172040 | tf_op jit(solution)/shard_map/ppermute | solution.py:450
  10.3 0.5 %collective-permute-start.2 = (f32[7,16,128]{2,1,0:T(8,128)S(1)}, f32[7,16,128]{2,1,0:T(8,128)S(1)}, u32[]{:S(2)}, u32[]{:S(2)}) collective-permute-start(f32[7,16,128]{2,1,0:T(8,128)S(1)} %get-tuple-element.62.after.refs_0_), channel_id=1, source_target_pairs={{0,4},{4,0},{8,12},{12,8},{16,20},{20,16},{24,28},{28,24},{1,5},{5... | collective-permute-start | bytes 172040 | tf_op jit(solution)/shard_map/ppermute | solution.py:450
  10.8 0.8 %shard_map.49 = (f32[16,8,8,128]{3,2,1,0:T(8,128)S(1)}, f32[16,8,8,128]{3,2,1,0:T(8,128)S(1)}, f32[16,8,8,128]{3,2,1,0:T(8,128)S(1)}, f32[7,3,8,128]{3,2,1,0:T(8...) custom-call(f32[4,4,64,128]{3,2,1,0:T(8,128)S(1)} %get-tuple-element, ...), custom_call_target="tpu_custom_call" | custom-call | flops 2621440 | bytes 2097152 | tf_op jit(solution)/shard_map/pallas_call | solution.py:666
  11.7 0.2 shard_map.50
  11.9 0.9 %collective-permute-done.4.refs_3_ = f32[7,16,128]{2,1,0:T(8,128)S(1)} collective-permute-done((f32[7,16,128]{2,1,0:T(8,128)S(1)}, f32[7,16,128]{2,1,0:T(8,128)S(1)}, u32[]{:S(2)}, u32[]{:S(2)}) %collective-permute-start.4) | collective-permute-done | bytes 57376 | tf_op jit(solution)/shard_map/ppermute | solution.py:450
  12.7 1.3 %collective-permute-done.3.refs_2_ = f32[7,16,128]{2,1,0:T(8,128)S(1)} collective-permute-done((f32[7,16,128]{2,1,0:T(8,128)S(1)}, f32[7,16,128]{2,1,0:T(8,128)S(1)}, u32[]{:S(2)}, u32[]{:S(2)}) %collective-permute-start.3) | collective-permute-done | bytes 57376 | tf_op jit(solution)/shard_map/ppermute | solution.py:450
  14.0 0.4 %collective-permute-done.2.refs_1_ = f32[7,16,128]{2,1,0:T(8,128)S(1)} collective-permute-done((f32[7,16,128]{2,1,0:T(8,128)S(1)}, f32[7,16,128]{2,1,0:T(8,128)S(1)}, u32[]{:S(2)}, u32[]{:S(2)}) %collective-permute-start.2) | collective-permute-done | bytes 57376 | tf_op jit(solution)/shard_map/ppermute | solution.py:450
  14.5 0.1 shard_map.51
  14.5 2.7 %collective-permute-start.5 = (f32[3,16,128]{2,1,0:T(8,128)S(1)}, f32[3,16,128]{2,1,0:T(8,128)S(1)}, u32[]{:S(2)}, u32[]{:S(2)}) collective-permute-start(f32[3,16,128]{2,1,0:T(8,128)S(1)} %get-tuple-element.66.own), channel_id=1, source_target_pairs={{0,16},{4,20},{8,24},{12,28},{16,0},{20,4},{24,8},{28,12},{1,17},{... | collective-permute-start | bytes 73736 | tf_op jit(solution)/shard_map/ppermute | solution.py:450
  17.2 0.7 %shard_map.52 = (f32[4,128,256]{2,1,0:T(8,128)S(1)}, f32[4,128,256]{2,1,0:T(8,128)S(1)}, f32[4,128,256]{2,1,0:T(8,128)S(1)}, f32[4,128,256]{2,1,0:T(8,128)S(1)}, f32[2,2,128]{2,1,0:T(2,128)S(1)}) custom-call(f32[3,16,128]{2,1,0:T(8,128)S(1)} %get-tuple-element.67.refs_0_, f32[3,16,128]{2,1,0:T(8,128)S(1)} %get-tuple-element.68.refs_1_, ...), custom_call_target="tpu_custom_call" | custom-call | flops 1048576 | bytes 2097152 | tf_op jit(solution)/shard_map/pallas_call | solution.py:805
  17.9 1.5 %collective-permute-done.5.got = f32[3,16,128]{2,1,0:T(8,128)S(1)} collective-permute-done((f32[3,16,128]{2,1,0:T(8,128)S(1)}, f32[3,16,128]{2,1,0:T(8,128)S(1)}, u32[]{:S(2)}, u32[]{:S(2)}) %collective-permute-start.5) | collective-permute-done | bytes 24608 | tf_op jit(solution)/shard_map/ppermute | solution.py:450
  19.3 0.4 %shard_map.53 = (f32[4,128,256]{2,1,0:T(8,128)S(1)}, f32[7,2,128]{2,1,0:T(2,128)S(1)}) custom-call(f32[3,16,128]{2,1,0:T(8,128)S(1)} %get-tuple-element.66.own, f32[3,16,128]{2,1,0:T(8,128)S(1)} %collective-permute-done.5.got, f32[4,128,256]{2,1,0:T(8,128)S(1)} %get-tuple-element.76.to_first, f32[4,128,256]{2,1,0:T(8,128)S(1)} %get-tuple-element.77.to_last, ...), custom_call_target="tpu_custom_call" | custom-call | tf_op jit(solution)/shard_map/pallas_call | solution.py:841
  19.7 0.1 collective-permute-start.6
  19.8 0.3 %shard_map.54 = (f32[16,8,8,128]{3,2,1,0:T(8,128)S(1)}, f32[7,8,128]{2,1,0:T(8,128)S(1)}, f32[3,2,128]{2,1,0:T(2,128)S(1)}) custom-call(f32[4,128,256]{2,1,0:T(8,128)S(1)} %get-tuple-element.80.base, f32[4,128,256]{2,1,0:T(8,128)S(1)} %get-tuple-element.81.response, f32[4,128,256]{2,1,0:T(8,128)S(1)} %get-tuple-element.82.spread, ...), custom_call_target="tpu_custom_call" | custom-call | flops 1048576 | bytes 2097152 | tf_op jit(solution)/shard_map/pallas_call | solution.py:886
  20.0 0.9 %collective-permute-done.6.refs_1_ = f32[7,2,128]{2,1,0:T(2,128)S(1)} collective-permute-done((f32[7,2,128]{2,1,0:T(2,128)S(1)}, f32[7,2,128]{2,1,0:T(2,128)S(1)}, u32[]{:S(2)}, u32[]{:S(2)}) %collective-permute-start.6) | collective-permute-done | bytes 7200 | tf_op jit(solution)/shard_map/ppermute | solution.py:450
  20.9 0.4 %collective-permute-start.7 = (f32[3,2,128]{2,1,0:T(2,128)S(1)}, f32[3,2,128]{2,1,0:T(2,128)S(1)}, u32[]{:S(2)}, u32[]{:S(2)}) collective-permute-start(f32[3,2,128]{2,1,0:T(2,128)S(1)} %get-tuple-element.89.own), channel_id=1, source_target_pairs={{0,3},{1,2},{2,1},{3,0},{4,7},{5,6},{6,5},{7,4},{8,11},{9,10},{10,... | collective-permute-start | bytes 9224 | tf_op jit(solution)/shard_map/ppermute | solution.py:450
  21.3 0.8 %shard_map.56 = (f32[4,4,64,128]{3,2,1,0:T(8,128)S(1)}, f32[4,4,64,128]{3,2,1,0:T(8,128)S(1)}) custom-call(f32[3,2,128]{2,1,0:T(2,128)S(1)} %get-tuple-element.90.refs_0_, f32[16,8,8,128]{3,2,1,0:T(8,128)S(1)} %get-tuple-element.83.yw.refs_1_, f32[16,8,8,128]{3,2,1,0:T(8,128)S(1)} %get-tuple-element.88.refs_2_, ...), custom_call_target="tpu_custom_call" | custom-call | flops 1572864 | bytes 2621440 | tf_op jit(solution)/shard_map/pallas_call | solution.py:979
  22.1 1.9 %collective-permute-done.7.got = f32[3,2,128]{2,1,0:T(2,128)S(1)} collective-permute-done((f32[3,2,128]{2,1,0:T(2,128)S(1)}, f32[3,2,128]{2,1,0:T(2,128)S(1)}, u32[]{:S(2)}, u32[]{:S(2)}) %collective-permute-start.7) | collective-permute-done | bytes 3104 | tf_op jit(solution)/shard_map/ppermute | solution.py:450
  24.0 1.1 %shard_map.57 = f32[4,64,512]{2,1,0:T(8,128)} custom-call(f32[3,2,128]{2,1,0:T(2,128)S(1)} %get-tuple-element.89.own, f32[3,2,128]{2,1,0:T(2,128)S(1)} %collective-permute-done.7.got, f32[4,4,64,128]{3,2,1,0:T(8,128)S(1)} %get-tuple-element.95.base, f32[4,4,64,128]{3,2,1,0:T(8,128)S(1)} %get-tuple-element.96.response, ...), custom_call_target="tpu_custom_call" | custom-call | tf_op jit(solution)/shard_map/pallas_call | solution.py:1025
  (1 shorter events, 0.0 us)
Async XLA Ops:
  1.4 5.6 %collective-permute-start.1 = (f32[16,128]{1,0:T(8,128)S(1)}, f32[16,128]{1,0:T(8,128)S(1)}, u32[]{:S(2)}, u32[]{:S(2)}) collective-permute-start(f32[16,128]{1,0:T(8,128)S(1)} %get-tuple-element.53.own_cells), channel_id=1, source_target_pairs={{0,3},{1,2},{2,1},{3,0},{4,7},{5,6},{6,5},{7,4},{8,11},{9,10},{10,... | collective-permute-start | bytes 24584 | tf_op jit(solution)/shard_map/ppermute | solution.py:1039
  3.9 3.2 %collective-permute-start = (f32[16,128]{1,0:T(8,128)S(1)}, f32[16,128]{1,0:T(8,128)S(1)}, u32[]{:S(2)}, u32[]{:S(2)}) collective-permute-start(f32[16,128]{1,0:T(8,128)S(1)} %get-tuple-element.53.own_cells), channel_id=1, source_target_pairs={{0,1},{1,0},{2,3},{3,2},{4,5},{5,4},{6,7},{7,6},{8,9},{9,8},{10,11... | collective-permute-start | bytes 24584 | tf_op jit(solution)/shard_map/ppermute | solution.py:450
  7.3 5.4 %collective-permute-start.4 = (f32[7,16,128]{2,1,0:T(8,128)S(1)}, f32[7,16,128]{2,1,0:T(8,128)S(1)}, u32[]{:S(2)}, u32[]{:S(2)}) collective-permute-start(f32[7,16,128]{2,1,0:T(8,128)S(1)} %get-tuple-element.62.after.refs_0_), channel_id=1, source_target_pairs={{0,12},{4,8},{8,4},{12,0},{16,28},{20,24},{24,20},{28,16},{1,13},{... | collective-permute-start | bytes 172040 | tf_op jit(solution)/shard_map/ppermute | solution.py:450
  9.9 4.2 %collective-permute-start.3 = (f32[7,16,128]{2,1,0:T(8,128)S(1)}, f32[7,16,128]{2,1,0:T(8,128)S(1)}, u32[]{:S(2)}, u32[]{:S(2)}) collective-permute-start(f32[7,16,128]{2,1,0:T(8,128)S(1)} %get-tuple-element.62.after.refs_0_), channel_id=1, source_target_pairs={{0,8},{4,12},{8,0},{12,4},{16,24},{20,28},{24,16},{28,20},{1,9},{5... | collective-permute-start | bytes 172040 | tf_op jit(solution)/shard_map/ppermute | solution.py:450
  10.3 4.2 %collective-permute-start.2 = (f32[7,16,128]{2,1,0:T(8,128)S(1)}, f32[7,16,128]{2,1,0:T(8,128)S(1)}, u32[]{:S(2)}, u32[]{:S(2)}) collective-permute-start(f32[7,16,128]{2,1,0:T(8,128)S(1)} %get-tuple-element.62.after.refs_0_), channel_id=1, source_target_pairs={{0,4},{4,0},{8,12},{12,8},{16,20},{20,16},{24,28},{28,24},{1,5},{5... | collective-permute-start | bytes 172040 | tf_op jit(solution)/shard_map/ppermute | solution.py:450
  14.5 4.8 %collective-permute-start.5 = (f32[3,16,128]{2,1,0:T(8,128)S(1)}, f32[3,16,128]{2,1,0:T(8,128)S(1)}, u32[]{:S(2)}, u32[]{:S(2)}) collective-permute-start(f32[3,16,128]{2,1,0:T(8,128)S(1)} %get-tuple-element.66.own), channel_id=1, source_target_pairs={{0,16},{4,20},{8,24},{12,28},{16,0},{20,4},{24,8},{28,12},{1,17},{... | collective-permute-start | bytes 73736 | tf_op jit(solution)/shard_map/ppermute | solution.py:450
  19.7 1.2 %collective-permute-start.6 = (f32[7,2,128]{2,1,0:T(2,128)S(1)}, f32[7,2,128]{2,1,0:T(2,128)S(1)}, u32[]{:S(2)}, u32[]{:S(2)}) collective-permute-start(f32[7,2,128]{2,1,0:T(2,128)S(1)} %get-tuple-element.79.after.refs_0_), channel_id=1, source_target_pairs={{0,1},{1,0},{2,3},{3,2},{4,5},{5,4},{6,7},{7,6},{8,9},{9,8},{10,11... | collective-permute-start | bytes 21512 | tf_op jit(solution)/shard_map/ppermute | solution.py:450
  20.9 3.1 %collective-permute-start.7 = (f32[3,2,128]{2,1,0:T(2,128)S(1)}, f32[3,2,128]{2,1,0:T(2,128)S(1)}, u32[]{:S(2)}, u32[]{:S(2)}) collective-permute-start(f32[3,2,128]{2,1,0:T(2,128)S(1)} %get-tuple-element.89.own), channel_id=1, source_target_pairs={{0,3},{1,2},{2,1},{3,0},{4,7},{5,6},{6,5},{7,4},{8,11},{9,10},{10,... | collective-permute-start | bytes 9224 | tf_op jit(solution)/shard_map/ppermute | solution.py:450

commit v23 on v20

--- a/solution.py
+++ b/solution.py
@@ -145,12 +145,14 @@
 
 def load_kernel(t_hbm, b_hbm, loc_hbm, energy_hbm, t_out, b_out, loc, energy, packed, cells, sems):
     sheets, rows, columns = t_hbm.shape
-    halves = 2
+    parts = [(0, LANES), (columns - LANES, LANES), (LANES, columns - 2 * LANES)]
     copies = []
-    for n in range(halves):
-        part = pl.ds(n * sheets // halves, sheets // halves)
+    for n, (start, size) in enumerate(parts):
+        part = pl.ds(start, size)
         for i, (src, dst) in enumerate(((t_hbm, t_out), (b_hbm, b_out))):
-            copies.append(pltpu.make_async_copy(src.at[part], dst.at[part], sems.at[i, n]))
+            copies.append(
+                pltpu.make_async_copy(src.at[:, :, part], dst.at[:, :, part], sems.at[i, n])
+            )
     copies.append(pltpu.make_async_copy(loc_hbm, loc, sems.at[2, 0]))
     copies.append(pltpu.make_async_copy(energy_hbm, energy, sems.at[2, 1]))
     for copy in copies:
@@ -158,21 +160,20 @@
     lane = lax.broadcasted_iota(jnp.int32, (rows, LANES), 1)
     edge_t = jnp.zeros((rows, LANES), F32)
     edge_c = edge_t
-    for n in range(halves):
-        for copy in copies[2 * n : 2 * n + 2]:
+    for side, source in enumerate((0, LANES - 1)):
+        for copy in copies[2 * side : 2 * side + 2]:
             copy.wait()
-        for z in range(n * sheets // halves, (n + 1) * sheets // halves):
-            for side, part in enumerate((slice(0, LANES), slice(columns - LANES, columns))):
-                source = 0 if side == 0 else LANES - 1
-                t = t_out[z, :, part]
-                c = half_conduct(b_out[z, :, part], t)
-                place = lane == sheets * side + z
-                edge_t = jnp.where(place, t[:, source : source + 1], edge_t)
-                edge_c = jnp.where(place, c[:, source : source + 1], edge_c)
+        part = slice(parts[side][0], parts[side][0] + LANES)
+        for z in range(sheets):
+            t = t_out[z, :, part]
+            c = half_conduct(b_out[z, :, part], t)
+            place = lane == sheets * side + z
+            edge_t = jnp.where(place, t[:, source : source + 1], edge_t)
+            edge_c = jnp.where(place, c[:, source : source + 1], edge_c)
     cells[0], cells[1] = edge_t, edge_c
     for i in range(2):
         packed[i * SUBLANES : (i + 1) * SUBLANES, :] = fold(cells.at[i], 2 * sheets)
-    for copy in copies[2 * halves :]:
+    for copy in copies[4:]:
         copy.wait()
 
 

time: 25 us -> 24.9 us (level)
  no operation moved by 1% of the time
where the time goes in v23:
time: 24.9 us; the launch traced here: 24.8 us
  starting transfers between devices  10.1 us (41%)
  Pallas kernels  8.01 us (32%)
  waiting for transfers between devices  6.56 us (26%)
    ppermute x7, starting transfers between devices, swap(): return lax.ppermute(value, axis, [(i, i ^ flip) for i in range(count)])  7.66 us
    ppermute x7, waiting for transfers between devices, swap(): return lax.ppermute(value, axis, [(i, i ^ flip) for i in range(count)])  6.56 us
    ppermute x1, starting transfers between devices, per_device(): lax.ppermute(packed, 'gy', [(i, ((i + 1) % gy ^ 1) - 1 if i else gy - 1)...  2.47 us
    pallas_call x1, Pallas kernels, x_factor(): pl.pallas_call(functools.partial(x_factor_kernel, plate), in_specs=[IN_VM...  2.13 us
    pallas_call x1, Pallas kernels, load(): pl.pallas_call(load_kernel, in_specs=[IN_HBM] * 4, out_shape=[pltpu.VMEM(...  1.42 us
    pallas_call x1, Pallas kernels, finish(): pl.pallas_call(functools.partial(finish_kernel, stages_of('gy')), out_sha...  1.07 us
    pallas_call x1, Pallas kernels, y_factor(): pl.pallas_call(y_factor_kernel, in_specs=[IN_VMEM, ANYWHERE], out_shape=[...  0.84 us
    pallas_call x1, Pallas kernels, finish_prepare(): pl.pallas_call(functools.partial(finish_prepare_kernel, len(ties) + 1), o...  0.82 us
  transfers between devices with their start and end apart: 8, of which 6 were waited for; matrix products, arithmetic and copies ran while one was open for 0% of the time, Pallas kernels for 20%

profile of v23, /device:TPU:0, one launch (start us, length us, event | category | flops | bytes accessed | tf_op | source)
XLA Modules:
  0.0 24.8 jit_solution(147675914727054867)
XLA Ops:
  0.0 1.4 %shard_map.46 = (f32[4,64,512]{2,1,0:T(8,128)S(1)}, f32[4,64,512]{2,1,0:T(8,128)S(1)}, s32[1,64]{1,0:T(1,128)S(1)}, f32[1,64]{1,0:T(1,128)S(1)}, f32[16,128]{1,0:T(8,128)S(1)}) custom-call(f32[4,64,512]{2,1,0:T(8,128)} %t_hbm.1, f32[4,64,512]{2,1,0:T(8,128)} %b_hbm.1, s32[1,64]{1,0:T(1,128)} %bitcast.2, f32[1,64]{1,0:T(1,128)} %bitcast.3), custom_call_target="tpu_custom_call" | custom-call | tf_op jit(solution)/shard_map/pallas_call | solution.py:184
  1.4 2.5 %collective-permute-start.1 = (f32[16,128]{1,0:T(8,128)S(1)}, f32[16,128]{1,0:T(8,128)S(1)}, u32[]{:S(2)}, u32[]{:S(2)}) collective-permute-start(f32[16,128]{1,0:T(8,128)S(1)} %get-tuple-element.57.own_cells), channel_id=1, source_target_pairs={{0,3},{1,2},{2,1},{3,0},{4,7},{5,6},{6,5},{7,4},{8,11},{9,10},{10,... | collective-permute-start | bytes 24584 | tf_op jit(solution)/shard_map/ppermute | solution.py:1029
  3.9 0.7 %collective-permute-start = (f32[16,128]{1,0:T(8,128)S(1)}, f32[16,128]{1,0:T(8,128)S(1)}, u32[]{:S(2)}, u32[]{:S(2)}) collective-permute-start(f32[16,128]{1,0:T(8,128)S(1)} %get-tuple-element.57.own_cells), channel_id=1, source_target_pairs={{0,1},{1,0},{2,3},{3,2},{4,5},{5,4},{6,7},{7,6},{8,9},{9,8},{10,11... | collective-permute-start | bytes 24584 | tf_op jit(solution)/shard_map/ppermute | solution.py:440
  4.6 2.1 %shard_map.47 = (f32[4,4,64,128]{3,2,1,0:T(8,128)S(1)}, f32[4,4,64,128]{3,2,1,0:T(8,128)S(1)}, f32[8,16,8,128]{3,2,1,0:T(8,128)S(1)}, f32[8,16,8,128]{3,2,1,0:T(...) custom-call(s32[1,64]{1,0:T(1,128)S(1)} %get-tuple-element.53.loc, ...), custom_call_target="tpu_custom_call" | custom-call | flops 5242880 | bytes 3670016 | tf_op jit(solution)/shard_map/pallas_call | solution.py:338
  6.7 0.0 collective-permute-done.1.far
  6.7 0.0 collective-permute-done.near
  6.7 0.2 shard_map.48
  7.0 2.6 %collective-permute-start.4 = (f32[7,16,128]{2,1,0:T(8,128)S(1)}, f32[7,16,128]{2,1,0:T(8,128)S(1)}, u32[]{:S(2)}, u32[]{:S(2)}) collective-permute-start(f32[7,16,128]{2,1,0:T(8,128)S(1)} %get-tuple-element.66.after.refs_0_), channel_id=1, source_target_pairs={{0,12},{4,8},{8,4},{12,0},{16,28},{20,24},{24,20},{28,16},{1,13},{... | collective-permute-start | bytes 172040 | tf_op jit(solution)/shard_map/ppermute | solution.py:440
  9.5 0.4 %collective-permute-start.3 = (f32[7,16,128]{2,1,0:T(8,128)S(1)}, f32[7,16,128]{2,1,0:T(8,128)S(1)}, u32[]{:S(2)}, u32[]{:S(2)}) collective-permute-start(f32[7,16,128]{2,1,0:T(8,128)S(1)} %get-tuple-element.66.after.refs_0_), channel_id=1, source_target_pairs={{0,8},{4,12},{8,0},{12,4},{16,24},{20,28},{24,16},{28,20},{1,9},{5... | collective-permute-start | bytes 172040 | tf_op jit(solution)/shard_map/ppermute | solution.py:440
  10.0 0.5 %collective-permute-start.2 = (f32[7,16,128]{2,1,0:T(8,128)S(1)}, f32[7,16,128]{2,1,0:T(8,128)S(1)}, u32[]{:S(2)}, u32[]{:S(2)}) collective-permute-start(f32[7,16,128]{2,1,0:T(8,128)S(1)} %get-tuple-element.66.after.refs_0_), channel_id=1, source_target_pairs={{0,4},{4,0},{8,12},{12,8},{16,20},{20,16},{24,28},{28,24},{1,5},{5... | collective-permute-start | bytes 172040 | tf_op jit(solution)/shard_map/ppermute | solution.py:440
  10.5 0.8 %shard_map.49 = (f32[16,8,8,128]{3,2,1,0:T(8,128)S(1)}, f32[16,8,8,128]{3,2,1,0:T(8,128)S(1)}, f32[16,8,8,128]{3,2,1,0:T(8,128)S(1)}, f32[7,3,8,128]{3,2,1,0:T(8...) custom-call(f32[4,4,64,128]{3,2,1,0:T(8,128)S(1)} %get-tuple-element, ...), custom_call_target="tpu_custom_call" | custom-call | flops 2621440 | bytes 2097152 | tf_op jit(solution)/shard_map/pallas_call | solution.py:656
  11.4 0.2 shard_map.50
  11.5 0.9 %collective-permute-done.4.refs_3_ = f32[7,16,128]{2,1,0:T(8,128)S(1)} collective-permute-done((f32[7,16,128]{2,1,0:T(8,128)S(1)}, f32[7,16,128]{2,1,0:T(8,128)S(1)}, u32[]{:S(2)}, u32[]{:S(2)}) %collective-permute-start.4) | collective-permute-done | bytes 57376 | tf_op jit(solution)/shard_map/ppermute | solution.py:440
  12.4 1.3 %collective-permute-done.3.refs_2_ = f32[7,16,128]{2,1,0:T(8,128)S(1)} collective-permute-done((f32[7,16,128]{2,1,0:T(8,128)S(1)}, f32[7,16,128]{2,1,0:T(8,128)S(1)}, u32[]{:S(2)}, u32[]{:S(2)}) %collective-permute-start.3) | collective-permute-done | bytes 57376 | tf_op jit(solution)/shard_map/ppermute | solution.py:440
  13.7 0.4 %collective-permute-done.2.refs_1_ = f32[7,16,128]{2,1,0:T(8,128)S(1)} collective-permute-done((f32[7,16,128]{2,1,0:T(8,128)S(1)}, f32[7,16,128]{2,1,0:T(8,128)S(1)}, u32[]{:S(2)}, u32[]{:S(2)}) %collective-permute-start.2) | collective-permute-done | bytes 57376 | tf_op jit(solution)/shard_map/ppermute | solution.py:440
  14.2 0.1 shard_map.51
  14.2 2.7 %collective-permute-start.5 = (f32[3,16,128]{2,1,0:T(8,128)S(1)}, f32[3,16,128]{2,1,0:T(8,128)S(1)}, u32[]{:S(2)}, u32[]{:S(2)}) collective-permute-start(f32[3,16,128]{2,1,0:T(8,128)S(1)} %get-tuple-element.70.own), channel_id=1, source_target_pairs={{0,16},{4,20},{8,24},{12,28},{16,0},{20,4},{24,8},{28,12},{1,17},{... | collective-permute-start | bytes 73736 | tf_op jit(solution)/shard_map/ppermute | solution.py:440
  16.9 0.7 %shard_map.52 = (f32[4,128,256]{2,1,0:T(8,128)S(1)}, f32[4,128,256]{2,1,0:T(8,128)S(1)}, f32[4,128,256]{2,1,0:T(8,128)S(1)}, f32[4,128,256]{2,1,0:T(8,128)S(1)}, f32[2,2,128]{2,1,0:T(2,128)S(1)}) custom-call(f32[3,16,128]{2,1,0:T(8,128)S(1)} %get-tuple-element.71.refs_0_, f32[3,16,128]{2,1,0:T(8,128)S(1)} %get-tuple-element.72.refs_1_, ...), custom_call_target="tpu_custom_call" | custom-call | flops 1048576 | bytes 2097152 | tf_op jit(solution)/shard_map/pallas_call | solution.py:795
  17.5 1.5 %collective-permute-done.5.got = f32[3,16,128]{2,1,0:T(8,128)S(1)} collective-permute-done((f32[3,16,128]{2,1,0:T(8,128)S(1)}, f32[3,16,128]{2,1,0:T(8,128)S(1)}, u32[]{:S(2)}, u32[]{:S(2)}) %collective-permute-start.5) | collective-permute-done | bytes 24608 | tf_op jit(solution)/shard_map/ppermute | solution.py:440
  19.0 0.3 %shard_map.53 = (f32[4,128,256]{2,1,0:T(8,128)S(1)}, f32[7,2,128]{2,1,0:T(2,128)S(1)}) custom-call(f32[3,16,128]{2,1,0:T(8,128)S(1)} %get-tuple-element.70.own, f32[3,16,128]{2,1,0:T(8,128)S(1)} %collective-permute-done.5.got, f32[4,128,256]{2,1,0:T(8,128)S(1)} %get-tuple-element.80.to_first, f32[4,128,256]{2,1,0:T(8,128)S(1)} %get-tuple-element.81.to_last, ...), custom_call_target="tpu_custom_call" | custom-call | tf_op jit(solution)/shard_map/pallas_call | solution.py:831
  19.4 0.1 collective-permute-start.6
  19.5 0.3 %shard_map.54 = (f32[16,8,8,128]{3,2,1,0:T(8,128)S(1)}, f32[7,8,128]{2,1,0:T(8,128)S(1)}, f32[3,2,128]{2,1,0:T(2,128)S(1)}) custom-call(f32[4,128,256]{2,1,0:T(8,128)S(1)} %get-tuple-element.84.base, f32[4,128,256]{2,1,0:T(8,128)S(1)} %get-tuple-element.85.response, f32[4,128,256]{2,1,0:T(8,128)S(1)} %get-tuple-element.86.spread, ...), custom_call_target="tpu_custom_call" | custom-call | flops 1048576 | bytes 2097152 | tf_op jit(solution)/shard_map/pallas_call | solution.py:876
  19.7 0.9 %collective-permute-done.6.refs_1_ = f32[7,2,128]{2,1,0:T(2,128)S(1)} collective-permute-done((f32[7,2,128]{2,1,0:T(2,128)S(1)}, f32[7,2,128]{2,1,0:T(2,128)S(1)}, u32[]{:S(2)}, u32[]{:S(2)}) %collective-permute-start.6) | collective-permute-done | bytes 7200 | tf_op jit(solution)/shard_map/ppermute | solution.py:440
  20.6 0.7 %collective-permute-start.7 = (f32[3,2,128]{2,1,0:T(2,128)S(1)}, f32[3,2,128]{2,1,0:T(2,128)S(1)}, u32[]{:S(2)}, u32[]{:S(2)}) collective-permute-start(f32[3,2,128]{2,1,0:T(2,128)S(1)} %get-tuple-element.93.own), channel_id=1, source_target_pairs={{0,3},{1,2},{2,1},{3,0},{4,7},{5,6},{6,5},{7,4},{8,11},{9,10},{10,... | collective-permute-start | bytes 9224 | tf_op jit(solution)/shard_map/ppermute | solution.py:440
  21.3 0.8 %shard_map.56 = (f32[4,4,64,128]{3,2,1,0:T(8,128)S(1)}, f32[4,4,64,128]{3,2,1,0:T(8,128)S(1)}) custom-call(f32[3,2,128]{2,1,0:T(2,128)S(1)} %get-tuple-element.94.refs_0_, f32[16,8,8,128]{3,2,1,0:T(8,128)S(1)} %get-tuple-element.87.yw.refs_1_, f32[16,8,8,128]{3,2,1,0:T(8,128)S(1)} %get-tuple-element.92.refs_2_, ...), custom_call_target="tpu_custom_call" | custom-call | flops 1572864 | bytes 2621440 | tf_op jit(solution)/shard_map/pallas_call | solution.py:969
  22.2 1.6 %collective-permute-done.7.got = f32[3,2,128]{2,1,0:T(2,128)S(1)} collective-permute-done((f32[3,2,128]{2,1,0:T(2,128)S(1)}, f32[3,2,128]{2,1,0:T(2,128)S(1)}, u32[]{:S(2)}, u32[]{:S(2)}) %collective-permute-start.7) | collective-permute-done | bytes 3104 | tf_op jit(solution)/shard_map/ppermute | solution.py:440
  23.7 1.1 %shard_map.57 = f32[4,64,512]{2,1,0:T(8,128)} custom-call(f32[3,2,128]{2,1,0:T(2,128)S(1)} %get-tuple-element.93.own, f32[3,2,128]{2,1,0:T(2,128)S(1)} %collective-permute-done.7.got, f32[4,4,64,128]{3,2,1,0:T(8,128)S(1)} %get-tuple-element.99.base, f32[4,4,64,128]{3,2,1,0:T(8,128)S(1)} %get-tuple-element.100.response, ...), custom_call_target="tpu_custom_call" | custom-call | tf_op jit(solution)/shard_map/pallas_call | solution.py:1015
  (1 shorter events, 0.0 us)
Async XLA Ops:
  1.4 5.3 %collective-permute-start.1 = (f32[16,128]{1,0:T(8,128)S(1)}, f32[16,128]{1,0:T(8,128)S(1)}, u32[]{:S(2)}, u32[]{:S(2)}) collective-permute-start(f32[16,128]{1,0:T(8,128)S(1)} %get-tuple-element.57.own_cells), channel_id=1, source_target_pairs={{0,3},{1,2},{2,1},{3,0},{4,7},{5,6},{6,5},{7,4},{8,11},{9,10},{10,... | collective-permute-start | bytes 24584 | tf_op jit(solution)/shard_map/ppermute | solution.py:1029
  3.9 2.8 %collective-permute-start = (f32[16,128]{1,0:T(8,128)S(1)}, f32[16,128]{1,0:T(8,128)S(1)}, u32[]{:S(2)}, u32[]{:S(2)}) collective-permute-start(f32[16,128]{1,0:T(8,128)S(1)} %get-tuple-element.57.own_cells), channel_id=1, source_target_pairs={{0,1},{1,0},{2,3},{3,2},{4,5},{5,4},{6,7},{7,6},{8,9},{9,8},{10,11... | collective-permute-start | bytes 24584 | tf_op jit(solution)/shard_map/ppermute | solution.py:440
  7.0 5.4 %collective-permute-start.4 = (f32[7,16,128]{2,1,0:T(8,128)S(1)}, f32[7,16,128]{2,1,0:T(8,128)S(1)}, u32[]{:S(2)}, u32[]{:S(2)}) collective-permute-start(f32[7,16,128]{2,1,0:T(8,128)S(1)} %get-tuple-element.66.after.refs_0_), channel_id=1, source_target_pairs={{0,12},{4,8},{8,4},{12,0},{16,28},{20,24},{24,20},{28,16},{1,13},{... | collective-permute-start | bytes 172040 | tf_op jit(solution)/shard_map/ppermute | solution.py:440
  9.5 4.2 %collective-permute-start.3 = (f32[7,16,128]{2,1,0:T(8,128)S(1)}, f32[7,16,128]{2,1,0:T(8,128)S(1)}, u32[]{:S(2)}, u32[]{:S(2)}) collective-permute-start(f32[7,16,128]{2,1,0:T(8,128)S(1)} %get-tuple-element.66.after.refs_0_), channel_id=1, source_target_pairs={{0,8},{4,12},{8,0},{12,4},{16,24},{20,28},{24,16},{28,20},{1,9},{5... | collective-permute-start | bytes 172040 | tf_op jit(solution)/shard_map/ppermute | solution.py:440
  10.0 4.2 %collective-permute-start.2 = (f32[7,16,128]{2,1,0:T(8,128)S(1)}, f32[7,16,128]{2,1,0:T(8,128)S(1)}, u32[]{:S(2)}, u32[]{:S(2)}) collective-permute-start(f32[7,16,128]{2,1,0:T(8,128)S(1)} %get-tuple-element.66.after.refs_0_), channel_id=1, source_target_pairs={{0,4},{4,0},{8,12},{12,8},{16,20},{20,16},{24,28},{28,24},{1,5},{5... | collective-permute-start | bytes 172040 | tf_op jit(solution)/shard_map/ppermute | solution.py:440
  14.2 4.8 %collective-permute-start.5 = (f32[3,16,128]{2,1,0:T(8,128)S(1)}, f32[3,16,128]{2,1,0:T(8,128)S(1)}, u32[]{:S(2)}, u32[]{:S(2)}) collective-permute-start(f32[3,16,128]{2,1,0:T(8,128)S(1)} %get-tuple-element.70.own), channel_id=1, source_target_pairs={{0,16},{4,20},{8,24},{12,28},{16,0},{20,4},{24,8},{28,12},{1,17},{... | collective-permute-start | bytes 73736 | tf_op jit(solution)/shard_map/ppermute | solution.py:440
  19.4 1.2 %collective-permute-start.6 = (f32[7,2,128]{2,1,0:T(2,128)S(1)}, f32[7,2,128]{2,1,0:T(2,128)S(1)}, u32[]{:S(2)}, u32[]{:S(2)}) collective-permute-start(f32[7,2,128]{2,1,0:T(2,128)S(1)} %get-tuple-element.83.after.refs_0_), channel_id=1, source_target_pairs={{0,1},{1,0},{2,3},{3,2},{4,5},{5,4},{6,7},{7,6},{8,9},{9,8},{10,11... | collective-permute-start | bytes 21512 | tf_op jit(solution)/shard_map/ppermute | solution.py:440
  20.6 3.1 %collective-permute-start.7 = (f32[3,2,128]{2,1,0:T(2,128)S(1)}, f32[3,2,128]{2,1,0:T(2,128)S(1)}, u32[]{:S(2)}, u32[]{:S(2)}) collective-permute-start(f32[3,2,128]{2,1,0:T(2,128)S(1)} %get-tuple-element.93.own), channel_id=1, source_target_pairs={{0,3},{1,2},{2,1},{3,0},{4,7},{5,6},{6,5},{7,4},{8,11},{9,10},{10,... | collective-permute-start | bytes 9224 | tf_op jit(solution)/shard_map/ppermute | solution.py:440

commit v24 on v23

--- a/solution.py
+++ b/solution.py
@@ -627,6 +627,7 @@
     for n, q in enumerate(COEFS):
         view[n] = whole[q]
 
+    same = turn_matrix(to_y.shape, True, 1)
     one = jnp.ones((pairs, LANES), F32)
     for n, (low, high, field) in enumerate(((one, 0.0 * one, unit_low), (0.0 * one, one, unit_high))):
         for y, pair in enumerate(tree_ends(chunks, outer, nothing, low, high)):
@@ -644,7 +645,9 @@
         for k in range(steps - 1, -1, -1):
             value = w_ref[k] * value + p_ref[k] * low
             for j, (y, m) in enumerate(members):
-                field[y, k * SUBLANES : (k + 1) * SUBLANES, part_of(m)] = value[j]
+                c_s[m, pl.ds(y * LANES + k, SUBLANES, stride=steps), :] = value[j]
+        for y, m in members:
+            field[y, part_of(m), :] = turned(same, c_s[m, part_of(y), :])
 
 
 def y_factor(c, after):
@@ -665,8 +668,8 @@
             shape_of(len(COEFS), pairs, LANES),
             matrix,
             matrix,
-            shape_of(chunks, LANES, pairs * LANES),
-            shape_of(chunks, LANES, pairs * LANES),
+            shape_of(chunks, pairs * LANES, LANES),
+            shape_of(chunks, pairs * LANES, LANES),
         ],
         scratch_shapes=[
             pltpu.VMEM((pairs, chunks * LANES, LANES), F32),
@@ -769,32 +772,31 @@
 
     totals = [None, None]
     for y in range(chunks):
-        field = turned(to_y[...], g_s[0, y])
-        answer = turned(to_y[...], g_s[1, y])
-        base[y] = field
-        response[y] = answer
+        base[y] = turned(to_y[...], g_s[0, y])
+        response[y] = turned(to_y[...], g_s[1, y])
         for i, (unit, weight) in enumerate(((y_low, to_first), (y_high, to_last))):
-            weight[y] = unit[y] * answer
-            part = unit[y] * field
+            weight[y] = unit[y] * g_s[1, y]
+            part = unit[y] * g_s[0, y]
             totals[i] = part if y == 0 else totals[i] + part
     for i in range(2):
         put_sums(fixed.at[i], totals[i])
 
 
 def put_sums(out, field):
-    total = jnp.sum(field, 0, keepdims=True)
+    ones = jnp.ones((2 * SUBLANES, 2 * LANES), jnp.bfloat16)
+    total = turned(ones, field)
     for m in range(out.shape[0]):
-        out[m : m + 1, :] = total[:, part_of(m)]
+        out[m : m + 1, :] = total[:1, part_of(m)]
 
 
 def y_prepare(ties, xw, xh, xm, xp, x_links, x_own, t, to_y, unit_low, unit_high):
     chunks = unit_low.shape[0]
     x_steps, lines = xw.shape[:2]
     width = lines // chunks * x_steps * SUBLANES
-    field = shape_of(chunks, LANES, width)
+    field, weight = shape_of(chunks, LANES, width), shape_of(chunks, width, LANES)
     return pl.pallas_call(
         functools.partial(y_prepare_kernel, len(ties) + 1),
-        out_shape=[field] * 4 + [shape_of(2, width // LANES, LANES)],
+        out_shape=[field] * 2 + [weight] * 2 + [shape_of(2, width // LANES, LANES)],
         scratch_shapes=[
             pltpu.VMEM((2, 2, lines * SUBLANES, LANES), F32),
             pltpu.VMEM((2, chunks, width, LANES), F32),
@@ -804,54 +806,56 @@
     )(*ties, xw, xh, xm, xp, x_links, x_own, t, to_y, unit_low, unit_high)
 
 
-def y_target_kernel(stages, own, got, to_first, to_last, fixed, view, to_y, spread, send, r_s):
-    chunks, _, width = to_first.shape
+def sheet_rows(values, y, chunks, sheets):
+    line_of = {member: n for n, member in enumerate(sum(line_groups(chunks, sheets), []))}
+    return [values[line_of[y, z] : line_of[y, z] + 1, :] for z in range(sheets)]
+
+
+def y_target_kernel(stages, own, got, to_first, to_last, fixed, view, flux_ref, send, r_s):
+    chunks, width, _ = to_first.shape
     sheets = own.shape[1] // chunks
     rows = width // sheets
 
     flux = top_flux("gx", stages, own, got)
-    line_of = {member: n for n, member in enumerate(sum(line_groups(chunks, sheets), []))}
-    totals = [None, None]
+    flux_ref[...] = flux
+    totals = [[None] * sheets, [None] * sheets]
     for y in range(chunks):
-        own_flux = jnp.concatenate([flux[line_of[y, z] : line_of[y, z] + 1, :] for z in range(sheets)], 0)
-        wide = turned(to_y[...], own_flux, rows)
-        spread[y] = wide
-        for i, weight in enumerate((to_first, to_last)):
-            part = weight[y] * wide
-            totals[i] = part if y == 0 else totals[i] + part
+        for z, row in enumerate(sheet_rows(flux, y, chunks, sheets)):
+            for total, weight in zip(totals, (to_first, to_last)):
+                part = weight[y, z * rows : (z + 1) * rows, :] * row
+                total[z] = part if y == 0 else total[z] + part
     for n, q in enumerate(COEFS):
         send[q] = view[n]
     for i, q in enumerate((FIRST, LAST)):
-        put_sums(r_s.at[i], totals[i])
+        put_sums(r_s.at[i], jnp.concatenate(totals[i], 0))
         send[q] = fixed[i] + r_s[i]
 
 
-def y_target(own, got, to_first, to_last, fixed, view, to_y):
+def y_target(own, got, to_first, to_last, fixed, view):
     pairs = view.shape[1]
     return pl.pallas_call(
         functools.partial(y_target_kernel, stages_of("gx")),
-        out_shape=[shape_of(*to_first.shape), shape_of(7, pairs, LANES)],
+        out_shape=[shape_of(*own.shape[1:]), shape_of(7, pairs, LANES)],
         scratch_shapes=[pltpu.VMEM((2, pairs, LANES), F32)],
         compiler_params=params(),
-    )(own, got, to_first, to_last, fixed, view, to_y)
-
-
-def y_eliminate_kernel(base, response, spread, yw, yi, yp, inner, outer, after, *refs):
+    )(own, got, to_first, to_last, fixed, view)
+
+
+def y_eliminate_kernel(base, response, flux, to_y, yw, yi, yp, inner, outer, after, *refs):
     h_ref, inner_own, outer_own, q_s, r_s = refs
     chunks, _, width = base.shape
     pairs = width // LANES
+    sheets = flux.shape[0] // chunks
     steps = yw.shape[0]
     members = [(y, m) for y in range(chunks) for m in range(pairs)]
+    fields = []
+    for y in range(chunks):
+        by_sheet = jnp.concatenate(sheet_rows(flux[...], y, chunks, sheets), 0)
+        fields.append(base[y] + response[y] * turned(to_y[...], by_sheet, width // sheets))
 
     def target(k):
         at = slice(k * SUBLANES, (k + 1) * SUBLANES)
-        return jnp.stack(
-            [
-                base[y, at, part_of(m)] + response[y, at, part_of(m)] * spread[y, at, part_of(m)]
-                for y, m in members
-            ],
-            0,
-        )
+        return jnp.stack([fields[y][at, part_of(m)] for y, m in members], 0)
 
     def keep(k, h):
         h_ref[k] = h
@@ -869,13 +873,13 @@
     join_tree(items, outer, outer_own)
 
 
-def y_eliminate(base, response, spread, yw, yi, yp, inner, outer, after):
+def y_eliminate(base, response, flux, to_y, yw, yi, yp, inner, outer, after):
     y_lines = yw.shape[1]
     pairs = outer.shape[2]
     chunks = y_lines // pairs
     return pl.pallas_call(
         y_eliminate_kernel,
-        in_specs=[IN_VMEM] * 8 + [ANYWHERE],
+        in_specs=[IN_VMEM] * 9 + [ANYWHERE],
         out_shape=[
             shape_of(*yw.shape),
             shape_of(SUBLANES - 1, y_lines, LANES),
@@ -887,7 +891,7 @@
         ],
         compiler_params=params(),
         cost_estimate=pl.CostEstimate(flops=8 * base.size, bytes_accessed=16 * base.size, transcendentals=0),
-    )(base, response, spread, yw, yi, yp, inner, outer, after)
+    )(base, response, flux, to_y, yw, yi, yp, inner, outer, after)
 
 
 def z_solve(zw, zi, field, at, keep):
@@ -1035,8 +1039,10 @@
     base, response, to_first, to_last, fixed = y_prepare(
         ties, xw, xh, xm, xp, x_links, x_own, t_steps, to_y, unit_low, unit_high
     )
-    spread, view = y_target(own, got, to_first, to_last, fixed, y_view, to_y)
-    yh, inner_own, outer_own = y_eliminate(base, response, spread, yw, yi, yp, inner, outer, view)
+    flux, view = y_target(own, got, to_first, to_last, fixed, y_view)
+    yh, inner_own, outer_own = y_eliminate(
+        base, response, flux, to_y, yw, yi, yp, inner, outer, view
+    )
     own, got, ties = gather_line(view, "gy", meanwhile=(yh,), cross=True)
     base, response = finish_prepare(
         ties, yw, yh, yp, inner, inner_own, outer, outer_own, zw, zi, t, to_x

time: 24.9 us -> 24.7 us (level)
  waiting for transfers between devices: 6.56 us -> 5.84 us
  Pallas kernels: 8.01 us -> 8.6 us
    ppermute x7, waiting for transfers between devices: 6.56 us -> 5.84 us  [swap(): return lax.ppermute(value, axis, [(i, i ^ flip) for i in range(count)])]
    pallas_call x1, Pallas kernels: 0.84 us -> 1.4 us  [y_factor(): pl.pallas_call(y_factor_kernel, in_specs=[IN_VMEM, ANYWHERE], out_shape=[...]
  transfers between devices with their start and end apart: 8 -> 8, of which waited for: 6 -> 6; matrix products, arithmetic and copies ran while one was open for 0% -> 0% of each run, Pallas kernels for 20% -> 23%
where the time goes in v24:
time: 24.7 us; the launch traced here: 24.6 us
  starting transfers between devices  10.1 us (41%)
  Pallas kernels  8.6 us (35%)
  waiting for transfers between devices  5.84 us (24%)
    ppermute x7, starting transfers between devices, swap(): return lax.ppermute(value, axis, [(i, i ^ flip) for i in range(count)])  7.59 us
    ppermute x7, waiting for transfers between devices, swap(): return lax.ppermute(value, axis, [(i, i ^ flip) for i in range(count)])  5.84 us
    ppermute x1, starting transfers between devices, per_device(): lax.ppermute(packed, 'gy', [(i, ((i + 1) % gy ^ 1) - 1 if i else gy - 1)...  2.47 us
    pallas_call x1, Pallas kernels, x_factor(): pl.pallas_call(functools.partial(x_factor_kernel, plate), in_specs=[IN_VM...  2.13 us
    pallas_call x1, Pallas kernels, load(): pl.pallas_call(load_kernel, in_specs=[IN_HBM] * 4, out_shape=[pltpu.VMEM(...  1.42 us
    pallas_call x1, Pallas kernels, y_factor(): pl.pallas_call(y_factor_kernel, in_specs=[IN_VMEM, ANYWHERE], out_shape=[...  1.4 us
    pallas_call x1, Pallas kernels, finish(): pl.pallas_call(functools.partial(finish_kernel, stages_of('gy')), out_sha...  1.06 us
    pallas_call x1, Pallas kernels, finish_prepare(): pl.pallas_call(functools.partial(finish_prepare_kernel, len(ties) + 1), o...  0.79 us
  transfers between devices with their start and end apart: 8, of which 6 were waited for; matrix products, arithmetic and copies ran while one was open for 0% of the time, Pallas kernels for 23%

profile of v24, /device:TPU:0, one launch (start us, length us, event | category | flops | bytes accessed | tf_op | source)
XLA Modules:
  0.0 24.6 jit_solution(6192999386115503087)
XLA Ops:
  0.0 1.4 %shard_map.46 = (f32[4,64,512]{2,1,0:T(8,128)S(1)}, f32[4,64,512]{2,1,0:T(8,128)S(1)}, s32[1,64]{1,0:T(1,128)S(1)}, f32[1,64]{1,0:T(1,128)S(1)}, f32[16,128]{1,0:T(8,128)S(1)}) custom-call(f32[4,64,512]{2,1,0:T(8,128)} %t_hbm.1, f32[4,64,512]{2,1,0:T(8,128)} %b_hbm.1, s32[1,64]{1,0:T(1,128)} %bitcast.2, f32[1,64]{1,0:T(1,128)} %bitcast.3), custom_call_target="tpu_custom_call" | custom-call | tf_op jit(solution)/shard_map/pallas_call | solution.py:184
  1.4 2.5 %collective-permute-start.1 = (f32[16,128]{1,0:T(8,128)S(1)}, f32[16,128]{1,0:T(8,128)S(1)}, u32[]{:S(2)}, u32[]{:S(2)}) collective-permute-start(f32[16,128]{1,0:T(8,128)S(1)} %get-tuple-element.57.own_cells), channel_id=1, source_target_pairs={{0,3},{1,2},{2,1},{3,0},{4,7},{5,6},{6,5},{7,4},{8,11},{9,10},{10,... | collective-permute-start | bytes 24584 | tf_op jit(solution)/shard_map/ppermute | solution.py:1033
  3.9 0.7 %collective-permute-start = (f32[16,128]{1,0:T(8,128)S(1)}, f32[16,128]{1,0:T(8,128)S(1)}, u32[]{:S(2)}, u32[]{:S(2)}) collective-permute-start(f32[16,128]{1,0:T(8,128)S(1)} %get-tuple-element.57.own_cells), channel_id=1, source_target_pairs={{0,1},{1,0},{2,3},{3,2},{4,5},{5,4},{6,7},{7,6},{8,9},{9,8},{10,11... | collective-permute-start | bytes 24584 | tf_op jit(solution)/shard_map/ppermute | solution.py:440
  4.6 2.1 %shard_map.47 = (f32[4,4,64,128]{3,2,1,0:T(8,128)S(1)}, f32[4,4,64,128]{3,2,1,0:T(8,128)S(1)}, f32[8,16,8,128]{3,2,1,0:T(8,128)S(1)}, f32[8,16,8,128]{3,2,1,0:T(...) custom-call(s32[1,64]{1,0:T(1,128)S(1)} %get-tuple-element.53.loc, ...), custom_call_target="tpu_custom_call" | custom-call | flops 5242880 | bytes 3670016 | tf_op jit(solution)/shard_map/pallas_call | solution.py:338
  6.7 0.0 collective-permute-done.1.far
  6.7 0.0 collective-permute-done.near
  6.7 0.2 shard_map.48
  7.0 2.6 %collective-permute-start.4 = (f32[7,16,128]{2,1,0:T(8,128)S(1)}, f32[7,16,128]{2,1,0:T(8,128)S(1)}, u32[]{:S(2)}, u32[]{:S(2)}) collective-permute-start(f32[7,16,128]{2,1,0:T(8,128)S(1)} %get-tuple-element.66.after.refs_0_), channel_id=1, source_target_pairs={{0,12},{4,8},{8,4},{12,0},{16,28},{20,24},{24,20},{28,16},{1,13},{... | collective-permute-start | bytes 172040 | tf_op jit(solution)/shard_map/ppermute | solution.py:440
  9.5 0.4 %collective-permute-start.3 = (f32[7,16,128]{2,1,0:T(8,128)S(1)}, f32[7,16,128]{2,1,0:T(8,128)S(1)}, u32[]{:S(2)}, u32[]{:S(2)}) collective-permute-start(f32[7,16,128]{2,1,0:T(8,128)S(1)} %get-tuple-element.66.after.refs_0_), channel_id=1, source_target_pairs={{0,8},{4,12},{8,0},{12,4},{16,24},{20,28},{24,16},{28,20},{1,9},{5... | collective-permute-start | bytes 172040 | tf_op jit(solution)/shard_map/ppermute | solution.py:440
  10.0 0.5 %collective-permute-start.2 = (f32[7,16,128]{2,1,0:T(8,128)S(1)}, f32[7,16,128]{2,1,0:T(8,128)S(1)}, u32[]{:S(2)}, u32[]{:S(2)}) collective-permute-start(f32[7,16,128]{2,1,0:T(8,128)S(1)} %get-tuple-element.66.after.refs_0_), channel_id=1, source_target_pairs={{0,4},{4,0},{8,12},{12,8},{16,20},{20,16},{24,28},{28,24},{1,5},{5... | collective-permute-start | bytes 172040 | tf_op jit(solution)/shard_map/ppermute | solution.py:440
  10.5 1.4 %shard_map.49 = (f32[16,8,8,128]{3,2,1,0:T(8,128)S(1)}, f32[16,8,8,128]{3,2,1,0:T(8,128)S(1)}, f32[16,8,8,128]{3,2,1,0:T(8,128)S(1)}, f32[7,3,8,128]{3,2,1,0:T(8...) custom-call(f32[4,4,64,128]{3,2,1,0:T(8,128)S(1)} %get-tuple-element, ...), custom_call_target="tpu_custom_call" | custom-call | flops 2621440 | bytes 2097152 | tf_op jit(solution)/shard_map/pallas_call | solution.py:659
  11.9 0.2 shard_map.50
  12.1 0.3 %collective-permute-done.4.refs_3_ = f32[7,16,128]{2,1,0:T(8,128)S(1)} collective-permute-done((f32[7,16,128]{2,1,0:T(8,128)S(1)}, f32[7,16,128]{2,1,0:T(8,128)S(1)}, u32[]{:S(2)}, u32[]{:S(2)}) %collective-permute-start.4) | collective-permute-done | bytes 57376 | tf_op jit(solution)/shard_map/ppermute | solution.py:440
  12.4 1.3 %collective-permute-done.3.refs_2_ = f32[7,16,128]{2,1,0:T(8,128)S(1)} collective-permute-done((f32[7,16,128]{2,1,0:T(8,128)S(1)}, f32[7,16,128]{2,1,0:T(8,128)S(1)}, u32[]{:S(2)}, u32[]{:S(2)}) %collective-permute-start.3) | collective-permute-done | bytes 57376 | tf_op jit(solution)/shard_map/ppermute | solution.py:440
  13.7 0.4 %collective-permute-done.2.refs_1_ = f32[7,16,128]{2,1,0:T(8,128)S(1)} collective-permute-done((f32[7,16,128]{2,1,0:T(8,128)S(1)}, f32[7,16,128]{2,1,0:T(8,128)S(1)}, u32[]{:S(2)}, u32[]{:S(2)}) %collective-permute-start.2) | collective-permute-done | bytes 57376 | tf_op jit(solution)/shard_map/ppermute | solution.py:440
  14.2 0.1 shard_map.51
  14.2 2.7 %collective-permute-start.5 = (f32[3,16,128]{2,1,0:T(8,128)S(1)}, f32[3,16,128]{2,1,0:T(8,128)S(1)}, u32[]{:S(2)}, u32[]{:S(2)}) collective-permute-start(f32[3,16,128]{2,1,0:T(8,128)S(1)} %get-tuple-element.70.own), channel_id=1, source_target_pairs={{0,16},{4,20},{8,24},{12,28},{16,0},{20,4},{24,8},{28,12},{1,17},{... | collective-permute-start | bytes 73736 | tf_op jit(solution)/shard_map/ppermute | solution.py:440
  16.9 0.7 %shard_map.52 = (f32[4,128,256]{2,1,0:T(8,128)S(1)}, f32[4,128,256]{2,1,0:T(8,128)S(1)}, f32[4,256,128]{2,1,0:T(8,128)S(1)}, f32[4,256,128]{2,1,0:T(8,128)S(1)}, f32[2,2,128]{2,1,0:T(2,128)S(1)}) custom-call(f32[3,16,128]{2,1,0:T(8,128)S(1)} %get-tuple-element.71.refs_0_, f32[3,16,128]{2,1,0:T(8,128)S(1)} %get-tuple-element.72.refs_1_, ...), custom_call_target="tpu_custom_call" | custom-call | flops 1048576 | bytes 2097152 | tf_op jit(solution)/shard_map/pallas_call | solution.py:797
  17.6 1.4 %collective-permute-done.5.got = f32[3,16,128]{2,1,0:T(8,128)S(1)} collective-permute-done((f32[3,16,128]{2,1,0:T(8,128)S(1)}, f32[3,16,128]{2,1,0:T(8,128)S(1)}, u32[]{:S(2)}, u32[]{:S(2)}) %collective-permute-start.5) | collective-permute-done | bytes 24608 | tf_op jit(solution)/shard_map/ppermute | solution.py:440
  19.0 0.2 shard_map.53
  19.2 0.0 collective-permute-start.6
  19.3 0.4 %shard_map.54 = (f32[16,8,8,128]{3,2,1,0:T(8,128)S(1)}, f32[7,8,128]{2,1,0:T(8,128)S(1)}, f32[3,2,128]{2,1,0:T(2,128)S(1)}) custom-call(f32[4,128,256]{2,1,0:T(8,128)S(1)} %get-tuple-element.84.base, f32[4,128,256]{2,1,0:T(8,128)S(1)} %get-tuple-element.85.response, f32[16,128]{1,0:T(8,128)S(1)} %get-tuple-element.86.flux, ...), custom_call_target="tpu_custom_call" | custom-call | flops 1048576 | bytes 2097152 | tf_op jit(solution)/shard_map/pallas_call | solution.py:880
  19.7 0.8 %collective-permute-done.6.refs_1_ = f32[7,2,128]{2,1,0:T(2,128)S(1)} collective-permute-done((f32[7,2,128]{2,1,0:T(2,128)S(1)}, f32[7,2,128]{2,1,0:T(2,128)S(1)}, u32[]{:S(2)}, u32[]{:S(2)}) %collective-permute-start.6) | collective-permute-done | bytes 7200 | tf_op jit(solution)/shard_map/ppermute | solution.py:440
  20.4 0.7 %collective-permute-start.7 = (f32[3,2,128]{2,1,0:T(2,128)S(1)}, f32[3,2,128]{2,1,0:T(2,128)S(1)}, u32[]{:S(2)}, u32[]{:S(2)}) collective-permute-start(f32[3,2,128]{2,1,0:T(2,128)S(1)} %get-tuple-element.93.own), channel_id=1, source_target_pairs={{0,3},{1,2},{2,1},{3,0},{4,7},{5,6},{6,5},{7,4},{8,11},{9,10},{10,... | collective-permute-start | bytes 9224 | tf_op jit(solution)/shard_map/ppermute | solution.py:440
  21.1 0.8 %shard_map.56 = (f32[4,4,64,128]{3,2,1,0:T(8,128)S(1)}, f32[4,4,64,128]{3,2,1,0:T(8,128)S(1)}) custom-call(f32[3,2,128]{2,1,0:T(2,128)S(1)} %get-tuple-element.94.refs_0_, f32[16,8,8,128]{3,2,1,0:T(8,128)S(1)} %get-tuple-element.87.yw.refs_1_, f32[16,8,8,128]{3,2,1,0:T(8,128)S(1)} %get-tuple-element.92.refs_2_, ...), custom_call_target="tpu_custom_call" | custom-call | flops 1572864 | bytes 2621440 | tf_op jit(solution)/shard_map/pallas_call | solution.py:973
  21.9 1.6 %collective-permute-done.7.got = f32[3,2,128]{2,1,0:T(2,128)S(1)} collective-permute-done((f32[3,2,128]{2,1,0:T(2,128)S(1)}, f32[3,2,128]{2,1,0:T(2,128)S(1)}, u32[]{:S(2)}, u32[]{:S(2)}) %collective-permute-start.7) | collective-permute-done | bytes 3104 | tf_op jit(solution)/shard_map/ppermute | solution.py:440
  23.5 1.1 %shard_map.57 = f32[4,64,512]{2,1,0:T(8,128)} custom-call(f32[3,2,128]{2,1,0:T(2,128)S(1)} %get-tuple-element.93.own, f32[3,2,128]{2,1,0:T(2,128)S(1)} %collective-permute-done.7.got, f32[4,4,64,128]{3,2,1,0:T(8,128)S(1)} %get-tuple-element.99.base, f32[4,4,64,128]{3,2,1,0:T(8,128)S(1)} %get-tuple-element.100.response, ...), custom_call_target="tpu_custom_call" | custom-call | tf_op jit(solution)/shard_map/pallas_call | solution.py:1019
  (1 shorter events, 0.0 us)
Async XLA Ops:
  1.4 5.3 %collective-permute-start.1 = (f32[16,128]{1,0:T(8,128)S(1)}, f32[16,128]{1,0:T(8,128)S(1)}, u32[]{:S(2)}, u32[]{:S(2)}) collective-permute-start(f32[16,128]{1,0:T(8,128)S(1)} %get-tuple-element.57.own_cells), channel_id=1, source_target_pairs={{0,3},{1,2},{2,1},{3,0},{4,7},{5,6},{6,5},{7,4},{8,11},{9,10},{10,... | collective-permute-start | bytes 24584 | tf_op jit(solution)/shard_map/ppermute | solution.py:1033
  3.9 2.8 %collective-permute-start = (f32[16,128]{1,0:T(8,128)S(1)}, f32[16,128]{1,0:T(8,128)S(1)}, u32[]{:S(2)}, u32[]{:S(2)}) collective-permute-start(f32[16,128]{1,0:T(8,128)S(1)} %get-tuple-element.57.own_cells), channel_id=1, source_target_pairs={{0,1},{1,0},{2,3},{3,2},{4,5},{5,4},{6,7},{7,6},{8,9},{9,8},{10,11... | collective-permute-start | bytes 24584 | tf_op jit(solution)/shard_map/ppermute | solution.py:440
  7.0 5.4 %collective-permute-start.4 = (f32[7,16,128]{2,1,0:T(8,128)S(1)}, f32[7,16,128]{2,1,0:T(8,128)S(1)}, u32[]{:S(2)}, u32[]{:S(2)}) collective-permute-start(f32[7,16,128]{2,1,0:T(8,128)S(1)} %get-tuple-element.66.after.refs_0_), channel_id=1, source_target_pairs={{0,12},{4,8},{8,4},{12,0},{16,28},{20,24},{24,20},{28,16},{1,13},{... | collective-permute-start | bytes 172040 | tf_op jit(solution)/shard_map/ppermute | solution.py:440
  9.5 4.2 %collective-permute-start.3 = (f32[7,16,128]{2,1,0:T(8,128)S(1)}, f32[7,16,128]{2,1,0:T(8,128)S(1)}, u32[]{:S(2)}, u32[]{:S(2)}) collective-permute-start(f32[7,16,128]{2,1,0:T(8,128)S(1)} %get-tuple-element.66.after.refs_0_), channel_id=1, source_target_pairs={{0,8},{4,12},{8,0},{12,4},{16,24},{20,28},{24,16},{28,20},{1,9},{5... | collective-permute-start | bytes 172040 | tf_op jit(solution)/shard_map/ppermute | solution.py:440
  10.0 4.2 %collective-permute-start.2 = (f32[7,16,128]{2,1,0:T(8,128)S(1)}, f32[7,16,128]{2,1,0:T(8,128)S(1)}, u32[]{:S(2)}, u32[]{:S(2)}) collective-permute-start(f32[7,16,128]{2,1,0:T(8,128)S(1)} %get-tuple-element.66.after.refs_0_), channel_id=1, source_target_pairs={{0,4},{4,0},{8,12},{12,8},{16,20},{20,16},{24,28},{28,24},{1,5},{5... | collective-permute-start | bytes 172040 | tf_op jit(solution)/shard_map/ppermute | solution.py:440
  14.2 4.8 %collective-permute-start.5 = (f32[3,16,128]{2,1,0:T(8,128)S(1)}, f32[3,16,128]{2,1,0:T(8,128)S(1)}, u32[]{:S(2)}, u32[]{:S(2)}) collective-permute-start(f32[3,16,128]{2,1,0:T(8,128)S(1)} %get-tuple-element.70.own), channel_id=1, source_target_pairs={{0,16},{4,20},{8,24},{12,28},{16,0},{20,4},{24,8},{28,12},{1,17},{... | collective-permute-start | bytes 73736 | tf_op jit(solution)/shard_map/ppermute | solution.py:440
  19.2 1.2 %collective-permute-start.6 = (f32[7,2,128]{2,1,0:T(2,128)S(1)}, f32[7,2,128]{2,1,0:T(2,128)S(1)}, u32[]{:S(2)}, u32[]{:S(2)}) collective-permute-start(f32[7,2,128]{2,1,0:T(2,128)S(1)} %get-tuple-element.83.after.refs_0_), channel_id=1, source_target_pairs={{0,1},{1,0},{2,3},{3,2},{4,5},{5,4},{6,7},{7,6},{8,9},{9,8},{10,11... | collective-permute-start | bytes 21512 | tf_op jit(solution)/shard_map/ppermute | solution.py:440
  20.4 3.1 %collective-permute-start.7 = (f32[3,2,128]{2,1,0:T(2,128)S(1)}, f32[3,2,128]{2,1,0:T(2,128)S(1)}, u32[]{:S(2)}, u32[]{:S(2)}) collective-permute-start(f32[3,2,128]{2,1,0:T(2,128)S(1)} %get-tuple-element.93.own), channel_id=1, source_target_pairs={{0,3},{1,2},{2,1},{3,0},{4,7},{5,6},{6,5},{7,4},{8,11},{9,10},{10,... | collective-permute-start | bytes 9224 | tf_op jit(solution)/shard_map/ppermute | solution.py:440

commit v25 on v24

--- a/solution.py
+++ b/solution.py
@@ -13,7 +13,7 @@
 SUBLANES = 8
 F32 = jnp.float32
 MIB = 1024 * 1024
-OUT_COPIES = 4
+OUT_COPIES = 2
 ANYWHERE = pl.BlockSpec(memory_space=pl.ANY)
 IN_HBM = pl.BlockSpec(memory_space=pltpu.HBM)
 IN_VMEM = pl.BlockSpec(memory_space=pltpu.VMEM)

time: 24.7 us -> 24.7 us (level)
  no operation moved by 1% of the time
where the time goes in v25:
time: 24.7 us; the launch traced here: 24.6 us
  starting transfers between devices  10.1 us (41%)
  Pallas kernels  8.62 us (35%)
  waiting for transfers between devices  5.84 us (24%)
    ppermute x7, starting transfers between devices, swap(): return lax.ppermute(value, axis, [(i, i ^ flip) for i in range(count)])  7.59 us
    ppermute x7, waiting for transfers between devices, swap(): return lax.ppermute(value, axis, [(i, i ^ flip) for i in range(count)])  5.84 us
    ppermute x1, starting transfers between devices, per_device(): lax.ppermute(packed, 'gy', [(i, ((i + 1) % gy ^ 1) - 1 if i else gy - 1)...  2.47 us
    pallas_call x1, Pallas kernels, x_factor(): pl.pallas_call(functools.partial(x_factor_kernel, plate), in_specs=[IN_VM...  2.13 us
    pallas_call x1, Pallas kernels, load(): pl.pallas_call(load_kernel, in_specs=[IN_HBM] * 4, out_shape=[pltpu.VMEM(...  1.42 us
    pallas_call x1, Pallas kernels, y_factor(): pl.pallas_call(y_factor_kernel, in_specs=[IN_VMEM, ANYWHERE], out_shape=[...  1.4 us
    pallas_call x1, Pallas kernels, finish(): pl.pallas_call(functools.partial(finish_kernel, stages_of('gy')), out_sha...  1.08 us
    pallas_call x1, Pallas kernels, finish_prepare(): pl.pallas_call(functools.partial(finish_prepare_kernel, len(ties) + 1), o...  0.79 us
  transfers between devices with their start and end apart: 8, of which 6 were waited for; matrix products, arithmetic and copies ran while one was open for 0% of the time, Pallas kernels for 23%

profile of v25, /device:TPU:0, one launch (start us, length us, event | category | flops | bytes accessed | tf_op | source)
XLA Modules:
  0.0 24.6 jit_solution(6924449193906233557)
XLA Ops:
  0.0 1.4 %shard_map.46 = (f32[4,64,512]{2,1,0:T(8,128)S(1)}, f32[4,64,512]{2,1,0:T(8,128)S(1)}, s32[1,64]{1,0:T(1,128)S(1)}, f32[1,64]{1,0:T(1,128)S(1)}, f32[16,128]{1,0:T(8,128)S(1)}) custom-call(f32[4,64,512]{2,1,0:T(8,128)} %t_hbm.1, f32[4,64,512]{2,1,0:T(8,128)} %b_hbm.1, s32[1,64]{1,0:T(1,128)} %bitcast.2, f32[1,64]{1,0:T(1,128)} %bitcast.3), custom_call_target="tpu_custom_call" | custom-call | tf_op jit(solution)/shard_map/pallas_call | solution.py:184
  1.4 2.5 %collective-permute-start.1 = (f32[16,128]{1,0:T(8,128)S(1)}, f32[16,128]{1,0:T(8,128)S(1)}, u32[]{:S(2)}, u32[]{:S(2)}) collective-permute-start(f32[16,128]{1,0:T(8,128)S(1)} %get-tuple-element.57.own_cells), channel_id=1, source_target_pairs={{0,3},{1,2},{2,1},{3,0},{4,7},{5,6},{6,5},{7,4},{8,11},{9,10},{10,... | collective-permute-start | bytes 24584 | tf_op jit(solution)/shard_map/ppermute | solution.py:1033
  3.9 0.7 %collective-permute-start = (f32[16,128]{1,0:T(8,128)S(1)}, f32[16,128]{1,0:T(8,128)S(1)}, u32[]{:S(2)}, u32[]{:S(2)}) collective-permute-start(f32[16,128]{1,0:T(8,128)S(1)} %get-tuple-element.57.own_cells), channel_id=1, source_target_pairs={{0,1},{1,0},{2,3},{3,2},{4,5},{5,4},{6,7},{7,6},{8,9},{9,8},{10,11... | collective-permute-start | bytes 24584 | tf_op jit(solution)/shard_map/ppermute | solution.py:440
  4.6 2.1 %shard_map.47 = (f32[4,4,64,128]{3,2,1,0:T(8,128)S(1)}, f32[4,4,64,128]{3,2,1,0:T(8,128)S(1)}, f32[8,16,8,128]{3,2,1,0:T(8,128)S(1)}, f32[8,16,8,128]{3,2,1,0:T(...) custom-call(s32[1,64]{1,0:T(1,128)S(1)} %get-tuple-element.53.loc, ...), custom_call_target="tpu_custom_call" | custom-call | flops 5242880 | bytes 3670016 | tf_op jit(solution)/shard_map/pallas_call | solution.py:338
  6.7 0.0 collective-permute-done.1.far
  6.7 0.0 collective-permute-done.near
  6.7 0.2 shard_map.48
  7.0 2.6 %collective-permute-start.4 = (f32[7,16,128]{2,1,0:T(8,128)S(1)}, f32[7,16,128]{2,1,0:T(8,128)S(1)}, u32[]{:S(2)}, u32[]{:S(2)}) collective-permute-start(f32[7,16,128]{2,1,0:T(8,128)S(1)} %get-tuple-element.66.after.refs_0_), channel_id=1, source_target_pairs={{0,12},{4,8},{8,4},{12,0},{16,28},{20,24},{24,20},{28,16},{1,13},{... | collective-permute-start | bytes 172040 | tf_op jit(solution)/shard_map/ppermute | solution.py:440
  9.5 0.4 %collective-permute-start.3 = (f32[7,16,128]{2,1,0:T(8,128)S(1)}, f32[7,16,128]{2,1,0:T(8,128)S(1)}, u32[]{:S(2)}, u32[]{:S(2)}) collective-permute-start(f32[7,16,128]{2,1,0:T(8,128)S(1)} %get-tuple-element.66.after.refs_0_), channel_id=1, source_target_pairs={{0,8},{4,12},{8,0},{12,4},{16,24},{20,28},{24,16},{28,20},{1,9},{5... | collective-permute-start | bytes 172040 | tf_op jit(solution)/shard_map/ppermute | solution.py:440
  10.0 0.5 %collective-permute-start.2 = (f32[7,16,128]{2,1,0:T(8,128)S(1)}, f32[7,16,128]{2,1,0:T(8,128)S(1)}, u32[]{:S(2)}, u32[]{:S(2)}) collective-permute-start(f32[7,16,128]{2,1,0:T(8,128)S(1)} %get-tuple-element.66.after.refs_0_), channel_id=1, source_target_pairs={{0,4},{4,0},{8,12},{12,8},{16,20},{20,16},{24,28},{28,24},{1,5},{5... | collective-permute-start | bytes 172040 | tf_op jit(solution)/shard_map/ppermute | solution.py:440
  10.5 1.4 %shard_map.49 = (f32[16,8,8,128]{3,2,1,0:T(8,128)S(1)}, f32[16,8,8,128]{3,2,1,0:T(8,128)S(1)}, f32[16,8,8,128]{3,2,1,0:T(8,128)S(1)}, f32[7,3,8,128]{3,2,1,0:T(8...) custom-call(f32[4,4,64,128]{3,2,1,0:T(8,128)S(1)} %get-tuple-element, ...), custom_call_target="tpu_custom_call" | custom-call | flops 2621440 | bytes 2097152 | tf_op jit(solution)/shard_map/pallas_call | solution.py:659
  11.9 0.2 shard_map.50
  12.1 0.3 %collective-permute-done.4.refs_3_ = f32[7,16,128]{2,1,0:T(8,128)S(1)} collective-permute-done((f32[7,16,128]{2,1,0:T(8,128)S(1)}, f32[7,16,128]{2,1,0:T(8,128)S(1)}, u32[]{:S(2)}, u32[]{:S(2)}) %collective-permute-start.4) | collective-permute-done | bytes 57376 | tf_op jit(solution)/shard_map/ppermute | solution.py:440
  12.4 1.3 %collective-permute-done.3.refs_2_ = f32[7,16,128]{2,1,0:T(8,128)S(1)} collective-permute-done((f32[7,16,128]{2,1,0:T(8,128)S(1)}, f32[7,16,128]{2,1,0:T(8,128)S(1)}, u32[]{:S(2)}, u32[]{:S(2)}) %collective-permute-start.3) | collective-permute-done | bytes 57376 | tf_op jit(solution)/shard_map/ppermute | solution.py:440
  13.7 0.4 %collective-permute-done.2.refs_1_ = f32[7,16,128]{2,1,0:T(8,128)S(1)} collective-permute-done((f32[7,16,128]{2,1,0:T(8,128)S(1)}, f32[7,16,128]{2,1,0:T(8,128)S(1)}, u32[]{:S(2)}, u32[]{:S(2)}) %collective-permute-start.2) | collective-permute-done | bytes 57376 | tf_op jit(solution)/shard_map/ppermute | solution.py:440
  14.2 0.1 shard_map.51
  14.2 2.7 %collective-permute-start.5 = (f32[3,16,128]{2,1,0:T(8,128)S(1)}, f32[3,16,128]{2,1,0:T(8,128)S(1)}, u32[]{:S(2)}, u32[]{:S(2)}) collective-permute-start(f32[3,16,128]{2,1,0:T(8,128)S(1)} %get-tuple-element.70.own), channel_id=1, source_target_pairs={{0,16},{4,20},{8,24},{12,28},{16,0},{20,4},{24,8},{28,12},{1,17},{... | collective-permute-start | bytes 73736 | tf_op jit(solution)/shard_map/ppermute | solution.py:440
  16.9 0.7 %shard_map.52 = (f32[4,128,256]{2,1,0:T(8,128)S(1)}, f32[4,128,256]{2,1,0:T(8,128)S(1)}, f32[4,256,128]{2,1,0:T(8,128)S(1)}, f32[4,256,128]{2,1,0:T(8,128)S(1)}, f32[2,2,128]{2,1,0:T(2,128)S(1)}) custom-call(f32[3,16,128]{2,1,0:T(8,128)S(1)} %get-tuple-element.71.refs_0_, f32[3,16,128]{2,1,0:T(8,128)S(1)} %get-tuple-element.72.refs_1_, ...), custom_call_target="tpu_custom_call" | custom-call | flops 1048576 | bytes 2097152 | tf_op jit(solution)/shard_map/pallas_call | solution.py:797
  17.6 1.4 %collective-permute-done.5.got = f32[3,16,128]{2,1,0:T(8,128)S(1)} collective-permute-done((f32[3,16,128]{2,1,0:T(8,128)S(1)}, f32[3,16,128]{2,1,0:T(8,128)S(1)}, u32[]{:S(2)}, u32[]{:S(2)}) %collective-permute-start.5) | collective-permute-done | bytes 24608 | tf_op jit(solution)/shard_map/ppermute | solution.py:440
  19.0 0.2 shard_map.53
  19.2 0.0 collective-permute-start.6
  19.3 0.4 %shard_map.54 = (f32[16,8,8,128]{3,2,1,0:T(8,128)S(1)}, f32[7,8,128]{2,1,0:T(8,128)S(1)}, f32[3,2,128]{2,1,0:T(2,128)S(1)}) custom-call(f32[4,128,256]{2,1,0:T(8,128)S(1)} %get-tuple-element.84.base, f32[4,128,256]{2,1,0:T(8,128)S(1)} %get-tuple-element.85.response, f32[16,128]{1,0:T(8,128)S(1)} %get-tuple-element.86.flux, ...), custom_call_target="tpu_custom_call" | custom-call | flops 1048576 | bytes 2097152 | tf_op jit(solution)/shard_map/pallas_call | solution.py:880
  19.7 0.8 %collective-permute-done.6.refs_1_ = f32[7,2,128]{2,1,0:T(2,128)S(1)} collective-permute-done((f32[7,2,128]{2,1,0:T(2,128)S(1)}, f32[7,2,128]{2,1,0:T(2,128)S(1)}, u32[]{:S(2)}, u32[]{:S(2)}) %collective-permute-start.6) | collective-permute-done | bytes 7200 | tf_op jit(solution)/shard_map/ppermute | solution.py:440
  20.4 0.7 %collective-permute-start.7 = (f32[3,2,128]{2,1,0:T(2,128)S(1)}, f32[3,2,128]{2,1,0:T(2,128)S(1)}, u32[]{:S(2)}, u32[]{:S(2)}) collective-permute-start(f32[3,2,128]{2,1,0:T(2,128)S(1)} %get-tuple-element.93.own), channel_id=1, source_target_pairs={{0,3},{1,2},{2,1},{3,0},{4,7},{5,6},{6,5},{7,4},{8,11},{9,10},{10,... | collective-permute-start | bytes 9224 | tf_op jit(solution)/shard_map/ppermute | solution.py:440
  21.1 0.8 %shard_map.56 = (f32[4,4,64,128]{3,2,1,0:T(8,128)S(1)}, f32[4,4,64,128]{3,2,1,0:T(8,128)S(1)}) custom-call(f32[3,2,128]{2,1,0:T(2,128)S(1)} %get-tuple-element.94.refs_0_, f32[16,8,8,128]{3,2,1,0:T(8,128)S(1)} %get-tuple-element.87.yw.refs_1_, f32[16,8,8,128]{3,2,1,0:T(8,128)S(1)} %get-tuple-element.92.refs_2_, ...), custom_call_target="tpu_custom_call" | custom-call | flops 1572864 | bytes 2621440 | tf_op jit(solution)/shard_map/pallas_call | solution.py:973
  21.9 1.6 %collective-permute-done.7.got = f32[3,2,128]{2,1,0:T(2,128)S(1)} collective-permute-done((f32[3,2,128]{2,1,0:T(2,128)S(1)}, f32[3,2,128]{2,1,0:T(2,128)S(1)}, u32[]{:S(2)}, u32[]{:S(2)}) %collective-permute-start.7) | collective-permute-done | bytes 3104 | tf_op jit(solution)/shard_map/ppermute | solution.py:440
  23.5 1.1 %shard_map.57 = f32[4,64,512]{2,1,0:T(8,128)} custom-call(f32[3,2,128]{2,1,0:T(2,128)S(1)} %get-tuple-element.93.own, f32[3,2,128]{2,1,0:T(2,128)S(1)} %collective-permute-done.7.got, f32[4,4,64,128]{3,2,1,0:T(8,128)S(1)} %get-tuple-element.99.base, f32[4,4,64,128]{3,2,1,0:T(8,128)S(1)} %get-tuple-element.100.response, ...), custom_call_target="tpu_custom_call" | custom-call | tf_op jit(solution)/shard_map/pallas_call | solution.py:1019
  (1 shorter events, 0.0 us)
Async XLA Ops:
  1.4 5.3 %collective-permute-start.1 = (f32[16,128]{1,0:T(8,128)S(1)}, f32[16,128]{1,0:T(8,128)S(1)}, u32[]{:S(2)}, u32[]{:S(2)}) collective-permute-start(f32[16,128]{1,0:T(8,128)S(1)} %get-tuple-element.57.own_cells), channel_id=1, source_target_pairs={{0,3},{1,2},{2,1},{3,0},{4,7},{5,6},{6,5},{7,4},{8,11},{9,10},{10,... | collective-permute-start | bytes 24584 | tf_op jit(solution)/shard_map/ppermute | solution.py:1033
  3.9 2.8 %collective-permute-start = (f32[16,128]{1,0:T(8,128)S(1)}, f32[16,128]{1,0:T(8,128)S(1)}, u32[]{:S(2)}, u32[]{:S(2)}) collective-permute-start(f32[16,128]{1,0:T(8,128)S(1)} %get-tuple-element.57.own_cells), channel_id=1, source_target_pairs={{0,1},{1,0},{2,3},{3,2},{4,5},{5,4},{6,7},{7,6},{8,9},{9,8},{10,11... | collective-permute-start | bytes 24584 | tf_op jit(solution)/shard_map/ppermute | solution.py:440
  7.0 5.4 %collective-permute-start.4 = (f32[7,16,128]{2,1,0:T(8,128)S(1)}, f32[7,16,128]{2,1,0:T(8,128)S(1)}, u32[]{:S(2)}, u32[]{:S(2)}) collective-permute-start(f32[7,16,128]{2,1,0:T(8,128)S(1)} %get-tuple-element.66.after.refs_0_), channel_id=1, source_target_pairs={{0,12},{4,8},{8,4},{12,0},{16,28},{20,24},{24,20},{28,16},{1,13},{... | collective-permute-start | bytes 172040 | tf_op jit(solution)/shard_map/ppermute | solution.py:440
  9.5 4.2 %collective-permute-start.3 = (f32[7,16,128]{2,1,0:T(8,128)S(1)}, f32[7,16,128]{2,1,0:T(8,128)S(1)}, u32[]{:S(2)}, u32[]{:S(2)}) collective-permute-start(f32[7,16,128]{2,1,0:T(8,128)S(1)} %get-tuple-element.66.after.refs_0_), channel_id=1, source_target_pairs={{0,8},{4,12},{8,0},{12,4},{16,24},{20,28},{24,16},{28,20},{1,9},{5... | collective-permute-start | bytes 172040 | tf_op jit(solution)/shard_map/ppermute | solution.py:440
  10.0 4.2 %collective-permute-start.2 = (f32[7,16,128]{2,1,0:T(8,128)S(1)}, f32[7,16,128]{2,1,0:T(8,128)S(1)}, u32[]{:S(2)}, u32[]{:S(2)}) collective-permute-start(f32[7,16,128]{2,1,0:T(8,128)S(1)} %get-tuple-element.66.after.refs_0_), channel_id=1, source_target_pairs={{0,4},{4,0},{8,12},{12,8},{16,20},{20,16},{24,28},{28,24},{1,5},{5... | collective-permute-start | bytes 172040 | tf_op jit(solution)/shard_map/ppermute | solution.py:440
  14.2 4.8 %collective-permute-start.5 = (f32[3,16,128]{2,1,0:T(8,128)S(1)}, f32[3,16,128]{2,1,0:T(8,128)S(1)}, u32[]{:S(2)}, u32[]{:S(2)}) collective-permute-start(f32[3,16,128]{2,1,0:T(8,128)S(1)} %get-tuple-element.70.own), channel_id=1, source_target_pairs={{0,16},{4,20},{8,24},{12,28},{16,0},{20,4},{24,8},{28,12},{1,17},{... | collective-permute-start | bytes 73736 | tf_op jit(solution)/shard_map/ppermute | solution.py:440
  19.2 1.2 %collective-permute-start.6 = (f32[7,2,128]{2,1,0:T(2,128)S(1)}, f32[7,2,128]{2,1,0:T(2,128)S(1)}, u32[]{:S(2)}, u32[]{:S(2)}) collective-permute-start(f32[7,2,128]{2,1,0:T(2,128)S(1)} %get-tuple-element.83.after.refs_0_), channel_id=1, source_target_pairs={{0,1},{1,0},{2,3},{3,2},{4,5},{5,4},{6,7},{7,6},{8,9},{9,8},{10,11... | collective-permute-start | bytes 21512 | tf_op jit(solution)/shard_map/ppermute | solution.py:440
  20.4 3.1 %collective-permute-start.7 = (f32[3,2,128]{2,1,0:T(2,128)S(1)}, f32[3,2,128]{2,1,0:T(2,128)S(1)}, u32[]{:S(2)}, u32[]{:S(2)}) collective-permute-start(f32[3,2,128]{2,1,0:T(2,128)S(1)} %get-tuple-element.93.own), channel_id=1, source_target_pairs={{0,3},{1,2},{2,1},{3,0},{4,7},{5,6},{6,5},{7,4},{8,11},{9,10},{10,... | collective-permute-start | bytes 9224 | tf_op jit(solution)/shard_map/ppermute | solution.py:440

commit v26 on v24

--- a/solution.py
+++ b/solution.py
@@ -988,9 +988,8 @@
     each = LANES // rows
     pairs = sheets // each
     flux = top_flux("gy", stages, own, got)
-    spread = [
-        turned(to_x[...], flux[m : m + 1, :], LANES) for m in range(pairs)
-    ]
+    wide = turned(to_x[...], flux, LANES)
+    spread = [wide[:, part_of(m)] for m in range(pairs)]
     started = []
     block = rows // OUT_COPIES
     for n in range(OUT_COPIES):

time: 24.7 us -> 24.7 us (level)
  no operation moved by 1% of the time
where the time goes in v26:
time: 24.7 us; the launch traced here: 24.6 us
  starting transfers between devices  10.1 us (41%)
  Pallas kernels  8.62 us (35%)
  waiting for transfers between devices  5.84 us (24%)
    ppermute x7, starting transfers between devices, swap(): return lax.ppermute(value, axis, [(i, i ^ flip) for i in range(count)])  7.59 us
    ppermute x7, waiting for transfers between devices, swap(): return lax.ppermute(value, axis, [(i, i ^ flip) for i in range(count)])  5.84 us
    ppermute x1, starting transfers between devices, per_device(): lax.ppermute(packed, 'gy', [(i, ((i + 1) % gy ^ 1) - 1 if i else gy - 1)...  2.47 us
    pallas_call x1, Pallas kernels, x_factor(): pl.pallas_call(functools.partial(x_factor_kernel, plate), in_specs=[IN_VM...  2.13 us
    pallas_call x1, Pallas kernels, load(): pl.pallas_call(load_kernel, in_specs=[IN_HBM] * 4, out_shape=[pltpu.VMEM(...  1.42 us
    pallas_call x1, Pallas kernels, y_factor(): pl.pallas_call(y_factor_kernel, in_specs=[IN_VMEM, ANYWHERE], out_shape=[...  1.4 us
    pallas_call x1, Pallas kernels, finish(): pl.pallas_call(functools.partial(finish_kernel, stages_of('gy')), out_sha...  1.07 us
    pallas_call x1, Pallas kernels, finish_prepare(): pl.pallas_call(functools.partial(finish_prepare_kernel, len(ties) + 1), o...  0.79 us
  transfers between devices with their start and end apart: 8, of which 6 were waited for; matrix products, arithmetic and copies ran while one was open for 0% of the time, Pallas kernels for 23%

profile of v26, /device:TPU:0, one launch (start us, length us, event | category | flops | bytes accessed | tf_op | source)
XLA Modules:
  0.0 24.6 jit_solution(11028003989487755057)
XLA Ops:
  0.0 1.4 %shard_map.46 = (f32[4,64,512]{2,1,0:T(8,128)S(1)}, f32[4,64,512]{2,1,0:T(8,128)S(1)}, s32[1,64]{1,0:T(1,128)S(1)}, f32[1,64]{1,0:T(1,128)S(1)}, f32[16,128]{1,0:T(8,128)S(1)}) custom-call(f32[4,64,512]{2,1,0:T(8,128)} %t_hbm.1, f32[4,64,512]{2,1,0:T(8,128)} %b_hbm.1, s32[1,64]{1,0:T(1,128)} %bitcast.2, f32[1,64]{1,0:T(1,128)} %bitcast.3), custom_call_target="tpu_custom_call" | custom-call | tf_op jit(solution)/shard_map/pallas_call | solution.py:184
  1.4 2.5 %collective-permute-start.1 = (f32[16,128]{1,0:T(8,128)S(1)}, f32[16,128]{1,0:T(8,128)S(1)}, u32[]{:S(2)}, u32[]{:S(2)}) collective-permute-start(f32[16,128]{1,0:T(8,128)S(1)} %get-tuple-element.57.own_cells), channel_id=1, source_target_pairs={{0,3},{1,2},{2,1},{3,0},{4,7},{5,6},{6,5},{7,4},{8,11},{9,10},{10,... | collective-permute-start | bytes 24584 | tf_op jit(solution)/shard_map/ppermute | solution.py:1032
  3.9 0.7 %collective-permute-start = (f32[16,128]{1,0:T(8,128)S(1)}, f32[16,128]{1,0:T(8,128)S(1)}, u32[]{:S(2)}, u32[]{:S(2)}) collective-permute-start(f32[16,128]{1,0:T(8,128)S(1)} %get-tuple-element.57.own_cells), channel_id=1, source_target_pairs={{0,1},{1,0},{2,3},{3,2},{4,5},{5,4},{6,7},{7,6},{8,9},{9,8},{10,11... | collective-permute-start | bytes 24584 | tf_op jit(solution)/shard_map/ppermute | solution.py:440
  4.6 2.1 %shard_map.47 = (f32[4,4,64,128]{3,2,1,0:T(8,128)S(1)}, f32[4,4,64,128]{3,2,1,0:T(8,128)S(1)}, f32[8,16,8,128]{3,2,1,0:T(8,128)S(1)}, f32[8,16,8,128]{3,2,1,0:T(...) custom-call(s32[1,64]{1,0:T(1,128)S(1)} %get-tuple-element.53.loc, ...), custom_call_target="tpu_custom_call" | custom-call | flops 5242880 | bytes 3670016 | tf_op jit(solution)/shard_map/pallas_call | solution.py:338
  6.7 0.0 collective-permute-done.1.far
  6.7 0.0 collective-permute-done.near
  6.7 0.2 shard_map.48
  7.0 2.6 %collective-permute-start.4 = (f32[7,16,128]{2,1,0:T(8,128)S(1)}, f32[7,16,128]{2,1,0:T(8,128)S(1)}, u32[]{:S(2)}, u32[]{:S(2)}) collective-permute-start(f32[7,16,128]{2,1,0:T(8,128)S(1)} %get-tuple-element.66.after.refs_0_), channel_id=1, source_target_pairs={{0,12},{4,8},{8,4},{12,0},{16,28},{20,24},{24,20},{28,16},{1,13},{... | collective-permute-start | bytes 172040 | tf_op jit(solution)/shard_map/ppermute | solution.py:440
  9.5 0.4 %collective-permute-start.3 = (f32[7,16,128]{2,1,0:T(8,128)S(1)}, f32[7,16,128]{2,1,0:T(8,128)S(1)}, u32[]{:S(2)}, u32[]{:S(2)}) collective-permute-start(f32[7,16,128]{2,1,0:T(8,128)S(1)} %get-tuple-element.66.after.refs_0_), channel_id=1, source_target_pairs={{0,8},{4,12},{8,0},{12,4},{16,24},{20,28},{24,16},{28,20},{1,9},{5... | collective-permute-start | bytes 172040 | tf_op jit(solution)/shard_map/ppermute | solution.py:440
  10.0 0.5 %collective-permute-start.2 = (f32[7,16,128]{2,1,0:T(8,128)S(1)}, f32[7,16,128]{2,1,0:T(8,128)S(1)}, u32[]{:S(2)}, u32[]{:S(2)}) collective-permute-start(f32[7,16,128]{2,1,0:T(8,128)S(1)} %get-tuple-element.66.after.refs_0_), channel_id=1, source_target_pairs={{0,4},{4,0},{8,12},{12,8},{16,20},{20,16},{24,28},{28,24},{1,5},{5... | collective-permute-start | bytes 172040 | tf_op jit(solution)/shard_map/ppermute | solution.py:440
  10.5 1.4 %shard_map.49 = (f32[16,8,8,128]{3,2,1,0:T(8,128)S(1)}, f32[16,8,8,128]{3,2,1,0:T(8,128)S(1)}, f32[16,8,8,128]{3,2,1,0:T(8,128)S(1)}, f32[7,3,8,128]{3,2,1,0:T(8...) custom-call(f32[4,4,64,128]{3,2,1,0:T(8,128)S(1)} %get-tuple-element, ...), custom_call_target="tpu_custom_call" | custom-call | flops 2621440 | bytes 2097152 | tf_op jit(solution)/shard_map/pallas_call | solution.py:659
  11.9 0.2 shard_map.50
  12.1 0.3 %collective-permute-done.4.refs_3_ = f32[7,16,128]{2,1,0:T(8,128)S(1)} collective-permute-done((f32[7,16,128]{2,1,0:T(8,128)S(1)}, f32[7,16,128]{2,1,0:T(8,128)S(1)}, u32[]{:S(2)}, u32[]{:S(2)}) %collective-permute-start.4) | collective-permute-done | bytes 57376 | tf_op jit(solution)/shard_map/ppermute | solution.py:440
  12.4 1.3 %collective-permute-done.3.refs_2_ = f32[7,16,128]{2,1,0:T(8,128)S(1)} collective-permute-done((f32[7,16,128]{2,1,0:T(8,128)S(1)}, f32[7,16,128]{2,1,0:T(8,128)S(1)}, u32[]{:S(2)}, u32[]{:S(2)}) %collective-permute-start.3) | collective-permute-done | bytes 57376 | tf_op jit(solution)/shard_map/ppermute | solution.py:440
  13.7 0.4 %collective-permute-done.2.refs_1_ = f32[7,16,128]{2,1,0:T(8,128)S(1)} collective-permute-done((f32[7,16,128]{2,1,0:T(8,128)S(1)}, f32[7,16,128]{2,1,0:T(8,128)S(1)}, u32[]{:S(2)}, u32[]{:S(2)}) %collective-permute-start.2) | collective-permute-done | bytes 57376 | tf_op jit(solution)/shard_map/ppermute | solution.py:440
  14.2 0.1 shard_map.51
  14.2 2.7 %collective-permute-start.5 = (f32[3,16,128]{2,1,0:T(8,128)S(1)}, f32[3,16,128]{2,1,0:T(8,128)S(1)}, u32[]{:S(2)}, u32[]{:S(2)}) collective-permute-start(f32[3,16,128]{2,1,0:T(8,128)S(1)} %get-tuple-element.70.own), channel_id=1, source_target_pairs={{0,16},{4,20},{8,24},{12,28},{16,0},{20,4},{24,8},{28,12},{1,17},{... | collective-permute-start | bytes 73736 | tf_op jit(solution)/shard_map/ppermute | solution.py:440
  16.9 0.7 %shard_map.52 = (f32[4,128,256]{2,1,0:T(8,128)S(1)}, f32[4,128,256]{2,1,0:T(8,128)S(1)}, f32[4,256,128]{2,1,0:T(8,128)S(1)}, f32[4,256,128]{2,1,0:T(8,128)S(1)}, f32[2,2,128]{2,1,0:T(2,128)S(1)}) custom-call(f32[3,16,128]{2,1,0:T(8,128)S(1)} %get-tuple-element.71.refs_0_, f32[3,16,128]{2,1,0:T(8,128)S(1)} %get-tuple-element.72.refs_1_, ...), custom_call_target="tpu_custom_call" | custom-call | flops 1048576 | bytes 2097152 | tf_op jit(solution)/shard_map/pallas_call | solution.py:797
  17.6 1.4 %collective-permute-done.5.got = f32[3,16,128]{2,1,0:T(8,128)S(1)} collective-permute-done((f32[3,16,128]{2,1,0:T(8,128)S(1)}, f32[3,16,128]{2,1,0:T(8,128)S(1)}, u32[]{:S(2)}, u32[]{:S(2)}) %collective-permute-start.5) | collective-permute-done | bytes 24608 | tf_op jit(solution)/shard_map/ppermute | solution.py:440
  19.0 0.2 shard_map.53
  19.2 0.0 collective-permute-start.6
  19.3 0.4 %shard_map.54 = (f32[16,8,8,128]{3,2,1,0:T(8,128)S(1)}, f32[7,8,128]{2,1,0:T(8,128)S(1)}, f32[3,2,128]{2,1,0:T(2,128)S(1)}) custom-call(f32[4,128,256]{2,1,0:T(8,128)S(1)} %get-tuple-element.84.base, f32[4,128,256]{2,1,0:T(8,128)S(1)} %get-tuple-element.85.response, f32[16,128]{1,0:T(8,128)S(1)} %get-tuple-element.86.flux, ...), custom_call_target="tpu_custom_call" | custom-call | flops 1048576 | bytes 2097152 | tf_op jit(solution)/shard_map/pallas_call | solution.py:880
  19.7 0.8 %collective-permute-done.6.refs_1_ = f32[7,2,128]{2,1,0:T(2,128)S(1)} collective-permute-done((f32[7,2,128]{2,1,0:T(2,128)S(1)}, f32[7,2,128]{2,1,0:T(2,128)S(1)}, u32[]{:S(2)}, u32[]{:S(2)}) %collective-permute-start.6) | collective-permute-done | bytes 7200 | tf_op jit(solution)/shard_map/ppermute | solution.py:440
  20.4 0.7 %collective-permute-start.7 = (f32[3,2,128]{2,1,0:T(2,128)S(1)}, f32[3,2,128]{2,1,0:T(2,128)S(1)}, u32[]{:S(2)}, u32[]{:S(2)}) collective-permute-start(f32[3,2,128]{2,1,0:T(2,128)S(1)} %get-tuple-element.93.own), channel_id=1, source_target_pairs={{0,3},{1,2},{2,1},{3,0},{4,7},{5,6},{6,5},{7,4},{8,11},{9,10},{10,... | collective-permute-start | bytes 9224 | tf_op jit(solution)/shard_map/ppermute | solution.py:440
  21.1 0.8 %shard_map.56 = (f32[4,4,64,128]{3,2,1,0:T(8,128)S(1)}, f32[4,4,64,128]{3,2,1,0:T(8,128)S(1)}) custom-call(f32[3,2,128]{2,1,0:T(2,128)S(1)} %get-tuple-element.94.refs_0_, f32[16,8,8,128]{3,2,1,0:T(8,128)S(1)} %get-tuple-element.87.yw.refs_1_, f32[16,8,8,128]{3,2,1,0:T(8,128)S(1)} %get-tuple-element.92.refs_2_, ...), custom_call_target="tpu_custom_call" | custom-call | flops 1572864 | bytes 2621440 | tf_op jit(solution)/shard_map/pallas_call | solution.py:973
  21.9 1.6 %collective-permute-done.7.got = f32[3,2,128]{2,1,0:T(2,128)S(1)} collective-permute-done((f32[3,2,128]{2,1,0:T(2,128)S(1)}, f32[3,2,128]{2,1,0:T(2,128)S(1)}, u32[]{:S(2)}, u32[]{:S(2)}) %collective-permute-start.7) | collective-permute-done | bytes 3104 | tf_op jit(solution)/shard_map/ppermute | solution.py:440
  23.5 1.1 %shard_map.57 = f32[4,64,512]{2,1,0:T(8,128)} custom-call(f32[3,2,128]{2,1,0:T(2,128)S(1)} %get-tuple-element.93.own, f32[3,2,128]{2,1,0:T(2,128)S(1)} %collective-permute-done.7.got, f32[4,4,64,128]{3,2,1,0:T(8,128)S(1)} %get-tuple-element.99.base, f32[4,4,64,128]{3,2,1,0:T(8,128)S(1)} %get-tuple-element.100.response, ...), custom_call_target="tpu_custom_call" | custom-call | tf_op jit(solution)/shard_map/pallas_call | solution.py:1018
  (1 shorter events, 0.0 us)
Async XLA Ops:
  1.4 5.3 %collective-permute-start.1 = (f32[16,128]{1,0:T(8,128)S(1)}, f32[16,128]{1,0:T(8,128)S(1)}, u32[]{:S(2)}, u32[]{:S(2)}) collective-permute-start(f32[16,128]{1,0:T(8,128)S(1)} %get-tuple-element.57.own_cells), channel_id=1, source_target_pairs={{0,3},{1,2},{2,1},{3,0},{4,7},{5,6},{6,5},{7,4},{8,11},{9,10},{10,... | collective-permute-start | bytes 24584 | tf_op jit(solution)/shard_map/ppermute | solution.py:1032
  3.9 2.8 %collective-permute-start = (f32[16,128]{1,0:T(8,128)S(1)}, f32[16,128]{1,0:T(8,128)S(1)}, u32[]{:S(2)}, u32[]{:S(2)}) collective-permute-start(f32[16,128]{1,0:T(8,128)S(1)} %get-tuple-element.57.own_cells), channel_id=1, source_target_pairs={{0,1},{1,0},{2,3},{3,2},{4,5},{5,4},{6,7},{7,6},{8,9},{9,8},{10,11... | collective-permute-start | bytes 24584 | tf_op jit(solution)/shard_map/ppermute | solution.py:440
  7.0 5.4 %collective-permute-start.4 = (f32[7,16,128]{2,1,0:T(8,128)S(1)}, f32[7,16,128]{2,1,0:T(8,128)S(1)}, u32[]{:S(2)}, u32[]{:S(2)}) collective-permute-start(f32[7,16,128]{2,1,0:T(8,128)S(1)} %get-tuple-element.66.after.refs_0_), channel_id=1, source_target_pairs={{0,12},{4,8},{8,4},{12,0},{16,28},{20,24},{24,20},{28,16},{1,13},{... | collective-permute-start | bytes 172040 | tf_op jit(solution)/shard_map/ppermute | solution.py:440
  9.5 4.2 %collective-permute-start.3 = (f32[7,16,128]{2,1,0:T(8,128)S(1)}, f32[7,16,128]{2,1,0:T(8,128)S(1)}, u32[]{:S(2)}, u32[]{:S(2)}) collective-permute-start(f32[7,16,128]{2,1,0:T(8,128)S(1)} %get-tuple-element.66.after.refs_0_), channel_id=1, source_target_pairs={{0,8},{4,12},{8,0},{12,4},{16,24},{20,28},{24,16},{28,20},{1,9},{5... | collective-permute-start | bytes 172040 | tf_op jit(solution)/shard_map/ppermute | solution.py:440
  10.0 4.2 %collective-permute-start.2 = (f32[7,16,128]{2,1,0:T(8,128)S(1)}, f32[7,16,128]{2,1,0:T(8,128)S(1)}, u32[]{:S(2)}, u32[]{:S(2)}) collective-permute-start(f32[7,16,128]{2,1,0:T(8,128)S(1)} %get-tuple-element.66.after.refs_0_), channel_id=1, source_target_pairs={{0,4},{4,0},{8,12},{12,8},{16,20},{20,16},{24,28},{28,24},{1,5},{5... | collective-permute-start | bytes 172040 | tf_op jit(solution)/shard_map/ppermute | solution.py:440
  14.2 4.8 %collective-permute-start.5 = (f32[3,16,128]{2,1,0:T(8,128)S(1)}, f32[3,16,128]{2,1,0:T(8,128)S(1)}, u32[]{:S(2)}, u32[]{:S(2)}) collective-permute-start(f32[3,16,128]{2,1,0:T(8,128)S(1)} %get-tuple-element.70.own), channel_id=1, source_target_pairs={{0,16},{4,20},{8,24},{12,28},{16,0},{20,4},{24,8},{28,12},{1,17},{... | collective-permute-start | bytes 73736 | tf_op jit(solution)/shard_map/ppermute | solution.py:440
  19.2 1.2 %collective-permute-start.6 = (f32[7,2,128]{2,1,0:T(2,128)S(1)}, f32[7,2,128]{2,1,0:T(2,128)S(1)}, u32[]{:S(2)}, u32[]{:S(2)}) collective-permute-start(f32[7,2,128]{2,1,0:T(2,128)S(1)} %get-tuple-element.83.after.refs_0_), channel_id=1, source_target_pairs={{0,1},{1,0},{2,3},{3,2},{4,5},{5,4},{6,7},{7,6},{8,9},{9,8},{10,11... | collective-permute-start | bytes 21512 | tf_op jit(solution)/shard_map/ppermute | solution.py:440
  20.4 3.1 %collective-permute-start.7 = (f32[3,2,128]{2,1,0:T(2,128)S(1)}, f32[3,2,128]{2,1,0:T(2,128)S(1)}, u32[]{:S(2)}, u32[]{:S(2)}) collective-permute-start(f32[3,2,128]{2,1,0:T(2,128)S(1)} %get-tuple-element.93.own), channel_id=1, source_target_pairs={{0,3},{1,2},{2,1},{3,0},{4,7},{5,6},{6,5},{7,4},{8,11},{9,10},{10,... | collective-permute-start | bytes 9224 | tf_op jit(solution)/shard_map/ppermute | solution.py:440

commit v27 on v26

--- a/solution.py
+++ b/solution.py
@@ -464,9 +464,14 @@
     return first, second
 
 
+def flips_of(width):
+    return (1, 3, 2) if width == 2 else range(1, 1 << width)
+
+
 def join_kernel(axis, stage, width, last, *refs):
     count = 1 << width
-    blocks = [[refs[i][q] for q in range(7)] for i in range(count)]
+    at = {flip: 1 + n for n, flip in enumerate(flips_of(width))}
+    blocks = [[refs[at.get(i, 0)][q] for q in range(7)] for i in range(count)]
     send = refs[-1 - width]
     links = refs[-width:]
     for bit in range(width):
@@ -511,7 +516,7 @@
     links, stage = [], 0
     while stage < stages - 1:
         width = min(widest, stages - 1 - stage)
-        got = [swap(view, axis, flip << stage) for flip in range(1, 1 << width)]
+        got = [swap(view, axis, flip << stage) for flip in flips_of(width)]
         last = stage + width == stages - 1
         view, *ties = join_stage(view, got, axis, stage, width, last, meanwhile)
         links += ties

time: 24.7 us -> 25 us (1.012)
  transfers between devices with their start and end apart: 8 -> 8, of which waited for: 6 -> 5; matrix products, arithmetic and copies ran while one was open for 0% -> 0% of each run, Pallas kernels for 23% -> 23%
where the time goes in v27:
time: 25 us; the launch traced here: 24.8 us
  starting transfers between devices  10.1 us (40%)
  Pallas kernels  8.61 us (34%)
  waiting for transfers between devices  5.98 us (24%)
    ppermute x7, starting transfers between devices, swap(): return lax.ppermute(value, axis, [(i, i ^ flip) for i in range(count)])  7.66 us
    ppermute x7, waiting for transfers between devices, swap(): return lax.ppermute(value, axis, [(i, i ^ flip) for i in range(count)])  5.98 us
    ppermute x1, starting transfers between devices, per_device(): lax.ppermute(packed, 'gy', [(i, ((i + 1) % gy ^ 1) - 1 if i else gy - 1)...  2.47 us
    pallas_call x1, Pallas kernels, x_factor(): pl.pallas_call(functools.partial(x_factor_kernel, plate), in_specs=[IN_VM...  2.13 us
    pallas_call x1, Pallas kernels, load(): pl.pallas_call(load_kernel, in_specs=[IN_HBM] * 4, out_shape=[pltpu.VMEM(...  1.42 us
    pallas_call x1, Pallas kernels, y_factor(): pl.pallas_call(y_factor_kernel, in_specs=[IN_VMEM, ANYWHERE], out_shape=[...  1.4 us
    pallas_call x1, Pallas kernels, finish(): pl.pallas_call(functools.partial(finish_kernel, stages_of('gy')), out_sha...  1.07 us
    pallas_call x1, Pallas kernels, finish_prepare(): pl.pallas_call(functools.partial(finish_prepare_kernel, len(ties) + 1), o...  0.79 us
  transfers between devices with their start and end apart: 8, of which 5 were waited for; matrix products, arithmetic and copies ran while one was open for 0% of the time, Pallas kernels for 23%

profile of v27, /device:TPU:0, one launch (start us, length us, event | category | flops | bytes accessed | tf_op | source)
XLA Modules:
  0.0 24.8 jit_solution(16126378159268248280)
XLA Ops:
  0.0 1.4 %shard_map.46 = (f32[4,64,512]{2,1,0:T(8,128)S(1)}, f32[4,64,512]{2,1,0:T(8,128)S(1)}, s32[1,64]{1,0:T(1,128)S(1)}, f32[1,64]{1,0:T(1,128)S(1)}, f32[16,128]{1,0:T(8,128)S(1)}) custom-call(f32[4,64,512]{2,1,0:T(8,128)} %t_hbm.1, f32[4,64,512]{2,1,0:T(8,128)} %b_hbm.1, s32[1,64]{1,0:T(1,128)} %bitcast.2, f32[1,64]{1,0:T(1,128)} %bitcast.3), custom_call_target="tpu_custom_call" | custom-call | tf_op jit(solution)/shard_map/pallas_call | solution.py:184
  1.4 2.5 %collective-permute-start.1 = (f32[16,128]{1,0:T(8,128)S(1)}, f32[16,128]{1,0:T(8,128)S(1)}, u32[]{:S(2)}, u32[]{:S(2)}) collective-permute-start(f32[16,128]{1,0:T(8,128)S(1)} %get-tuple-element.57.own_cells), channel_id=1, source_target_pairs={{0,3},{1,2},{2,1},{3,0},{4,7},{5,6},{6,5},{7,4},{8,11},{9,10},{10,... | collective-permute-start | bytes 24584 | tf_op jit(solution)/shard_map/ppermute | solution.py:1037
  3.9 0.7 %collective-permute-start = (f32[16,128]{1,0:T(8,128)S(1)}, f32[16,128]{1,0:T(8,128)S(1)}, u32[]{:S(2)}, u32[]{:S(2)}) collective-permute-start(f32[16,128]{1,0:T(8,128)S(1)} %get-tuple-element.57.own_cells), channel_id=1, source_target_pairs={{0,1},{1,0},{2,3},{3,2},{4,5},{5,4},{6,7},{7,6},{8,9},{9,8},{10,11... | collective-permute-start | bytes 24584 | tf_op jit(solution)/shard_map/ppermute | solution.py:440
  4.6 2.1 %shard_map.47 = (f32[4,4,64,128]{3,2,1,0:T(8,128)S(1)}, f32[4,4,64,128]{3,2,1,0:T(8,128)S(1)}, f32[8,16,8,128]{3,2,1,0:T(8,128)S(1)}, f32[8,16,8,128]{3,2,1,0:T(...) custom-call(s32[1,64]{1,0:T(1,128)S(1)} %get-tuple-element.53.loc, ...), custom_call_target="tpu_custom_call" | custom-call | flops 5242880 | bytes 3670016 | tf_op jit(solution)/shard_map/pallas_call | solution.py:338
  6.7 0.0 collective-permute-done.1.far
  6.7 0.0 collective-permute-done.near
  6.7 0.2 shard_map.48
  7.0 1.6 %collective-permute-start.4 = (f32[7,16,128]{2,1,0:T(8,128)S(1)}, f32[7,16,128]{2,1,0:T(8,128)S(1)}, u32[]{:S(2)}, u32[]{:S(2)}) collective-permute-start(f32[7,16,128]{2,1,0:T(8,128)S(1)} %get-tuple-element.66.after.refs_0_), channel_id=1, source_target_pairs={{0,8},{4,12},{8,0},{12,4},{16,24},{20,28},{24,16},{28,20},{1,9},{5... | collective-permute-start | bytes 172040 | tf_op jit(solution)/shard_map/ppermute | solution.py:440
  8.6 1.4 %collective-permute-start.3 = (f32[7,16,128]{2,1,0:T(8,128)S(1)}, f32[7,16,128]{2,1,0:T(8,128)S(1)}, u32[]{:S(2)}, u32[]{:S(2)}) collective-permute-start(f32[7,16,128]{2,1,0:T(8,128)S(1)} %get-tuple-element.66.after.refs_0_), channel_id=1, source_target_pairs={{0,12},{4,8},{8,4},{12,0},{16,28},{20,24},{24,20},{28,16},{1,13},{... | collective-permute-start | bytes 172040 | tf_op jit(solution)/shard_map/ppermute | solution.py:440
  10.0 0.5 %collective-permute-start.2 = (f32[7,16,128]{2,1,0:T(8,128)S(1)}, f32[7,16,128]{2,1,0:T(8,128)S(1)}, u32[]{:S(2)}, u32[]{:S(2)}) collective-permute-start(f32[7,16,128]{2,1,0:T(8,128)S(1)} %get-tuple-element.66.after.refs_0_), channel_id=1, source_target_pairs={{0,4},{4,0},{8,12},{12,8},{16,20},{20,16},{24,28},{28,24},{1,5},{5... | collective-permute-start | bytes 172040 | tf_op jit(solution)/shard_map/ppermute | solution.py:440
  10.5 1.4 %shard_map.49 = (f32[16,8,8,128]{3,2,1,0:T(8,128)S(1)}, f32[16,8,8,128]{3,2,1,0:T(8,128)S(1)}, f32[16,8,8,128]{3,2,1,0:T(8,128)S(1)}, f32[7,3,8,128]{3,2,1,0:T(8...) custom-call(f32[4,4,64,128]{3,2,1,0:T(8,128)S(1)} %get-tuple-element, ...), custom_call_target="tpu_custom_call" | custom-call | flops 2621440 | bytes 2097152 | tf_op jit(solution)/shard_map/pallas_call | solution.py:664
  11.9 0.2 shard_map.50
  12.1 0.0 collective-permute-done.4.refs_3_
  12.1 1.6 %collective-permute-done.3.refs_2_ = f32[7,16,128]{2,1,0:T(8,128)S(1)} collective-permute-done((f32[7,16,128]{2,1,0:T(8,128)S(1)}, f32[7,16,128]{2,1,0:T(8,128)S(1)}, u32[]{:S(2)}, u32[]{:S(2)}) %collective-permute-start.3) | collective-permute-done | bytes 57376 | tf_op jit(solution)/shard_map/ppermute | solution.py:440
  13.8 0.6 %collective-permute-done.2.refs_1_ = f32[7,16,128]{2,1,0:T(8,128)S(1)} collective-permute-done((f32[7,16,128]{2,1,0:T(8,128)S(1)}, f32[7,16,128]{2,1,0:T(8,128)S(1)}, u32[]{:S(2)}, u32[]{:S(2)}) %collective-permute-start.2) | collective-permute-done | bytes 57376 | tf_op jit(solution)/shard_map/ppermute | solution.py:440
  14.4 0.1 shard_map.51
  14.4 2.7 %collective-permute-start.5 = (f32[3,16,128]{2,1,0:T(8,128)S(1)}, f32[3,16,128]{2,1,0:T(8,128)S(1)}, u32[]{:S(2)}, u32[]{:S(2)}) collective-permute-start(f32[3,16,128]{2,1,0:T(8,128)S(1)} %get-tuple-element.70.own), channel_id=1, source_target_pairs={{0,16},{4,20},{8,24},{12,28},{16,0},{20,4},{24,8},{28,12},{1,17},{... | collective-permute-start | bytes 73736 | tf_op jit(solution)/shard_map/ppermute | solution.py:440
  17.1 0.7 %shard_map.52 = (f32[4,128,256]{2,1,0:T(8,128)S(1)}, f32[4,128,256]{2,1,0:T(8,128)S(1)}, f32[4,256,128]{2,1,0:T(8,128)S(1)}, f32[4,256,128]{2,1,0:T(8,128)S(1)}, f32[2,2,128]{2,1,0:T(2,128)S(1)}) custom-call(f32[3,16,128]{2,1,0:T(8,128)S(1)} %get-tuple-element.71.refs_0_, f32[3,16,128]{2,1,0:T(8,128)S(1)} %get-tuple-element.72.refs_1_, ...), custom_call_target="tpu_custom_call" | custom-call | flops 1048576 | bytes 2097152 | tf_op jit(solution)/shard_map/pallas_call | solution.py:802
  17.8 1.4 %collective-permute-done.5.got = f32[3,16,128]{2,1,0:T(8,128)S(1)} collective-permute-done((f32[3,16,128]{2,1,0:T(8,128)S(1)}, f32[3,16,128]{2,1,0:T(8,128)S(1)}, u32[]{:S(2)}, u32[]{:S(2)}) %collective-permute-start.5) | collective-permute-done | bytes 24608 | tf_op jit(solution)/shard_map/ppermute | solution.py:440
  19.2 0.2 shard_map.53
  19.5 0.0 collective-permute-start.6
  19.5 0.4 %shard_map.54 = (f32[16,8,8,128]{3,2,1,0:T(8,128)S(1)}, f32[7,8,128]{2,1,0:T(8,128)S(1)}, f32[3,2,128]{2,1,0:T(2,128)S(1)}) custom-call(f32[4,128,256]{2,1,0:T(8,128)S(1)} %get-tuple-element.84.base, f32[4,128,256]{2,1,0:T(8,128)S(1)} %get-tuple-element.85.response, f32[16,128]{1,0:T(8,128)S(1)} %get-tuple-element.86.flux, ...), custom_call_target="tpu_custom_call" | custom-call | flops 1048576 | bytes 2097152 | tf_op jit(solution)/shard_map/pallas_call | solution.py:885
  19.9 0.8 %collective-permute-done.6.refs_1_ = f32[7,2,128]{2,1,0:T(2,128)S(1)} collective-permute-done((f32[7,2,128]{2,1,0:T(2,128)S(1)}, f32[7,2,128]{2,1,0:T(2,128)S(1)}, u32[]{:S(2)}, u32[]{:S(2)}) %collective-permute-start.6) | collective-permute-done | bytes 7200 | tf_op jit(solution)/shard_map/ppermute | solution.py:440
  20.7 0.8 %collective-permute-start.7 = (f32[3,2,128]{2,1,0:T(2,128)S(1)}, f32[3,2,128]{2,1,0:T(2,128)S(1)}, u32[]{:S(2)}, u32[]{:S(2)}) collective-permute-start(f32[3,2,128]{2,1,0:T(2,128)S(1)} %get-tuple-element.93.own), channel_id=1, source_target_pairs={{0,3},{1,2},{2,1},{3,0},{4,7},{5,6},{6,5},{7,4},{8,11},{9,10},{10,... | collective-permute-start | bytes 9224 | tf_op jit(solution)/shard_map/ppermute | solution.py:440
  21.4 0.8 %shard_map.56 = (f32[4,4,64,128]{3,2,1,0:T(8,128)S(1)}, f32[4,4,64,128]{3,2,1,0:T(8,128)S(1)}) custom-call(f32[3,2,128]{2,1,0:T(2,128)S(1)} %get-tuple-element.94.refs_0_, f32[16,8,8,128]{3,2,1,0:T(8,128)S(1)} %get-tuple-element.87.yw.refs_1_, f32[16,8,8,128]{3,2,1,0:T(8,128)S(1)} %get-tuple-element.92.refs_2_, ...), custom_call_target="tpu_custom_call" | custom-call | flops 1572864 | bytes 2621440 | tf_op jit(solution)/shard_map/pallas_call | solution.py:978
  22.2 1.5 %collective-permute-done.7.got = f32[3,2,128]{2,1,0:T(2,128)S(1)} collective-permute-done((f32[3,2,128]{2,1,0:T(2,128)S(1)}, f32[3,2,128]{2,1,0:T(2,128)S(1)}, u32[]{:S(2)}, u32[]{:S(2)}) %collective-permute-start.7) | collective-permute-done | bytes 3104 | tf_op jit(solution)/shard_map/ppermute | solution.py:440
  23.7 1.1 %shard_map.57 = f32[4,64,512]{2,1,0:T(8,128)} custom-call(f32[3,2,128]{2,1,0:T(2,128)S(1)} %get-tuple-element.93.own, f32[3,2,128]{2,1,0:T(2,128)S(1)} %collective-permute-done.7.got, f32[4,4,64,128]{3,2,1,0:T(8,128)S(1)} %get-tuple-element.99.base, f32[4,4,64,128]{3,2,1,0:T(8,128)S(1)} %get-tuple-element.100.response, ...), custom_call_target="tpu_custom_call" | custom-call | tf_op jit(solution)/shard_map/pallas_call | solution.py:1023
  (1 shorter events, 0.0 us)
Async XLA Ops:
  1.4 5.3 %collective-permute-start.1 = (f32[16,128]{1,0:T(8,128)S(1)}, f32[16,128]{1,0:T(8,128)S(1)}, u32[]{:S(2)}, u32[]{:S(2)}) collective-permute-start(f32[16,128]{1,0:T(8,128)S(1)} %get-tuple-element.57.own_cells), channel_id=1, source_target_pairs={{0,3},{1,2},{2,1},{3,0},{4,7},{5,6},{6,5},{7,4},{8,11},{9,10},{10,... | collective-permute-start | bytes 24584 | tf_op jit(solution)/shard_map/ppermute | solution.py:1037
  3.9 2.8 %collective-permute-start = (f32[16,128]{1,0:T(8,128)S(1)}, f32[16,128]{1,0:T(8,128)S(1)}, u32[]{:S(2)}, u32[]{:S(2)}) collective-permute-start(f32[16,128]{1,0:T(8,128)S(1)} %get-tuple-element.57.own_cells), channel_id=1, source_target_pairs={{0,1},{1,0},{2,3},{3,2},{4,5},{5,4},{6,7},{7,6},{8,9},{9,8},{10,11... | collective-permute-start | bytes 24584 | tf_op jit(solution)/shard_map/ppermute | solution.py:440
  7.0 5.1 %collective-permute-start.4 = (f32[7,16,128]{2,1,0:T(8,128)S(1)}, f32[7,16,128]{2,1,0:T(8,128)S(1)}, u32[]{:S(2)}, u32[]{:S(2)}) collective-permute-start(f32[7,16,128]{2,1,0:T(8,128)S(1)} %get-tuple-element.66.after.refs_0_), channel_id=1, source_target_pairs={{0,8},{4,12},{8,0},{12,4},{16,24},{20,28},{24,16},{28,20},{1,9},{5... | collective-permute-start | bytes 172040 | tf_op jit(solution)/shard_map/ppermute | solution.py:440
  8.6 5.1 %collective-permute-start.3 = (f32[7,16,128]{2,1,0:T(8,128)S(1)}, f32[7,16,128]{2,1,0:T(8,128)S(1)}, u32[]{:S(2)}, u32[]{:S(2)}) collective-permute-start(f32[7,16,128]{2,1,0:T(8,128)S(1)} %get-tuple-element.66.after.refs_0_), channel_id=1, source_target_pairs={{0,12},{4,8},{8,4},{12,0},{16,28},{20,24},{24,20},{28,16},{1,13},{... | collective-permute-start | bytes 172040 | tf_op jit(solution)/shard_map/ppermute | solution.py:440
  10.0 4.4 %collective-permute-start.2 = (f32[7,16,128]{2,1,0:T(8,128)S(1)}, f32[7,16,128]{2,1,0:T(8,128)S(1)}, u32[]{:S(2)}, u32[]{:S(2)}) collective-permute-start(f32[7,16,128]{2,1,0:T(8,128)S(1)} %get-tuple-element.66.after.refs_0_), channel_id=1, source_target_pairs={{0,4},{4,0},{8,12},{12,8},{16,20},{20,16},{24,28},{28,24},{1,5},{5... | collective-permute-start | bytes 172040 | tf_op jit(solution)/shard_map/ppermute | solution.py:440
  14.4 4.8 %collective-permute-start.5 = (f32[3,16,128]{2,1,0:T(8,128)S(1)}, f32[3,16,128]{2,1,0:T(8,128)S(1)}, u32[]{:S(2)}, u32[]{:S(2)}) collective-permute-start(f32[3,16,128]{2,1,0:T(8,128)S(1)} %get-tuple-element.70.own), channel_id=1, source_target_pairs={{0,16},{4,20},{8,24},{12,28},{16,0},{20,4},{24,8},{28,12},{1,17},{... | collective-permute-start | bytes 73736 | tf_op jit(solution)/shard_map/ppermute | solution.py:440
  19.5 1.2 %collective-permute-start.6 = (f32[7,2,128]{2,1,0:T(2,128)S(1)}, f32[7,2,128]{2,1,0:T(2,128)S(1)}, u32[]{:S(2)}, u32[]{:S(2)}) collective-permute-start(f32[7,2,128]{2,1,0:T(2,128)S(1)} %get-tuple-element.83.after.refs_0_), channel_id=1, source_target_pairs={{0,1},{1,0},{2,3},{3,2},{4,5},{5,4},{6,7},{7,6},{8,9},{9,8},{10,11... | collective-permute-start | bytes 21512 | tf_op jit(solution)/shard_map/ppermute | solution.py:440
  20.7 3.1 %collective-permute-start.7 = (f32[3,2,128]{2,1,0:T(2,128)S(1)}, f32[3,2,128]{2,1,0:T(2,128)S(1)}, u32[]{:S(2)}, u32[]{:S(2)}) collective-permute-start(f32[3,2,128]{2,1,0:T(2,128)S(1)} %get-tuple-element.93.own), channel_id=1, source_target_pairs={{0,3},{1,2},{2,1},{3,0},{4,7},{5,6},{6,5},{7,4},{8,11},{9,10},{10,... | collective-permute-start | bytes 9224 | tf_op jit(solution)/shard_map/ppermute | solution.py:440

commit v28 on v26

--- a/solution.py
+++ b/solution.py
@@ -826,9 +826,10 @@
                 total[z] = part if y == 0 else total[z] + part
     for n, q in enumerate(COEFS):
         send[q] = view[n]
+    put_sums(r_s, jnp.concatenate(totals[0] + totals[1], 0))
+    pairs = view.shape[1]
     for i, q in enumerate((FIRST, LAST)):
-        put_sums(r_s.at[i], jnp.concatenate(totals[i], 0))
-        send[q] = fixed[i] + r_s[i]
+        send[q] = fixed[i] + r_s[i * pairs : (i + 1) * pairs, :]
 
 
 def y_target(own, got, to_first, to_last, fixed, view):
@@ -836,7 +837,7 @@
     return pl.pallas_call(
         functools.partial(y_target_kernel, stages_of("gx")),
         out_shape=[shape_of(*own.shape[1:]), shape_of(7, pairs, LANES)],
-        scratch_shapes=[pltpu.VMEM((2, pairs, LANES), F32)],
+        scratch_shapes=[pltpu.VMEM((2 * pairs, LANES), F32)],
         compiler_params=params(),
     )(own, got, to_first, to_last, fixed, view)
 

time: 24.7 us -> 24.7 us (level)
  no operation moved by 1% of the time
where the time goes in v28:
time: 24.7 us; the launch traced here: 24.6 us
  starting transfers between devices  10.1 us (41%)
  Pallas kernels  8.62 us (35%)
  waiting for transfers between devices  5.84 us (24%)
    ppermute x7, starting transfers between devices, swap(): return lax.ppermute(value, axis, [(i, i ^ flip) for i in range(count)])  7.59 us
    ppermute x7, waiting for transfers between devices, swap(): return lax.ppermute(value, axis, [(i, i ^ flip) for i in range(count)])  5.84 us
    ppermute x1, starting transfers between devices, per_device(): lax.ppermute(packed, 'gy', [(i, ((i + 1) % gy ^ 1) - 1 if i else gy - 1)...  2.47 us
    pallas_call x1, Pallas kernels, x_factor(): pl.pallas_call(functools.partial(x_factor_kernel, plate), in_specs=[IN_VM...  2.13 us
    pallas_call x1, Pallas kernels, load(): pl.pallas_call(load_kernel, in_specs=[IN_HBM] * 4, out_shape=[pltpu.VMEM(...  1.42 us
    pallas_call x1, Pallas kernels, y_factor(): pl.pallas_call(y_factor_kernel, in_specs=[IN_VMEM, ANYWHERE], out_shape=[...  1.4 us
    pallas_call x1, Pallas kernels, finish(): pl.pallas_call(functools.partial(finish_kernel, stages_of('gy')), out_sha...  1.07 us
    pallas_call x1, Pallas kernels, finish_prepare(): pl.pallas_call(functools.partial(finish_prepare_kernel, len(ties) + 1), o...  0.79 us
  transfers between devices with their start and end apart: 8, of which 6 were waited for; matrix products, arithmetic and copies ran while one was open for 0% of the time, Pallas kernels for 23%

profile of v28, /device:TPU:0, one launch (start us, length us, event | category | flops | bytes accessed | tf_op | source)
XLA Modules:
  0.0 24.6 jit_solution(11028003989487755057)
XLA Ops:
  0.0 1.4 %shard_map.46 = (f32[4,64,512]{2,1,0:T(8,128)S(1)}, f32[4,64,512]{2,1,0:T(8,128)S(1)}, s32[1,64]{1,0:T(1,128)S(1)}, f32[1,64]{1,0:T(1,128)S(1)}, f32[16,128]{1,0:T(8,128)S(1)}) custom-call(f32[4,64,512]{2,1,0:T(8,128)} %t_hbm.1, f32[4,64,512]{2,1,0:T(8,128)} %b_hbm.1, s32[1,64]{1,0:T(1,128)} %bitcast.2, f32[1,64]{1,0:T(1,128)} %bitcast.3), custom_call_target="tpu_custom_call" | custom-call | tf_op jit(solution)/shard_map/pallas_call | solution.py:184
  1.4 2.5 %collective-permute-start.1 = (f32[16,128]{1,0:T(8,128)S(1)}, f32[16,128]{1,0:T(8,128)S(1)}, u32[]{:S(2)}, u32[]{:S(2)}) collective-permute-start(f32[16,128]{1,0:T(8,128)S(1)} %get-tuple-element.57.own_cells), channel_id=1, source_target_pairs={{0,3},{1,2},{2,1},{3,0},{4,7},{5,6},{6,5},{7,4},{8,11},{9,10},{10,... | collective-permute-start | bytes 24584 | tf_op jit(solution)/shard_map/ppermute | solution.py:1033
  3.9 0.7 %collective-permute-start = (f32[16,128]{1,0:T(8,128)S(1)}, f32[16,128]{1,0:T(8,128)S(1)}, u32[]{:S(2)}, u32[]{:S(2)}) collective-permute-start(f32[16,128]{1,0:T(8,128)S(1)} %get-tuple-element.57.own_cells), channel_id=1, source_target_pairs={{0,1},{1,0},{2,3},{3,2},{4,5},{5,4},{6,7},{7,6},{8,9},{9,8},{10,11... | collective-permute-start | bytes 24584 | tf_op jit(solution)/shard_map/ppermute | solution.py:440
  4.6 2.1 %shard_map.47 = (f32[4,4,64,128]{3,2,1,0:T(8,128)S(1)}, f32[4,4,64,128]{3,2,1,0:T(8,128)S(1)}, f32[8,16,8,128]{3,2,1,0:T(8,128)S(1)}, f32[8,16,8,128]{3,2,1,0:T(...) custom-call(s32[1,64]{1,0:T(1,128)S(1)} %get-tuple-element.53.loc, ...), custom_call_target="tpu_custom_call" | custom-call | flops 5242880 | bytes 3670016 | tf_op jit(solution)/shard_map/pallas_call | solution.py:338
  6.7 0.0 collective-permute-done.1.far
  6.7 0.0 collective-permute-done.near
  6.7 0.2 shard_map.48
  7.0 2.6 %collective-permute-start.4 = (f32[7,16,128]{2,1,0:T(8,128)S(1)}, f32[7,16,128]{2,1,0:T(8,128)S(1)}, u32[]{:S(2)}, u32[]{:S(2)}) collective-permute-start(f32[7,16,128]{2,1,0:T(8,128)S(1)} %get-tuple-element.66.after.refs_0_), channel_id=1, source_target_pairs={{0,12},{4,8},{8,4},{12,0},{16,28},{20,24},{24,20},{28,16},{1,13},{... | collective-permute-start | bytes 172040 | tf_op jit(solution)/shard_map/ppermute | solution.py:440
  9.5 0.4 %collective-permute-start.3 = (f32[7,16,128]{2,1,0:T(8,128)S(1)}, f32[7,16,128]{2,1,0:T(8,128)S(1)}, u32[]{:S(2)}, u32[]{:S(2)}) collective-permute-start(f32[7,16,128]{2,1,0:T(8,128)S(1)} %get-tuple-element.66.after.refs_0_), channel_id=1, source_target_pairs={{0,8},{4,12},{8,0},{12,4},{16,24},{20,28},{24,16},{28,20},{1,9},{5... | collective-permute-start | bytes 172040 | tf_op jit(solution)/shard_map/ppermute | solution.py:440
  10.0 0.5 %collective-permute-start.2 = (f32[7,16,128]{2,1,0:T(8,128)S(1)}, f32[7,16,128]{2,1,0:T(8,128)S(1)}, u32[]{:S(2)}, u32[]{:S(2)}) collective-permute-start(f32[7,16,128]{2,1,0:T(8,128)S(1)} %get-tuple-element.66.after.refs_0_), channel_id=1, source_target_pairs={{0,4},{4,0},{8,12},{12,8},{16,20},{20,16},{24,28},{28,24},{1,5},{5... | collective-permute-start | bytes 172040 | tf_op jit(solution)/shard_map/ppermute | solution.py:440
  10.5 1.4 %shard_map.49 = (f32[16,8,8,128]{3,2,1,0:T(8,128)S(1)}, f32[16,8,8,128]{3,2,1,0:T(8,128)S(1)}, f32[16,8,8,128]{3,2,1,0:T(8,128)S(1)}, f32[7,3,8,128]{3,2,1,0:T(8...) custom-call(f32[4,4,64,128]{3,2,1,0:T(8,128)S(1)} %get-tuple-element, ...), custom_call_target="tpu_custom_call" | custom-call | flops 2621440 | bytes 2097152 | tf_op jit(solution)/shard_map/pallas_call | solution.py:659
  11.9 0.2 shard_map.50
  12.1 0.3 %collective-permute-done.4.refs_3_ = f32[7,16,128]{2,1,0:T(8,128)S(1)} collective-permute-done((f32[7,16,128]{2,1,0:T(8,128)S(1)}, f32[7,16,128]{2,1,0:T(8,128)S(1)}, u32[]{:S(2)}, u32[]{:S(2)}) %collective-permute-start.4) | collective-permute-done | bytes 57376 | tf_op jit(solution)/shard_map/ppermute | solution.py:440
  12.4 1.3 %collective-permute-done.3.refs_2_ = f32[7,16,128]{2,1,0:T(8,128)S(1)} collective-permute-done((f32[7,16,128]{2,1,0:T(8,128)S(1)}, f32[7,16,128]{2,1,0:T(8,128)S(1)}, u32[]{:S(2)}, u32[]{:S(2)}) %collective-permute-start.3) | collective-permute-done | bytes 57376 | tf_op jit(solution)/shard_map/ppermute | solution.py:440
  13.7 0.4 %collective-permute-done.2.refs_1_ = f32[7,16,128]{2,1,0:T(8,128)S(1)} collective-permute-done((f32[7,16,128]{2,1,0:T(8,128)S(1)}, f32[7,16,128]{2,1,0:T(8,128)S(1)}, u32[]{:S(2)}, u32[]{:S(2)}) %collective-permute-start.2) | collective-permute-done | bytes 57376 | tf_op jit(solution)/shard_map/ppermute | solution.py:440
  14.2 0.1 shard_map.51
  14.2 2.7 %collective-permute-start.5 = (f32[3,16,128]{2,1,0:T(8,128)S(1)}, f32[3,16,128]{2,1,0:T(8,128)S(1)}, u32[]{:S(2)}, u32[]{:S(2)}) collective-permute-start(f32[3,16,128]{2,1,0:T(8,128)S(1)} %get-tuple-element.70.own), channel_id=1, source_target_pairs={{0,16},{4,20},{8,24},{12,28},{16,0},{20,4},{24,8},{28,12},{1,17},{... | collective-permute-start | bytes 73736 | tf_op jit(solution)/shard_map/ppermute | solution.py:440
  16.9 0.7 %shard_map.52 = (f32[4,128,256]{2,1,0:T(8,128)S(1)}, f32[4,128,256]{2,1,0:T(8,128)S(1)}, f32[4,256,128]{2,1,0:T(8,128)S(1)}, f32[4,256,128]{2,1,0:T(8,128)S(1)}, f32[2,2,128]{2,1,0:T(2,128)S(1)}) custom-call(f32[3,16,128]{2,1,0:T(8,128)S(1)} %get-tuple-element.71.refs_0_, f32[3,16,128]{2,1,0:T(8,128)S(1)} %get-tuple-element.72.refs_1_, ...), custom_call_target="tpu_custom_call" | custom-call | flops 1048576 | bytes 2097152 | tf_op jit(solution)/shard_map/pallas_call | solution.py:797
  17.6 1.4 %collective-permute-done.5.got = f32[3,16,128]{2,1,0:T(8,128)S(1)} collective-permute-done((f32[3,16,128]{2,1,0:T(8,128)S(1)}, f32[3,16,128]{2,1,0:T(8,128)S(1)}, u32[]{:S(2)}, u32[]{:S(2)}) %collective-permute-start.5) | collective-permute-done | bytes 24608 | tf_op jit(solution)/shard_map/ppermute | solution.py:440
  19.0 0.2 shard_map.53
  19.2 0.0 collective-permute-start.6
  19.3 0.4 %shard_map.54 = (f32[16,8,8,128]{3,2,1,0:T(8,128)S(1)}, f32[7,8,128]{2,1,0:T(8,128)S(1)}, f32[3,2,128]{2,1,0:T(2,128)S(1)}) custom-call(f32[4,128,256]{2,1,0:T(8,128)S(1)} %get-tuple-element.84.base, f32[4,128,256]{2,1,0:T(8,128)S(1)} %get-tuple-element.85.response, f32[16,128]{1,0:T(8,128)S(1)} %get-tuple-element.86.flux, ...), custom_call_target="tpu_custom_call" | custom-call | flops 1048576 | bytes 2097152 | tf_op jit(solution)/shard_map/pallas_call | solution.py:881
  19.7 0.8 %collective-permute-done.6.refs_1_ = f32[7,2,128]{2,1,0:T(2,128)S(1)} collective-permute-done((f32[7,2,128]{2,1,0:T(2,128)S(1)}, f32[7,2,128]{2,1,0:T(2,128)S(1)}, u32[]{:S(2)}, u32[]{:S(2)}) %collective-permute-start.6) | collective-permute-done | bytes 7200 | tf_op jit(solution)/shard_map/ppermute | solution.py:440
  20.4 0.7 %collective-permute-start.7 = (f32[3,2,128]{2,1,0:T(2,128)S(1)}, f32[3,2,128]{2,1,0:T(2,128)S(1)}, u32[]{:S(2)}, u32[]{:S(2)}) collective-permute-start(f32[3,2,128]{2,1,0:T(2,128)S(1)} %get-tuple-element.93.own), channel_id=1, source_target_pairs={{0,3},{1,2},{2,1},{3,0},{4,7},{5,6},{6,5},{7,4},{8,11},{9,10},{10,... | collective-permute-start | bytes 9224 | tf_op jit(solution)/shard_map/ppermute | solution.py:440
  21.1 0.8 %shard_map.56 = (f32[4,4,64,128]{3,2,1,0:T(8,128)S(1)}, f32[4,4,64,128]{3,2,1,0:T(8,128)S(1)}) custom-call(f32[3,2,128]{2,1,0:T(2,128)S(1)} %get-tuple-element.94.refs_0_, f32[16,8,8,128]{3,2,1,0:T(8,128)S(1)} %get-tuple-element.87.yw.refs_1_, f32[16,8,8,128]{3,2,1,0:T(8,128)S(1)} %get-tuple-element.92.refs_2_, ...), custom_call_target="tpu_custom_call" | custom-call | flops 1572864 | bytes 2621440 | tf_op jit(solution)/shard_map/pallas_call | solution.py:974
  21.9 1.6 %collective-permute-done.7.got = f32[3,2,128]{2,1,0:T(2,128)S(1)} collective-permute-done((f32[3,2,128]{2,1,0:T(2,128)S(1)}, f32[3,2,128]{2,1,0:T(2,128)S(1)}, u32[]{:S(2)}, u32[]{:S(2)}) %collective-permute-start.7) | collective-permute-done | bytes 3104 | tf_op jit(solution)/shard_map/ppermute | solution.py:440
  23.5 1.1 %shard_map.57 = f32[4,64,512]{2,1,0:T(8,128)} custom-call(f32[3,2,128]{2,1,0:T(2,128)S(1)} %get-tuple-element.93.own, f32[3,2,128]{2,1,0:T(2,128)S(1)} %collective-permute-done.7.got, f32[4,4,64,128]{3,2,1,0:T(8,128)S(1)} %get-tuple-element.99.base, f32[4,4,64,128]{3,2,1,0:T(8,128)S(1)} %get-tuple-element.100.response, ...), custom_call_target="tpu_custom_call" | custom-call | tf_op jit(solution)/shard_map/pallas_call | solution.py:1019
  (1 shorter events, 0.0 us)
Async XLA Ops:
  1.4 5.3 %collective-permute-start.1 = (f32[16,128]{1,0:T(8,128)S(1)}, f32[16,128]{1,0:T(8,128)S(1)}, u32[]{:S(2)}, u32[]{:S(2)}) collective-permute-start(f32[16,128]{1,0:T(8,128)S(1)} %get-tuple-element.57.own_cells), channel_id=1, source_target_pairs={{0,3},{1,2},{2,1},{3,0},{4,7},{5,6},{6,5},{7,4},{8,11},{9,10},{10,... | collective-permute-start | bytes 24584 | tf_op jit(solution)/shard_map/ppermute | solution.py:1033
  3.9 2.8 %collective-permute-start = (f32[16,128]{1,0:T(8,128)S(1)}, f32[16,128]{1,0:T(8,128)S(1)}, u32[]{:S(2)}, u32[]{:S(2)}) collective-permute-start(f32[16,128]{1,0:T(8,128)S(1)} %get-tuple-element.57.own_cells), channel_id=1, source_target_pairs={{0,1},{1,0},{2,3},{3,2},{4,5},{5,4},{6,7},{7,6},{8,9},{9,8},{10,11... | collective-permute-start | bytes 24584 | tf_op jit(solution)/shard_map/ppermute | solution.py:440
  7.0 5.4 %collective-permute-start.4 = (f32[7,16,128]{2,1,0:T(8,128)S(1)}, f32[7,16,128]{2,1,0:T(8,128)S(1)}, u32[]{:S(2)}, u32[]{:S(2)}) collective-permute-start(f32[7,16,128]{2,1,0:T(8,128)S(1)} %get-tuple-element.66.after.refs_0_), channel_id=1, source_target_pairs={{0,12},{4,8},{8,4},{12,0},{16,28},{20,24},{24,20},{28,16},{1,13},{... | collective-permute-start | bytes 172040 | tf_op jit(solution)/shard_map/ppermute | solution.py:440
  9.5 4.2 %collective-permute-start.3 = (f32[7,16,128]{2,1,0:T(8,128)S(1)}, f32[7,16,128]{2,1,0:T(8,128)S(1)}, u32[]{:S(2)}, u32[]{:S(2)}) collective-permute-start(f32[7,16,128]{2,1,0:T(8,128)S(1)} %get-tuple-element.66.after.refs_0_), channel_id=1, source_target_pairs={{0,8},{4,12},{8,0},{12,4},{16,24},{20,28},{24,16},{28,20},{1,9},{5... | collective-permute-start | bytes 172040 | tf_op jit(solution)/shard_map/ppermute | solution.py:440
  10.0 4.2 %collective-permute-start.2 = (f32[7,16,128]{2,1,0:T(8,128)S(1)}, f32[7,16,128]{2,1,0:T(8,128)S(1)}, u32[]{:S(2)}, u32[]{:S(2)}) collective-permute-start(f32[7,16,128]{2,1,0:T(8,128)S(1)} %get-tuple-element.66.after.refs_0_), channel_id=1, source_target_pairs={{0,4},{4,0},{8,12},{12,8},{16,20},{20,16},{24,28},{28,24},{1,5},{5... | collective-permute-start | bytes 172040 | tf_op jit(solution)/shard_map/ppermute | solution.py:440
  14.2 4.8 %collective-permute-start.5 = (f32[3,16,128]{2,1,0:T(8,128)S(1)}, f32[3,16,128]{2,1,0:T(8,128)S(1)}, u32[]{:S(2)}, u32[]{:S(2)}) collective-permute-start(f32[3,16,128]{2,1,0:T(8,128)S(1)} %get-tuple-element.70.own), channel_id=1, source_target_pairs={{0,16},{4,20},{8,24},{12,28},{16,0},{20,4},{24,8},{28,12},{1,17},{... | collective-permute-start | bytes 73736 | tf_op jit(solution)/shard_map/ppermute | solution.py:440
  19.2 1.2 %collective-permute-start.6 = (f32[7,2,128]{2,1,0:T(2,128)S(1)}, f32[7,2,128]{2,1,0:T(2,128)S(1)}, u32[]{:S(2)}, u32[]{:S(2)}) collective-permute-start(f32[7,2,128]{2,1,0:T(2,128)S(1)} %get-tuple-element.83.after.refs_0_), channel_id=1, source_target_pairs={{0,1},{1,0},{2,3},{3,2},{4,5},{5,4},{6,7},{7,6},{8,9},{9,8},{10,11... | collective-permute-start | bytes 21512 | tf_op jit(solution)/shard_map/ppermute | solution.py:440
  20.4 3.1 %collective-permute-start.7 = (f32[3,2,128]{2,1,0:T(2,128)S(1)}, f32[3,2,128]{2,1,0:T(2,128)S(1)}, u32[]{:S(2)}, u32[]{:S(2)}) collective-permute-start(f32[3,2,128]{2,1,0:T(2,128)S(1)} %get-tuple-element.93.own), channel_id=1, source_target_pairs={{0,3},{1,2},{2,1},{3,0},{4,7},{5,6},{6,5},{7,4},{8,11},{9,10},{10,... | collective-permute-start | bytes 9224 | tf_op jit(solution)/shard_map/ppermute | solution.py:440
